TPU v7x, 32 devices: a whole 2x2x4 slice. The times are simulated.
32 devices in a mesh: grp: 2 (over x), inst: 2 (over core), tp: 8 (over z, y).
Axes of the slice: x: 2, y: 2, z: 4, core: 2. Of those that a mesh axis runs over, the one named last changes fastest.
Arguments:
- attention_output: bfloat16 [3, 1024, 8192], P(None, ('grp', 'inst'), 'tp'), parts along dimension 1, may hold values from -6 to 6
- output_weight: bfloat16 [8192, 8192], P('tp'), may hold values from -0.09375 to 0.09375
- adapter_down_weight: bfloat16 [192, 64, 8192], P('inst', None, 'tp'), may hold values from -0.0625 to 0.0625
- adapter_up_weight: bfloat16 [192, 64, 8192], P('inst', None, 'tp'), may hold values from -0.75 to 0.75
- adapter_page_table: int32 [192], replicated, may hold values from 0 to 191, each once
- block_adapter_ids: int32 [3, 8, 4], P(None, ('grp', 'inst')), parts along dimension 1, may hold values from 0 to 191, as said below
- row_list_position: int32 [3, 1024], P(None, ('grp', 'inst')), parts along dimension 1, may hold values from 0 to 3
- live_row_count: int32 [3, 4], P(None, ('grp', 'inst')), parts along dimension 1, may hold values from 1 to 256, as said below
Outputs:
- projected: bfloat16 [3, 1024, 8192], P(None, ('grp', 'inst'), 'tp'), parts along dimension 1
There are 2 independent parts, one for each index of `grp`. A program takes and returns all parts, laid end to end along the dimension named above; an argument that names none is the same for every part. Nothing has to cross between parts.
Inputs may be any that keep to these rules, and one draw needn't show every extreme that they name: `block_adapter_ids`: the 4 ids of one block are distinct. `live_row_count`: in every step some instance has all 256 of its rows live.
All inputs are finite; a program needn't handle non-finite values.
Results may differ from a plain program's by a relative error of at most 0.0037.
Values may be sent and summed in bfloat16 or wider, within the bound.
No kernel may reach another device: no remote copies, remote signals or barrier semaphores. Data moves between devices by JAX's collectives and lax.ppermute only.
A program may use at most 192 MiB of HBM per device.

v0:
```python
import jax
import jax.numpy as jnp
from jax import lax
from jax.sharding import PartitionSpec as P


def assemble_pieces(
    needed_adapters, adapter_page_table, adapter_down_weight, adapter_up_weight, local_instance
):
    resident_pages = adapter_down_weight.shape[0]
    paged = adapter_page_table[needed_adapters]
    home = paged // resident_pages
    local_page_index = paged % resident_pages
    owned = (home == local_instance)[:, :, None]
    flattened_down = adapter_down_weight[local_page_index].reshape(
        needed_adapters.shape[0], needed_adapters.shape[1], -1
    )
    flattened_up = adapter_up_weight[local_page_index].reshape(
        needed_adapters.shape[0], needed_adapters.shape[1], -1
    )
    nothing = jnp.zeros((), jnp.bfloat16)
    home_is_local = lax.dynamic_index_in_dim(home, local_instance, 0, keepdims=False)
    return (
        jnp.where(owned, flattened_down, nothing),
        jnp.where(owned, flattened_up, nothing),
        home_is_local,
    )


def choose_pieces(received, home_is_local):
    sources = jnp.arange(received.shape[0], dtype=jnp.int32)
    chosen = (sources[:, None] == home_is_local[None, :])[:, :, None]
    return jnp.sum(
        jnp.where(chosen, received, jnp.zeros((), jnp.bfloat16)), axis=0, dtype=jnp.bfloat16
    )


def per_device(
    attention_output,
    output_weight,
    adapter_down_weight,
    adapter_up_weight,
    adapter_page_table,
    block_adapter_ids,
    row_list_position,
    live_row_count,
):
    local_instance = lax.axis_index("inst")
    step_count, row_count, shard_cols = attention_output.shape
    rank_columns = adapter_down_weight.shape[1]
    block_count = block_adapter_ids.shape[1]
    listed = block_adapter_ids.shape[2]
    block_rows = row_count // block_count
    results = []
    for current in range(step_count):
        needed_adapters = lax.all_gather(
            block_adapter_ids[current].reshape(1, -1), "inst", axis=0, tiled=True
        )
        outgoing_down, outgoing_up, home_is_local = assemble_pieces(
            needed_adapters,
            adapter_page_table,
            adapter_down_weight,
            adapter_up_weight,
            local_instance,
        )
        got_down, got_up = (
            lax.all_to_all(outgoing_down, "inst", split_axis=0, concat_axis=0, tiled=True),
            lax.all_to_all(outgoing_up, "inst", split_axis=0, concat_axis=0, tiled=True),
        )
        down_matrices = choose_pieces(got_down, home_is_local).reshape(
            block_count, listed, rank_columns, shard_cols
        )
        up_matrices = choose_pieces(got_up, home_is_local).reshape(
            block_count, listed, rank_columns, shard_cols
        )
        inputs = attention_output[current]
        in_blocks = inputs.reshape(block_count, block_rows, shard_cols)
        low_all = jnp.einsum(
            "brd,blkd->brlk", in_blocks, down_matrices, preferred_element_type=jnp.float32
        )
        slots = row_list_position[current].reshape(block_count, block_rows)
        picked = slots[:, :, None] == jnp.arange(listed, dtype=jnp.int32)[None, None, :]
        low_part = jnp.sum(jnp.where(picked[:, :, :, None], low_all, 0.0), axis=2).reshape(
            row_count, rank_columns
        )
        low = lax.psum(low_part, "tp")
        base = lax.psum_scatter(
            lax.dot_general(
                output_weight, inputs, (((0,), (1,)), ((), ())), preferred_element_type=jnp.float32
            ),
            "tp",
            scatter_dimension=0,
            tiled=True,
        ).T
        low_b = low.astype(jnp.bfloat16).reshape(block_count, block_rows, 1, rank_columns)
        expanded = jnp.where(picked[:, :, :, None], low_b, jnp.zeros((), jnp.bfloat16))
        delta = jnp.einsum(
            "brlk,blkd->brd", expanded, up_matrices, preferred_element_type=jnp.float32
        ).reshape(row_count, shard_cols)
        alive = jnp.arange(row_count, dtype=jnp.int32) < live_row_count[current, 0]
        results.append(jnp.where(alive[:, None], base + delta, 0.0).astype(jnp.bfloat16))
    return jnp.stack(results)


def solution(mesh):
    in_specs = (
        P(None, ("grp", "inst"), "tp"),
        P("tp", None),
        P("inst", None, "tp"),
        P("inst", None, "tp"),
        P(),
        P(None, ("grp", "inst"), None),
        P(None, ("grp", "inst")),
        P(None, ("grp", "inst")),
    )
    out_specs = P(None, ("grp", "inst"), "tp")
    return jax.shard_map(
        per_device, mesh=mesh, in_specs=in_specs, out_specs=out_specs, check_vma=False
    )
```

profile of v0, /device:TPU:0, one launch (start us, length us, event | category | flops | bytes accessed | tf_op | source)
XLA Modules:
  0.0 489.5 jit_solution(10287385006173868368)
XLA Ops:
  6.5 13.8 %fusion.19 = f32[8192,256]{1,0:T(8,128)} fusion(bf16[1024,8192]{1,0:T(8,128)(2,1)} %param.9, bf16[3,256,1024]{2,1,0:T(8,128)(2,1)} %param.8), kind=kOutput, calls=%fused_computation.47 | convolution fusion | flops 4294967296 | bytes 25690112 | tf_op jit(solution)/shard_map/dot_general | solution.py:88
  20.4 13.8 %fusion.15 = f32[8192,256]{1,0:T(8,128)} fusion(bf16[1024,8192]{1,0:T(8,128)(2,1)} %param.9, bf16[3,256,1024]{2,1,0:T(8,128)(2,1)} %param.8), kind=kOutput, calls=%fused_computation.43 | convolution fusion | flops 4294967296 | bytes 25690112 | tf_op jit(solution)/shard_map/dot_general | solution.py:88
  38.0 5.3 %gather_fusion.2 = bf16[16,64,1024]{2,1,0:T(8,128)(2,1)S(1)} fusion(bf16[96,64,1024]{2,1,0:T(8,128)(2,1)} %param.11, s32[1024]{0:T(1024)S(1)} %pad_clamp_fusion.4), kind=kCustom, calls=%fused_computation.2 | custom fusion | bytes 4194368 | tf_op jit(solution)/shard_map/gather | solution.py:18
  45.3 5.4 %gather_fusion.1 = bf16[16,64,1024]{2,1,0:T(8,128)(2,1)S(1)} fusion(bf16[96,64,1024]{2,1,0:T(8,128)(2,1)} %param.10, s32[1024]{0:T(1024)S(1)} %pad_clamp_fusion.4), kind=kCustom, calls=%fused_computation.1 | custom fusion | bytes 4194368 | tf_op jit(solution)/shard_map/gather | solution.py:15
  52.7 4.6 broadcast_select_fusion.4
  57.3 3.9 all-to-all-start.1
  61.4 14.2 %fusion.17 = f32[8192,256]{1,0:T(8,128)} fusion(bf16[1024,8192]{1,0:T(8,128)(2,1)} %param.9, bf16[3,256,1024]{2,1,0:T(8,128)(2,1)} %param.8), kind=kOutput, calls=%fused_computation.45 | convolution fusion | flops 4294967296 | bytes 25690112 | tf_op jit(solution)/shard_map/dot_general | solution.py:88
  83.6 6.7 %gather_fusion.8 = bf16[16,64,1024]{2,1,0:T(8,128)(2,1)} fusion(bf16[96,64,1024]{2,1,0:T(8,128)(2,1)} %param.11, s32[1024]{0:T(1024)S(1)} %pad_clamp_fusion), kind=kCustom, calls=%fused_computation.8 | custom fusion | bytes 4194368 | tf_op jit(solution)/shard_map/gather | solution.py:18
  90.3 6.7 %gather_fusion.7 = bf16[16,64,1024]{2,1,0:T(8,128)(2,1)} fusion(bf16[96,64,1024]{2,1,0:T(8,128)(2,1)} %param.10, s32[1024]{0:T(1024)S(1)} %pad_clamp_fusion), kind=kCustom, calls=%fused_computation.7 | custom fusion | bytes 4194368 | tf_op jit(solution)/shard_map/gather | solution.py:15
  97.0 6.8 %gather_fusion.5 = bf16[16,64,1024]{2,1,0:T(8,128)(2,1)} fusion(bf16[96,64,1024]{2,1,0:T(8,128)(2,1)} %param.11, s32[1024]{0:T(1024)S(1)} %pad_clamp_fusion.2), kind=kCustom, calls=%fused_computation.5 | custom fusion | bytes 4194368 | tf_op jit(solution)/shard_map/gather | solution.py:18
  103.8 6.6 %gather_fusion.4 = bf16[16,64,1024]{2,1,0:T(8,128)(2,1)} fusion(bf16[96,64,1024]{2,1,0:T(8,128)(2,1)} %param.10, s32[1024]{0:T(1024)S(1)} %pad_clamp_fusion.2), kind=kCustom, calls=%fused_computation.4 | custom fusion | bytes 4194368 | tf_op jit(solution)/shard_map/gather | solution.py:15
  117.3 4.5 broadcast_select_fusion
  121.8 8.6 %all_to_all.30 = bf16[2,8,65536]{2,1,0:T(8,128)(2,1)} all-to-all(bf16[2,8,65536]{2,1,0:T(8,128)(2,1)} %get-tuple-element.33), channel_id=1, replica_groups=mesh['grp'=2,'inst'=2,'tp'=8] {'inst'}, dimensions={0} | all-to-all | bytes 4194304 | tf_op jit(solution)/shard_map/all_to_all | solution.py:67
  130.4 5.1 %all-to-all-start.5 = ((bf16[2,8,65536]{2,1,0:T(8,128)(2,1)}), bf16[2,8,65536]{2,1,0:T(8,128)(2,1)}, u32[]{:S(2)}, u32[]{:S(2)}) async-start(bf16[2,8,65536]{2,1,0:T(8,128)(2,1)} %get-tuple-element.40), calls=%async_computation.8 | async-start | bytes 4194304 | tf_op jit(solution)/shard_map/all_to_all | solution.py:68
  135.5 3.3 select_reduce_fusion.5
  141.4 3.4 reshape.279
  146.8 4.9 broadcast_select_fusion.2
  151.7 6.3 %all_to_all.31 = bf16[2,8,65536]{2,1,0:T(8,128)(2,1)} all-to-all(bf16[2,8,65536]{2,1,0:T(8,128)(2,1)S(1)} %copy-done.3), channel_id=1, replica_groups=mesh['grp'=2,'inst'=2,'tp'=8] {'inst'}, dimensions={0} | all-to-all | bytes 4194304 | tf_op jit(solution)/shard_map/all_to_all | solution.py:67
  157.9 3.8 all-to-all-start.3
  161.7 3.9 select_reduce_fusion.1
  168.2 6.7 %all_to_all.32 = bf16[2,8,65536]{2,1,0:T(8,128)(2,1)S(1)} all-to-all(bf16[2,8,65536]{2,1,0:T(8,128)(2,1)} %get-tuple-element.37), channel_id=1, replica_groups=mesh['grp'=2,'inst'=2,'tp'=8] {'inst'}, dimensions={0} | all-to-all | bytes 4194304 | tf_op jit(solution)/shard_map/all_to_all | solution.py:67
  178.1 47.1 %all-reduce.2 = (bf16[256,64]{0,1:T(8,128)(2,1)S(1)}, bf16[256,64]{0,1:T(8,128)(2,1)S(1)}, bf16[256,64]{0,1:T(8,128)(2,1)S(1)}) all-reduce(f32[256,64]{0,1:T(8,128)S(1)} %copy_bitcast_fusion, f32[256,64]{0,1:T(8,128)S(1)} %copy_bitcast_fusion.1, f32[256,64]{0,1:T(8,128)S(1)} %copy_bitcast_fusion.2), channel_id=1, replica_groups=mesh['grp'=2,'inst'=2,'tp'=8] {'tp'}, use_global_device_ids=true, to_apply=%region_13.14 | all-reduce | flops 49152 | bytes 294912 | tf_op jit(solution)/shard_map/psum | solution.py:86
  237.2 90.7 %reduce-scatter.8.cloned.1.call-done = f32[1024,256]{1,0:T(8,128)} async-done(((f32[8192,256]{1,0:T(8,128)}), f32[1024,256]{1,0:T(8,128)}) %reduce-scatter.8.cloned.1.call-update) | async-done | bytes 1048592 | tf_op jit(solution)/shard_map/reduce_scatter | solution.py:87
  329.4 150.2 %reduce-scatter.6.cloned.1.call-done = f32[1024,256]{1,0:T(8,128)} async-done(((f32[8192,256]{1,0:T(8,128)}), f32[1024,256]{1,0:T(8,128)}) %reduce-scatter.6.cloned.1.call-update) | async-done | bytes 1048592 | tf_op jit(solution)/shard_map/reduce_scatter | solution.py:87
  (123 shorter events, 49.7 us)
Async XLA Ops:
  6.5 30.4 %copy-start = (s32[192]{0:T(256)S(1)}, s32[192]{0:T(256)}, u32[]{:S(2)}) copy-start(s32[192]{0:T(256)} %param.12) | copy-start | bytes 2308
  6.5 228.5 %reduce-scatter.4.cloned.1.call-start = ((), (), s32[]{:S(2)}) async-start(), calls=%async_computation.9 | async-start | bytes 9437184 | tf_op jit(solution)/shard_map/reduce_scatter | solution.py:87
  20.4 307.6 %reduce-scatter.8.cloned.1.call-start = ((), (), s32[]{:S(2)}) async-start(), calls=%async_computation.11 | async-start | bytes 9437184 | tf_op jit(solution)/shard_map/reduce_scatter | solution.py:87
  34.2 0.7 copy-start.9
  57.3 64.5 %all-to-all-start.1 = ((bf16[2,8,65536]{2,1,0:T(8,128)(2,1)}), bf16[2,8,65536]{2,1,0:T(8,128)(2,1)S(1)}, u32[]{:S(2)}, u32[]{:S(2)}) async-start(bf16[2,8,65536]{2,1,0:T(8,128)(2,1)} %get-tuple-element.32), calls=%async_computation.2 | async-start | bytes 4194304 | tf_op jit(solution)/shard_map/all_to_all | solution.py:68
  61.3 418.4 %reduce-scatter.6.cloned.1.call-start = ((), (), s32[]{:S(2)}) async-start(), calls=%async_computation.10 | async-start | bytes 9437184 | tf_op jit(solution)/shard_map/reduce_scatter | solution.py:87
  103.8 6.6 %copy-start.10 = (s32[3,256]{1,0:T(4,128)S(1)}, s32[3,256]{1,0:T(4,128)}, u32[]{:S(2)}) copy-start(s32[3,256]{1,0:T(4,128)} %param.14) | copy-start | bytes 9220
  130.4 21.2 %all-to-all-start.5 = ((bf16[2,8,65536]{2,1,0:T(8,128)(2,1)}), bf16[2,8,65536]{2,1,0:T(8,128)(2,1)}, u32[]{:S(2)}, u32[]{:S(2)}) async-start(bf16[2,8,65536]{2,1,0:T(8,128)(2,1)} %get-tuple-element.40), calls=%async_computation.8 | async-start | bytes 4194304 | tf_op jit(solution)/shard_map/all_to_all | solution.py:68
  141.4 3.4 copy-start.2
  146.8 4.9 copy-start.3
  157.9 10.3 %all-to-all-start.3 = ((bf16[2,8,65536]{2,1,0:T(8,128)(2,1)}), bf16[2,8,65536]{2,1,0:T(8,128)(2,1)S(1)}, u32[]{:S(2)}, u32[]{:S(2)}) async-start(bf16[2,8,65536]{2,1,0:T(8,128)(2,1)} %get-tuple-element.36), calls=%async_computation.5 | async-start | bytes 4194304 | tf_op jit(solution)/shard_map/all_to_all | solution.py:68
  176.6 1.0 copy-start.7
  176.6 48.6 %copy-start.5 = (bf16[1,8,64,1024]{3,2,1,0:T(8,128)(2,1)S(1)}, bf16[1,8,64,1024]{3,2,1,0:T(8,128)(2,1)}, u32[]{:S(2)}) copy-start(bf16[1,8,64,1024]{3,2,1,0:T(8,128)(2,1)} %copy.57) | copy-start | bytes 3145732
  226.6 2.9 copy-start.4
  229.5 2.9 copy-start.8
  237.2 243.8 %copy-start.6 = (bf16[1,256,1024]{1,2,0:T(8,128)(2,1)S(1)}, bf16[1,256,1024]{1,2,0:T(8,128)(2,1)}, u32[]{:S(2)}) copy-start(bf16[1,256,1024]{1,2,0:T(8,128)(2,1)} %fusion.12) | copy-start | bytes 1572868
  481.1 1.9 copy-start.1
Sparse Core Ops, SparseCore 0:
  20.5 151.7 reduce-scatter.3
  176.3 151.5 reduce-scatter.7
  331.6 147.9 reduce-scatter.5
where the time goes:
time: 491 us; the launch traced here: 490 us
  waiting for transfers between devices  241 us (49%)
  blocking collectives  74.3 us (15%)
  local copies, waits for them, and re-layouts  71.4 us (15%)
  matrix products  46.1 us (9%)
  other arithmetic  30.3 us (6%)
  between operations  13.5 us (3%)
  starting transfers between devices  12.9 us (3%)
    reduce_scatter x3, waiting for transfers between devices, per_device(): lax.psum_scatter(lax.dot_general(output_weight, inputs, (((0,), (1,)), ((...  241 us
    psum x1, blocking collectives, per_device(): low = lax.psum(low_part, 'tp')  47.1 us
    dot_general x3, matrix products, per_device(): lax.dot_general(output_weight, inputs, (((0,), (1,)), ((), ())), preferre...  41.8 us
    all_to_all x3, blocking collectives, per_device(): lax.all_to_all(outgoing_down, 'inst', split_axis=0, concat_axis=0, tiled=...  21.6 us
    gather x3, local copies, waits for them, and re-layouts, assemble_pieces(): adapter_up_weight[local_page_index]  18.8 us
    gather x3, local copies, waits for them, and re-layouts, assemble_pieces(): adapter_down_weight[local_page_index]  18.7 us
    select_n x3, other arithmetic, assemble_pieces(): jnp.where(owned, flattened_up, nothing)  14 us
    all_to_all x3, starting transfers between devices, per_device(): lax.all_to_all(outgoing_up, 'inst', split_axis=0, concat_axis=0, tiled=True)  12.8 us
  transfers between devices with their start and end apart: 6, of which 2 were waited for; matrix products, arithmetic and copies ran while one was open for 26% of the time, Pallas kernels for 0%

commit v1 on v0

v1 whole, which is shorter than its diff:
```python
import functools

import jax
import jax.numpy as jnp
from jax import lax
from jax.experimental import pallas as pl
from jax.experimental.pallas import tpu as pltpu
from jax.sharding import PartitionSpec as P

VMEM_LIMIT = 40 * 1024 * 1024


def ring_order(size):
    if size == 8:
        return list(range(0, size, 2)) + list(range(size - 1, 0, -2))
    return list(range(size))


def params():
    return pltpu.CompilerParams(vmem_limit_bytes=VMEM_LIMIT)


def hop_kernel(with_received, dests, x_ref, w_ref, *refs):
    total = jnp.dot(x_ref[...], w_ref[...], preferred_element_type=jnp.float32)
    if with_received:
        total = total + refs[0][...].astype(jnp.float32)
    refs[-1][...] = total.astype(refs[-1].dtype)


def hop(dests, offset, half, x, weight, received):
    rows, depth = x.shape
    block_cols = weight.shape[1] // dests.shape[0]
    half_cols = block_cols // 2
    tile = min(256, half_cols)
    tiles = half_cols // tile
    in_specs = [
        pl.BlockSpec((rows, depth), lambda j, d: (0, 0)),
        pl.BlockSpec(
            (depth, tile), lambda j, d: (0, (d[offset] * 2 + half) * tiles + j)
        ),
    ]
    operands = [x, weight]
    if received is not None:
        in_specs.append(pl.BlockSpec((rows, tile), lambda j, d: (0, j)))
        operands.append(received)
    return pl.pallas_call(
        functools.partial(hop_kernel, received is not None),
        grid_spec=pltpu.PrefetchScalarGridSpec(
            num_scalar_prefetch=1,
            grid=(tiles,),
            in_specs=in_specs,
            out_specs=pl.BlockSpec((rows, tile), lambda j, d: (0, j)),
        ),
        out_shape=jax.ShapeDtypeStruct((rows, half_cols), jnp.bfloat16),
        compiler_params=params(),
        cost_estimate=pl.CostEstimate(
            flops=2 * rows * depth * half_cols,
            bytes_accessed=2 * (rows * depth + depth * half_cols + 2 * rows * half_cols),
            transcendentals=0,
        ),
    )(dests, *operands)


def collect_kernel(count, index, table_ref, out_ref, sems):
    for slot in range(count):
        pltpu.make_async_copy(
            table_ref.at[index[slot]], out_ref.at[slot], sems.at[slot]
        ).start()
    for slot in range(count):
        pltpu.make_async_copy(
            table_ref.at[index[slot]], out_ref.at[slot], sems.at[slot]
        ).wait()


def collect(index, table):
    count = index.shape[0]
    shape = (count,) + table.shape[1:]
    return pl.pallas_call(
        functools.partial(collect_kernel, count),
        grid_spec=pltpu.PrefetchScalarGridSpec(
            num_scalar_prefetch=1,
            grid=(1,),
            in_specs=[pl.BlockSpec(memory_space=pl.ANY)],
            out_specs=pl.BlockSpec(memory_space=pl.ANY),
            scratch_shapes=[pltpu.SemaphoreType.DMA((count,))],
        ),
        out_shape=jax.ShapeDtypeStruct(shape, table.dtype),
        compiler_params=params(),
        cost_estimate=pl.CostEstimate(
            flops=0, bytes_accessed=4 * shape[0] * shape[1] * shape[2], transcendentals=0
        ),
    )(index, table)


def load_pages(count, local, index, table_ref, got_ref, pages, sems):
    for slot in range(count):
        own = local[slot] == 1

        @pl.when(own)
        def _():
            pltpu.make_async_copy(
                table_ref.at[index[slot]], pages.at[slot], sems.at[slot]
            ).start()

        @pl.when(jnp.logical_not(own))
        def _():
            pltpu.make_async_copy(got_ref.at[slot], pages.at[slot], sems.at[slot]).start()

    for slot in range(count):
        pltpu.make_async_copy(got_ref.at[slot], pages.at[slot], sems.at[slot]).wait()


def low_kernel(sizes, local, index, x_ref, place_ref, table_ref, got_ref, out_ref, pages, sems):
    steps, blocks, listed, rank, block_rows = sizes
    load_pages(steps * blocks * listed, local, index, table_ref, got_ref, pages, sems)
    column = lax.broadcasted_iota(jnp.int32, (block_rows, listed * rank), 1) // rank
    for step in range(steps):
        for block in range(blocks):
            at = step * blocks + block
            rows = pl.ds(at * block_rows, block_rows)
            listing = pages[at * listed : (at + 1) * listed].reshape(listed * rank, -1)
            every = lax.dot_general(
                x_ref[rows, :], listing, (((1,), (1,)), ((), ())),
                preferred_element_type=jnp.float32,
            )
            every = jnp.where(column == place_ref[rows, :], every, 0.0)
            low = every[:, :rank]
            for entry in range(1, listed):
                low = low + every[:, entry * rank : (entry + 1) * rank]
            out_ref[step, :, block * rank : (block + 1) * rank] = low


def low_rank(sizes, local, index, x, place, table, got):
    steps, blocks, listed, rank, block_rows = sizes
    count = steps * blocks * listed
    depth = x.shape[1]
    whole = pl.BlockSpec(memory_space=pltpu.VMEM)
    return pl.pallas_call(
        functools.partial(low_kernel, sizes),
        grid_spec=pltpu.PrefetchScalarGridSpec(
            num_scalar_prefetch=2,
            grid=(1,),
            in_specs=[
                whole, whole, pl.BlockSpec(memory_space=pl.ANY), pl.BlockSpec(memory_space=pl.ANY)
            ],
            out_specs=whole,
            scratch_shapes=[
                pltpu.VMEM((count, rank, depth), table.dtype),
                pltpu.SemaphoreType.DMA((count,)),
            ],
        ),
        out_shape=jax.ShapeDtypeStruct((steps, block_rows, blocks * rank), jnp.float32),
        compiler_params=params(),
        cost_estimate=pl.CostEstimate(
            flops=2 * x.shape[0] * depth * listed * rank,
            bytes_accessed=2 * (x.shape[0] * depth + count * rank * depth),
            transcendentals=0,
        ),
    )(local, index, x, place, table, got)


def own_kernel(
    sizes, dests, local, index, x_ref, w_ref, place_ref, low_ref, table_ref, got_ref, out_ref,
    pages, sems,
):
    steps, blocks, listed, rank, block_rows = sizes
    tile = w_ref.shape[1]
    now = pl.program_id(0)

    @pl.when(now == 0)
    def _():
        load_pages(steps * blocks * listed, local, index, table_ref, got_ref, pages, sems)

    columns = pl.ds(pl.multiple_of(now * tile, tile), tile)
    out_ref[...] = jnp.dot(x_ref[...], w_ref[...], preferred_element_type=jnp.float32)
    column = lax.broadcasted_iota(jnp.int32, (block_rows, listed * rank), 1) // rank
    for step in range(steps):
        for block in range(blocks):
            at = step * blocks + block
            rows = pl.ds(at * block_rows, block_rows)
            low = low_ref[step, :, block * rank : (block + 1) * rank]
            spread = jnp.concatenate([low] * listed, axis=1)
            spread = jnp.where(column == place_ref[rows, :], spread, 0.0).astype(jnp.bfloat16)
            listing = pages[at * listed : (at + 1) * listed, :, columns]
            out_ref[rows, :] += jnp.dot(
                spread, listing.reshape(listed * rank, tile), preferred_element_type=jnp.float32
            )


def own_terms(sizes, dests, local, index, x, weight, place, low, table, got):
    steps, blocks, listed, rank, block_rows = sizes
    count = steps * blocks * listed
    rows, depth = x.shape
    cols = weight.shape[1] // dests.shape[0]
    tile = min(256, cols)
    tiles = cols // tile
    whole = pl.BlockSpec(memory_space=pltpu.VMEM)
    return pl.pallas_call(
        functools.partial(own_kernel, sizes),
        grid_spec=pltpu.PrefetchScalarGridSpec(
            num_scalar_prefetch=3,
            grid=(tiles,),
            in_specs=[
                whole,
                pl.BlockSpec((depth, tile), lambda j, d, l, i: (0, d[0] * tiles + j)),
                whole,
                whole,
                pl.BlockSpec(memory_space=pl.ANY),
                pl.BlockSpec(memory_space=pl.ANY),
            ],
            out_specs=pl.BlockSpec((rows, tile), lambda j, d, l, i: (0, j)),
            scratch_shapes=[
                pltpu.VMEM((count, rank, cols), table.dtype),
                pltpu.SemaphoreType.DMA((count,)),
            ],
        ),
        out_shape=jax.ShapeDtypeStruct((rows, cols), jnp.float32),
        compiler_params=params(),
        cost_estimate=pl.CostEstimate(
            flops=2 * rows * cols * (depth + listed * rank),
            bytes_accessed=2 * (rows * depth + depth * cols + count * rank * cols) + 4 * rows * cols,
            transcendentals=0,
        ),
    )(dests, local, index, x, weight, place, low, table, got)


def sum_over(value, axis, size):
    if size & (size - 1):
        return lax.psum(value, axis)
    apart = 1
    while apart < size:
        value = value + lax.ppermute(value, axis, [(i, i ^ apart) for i in range(size)])
        apart *= 2
    return value


def per_device(
    ring,
    attention_output,
    output_weight,
    adapter_down_weight,
    adapter_up_weight,
    adapter_page_table,
    block_adapter_ids,
    row_list_position,
    live_row_count,
):
    size = len(ring)
    steps, row_count, depth = attention_output.shape
    resident, rank, _ = adapter_down_weight.shape
    _, blocks, listed = block_adapter_ids.shape
    sizes = (steps, blocks, listed, rank, row_count // blocks)
    rows = steps * row_count
    x = attention_output.reshape(rows, depth)

    instance = lax.axis_index("inst")
    tp = lax.axis_index("tp")
    ring_at = jnp.array(ring, dtype=jnp.int32)
    place_of = [0] * size
    for at, index in enumerate(ring):
        place_of[index] = at
    place = jnp.array(place_of, dtype=jnp.int32)[tp]
    dests = ring_at[(place + jnp.arange(size, dtype=jnp.int32)) % size]

    swap = [(0, 1), (1, 0)]
    ids = block_adapter_ids.reshape(-1)
    ids_there = lax.ppermute(ids, "inst", swap)
    pages = adapter_page_table[ids]
    index = pages % resident
    local = (pages // resident == instance).astype(jnp.int32)
    index_there = adapter_page_table[ids_there] % resident
    got_down = lax.ppermute(collect(index_there, adapter_down_weight), "inst", swap)
    got_up = lax.ppermute(collect(index_there, adapter_up_weight), "inst", swap)

    forward = [(ring[i], ring[(i + 1) % size]) for i in range(size)]
    backward = [(ring[i], ring[i - 1]) for i in range(size)]
    far = size // 2
    chains = [
        (0, 1, forward, far),
        (1, -1, backward, far),
        (1, 1, forward, size - 1 - far),
        (0, -1, backward, size - 1 - far),
    ]
    arrived = [None] * len(chains)
    for left in range(far, 0, -1):
        for chain, (half, sign, moves, length) in enumerate(chains):
            if left <= length:
                partial = hop(
                    dests, (sign * left) % size, half, x, output_weight, arrived[chain]
                )
                arrived[chain] = lax.ppermute(partial, "tp", moves)

    slots = row_list_position.reshape(rows, 1)
    low = low_rank(sizes, local, index, x, slots, adapter_down_weight, got_down)
    low = sum_over(low, "tp", size)
    own = own_terms(
        sizes, dests, local, index, x, output_weight, slots, low, adapter_up_weight, got_up
    )
    halves = []
    for half in range(2):
        there = [a for a, c in zip(arrived, chains) if c[0] == half]
        halves.append(sum(a.astype(jnp.float32) for a in there))
    total = own + jnp.concatenate(halves, axis=1)
    alive = jnp.arange(row_count, dtype=jnp.int32)[None, :] < live_row_count
    total = jnp.where(alive[:, :, None], total.reshape(steps, row_count, -1), 0.0)
    return total.astype(jnp.bfloat16)


def solution(mesh):
    in_specs = (
        P(None, ("grp", "inst"), "tp"),
        P("tp", None),
        P("inst", None, "tp"),
        P("inst", None, "tp"),
        P(),
        P(None, ("grp", "inst"), None),
        P(None, ("grp", "inst")),
        P(None, ("grp", "inst")),
    )
    out_specs = P(None, ("grp", "inst"), "tp")
    ring = ring_order(mesh.shape["tp"])
    return jax.shard_map(
        functools.partial(per_device, ring),
        mesh=mesh, in_specs=in_specs, out_specs=out_specs, check_vma=False,
    )
```

time: 491 us -> 354 us (0.72)
  Pallas kernels: 0 us -> 250 us
  waiting for transfers between devices: 241 us -> 73 us
  blocking collectives: 74.3 us -> 0 us
  local copies, waits for them, and re-layouts: 71.4 us -> 5.64 us
  matrix products: 46.1 us -> 0 us
  other arithmetic: 30.3 us -> 4.98 us
  between operations: 13.5 us -> 0.29 us
  starting transfers between devices: 12.9 us -> 19.1 us
    pallas_call x0 -> x18, Pallas kernels: none -> 250 us  [the longest x2 194 us: collect(): pl.pallas_call(functools.partial(collect_kernel, count), grid_spec=pltpu....]
    reduce_scatter x3 -> x0, waiting for transfers between devices: 241 us -> none  [per_device(): lax.psum_scatter(lax.dot_general(output_weight, inputs, (((0,), (1,)), ((...]
    ppermute x0 -> x20, waiting for transfers between devices: none -> 73 us  [the longest x3 43.4 us: sum_over(): lax.ppermute(value, axis, [(i, i ^ apart) for i in range(size)])]
    psum x1 -> x0, blocking collectives: 47.1 us -> none  [per_device(): low = lax.psum(low_part, 'tp')]
    dot_general x9 -> x0, matrix products: 46.1 us -> none  [the longest x3 41.8 us: per_device(): lax.dot_general(output_weight, inputs, (((0,), (1,)), ((), ())), preferre...]
    gather x9 -> x3, local copies, waits for them, and re-layouts: 39.4 us -> 2.06 us  [the longest x1 0.71 us: per_device(): index_there = adapter_page_table[ids_there] % resident]
    all_to_all x3 -> x0, blocking collectives: 21.6 us -> none  [per_device(): lax.all_to_all(outgoing_down, 'inst', split_axis=0, concat_axis=0, tiled=...]
    ppermute x0 -> x20, starting transfers between devices: none -> 19.1 us  [the longest x14 16.7 us: per_device(): arrived[chain] = lax.ppermute(partial, 'tp', moves)]
  transfers between devices with their start and end apart: 6 -> 20, of which waited for: 2 -> 7; matrix products, arithmetic and copies ran while one was open for 26% -> 2% of each run, Pallas kernels for 0% -> 41%
where the time goes in v1:
time: 354 us; the launch traced here: 353 us
  Pallas kernels  250 us (71%)
  waiting for transfers between devices  73 us (21%)
  starting transfers between devices  19.1 us (5%)
  local copies, waits for them, and re-layouts  5.64 us (2%)
  other arithmetic  4.98 us (1%)
    pallas_call x2, Pallas kernels, collect(): pl.pallas_call(functools.partial(collect_kernel, count), grid_spec=pltpu....  194 us
    pallas_call x14, Pallas kernels, hop(): pl.pallas_call(functools.partial(hop_kernel, received is not None), grid_...  45 us
    ppermute x3, waiting for transfers between devices, sum_over(): lax.ppermute(value, axis, [(i, i ^ apart) for i in range(size)])  43.4 us
    ppermute x14, waiting for transfers between devices, per_device(): arrived[chain] = lax.ppermute(partial, 'tp', moves)  29.5 us
    ppermute x14, starting transfers between devices, per_device(): arrived[chain] = lax.ppermute(partial, 'tp', moves)  16.7 us
  transfers between devices with their start and end apart: 20, of which 7 were waited for; matrix products, arithmetic and copies ran while one was open for 2% of the time, Pallas kernels for 41%

profile of v1, /device:TPU:0, one launch (start us, length us, event | category | flops | bytes accessed | tf_op | source)
XLA Modules:
  0.0 353.4 jit_solution(5479956708549966774)
XLA Ops:
  3.2 97.2 %shard_map.103 = bf16[24,64,1024]{2,1,0:T(8,128)(2,1)} custom-call(s32[24]{0:T(128)S(1)} %and_select_fusion.index, bf16[96,64,1024]{2,1,0:T(8,128)(2,1)} %table_ref.5), custom_call_target="tpu_custom_call" | custom-call | bytes 6291456 | tf_op jit(solution)/shard_map/pallas_call | solution.py:78
  101.9 2.8 shard_map.114
  104.7 3.0 collective-permute-start.13
  110.6 2.8 shard_map.118
  115.5 10.0 %collective-permute-done.13.refs_0_ = bf16[768,512]{1,0:T(8,128)(2,1)S(1)} collective-permute-done((bf16[768,512]{1,0:T(8,128)(2,1)S(1)}, bf16[768,512]{1,0:T(8,128)(2,1)S(1)}, u32[]{:S(2)}, u32[]{:S(2)}) %collective-permute-start.13) | collective-permute-done | bytes 786464 | tf_op jit(solution)/shard_map/ppermute | solution.py:291
  125.5 2.8 shard_map.115
  130.0 3.5 %shard_map.111 = bf16[768,512]{1,0:T(8,128)(2,1)} custom-call(s32[8]{0:T(128)S(1)} %gather_fusion, bf16[768,1024]{1,0:T(8,128)(2,1)S(1)} %bitcast.16, bf16[1024,8192]{1,0:T(8,128)(2,1)} %w_ref.29), custom_call_target="tpu_custom_call" | custom-call | flops 805306368 | bytes 4194304 | tf_op jit(solution)/shard_map/pallas_call | solution.py:46
  135.1 97.1 %shard_map.105 = bf16[24,64,1024]{2,1,0:T(8,128)(2,1)} custom-call(s32[24]{0:T(128)S(1)} %and_select_fusion.index, bf16[96,64,1024]{2,1,0:T(8,128)(2,1)} %table_ref.7), custom_call_target="tpu_custom_call" | custom-call | bytes 6291456 | tf_op jit(solution)/shard_map/pallas_call | solution.py:78
  232.4 3.6 %shard_map.108 = bf16[768,512]{1,0:T(8,128)(2,1)} custom-call(s32[8]{0:T(128)S(1)} %gather_fusion, bf16[768,1024]{1,0:T(8,128)(2,1)S(1)} %bitcast.17, bf16[1024,8192]{1,0:T(8,128)(2,1)} %w_ref.29, bf16[768,512]{1,0:T(8,128)(2,1)S(1)} %collective-permute-done.6.refs_0_), custom_call_target="tpu_custom_call" | custom-call | flops 805306368 | bytes 4194304 | tf_op jit(solution)/shard_map/pallas_call | solution.py:46
  236.5 3.5 shard_map.119
  240.4 3.6 %shard_map.116 = bf16[768,512]{1,0:T(8,128)(2,1)} custom-call(s32[8]{0:T(128)S(1)} %gather_fusion, bf16[768,1024]{1,0:T(8,128)(2,1)S(1)} %bitcast.19, bf16[1024,8192]{1,0:T(8,128)(2,1)} %w_ref.29, bf16[768,512]{1,0:T(8,128)(2,1)S(1)} %collective-permute-done.14.refs_0_), custom_call_target="tpu_custom_call" | custom-call | flops 805306368 | bytes 4194304 | tf_op jit(solution)/shard_map/pallas_call | solution.py:46
  245.7 2.8 shard_map.112
  248.5 8.2 %collective-permute-done.7.refs_0_ = bf16[768,512]{1,0:T(8,128)(2,1)} collective-permute-done((bf16[768,512]{1,0:T(8,128)(2,1)}, bf16[768,512]{1,0:T(8,128)(2,1)}, u32[]{:S(2)}, u32[]{:S(2)}) %collective-permute-start.7) | collective-permute-done | bytes 786464 | tf_op jit(solution)/shard_map/ppermute | solution.py:291
  258.2 3.7 %shard_map.109 = bf16[768,512]{1,0:T(8,128)(2,1)} custom-call(s32[8]{0:T(128)S(1)} %gather_fusion, bf16[768,1024]{1,0:T(8,128)(2,1)S(1)} %bitcast.21, bf16[1024,8192]{1,0:T(8,128)(2,1)} %w_ref.29, bf16[768,512]{1,0:T(8,128)(2,1)} %collective-permute-done.7.refs_0_), custom_call_target="tpu_custom_call" | custom-call | flops 805306368 | bytes 4194304 | tf_op jit(solution)/shard_map/pallas_call | solution.py:46
  262.0 11.1 %collective-permute-done.18.refs_0_ = bf16[768,512]{1,0:T(8,128)(2,1)} collective-permute-done((bf16[768,512]{1,0:T(8,128)(2,1)}, bf16[768,512]{1,0:T(8,128)(2,1)}, u32[]{:S(2)}, u32[]{:S(2)}) %collective-permute-start.18) | collective-permute-done | bytes 786464 | tf_op jit(solution)/shard_map/ppermute | solution.py:291
  274.3 3.6 %shard_map.120 = bf16[768,512]{1,0:T(8,128)(2,1)} custom-call(s32[8]{0:T(128)S(1)} %gather_fusion, bf16[768,1024]{1,0:T(8,128)(2,1)S(1)} %bitcast.22, bf16[1024,8192]{1,0:T(8,128)(2,1)} %w_ref.29, bf16[768,512]{1,0:T(8,128)(2,1)} %collective-permute-done.18.refs_0_), custom_call_target="tpu_custom_call" | custom-call | flops 805306368 | bytes 4194304 | tf_op jit(solution)/shard_map/pallas_call | solution.py:46
  278.3 3.7 %shard_map.117 = bf16[768,512]{1,0:T(8,128)(2,1)} custom-call(s32[8]{0:T(128)S(1)} %gather_fusion, bf16[768,1024]{1,0:T(8,128)(2,1)S(1)} %bitcast.23, bf16[1024,8192]{1,0:T(8,128)(2,1)} %w_ref.29, bf16[768,512]{1,0:T(8,128)(2,1)} %collective-permute-done.15.refs_0_), custom_call_target="tpu_custom_call" | custom-call | flops 805306368 | bytes 4194304 | tf_op jit(solution)/shard_map/pallas_call | solution.py:46
  285.2 4.0 %shard_map.104 = f32[3,128,128]{2,1,0:T(8,128)S(1)} custom-call(s32[24]{0:T(128)S(1)} %compare_convert_fusion.local, s32[24]{0:T(128)S(1)} %and_select_fusion.1.index, bf16[768,1024]{1,0:T(8,128)(2,1)S(1)} %bitcast.24, s32[768,1]{1,0:T(8,128)S(1)} %bitcast.28, bf16[96,64,1024]{2,1,0:T(8,128)(2,1)} %table_ref.5, ...), custom_call_target="tpu_custom_call" | custom-call | flops 402653184 | bytes 4718592 | tf_op jit(solution)/shard_map/pallas_call | solution.py:138
  290.9 2.8 shard_map.113
  295.5 2.9 shard_map.110
  298.4 15.1 %collective-permute-done.2 = f32[3,128,128]{2,1,0:T(8,128)S(1)} collective-permute-done((f32[3,128,128]{2,1,0:T(8,128)S(1)}, f32[3,128,128]{2,1,0:T(8,128)S(1)}, u32[]{:S(2)}, u32[]{:S(2)}) %collective-permute-start.2) | collective-permute-done | bytes 196640 | tf_op jit(solution)/shard_map/ppermute | solution.py:232
  315.4 19.5 %collective-permute-done.3 = f32[3,128,128]{2,1,0:T(8,128)S(1)} collective-permute-done((f32[3,128,128]{2,1,0:T(8,128)S(1)}, f32[3,128,128]{2,1,0:T(8,128)S(1)}, u32[]{:S(2)}, u32[]{:S(2)}) %collective-permute-start.3) | collective-permute-done | bytes 196640 | tf_op jit(solution)/shard_map/ppermute | solution.py:232
  335.2 8.8 %collective-permute-done.4 = f32[3,128,128]{2,1,0:T(8,128)S(1)} collective-permute-done((f32[3,128,128]{2,1,0:T(8,128)S(1)}, f32[3,128,128]{2,1,0:T(8,128)S(1)}, u32[]{:S(2)}, u32[]{:S(2)}) %collective-permute-start.4) | collective-permute-done | bytes 196640 | tf_op jit(solution)/shard_map/ppermute | solution.py:232
  344.0 7.1 %shard_map.106 = f32[768,1024]{1,0:T(8,128)S(1)} custom-call(s32[8]{0:T(128)S(1)} %gather_fusion, s32[24]{0:T(128)S(1)} %compare_convert_fusion.local, s32[24]{0:T(128)S(1)} %and_select_fusion.1.index, bf16[768,1024]{1,0:T(8,128)(2,1)S(1)} %bitcast.27, bf16[1024,8192]{1,0:T(8,128)(2,1)} %w_ref.29, s32[768,1]{1,0:T(8,128)S(1)} %bitcast.29, ...), custom_call_target="tpu_custom_call" | custom-call | flops 2013265920 | bytes 9961472 | tf_op jit(solution)/shard_map/pallas_call | solution.py:198
  (71 shorter events, 29.7 us)
Async XLA Ops:
  0.8 1.7 collective-permute-start
  3.2 98.0 %copy-start.2 = (s32[8]{0:T(128)S(1)}, s32[8]{0:T(128)}, u32[]{:S(2)}) copy-start(s32[8]{0:T(128)} %constant.58.clone) | copy-start | bytes 100
  3.2 98.6 %copy-start.1 = (bf16[3,256,1024]{2,1,0:T(8,128)(2,1)S(1)}, bf16[3,256,1024]{2,1,0:T(8,128)(2,1)}, u32[]{:S(2)}) copy-start(bf16[3,256,1024]{2,1,0:T(8,128)(2,1)} %param.10) | copy-start | bytes 4718596
  100.4 181.6 %collective-permute-start.1 = (bf16[24,64,1024]{2,1,0:T(8,128)(2,1)}, bf16[24,64,1024]{2,1,0:T(8,128)(2,1)}, u32[]{:S(2)}, u32[]{:S(2)}) collective-permute-start(bf16[24,64,1024]{2,1,0:T(8,128)(2,1)} %shard_map.103), channel_id=1, source_target_pairs={{0,8},{8,0},{1,9},{9,1},{2,10},{10,2},{3,11},{11,3},{4,12},{12,4},... | collective-permute-start | bytes 9437192 | tf_op jit(solution)/shard_map/ppermute | solution.py:272
  104.7 20.8 %collective-permute-start.13 = (bf16[768,512]{1,0:T(8,128)(2,1)S(1)}, bf16[768,512]{1,0:T(8,128)(2,1)S(1)}, u32[]{:S(2)}, u32[]{:S(2)}) collective-permute-start(bf16[768,512]{1,0:T(8,128)(2,1)S(1)} %shard_map.114), channel_id=1, source_target_pairs={{0,1},{2,0},{4,2},{6,4},{7,6},{5,7},{3,5},{1,3},{8,9},{10,8},{12,1... | collective-permute-start | bytes 2359304 | tf_op jit(solution)/shard_map/ppermute | solution.py:291
  110.5 121.8 %collective-permute-start.6 = (bf16[768,512]{1,0:T(8,128)(2,1)S(1)}, bf16[768,512]{1,0:T(8,128)(2,1)S(1)}, u32[]{:S(2)}, u32[]{:S(2)}) collective-permute-start(bf16[768,512]{1,0:T(8,128)(2,1)S(1)} %shard_map.107), channel_id=1, source_target_pairs={{0,2},{2,4},{4,6},{6,7},{7,5},{5,3},{3,1},{1,0},{8,10},{10,12},{12... | collective-permute-start | bytes 2359304 | tf_op jit(solution)/shard_map/ppermute | solution.py:291
  113.4 122.6 %collective-permute-start.17 = (bf16[768,512]{1,0:T(8,128)(2,1)S(1)}, bf16[768,512]{1,0:T(8,128)(2,1)S(1)}, u32[]{:S(2)}, u32[]{:S(2)}) collective-permute-start(bf16[768,512]{1,0:T(8,128)(2,1)S(1)} %shard_map.118), channel_id=1, source_target_pairs={{0,2},{2,4},{4,6},{6,7},{7,5},{5,3},{3,1},{1,0},{8,10},{10,12},{12... | collective-permute-start | bytes 2359304 | tf_op jit(solution)/shard_map/ppermute | solution.py:291
  128.3 111.7 %collective-permute-start.14 = (bf16[768,512]{1,0:T(8,128)(2,1)S(1)}, bf16[768,512]{1,0:T(8,128)(2,1)S(1)}, u32[]{:S(2)}, u32[]{:S(2)}) collective-permute-start(bf16[768,512]{1,0:T(8,128)(2,1)S(1)} %shard_map.115), channel_id=1, source_target_pairs={{0,1},{2,0},{4,2},{6,4},{7,6},{5,7},{3,5},{1,3},{8,9},{10,8},{12,1... | collective-permute-start | bytes 2359304 | tf_op jit(solution)/shard_map/ppermute | solution.py:291
  133.6 110.4 %collective-permute-start.10 = (bf16[768,512]{1,0:T(8,128)(2,1)}, bf16[768,512]{1,0:T(8,128)(2,1)S(1)}, u32[]{:S(2)}, u32[]{:S(2)}) collective-permute-start(bf16[768,512]{1,0:T(8,128)(2,1)} %shard_map.111), channel_id=1, source_target_pairs={{0,1},{2,0},{4,2},{6,4},{7,6},{5,7},{3,5},{1,3},{8,9},{10,8},{12,1... | collective-permute-start | bytes 2359304 | tf_op jit(solution)/shard_map/ppermute | solution.py:291
  232.3 111.7 %collective-permute-start.5 = (bf16[24,64,1024]{2,1,0:T(8,128)(2,1)}, bf16[24,64,1024]{2,1,0:T(8,128)(2,1)}, u32[]{:S(2)}, u32[]{:S(2)}) collective-permute-start(bf16[24,64,1024]{2,1,0:T(8,128)(2,1)} %shard_map.105), channel_id=1, source_target_pairs={{0,8},{8,0},{1,9},{9,1},{2,10},{10,2},{3,11},{11,3},{4,12},{12,4},... | collective-permute-start | bytes 9437192 | tf_op jit(solution)/shard_map/ppermute | solution.py:273
  236.0 20.7 %collective-permute-start.7 = (bf16[768,512]{1,0:T(8,128)(2,1)}, bf16[768,512]{1,0:T(8,128)(2,1)}, u32[]{:S(2)}, u32[]{:S(2)}) collective-permute-start(bf16[768,512]{1,0:T(8,128)(2,1)} %shard_map.108), channel_id=1, source_target_pairs={{0,2},{2,4},{4,6},{6,7},{7,5},{5,3},{3,1},{1,0},{8,10},{10,12},{12... | collective-permute-start | bytes 2359304 | tf_op jit(solution)/shard_map/ppermute | solution.py:291
  240.0 33.1 %collective-permute-start.18 = (bf16[768,512]{1,0:T(8,128)(2,1)}, bf16[768,512]{1,0:T(8,128)(2,1)}, u32[]{:S(2)}, u32[]{:S(2)}) collective-permute-start(bf16[768,512]{1,0:T(8,128)(2,1)} %shard_map.119), channel_id=1, source_target_pairs={{0,2},{2,4},{4,6},{6,7},{7,5},{5,3},{3,1},{1,0},{8,10},{10,12},{12... | collective-permute-start | bytes 2359304 | tf_op jit(solution)/shard_map/ppermute | solution.py:291
  244.0 34.0 %collective-permute-start.15 = (bf16[768,512]{1,0:T(8,128)(2,1)}, bf16[768,512]{1,0:T(8,128)(2,1)}, u32[]{:S(2)}, u32[]{:S(2)}) collective-permute-start(bf16[768,512]{1,0:T(8,128)(2,1)} %shard_map.116), channel_id=1, source_target_pairs={{0,1},{2,0},{4,2},{6,4},{7,6},{5,7},{3,5},{1,3},{8,9},{10,8},{12,1... | collective-permute-start | bytes 2359304 | tf_op jit(solution)/shard_map/ppermute | solution.py:291
  256.7 32.5 %collective-permute-start.11 = (bf16[768,512]{1,0:T(8,128)(2,1)S(1)}, bf16[768,512]{1,0:T(8,128)(2,1)S(1)}, u32[]{:S(2)}, u32[]{:S(2)}) collective-permute-start(bf16[768,512]{1,0:T(8,128)(2,1)S(1)} %shard_map.112), channel_id=1, source_target_pairs={{0,1},{2,0},{4,2},{6,4},{7,6},{5,7},{3,5},{1,3},{8,9},{10,8},{12,1... | collective-permute-start | bytes 2359304 | tf_op jit(solution)/shard_map/ppermute | solution.py:291
  273.1 20.8 %collective-permute-start.8 = (bf16[768,512]{1,0:T(8,128)(2,1)}, bf16[768,512]{1,0:T(8,128)(2,1)}, u32[]{:S(2)}, u32[]{:S(2)}) collective-permute-start(bf16[768,512]{1,0:T(8,128)(2,1)} %shard_map.109), channel_id=1, source_target_pairs={{0,2},{2,4},{4,6},{6,7},{7,5},{5,3},{3,1},{1,0},{8,10},{10,12},{12... | collective-permute-start | bytes 2359304 | tf_op jit(solution)/shard_map/ppermute | solution.py:291
  277.9 5.8 %copy-start.4 = (s32[3,256]{1,0:T(4,128)S(1)}, s32[3,256]{1,0:T(4,128)}, u32[]{:S(2)}) copy-start(s32[3,256]{1,0:T(4,128)} %param.16) | copy-start | bytes 9220
  277.9 35.7 %collective-permute-start.19 = (bf16[768,512]{1,0:T(8,128)(2,1)}, bf16[768,512]{1,0:T(8,128)(2,1)}, u32[]{:S(2)}, u32[]{:S(2)}) collective-permute-start(bf16[768,512]{1,0:T(8,128)(2,1)} %shard_map.120), channel_id=1, source_target_pairs={{0,2},{2,4},{4,6},{6,7},{7,5},{5,3},{3,1},{1,0},{8,10},{10,12},{12... | collective-permute-start | bytes 2359304 | tf_op jit(solution)/shard_map/ppermute | solution.py:291
  282.0 31.7 %collective-permute-start.16 = (bf16[768,512]{1,0:T(8,128)(2,1)}, bf16[768,512]{1,0:T(8,128)(2,1)}, u32[]{:S(2)}, u32[]{:S(2)}) collective-permute-start(bf16[768,512]{1,0:T(8,128)(2,1)} %shard_map.117), channel_id=1, source_target_pairs={{0,1},{2,0},{4,2},{6,4},{7,6},{5,7},{3,5},{1,3},{8,9},{10,8},{12,1... | collective-permute-start | bytes 2359304 | tf_op jit(solution)/shard_map/ppermute | solution.py:291
  289.2 24.3 %collective-permute-start.2 = (f32[3,128,128]{2,1,0:T(8,128)S(1)}, f32[3,128,128]{2,1,0:T(8,128)S(1)}, u32[]{:S(2)}, u32[]{:S(2)}) collective-permute-start(f32[3,128,128]{2,1,0:T(8,128)S(1)} %shard_map.104), channel_id=1, source_target_pairs={{0,1},{1,0},{2,3},{3,2},{4,5},{5,4},{6,7},{7,6},{8,9},{9,8},{10,11... | collective-permute-start | bytes 589832 | tf_op jit(solution)/shard_map/ppermute | solution.py:232
  293.7 19.9 %copy-start.5 = (s32[3,1]{0,1:T(1,128)S(1)}, s32[3,1]{0,1:T(1,128)}, u32[]{:S(2)}) copy-start(s32[3,1]{0,1:T(1,128)} %param.17) | copy-start | bytes 40
  293.9 41.1 %collective-permute-start.12 = (bf16[768,512]{1,0:T(8,128)(2,1)S(1)}, bf16[768,512]{1,0:T(8,128)(2,1)S(1)}, u32[]{:S(2)}, u32[]{:S(2)}) collective-permute-start(bf16[768,512]{1,0:T(8,128)(2,1)S(1)} %shard_map.113), channel_id=1, source_target_pairs={{0,1},{2,0},{4,2},{6,4},{7,6},{5,7},{3,5},{1,3},{8,9},{10,8},{12,1... | collective-permute-start | bytes 2359304 | tf_op jit(solution)/shard_map/ppermute | solution.py:291
  313.5 21.4 %collective-permute-start.9 = (bf16[768,512]{1,0:T(8,128)(2,1)S(1)}, bf16[768,512]{1,0:T(8,128)(2,1)S(1)}, u32[]{:S(2)}, u32[]{:S(2)}) collective-permute-start(bf16[768,512]{1,0:T(8,128)(2,1)S(1)} %shard_map.110), channel_id=1, source_target_pairs={{0,2},{2,4},{4,6},{6,7},{7,5},{5,3},{3,1},{1,0},{8,10},{10,12},{12... | collective-permute-start | bytes 2359304 | tf_op jit(solution)/shard_map/ppermute | solution.py:291
  313.7 21.2 %collective-permute-start.3 = (f32[3,128,128]{2,1,0:T(8,128)S(1)}, f32[3,128,128]{2,1,0:T(8,128)S(1)}, u32[]{:S(2)}, u32[]{:S(2)}) collective-permute-start(f32[3,128,128]{2,1,0:T(8,128)S(1)} %add.90), channel_id=1, source_target_pairs={{0,2},{1,3},{2,0},{3,1},{4,6},{5,7},{6,4},{7,5},{8,10},{9,11},{10,... | collective-permute-start | bytes 589832 | tf_op jit(solution)/shard_map/ppermute | solution.py:232
  334.9 9.1 %collective-permute-start.4 = (f32[3,128,128]{2,1,0:T(8,128)S(1)}, f32[3,128,128]{2,1,0:T(8,128)S(1)}, u32[]{:S(2)}, u32[]{:S(2)}) collective-permute-start(f32[3,128,128]{2,1,0:T(8,128)S(1)} %add.91), channel_id=1, source_target_pairs={{0,4},{1,5},{2,6},{3,7},{4,0},{5,1},{6,2},{7,3},{8,12},{9,13},{10,... | collective-permute-start | bytes 589832 | tf_op jit(solution)/shard_map/ppermute | solution.py:232
  (2 other events, 6.8 us)

commit v2 on v1

--- a/solution.py
+++ b/solution.py
@@ -81,7 +81,7 @@
             num_scalar_prefetch=1,
             grid=(1,),
             in_specs=[pl.BlockSpec(memory_space=pl.ANY)],
-            out_specs=pl.BlockSpec(memory_space=pl.ANY),
+            out_specs=pl.BlockSpec(memory_space=pltpu.VMEM),
             scratch_shapes=[pltpu.SemaphoreType.DMA((count,))],
         ),
         out_shape=jax.ShapeDtypeStruct(shape, table.dtype),

time: 354 us -> 168 us (0.47)
  Pallas kernels: 250 us -> 64.7 us
  waiting for transfers between devices: 73 us -> 68.9 us
  starting transfers between devices: 19.1 us -> 22.8 us
    pallas_call x2, Pallas kernels: 194 us -> 8.63 us  [collect(): pl.pallas_call(functools.partial(collect_kernel, count), grid_spec=pltpu....]
    ppermute x3, waiting for transfers between devices: 43.4 us -> 35.5 us  [sum_over(): lax.ppermute(value, axis, [(i, i ^ apart) for i in range(size)])]
    ppermute x14, waiting for transfers between devices: 29.5 us -> 33.4 us  [per_device(): arrived[chain] = lax.ppermute(partial, 'tp', moves)]
  transfers between devices with their start and end apart: 20 -> 20, of which waited for: 7 -> 8; matrix products, arithmetic and copies ran while one was open for 2% -> 4% of each run, Pallas kernels for 41% -> 32%
where the time goes in v2:
time: 168 us; the launch traced here: 167 us
  waiting for transfers between devices  68.9 us (41%)
  Pallas kernels  64.7 us (39%)
  starting transfers between devices  22.8 us (14%)
  local copies, waits for them, and re-layouts  5.64 us (3%)
  other arithmetic  4.98 us (3%)
    pallas_call x14, Pallas kernels, hop(): pl.pallas_call(functools.partial(hop_kernel, received is not None), grid_...  45 us
    ppermute x3, waiting for transfers between devices, sum_over(): lax.ppermute(value, axis, [(i, i ^ apart) for i in range(size)])  35.5 us
    ppermute x14, waiting for transfers between devices, per_device(): arrived[chain] = lax.ppermute(partial, 'tp', moves)  33.4 us
    ppermute x14, starting transfers between devices, per_device(): arrived[chain] = lax.ppermute(partial, 'tp', moves)  17.1 us
    pallas_call x2, Pallas kernels, collect(): pl.pallas_call(functools.partial(collect_kernel, count), grid_spec=pltpu....  8.63 us
    pallas_call x1, Pallas kernels, own_terms(): pl.pallas_call(functools.partial(own_kernel, sizes), grid_spec=pltpu.Pref...  7.05 us
    ppermute x3, starting transfers between devices, sum_over(): lax.ppermute(value, axis, [(i, i ^ apart) for i in range(size)])  5.03 us
    pallas_call x1, Pallas kernels, low_rank(): pl.pallas_call(functools.partial(low_kernel, sizes), grid_spec=pltpu.Pref...  4.02 us
  transfers between devices with their start and end apart: 20, of which 8 were waited for; matrix products, arithmetic and copies ran while one was open for 4% of the time, Pallas kernels for 32%

profile of v2, /device:TPU:0, one launch (start us, length us, event | category | flops | bytes accessed | tf_op | source)
XLA Modules:
  0.0 167.3 jit_solution(13417695978996605833)
XLA Ops:
  3.2 4.3 %shard_map.103 = bf16[24,64,1024]{2,1,0:T(8,128)(2,1)} custom-call(s32[24]{0:T(128)S(1)} %and_select_fusion.index, bf16[96,64,1024]{2,1,0:T(8,128)(2,1)} %table_ref.5), custom_call_target="tpu_custom_call" | custom-call | bytes 6291456 | tf_op jit(solution)/shard_map/pallas_call | solution.py:78
  11.9 3.0 %collective-permute-start.13 = (bf16[768,512]{1,0:T(8,128)(2,1)S(1)}, bf16[768,512]{1,0:T(8,128)(2,1)S(1)}, u32[]{:S(2)}, u32[]{:S(2)}) collective-permute-start(bf16[768,512]{1,0:T(8,128)(2,1)S(1)} %shard_map.114), channel_id=1, source_target_pairs={{0,1},{2,0},{4,2},{6,4},{7,6},{5,7},{3,5},{1,3},{8,9},{10,8},{12,1... | collective-permute-start | bytes 2359304 | tf_op jit(solution)/shard_map/ppermute | solution.py:291
  22.7 10.0 %collective-permute-done.13.refs_0_ = bf16[768,512]{1,0:T(8,128)(2,1)S(1)} collective-permute-done((bf16[768,512]{1,0:T(8,128)(2,1)S(1)}, bf16[768,512]{1,0:T(8,128)(2,1)S(1)}, u32[]{:S(2)}, u32[]{:S(2)}) %collective-permute-start.13) | collective-permute-done | bytes 786464 | tf_op jit(solution)/shard_map/ppermute | solution.py:291
  37.2 3.5 %shard_map.111 = bf16[768,512]{1,0:T(8,128)(2,1)} custom-call(s32[8]{0:T(128)S(1)} %gather_fusion, bf16[768,1024]{1,0:T(8,128)(2,1)S(1)} %bitcast.16, bf16[1024,8192]{1,0:T(8,128)(2,1)} %w_ref.29), custom_call_target="tpu_custom_call" | custom-call | flops 805306368 | bytes 4194304 | tf_op jit(solution)/shard_map/pallas_call | solution.py:46
  42.3 4.3 %shard_map.105 = bf16[24,64,1024]{2,1,0:T(8,128)(2,1)} custom-call(s32[24]{0:T(128)S(1)} %and_select_fusion.index, bf16[96,64,1024]{2,1,0:T(8,128)(2,1)} %table_ref.7), custom_call_target="tpu_custom_call" | custom-call | bytes 6291456 | tf_op jit(solution)/shard_map/pallas_call | solution.py:78
  46.7 3.6 %shard_map.108 = bf16[768,512]{1,0:T(8,128)(2,1)} custom-call(s32[8]{0:T(128)S(1)} %gather_fusion, bf16[768,1024]{1,0:T(8,128)(2,1)S(1)} %bitcast.17, bf16[1024,8192]{1,0:T(8,128)(2,1)} %w_ref.29, bf16[768,512]{1,0:T(8,128)(2,1)S(1)} %collective-permute-done.6.refs_0_), custom_call_target="tpu_custom_call" | custom-call | flops 805306368 | bytes 4194304 | tf_op jit(solution)/shard_map/pallas_call | solution.py:46
  50.3 3.4 %collective-permute-done.17.refs_0_ = bf16[768,512]{1,0:T(8,128)(2,1)S(1)} collective-permute-done((bf16[768,512]{1,0:T(8,128)(2,1)S(1)}, bf16[768,512]{1,0:T(8,128)(2,1)S(1)}, u32[]{:S(2)}, u32[]{:S(2)}) %collective-permute-start.17) | collective-permute-done | bytes 786464 | tf_op jit(solution)/shard_map/ppermute | solution.py:291
  54.1 3.5 %shard_map.119 = bf16[768,512]{1,0:T(8,128)(2,1)} custom-call(s32[8]{0:T(128)S(1)} %gather_fusion, bf16[768,1024]{1,0:T(8,128)(2,1)S(1)} %bitcast.18, bf16[1024,8192]{1,0:T(8,128)(2,1)} %w_ref.29, bf16[768,512]{1,0:T(8,128)(2,1)S(1)} %collective-permute-done.17.refs_0_), custom_call_target="tpu_custom_call" | custom-call | flops 805306368 | bytes 4194304 | tf_op jit(solution)/shard_map/pallas_call | solution.py:46
  59.5 3.6 %shard_map.116 = bf16[768,512]{1,0:T(8,128)(2,1)} custom-call(s32[8]{0:T(128)S(1)} %gather_fusion, bf16[768,1024]{1,0:T(8,128)(2,1)S(1)} %bitcast.19, bf16[1024,8192]{1,0:T(8,128)(2,1)} %w_ref.29, bf16[768,512]{1,0:T(8,128)(2,1)S(1)} %collective-permute-done.14.refs_0_), custom_call_target="tpu_custom_call" | custom-call | flops 805306368 | bytes 4194304 | tf_op jit(solution)/shard_map/pallas_call | solution.py:46
  63.0 8.3 %collective-permute-done.10.refs_0_ = bf16[768,512]{1,0:T(8,128)(2,1)S(1)} collective-permute-done((bf16[768,512]{1,0:T(8,128)(2,1)}, bf16[768,512]{1,0:T(8,128)(2,1)S(1)}, u32[]{:S(2)}, u32[]{:S(2)}) %collective-permute-start.10) | collective-permute-done | bytes 786464 | tf_op jit(solution)/shard_map/ppermute | solution.py:291
  72.7 2.8 %shard_map.112 = bf16[768,512]{1,0:T(8,128)(2,1)S(1)} custom-call(s32[8]{0:T(128)S(1)} %gather_fusion, bf16[768,1024]{1,0:T(8,128)(2,1)S(1)} %bitcast.20, bf16[1024,8192]{1,0:T(8,128)(2,1)} %w_ref.29, bf16[768,512]{1,0:T(8,128)(2,1)S(1)} %collective-permute-done.10.refs_0_), custom_call_target="tpu_custom_call" | custom-call | flops 805306368 | bytes 4194304 | tf_op jit(solution)/shard_map/pallas_call | solution.py:46
  77.1 3.7 %shard_map.109 = bf16[768,512]{1,0:T(8,128)(2,1)} custom-call(s32[8]{0:T(128)S(1)} %gather_fusion, bf16[768,1024]{1,0:T(8,128)(2,1)S(1)} %bitcast.21, bf16[1024,8192]{1,0:T(8,128)(2,1)} %w_ref.29, bf16[768,512]{1,0:T(8,128)(2,1)} %collective-permute-done.7.refs_0_), custom_call_target="tpu_custom_call" | custom-call | flops 805306368 | bytes 4194304 | tf_op jit(solution)/shard_map/pallas_call | solution.py:46
  80.9 8.3 %collective-permute-done.18.refs_0_ = bf16[768,512]{1,0:T(8,128)(2,1)} collective-permute-done((bf16[768,512]{1,0:T(8,128)(2,1)}, bf16[768,512]{1,0:T(8,128)(2,1)}, u32[]{:S(2)}, u32[]{:S(2)}) %collective-permute-start.18) | collective-permute-done | bytes 786464 | tf_op jit(solution)/shard_map/ppermute | solution.py:291
  90.6 3.6 %shard_map.120 = bf16[768,512]{1,0:T(8,128)(2,1)} custom-call(s32[8]{0:T(128)S(1)} %gather_fusion, bf16[768,1024]{1,0:T(8,128)(2,1)S(1)} %bitcast.22, bf16[1024,8192]{1,0:T(8,128)(2,1)} %w_ref.29, bf16[768,512]{1,0:T(8,128)(2,1)} %collective-permute-done.18.refs_0_), custom_call_target="tpu_custom_call" | custom-call | flops 805306368 | bytes 4194304 | tf_op jit(solution)/shard_map/pallas_call | solution.py:46
  95.7 3.7 %shard_map.117 = bf16[768,512]{1,0:T(8,128)(2,1)} custom-call(s32[8]{0:T(128)S(1)} %gather_fusion, bf16[768,1024]{1,0:T(8,128)(2,1)S(1)} %bitcast.23, bf16[1024,8192]{1,0:T(8,128)(2,1)} %w_ref.29, bf16[768,512]{1,0:T(8,128)(2,1)} %collective-permute-done.15.refs_0_), custom_call_target="tpu_custom_call" | custom-call | flops 805306368 | bytes 4194304 | tf_op jit(solution)/shard_map/pallas_call | solution.py:46
  101.5 4.0 %shard_map.104 = f32[3,128,128]{2,1,0:T(8,128)S(1)} custom-call(s32[24]{0:T(128)S(1)} %compare_convert_fusion.local, s32[24]{0:T(128)S(1)} %and_select_fusion.1.index, bf16[768,1024]{1,0:T(8,128)(2,1)S(1)} %bitcast.24, s32[768,1]{1,0:T(8,128)S(1)} %bitcast.28, bf16[96,64,1024]{2,1,0:T(8,128)(2,1)} %table_ref.5, ...), custom_call_target="tpu_custom_call" | custom-call | flops 402653184 | bytes 4718592 | tf_op jit(solution)/shard_map/pallas_call | solution.py:138
  105.6 3.3 %collective-permute-done.11.refs_0_ = bf16[768,512]{1,0:T(8,128)(2,1)S(1)} collective-permute-done((bf16[768,512]{1,0:T(8,128)(2,1)S(1)}, bf16[768,512]{1,0:T(8,128)(2,1)S(1)}, u32[]{:S(2)}, u32[]{:S(2)}) %collective-permute-start.11) | collective-permute-done | bytes 786464 | tf_op jit(solution)/shard_map/ppermute | solution.py:291
  110.2 2.8 %shard_map.113 = bf16[768,512]{1,0:T(8,128)(2,1)S(1)} custom-call(s32[8]{0:T(128)S(1)} %gather_fusion, bf16[768,1024]{1,0:T(8,128)(2,1)S(1)} %bitcast.25, bf16[1024,8192]{1,0:T(8,128)(2,1)} %w_ref.29, bf16[768,512]{1,0:T(8,128)(2,1)S(1)} %collective-permute-done.11.refs_0_), custom_call_target="tpu_custom_call" | custom-call | flops 805306368 | bytes 4194304 | tf_op jit(solution)/shard_map/pallas_call | solution.py:46
  113.8 2.9 %shard_map.110 = bf16[768,512]{1,0:T(8,128)(2,1)S(1)} custom-call(s32[8]{0:T(128)S(1)} %gather_fusion, bf16[768,1024]{1,0:T(8,128)(2,1)S(1)} %bitcast.26, bf16[1024,8192]{1,0:T(8,128)(2,1)} %w_ref.29, bf16[768,512]{1,0:T(8,128)(2,1)} %collective-permute-done.8.refs_0_), custom_call_target="tpu_custom_call" | custom-call | flops 805306368 | bytes 4194304 | tf_op jit(solution)/shard_map/pallas_call | solution.py:46
  116.7 12.1 %collective-permute-done.2 = f32[3,128,128]{2,1,0:T(8,128)S(1)} collective-permute-done((f32[3,128,128]{2,1,0:T(8,128)S(1)}, f32[3,128,128]{2,1,0:T(8,128)S(1)}, u32[]{:S(2)}, u32[]{:S(2)}) %collective-permute-start.2) | collective-permute-done | bytes 196640 | tf_op jit(solution)/shard_map/ppermute | solution.py:232
  130.6 17.9 %collective-permute-done.3 = f32[3,128,128]{2,1,0:T(8,128)S(1)} collective-permute-done((f32[3,128,128]{2,1,0:T(8,128)S(1)}, f32[3,128,128]{2,1,0:T(8,128)S(1)}, u32[]{:S(2)}, u32[]{:S(2)}) %collective-permute-start.3) | collective-permute-done | bytes 196640 | tf_op jit(solution)/shard_map/ppermute | solution.py:232
  148.6 3.6 %collective-permute-start.4 = (f32[3,128,128]{2,1,0:T(8,128)S(1)}, f32[3,128,128]{2,1,0:T(8,128)S(1)}, u32[]{:S(2)}, u32[]{:S(2)}) collective-permute-start(f32[3,128,128]{2,1,0:T(8,128)S(1)} %add.91), channel_id=1, source_target_pairs={{0,4},{1,5},{2,6},{3,7},{4,0},{5,1},{6,2},{7,3},{8,12},{9,13},{10,... | collective-permute-start | bytes 589832 | tf_op jit(solution)/shard_map/ppermute | solution.py:232
  152.4 5.5 %collective-permute-done.4 = f32[3,128,128]{2,1,0:T(8,128)S(1)} collective-permute-done((f32[3,128,128]{2,1,0:T(8,128)S(1)}, f32[3,128,128]{2,1,0:T(8,128)S(1)}, u32[]{:S(2)}, u32[]{:S(2)}) %collective-permute-start.4) | collective-permute-done | bytes 196640 | tf_op jit(solution)/shard_map/ppermute | solution.py:232
  158.0 7.1 %shard_map.106 = f32[768,1024]{1,0:T(8,128)S(1)} custom-call(s32[8]{0:T(128)S(1)} %gather_fusion, s32[24]{0:T(128)S(1)} %compare_convert_fusion.local, s32[24]{0:T(128)S(1)} %and_select_fusion.1.index, bf16[768,1024]{1,0:T(8,128)(2,1)S(1)} %bitcast.27, bf16[1024,8192]{1,0:T(8,128)(2,1)} %w_ref.29, s32[768,1]{1,0:T(8,128)S(1)} %bitcast.29, ...), custom_call_target="tpu_custom_call" | custom-call | flops 2013265920 | bytes 9961472 | tf_op jit(solution)/shard_map/pallas_call | solution.py:198
  (71 shorter events, 38.0 us)
Async XLA Ops:
  0.8 1.7 %collective-permute-start = (s32[24]{0:T(128)S(1)}, s32[24]{0:T(128)S(1)}, u32[]{:S(2)}, u32[]{:S(2)}) collective-permute-start(s32[24]{0:T(128)S(1)} %reshape.116), channel_id=1, source_target_pairs={{0,8},{8,0},{1,9},{9,1},{2,10},{10,2},{3,11},{11,3},{4,12},{12,4},... | collective-permute-start | bytes 296 | tf_op jit(solution)/shard_map/ppermute | solution.py:267
  3.2 5.8 %copy-start.1 = (bf16[3,256,1024]{2,1,0:T(8,128)(2,1)S(1)}, bf16[3,256,1024]{2,1,0:T(8,128)(2,1)}, u32[]{:S(2)}) copy-start(bf16[3,256,1024]{2,1,0:T(8,128)(2,1)} %param.10) | copy-start | bytes 4718596
  7.6 91.8 %collective-permute-start.1 = (bf16[24,64,1024]{2,1,0:T(8,128)(2,1)}, bf16[24,64,1024]{2,1,0:T(8,128)(2,1)}, u32[]{:S(2)}, u32[]{:S(2)}) collective-permute-start(bf16[24,64,1024]{2,1,0:T(8,128)(2,1)} %shard_map.103), channel_id=1, source_target_pairs={{0,8},{8,0},{1,9},{9,1},{2,10},{10,2},{3,11},{11,3},{4,12},{12,4},... | collective-permute-start | bytes 9437192 | tf_op jit(solution)/shard_map/ppermute | solution.py:272
  11.9 20.8 %collective-permute-start.13 = (bf16[768,512]{1,0:T(8,128)(2,1)S(1)}, bf16[768,512]{1,0:T(8,128)(2,1)S(1)}, u32[]{:S(2)}, u32[]{:S(2)}) collective-permute-start(bf16[768,512]{1,0:T(8,128)(2,1)S(1)} %shard_map.114), channel_id=1, source_target_pairs={{0,1},{2,0},{4,2},{6,4},{7,6},{5,7},{3,5},{1,3},{8,9},{10,8},{12,1... | collective-permute-start | bytes 2359304 | tf_op jit(solution)/shard_map/ppermute | solution.py:291
  17.7 29.0 %collective-permute-start.6 = (bf16[768,512]{1,0:T(8,128)(2,1)S(1)}, bf16[768,512]{1,0:T(8,128)(2,1)S(1)}, u32[]{:S(2)}, u32[]{:S(2)}) collective-permute-start(bf16[768,512]{1,0:T(8,128)(2,1)S(1)} %shard_map.107), channel_id=1, source_target_pairs={{0,2},{2,4},{4,6},{6,7},{7,5},{5,3},{3,1},{1,0},{8,10},{10,12},{12... | collective-permute-start | bytes 2359304 | tf_op jit(solution)/shard_map/ppermute | solution.py:291
  20.6 33.2 %collective-permute-start.17 = (bf16[768,512]{1,0:T(8,128)(2,1)S(1)}, bf16[768,512]{1,0:T(8,128)(2,1)S(1)}, u32[]{:S(2)}, u32[]{:S(2)}) collective-permute-start(bf16[768,512]{1,0:T(8,128)(2,1)S(1)} %shard_map.118), channel_id=1, source_target_pairs={{0,2},{2,4},{4,6},{6,7},{7,5},{5,3},{3,1},{1,0},{8,10},{10,12},{12... | collective-permute-start | bytes 2359304 | tf_op jit(solution)/shard_map/ppermute | solution.py:291
  35.5 22.2 %collective-permute-start.14 = (bf16[768,512]{1,0:T(8,128)(2,1)S(1)}, bf16[768,512]{1,0:T(8,128)(2,1)S(1)}, u32[]{:S(2)}, u32[]{:S(2)}) collective-permute-start(bf16[768,512]{1,0:T(8,128)(2,1)S(1)} %shard_map.115), channel_id=1, source_target_pairs={{0,1},{2,0},{4,2},{6,4},{7,6},{5,7},{3,5},{1,3},{8,9},{10,8},{12,1... | collective-permute-start | bytes 2359304 | tf_op jit(solution)/shard_map/ppermute | solution.py:291
  40.8 30.6 %collective-permute-start.10 = (bf16[768,512]{1,0:T(8,128)(2,1)}, bf16[768,512]{1,0:T(8,128)(2,1)S(1)}, u32[]{:S(2)}, u32[]{:S(2)}) collective-permute-start(bf16[768,512]{1,0:T(8,128)(2,1)} %shard_map.111), channel_id=1, source_target_pairs={{0,1},{2,0},{4,2},{6,4},{7,6},{5,7},{3,5},{1,3},{8,9},{10,8},{12,1... | collective-permute-start | bytes 2359304 | tf_op jit(solution)/shard_map/ppermute | solution.py:291
  46.6 111.3 %collective-permute-start.5 = (bf16[24,64,1024]{2,1,0:T(8,128)(2,1)}, bf16[24,64,1024]{2,1,0:T(8,128)(2,1)}, u32[]{:S(2)}, u32[]{:S(2)}) collective-permute-start(bf16[24,64,1024]{2,1,0:T(8,128)(2,1)} %shard_map.105), channel_id=1, source_target_pairs={{0,8},{8,0},{1,9},{9,1},{2,10},{10,2},{3,11},{11,3},{4,12},{12,4},... | collective-permute-start | bytes 9437192 | tf_op jit(solution)/shard_map/ppermute | solution.py:273
  50.3 9.0 %copy-start.3 = (s32[3,2,4]{2,1,0:T(2,128)S(1)}, s32[3,2,4]{2,1,0:T(2,128)}, u32[]{:S(2)}) copy-start(s32[3,2,4]{2,1,0:T(2,128)} %param.15) | copy-start | bytes 292
  53.8 21.7 %collective-permute-start.7 = (bf16[768,512]{1,0:T(8,128)(2,1)}, bf16[768,512]{1,0:T(8,128)(2,1)}, u32[]{:S(2)}, u32[]{:S(2)}) collective-permute-start(bf16[768,512]{1,0:T(8,128)(2,1)} %shard_map.108), channel_id=1, source_target_pairs={{0,2},{2,4},{4,6},{6,7},{7,5},{5,3},{3,1},{1,0},{8,10},{10,12},{12... | collective-permute-start | bytes 2359304 | tf_op jit(solution)/shard_map/ppermute | solution.py:291
  57.6 31.6 %collective-permute-start.18 = (bf16[768,512]{1,0:T(8,128)(2,1)}, bf16[768,512]{1,0:T(8,128)(2,1)}, u32[]{:S(2)}, u32[]{:S(2)}) collective-permute-start(bf16[768,512]{1,0:T(8,128)(2,1)} %shard_map.119), channel_id=1, source_target_pairs={{0,2},{2,4},{4,6},{6,7},{7,5},{5,3},{3,1},{1,0},{8,10},{10,12},{12... | collective-permute-start | bytes 2359304 | tf_op jit(solution)/shard_map/ppermute | solution.py:291
  71.3 23.0 %collective-permute-start.15 = (bf16[768,512]{1,0:T(8,128)(2,1)}, bf16[768,512]{1,0:T(8,128)(2,1)}, u32[]{:S(2)}, u32[]{:S(2)}) collective-permute-start(bf16[768,512]{1,0:T(8,128)(2,1)} %shard_map.116), channel_id=1, source_target_pairs={{0,1},{2,0},{4,2},{6,4},{7,6},{5,7},{3,5},{1,3},{8,9},{10,8},{12,1... | collective-permute-start | bytes 2359304 | tf_op jit(solution)/shard_map/ppermute | solution.py:291
  75.5 33.3 %collective-permute-start.11 = (bf16[768,512]{1,0:T(8,128)(2,1)S(1)}, bf16[768,512]{1,0:T(8,128)(2,1)S(1)}, u32[]{:S(2)}, u32[]{:S(2)}) collective-permute-start(bf16[768,512]{1,0:T(8,128)(2,1)S(1)} %shard_map.112), channel_id=1, source_target_pairs={{0,1},{2,0},{4,2},{6,4},{7,6},{5,7},{3,5},{1,3},{8,9},{10,8},{12,1... | collective-permute-start | bytes 2359304 | tf_op jit(solution)/shard_map/ppermute | solution.py:291
  89.2 23.8 %collective-permute-start.8 = (bf16[768,512]{1,0:T(8,128)(2,1)}, bf16[768,512]{1,0:T(8,128)(2,1)}, u32[]{:S(2)}, u32[]{:S(2)}) collective-permute-start(bf16[768,512]{1,0:T(8,128)(2,1)} %shard_map.109), channel_id=1, source_target_pairs={{0,2},{2,4},{4,6},{6,7},{7,5},{5,3},{3,1},{1,0},{8,10},{10,12},{12... | collective-permute-start | bytes 2359304 | tf_op jit(solution)/shard_map/ppermute | solution.py:291
  94.3 5.8 %copy-start.4 = (s32[3,256]{1,0:T(4,128)S(1)}, s32[3,256]{1,0:T(4,128)}, u32[]{:S(2)}) copy-start(s32[3,256]{1,0:T(4,128)} %param.16) | copy-start | bytes 9220
  94.3 34.6 %collective-permute-start.19 = (bf16[768,512]{1,0:T(8,128)(2,1)}, bf16[768,512]{1,0:T(8,128)(2,1)}, u32[]{:S(2)}, u32[]{:S(2)}) collective-permute-start(bf16[768,512]{1,0:T(8,128)(2,1)} %shard_map.120), channel_id=1, source_target_pairs={{0,2},{2,4},{4,6},{6,7},{7,5},{5,3},{3,1},{1,0},{8,10},{10,12},{12... | collective-permute-start | bytes 2359304 | tf_op jit(solution)/shard_map/ppermute | solution.py:291
  99.4 29.6 %collective-permute-start.16 = (bf16[768,512]{1,0:T(8,128)(2,1)}, bf16[768,512]{1,0:T(8,128)(2,1)}, u32[]{:S(2)}, u32[]{:S(2)}) collective-permute-start(bf16[768,512]{1,0:T(8,128)(2,1)} %shard_map.117), channel_id=1, source_target_pairs={{0,1},{2,0},{4,2},{6,4},{7,6},{5,7},{3,5},{1,3},{8,9},{10,8},{12,1... | collective-permute-start | bytes 2359304 | tf_op jit(solution)/shard_map/ppermute | solution.py:291
  108.9 19.9 %collective-permute-start.2 = (f32[3,128,128]{2,1,0:T(8,128)S(1)}, f32[3,128,128]{2,1,0:T(8,128)S(1)}, u32[]{:S(2)}, u32[]{:S(2)}) collective-permute-start(f32[3,128,128]{2,1,0:T(8,128)S(1)} %shard_map.104), channel_id=1, source_target_pairs={{0,1},{1,0},{2,3},{3,2},{4,5},{5,4},{6,7},{7,6},{8,9},{9,8},{10,11... | collective-permute-start | bytes 589832 | tf_op jit(solution)/shard_map/ppermute | solution.py:232
  113.0 15.8 %copy-start.5 = (s32[3,1]{0,1:T(1,128)S(1)}, s32[3,1]{0,1:T(1,128)}, u32[]{:S(2)}) copy-start(s32[3,1]{0,1:T(1,128)} %param.17) | copy-start | bytes 40
  113.1 39.1 %collective-permute-start.12 = (bf16[768,512]{1,0:T(8,128)(2,1)S(1)}, bf16[768,512]{1,0:T(8,128)(2,1)S(1)}, u32[]{:S(2)}, u32[]{:S(2)}) collective-permute-start(bf16[768,512]{1,0:T(8,128)(2,1)S(1)} %shard_map.113), channel_id=1, source_target_pairs={{0,1},{2,0},{4,2},{6,4},{7,6},{5,7},{3,5},{1,3},{8,9},{10,8},{12,1... | collective-permute-start | bytes 2359304 | tf_op jit(solution)/shard_map/ppermute | solution.py:291
  128.8 23.4 %collective-permute-start.9 = (bf16[768,512]{1,0:T(8,128)(2,1)S(1)}, bf16[768,512]{1,0:T(8,128)(2,1)S(1)}, u32[]{:S(2)}, u32[]{:S(2)}) collective-permute-start(bf16[768,512]{1,0:T(8,128)(2,1)S(1)} %shard_map.110), channel_id=1, source_target_pairs={{0,2},{2,4},{4,6},{6,7},{7,5},{5,3},{3,1},{1,0},{8,10},{10,12},{12... | collective-permute-start | bytes 2359304 | tf_op jit(solution)/shard_map/ppermute | solution.py:291
  128.9 19.6 %collective-permute-start.3 = (f32[3,128,128]{2,1,0:T(8,128)S(1)}, f32[3,128,128]{2,1,0:T(8,128)S(1)}, u32[]{:S(2)}, u32[]{:S(2)}) collective-permute-start(f32[3,128,128]{2,1,0:T(8,128)S(1)} %add.90), channel_id=1, source_target_pairs={{0,2},{1,3},{2,0},{3,1},{4,6},{5,7},{6,4},{7,5},{8,10},{9,11},{10,... | collective-permute-start | bytes 589832 | tf_op jit(solution)/shard_map/ppermute | solution.py:232
  148.6 9.4 %collective-permute-start.4 = (f32[3,128,128]{2,1,0:T(8,128)S(1)}, f32[3,128,128]{2,1,0:T(8,128)S(1)}, u32[]{:S(2)}, u32[]{:S(2)}) collective-permute-start(f32[3,128,128]{2,1,0:T(8,128)S(1)} %add.91), channel_id=1, source_target_pairs={{0,4},{1,5},{2,6},{3,7},{4,0},{5,1},{6,2},{7,3},{8,12},{9,13},{10,... | collective-permute-start | bytes 589832 | tf_op jit(solution)/shard_map/ppermute | solution.py:232
  (2 other events, 7.7 us)

commit v3 on v2

v3 whole, which is shorter than its diff:
```python
import functools

import jax
import jax.numpy as jnp
from jax import lax
from jax.experimental import pallas as pl
from jax.experimental.pallas import tpu as pltpu
from jax.sharding import PartitionSpec as P

VMEM_LIMIT = 40 * 1024 * 1024
SWAP = [(0, 1), (1, 0)]
WHOLE = pl.BlockSpec(memory_space=pltpu.VMEM)
ANYWHERE = pl.BlockSpec(memory_space=pl.ANY)


def serpentine(size):
    return size == 8


def ring_index(place, size):
    if not serpentine(size):
        return place
    return jnp.where(place < size // 2, 2 * place, 2 * (size - 1 - place) + 1)


def ring_place(index, size):
    if not serpentine(size):
        return index
    return jnp.where(index & 1 == 0, index >> 1, size - 1 - (index >> 1))


def ring_order(size):
    if not serpentine(size):
        return list(range(size))
    return list(range(0, size, 2)) + list(range(size - 1, 0, -2))


def params():
    return pltpu.CompilerParams(vmem_limit_bytes=VMEM_LIMIT)


def cost(flops, size):
    return pl.CostEstimate(flops=flops, bytes_accessed=size, transcendentals=0)


def hop_kernel(with_received, dests, x_ref, w_ref, *refs):
    total = jnp.dot(x_ref[...], w_ref[...], preferred_element_type=jnp.float32)
    if with_received:
        total = total + refs[0][...].astype(jnp.float32)
    refs[-1][...] = total.astype(refs[-1].dtype)


def hop(dests, offset, half, x, weight, received, after):
    rows, depth = x.shape
    half_cols = weight.shape[1] // dests.shape[0] // 2
    tile = min(256, half_cols)
    tiles = half_cols // tile
    in_specs = [
        pl.BlockSpec((rows, depth), lambda j, d: (0, 0)),
        pl.BlockSpec(
            (depth, tile), lambda j, d: (0, (d[offset] * 2 + half) * tiles + j)
        ),
    ]
    operands = [x, weight]
    if received is not None:
        in_specs.append(pl.BlockSpec((rows, tile), lambda j, d: (0, j)))
        operands.append(received)
    if after is not None:
        in_specs.append(ANYWHERE)
        operands.append(after)
    return pl.pallas_call(
        functools.partial(hop_kernel, received is not None),
        grid_spec=pltpu.PrefetchScalarGridSpec(
            num_scalar_prefetch=1,
            grid=(tiles,),
            in_specs=in_specs,
            out_specs=pl.BlockSpec((rows, tile), lambda j, d: (0, j)),
        ),
        out_shape=jax.ShapeDtypeStruct((rows, half_cols), jnp.bfloat16),
        compiler_params=params(),
        cost_estimate=cost(
            2 * rows * depth * half_cols,
            2 * (rows * depth + depth * half_cols + 2 * rows * half_cols),
        ),
    )(dests, *operands)


def collect_kernel(count, index, table_ref, after_ref, out_ref, sems):
    copies = [
        pltpu.make_async_copy(table_ref.at[index[slot]], out_ref.at[slot], sems.at[slot])
        for slot in range(count)
    ]
    for copy in copies:
        copy.start()
    for copy in copies:
        copy.wait()


def collect(index, table, after):
    count = index.shape[0]
    shape = (count,) + table.shape[1:]
    return pl.pallas_call(
        functools.partial(collect_kernel, count),
        grid_spec=pltpu.PrefetchScalarGridSpec(
            num_scalar_prefetch=1,
            grid=(1,),
            in_specs=[ANYWHERE, ANYWHERE],
            out_specs=WHOLE,
            scratch_shapes=[pltpu.SemaphoreType.DMA((count,))],
        ),
        out_shape=jax.ShapeDtypeStruct(shape, table.dtype),
        compiler_params=params(),
        cost_estimate=cost(0, 4 * shape[0] * shape[1] * shape[2]),
    )(index, table, after)


def load_pages(count, local, index, table_ref, got_ref, pages, sems):
    for slot in range(count):
        own = local[slot] == 1

        @pl.when(own)
        def _():
            pltpu.make_async_copy(
                table_ref.at[index[slot]], pages.at[slot], sems.at[slot]
            ).start()

        @pl.when(jnp.logical_not(own))
        def _():
            pltpu.make_async_copy(got_ref.at[slot], pages.at[slot], sems.at[slot]).start()

    for slot in range(count):
        pltpu.make_async_copy(got_ref.at[slot], pages.at[slot], sems.at[slot]).wait()


def low_kernel(
    sizes, local, index, x_ref, place_ref, table_ref, got_ref, after_ref, out_ref, pages, sems
):
    steps, blocks, listed, rank, block_rows = sizes
    load_pages(steps * blocks * listed, local, index, table_ref, got_ref, pages, sems)
    for step in range(steps):
        for block in range(blocks):
            at = step * blocks + block
            rows = slice(at * block_rows, (at + 1) * block_rows)
            listing = pages[at * listed : (at + 1) * listed].reshape(listed * rank, -1)
            every = lax.dot_general(
                listing, x_ref[rows, :], (((1,), (1,)), ((), ())),
                preferred_element_type=jnp.float32,
            )
            place = place_ref[step : step + 1, block * block_rows : (block + 1) * block_rows]
            low = jnp.zeros((rank, block_rows), jnp.float32)
            for entry in range(listed):
                low = jnp.where(place == entry, every[entry * rank : (entry + 1) * rank], low)
            out_ref[:, rows] = low


def low_rank(sizes, local, index, x, place, table, got, after):
    steps, blocks, listed, rank, block_rows = sizes
    count = steps * blocks * listed
    rows, depth = x.shape
    return pl.pallas_call(
        functools.partial(low_kernel, sizes),
        grid_spec=pltpu.PrefetchScalarGridSpec(
            num_scalar_prefetch=2,
            grid=(1,),
            in_specs=[WHOLE, WHOLE, ANYWHERE, ANYWHERE, ANYWHERE],
            out_specs=WHOLE,
            scratch_shapes=[
                pltpu.VMEM((count, rank, depth), table.dtype),
                pltpu.SemaphoreType.DMA((count,)),
            ],
        ),
        out_shape=jax.ShapeDtypeStruct((rank, rows), jnp.float32),
        compiler_params=params(),
        cost_estimate=cost(
            2 * rows * depth * listed * rank, 2 * (rows * depth + count * rank * depth)
        ),
    )(local, index, x, place, table, got, after)


def add_kernel(one_ref, two_ref, after_ref, out_ref):
    out_ref[...] = one_ref[...] + two_ref[...]


def add(one, two, after):
    return pl.pallas_call(
        add_kernel,
        in_specs=[WHOLE, WHOLE, ANYWHERE],
        out_specs=WHOLE,
        out_shape=jax.ShapeDtypeStruct(one.shape, one.dtype),
        compiler_params=params(),
        cost_estimate=cost(one.size, 12 * one.size),
    )(one, two, after)


def own_kernel(
    sizes, dests, local, index, x_ref, w_ref, place_ref, low_ref, table_ref, got_ref, after_ref,
    out_ref, pages, sems,
):
    steps, blocks, listed, rank, block_rows = sizes
    tile = w_ref.shape[1]
    now = pl.program_id(0)

    @pl.when(now == 0)
    def _():
        load_pages(steps * blocks * listed, local, index, table_ref, got_ref, pages, sems)

    columns = pl.ds(pl.multiple_of(now * tile, tile), tile)
    entry_of = lax.broadcasted_iota(jnp.int32, (listed * rank, block_rows), 0) // rank
    for step in range(steps):
        for block in range(blocks):
            at = step * blocks + block
            rows = slice(at * block_rows, (at + 1) * block_rows)
            low = low_ref[:, rows]
            spread = jnp.concatenate([low] * listed, axis=0)
            place = place_ref[step : step + 1, block * block_rows : (block + 1) * block_rows]
            spread = jnp.where(entry_of == place, spread, 0.0)
            listing = pages[at * listed : (at + 1) * listed, :, columns]
            out_ref[rows, :] = jnp.dot(
                x_ref[rows, :], w_ref[...], preferred_element_type=jnp.float32
            ) + jnp.dot(
                spread.T.astype(jnp.bfloat16),
                listing.reshape(listed * rank, tile),
                preferred_element_type=jnp.float32,
            )


def own_terms(sizes, dests, local, index, x, weight, place, low, table, got, after):
    steps, blocks, listed, rank, block_rows = sizes
    count = steps * blocks * listed
    rows, depth = x.shape
    cols = weight.shape[1] // dests.shape[0]
    tile = min(256, cols)
    tiles = cols // tile
    return pl.pallas_call(
        functools.partial(own_kernel, sizes),
        grid_spec=pltpu.PrefetchScalarGridSpec(
            num_scalar_prefetch=3,
            grid=(tiles,),
            in_specs=[
                WHOLE,
                pl.BlockSpec((depth, tile), lambda j, d, l, i: (0, d[0] * tiles + j)),
                WHOLE,
                WHOLE,
                ANYWHERE,
                ANYWHERE,
                ANYWHERE,
            ],
            out_specs=pl.BlockSpec((rows, tile), lambda j, d, l, i: (0, j)),
            scratch_shapes=[
                pltpu.VMEM((count, rank, cols), table.dtype),
                pltpu.SemaphoreType.DMA((count,)),
            ],
        ),
        out_shape=jax.ShapeDtypeStruct((rows, cols), jnp.float32),
        compiler_params=params(),
        cost_estimate=cost(
            2 * rows * cols * (depth + listed * rank),
            2 * (rows * depth + depth * cols + count * rank * cols) + 4 * rows * cols,
        ),
    )(dests, local, index, x, weight, place, low, table, got, after)


def finish_kernel(live, own_ref, one_ref, two_ref, *refs):
    out_ref = refs[-1]
    total = (
        own_ref[...] + one_ref[...].astype(jnp.float32) + two_ref[...].astype(jnp.float32)
    )
    row = lax.broadcasted_iota(jnp.int32, total.shape, 0)
    out_ref[...] = jnp.where(row < live[pl.program_id(0)], total, 0.0).astype(out_ref.dtype)


def finish(live, half, own, one, two, result):
    rows, cols = own.shape
    steps = live.shape[0]
    block = (rows // steps, cols // 2)
    in_specs = [
        pl.BlockSpec(block, lambda s, l: (s, half)),
        pl.BlockSpec(block, lambda s, l: (s, 0)),
        pl.BlockSpec(block, lambda s, l: (s, 0)),
    ]
    operands = [own, one, two]
    aliases = {}
    if result is not None:
        in_specs.append(ANYWHERE)
        operands.append(result)
        aliases = {4: 0}
    return pl.pallas_call(
        finish_kernel,
        grid_spec=pltpu.PrefetchScalarGridSpec(
            num_scalar_prefetch=1,
            grid=(steps,),
            in_specs=in_specs,
            out_specs=pl.BlockSpec(block, lambda s, l: (s, half)),
        ),
        out_shape=jax.ShapeDtypeStruct((rows, cols), jnp.bfloat16),
        input_output_aliases=aliases,
        compiler_params=params(),
        cost_estimate=cost(0, rows * cols * 5),
    )(live, *operands)


def per_device(
    size,
    attention_output,
    output_weight,
    adapter_down_weight,
    adapter_up_weight,
    adapter_page_table,
    block_adapter_ids,
    row_list_position,
    live_row_count,
):
    steps, row_count, depth = attention_output.shape
    resident, rank, _ = adapter_down_weight.shape
    _, blocks, listed = block_adapter_ids.shape
    sizes = (steps, blocks, listed, rank, row_count // blocks)
    x = attention_output.reshape(steps * row_count, depth)
    ring = ring_order(size)

    instance = lax.axis_index("inst")
    place = ring_place(lax.axis_index("tp"), size)
    dests = ring_index(lax.rem(place + jnp.arange(size, dtype=jnp.int32), size), size)

    forward = [(ring[i], ring[(i + 1) % size]) for i in range(size)]
    backward = [(ring[i], ring[i - 1]) for i in range(size)]
    far = size // 2
    pairs = [[(0, 1, forward), (1, -1, backward)], [(1, 1, forward), (0, -1, backward)]]
    arrived = {}
    last = None

    def turn(number, last):
        left = far - (number + 1) // 2
        for half, sign, moves in pairs[number % 2]:
            last = hop(
                dests, (sign * left) % size, half, x, output_weight,
                arrived.get((half, sign)), last,
            )
            arrived[half, sign] = lax.ppermute(last, "tp", moves)
        return last

    ids = block_adapter_ids.reshape(-1)
    ids_there = lax.ppermute(ids, "inst", SWAP)
    last = turn(0, last)
    pages = adapter_page_table[jnp.concatenate([ids, ids_there])]
    places = pages % resident
    index, index_there = places[: ids.shape[0]], places[ids.shape[0] :]
    local = (pages[: ids.shape[0]] // resident == instance).astype(jnp.int32)
    last = collect(index_there, adapter_down_weight, last)
    got_down = lax.ppermute(last, "inst", SWAP)
    last = turn(1, last)
    last = collect(index_there, adapter_up_weight, last)
    got_up = lax.ppermute(last, "inst", SWAP)
    low = last = low_rank(
        sizes, local, index, x, row_list_position, adapter_down_weight, got_down, last
    )

    last = turn(2, last)
    number, turns = 3, 2 * far - 1
    if size & (size - 1):
        low = lax.psum(low, "tp")
    else:
        apart = 1
        while apart < size:
            sent = lax.ppermute(low, "tp", [(i, i ^ apart) for i in range(size)])
            if number < turns:
                last = turn(number, last)
                number += 1
            low = last = add(low, sent, last)
            apart *= 2
    while number < turns:
        last = turn(number, last)
        number += 1
    low = low.astype(jnp.bfloat16).astype(jnp.float32)
    own = own_terms(
        sizes, dests, local, index, x, output_weight, row_list_position, low,
        adapter_up_weight, got_up, last,
    )
    result = None
    for half in range(2):
        result = finish(
            live_row_count.reshape(-1), half, own, arrived[half, 1], arrived[half, -1], result
        )
    return result.reshape(steps, row_count, -1)


def solution(mesh):
    in_specs = (
        P(None, ("grp", "inst"), "tp"),
        P("tp", None),
        P("inst", None, "tp"),
        P("inst", None, "tp"),
        P(),
        P(None, ("grp", "inst"), None),
        P(None, ("grp", "inst")),
        P(None, ("grp", "inst")),
    )
    out_specs = P(None, ("grp", "inst"), "tp")
    return jax.shard_map(
        functools.partial(per_device, mesh.shape["tp"]),
        mesh=mesh, in_specs=in_specs, out_specs=out_specs, check_vma=False,
    )
```

time: 168 us -> 155 us (0.923)
  waiting for transfers between devices: 68.9 us -> 64 us
  other arithmetic: 4.98 us -> 0.14 us
    pallas_call x14, Pallas kernels: 45 us -> 39.7 us  [hop(): pl.pallas_call(functools.partial(hop_kernel, received is not None), grid_...]
    ppermute x20, waiting for transfers between devices: 68.9 us -> 64 us  [the longest x3 33.7 us: per_device(): sent = lax.ppermute(low, 'tp', [(i, i ^ apart) for i in range(size)])]
    pallas_call x0 -> x5, Pallas kernels: none -> 4.58 us  [the longest x2 4.51 us: finish(): pl.pallas_call(finish_kernel, grid_spec=pltpu.PrefetchScalarGridSpec(num_...]
    add x6 -> x0, other arithmetic: 2.7 us -> none  [the longest x2 1.83 us: per_device(): halves.append(sum((a.astype(jnp.float32) for a in there)))]
  transfers between devices with their start and end apart: 20 -> 20, of which waited for: 8 -> 9; matrix products, arithmetic and copies ran while one was open for 4% -> 0% of each run, Pallas kernels for 32% -> 37%
where the time goes in v3:
time: 155 us; the launch traced here: 154 us
  waiting for transfers between devices  64 us (41%)
  Pallas kernels  63.9 us (41%)
  starting transfers between devices  21.7 us (14%)
  local copies, waits for them, and re-layouts  4.05 us (3%)
    pallas_call x14, Pallas kernels, hop(): pl.pallas_call(functools.partial(hop_kernel, received is not None), grid_...  39.7 us
    ppermute x3, waiting for transfers between devices, per_device(): sent = lax.ppermute(low, 'tp', [(i, i ^ apart) for i in range(size)])  33.7 us
    ppermute x14, waiting for transfers between devices, turn(): arrived[half, sign] = lax.ppermute(last, 'tp', moves)  30.3 us
    ppermute x14, starting transfers between devices, turn(): arrived[half, sign] = lax.ppermute(last, 'tp', moves)  19.3 us
    pallas_call x2, Pallas kernels, collect(): pl.pallas_call(functools.partial(collect_kernel, count), grid_spec=pltpu....  8.68 us
    pallas_call x1, Pallas kernels, own_terms(): pl.pallas_call(functools.partial(own_kernel, sizes), grid_spec=pltpu.Pref...  7.24 us
    pallas_call x2, Pallas kernels, finish(): pl.pallas_call(finish_kernel, grid_spec=pltpu.PrefetchScalarGridSpec(num_...  4.51 us
    pallas_call x1, Pallas kernels, low_rank(): pl.pallas_call(functools.partial(low_kernel, sizes), grid_spec=pltpu.Pref...  3.67 us
  transfers between devices with their start and end apart: 20, of which 9 were waited for; matrix products, arithmetic and copies ran while one was open for 0% of the time, Pallas kernels for 37%

profile of v3, /device:TPU:0, one launch (start us, length us, event | category | flops | bytes accessed | tf_op | source)
XLA Modules:
  0.0 154.1 jit_solution(14686842429915065110)
XLA Ops:
  9.4 4.3 %shard_map.84.refs_0_ = bf16[24,64,1024]{2,1,0:T(8,128)(2,1)} custom-call(s32[24]{0:T(128)S(1)} %get-tuple-element.5.index, bf16[96,64,1024]{2,1,0:T(8,128)(2,1)} %table_ref.6, bf16[768,512]{1,0:T(8,128)(2,1)S(1)} %shard_map.83.after_ref), custom_call_target="tpu_custom_call" | custom-call | bytes 6291456 | tf_op jit(solution)/shard_map/pallas_call | solution.py:102
  13.8 3.0 %collective-permute-start.5 = (bf16[768,512]{1,0:T(8,128)(2,1)S(1)}, bf16[768,512]{1,0:T(8,128)(2,1)}, u32[]{:S(2)}, u32[]{:S(2)}) collective-permute-start(bf16[768,512]{1,0:T(8,128)(2,1)S(1)} %shard_map.83.after_ref), channel_id=1, source_target_pairs={{0,1},{2,0},{4,2},{6,4},{7,6},{5,7},{3,5},{1,3},{8,9},{10,8},{12,1... | collective-permute-start | bytes 2359304 | tf_op jit(solution)/shard_map/ppermute | solution.py:338
  23.4 4.4 %shard_map.87.after_ref = bf16[24,64,1024]{2,1,0:T(8,128)(2,1)} custom-call(s32[24]{0:T(128)S(1)} %get-tuple-element.5.index, bf16[96,64,1024]{2,1,0:T(8,128)(2,1)} %table_ref.7, bf16[768,512]{1,0:T(8,128)(2,1)S(1)} %shard_map.86.after_ref), custom_call_target="tpu_custom_call" | custom-call | bytes 6291456 | tf_op jit(solution)/shard_map/pallas_call | solution.py:102
  30.0 3.7 %shard_map.88.refs_1_.one_ref = f32[64,768]{1,0:T(8,128)S(1)} custom-call(s32[24]{0:T(128)S(1)} %compare_convert_fusion.local, s32[24]{0:T(128)S(1)} %get-tuple-element.6.index, bf16[768,1024]{1,0:T(8,128)(2,1)S(1)} %bitcast.10, s32[3,256]{1,0:T(4,128)S(1)} %copy-done.6, bf16[96,64,1024]{2,1,0:T(8,128)(2,1)} %table_ref.6, ...), custom_call_target="tpu_custom_call" | custom-call | flops 402653184 | bytes 4718592 | tf_op jit(solution)/shard_map/pallas_call | solution.py:160
  33.7 3.6 %collective-permute-done.6.refs_0_ = bf16[768,512]{1,0:T(8,128)(2,1)} collective-permute-done((bf16[768,512]{1,0:T(8,128)(2,1)S(1)}, bf16[768,512]{1,0:T(8,128)(2,1)}, u32[]{:S(2)}, u32[]{:S(2)}) %collective-permute-start.6) | collective-permute-done | bytes 786464 | tf_op jit(solution)/shard_map/ppermute | solution.py:338
  37.3 2.9 %shard_map.89.refs_1_ = bf16[768,512]{1,0:T(8,128)(2,1)S(1)} custom-call(s32[8]{0:T(128)S(1)} %compare_select_fusion.3.dests, bf16[768,1024]{1,0:T(8,128)(2,1)S(1)} %bitcast.11, bf16[1024,8192]{1,0:T(8,128)(2,1)} %w_ref.29, bf16[768,512]{1,0:T(8,128)(2,1)} %collective-permute-done.6.refs_0_, f32[64,768]{1,0:T(8,128)S(1)} %shard_map.88.refs_1_.one_ref), custom_call_target="tpu_custom_call" | custom-call | flops 805306368 | bytes 4194304 | tf_op jit(solution)/shard_map/pallas_call | solution.py:71
  40.3 3.0 %shard_map.90.refs_1_ = bf16[768,512]{1,0:T(8,128)(2,1)S(1)} custom-call(s32[8]{0:T(128)S(1)} %compare_select_fusion.3.dests, bf16[768,1024]{1,0:T(8,128)(2,1)S(1)} %bitcast.12, bf16[1024,8192]{1,0:T(8,128)(2,1)} %w_ref.29, bf16[768,512]{1,0:T(8,128)(2,1)} %collective-permute-done.5.refs_0_, bf16[768,512]{1,0:T(8,128)(2,1)S(1)} %shard_map.89.refs_1_), custom_call_target="tpu_custom_call" | custom-call | flops 805306368 | bytes 4194304 | tf_op jit(solution)/shard_map/pallas_call | solution.py:71
  45.4 8.7 %collective-permute-done.4.refs_0_ = bf16[768,512]{1,0:T(8,128)(2,1)S(1)} collective-permute-done((bf16[768,512]{1,0:T(8,128)(2,1)}, bf16[768,512]{1,0:T(8,128)(2,1)S(1)}, u32[]{:S(2)}, u32[]{:S(2)}) %collective-permute-start.4) | collective-permute-done | bytes 786464 | tf_op jit(solution)/shard_map/ppermute | solution.py:338
  60.1 2.8 %shard_map.92.after_ref = bf16[768,512]{1,0:T(8,128)(2,1)S(1)} custom-call(s32[8]{0:T(128)S(1)} %compare_select_fusion.3.dests, bf16[768,1024]{1,0:T(8,128)(2,1)S(1)} %bitcast.14, bf16[1024,8192]{1,0:T(8,128)(2,1)} %w_ref.29, bf16[768,512]{1,0:T(8,128)(2,1)S(1)} %collective-permute-done.3.refs_0_, bf16[768,512]{1,0:T(8,128)(2,1)S(1)} %shard_map.91.refs_1_), custom_call_target="tpu_custom_call" | custom-call | flops 805306368 | bytes 4194304 | tf_op jit(solution)/shard_map/pallas_call | solution.py:71
  62.9 12.2 %collective-permute-done.2.two_ref = f32[64,768]{1,0:T(8,128)S(1)} collective-permute-done((f32[64,768]{1,0:T(8,128)S(1)}, f32[64,768]{1,0:T(8,128)S(1)}, u32[]{:S(2)}, u32[]{:S(2)}) %collective-permute-start.2) | collective-permute-done | bytes 196640 | tf_op jit(solution)/shard_map/ppermute | solution.py:364
  75.3 2.8 %shard_map.94.refs_1_ = bf16[768,512]{1,0:T(8,128)(2,1)S(1)} custom-call(s32[8]{0:T(128)S(1)} %compare_select_fusion.3.dests, bf16[768,1024]{1,0:T(8,128)(2,1)S(1)} %bitcast.15, bf16[1024,8192]{1,0:T(8,128)(2,1)} %w_ref.29, bf16[768,512]{1,0:T(8,128)(2,1)S(1)} %collective-permute-done.9.refs_0_, f32[64,768]{1,0:T(8,128)S(1)} %shard_map.93.refs_1_.one_ref), custom_call_target="tpu_custom_call" | custom-call | flops 805306368 | bytes 4194304 | tf_op jit(solution)/shard_map/pallas_call | solution.py:71
  80.2 2.8 %shard_map.95.after_ref = bf16[768,512]{1,0:T(8,128)(2,1)S(1)} custom-call(s32[8]{0:T(128)S(1)} %compare_select_fusion.3.dests, bf16[768,1024]{1,0:T(8,128)(2,1)S(1)} %bitcast.16, bf16[1024,8192]{1,0:T(8,128)(2,1)} %w_ref.29, bf16[768,512]{1,0:T(8,128)(2,1)S(1)} %collective-permute-done.8.refs_0_, bf16[768,512]{1,0:T(8,128)(2,1)S(1)} %shard_map.94.refs_1_), custom_call_target="tpu_custom_call" | custom-call | flops 805306368 | bytes 4194304 | tf_op jit(solution)/shard_map/pallas_call | solution.py:71
  83.0 6.5 %collective-permute-done.7.two_ref = f32[64,768]{1,0:T(8,128)S(1)} collective-permute-done((f32[64,768]{1,0:T(8,128)S(1)}, f32[64,768]{1,0:T(8,128)S(1)}, u32[]{:S(2)}, u32[]{:S(2)}) %collective-permute-start.7) | collective-permute-done | bytes 196640 | tf_op jit(solution)/shard_map/ppermute | solution.py:364
  89.5 4.0 %collective-permute-start.14 = (bf16[768,512]{1,0:T(8,128)(2,1)S(1)}, bf16[768,512]{1,0:T(8,128)(2,1)S(1)}, u32[]{:S(2)}, u32[]{:S(2)}) collective-permute-start(bf16[768,512]{1,0:T(8,128)(2,1)S(1)} %shard_map.95.after_ref), channel_id=1, source_target_pairs={{0,1},{2,0},{4,2},{6,4},{7,6},{5,7},{3,5},{1,3},{8,9},{10,8},{12,1... | collective-permute-start | bytes 2359304 | tf_op jit(solution)/shard_map/ppermute | solution.py:338
  93.7 2.8 %shard_map.97.refs_1_ = bf16[768,512]{1,0:T(8,128)(2,1)S(1)} custom-call(s32[8]{0:T(128)S(1)} %compare_select_fusion.3.dests, bf16[768,1024]{1,0:T(8,128)(2,1)S(1)} %bitcast.17, bf16[1024,8192]{1,0:T(8,128)(2,1)} %w_ref.29, bf16[768,512]{1,0:T(8,128)(2,1)S(1)} %collective-permute-done.12.refs_0_, f32[64,768]{1,0:T(8,128)S(1)} %shard_map.96.refs_1_.one_ref), custom_call_target="tpu_custom_call" | custom-call | flops 805306368 | bytes 4194304 | tf_op jit(solution)/shard_map/pallas_call | solution.py:71
  96.5 3.4 %collective-permute-done.11.refs_0_ = bf16[768,512]{1,0:T(8,128)(2,1)S(1)} collective-permute-done((bf16[768,512]{1,0:T(8,128)(2,1)S(1)}, bf16[768,512]{1,0:T(8,128)(2,1)S(1)}, u32[]{:S(2)}, u32[]{:S(2)}) %collective-permute-start.11) | collective-permute-done | bytes 786464 | tf_op jit(solution)/shard_map/ppermute | solution.py:338
  102.7 15.0 %collective-permute-done.10.two_ref = f32[64,768]{1,0:T(8,128)S(1)} collective-permute-done((f32[64,768]{1,0:T(8,128)S(1)}, f32[64,768]{1,0:T(8,128)S(1)}, u32[]{:S(2)}, u32[]{:S(2)}) %collective-permute-start.10) | collective-permute-done | bytes 196640 | tf_op jit(solution)/shard_map/ppermute | solution.py:364
  117.8 2.8 %shard_map.100.refs_1_ = bf16[768,512]{1,0:T(8,128)(2,1)S(1)} custom-call(s32[8]{0:T(128)S(1)} %compare_select_fusion.3.dests, bf16[768,1024]{1,0:T(8,128)(2,1)S(1)} %bitcast.19, bf16[1024,8192]{1,0:T(8,128)(2,1)} %w_ref.29, bf16[768,512]{1,0:T(8,128)(2,1)S(1)} %collective-permute-done.15.refs_0_, f32[64,768]{1,0:T(8,128)S(1)} %shard_map.99.refs_1_), custom_call_target="tpu_custom_call" | custom-call | flops 805306368 | bytes 4194304 | tf_op jit(solution)/shard_map/pallas_call | solution.py:71
  120.6 2.9 %collective-permute-start.18 = (bf16[768,512]{1,0:T(8,128)(2,1)S(1)}, bf16[768,512]{1,0:T(8,128)(2,1)S(1)}, u32[]{:S(2)}, u32[]{:S(2)}) collective-permute-start(bf16[768,512]{1,0:T(8,128)(2,1)S(1)} %shard_map.100.refs_1_), channel_id=1, source_target_pairs={{0,2},{2,4},{4,6},{6,7},{7,5},{5,3},{3,1},{1,0},{8,10},{10,12},{12... | collective-permute-start | bytes 2359304 | tf_op jit(solution)/shard_map/ppermute | solution.py:338
  123.5 2.8 %shard_map.101.after_ref = bf16[768,512]{1,0:T(8,128)(2,1)S(1)} custom-call(s32[8]{0:T(128)S(1)} %compare_select_fusion.3.dests, bf16[768,1024]{1,0:T(8,128)(2,1)S(1)} %bitcast.20, bf16[1024,8192]{1,0:T(8,128)(2,1)} %w_ref.29, bf16[768,512]{1,0:T(8,128)(2,1)S(1)} %collective-permute-done.14.refs_0_, bf16[768,512]{1,0:T(8,128)(2,1)S(1)} %shard_map.100.refs_1_), custom_call_target="tpu_custom_call" | custom-call | flops 805306368 | bytes 4194304 | tf_op jit(solution)/shard_map/pallas_call | solution.py:71
  127.7 7.2 %shard_map.102.own_ref = f32[768,1024]{1,0:T(8,128)S(1)} custom-call(s32[8]{0:T(128)S(1)} %compare_select_fusion.3.dests, s32[24]{0:T(128)S(1)} %compare_convert_fusion.local, s32[24]{0:T(128)S(1)} %get-tuple-element.6.index, bf16[768,1024]{1,0:T(8,128)(2,1)S(1)} %bitcast.21, bf16[1024,8192]{1,0:T(8,128)(2,1)} %w_ref.29, s32[3,256]{1,0:T(4,128)S(1)} %copy-done.6, ...), custom_call_target="tpu_custom_call" | custom-call | flops 2013265920 | bytes 9961472 | tf_op jit(solution)/shard_map/pallas_call | solution.py:234
  135.0 4.1 %collective-permute-done.19.two_ref = bf16[768,512]{1,0:T(8,128)(2,1)S(1)} collective-permute-done((bf16[768,512]{1,0:T(8,128)(2,1)S(1)}, bf16[768,512]{1,0:T(8,128)(2,1)S(1)}, u32[]{:S(2)}, u32[]{:S(2)}) %collective-permute-start.19) | collective-permute-done | bytes 786464 | tf_op jit(solution)/shard_map/ppermute | solution.py:338
  139.0 4.5 %collective-permute-done.18.one_ref = bf16[768,512]{1,0:T(8,128)(2,1)S(1)} collective-permute-done((bf16[768,512]{1,0:T(8,128)(2,1)S(1)}, bf16[768,512]{1,0:T(8,128)(2,1)S(1)}, u32[]{:S(2)}, u32[]{:S(2)}) %collective-permute-start.18) | collective-permute-done | bytes 786464 | tf_op jit(solution)/shard_map/ppermute | solution.py:338
  145.8 6.0 %collective-permute-done.17.two_ref = bf16[768,512]{1,0:T(8,128)(2,1)S(1)} collective-permute-done((bf16[768,512]{1,0:T(8,128)(2,1)S(1)}, bf16[768,512]{1,0:T(8,128)(2,1)S(1)}, u32[]{:S(2)}, u32[]{:S(2)}) %collective-permute-start.17) | collective-permute-done | bytes 786464 | tf_op jit(solution)/shard_map/ppermute | solution.py:338
  (67 shorter events, 37.5 us)
Async XLA Ops:
  0.0 8.5 %copy-start = (s32[192]{0:T(256)S(1)}, s32[192]{0:T(256)}, u32[]{:S(2)}) copy-start(s32[192]{0:T(256)} %param.12) | copy-start | bytes 2308
  0.8 7.6 %collective-permute-start = (s32[24]{0:T(128)S(1)}, s32[24]{0:T(128)S(1)}, u32[]{:S(2)}, u32[]{:S(2)}) collective-permute-start(s32[24]{0:T(128)S(1)} %reshape.98), channel_id=1, source_target_pairs={{0,8},{8,0},{1,9},{9,1},{2,10},{10,2},{3,11},{11,3},{4,12},{12,4},... | collective-permute-start | bytes 296 | tf_op jit(solution)/shard_map/ppermute | solution.py:342
  9.4 7.5 %copy-start.3 = (bf16[3,256,1024]{2,1,0:T(8,128)(2,1)S(1)}, bf16[3,256,1024]{2,1,0:T(8,128)(2,1)}, u32[]{:S(2)}) copy-start(bf16[3,256,1024]{2,1,0:T(8,128)(2,1)} %param.8) | copy-start | bytes 4718596
  13.7 16.2 %collective-permute-start.1 = (bf16[24,64,1024]{2,1,0:T(8,128)(2,1)}, bf16[24,64,1024]{2,1,0:T(8,128)(2,1)}, u32[]{:S(2)}, u32[]{:S(2)}) collective-permute-start(bf16[24,64,1024]{2,1,0:T(8,128)(2,1)} %shard_map.84.refs_0_), channel_id=1, source_target_pairs={{0,8},{8,0},{1,9},{9,1},{2,10},{10,2},{3,11},{11,3},{4,12},{12,4},... | collective-permute-start | bytes 9437192 | tf_op jit(solution)/shard_map/ppermute | solution.py:349
  13.8 26.5 %collective-permute-start.5 = (bf16[768,512]{1,0:T(8,128)(2,1)S(1)}, bf16[768,512]{1,0:T(8,128)(2,1)}, u32[]{:S(2)}, u32[]{:S(2)}) collective-permute-start(bf16[768,512]{1,0:T(8,128)(2,1)S(1)} %shard_map.83.after_ref), channel_id=1, source_target_pairs={{0,1},{2,0},{4,2},{6,4},{7,6},{5,7},{3,5},{1,3},{8,9},{10,8},{12,1... | collective-permute-start | bytes 2359304 | tf_op jit(solution)/shard_map/ppermute | solution.py:338
  16.8 20.5 %collective-permute-start.6 = (bf16[768,512]{1,0:T(8,128)(2,1)S(1)}, bf16[768,512]{1,0:T(8,128)(2,1)}, u32[]{:S(2)}, u32[]{:S(2)}) collective-permute-start(bf16[768,512]{1,0:T(8,128)(2,1)S(1)} %shard_map.82.refs_0_), channel_id=1, source_target_pairs={{0,2},{2,4},{4,6},{6,7},{7,5},{5,3},{3,1},{1,0},{8,10},{10,12},{12... | collective-permute-start | bytes 2359304 | tf_op jit(solution)/shard_map/ppermute | solution.py:338
  27.8 99.9 %collective-permute-start.13 = (bf16[24,64,1024]{2,1,0:T(8,128)(2,1)}, bf16[24,64,1024]{2,1,0:T(8,128)(2,1)}, u32[]{:S(2)}, u32[]{:S(2)}) collective-permute-start(bf16[24,64,1024]{2,1,0:T(8,128)(2,1)} %shard_map.87.after_ref), channel_id=1, source_target_pairs={{0,8},{8,0},{1,9},{9,1},{2,10},{10,2},{3,11},{11,3},{4,12},{12,4},... | collective-permute-start | bytes 9437192 | tf_op jit(solution)/shard_map/ppermute | solution.py:352
  27.9 30.6 %collective-permute-start.3 = (bf16[768,512]{1,0:T(8,128)(2,1)}, bf16[768,512]{1,0:T(8,128)(2,1)S(1)}, u32[]{:S(2)}, u32[]{:S(2)}) collective-permute-start(bf16[768,512]{1,0:T(8,128)(2,1)} %copy-done.4), channel_id=1, source_target_pairs={{0,1},{2,0},{4,2},{6,4},{7,6},{5,7},{3,5},{1,3},{8,9},{10,8},{12,1... | collective-permute-start | bytes 2359304 | tf_op jit(solution)/shard_map/ppermute | solution.py:338
  29.9 24.2 %collective-permute-start.4 = (bf16[768,512]{1,0:T(8,128)(2,1)}, bf16[768,512]{1,0:T(8,128)(2,1)S(1)}, u32[]{:S(2)}, u32[]{:S(2)}) collective-permute-start(bf16[768,512]{1,0:T(8,128)(2,1)} %copy-done.5), channel_id=1, source_target_pairs={{0,2},{2,4},{4,6},{6,7},{7,5},{5,3},{3,1},{1,0},{8,10},{10,12},{12... | collective-permute-start | bytes 2359304 | tf_op jit(solution)/shard_map/ppermute | solution.py:338
  40.3 35.0 %collective-permute-start.9 = (bf16[768,512]{1,0:T(8,128)(2,1)S(1)}, bf16[768,512]{1,0:T(8,128)(2,1)S(1)}, u32[]{:S(2)}, u32[]{:S(2)}) collective-permute-start(bf16[768,512]{1,0:T(8,128)(2,1)S(1)} %shard_map.89.refs_1_), channel_id=1, source_target_pairs={{0,2},{2,4},{4,6},{6,7},{7,5},{5,3},{3,1},{1,0},{8,10},{10,12},{12... | collective-permute-start | bytes 2359304 | tf_op jit(solution)/shard_map/ppermute | solution.py:338
  43.3 34.8 %collective-permute-start.8 = (bf16[768,512]{1,0:T(8,128)(2,1)S(1)}, bf16[768,512]{1,0:T(8,128)(2,1)S(1)}, u32[]{:S(2)}, u32[]{:S(2)}) collective-permute-start(bf16[768,512]{1,0:T(8,128)(2,1)S(1)} %shard_map.90.refs_1_), channel_id=1, source_target_pairs={{0,1},{2,0},{4,2},{6,4},{7,6},{5,7},{3,5},{1,3},{8,9},{10,8},{12,1... | collective-permute-start | bytes 2359304 | tf_op jit(solution)/shard_map/ppermute | solution.py:338
  54.1 21.1 %collective-permute-start.2 = (f32[64,768]{1,0:T(8,128)S(1)}, f32[64,768]{1,0:T(8,128)S(1)}, u32[]{:S(2)}, u32[]{:S(2)}) collective-permute-start(f32[64,768]{1,0:T(8,128)S(1)} %shard_map.88.refs_1_.one_ref), channel_id=1, source_target_pairs={{0,1},{1,0},{2,3},{3,2},{4,5},{5,4},{6,7},{7,6},{8,9},{9,8},{10,11... | collective-permute-start | bytes 589832 | tf_op jit(solution)/shard_map/ppermute | solution.py:364
  58.5 35.1 %collective-permute-start.12 = (bf16[768,512]{1,0:T(8,128)(2,1)S(1)}, bf16[768,512]{1,0:T(8,128)(2,1)S(1)}, u32[]{:S(2)}, u32[]{:S(2)}) collective-permute-start(bf16[768,512]{1,0:T(8,128)(2,1)S(1)} %shard_map.91.refs_1_), channel_id=1, source_target_pairs={{0,2},{2,4},{4,6},{6,7},{7,5},{5,3},{3,1},{1,0},{8,10},{10,12},{12... | collective-permute-start | bytes 2359304 | tf_op jit(solution)/shard_map/ppermute | solution.py:338
  75.2 14.4 %collective-permute-start.7 = (f32[64,768]{1,0:T(8,128)S(1)}, f32[64,768]{1,0:T(8,128)S(1)}, u32[]{:S(2)}, u32[]{:S(2)}) collective-permute-start(f32[64,768]{1,0:T(8,128)S(1)} %shard_map.93.refs_1_.one_ref), channel_id=1, source_target_pairs={{0,2},{1,3},{2,0},{3,1},{4,6},{5,7},{6,4},{7,5},{8,10},{9,11},{10,... | collective-permute-start | bytes 589832 | tf_op jit(solution)/shard_map/ppermute | solution.py:364
  75.2 24.7 %collective-permute-start.11 = (bf16[768,512]{1,0:T(8,128)(2,1)S(1)}, bf16[768,512]{1,0:T(8,128)(2,1)S(1)}, u32[]{:S(2)}, u32[]{:S(2)}) collective-permute-start(bf16[768,512]{1,0:T(8,128)(2,1)S(1)} %shard_map.92.after_ref), channel_id=1, source_target_pairs={{0,1},{2,0},{4,2},{6,4},{7,6},{5,7},{3,5},{1,3},{8,9},{10,8},{12,1... | collective-permute-start | bytes 2359304 | tf_op jit(solution)/shard_map/ppermute | solution.py:338
  78.2 39.6 %collective-permute-start.15 = (bf16[768,512]{1,0:T(8,128)(2,1)S(1)}, bf16[768,512]{1,0:T(8,128)(2,1)S(1)}, u32[]{:S(2)}, u32[]{:S(2)}) collective-permute-start(bf16[768,512]{1,0:T(8,128)(2,1)S(1)} %shard_map.94.refs_1_), channel_id=1, source_target_pairs={{0,2},{2,4},{4,6},{6,7},{7,5},{5,3},{3,1},{1,0},{8,10},{10,12},{12... | collective-permute-start | bytes 2359304 | tf_op jit(solution)/shard_map/ppermute | solution.py:338
  89.5 34.0 %collective-permute-start.14 = (bf16[768,512]{1,0:T(8,128)(2,1)S(1)}, bf16[768,512]{1,0:T(8,128)(2,1)S(1)}, u32[]{:S(2)}, u32[]{:S(2)}) collective-permute-start(bf16[768,512]{1,0:T(8,128)(2,1)S(1)} %shard_map.95.after_ref), channel_id=1, source_target_pairs={{0,1},{2,0},{4,2},{6,4},{7,6},{5,7},{3,5},{1,3},{8,9},{10,8},{12,1... | collective-permute-start | bytes 2359304 | tf_op jit(solution)/shard_map/ppermute | solution.py:338
  93.6 24.1 %collective-permute-start.10 = (f32[64,768]{1,0:T(8,128)S(1)}, f32[64,768]{1,0:T(8,128)S(1)}, u32[]{:S(2)}, u32[]{:S(2)}) collective-permute-start(f32[64,768]{1,0:T(8,128)S(1)} %shard_map.96.refs_1_.one_ref), channel_id=1, source_target_pairs={{0,4},{1,5},{2,6},{3,7},{4,0},{5,1},{6,2},{7,3},{8,12},{9,13},{10,... | collective-permute-start | bytes 589832 | tf_op jit(solution)/shard_map/ppermute | solution.py:364
  99.9 45.9 %collective-permute-start.16 = (bf16[768,512]{1,0:T(8,128)(2,1)S(1)}, bf16[768,512]{1,0:T(8,128)(2,1)S(1)}, u32[]{:S(2)}, u32[]{:S(2)}) collective-permute-start(bf16[768,512]{1,0:T(8,128)(2,1)S(1)} %shard_map.97.refs_1_), channel_id=1, source_target_pairs={{0,2},{2,4},{4,6},{6,7},{7,5},{5,3},{3,1},{1,0},{8,10},{10,12},{12... | collective-permute-start | bytes 2359304 | tf_op jit(solution)/shard_map/ppermute | solution.py:338
  117.7 21.3 %collective-permute-start.19 = (bf16[768,512]{1,0:T(8,128)(2,1)S(1)}, bf16[768,512]{1,0:T(8,128)(2,1)S(1)}, u32[]{:S(2)}, u32[]{:S(2)}) collective-permute-start(bf16[768,512]{1,0:T(8,128)(2,1)S(1)} %shard_map.98.after_ref), channel_id=1, source_target_pairs={{0,1},{2,0},{4,2},{6,4},{7,6},{5,7},{3,5},{1,3},{8,9},{10,8},{12,1... | collective-permute-start | bytes 2359304 | tf_op jit(solution)/shard_map/ppermute | solution.py:338
  120.6 22.9 %collective-permute-start.18 = (bf16[768,512]{1,0:T(8,128)(2,1)S(1)}, bf16[768,512]{1,0:T(8,128)(2,1)S(1)}, u32[]{:S(2)}, u32[]{:S(2)}) collective-permute-start(bf16[768,512]{1,0:T(8,128)(2,1)S(1)} %shard_map.100.refs_1_), channel_id=1, source_target_pairs={{0,2},{2,4},{4,6},{6,7},{7,5},{5,3},{3,1},{1,0},{8,10},{10,12},{12... | collective-permute-start | bytes 2359304 | tf_op jit(solution)/shard_map/ppermute | solution.py:338
  126.3 25.5 %collective-permute-start.17 = (bf16[768,512]{1,0:T(8,128)(2,1)S(1)}, bf16[768,512]{1,0:T(8,128)(2,1)S(1)}, u32[]{:S(2)}, u32[]{:S(2)}) collective-permute-start(bf16[768,512]{1,0:T(8,128)(2,1)S(1)} %shard_map.101.after_ref), channel_id=1, source_target_pairs={{0,1},{2,0},{4,2},{6,4},{7,6},{5,7},{3,5},{1,3},{8,9},{10,8},{12,1... | collective-permute-start | bytes 2359304 | tf_op jit(solution)/shard_map/ppermute | solution.py:338
  127.7 15.8 %copy-start.7 = (s32[3,1]{0,1:T(1,128)S(1)}, s32[3,1]{0,1:T(1,128)}, u32[]{:S(2)}) copy-start(s32[3,1]{0,1:T(1,128)} %param.15) | copy-start | bytes 40
  143.5 10.6 %copy-start.1 = (s32[192]{0:T(256)S(1)}, s32[192]{0:T(256)}, u32[]{:S(2)}) copy-start(s32[192]{0:T(256)} %param.12) | copy-start | bytes 2308
  (5 other events, 16.2 us)

commit v4 on v3

--- a/solution.py
+++ b/solution.py
@@ -40,7 +40,7 @@
 
 
 def cost(flops, size):
-    return pl.CostEstimate(flops=flops, bytes_accessed=size, transcendentals=0)
+    return pl.CostEstimate(flops=30 * flops, bytes_accessed=size, transcendentals=0)
 
 
 def hop_kernel(with_received, dests, x_ref, w_ref, *refs):

time: 155 us -> 151 us (0.974)
  Pallas kernels: 63.9 us -> 62.2 us
    ppermute x3, starting transfers between devices: 1.72 us -> 4.49 us  [per_device(): sent = lax.ppermute(low, 'tp', [(i, i ^ apart) for i in range(size)])]
    ppermute x14, starting transfers between devices: 19.3 us -> 16.8 us  [turn(): arrived[half, sign] = lax.ppermute(last, 'tp', moves)]
    ppermute x3, waiting for transfers between devices: 33.7 us -> 31.7 us  [per_device(): sent = lax.ppermute(low, 'tp', [(i, i ^ apart) for i in range(size)])]
    pallas_call x2, Pallas kernels: 8.68 us -> 7.01 us  [collect(): pl.pallas_call(functools.partial(collect_kernel, count), grid_spec=pltpu....]
  transfers between devices with their start and end apart: 20 -> 20, of which waited for: 9 -> 8; matrix products, arithmetic and copies ran while one was open for 0% -> 1% of each run, Pallas kernels for 37% -> 40%
where the time goes in v4:
time: 151 us
  waiting for transfers between devices  62.9 us (42%)
  Pallas kernels  62.2 us (41%)
  starting transfers between devices  22.1 us (15%)
  local copies, waits for them, and re-layouts  3.19 us (2%)
    pallas_call x14, Pallas kernels, hop(): pl.pallas_call(functools.partial(hop_kernel, received is not None), grid_...  39.3 us
    ppermute x3, waiting for transfers between devices, per_device(): sent = lax.ppermute(low, 'tp', [(i, i ^ apart) for i in range(size)])  31.7 us
    ppermute x14, waiting for transfers between devices, turn(): arrived[half, sign] = lax.ppermute(last, 'tp', moves)  31.1 us
    ppermute x14, starting transfers between devices, turn(): arrived[half, sign] = lax.ppermute(last, 'tp', moves)  16.8 us
    pallas_call x1, Pallas kernels, own_terms(): pl.pallas_call(functools.partial(own_kernel, sizes), grid_spec=pltpu.Pref...  7.16 us
    pallas_call x2, Pallas kernels, collect(): pl.pallas_call(functools.partial(collect_kernel, count), grid_spec=pltpu....  7.01 us
    pallas_call x2, Pallas kernels, finish(): pl.pallas_call(finish_kernel, grid_spec=pltpu.PrefetchScalarGridSpec(num_...  4.51 us
    ppermute x3, starting transfers between devices, per_device(): sent = lax.ppermute(low, 'tp', [(i, i ^ apart) for i in range(size)])  4.49 us
  transfers between devices with their start and end apart: 20, of which 8 were waited for; matrix products, arithmetic and copies ran while one was open for 1% of the time, Pallas kernels for 40%

profile of v4, /device:TPU:0, one launch (start us, length us, event | category | flops | bytes accessed | tf_op | source)
XLA Modules:
  0.0 150.8 jit_solution(13928092016841728598)
XLA Ops:
  2.7 2.8 %shard_map.82.refs_0_ = bf16[768,512]{1,0:T(8,128)(2,1)S(1)} custom-call(s32[8]{0:T(128)S(1)} %compare_select_fusion.3.dests, bf16[768,1024]{1,0:T(8,128)(2,1)S(1)} %bitcast.8, bf16[1024,8192]{1,0:T(8,128)(2,1)} %w_ref.29), custom_call_target="tpu_custom_call" | custom-call | flops 24159191040 | bytes 4194304 | tf_op jit(solution)/shard_map/pallas_call | solution.py:71
  8.1 2.8 %shard_map.83.after_ref = bf16[768,512]{1,0:T(8,128)(2,1)S(1)} custom-call(s32[8]{0:T(128)S(1)} %compare_select_fusion.3.dests, bf16[768,1024]{1,0:T(8,128)(2,1)S(1)} %bitcast.9, bf16[1024,8192]{1,0:T(8,128)(2,1)} %w_ref.29, bf16[768,512]{1,0:T(8,128)(2,1)S(1)} %shard_map.82.refs_0_), custom_call_target="tpu_custom_call" | custom-call | flops 24159191040 | bytes 4194304 | tf_op jit(solution)/shard_map/pallas_call | solution.py:71
  12.1 2.7 %shard_map.84.refs_0_ = bf16[24,64,1024]{2,1,0:T(8,128)(2,1)S(1)} custom-call(s32[24]{0:T(128)S(1)} %get-tuple-element.5.index, bf16[96,64,1024]{2,1,0:T(8,128)(2,1)} %table_ref.6, bf16[768,512]{1,0:T(8,128)(2,1)S(1)} %shard_map.83.after_ref), custom_call_target="tpu_custom_call" | custom-call | bytes 6291456 | tf_op jit(solution)/shard_map/pallas_call | solution.py:102
  15.0 2.8 %shard_map.85.refs_0_ = bf16[768,512]{1,0:T(8,128)(2,1)S(1)} custom-call(s32[8]{0:T(128)S(1)} %compare_select_fusion.3.dests, bf16[768,1024]{1,0:T(8,128)(2,1)S(1)} %bitcast.10, bf16[1024,8192]{1,0:T(8,128)(2,1)} %w_ref.29, bf16[24,64,1024]{2,1,0:T(8,128)(2,1)S(1)} %shard_map.84.refs_0_), custom_call_target="tpu_custom_call" | custom-call | flops 24159191040 | bytes 4194304 | tf_op jit(solution)/shard_map/pallas_call | solution.py:71
  19.7 2.8 %shard_map.86.after_ref = bf16[768,512]{1,0:T(8,128)(2,1)S(1)} custom-call(s32[8]{0:T(128)S(1)} %compare_select_fusion.3.dests, bf16[768,1024]{1,0:T(8,128)(2,1)S(1)} %bitcast.11, bf16[1024,8192]{1,0:T(8,128)(2,1)} %w_ref.29, bf16[768,512]{1,0:T(8,128)(2,1)S(1)} %shard_map.85.refs_0_), custom_call_target="tpu_custom_call" | custom-call | flops 24159191040 | bytes 4194304 | tf_op jit(solution)/shard_map/pallas_call | solution.py:71
  22.8 4.3 %shard_map.87.after_ref = bf16[24,64,1024]{2,1,0:T(8,128)(2,1)} custom-call(s32[24]{0:T(128)S(1)} %get-tuple-element.5.index, bf16[96,64,1024]{2,1,0:T(8,128)(2,1)} %table_ref.7, bf16[768,512]{1,0:T(8,128)(2,1)S(1)} %shard_map.86.after_ref), custom_call_target="tpu_custom_call" | custom-call | bytes 6291456 | tf_op jit(solution)/shard_map/pallas_call | solution.py:102
  27.3 4.1 %shard_map.88.refs_1_.one_ref = f32[64,768]{1,0:T(8,128)S(1)} custom-call(s32[24]{0:T(128)S(1)} %compare_convert_fusion.local, s32[24]{0:T(128)S(1)} %get-tuple-element.6.index, bf16[768,1024]{1,0:T(8,128)(2,1)S(1)} %bitcast.12, s32[3,256]{1,0:T(4,128)S(1)} %copy-done.7, bf16[96,64,1024]{2,1,0:T(8,128)(2,1)} %table_ref.6, ...), custom_call_target="tpu_custom_call" | custom-call | flops 12079595520 | bytes 4718592 | tf_op jit(solution)/shard_map/pallas_call | solution.py:160
  33.2 2.8 %shard_map.89.refs_1_ = bf16[768,512]{1,0:T(8,128)(2,1)S(1)} custom-call(s32[8]{0:T(128)S(1)} %compare_select_fusion.3.dests, bf16[768,1024]{1,0:T(8,128)(2,1)S(1)} %bitcast.13, bf16[1024,8192]{1,0:T(8,128)(2,1)} %w_ref.29, bf16[768,512]{1,0:T(8,128)(2,1)S(1)} %collective-permute-done.6.refs_0_, f32[64,768]{1,0:T(8,128)S(1)} %shard_map.88.refs_1_.one_ref), custom_call_target="tpu_custom_call" | custom-call | flops 24159191040 | bytes 4194304 | tf_op jit(solution)/shard_map/pallas_call | solution.py:71
  37.7 2.8 %shard_map.90.refs_1_ = bf16[768,512]{1,0:T(8,128)(2,1)S(1)} custom-call(s32[8]{0:T(128)S(1)} %compare_select_fusion.3.dests, bf16[768,1024]{1,0:T(8,128)(2,1)S(1)} %bitcast.14, bf16[1024,8192]{1,0:T(8,128)(2,1)} %w_ref.29, bf16[768,512]{1,0:T(8,128)(2,1)S(1)} %collective-permute-done.5.refs_0_, bf16[768,512]{1,0:T(8,128)(2,1)S(1)} %shard_map.89.refs_1_), custom_call_target="tpu_custom_call" | custom-call | flops 24159191040 | bytes 4194304 | tf_op jit(solution)/shard_map/pallas_call | solution.py:71
  40.5 2.8 %collective-permute-done.4.refs_0_ = bf16[768,512]{1,0:T(8,128)(2,1)S(1)} collective-permute-done((bf16[768,512]{1,0:T(8,128)(2,1)S(1)}, bf16[768,512]{1,0:T(8,128)(2,1)S(1)}, u32[]{:S(2)}, u32[]{:S(2)}) %collective-permute-start.4) | collective-permute-done | bytes 786464 | tf_op jit(solution)/shard_map/ppermute | solution.py:338
  45.3 2.8 %shard_map.91.refs_1_ = bf16[768,512]{1,0:T(8,128)(2,1)S(1)} custom-call(s32[8]{0:T(128)S(1)} %compare_select_fusion.3.dests, bf16[768,1024]{1,0:T(8,128)(2,1)S(1)} %bitcast.15, bf16[1024,8192]{1,0:T(8,128)(2,1)} %w_ref.29, bf16[768,512]{1,0:T(8,128)(2,1)S(1)} %collective-permute-done.4.refs_0_, bf16[768,512]{1,0:T(8,128)(2,1)S(1)} %shard_map.90.refs_1_), custom_call_target="tpu_custom_call" | custom-call | flops 24159191040 | bytes 4194304 | tf_op jit(solution)/shard_map/pallas_call | solution.py:71
  49.8 2.8 %shard_map.92.after_ref = bf16[768,512]{1,0:T(8,128)(2,1)S(1)} custom-call(s32[8]{0:T(128)S(1)} %compare_select_fusion.3.dests, bf16[768,1024]{1,0:T(8,128)(2,1)S(1)} %bitcast.16, bf16[1024,8192]{1,0:T(8,128)(2,1)} %w_ref.29, bf16[768,512]{1,0:T(8,128)(2,1)S(1)} %collective-permute-done.3.refs_0_, bf16[768,512]{1,0:T(8,128)(2,1)S(1)} %shard_map.91.refs_1_), custom_call_target="tpu_custom_call" | custom-call | flops 24159191040 | bytes 4194304 | tf_op jit(solution)/shard_map/pallas_call | solution.py:71
  53.1 11.2 %collective-permute-done.9.refs_0_ = bf16[768,512]{1,0:T(8,128)(2,1)S(1)} collective-permute-done((bf16[768,512]{1,0:T(8,128)(2,1)S(1)}, bf16[768,512]{1,0:T(8,128)(2,1)S(1)}, u32[]{:S(2)}, u32[]{:S(2)}) %collective-permute-start.9) | collective-permute-done | bytes 786464 | tf_op jit(solution)/shard_map/ppermute | solution.py:338
  64.4 2.8 %shard_map.94.refs_1_ = bf16[768,512]{1,0:T(8,128)(2,1)S(1)} custom-call(s32[8]{0:T(128)S(1)} %compare_select_fusion.3.dests, bf16[768,1024]{1,0:T(8,128)(2,1)S(1)} %bitcast.17, bf16[1024,8192]{1,0:T(8,128)(2,1)} %w_ref.29, bf16[768,512]{1,0:T(8,128)(2,1)S(1)} %collective-permute-done.9.refs_0_, f32[64,768]{1,0:T(8,128)S(1)} %shard_map.93.refs_1_.one_ref), custom_call_target="tpu_custom_call" | custom-call | flops 24159191040 | bytes 4194304 | tf_op jit(solution)/shard_map/pallas_call | solution.py:71
  69.3 2.8 %shard_map.95.after_ref = bf16[768,512]{1,0:T(8,128)(2,1)S(1)} custom-call(s32[8]{0:T(128)S(1)} %compare_select_fusion.3.dests, bf16[768,1024]{1,0:T(8,128)(2,1)S(1)} %bitcast.18, bf16[1024,8192]{1,0:T(8,128)(2,1)} %w_ref.29, bf16[768,512]{1,0:T(8,128)(2,1)S(1)} %collective-permute-done.8.refs_0_, bf16[768,512]{1,0:T(8,128)(2,1)S(1)} %shard_map.94.refs_1_), custom_call_target="tpu_custom_call" | custom-call | flops 24159191040 | bytes 4194304 | tf_op jit(solution)/shard_map/pallas_call | solution.py:71
  72.1 13.3 %collective-permute-done.7.two_ref = f32[64,768]{1,0:T(8,128)S(1)} collective-permute-done((f32[64,768]{1,0:T(8,128)S(1)}, f32[64,768]{1,0:T(8,128)S(1)}, u32[]{:S(2)}, u32[]{:S(2)}) %collective-permute-start.7) | collective-permute-done | bytes 196640 | tf_op jit(solution)/shard_map/ppermute | solution.py:364
  88.1 2.8 %shard_map.97.refs_1_ = bf16[768,512]{1,0:T(8,128)(2,1)S(1)} custom-call(s32[8]{0:T(128)S(1)} %compare_select_fusion.3.dests, bf16[768,1024]{1,0:T(8,128)(2,1)S(1)} %bitcast.19, bf16[1024,8192]{1,0:T(8,128)(2,1)} %w_ref.29, bf16[768,512]{1,0:T(8,128)(2,1)S(1)} %collective-permute-done.12.refs_0_, f32[64,768]{1,0:T(8,128)S(1)} %shard_map.96.refs_1_.one_ref), custom_call_target="tpu_custom_call" | custom-call | flops 24159191040 | bytes 4194304 | tf_op jit(solution)/shard_map/pallas_call | solution.py:71
  93.0 2.8 %shard_map.98.after_ref = bf16[768,512]{1,0:T(8,128)(2,1)S(1)} custom-call(s32[8]{0:T(128)S(1)} %compare_select_fusion.3.dests, bf16[768,1024]{1,0:T(8,128)(2,1)S(1)} %bitcast.20, bf16[1024,8192]{1,0:T(8,128)(2,1)} %w_ref.29, bf16[768,512]{1,0:T(8,128)(2,1)S(1)} %collective-permute-done.11.refs_0_, bf16[768,512]{1,0:T(8,128)(2,1)S(1)} %shard_map.97.refs_1_), custom_call_target="tpu_custom_call" | custom-call | flops 24159191040 | bytes 4194304 | tf_op jit(solution)/shard_map/pallas_call | solution.py:71
  95.8 18.4 %collective-permute-done.10.two_ref = f32[64,768]{1,0:T(8,128)S(1)} collective-permute-done((f32[64,768]{1,0:T(8,128)S(1)}, f32[64,768]{1,0:T(8,128)S(1)}, u32[]{:S(2)}, u32[]{:S(2)}) %collective-permute-start.10) | collective-permute-done | bytes 196640 | tf_op jit(solution)/shard_map/ppermute | solution.py:364
  114.3 2.8 %shard_map.100.refs_1_ = bf16[768,512]{1,0:T(8,128)(2,1)S(1)} custom-call(s32[8]{0:T(128)S(1)} %compare_select_fusion.3.dests, bf16[768,1024]{1,0:T(8,128)(2,1)S(1)} %bitcast.21, bf16[1024,8192]{1,0:T(8,128)(2,1)} %w_ref.29, bf16[768,512]{1,0:T(8,128)(2,1)S(1)} %collective-permute-done.15.refs_0_, f32[64,768]{1,0:T(8,128)S(1)} %shard_map.99.refs_1_), custom_call_target="tpu_custom_call" | custom-call | flops 24159191040 | bytes 4194304 | tf_op jit(solution)/shard_map/pallas_call | solution.py:71
  119.3 2.8 %shard_map.101.after_ref = bf16[768,512]{1,0:T(8,128)(2,1)S(1)} custom-call(s32[8]{0:T(128)S(1)} %compare_select_fusion.3.dests, bf16[768,1024]{1,0:T(8,128)(2,1)S(1)} %bitcast.22, bf16[1024,8192]{1,0:T(8,128)(2,1)} %w_ref.29, bf16[768,512]{1,0:T(8,128)(2,1)S(1)} %collective-permute-done.14.refs_0_, bf16[768,512]{1,0:T(8,128)(2,1)S(1)} %shard_map.100.refs_1_), custom_call_target="tpu_custom_call" | custom-call | flops 24159191040 | bytes 4194304 | tf_op jit(solution)/shard_map/pallas_call | solution.py:71
  122.2 7.2 %shard_map.102.own_ref = f32[768,1024]{1,0:T(8,128)S(1)} custom-call(s32[8]{0:T(128)S(1)} %compare_select_fusion.3.dests, s32[24]{0:T(128)S(1)} %copy-done.10, s32[24]{0:T(128)S(1)} %copy-done.4, bf16[768,1024]{1,0:T(8,128)(2,1)S(1)} %bitcast.23, bf16[1024,8192]{1,0:T(8,128)(2,1)} %w_ref.29, s32[3,256]{1,0:T(4,128)S(1)} %copy-done.8, ...), custom_call_target="tpu_custom_call" | custom-call | flops 60397977600 | bytes 9961472 | tf_op jit(solution)/shard_map/pallas_call | solution.py:234
  129.4 5.4 %collective-permute-done.19.two_ref = bf16[768,512]{1,0:T(8,128)(2,1)S(1)} collective-permute-done((bf16[768,512]{1,0:T(8,128)(2,1)S(1)}, bf16[768,512]{1,0:T(8,128)(2,1)S(1)}, u32[]{:S(2)}, u32[]{:S(2)}) %collective-permute-start.19) | collective-permute-done | bytes 786464 | tf_op jit(solution)/shard_map/ppermute | solution.py:338
  137.4 11.1 %collective-permute-done.17.two_ref = bf16[768,512]{1,0:T(8,128)(2,1)S(1)} collective-permute-done((bf16[768,512]{1,0:T(8,128)(2,1)S(1)}, bf16[768,512]{1,0:T(8,128)(2,1)S(1)}, u32[]{:S(2)}, u32[]{:S(2)}) %collective-permute-start.17) | collective-permute-done | bytes 786464 | tf_op jit(solution)/shard_map/ppermute | solution.py:338
  (73 shorter events, 30.6 us)
Async XLA Ops:
  0.0 11.2 %copy-start = (s32[192]{0:T(256)S(1)}, s32[192]{0:T(256)}, u32[]{:S(2)}) copy-start(s32[192]{0:T(256)} %param.12) | copy-start | bytes 2308
  0.8 10.3 %collective-permute-start = (s32[24]{0:T(128)S(1)}, s32[24]{0:T(128)S(1)}, u32[]{:S(2)}, u32[]{:S(2)}) collective-permute-start(s32[24]{0:T(128)S(1)} %reshape.98), channel_id=1, source_target_pairs={{0,8},{8,0},{1,9},{9,1},{2,10},{10,2},{3,11},{11,3},{4,12},{12,4},... | collective-permute-start | bytes 296 | tf_op jit(solution)/shard_map/ppermute | solution.py:342
  5.5 25.9 %collective-permute-start.6 = (bf16[768,512]{1,0:T(8,128)(2,1)S(1)}, bf16[768,512]{1,0:T(8,128)(2,1)S(1)}, u32[]{:S(2)}, u32[]{:S(2)}) collective-permute-start(bf16[768,512]{1,0:T(8,128)(2,1)S(1)} %shard_map.82.refs_0_), channel_id=1, source_target_pairs={{0,2},{2,4},{4,6},{6,7},{7,5},{5,3},{3,1},{1,0},{8,10},{10,12},{12... | collective-permute-start | bytes 2359304 | tf_op jit(solution)/shard_map/ppermute | solution.py:338
  10.9 25.1 %collective-permute-start.5 = (bf16[768,512]{1,0:T(8,128)(2,1)S(1)}, bf16[768,512]{1,0:T(8,128)(2,1)S(1)}, u32[]{:S(2)}, u32[]{:S(2)}) collective-permute-start(bf16[768,512]{1,0:T(8,128)(2,1)S(1)} %shard_map.83.after_ref), channel_id=1, source_target_pairs={{0,1},{2,0},{4,2},{6,4},{7,6},{5,7},{3,5},{1,3},{8,9},{10,8},{12,1... | collective-permute-start | bytes 2359304 | tf_op jit(solution)/shard_map/ppermute | solution.py:338
  12.1 15.2 %copy-start.3 = (s32[24]{0:T(128)}, s32[24]{0:T(128)S(1)}, u32[]{:S(2)}) copy-start(s32[24]{0:T(128)S(1)} %get-tuple-element.6.index) | copy-start | bytes 292
  14.7 12.4 %collective-permute-start.1 = (bf16[24,64,1024]{2,1,0:T(8,128)(2,1)S(1)}, bf16[24,64,1024]{2,1,0:T(8,128)(2,1)S(1)}, u32[]{:S(2)}, u32[]{:S(2)}) collective-permute-start(bf16[24,64,1024]{2,1,0:T(8,128)(2,1)S(1)} %shard_map.84.refs_0_), channel_id=1, source_target_pairs={{0,8},{8,0},{1,9},{9,1},{2,10},{10,2},{3,11},{11,3},{4,12},{12,4},... | collective-permute-start | bytes 9437192 | tf_op jit(solution)/shard_map/ppermute | solution.py:349
  17.8 25.5 %collective-permute-start.4 = (bf16[768,512]{1,0:T(8,128)(2,1)S(1)}, bf16[768,512]{1,0:T(8,128)(2,1)S(1)}, u32[]{:S(2)}, u32[]{:S(2)}) collective-permute-start(bf16[768,512]{1,0:T(8,128)(2,1)S(1)} %shard_map.85.refs_0_), channel_id=1, source_target_pairs={{0,2},{2,4},{4,6},{6,7},{7,5},{5,3},{3,1},{1,0},{8,10},{10,12},{12... | collective-permute-start | bytes 2359304 | tf_op jit(solution)/shard_map/ppermute | solution.py:338
  22.5 25.7 %collective-permute-start.3 = (bf16[768,512]{1,0:T(8,128)(2,1)S(1)}, bf16[768,512]{1,0:T(8,128)(2,1)S(1)}, u32[]{:S(2)}, u32[]{:S(2)}) collective-permute-start(bf16[768,512]{1,0:T(8,128)(2,1)S(1)} %shard_map.86.after_ref), channel_id=1, source_target_pairs={{0,1},{2,0},{4,2},{6,4},{7,6},{5,7},{3,5},{1,3},{8,9},{10,8},{12,1... | collective-permute-start | bytes 2359304 | tf_op jit(solution)/shard_map/ppermute | solution.py:338
  27.2 95.0 %collective-permute-start.13 = (bf16[24,64,1024]{2,1,0:T(8,128)(2,1)}, bf16[24,64,1024]{2,1,0:T(8,128)(2,1)}, u32[]{:S(2)}, u32[]{:S(2)}) collective-permute-start(bf16[24,64,1024]{2,1,0:T(8,128)(2,1)} %shard_map.87.after_ref), channel_id=1, source_target_pairs={{0,8},{8,0},{1,9},{9,1},{2,10},{10,2},{3,11},{11,3},{4,12},{12,4},... | collective-permute-start | bytes 9437192 | tf_op jit(solution)/shard_map/ppermute | solution.py:352
  31.4 21.2 %collective-permute-start.2 = (f32[64,768]{1,0:T(8,128)S(1)}, f32[64,768]{1,0:T(8,128)S(1)}, u32[]{:S(2)}, u32[]{:S(2)}) collective-permute-start(f32[64,768]{1,0:T(8,128)S(1)} %shard_map.88.refs_1_.one_ref), channel_id=1, source_target_pairs={{0,1},{1,0},{2,3},{3,2},{4,5},{5,4},{6,7},{7,6},{8,9},{9,8},{10,11... | collective-permute-start | bytes 589832 | tf_op jit(solution)/shard_map/ppermute | solution.py:364
  36.1 28.3 %collective-permute-start.9 = (bf16[768,512]{1,0:T(8,128)(2,1)S(1)}, bf16[768,512]{1,0:T(8,128)(2,1)S(1)}, u32[]{:S(2)}, u32[]{:S(2)}) collective-permute-start(bf16[768,512]{1,0:T(8,128)(2,1)S(1)} %shard_map.89.refs_1_), channel_id=1, source_target_pairs={{0,2},{2,4},{4,6},{6,7},{7,5},{5,3},{3,1},{1,0},{8,10},{10,12},{12... | collective-permute-start | bytes 2359304 | tf_op jit(solution)/shard_map/ppermute | solution.py:338
  43.3 23.9 %collective-permute-start.8 = (bf16[768,512]{1,0:T(8,128)(2,1)S(1)}, bf16[768,512]{1,0:T(8,128)(2,1)S(1)}, u32[]{:S(2)}, u32[]{:S(2)}) collective-permute-start(bf16[768,512]{1,0:T(8,128)(2,1)S(1)} %shard_map.90.refs_1_), channel_id=1, source_target_pairs={{0,1},{2,0},{4,2},{6,4},{7,6},{5,7},{3,5},{1,3},{8,9},{10,8},{12,1... | collective-permute-start | bytes 2359304 | tf_op jit(solution)/shard_map/ppermute | solution.py:338
  48.2 37.2 %collective-permute-start.12 = (bf16[768,512]{1,0:T(8,128)(2,1)S(1)}, bf16[768,512]{1,0:T(8,128)(2,1)S(1)}, u32[]{:S(2)}, u32[]{:S(2)}) collective-permute-start(bf16[768,512]{1,0:T(8,128)(2,1)S(1)} %shard_map.91.refs_1_), channel_id=1, source_target_pairs={{0,2},{2,4},{4,6},{6,7},{7,5},{5,3},{3,1},{1,0},{8,10},{10,12},{12... | collective-permute-start | bytes 2359304 | tf_op jit(solution)/shard_map/ppermute | solution.py:338
  52.6 38.3 %collective-permute-start.11 = (bf16[768,512]{1,0:T(8,128)(2,1)S(1)}, bf16[768,512]{1,0:T(8,128)(2,1)S(1)}, u32[]{:S(2)}, u32[]{:S(2)}) collective-permute-start(bf16[768,512]{1,0:T(8,128)(2,1)S(1)} %shard_map.92.after_ref), channel_id=1, source_target_pairs={{0,1},{2,0},{4,2},{6,4},{7,6},{5,7},{3,5},{1,3},{8,9},{10,8},{12,1... | collective-permute-start | bytes 2359304 | tf_op jit(solution)/shard_map/ppermute | solution.py:338
  64.4 21.0 %collective-permute-start.7 = (f32[64,768]{1,0:T(8,128)S(1)}, f32[64,768]{1,0:T(8,128)S(1)}, u32[]{:S(2)}, u32[]{:S(2)}) collective-permute-start(f32[64,768]{1,0:T(8,128)S(1)} %shard_map.93.refs_1_.one_ref), channel_id=1, source_target_pairs={{0,2},{1,3},{2,0},{3,1},{4,6},{5,7},{6,4},{7,5},{8,10},{9,11},{10,... | collective-permute-start | bytes 589832 | tf_op jit(solution)/shard_map/ppermute | solution.py:364
  67.2 47.1 %collective-permute-start.15 = (bf16[768,512]{1,0:T(8,128)(2,1)S(1)}, bf16[768,512]{1,0:T(8,128)(2,1)S(1)}, u32[]{:S(2)}, u32[]{:S(2)}) collective-permute-start(bf16[768,512]{1,0:T(8,128)(2,1)S(1)} %shard_map.94.refs_1_), channel_id=1, source_target_pairs={{0,2},{2,4},{4,6},{6,7},{7,5},{5,3},{3,1},{1,0},{8,10},{10,12},{12... | collective-permute-start | bytes 2359304 | tf_op jit(solution)/shard_map/ppermute | solution.py:338
  85.4 33.9 %collective-permute-start.14 = (bf16[768,512]{1,0:T(8,128)(2,1)S(1)}, bf16[768,512]{1,0:T(8,128)(2,1)S(1)}, u32[]{:S(2)}, u32[]{:S(2)}) collective-permute-start(bf16[768,512]{1,0:T(8,128)(2,1)S(1)} %shard_map.95.after_ref), channel_id=1, source_target_pairs={{0,1},{2,0},{4,2},{6,4},{7,6},{5,7},{3,5},{1,3},{8,9},{10,8},{12,1... | collective-permute-start | bytes 2359304 | tf_op jit(solution)/shard_map/ppermute | solution.py:338
  85.4 28.8 %collective-permute-start.10 = (f32[64,768]{1,0:T(8,128)S(1)}, f32[64,768]{1,0:T(8,128)S(1)}, u32[]{:S(2)}, u32[]{:S(2)}) collective-permute-start(f32[64,768]{1,0:T(8,128)S(1)} %shard_map.96.refs_1_.one_ref), channel_id=1, source_target_pairs={{0,4},{1,5},{2,6},{3,7},{4,0},{5,1},{6,2},{7,3},{8,12},{9,13},{10,... | collective-permute-start | bytes 589832 | tf_op jit(solution)/shard_map/ppermute | solution.py:364
  90.9 46.5 %collective-permute-start.16 = (bf16[768,512]{1,0:T(8,128)(2,1)S(1)}, bf16[768,512]{1,0:T(8,128)(2,1)S(1)}, u32[]{:S(2)}, u32[]{:S(2)}) collective-permute-start(bf16[768,512]{1,0:T(8,128)(2,1)S(1)} %shard_map.97.refs_1_), channel_id=1, source_target_pairs={{0,2},{2,4},{4,6},{6,7},{7,5},{5,3},{3,1},{1,0},{8,10},{10,12},{12... | collective-permute-start | bytes 2359304 | tf_op jit(solution)/shard_map/ppermute | solution.py:338
  114.3 20.5 %collective-permute-start.19 = (bf16[768,512]{1,0:T(8,128)(2,1)S(1)}, bf16[768,512]{1,0:T(8,128)(2,1)S(1)}, u32[]{:S(2)}, u32[]{:S(2)}) collective-permute-start(bf16[768,512]{1,0:T(8,128)(2,1)S(1)} %shard_map.98.after_ref), channel_id=1, source_target_pairs={{0,1},{2,0},{4,2},{6,4},{7,6},{5,7},{3,5},{1,3},{8,9},{10,8},{12,1... | collective-permute-start | bytes 2359304 | tf_op jit(solution)/shard_map/ppermute | solution.py:338
  117.2 18.0 %collective-permute-start.18 = (bf16[768,512]{1,0:T(8,128)(2,1)S(1)}, bf16[768,512]{1,0:T(8,128)(2,1)S(1)}, u32[]{:S(2)}, u32[]{:S(2)}) collective-permute-start(bf16[768,512]{1,0:T(8,128)(2,1)S(1)} %shard_map.100.refs_1_), channel_id=1, source_target_pairs={{0,2},{2,4},{4,6},{6,7},{7,5},{5,3},{3,1},{1,0},{8,10},{10,12},{12... | collective-permute-start | bytes 2359304 | tf_op jit(solution)/shard_map/ppermute | solution.py:338
  122.1 13.1 %copy-start.2 = (s32[3,1]{0,1:T(1,128)S(1)}, s32[3,1]{0,1:T(1,128)}, u32[]{:S(2)}) copy-start(s32[3,1]{0,1:T(1,128)} %param.15) | copy-start | bytes 40
  122.1 26.5 %collective-permute-start.17 = (bf16[768,512]{1,0:T(8,128)(2,1)S(1)}, bf16[768,512]{1,0:T(8,128)(2,1)S(1)}, u32[]{:S(2)}, u32[]{:S(2)}) collective-permute-start(bf16[768,512]{1,0:T(8,128)(2,1)S(1)} %shard_map.101.after_ref), channel_id=1, source_target_pairs={{0,1},{2,0},{4,2},{6,4},{7,6},{5,7},{3,5},{1,3},{8,9},{10,8},{12,1... | collective-permute-start | bytes 2359304 | tf_op jit(solution)/shard_map/ppermute | solution.py:338
  135.2 15.7 %copy-start.1 = (s32[192]{0:T(256)S(1)}, s32[192]{0:T(256)}, u32[]{:S(2)}) copy-start(s32[192]{0:T(256)} %param.12) | copy-start | bytes 2308
  (8 other events, 34.0 us)

commit v5 on v4

--- a/solution.py
+++ b/solution.py
@@ -44,10 +44,12 @@
 
 
 def hop_kernel(with_received, dests, x_ref, w_ref, *refs):
+    tile = w_ref.shape[1]
+    columns = pl.ds(pl.multiple_of(pl.program_id(0) * tile, tile), tile)
     total = jnp.dot(x_ref[...], w_ref[...], preferred_element_type=jnp.float32)
     if with_received:
-        total = total + refs[0][...].astype(jnp.float32)
-    refs[-1][...] = total.astype(refs[-1].dtype)
+        total = total + refs[0][:, columns].astype(jnp.float32)
+    refs[-1][:, columns] = total.astype(refs[-1].dtype)
 
 
 def hop(dests, offset, half, x, weight, received, after):
@@ -56,14 +58,14 @@
     tile = min(256, half_cols)
     tiles = half_cols // tile
     in_specs = [
-        pl.BlockSpec((rows, depth), lambda j, d: (0, 0)),
+        WHOLE,
         pl.BlockSpec(
             (depth, tile), lambda j, d: (0, (d[offset] * 2 + half) * tiles + j)
         ),
     ]
     operands = [x, weight]
     if received is not None:
-        in_specs.append(pl.BlockSpec((rows, tile), lambda j, d: (0, j)))
+        in_specs.append(WHOLE)
         operands.append(received)
     if after is not None:
         in_specs.append(ANYWHERE)
@@ -74,7 +76,7 @@
             num_scalar_prefetch=1,
             grid=(tiles,),
             in_specs=in_specs,
-            out_specs=pl.BlockSpec((rows, tile), lambda j, d: (0, j)),
+            out_specs=WHOLE,
         ),
         out_shape=jax.ShapeDtypeStruct((rows, half_cols), jnp.bfloat16),
         compiler_params=params(),
@@ -193,18 +195,54 @@
 
 
 def own_kernel(
-    sizes, dests, local, index, x_ref, w_ref, place_ref, low_ref, table_ref, got_ref, after_ref,
-    out_ref, pages, sems,
+    local, index, dests, x_ref, w_ref, table_ref, got_ref, after_ref, out_ref, pages, sems
 ):
-    steps, blocks, listed, rank, block_rows = sizes
     tile = w_ref.shape[1]
     now = pl.program_id(0)
+    count = pages.shape[0]
 
     @pl.when(now == 0)
     def _():
-        load_pages(steps * blocks * listed, local, index, table_ref, got_ref, pages, sems)
+        load_pages(count, local, index, table_ref, got_ref, pages, sems)
 
     columns = pl.ds(pl.multiple_of(now * tile, tile), tile)
+    out_ref[:, columns] = jnp.dot(x_ref[...], w_ref[...], preferred_element_type=jnp.float32)
+
+
+def own_terms(dests, local, index, x, weight, table, got, after):
+    count, rank, cols = got.shape
+    rows, depth = x.shape
+    tile = min(256, cols)
+    tiles = cols // tile
+    return pl.pallas_call(
+        own_kernel,
+        grid_spec=pltpu.PrefetchScalarGridSpec(
+            num_scalar_prefetch=3,
+            grid=(tiles,),
+            in_specs=[
+                WHOLE,
+                pl.BlockSpec((depth, tile), lambda j, l, i, d: (0, d[0] * tiles + j)),
+                ANYWHERE,
+                ANYWHERE,
+                ANYWHERE,
+            ],
+            out_specs=[WHOLE, WHOLE],
+            scratch_shapes=[pltpu.SemaphoreType.DMA((count,))],
+        ),
+        out_shape=[
+            jax.ShapeDtypeStruct((rows, cols), jnp.float32),
+            jax.ShapeDtypeStruct((count, rank, cols), table.dtype),
+        ],
+        compiler_params=params(),
+        cost_estimate=cost(
+            2 * rows * cols * depth,
+            2 * (rows * depth + depth * cols + 2 * count * rank * cols) + 4 * rows * cols,
+        ),
+    )(local, index, dests, x, weight, table, got, after)
+
+
+def delta_kernel(sizes, own_ref, pages_ref, place_ref, low_ref, after_ref, out_ref):
+    steps, blocks, listed, rank, block_rows = sizes
     entry_of = lax.broadcasted_iota(jnp.int32, (listed * rank, block_rows), 0) // rank
     for step in range(steps):
         for block in range(blocks):
@@ -214,50 +252,24 @@
             spread = jnp.concatenate([low] * listed, axis=0)
             place = place_ref[step : step + 1, block * block_rows : (block + 1) * block_rows]
             spread = jnp.where(entry_of == place, spread, 0.0)
-            listing = pages[at * listed : (at + 1) * listed, :, columns]
-            out_ref[rows, :] = jnp.dot(
-                x_ref[rows, :], w_ref[...], preferred_element_type=jnp.float32
-            ) + jnp.dot(
-                spread.T.astype(jnp.bfloat16),
-                listing.reshape(listed * rank, tile),
-                preferred_element_type=jnp.float32,
+            listing = pages_ref[at * listed : (at + 1) * listed].reshape(listed * rank, -1)
+            out_ref[rows, :] = own_ref[rows, :] + jnp.dot(
+                spread.T.astype(jnp.bfloat16), listing, preferred_element_type=jnp.float32
             )
 
 
-def own_terms(sizes, dests, local, index, x, weight, place, low, table, got, after):
-    steps, blocks, listed, rank, block_rows = sizes
-    count = steps * blocks * listed
-    rows, depth = x.shape
-    cols = weight.shape[1] // dests.shape[0]
-    tile = min(256, cols)
-    tiles = cols // tile
-    return pl.pallas_call(
-        functools.partial(own_kernel, sizes),
-        grid_spec=pltpu.PrefetchScalarGridSpec(
-            num_scalar_prefetch=3,
-            grid=(tiles,),
-            in_specs=[
-                WHOLE,
-                pl.BlockSpec((depth, tile), lambda j, d, l, i: (0, d[0] * tiles + j)),
-                WHOLE,
-                WHOLE,
-                ANYWHERE,
-                ANYWHERE,
-                ANYWHERE,
-            ],
-            out_specs=pl.BlockSpec((rows, tile), lambda j, d, l, i: (0, j)),
-            scratch_shapes=[
-                pltpu.VMEM((count, rank, cols), table.dtype),
-                pltpu.SemaphoreType.DMA((count,)),
-            ],
-        ),
-        out_shape=jax.ShapeDtypeStruct((rows, cols), jnp.float32),
+def add_delta(sizes, own, pages, place, low, after):
+    rows, cols = own.shape
+    return pl.pallas_call(
+        functools.partial(delta_kernel, sizes),
+        in_specs=[WHOLE, WHOLE, WHOLE, WHOLE, ANYWHERE],
+        out_specs=WHOLE,
+        out_shape=jax.ShapeDtypeStruct(own.shape, own.dtype),
         compiler_params=params(),
         cost_estimate=cost(
-            2 * rows * cols * (depth + listed * rank),
-            2 * (rows * depth + depth * cols + count * rank * cols) + 4 * rows * cols,
-        ),
-    )(dests, local, index, x, weight, place, low, table, got, after)
+            2 * rows * cols * sizes[2] * sizes[3], 8 * rows * cols + 2 * pages.size
+        ),
+    )(own, pages, place, low, after)
 
 
 def finish_kernel(live, own_ref, one_ref, two_ref, *refs):
@@ -355,6 +367,10 @@
     )
 
     last = turn(2, last)
+    own, up_pages = own_terms(
+        dests, local, index, x, output_weight, adapter_up_weight, got_up, last
+    )
+    last = own
     number, turns = 3, 2 * far - 1
     if size & (size - 1):
         low = lax.psum(low, "tp")
@@ -362,19 +378,17 @@
         apart = 1
         while apart < size:
             sent = lax.ppermute(low, "tp", [(i, i ^ apart) for i in range(size)])
-            if number < turns:
-                last = turn(number, last)
-                number += 1
+            apart *= 2
+            for _ in range(1 if apart < size else 2):
+                if number < turns:
+                    last = turn(number, last)
+                    number += 1
             low = last = add(low, sent, last)
-            apart *= 2
     while number < turns:
         last = turn(number, last)
         number += 1
     low = low.astype(jnp.bfloat16).astype(jnp.float32)
-    own = own_terms(
-        sizes, dests, local, index, x, output_weight, row_list_position, low,
-        adapter_up_weight, got_up, last,
-    )
+    own = add_delta(sizes, own, up_pages, row_list_position, low, last)
     result = None
     for half in range(2):
         result = finish(

time: 151 us -> 144 us (0.954)
  waiting for transfers between devices: 62.9 us -> 49.1 us
  Pallas kernels: 62.2 us -> 65.9 us
  local copies, waits for them, and re-layouts: 3.19 us -> 4.87 us
    ppermute x3, waiting for transfers between devices: 31.7 us -> 13.8 us  [per_device(): sent = lax.ppermute(low, 'tp', [(i, i ^ apart) for i in range(size)])]
    ppermute x14, waiting for transfers between devices: 31.1 us -> 35.3 us  [turn(): arrived[half, sign] = lax.ppermute(last, 'tp', moves)]
    pallas_call x1, Pallas kernels: 4.12 us -> 5.87 us  [low_rank(): pl.pallas_call(functools.partial(low_kernel, sizes), grid_spec=pltpu.Pref...]
    pallas_call x2, Pallas kernels: 7.01 us -> 5.33 us  [collect(): pl.pallas_call(functools.partial(collect_kernel, count), grid_spec=pltpu....]
    unnamed x24, local copies, waits for them, and re-layouts: 1.46 us -> 3.14 us
    ppermute x3, starting transfers between devices: 4.49 us -> 6.15 us  [per_device(): sent = lax.ppermute(low, 'tp', [(i, i ^ apart) for i in range(size)])]
    pallas_call x1 -> x2, Pallas kernels: 7.16 us -> 8.76 us  [the longest x1 8.06 us: own_terms(): pl.pallas_call(own_kernel, grid_spec=pltpu.PrefetchScalarGridSpec(num_sca...]
  transfers between devices with their start and end apart: 20 -> 20, of which waited for: 8 -> 7; matrix products, arithmetic and copies ran while one was open for 1% -> 1% of each run, Pallas kernels for 40% -> 44%
where the time goes in v5:
time: 144 us; the launch traced here: 143 us
  Pallas kernels  65.9 us (46%)
  waiting for transfers between devices  49.1 us (34%)
  starting transfers between devices  22.8 us (16%)
  local copies, waits for them, and re-layouts  4.87 us (3%)
    pallas_call x14, Pallas kernels, hop(): pl.pallas_call(functools.partial(hop_kernel, received is not None), grid_...  40.3 us
    ppermute x14, waiting for transfers between devices, turn(): arrived[half, sign] = lax.ppermute(last, 'tp', moves)  35.3 us
    ppermute x14, starting transfers between devices, turn(): arrived[half, sign] = lax.ppermute(last, 'tp', moves)  15.8 us
    ppermute x3, waiting for transfers between devices, per_device(): sent = lax.ppermute(low, 'tp', [(i, i ^ apart) for i in range(size)])  13.8 us
    pallas_call x1, Pallas kernels, own_terms(): pl.pallas_call(own_kernel, grid_spec=pltpu.PrefetchScalarGridSpec(num_sca...  8.06 us
    ppermute x3, starting transfers between devices, per_device(): sent = lax.ppermute(low, 'tp', [(i, i ^ apart) for i in range(size)])  6.15 us
    pallas_call x1, Pallas kernels, low_rank(): pl.pallas_call(functools.partial(low_kernel, sizes), grid_spec=pltpu.Pref...  5.87 us
    pallas_call x2, Pallas kernels, collect(): pl.pallas_call(functools.partial(collect_kernel, count), grid_spec=pltpu....  5.33 us
  transfers between devices with their start and end apart: 20, of which 7 were waited for; matrix products, arithmetic and copies ran while one was open for 1% of the time, Pallas kernels for 44%

profile of v5, /device:TPU:0, one launch (start us, length us, event | category | flops | bytes accessed | tf_op | source)
XLA Modules:
  0.0 143.2 jit_solution(10081999332518000970)
XLA Ops:
  2.7 3.6 %shard_map.82.refs_0_ = bf16[768,512]{1,0:T(8,128)(2,1)} custom-call(s32[8]{0:T(128)S(1)} %compare_select_fusion.3.dests, bf16[768,1024]{1,0:T(8,128)(2,1)S(1)} %bitcast.8, bf16[1024,8192]{1,0:T(8,128)(2,1)} %w_ref.29), custom_call_target="tpu_custom_call" | custom-call | flops 24159191040 | bytes 4194304 | tf_op jit(solution)/shard_map/pallas_call | solution.py:73
  8.9 2.8 %shard_map.83.after_ref = bf16[768,512]{1,0:T(8,128)(2,1)S(1)} custom-call(s32[8]{0:T(128)S(1)} %compare_select_fusion.3.dests, bf16[768,1024]{1,0:T(8,128)(2,1)S(1)} %bitcast.9, bf16[1024,8192]{1,0:T(8,128)(2,1)} %w_ref.29, bf16[768,512]{1,0:T(8,128)(2,1)} %shard_map.82.refs_0_), custom_call_target="tpu_custom_call" | custom-call | flops 24159191040 | bytes 4194304 | tf_op jit(solution)/shard_map/pallas_call | solution.py:73
  12.8 2.7 %shard_map.84.refs_0_ = bf16[24,64,1024]{2,1,0:T(8,128)(2,1)S(1)} custom-call(s32[24]{0:T(128)S(1)} %get-tuple-element.9.index, bf16[96,64,1024]{2,1,0:T(8,128)(2,1)} %table_ref.6, bf16[768,512]{1,0:T(8,128)(2,1)S(1)} %shard_map.83.after_ref), custom_call_target="tpu_custom_call" | custom-call | bytes 6291456 | tf_op jit(solution)/shard_map/pallas_call | solution.py:104
  15.7 2.8 %shard_map.85.refs_0_ = bf16[768,512]{1,0:T(8,128)(2,1)S(1)} custom-call(s32[8]{0:T(128)S(1)} %compare_select_fusion.3.dests, bf16[768,1024]{1,0:T(8,128)(2,1)S(1)} %bitcast.10, bf16[1024,8192]{1,0:T(8,128)(2,1)} %w_ref.29, bf16[24,64,1024]{2,1,0:T(8,128)(2,1)S(1)} %shard_map.84.refs_0_), custom_call_target="tpu_custom_call" | custom-call | flops 24159191040 | bytes 4194304 | tf_op jit(solution)/shard_map/pallas_call | solution.py:73
  20.4 2.8 %shard_map.86.after_ref = bf16[768,512]{1,0:T(8,128)(2,1)S(1)} custom-call(s32[8]{0:T(128)S(1)} %compare_select_fusion.3.dests, bf16[768,1024]{1,0:T(8,128)(2,1)S(1)} %bitcast.11, bf16[1024,8192]{1,0:T(8,128)(2,1)} %w_ref.29, bf16[768,512]{1,0:T(8,128)(2,1)S(1)} %shard_map.85.refs_0_), custom_call_target="tpu_custom_call" | custom-call | flops 24159191040 | bytes 4194304 | tf_op jit(solution)/shard_map/pallas_call | solution.py:73
  23.4 2.7 %shard_map.87.after_ref = bf16[24,64,1024]{2,1,0:T(8,128)(2,1)S(1)} custom-call(s32[24]{0:T(128)S(1)} %get-tuple-element.9.index, bf16[96,64,1024]{2,1,0:T(8,128)(2,1)} %table_ref.7, bf16[768,512]{1,0:T(8,128)(2,1)S(1)} %shard_map.86.after_ref), custom_call_target="tpu_custom_call" | custom-call | bytes 6291456 | tf_op jit(solution)/shard_map/pallas_call | solution.py:104
  26.2 5.9 %shard_map.88.refs_1_.one_ref = f32[64,768]{1,0:T(8,128)} custom-call(s32[24]{0:T(128)S(1)} %compare_convert_fusion.local, s32[24]{0:T(128)S(1)} %get-tuple-element.10.index, bf16[768,1024]{1,0:T(8,128)(2,1)S(1)} %bitcast.12, s32[3,256]{1,0:T(4,128)S(1)} %copy-done.5, bf16[96,64,1024]{2,1,0:T(8,128)(2,1)} %table_ref.6, ...), custom_call_target="tpu_custom_call" | custom-call | flops 12079595520 | bytes 4718592 | tf_op jit(solution)/shard_map/pallas_call | solution.py:162
  33.9 3.0 %shard_map.89.refs_1_ = bf16[768,512]{1,0:T(8,128)(2,1)S(1)} custom-call(s32[8]{0:T(128)S(1)} %compare_select_fusion.3.dests, bf16[768,1024]{1,0:T(8,128)(2,1)S(1)} %bitcast.13, bf16[1024,8192]{1,0:T(8,128)(2,1)} %w_ref.29, bf16[768,512]{1,0:T(8,128)(2,1)} %collective-permute-done.3.refs_0_, f32[64,768]{1,0:T(8,128)} %shard_map.88.refs_1_.one_ref), custom_call_target="tpu_custom_call" | custom-call | flops 24159191040 | bytes 4194304 | tf_op jit(solution)/shard_map/pallas_call | solution.py:73
  38.6 2.8 %shard_map.90.after_ref = bf16[768,512]{1,0:T(8,128)(2,1)S(1)} custom-call(s32[8]{0:T(128)S(1)} %compare_select_fusion.3.dests, bf16[768,1024]{1,0:T(8,128)(2,1)S(1)} %bitcast.14, bf16[1024,8192]{1,0:T(8,128)(2,1)} %w_ref.29, bf16[768,512]{1,0:T(8,128)(2,1)S(1)} %collective-permute-done.2.refs_0_, bf16[768,512]{1,0:T(8,128)(2,1)S(1)} %shard_map.89.refs_1_), custom_call_target="tpu_custom_call" | custom-call | flops 24159191040 | bytes 4194304 | tf_op jit(solution)/shard_map/pallas_call | solution.py:73
  41.9 8.1 %shard_map.91 = (f32[768,1024]{1,0:T(8,128)S(1)}, bf16[24,64,1024]{2,1,0:T(8,128)(2,1)S(1)}) custom-call(s32[24]{0:T(128)S(1)} %compare_convert_fusion.local, s32[24]{0:T(128)S(1)} %get-tuple-element.10.index, s32[8]{0:T(128)S(1)} %compare_select_fusion.3.dests, bf16[768,1024]{1,0:T(8,128)(2,1)S(1)} %bitcast.15, bf16[1024,8192]{1,0:T(8,128)(2,1)} %w_ref.29, ...), custom_call_target="tpu_custom_call" | custom-call | flops 48318382080 | bytes 13107200 | tf_op jit(solution)/shard_map/pallas_call | solution.py:217
  50.0 3.2 %shard_map.92.refs_1_ = bf16[768,512]{1,0:T(8,128)(2,1)S(1)} custom-call(s32[8]{0:T(128)S(1)} %compare_select_fusion.3.dests, bf16[768,1024]{1,0:T(8,128)(2,1)S(1)} %bitcast.16, bf16[1024,8192]{1,0:T(8,128)(2,1)} %w_ref.29, bf16[768,512]{1,0:T(8,128)(2,1)S(1)} %collective-permute-done.7.refs_0_, f32[768,1024]{1,0:T(8,128)S(1)} %get-tuple-element.7.refs_1_.own_ref), custom_call_target="tpu_custom_call" | custom-call | flops 24159191040 | bytes 4194304 | tf_op jit(solution)/shard_map/pallas_call | solution.py:73
  56.5 2.8 %shard_map.93.after_ref = bf16[768,512]{1,0:T(8,128)(2,1)S(1)} custom-call(s32[8]{0:T(128)S(1)} %compare_select_fusion.3.dests, bf16[768,1024]{1,0:T(8,128)(2,1)S(1)} %bitcast.17, bf16[1024,8192]{1,0:T(8,128)(2,1)} %w_ref.29, bf16[768,512]{1,0:T(8,128)(2,1)S(1)} %collective-permute-done.6.refs_0_, bf16[768,512]{1,0:T(8,128)(2,1)S(1)} %shard_map.92.refs_1_), custom_call_target="tpu_custom_call" | custom-call | flops 24159191040 | bytes 4194304 | tf_op jit(solution)/shard_map/pallas_call | solution.py:73
  62.5 2.9 %collective-permute-done.10.refs_0_ = bf16[768,512]{1,0:T(8,128)(2,1)S(1)} collective-permute-done((bf16[768,512]{1,0:T(8,128)(2,1)S(1)}, bf16[768,512]{1,0:T(8,128)(2,1)S(1)}, u32[]{:S(2)}, u32[]{:S(2)}) %collective-permute-start.10) | collective-permute-done | bytes 786464 | tf_op jit(solution)/shard_map/ppermute | solution.py:350
  65.3 2.8 %shard_map.95.refs_1_ = bf16[768,512]{1,0:T(8,128)(2,1)S(1)} custom-call(s32[8]{0:T(128)S(1)} %compare_select_fusion.3.dests, bf16[768,1024]{1,0:T(8,128)(2,1)S(1)} %bitcast.18, bf16[1024,8192]{1,0:T(8,128)(2,1)} %w_ref.29, bf16[768,512]{1,0:T(8,128)(2,1)S(1)} %collective-permute-done.10.refs_0_, f32[64,768]{1,0:T(8,128)S(1)} %shard_map.94.refs_1_.one_ref), custom_call_target="tpu_custom_call" | custom-call | flops 24159191040 | bytes 4194304 | tf_op jit(solution)/shard_map/pallas_call | solution.py:73
  68.2 2.8 %shard_map.96.after_ref = bf16[768,512]{1,0:T(8,128)(2,1)S(1)} custom-call(s32[8]{0:T(128)S(1)} %compare_select_fusion.3.dests, bf16[768,1024]{1,0:T(8,128)(2,1)S(1)} %bitcast.19, bf16[1024,8192]{1,0:T(8,128)(2,1)} %w_ref.29, bf16[768,512]{1,0:T(8,128)(2,1)S(1)} %collective-permute-done.9.refs_0_, bf16[768,512]{1,0:T(8,128)(2,1)S(1)} %shard_map.95.refs_1_), custom_call_target="tpu_custom_call" | custom-call | flops 24159191040 | bytes 4194304 | tf_op jit(solution)/shard_map/pallas_call | solution.py:73
  73.0 13.8 %collective-permute-done.8.two_ref = f32[64,768]{1,0:T(8,128)S(1)} collective-permute-done((f32[64,768]{1,0:T(8,128)S(1)}, f32[64,768]{1,0:T(8,128)S(1)}, u32[]{:S(2)}, u32[]{:S(2)}) %collective-permute-start.8) | collective-permute-done | bytes 196640 | tf_op jit(solution)/shard_map/ppermute | solution.py:380
  86.9 2.7 %collective-permute-start.11 = (f32[64,768]{1,0:T(8,128)S(1)}, f32[64,768]{1,0:T(8,128)S(1)}, u32[]{:S(2)}, u32[]{:S(2)}) collective-permute-start(f32[64,768]{1,0:T(8,128)S(1)} %shard_map.97.refs_1_.one_ref), channel_id=1, source_target_pairs={{0,4},{1,5},{2,6},{3,7},{4,0},{5,1},{6,2},{7,3},{8,12},{9,13},{10,... | collective-permute-start | bytes 589832 | tf_op jit(solution)/shard_map/ppermute | solution.py:380
  89.6 2.8 %shard_map.98.refs_1_ = bf16[768,512]{1,0:T(8,128)(2,1)S(1)} custom-call(s32[8]{0:T(128)S(1)} %compare_select_fusion.3.dests, bf16[768,1024]{1,0:T(8,128)(2,1)S(1)} %bitcast.20, bf16[1024,8192]{1,0:T(8,128)(2,1)} %w_ref.29, bf16[768,512]{1,0:T(8,128)(2,1)S(1)} %collective-permute-done.15.refs_0_, f32[64,768]{1,0:T(8,128)S(1)} %shard_map.97.refs_1_.one_ref), custom_call_target="tpu_custom_call" | custom-call | flops 24159191040 | bytes 4194304 | tf_op jit(solution)/shard_map/pallas_call | solution.py:73
  92.4 2.8 %shard_map.99.refs_1_ = bf16[768,512]{1,0:T(8,128)(2,1)S(1)} custom-call(s32[8]{0:T(128)S(1)} %compare_select_fusion.3.dests, bf16[768,1024]{1,0:T(8,128)(2,1)S(1)} %bitcast.21, bf16[1024,8192]{1,0:T(8,128)(2,1)} %w_ref.29, bf16[768,512]{1,0:T(8,128)(2,1)S(1)} %collective-permute-done.14.refs_0_, bf16[768,512]{1,0:T(8,128)(2,1)S(1)} %shard_map.98.refs_1_), custom_call_target="tpu_custom_call" | custom-call | flops 24159191040 | bytes 4194304 | tf_op jit(solution)/shard_map/pallas_call | solution.py:73
  99.1 2.8 %shard_map.100.refs_1_ = bf16[768,512]{1,0:T(8,128)(2,1)S(1)} custom-call(s32[8]{0:T(128)S(1)} %compare_select_fusion.3.dests, bf16[768,1024]{1,0:T(8,128)(2,1)S(1)} %bitcast.22, bf16[1024,8192]{1,0:T(8,128)(2,1)} %w_ref.29, bf16[768,512]{1,0:T(8,128)(2,1)S(1)} %collective-permute-done.13.refs_0_, bf16[768,512]{1,0:T(8,128)(2,1)S(1)} %shard_map.99.refs_1_), custom_call_target="tpu_custom_call" | custom-call | flops 24159191040 | bytes 4194304 | tf_op jit(solution)/shard_map/pallas_call | solution.py:73
  103.9 4.0 %collective-permute-done.12.refs_0_ = bf16[768,512]{1,0:T(8,128)(2,1)S(1)} collective-permute-done((bf16[768,512]{1,0:T(8,128)(2,1)S(1)}, bf16[768,512]{1,0:T(8,128)(2,1)S(1)}, u32[]{:S(2)}, u32[]{:S(2)}) %collective-permute-start.12) | collective-permute-done | bytes 786464 | tf_op jit(solution)/shard_map/ppermute | solution.py:350
  107.9 2.8 %shard_map.101.after_ref = bf16[768,512]{1,0:T(8,128)(2,1)S(1)} custom-call(s32[8]{0:T(128)S(1)} %compare_select_fusion.3.dests, bf16[768,1024]{1,0:T(8,128)(2,1)S(1)} %bitcast.23, bf16[1024,8192]{1,0:T(8,128)(2,1)} %w_ref.29, bf16[768,512]{1,0:T(8,128)(2,1)S(1)} %collective-permute-done.12.refs_0_, bf16[768,512]{1,0:T(8,128)(2,1)S(1)} %shard_map.100.refs_1_), custom_call_target="tpu_custom_call" | custom-call | flops 24159191040 | bytes 4194304 | tf_op jit(solution)/shard_map/pallas_call | solution.py:73
  112.0 12.7 %collective-permute-done.19.two_ref = bf16[768,512]{1,0:T(8,128)(2,1)S(1)} collective-permute-done((bf16[768,512]{1,0:T(8,128)(2,1)S(1)}, bf16[768,512]{1,0:T(8,128)(2,1)S(1)}, u32[]{:S(2)}, u32[]{:S(2)}) %collective-permute-start.19) | collective-permute-done | bytes 786464 | tf_op jit(solution)/shard_map/ppermute | solution.py:350
  124.8 11.4 %collective-permute-done.18.one_ref = bf16[768,512]{1,0:T(8,128)(2,1)S(1)} collective-permute-done((bf16[768,512]{1,0:T(8,128)(2,1)S(1)}, bf16[768,512]{1,0:T(8,128)(2,1)S(1)}, u32[]{:S(2)}, u32[]{:S(2)}) %collective-permute-start.18) | collective-permute-done | bytes 786464 | tf_op jit(solution)/shard_map/ppermute | solution.py:350
  (74 shorter events, 35.8 us)
Async XLA Ops:
  0.0 11.9 %copy-start = (s32[192]{0:T(256)S(1)}, s32[192]{0:T(256)}, u32[]{:S(2)}) copy-start(s32[192]{0:T(256)} %param.12) | copy-start | bytes 2308
  0.8 11.0 %collective-permute-start = (s32[24]{0:T(128)S(1)}, s32[24]{0:T(128)S(1)}, u32[]{:S(2)}, u32[]{:S(2)}) collective-permute-start(s32[24]{0:T(128)S(1)} %reshape.98), channel_id=1, source_target_pairs={{0,8},{8,0},{1,9},{9,1},{2,10},{10,2},{3,11},{11,3},{4,12},{12,4},... | collective-permute-start | bytes 296 | tf_op jit(solution)/shard_map/ppermute | solution.py:354
  6.3 25.8 %collective-permute-start.3 = (bf16[768,512]{1,0:T(8,128)(2,1)}, bf16[768,512]{1,0:T(8,128)(2,1)}, u32[]{:S(2)}, u32[]{:S(2)}) collective-permute-start(bf16[768,512]{1,0:T(8,128)(2,1)} %shard_map.82.refs_0_), channel_id=1, source_target_pairs={{0,2},{2,4},{4,6},{6,7},{7,5},{5,3},{3,1},{1,0},{8,10},{10,12},{12... | collective-permute-start | bytes 2359304 | tf_op jit(solution)/shard_map/ppermute | solution.py:350
  11.7 25.3 %collective-permute-start.2 = (bf16[768,512]{1,0:T(8,128)(2,1)S(1)}, bf16[768,512]{1,0:T(8,128)(2,1)S(1)}, u32[]{:S(2)}, u32[]{:S(2)}) collective-permute-start(bf16[768,512]{1,0:T(8,128)(2,1)S(1)} %shard_map.83.after_ref), channel_id=1, source_target_pairs={{0,1},{2,0},{4,2},{6,4},{7,6},{5,7},{3,5},{1,3},{8,9},{10,8},{12,1... | collective-permute-start | bytes 2359304 | tf_op jit(solution)/shard_map/ppermute | solution.py:350
  15.5 10.7 %collective-permute-start.4 = (bf16[24,64,1024]{2,1,0:T(8,128)(2,1)S(1)}, bf16[24,64,1024]{2,1,0:T(8,128)(2,1)S(1)}, u32[]{:S(2)}, u32[]{:S(2)}) collective-permute-start(bf16[24,64,1024]{2,1,0:T(8,128)(2,1)S(1)} %shard_map.84.refs_0_), channel_id=1, source_target_pairs={{0,8},{8,0},{1,9},{9,1},{2,10},{10,2},{3,11},{11,3},{4,12},{12,4},... | collective-permute-start | bytes 9437192 | tf_op jit(solution)/shard_map/ppermute | solution.py:361
  18.5 31.5 %collective-permute-start.7 = (bf16[768,512]{1,0:T(8,128)(2,1)S(1)}, bf16[768,512]{1,0:T(8,128)(2,1)S(1)}, u32[]{:S(2)}, u32[]{:S(2)}) collective-permute-start(bf16[768,512]{1,0:T(8,128)(2,1)S(1)} %shard_map.85.refs_0_), channel_id=1, source_target_pairs={{0,2},{2,4},{4,6},{6,7},{7,5},{5,3},{3,1},{1,0},{8,10},{10,12},{12... | collective-permute-start | bytes 2359304 | tf_op jit(solution)/shard_map/ppermute | solution.py:350
  23.2 33.3 %collective-permute-start.6 = (bf16[768,512]{1,0:T(8,128)(2,1)S(1)}, bf16[768,512]{1,0:T(8,128)(2,1)S(1)}, u32[]{:S(2)}, u32[]{:S(2)}) collective-permute-start(bf16[768,512]{1,0:T(8,128)(2,1)S(1)} %shard_map.86.after_ref), channel_id=1, source_target_pairs={{0,1},{2,0},{4,2},{6,4},{7,6},{5,7},{3,5},{1,3},{8,9},{10,8},{12,1... | collective-permute-start | bytes 2359304 | tf_op jit(solution)/shard_map/ppermute | solution.py:350
  26.1 15.3 %collective-permute-start.1 = (bf16[24,64,1024]{2,1,0:T(8,128)(2,1)S(1)}, bf16[24,64,1024]{2,1,0:T(8,128)(2,1)S(1)}, u32[]{:S(2)}, u32[]{:S(2)}) collective-permute-start(bf16[24,64,1024]{2,1,0:T(8,128)(2,1)S(1)} %shard_map.87.after_ref), channel_id=1, source_target_pairs={{0,8},{8,0},{1,9},{9,1},{2,10},{10,2},{3,11},{11,3},{4,12},{12,4},... | collective-permute-start | bytes 9437192 | tf_op jit(solution)/shard_map/ppermute | solution.py:364
  32.1 27.7 %collective-permute-start.5 = (f32[64,768]{1,0:T(8,128)}, f32[64,768]{1,0:T(8,128)}, u32[]{:S(2)}, u32[]{:S(2)}) collective-permute-start(f32[64,768]{1,0:T(8,128)} %shard_map.88.refs_1_.one_ref), channel_id=1, source_target_pairs={{0,1},{1,0},{2,3},{3,2},{4,5},{5,4},{6,7},{7,6},{8,9},{9,8},{10,11... | collective-permute-start | bytes 589832 | tf_op jit(solution)/shard_map/ppermute | solution.py:380
  37.0 28.3 %collective-permute-start.10 = (bf16[768,512]{1,0:T(8,128)(2,1)S(1)}, bf16[768,512]{1,0:T(8,128)(2,1)S(1)}, u32[]{:S(2)}, u32[]{:S(2)}) collective-permute-start(bf16[768,512]{1,0:T(8,128)(2,1)S(1)} %shard_map.89.refs_1_), channel_id=1, source_target_pairs={{0,2},{2,4},{4,6},{6,7},{7,5},{5,3},{3,1},{1,0},{8,10},{10,12},{12... | collective-permute-start | bytes 2359304 | tf_op jit(solution)/shard_map/ppermute | solution.py:350
  41.4 26.8 %collective-permute-start.9 = (bf16[768,512]{1,0:T(8,128)(2,1)S(1)}, bf16[768,512]{1,0:T(8,128)(2,1)S(1)}, u32[]{:S(2)}, u32[]{:S(2)}) collective-permute-start(bf16[768,512]{1,0:T(8,128)(2,1)S(1)} %shard_map.90.after_ref), channel_id=1, source_target_pairs={{0,1},{2,0},{4,2},{6,4},{7,6},{5,7},{3,5},{1,3},{8,9},{10,8},{12,1... | collective-permute-start | bytes 2359304 | tf_op jit(solution)/shard_map/ppermute | solution.py:350
  54.9 34.6 %collective-permute-start.15 = (bf16[768,512]{1,0:T(8,128)(2,1)S(1)}, bf16[768,512]{1,0:T(8,128)(2,1)S(1)}, u32[]{:S(2)}, u32[]{:S(2)}) collective-permute-start(bf16[768,512]{1,0:T(8,128)(2,1)S(1)} %shard_map.92.refs_1_), channel_id=1, source_target_pairs={{0,2},{2,4},{4,6},{6,7},{7,5},{5,3},{3,1},{1,0},{8,10},{10,12},{12... | collective-permute-start | bytes 2359304 | tf_op jit(solution)/shard_map/ppermute | solution.py:350
  59.3 33.1 %collective-permute-start.14 = (bf16[768,512]{1,0:T(8,128)(2,1)S(1)}, bf16[768,512]{1,0:T(8,128)(2,1)S(1)}, u32[]{:S(2)}, u32[]{:S(2)}) collective-permute-start(bf16[768,512]{1,0:T(8,128)(2,1)S(1)} %shard_map.93.after_ref), channel_id=1, source_target_pairs={{0,1},{2,0},{4,2},{6,4},{7,6},{5,7},{3,5},{1,3},{8,9},{10,8},{12,1... | collective-permute-start | bytes 2359304 | tf_op jit(solution)/shard_map/ppermute | solution.py:350
  60.8 26.1 %collective-permute-start.8 = (f32[64,768]{1,0:T(8,128)S(1)}, f32[64,768]{1,0:T(8,128)S(1)}, u32[]{:S(2)}, u32[]{:S(2)}) collective-permute-start(f32[64,768]{1,0:T(8,128)S(1)} %shard_map.94.refs_1_.one_ref), channel_id=1, source_target_pairs={{0,2},{1,3},{2,0},{3,1},{4,6},{5,7},{6,4},{7,5},{8,10},{9,11},{10,... | collective-permute-start | bytes 589832 | tf_op jit(solution)/shard_map/ppermute | solution.py:380
  68.1 30.9 %collective-permute-start.13 = (bf16[768,512]{1,0:T(8,128)(2,1)S(1)}, bf16[768,512]{1,0:T(8,128)(2,1)S(1)}, u32[]{:S(2)}, u32[]{:S(2)}) collective-permute-start(bf16[768,512]{1,0:T(8,128)(2,1)S(1)} %shard_map.95.refs_1_), channel_id=1, source_target_pairs={{0,2},{2,4},{4,6},{6,7},{7,5},{5,3},{3,1},{1,0},{8,10},{10,12},{12... | collective-permute-start | bytes 2359304 | tf_op jit(solution)/shard_map/ppermute | solution.py:350
  71.0 36.9 %collective-permute-start.12 = (bf16[768,512]{1,0:T(8,128)(2,1)S(1)}, bf16[768,512]{1,0:T(8,128)(2,1)S(1)}, u32[]{:S(2)}, u32[]{:S(2)}) collective-permute-start(bf16[768,512]{1,0:T(8,128)(2,1)S(1)} %shard_map.96.after_ref), channel_id=1, source_target_pairs={{0,1},{2,0},{4,2},{6,4},{7,6},{5,7},{3,5},{1,3},{8,9},{10,8},{12,1... | collective-permute-start | bytes 2359304 | tf_op jit(solution)/shard_map/ppermute | solution.py:350
  86.9 24.4 %collective-permute-start.11 = (f32[64,768]{1,0:T(8,128)S(1)}, f32[64,768]{1,0:T(8,128)S(1)}, u32[]{:S(2)}, u32[]{:S(2)}) collective-permute-start(f32[64,768]{1,0:T(8,128)S(1)} %shard_map.97.refs_1_.one_ref), channel_id=1, source_target_pairs={{0,4},{1,5},{2,6},{3,7},{4,0},{5,1},{6,2},{7,3},{8,12},{9,13},{10,... | collective-permute-start | bytes 589832 | tf_op jit(solution)/shard_map/ppermute | solution.py:380
  92.3 46.1 %collective-permute-start.16 = (bf16[768,512]{1,0:T(8,128)(2,1)S(1)}, bf16[768,512]{1,0:T(8,128)(2,1)S(1)}, u32[]{:S(2)}, u32[]{:S(2)}) collective-permute-start(bf16[768,512]{1,0:T(8,128)(2,1)S(1)} %shard_map.98.refs_1_), channel_id=1, source_target_pairs={{0,2},{2,4},{4,6},{6,7},{7,5},{5,3},{3,1},{1,0},{8,10},{10,12},{12... | collective-permute-start | bytes 2359304 | tf_op jit(solution)/shard_map/ppermute | solution.py:350
  95.2 29.6 %collective-permute-start.19 = (bf16[768,512]{1,0:T(8,128)(2,1)S(1)}, bf16[768,512]{1,0:T(8,128)(2,1)S(1)}, u32[]{:S(2)}, u32[]{:S(2)}) collective-permute-start(bf16[768,512]{1,0:T(8,128)(2,1)S(1)} %shard_map.99.refs_1_), channel_id=1, source_target_pairs={{0,1},{2,0},{4,2},{6,4},{7,6},{5,7},{3,5},{1,3},{8,9},{10,8},{12,1... | collective-permute-start | bytes 2359304 | tf_op jit(solution)/shard_map/ppermute | solution.py:350
  101.8 9.5 %copy-start.6 = (s32[3,256]{1,0:T(4,128)S(1)}, s32[3,256]{1,0:T(4,128)}, u32[]{:S(2)}) copy-start(s32[3,256]{1,0:T(4,128)} %place_ref.3) | copy-start | bytes 9220
  101.8 9.5 %copy-start.8 = (f32[768,1024]{1,0:T(8,128)S(1)}, f32[768,1024]{1,0:T(8,128)}, u32[]{:S(2)}) copy-start(f32[768,1024]{1,0:T(8,128)} %copy-done.7) | copy-start | bytes 9437188
  101.9 34.3 %collective-permute-start.18 = (bf16[768,512]{1,0:T(8,128)(2,1)S(1)}, bf16[768,512]{1,0:T(8,128)(2,1)S(1)}, u32[]{:S(2)}, u32[]{:S(2)}) collective-permute-start(bf16[768,512]{1,0:T(8,128)(2,1)S(1)} %shard_map.100.refs_1_), channel_id=1, source_target_pairs={{0,2},{2,4},{4,6},{6,7},{7,5},{5,3},{3,1},{1,0},{8,10},{10,12},{12... | collective-permute-start | bytes 2359304 | tf_op jit(solution)/shard_map/ppermute | solution.py:350
  110.7 30.2 %collective-permute-start.17 = (bf16[768,512]{1,0:T(8,128)(2,1)S(1)}, bf16[768,512]{1,0:T(8,128)(2,1)S(1)}, u32[]{:S(2)}, u32[]{:S(2)}) collective-permute-start(bf16[768,512]{1,0:T(8,128)(2,1)S(1)} %shard_map.101.after_ref), channel_id=1, source_target_pairs={{0,1},{2,0},{4,2},{6,4},{7,6},{5,7},{3,5},{1,3},{8,9},{10,8},{12,1... | collective-permute-start | bytes 2359304 | tf_op jit(solution)/shard_map/ppermute | solution.py:350
  111.3 24.8 %copy-start.2 = (s32[3,1]{0,1:T(1,128)S(1)}, s32[3,1]{0,1:T(1,128)}, u32[]{:S(2)}) copy-start(s32[3,1]{0,1:T(1,128)} %param.15) | copy-start | bytes 40
  (8 other events, 34.3 us)

commit v6 on v5

--- a/solution.py
+++ b/solution.py
@@ -135,63 +135,73 @@
 
 
 def low_kernel(
-    sizes, local, index, x_ref, place_ref, table_ref, got_ref, after_ref, out_ref, pages, sems
+    sizes, local, index, side, x_ref, place_ref, table_ref, got_ref, after_ref, keep_ref, give_ref,
+    pages, sems,
 ):
     steps, blocks, listed, rank, block_rows = sizes
+    half = steps * blocks // 2
     load_pages(steps * blocks * listed, local, index, table_ref, got_ref, pages, sems)
     for step in range(steps):
         for block in range(blocks):
             at = step * blocks + block
-            rows = slice(at * block_rows, (at + 1) * block_rows)
             listing = pages[at * listed : (at + 1) * listed].reshape(listed * rank, -1)
             every = lax.dot_general(
-                listing, x_ref[rows, :], (((1,), (1,)), ((), ())),
-                preferred_element_type=jnp.float32,
+                listing, x_ref[at * block_rows : (at + 1) * block_rows, :],
+                (((1,), (1,)), ((), ())), preferred_element_type=jnp.float32,
             )
             place = place_ref[step : step + 1, block * block_rows : (block + 1) * block_rows]
             low = jnp.zeros((rank, block_rows), jnp.float32)
             for entry in range(listed):
                 low = jnp.where(place == entry, every[entry * rank : (entry + 1) * rank], low)
-            out_ref[:, rows] = low
-
-
-def low_rank(sizes, local, index, x, place, table, got, after):
+            rows = slice(at % half * block_rows, (at % half + 1) * block_rows)
+            mine = side[0] == at // half
+
+            @pl.when(mine)
+            def _():
+                keep_ref[:, rows] = low
+
+            @pl.when(jnp.logical_not(mine))
+            def _():
+                give_ref[:, rows] = low
+
+
+def low_rank(sizes, local, index, side, x, place, table, got, after):
     steps, blocks, listed, rank, block_rows = sizes
     count = steps * blocks * listed
     rows, depth = x.shape
     return pl.pallas_call(
         functools.partial(low_kernel, sizes),
         grid_spec=pltpu.PrefetchScalarGridSpec(
-            num_scalar_prefetch=2,
+            num_scalar_prefetch=3,
             grid=(1,),
             in_specs=[WHOLE, WHOLE, ANYWHERE, ANYWHERE, ANYWHERE],
-            out_specs=WHOLE,
+            out_specs=[WHOLE, WHOLE],
             scratch_shapes=[
                 pltpu.VMEM((count, rank, depth), table.dtype),
                 pltpu.SemaphoreType.DMA((count,)),
             ],
         ),
-        out_shape=jax.ShapeDtypeStruct((rank, rows), jnp.float32),
+        out_shape=[jax.ShapeDtypeStruct((rank, rows // 2), jnp.float32)] * 2,
         compiler_params=params(),
         cost_estimate=cost(
             2 * rows * depth * listed * rank, 2 * (rows * depth + count * rank * depth)
         ),
-    )(local, index, x, place, table, got, after)
-
-
-def add_kernel(one_ref, two_ref, after_ref, out_ref):
-    out_ref[...] = one_ref[...] + two_ref[...]
-
-
-def add(one, two, after):
+    )(local, index, side, x, place, table, got, after)
+
+
+def add_kernel(low_ref, sent_ref, after_ref, out_ref):
+    out_ref[...] = (low_ref[...] + sent_ref[...]).astype(out_ref.dtype)
+
+
+def add(low, sent, dtype, after):
     return pl.pallas_call(
         add_kernel,
         in_specs=[WHOLE, WHOLE, ANYWHERE],
         out_specs=WHOLE,
-        out_shape=jax.ShapeDtypeStruct(one.shape, one.dtype),
-        compiler_params=params(),
-        cost_estimate=cost(one.size, 12 * one.size),
-    )(one, two, after)
+        out_shape=jax.ShapeDtypeStruct(low.shape, dtype),
+        compiler_params=params(),
+        cost_estimate=cost(low.size, 12 * low.size),
+    )(low, sent, after)
 
 
 def own_kernel(
@@ -241,14 +251,22 @@
     )(local, index, dests, x, weight, table, got, after)
 
 
-def delta_kernel(sizes, own_ref, pages_ref, place_ref, low_ref, after_ref, out_ref):
+def delta_kernel(
+    sizes, side, own_ref, pages_ref, place_ref, low_ref, other_ref, after_ref, out_ref
+):
     steps, blocks, listed, rank, block_rows = sizes
+    half = steps * blocks // 2
     entry_of = lax.broadcasted_iota(jnp.int32, (listed * rank, block_rows), 0) // rank
     for step in range(steps):
         for block in range(blocks):
             at = step * blocks + block
             rows = slice(at * block_rows, (at + 1) * block_rows)
-            low = low_ref[:, rows]
+            in_half = slice(at % half * block_rows, (at % half + 1) * block_rows)
+            low = jnp.where(
+                side[0] == at // half,
+                low_ref[:, in_half].astype(jnp.float32),
+                other_ref[:, in_half].astype(jnp.float32),
+            )
             spread = jnp.concatenate([low] * listed, axis=0)
             place = place_ref[step : step + 1, block * block_rows : (block + 1) * block_rows]
             spread = jnp.where(entry_of == place, spread, 0.0)
@@ -258,38 +276,42 @@
             )
 
 
-def add_delta(sizes, own, pages, place, low, after):
+def add_delta(sizes, side, own, pages, place, low, other, after):
     rows, cols = own.shape
     return pl.pallas_call(
         functools.partial(delta_kernel, sizes),
-        in_specs=[WHOLE, WHOLE, WHOLE, WHOLE, ANYWHERE],
-        out_specs=WHOLE,
+        grid_spec=pltpu.PrefetchScalarGridSpec(
+            num_scalar_prefetch=1,
+            grid=(1,),
+            in_specs=[WHOLE] * 5 + [ANYWHERE],
+            out_specs=WHOLE,
+        ),
         out_shape=jax.ShapeDtypeStruct(own.shape, own.dtype),
         compiler_params=params(),
         cost_estimate=cost(
             2 * rows * cols * sizes[2] * sizes[3], 8 * rows * cols + 2 * pages.size
         ),
-    )(own, pages, place, low, after)
-
-
-def finish_kernel(live, own_ref, one_ref, two_ref, *refs):
+    )(side, own, pages, place, low, other, after)
+
+
+def finish_kernel(half, live, own_ref, one_ref, two_ref, *refs):
     out_ref = refs[-1]
+    count, cols = out_ref.shape
+    step = pl.program_id(0)
+    rows = pl.ds(pl.multiple_of(step * count, count), count)
     total = (
-        own_ref[...] + one_ref[...].astype(jnp.float32) + two_ref[...].astype(jnp.float32)
+        own_ref[rows, half * cols : (half + 1) * cols]
+        + one_ref[rows, :].astype(jnp.float32)
+        + two_ref[rows, :].astype(jnp.float32)
     )
     row = lax.broadcasted_iota(jnp.int32, total.shape, 0)
-    out_ref[...] = jnp.where(row < live[pl.program_id(0)], total, 0.0).astype(out_ref.dtype)
+    out_ref[...] = jnp.where(row < live[step], total, 0.0).astype(out_ref.dtype)
 
 
 def finish(live, half, own, one, two, result):
     rows, cols = own.shape
     steps = live.shape[0]
-    block = (rows // steps, cols // 2)
-    in_specs = [
-        pl.BlockSpec(block, lambda s, l: (s, half)),
-        pl.BlockSpec(block, lambda s, l: (s, 0)),
-        pl.BlockSpec(block, lambda s, l: (s, 0)),
-    ]
+    in_specs = [WHOLE, WHOLE, WHOLE]
     operands = [own, one, two]
     aliases = {}
     if result is not None:
@@ -297,12 +319,12 @@
         operands.append(result)
         aliases = {4: 0}
     return pl.pallas_call(
-        finish_kernel,
+        functools.partial(finish_kernel, half),
         grid_spec=pltpu.PrefetchScalarGridSpec(
             num_scalar_prefetch=1,
             grid=(steps,),
             in_specs=in_specs,
-            out_specs=pl.BlockSpec(block, lambda s, l: (s, half)),
+            out_specs=pl.BlockSpec((rows // steps, cols // 2), lambda s, l: (s, half)),
         ),
         out_shape=jax.ShapeDtypeStruct((rows, cols), jnp.bfloat16),
         input_output_aliases=aliases,
@@ -362,33 +384,34 @@
     last = turn(1, last)
     last = collect(index_there, adapter_up_weight, last)
     got_up = lax.ppermute(last, "inst", SWAP)
-    low = last = low_rank(
-        sizes, local, index, x, row_list_position, adapter_down_weight, got_down, last
+    side = (lax.axis_index("tp") & 1).reshape(1)
+    low, give = low_rank(
+        sizes, local, index, side, x, row_list_position, adapter_down_weight, got_down, last
     )
-
-    last = turn(2, last)
-    own, up_pages = own_terms(
-        dests, local, index, x, output_weight, adapter_up_weight, got_up, last
-    )
-    last = own
-    number, turns = 3, 2 * far - 1
-    if size & (size - 1):
-        low = lax.psum(low, "tp")
-    else:
-        apart = 1
-        while apart < size:
-            sent = lax.ppermute(low, "tp", [(i, i ^ apart) for i in range(size)])
-            apart *= 2
-            for _ in range(1 if apart < size else 2):
-                if number < turns:
-                    last = turn(number, last)
-                    number += 1
-            low = last = add(low, sent, last)
-    while number < turns:
+    last = low
+
+    def over(value, apart):
+        return lax.ppermute(value, "tp", [(i, i ^ apart) for i in range(size)])
+
+    number, turns = 2, 2 * far - 1
+    apart = 1
+    while apart < size:
+        sent = over(give if apart == 1 else low, apart)
         last = turn(number, last)
         number += 1
-    low = low.astype(jnp.bfloat16).astype(jnp.float32)
-    own = add_delta(sizes, own, up_pages, row_list_position, low, last)
+        if apart == 1:
+            own, up_pages = own_terms(
+                dests, local, index, x, output_weight, adapter_up_weight, got_up, last
+            )
+            last = own
+        apart *= 2
+        while apart == size and number < turns - 1:
+            last = turn(number, last)
+            number += 1
+        low = last = add(low, sent, jnp.float32 if apart < size else jnp.bfloat16, last)
+    other = over(low, 1)
+    last = turn(number, last)
+    own = add_delta(sizes, side, own, up_pages, row_list_position, low, other, last)
     result = None
     for half in range(2):
         result = finish(

time: 144 us -> 139 us (0.965)
  waiting for transfers between devices: 49.1 us -> 42.7 us
  starting transfers between devices: 22.8 us -> 25.2 us
    ppermute x14, waiting for transfers between devices: 35.3 us -> 27.3 us  [turn(): arrived[half, sign] = lax.ppermute(last, 'tp', moves)]
    ppermute x3 -> x4, starting transfers between devices: 6.15 us -> 8.18 us  [over(): return lax.ppermute(value, 'tp', [(i, i ^ apart) for i in range(size)])]
    ppermute x3 -> x4, waiting for transfers between devices: 13.8 us -> 15.3 us  [over(): return lax.ppermute(value, 'tp', [(i, i ^ apart) for i in range(size)])]
  transfers between devices with their start and end apart: 20 -> 21, of which waited for: 7 -> 8; matrix products, arithmetic and copies ran while one was open for 1% -> 1% of each run, Pallas kernels for 44% -> 46%
where the time goes in v6:
time: 139 us
  Pallas kernels  65.8 us (47%)
  waiting for transfers between devices  42.7 us (31%)
  starting transfers between devices  25.2 us (18%)
  local copies, waits for them, and re-layouts  4.8 us (3%)
    pallas_call x14, Pallas kernels, hop(): pl.pallas_call(functools.partial(hop_kernel, received is not None), grid_...  40.7 us
    ppermute x14, waiting for transfers between devices, turn(): arrived[half, sign] = lax.ppermute(last, 'tp', moves)  27.3 us
    ppermute x14, starting transfers between devices, turn(): arrived[half, sign] = lax.ppermute(last, 'tp', moves)  16.2 us
    ppermute x4, waiting for transfers between devices, over(): return lax.ppermute(value, 'tp', [(i, i ^ apart) for i in range(size)])  15.3 us
    ppermute x4, starting transfers between devices, over(): return lax.ppermute(value, 'tp', [(i, i ^ apart) for i in range(size)])  8.18 us
    pallas_call x1, Pallas kernels, own_terms(): pl.pallas_call(own_kernel, grid_spec=pltpu.PrefetchScalarGridSpec(num_sca...  8.01 us
    pallas_call x1, Pallas kernels, low_rank(): pl.pallas_call(functools.partial(low_kernel, sizes), grid_spec=pltpu.Pref...  6.68 us
    pallas_call x2, Pallas kernels, collect(): pl.pallas_call(functools.partial(collect_kernel, count), grid_spec=pltpu....  5.33 us
  transfers between devices with their start and end apart: 21, of which 8 were waited for; matrix products, arithmetic and copies ran while one was open for 1% of the time, Pallas kernels for 46%

profile of v6, /device:TPU:0, one launch (start us, length us, event | category | flops | bytes accessed | tf_op | source)
XLA Modules:
  0.0 138.9 jit_solution(11409459210221047386)
XLA Ops:
  2.7 3.6 %shard_map.82.refs_0_ = bf16[768,512]{1,0:T(8,128)(2,1)} custom-call(s32[8]{0:T(128)S(1)} %compare_select_fusion.3.dests, bf16[768,1024]{1,0:T(8,128)(2,1)S(1)} %bitcast.9, bf16[1024,8192]{1,0:T(8,128)(2,1)} %w_ref.29), custom_call_target="tpu_custom_call" | custom-call | flops 24159191040 | bytes 4194304 | tf_op jit(solution)/shard_map/pallas_call | solution.py:73
  8.9 2.8 %shard_map.83.after_ref = bf16[768,512]{1,0:T(8,128)(2,1)S(1)} custom-call(s32[8]{0:T(128)S(1)} %compare_select_fusion.3.dests, bf16[768,1024]{1,0:T(8,128)(2,1)S(1)} %bitcast.10, bf16[1024,8192]{1,0:T(8,128)(2,1)} %w_ref.29, bf16[768,512]{1,0:T(8,128)(2,1)} %shard_map.82.refs_0_), custom_call_target="tpu_custom_call" | custom-call | flops 24159191040 | bytes 4194304 | tf_op jit(solution)/shard_map/pallas_call | solution.py:73
  12.8 2.7 %shard_map.84.refs_0_ = bf16[24,64,1024]{2,1,0:T(8,128)(2,1)S(1)} custom-call(s32[24]{0:T(128)S(1)} %get-tuple-element.13.index, bf16[96,64,1024]{2,1,0:T(8,128)(2,1)} %table_ref.6, bf16[768,512]{1,0:T(8,128)(2,1)S(1)} %shard_map.83.after_ref), custom_call_target="tpu_custom_call" | custom-call | bytes 6291456 | tf_op jit(solution)/shard_map/pallas_call | solution.py:104
  15.7 3.6 %shard_map.85.refs_0_ = bf16[768,512]{1,0:T(8,128)(2,1)} custom-call(s32[8]{0:T(128)S(1)} %compare_select_fusion.3.dests, bf16[768,1024]{1,0:T(8,128)(2,1)S(1)} %bitcast.11, bf16[1024,8192]{1,0:T(8,128)(2,1)} %w_ref.29, bf16[24,64,1024]{2,1,0:T(8,128)(2,1)S(1)} %shard_map.84.refs_0_), custom_call_target="tpu_custom_call" | custom-call | flops 24159191040 | bytes 4194304 | tf_op jit(solution)/shard_map/pallas_call | solution.py:73
  21.2 2.8 %shard_map.86.after_ref = bf16[768,512]{1,0:T(8,128)(2,1)S(1)} custom-call(s32[8]{0:T(128)S(1)} %compare_select_fusion.3.dests, bf16[768,1024]{1,0:T(8,128)(2,1)S(1)} %bitcast.12, bf16[1024,8192]{1,0:T(8,128)(2,1)} %w_ref.29, bf16[768,512]{1,0:T(8,128)(2,1)} %shard_map.85.refs_0_), custom_call_target="tpu_custom_call" | custom-call | flops 24159191040 | bytes 4194304 | tf_op jit(solution)/shard_map/pallas_call | solution.py:73
  24.2 2.7 %shard_map.87.after_ref = bf16[24,64,1024]{2,1,0:T(8,128)(2,1)S(1)} custom-call(s32[24]{0:T(128)S(1)} %get-tuple-element.13.index, bf16[96,64,1024]{2,1,0:T(8,128)(2,1)} %table_ref.7, bf16[768,512]{1,0:T(8,128)(2,1)S(1)} %shard_map.86.after_ref), custom_call_target="tpu_custom_call" | custom-call | bytes 6291456 | tf_op jit(solution)/shard_map/pallas_call | solution.py:104
  27.0 6.7 %shard_map.88 = (f32[64,384]{1,0:T(8,128)S(1)}, f32[64,384]{1,0:T(8,128)S(1)}) custom-call(s32[24]{0:T(128)S(1)} %compare_convert_fusion.local, s32[24]{0:T(128)S(1)} %get-tuple-element.14.index, s32[1]{0:T(128)} %bitcast.1.side, bf16[768,1024]{1,0:T(8,128)(2,1)S(1)} %bitcast.13, s32[3,256]{1,0:T(4,128)S(1)} %copy-done.7, bf16[96,64,1024]{2,1,0:T(8,128)(2,1)} %table_ref.6, ...), custom_call_target="tpu_custom_call" | custom-call | flops 12079595520 | bytes 4718592 | tf_op jit(solution)/shard_map/pallas_call | solution.py:172
  35.6 3.0 %shard_map.89.refs_1_ = bf16[768,512]{1,0:T(8,128)(2,1)S(1)} custom-call(s32[8]{0:T(128)S(1)} %compare_select_fusion.3.dests, bf16[768,1024]{1,0:T(8,128)(2,1)S(1)} %bitcast.14, bf16[1024,8192]{1,0:T(8,128)(2,1)} %w_ref.29, bf16[768,512]{1,0:T(8,128)(2,1)} %collective-permute-done.3.refs_0_, f32[64,384]{1,0:T(8,128)S(1)} %get-tuple-element.9.refs_1_.low_ref), custom_call_target="tpu_custom_call" | custom-call | flops 24159191040 | bytes 4194304 | tf_op jit(solution)/shard_map/pallas_call | solution.py:73
  40.2 2.8 %shard_map.90.after_ref = bf16[768,512]{1,0:T(8,128)(2,1)S(1)} custom-call(s32[8]{0:T(128)S(1)} %compare_select_fusion.3.dests, bf16[768,1024]{1,0:T(8,128)(2,1)S(1)} %bitcast.15, bf16[1024,8192]{1,0:T(8,128)(2,1)} %w_ref.29, bf16[768,512]{1,0:T(8,128)(2,1)S(1)} %collective-permute-done.2.refs_0_, bf16[768,512]{1,0:T(8,128)(2,1)S(1)} %shard_map.89.refs_1_), custom_call_target="tpu_custom_call" | custom-call | flops 24159191040 | bytes 4194304 | tf_op jit(solution)/shard_map/pallas_call | solution.py:73
  43.5 8.0 %shard_map.91 = (f32[768,1024]{1,0:T(8,128)S(1)}, bf16[24,64,1024]{2,1,0:T(8,128)(2,1)S(1)}) custom-call(s32[24]{0:T(128)S(1)} %compare_convert_fusion.local, s32[24]{0:T(128)S(1)} %get-tuple-element.14.index, s32[8]{0:T(128)S(1)} %compare_select_fusion.3.dests, bf16[768,1024]{1,0:T(8,128)(2,1)S(1)} %bitcast.16, bf16[1024,8192]{1,0:T(8,128)(2,1)} %w_ref.29, ...), custom_call_target="tpu_custom_call" | custom-call | flops 48318382080 | bytes 13107200 | tf_op jit(solution)/shard_map/pallas_call | solution.py:227
  54.9 2.8 %shard_map.93.refs_1_ = bf16[768,512]{1,0:T(8,128)(2,1)S(1)} custom-call(s32[8]{0:T(128)S(1)} %compare_select_fusion.3.dests, bf16[768,1024]{1,0:T(8,128)(2,1)S(1)} %bitcast.17, bf16[1024,8192]{1,0:T(8,128)(2,1)} %w_ref.29, bf16[768,512]{1,0:T(8,128)(2,1)S(1)} %collective-permute-done.8.refs_0_, f32[64,384]{1,0:T(8,128)S(1)} %shard_map.92.refs_1_.low_ref), custom_call_target="tpu_custom_call" | custom-call | flops 24159191040 | bytes 4194304 | tf_op jit(solution)/shard_map/pallas_call | solution.py:73
  58.2 2.8 %shard_map.94.after_ref = bf16[768,512]{1,0:T(8,128)(2,1)S(1)} custom-call(s32[8]{0:T(128)S(1)} %compare_select_fusion.3.dests, bf16[768,1024]{1,0:T(8,128)(2,1)S(1)} %bitcast.18, bf16[1024,8192]{1,0:T(8,128)(2,1)} %w_ref.29, bf16[768,512]{1,0:T(8,128)(2,1)S(1)} %collective-permute-done.7.refs_0_, bf16[768,512]{1,0:T(8,128)(2,1)S(1)} %shard_map.93.refs_1_), custom_call_target="tpu_custom_call" | custom-call | flops 24159191040 | bytes 4194304 | tf_op jit(solution)/shard_map/pallas_call | solution.py:73
  62.5 5.4 %collective-permute-done.6.sent_ref = f32[64,384]{1,0:T(8,128)S(1)} collective-permute-done((f32[64,384]{1,0:T(8,128)S(1)}, f32[64,384]{1,0:T(8,128)S(1)}, u32[]{:S(2)}, u32[]{:S(2)}) %collective-permute-start.6) | collective-permute-done | bytes 98336 | tf_op jit(solution)/shard_map/ppermute | solution.py:394
  67.9 2.6 %collective-permute-start.9 = (f32[64,384]{1,0:T(8,128)S(1)}, f32[64,384]{1,0:T(8,128)S(1)}, u32[]{:S(2)}, u32[]{:S(2)}) collective-permute-start(f32[64,384]{1,0:T(8,128)S(1)} %shard_map.95.refs_1_.low_ref), channel_id=1, source_target_pairs={{0,4},{1,5},{2,6},{3,7},{4,0},{5,1},{6,2},{7,3},{8,12},{9,13},{10,... | collective-permute-start | bytes 294920 | tf_op jit(solution)/shard_map/ppermute | solution.py:394
  70.6 2.8 %shard_map.96.refs_1_ = bf16[768,512]{1,0:T(8,128)(2,1)S(1)} custom-call(s32[8]{0:T(128)S(1)} %compare_select_fusion.3.dests, bf16[768,1024]{1,0:T(8,128)(2,1)S(1)} %bitcast.19, bf16[1024,8192]{1,0:T(8,128)(2,1)} %w_ref.29, bf16[768,512]{1,0:T(8,128)(2,1)S(1)} %collective-permute-done.13.refs_0_, f32[64,384]{1,0:T(8,128)S(1)} %shard_map.95.refs_1_.low_ref), custom_call_target="tpu_custom_call" | custom-call | flops 24159191040 | bytes 4194304 | tf_op jit(solution)/shard_map/pallas_call | solution.py:73
  73.4 2.8 %shard_map.97.refs_1_ = bf16[768,512]{1,0:T(8,128)(2,1)S(1)} custom-call(s32[8]{0:T(128)S(1)} %compare_select_fusion.3.dests, bf16[768,1024]{1,0:T(8,128)(2,1)S(1)} %bitcast.20, bf16[1024,8192]{1,0:T(8,128)(2,1)} %w_ref.29, bf16[768,512]{1,0:T(8,128)(2,1)S(1)} %collective-permute-done.12.refs_0_, bf16[768,512]{1,0:T(8,128)(2,1)S(1)} %shard_map.96.refs_1_), custom_call_target="tpu_custom_call" | custom-call | flops 24159191040 | bytes 4194304 | tf_op jit(solution)/shard_map/pallas_call | solution.py:73
  80.1 2.8 %shard_map.98.refs_1_ = bf16[768,512]{1,0:T(8,128)(2,1)S(1)} custom-call(s32[8]{0:T(128)S(1)} %compare_select_fusion.3.dests, bf16[768,1024]{1,0:T(8,128)(2,1)S(1)} %bitcast.21, bf16[1024,8192]{1,0:T(8,128)(2,1)} %w_ref.29, bf16[768,512]{1,0:T(8,128)(2,1)S(1)} %collective-permute-done.11.refs_0_, bf16[768,512]{1,0:T(8,128)(2,1)S(1)} %shard_map.97.refs_1_), custom_call_target="tpu_custom_call" | custom-call | flops 24159191040 | bytes 4194304 | tf_op jit(solution)/shard_map/pallas_call | solution.py:73
  86.9 2.8 %shard_map.99.after_ref = bf16[768,512]{1,0:T(8,128)(2,1)S(1)} custom-call(s32[8]{0:T(128)S(1)} %compare_select_fusion.3.dests, bf16[768,1024]{1,0:T(8,128)(2,1)S(1)} %bitcast.22, bf16[1024,8192]{1,0:T(8,128)(2,1)} %w_ref.29, bf16[768,512]{1,0:T(8,128)(2,1)S(1)} %collective-permute-done.10.refs_0_, bf16[768,512]{1,0:T(8,128)(2,1)S(1)} %shard_map.98.refs_1_), custom_call_target="tpu_custom_call" | custom-call | flops 24159191040 | bytes 4194304 | tf_op jit(solution)/shard_map/pallas_call | solution.py:73
  91.9 6.7 %collective-permute-done.16.refs_0_ = bf16[768,512]{1,0:T(8,128)(2,1)S(1)} collective-permute-done((bf16[768,512]{1,0:T(8,128)(2,1)S(1)}, bf16[768,512]{1,0:T(8,128)(2,1)S(1)}, u32[]{:S(2)}, u32[]{:S(2)}) %collective-permute-start.16) | collective-permute-done | bytes 786464 | tf_op jit(solution)/shard_map/ppermute | solution.py:372
  98.6 2.8 %shard_map.101.refs_1_ = bf16[768,512]{1,0:T(8,128)(2,1)S(1)} custom-call(s32[8]{0:T(128)S(1)} %compare_select_fusion.3.dests, bf16[768,1024]{1,0:T(8,128)(2,1)S(1)} %bitcast.23, bf16[1024,8192]{1,0:T(8,128)(2,1)} %w_ref.29, bf16[768,512]{1,0:T(8,128)(2,1)S(1)} %collective-permute-done.16.refs_0_, bf16[64,384]{1,0:T(8,128)(2,1)S(1)} %shard_map.100.refs_1_.low_ref), custom_call_target="tpu_custom_call" | custom-call | flops 24159191040 | bytes 4194304 | tf_op jit(solution)/shard_map/pallas_call | solution.py:73
  104.0 2.8 %shard_map.102.after_ref = bf16[768,512]{1,0:T(8,128)(2,1)S(1)} custom-call(s32[8]{0:T(128)S(1)} %compare_select_fusion.3.dests, bf16[768,1024]{1,0:T(8,128)(2,1)S(1)} %bitcast.24, bf16[1024,8192]{1,0:T(8,128)(2,1)} %w_ref.29, bf16[768,512]{1,0:T(8,128)(2,1)S(1)} %collective-permute-done.15.refs_0_, bf16[768,512]{1,0:T(8,128)(2,1)S(1)} %shard_map.101.refs_1_), custom_call_target="tpu_custom_call" | custom-call | flops 24159191040 | bytes 4194304 | tf_op jit(solution)/shard_map/pallas_call | solution.py:73
  107.0 10.0 %collective-permute-done.14.other_ref = bf16[64,384]{1,0:T(8,128)(2,1)S(1)} collective-permute-done((bf16[64,384]{1,0:T(8,128)(2,1)S(1)}, bf16[64,384]{1,0:T(8,128)(2,1)S(1)}, u32[]{:S(2)}, u32[]{:S(2)}) %collective-permute-start.14) | collective-permute-done | bytes 49184 | tf_op jit(solution)/shard_map/ppermute | solution.py:394
  117.7 2.9 %collective-permute-done.20.two_ref = bf16[768,512]{1,0:T(8,128)(2,1)S(1)} collective-permute-done((bf16[768,512]{1,0:T(8,128)(2,1)S(1)}, bf16[768,512]{1,0:T(8,128)(2,1)S(1)}, u32[]{:S(2)}, u32[]{:S(2)}) %collective-permute-start.20) | collective-permute-done | bytes 786464 | tf_op jit(solution)/shard_map/ppermute | solution.py:372
  120.6 11.3 %collective-permute-done.19.one_ref = bf16[768,512]{1,0:T(8,128)(2,1)S(1)} collective-permute-done((bf16[768,512]{1,0:T(8,128)(2,1)S(1)}, bf16[768,512]{1,0:T(8,128)(2,1)S(1)}, u32[]{:S(2)}, u32[]{:S(2)}) %collective-permute-start.19) | collective-permute-done | bytes 786464 | tf_op jit(solution)/shard_map/ppermute | solution.py:372
  (75 shorter events, 38.9 us)
Async XLA Ops:
  0.8 11.0 %collective-permute-start = (s32[24]{0:T(128)S(1)}, s32[24]{0:T(128)S(1)}, u32[]{:S(2)}, u32[]{:S(2)}) collective-permute-start(s32[24]{0:T(128)S(1)} %reshape.102), channel_id=1, source_target_pairs={{0,8},{8,0},{1,9},{9,1},{2,10},{10,2},{3,11},{11,3},{4,12},{12,4},... | collective-permute-start | bytes 296 | tf_op jit(solution)/shard_map/ppermute | solution.py:376
  6.3 27.4 %collective-permute-start.3 = (bf16[768,512]{1,0:T(8,128)(2,1)}, bf16[768,512]{1,0:T(8,128)(2,1)}, u32[]{:S(2)}, u32[]{:S(2)}) collective-permute-start(bf16[768,512]{1,0:T(8,128)(2,1)} %shard_map.82.refs_0_), channel_id=1, source_target_pairs={{0,2},{2,4},{4,6},{6,7},{7,5},{5,3},{3,1},{1,0},{8,10},{10,12},{12... | collective-permute-start | bytes 2359304 | tf_op jit(solution)/shard_map/ppermute | solution.py:372
  11.7 26.9 %collective-permute-start.2 = (bf16[768,512]{1,0:T(8,128)(2,1)S(1)}, bf16[768,512]{1,0:T(8,128)(2,1)S(1)}, u32[]{:S(2)}, u32[]{:S(2)}) collective-permute-start(bf16[768,512]{1,0:T(8,128)(2,1)S(1)} %shard_map.83.after_ref), channel_id=1, source_target_pairs={{0,1},{2,0},{4,2},{6,4},{7,6},{5,7},{3,5},{1,3},{8,9},{10,8},{12,1... | collective-permute-start | bytes 2359304 | tf_op jit(solution)/shard_map/ppermute | solution.py:372
  15.5 11.5 %collective-permute-start.4 = (bf16[24,64,1024]{2,1,0:T(8,128)(2,1)S(1)}, bf16[24,64,1024]{2,1,0:T(8,128)(2,1)S(1)}, u32[]{:S(2)}, u32[]{:S(2)}) collective-permute-start(bf16[24,64,1024]{2,1,0:T(8,128)(2,1)S(1)} %shard_map.84.refs_0_), channel_id=1, source_target_pairs={{0,8},{8,0},{1,9},{9,1},{2,10},{10,2},{3,11},{11,3},{4,12},{12,4},... | collective-permute-start | bytes 9437192 | tf_op jit(solution)/shard_map/ppermute | solution.py:383
  19.4 35.5 %collective-permute-start.8 = (bf16[768,512]{1,0:T(8,128)(2,1)}, bf16[768,512]{1,0:T(8,128)(2,1)S(1)}, u32[]{:S(2)}, u32[]{:S(2)}) collective-permute-start(bf16[768,512]{1,0:T(8,128)(2,1)} %shard_map.85.refs_0_), channel_id=1, source_target_pairs={{0,2},{2,4},{4,6},{6,7},{7,5},{5,3},{3,1},{1,0},{8,10},{10,12},{12... | collective-permute-start | bytes 2359304 | tf_op jit(solution)/shard_map/ppermute | solution.py:372
  24.0 34.2 %collective-permute-start.7 = (bf16[768,512]{1,0:T(8,128)(2,1)S(1)}, bf16[768,512]{1,0:T(8,128)(2,1)S(1)}, u32[]{:S(2)}, u32[]{:S(2)}) collective-permute-start(bf16[768,512]{1,0:T(8,128)(2,1)S(1)} %shard_map.86.after_ref), channel_id=1, source_target_pairs={{0,1},{2,0},{4,2},{6,4},{7,6},{5,7},{3,5},{1,3},{8,9},{10,8},{12,1... | collective-permute-start | bytes 2359304 | tf_op jit(solution)/shard_map/ppermute | solution.py:372
  26.9 16.1 %collective-permute-start.1 = (bf16[24,64,1024]{2,1,0:T(8,128)(2,1)S(1)}, bf16[24,64,1024]{2,1,0:T(8,128)(2,1)S(1)}, u32[]{:S(2)}, u32[]{:S(2)}) collective-permute-start(bf16[24,64,1024]{2,1,0:T(8,128)(2,1)S(1)} %shard_map.87.after_ref), channel_id=1, source_target_pairs={{0,8},{8,0},{1,9},{9,1},{2,10},{10,2},{3,11},{11,3},{4,12},{12,4},... | collective-permute-start | bytes 9437192 | tf_op jit(solution)/shard_map/ppermute | solution.py:386
  33.7 19.5 %collective-permute-start.5 = (f32[64,384]{1,0:T(8,128)S(1)}, f32[64,384]{1,0:T(8,128)S(1)}, u32[]{:S(2)}, u32[]{:S(2)}) collective-permute-start(f32[64,384]{1,0:T(8,128)S(1)} %get-tuple-element.12), channel_id=1, source_target_pairs={{0,1},{1,0},{2,3},{3,2},{4,5},{5,4},{6,7},{7,6},{8,9},{9,8},{10,11... | collective-permute-start | bytes 294920 | tf_op jit(solution)/shard_map/ppermute | solution.py:394
  38.6 32.0 %collective-permute-start.13 = (bf16[768,512]{1,0:T(8,128)(2,1)S(1)}, bf16[768,512]{1,0:T(8,128)(2,1)S(1)}, u32[]{:S(2)}, u32[]{:S(2)}) collective-permute-start(bf16[768,512]{1,0:T(8,128)(2,1)S(1)} %shard_map.89.refs_1_), channel_id=1, source_target_pairs={{0,2},{2,4},{4,6},{6,7},{7,5},{5,3},{3,1},{1,0},{8,10},{10,12},{12... | collective-permute-start | bytes 2359304 | tf_op jit(solution)/shard_map/ppermute | solution.py:372
  43.0 30.4 %collective-permute-start.12 = (bf16[768,512]{1,0:T(8,128)(2,1)S(1)}, bf16[768,512]{1,0:T(8,128)(2,1)S(1)}, u32[]{:S(2)}, u32[]{:S(2)}) collective-permute-start(bf16[768,512]{1,0:T(8,128)(2,1)S(1)} %shard_map.90.after_ref), channel_id=1, source_target_pairs={{0,1},{2,0},{4,2},{6,4},{7,6},{5,7},{3,5},{1,3},{8,9},{10,8},{12,1... | collective-permute-start | bytes 2359304 | tf_op jit(solution)/shard_map/ppermute | solution.py:372
  53.2 14.7 %collective-permute-start.6 = (f32[64,384]{1,0:T(8,128)S(1)}, f32[64,384]{1,0:T(8,128)S(1)}, u32[]{:S(2)}, u32[]{:S(2)}) collective-permute-start(f32[64,384]{1,0:T(8,128)S(1)} %shard_map.92.refs_1_.low_ref), channel_id=1, source_target_pairs={{0,2},{1,3},{2,0},{3,1},{4,6},{5,7},{6,4},{7,5},{8,10},{9,11},{10,... | collective-permute-start | bytes 294920 | tf_op jit(solution)/shard_map/ppermute | solution.py:394
  57.6 22.5 %collective-permute-start.11 = (bf16[768,512]{1,0:T(8,128)(2,1)S(1)}, bf16[768,512]{1,0:T(8,128)(2,1)S(1)}, u32[]{:S(2)}, u32[]{:S(2)}) collective-permute-start(bf16[768,512]{1,0:T(8,128)(2,1)S(1)} %shard_map.93.refs_1_), channel_id=1, source_target_pairs={{0,2},{2,4},{4,6},{6,7},{7,5},{5,3},{3,1},{1,0},{8,10},{10,12},{12... | collective-permute-start | bytes 2359304 | tf_op jit(solution)/shard_map/ppermute | solution.py:372
  60.9 25.9 %collective-permute-start.10 = (bf16[768,512]{1,0:T(8,128)(2,1)S(1)}, bf16[768,512]{1,0:T(8,128)(2,1)S(1)}, u32[]{:S(2)}, u32[]{:S(2)}) collective-permute-start(bf16[768,512]{1,0:T(8,128)(2,1)S(1)} %shard_map.94.after_ref), channel_id=1, source_target_pairs={{0,1},{2,0},{4,2},{6,4},{7,6},{5,7},{3,5},{1,3},{8,9},{10,8},{12,1... | collective-permute-start | bytes 2359304 | tf_op jit(solution)/shard_map/ppermute | solution.py:372
  67.9 21.9 %collective-permute-start.9 = (f32[64,384]{1,0:T(8,128)S(1)}, f32[64,384]{1,0:T(8,128)S(1)}, u32[]{:S(2)}, u32[]{:S(2)}) collective-permute-start(f32[64,384]{1,0:T(8,128)S(1)} %shard_map.95.refs_1_.low_ref), channel_id=1, source_target_pairs={{0,4},{1,5},{2,6},{3,7},{4,0},{5,1},{6,2},{7,3},{8,12},{9,13},{10,... | collective-permute-start | bytes 294920 | tf_op jit(solution)/shard_map/ppermute | solution.py:394
  73.4 25.3 %collective-permute-start.16 = (bf16[768,512]{1,0:T(8,128)(2,1)S(1)}, bf16[768,512]{1,0:T(8,128)(2,1)S(1)}, u32[]{:S(2)}, u32[]{:S(2)}) collective-permute-start(bf16[768,512]{1,0:T(8,128)(2,1)S(1)} %shard_map.96.refs_1_), channel_id=1, source_target_pairs={{0,2},{2,4},{4,6},{6,7},{7,5},{5,3},{3,1},{1,0},{8,10},{10,12},{12... | collective-permute-start | bytes 2359304 | tf_op jit(solution)/shard_map/ppermute | solution.py:372
  76.2 27.8 %collective-permute-start.15 = (bf16[768,512]{1,0:T(8,128)(2,1)S(1)}, bf16[768,512]{1,0:T(8,128)(2,1)S(1)}, u32[]{:S(2)}, u32[]{:S(2)}) collective-permute-start(bf16[768,512]{1,0:T(8,128)(2,1)S(1)} %shard_map.97.refs_1_), channel_id=1, source_target_pairs={{0,1},{2,0},{4,2},{6,4},{7,6},{5,7},{3,5},{1,3},{8,9},{10,8},{12,1... | collective-permute-start | bytes 2359304 | tf_op jit(solution)/shard_map/ppermute | solution.py:372
  82.9 51.2 %collective-permute-start.17 = (bf16[768,512]{1,0:T(8,128)(2,1)S(1)}, bf16[768,512]{1,0:T(8,128)(2,1)S(1)}, u32[]{:S(2)}, u32[]{:S(2)}) collective-permute-start(bf16[768,512]{1,0:T(8,128)(2,1)S(1)} %shard_map.98.refs_1_), channel_id=1, source_target_pairs={{0,2},{2,4},{4,6},{6,7},{7,5},{5,3},{3,1},{1,0},{8,10},{10,12},{12... | collective-permute-start | bytes 2359304 | tf_op jit(solution)/shard_map/ppermute | solution.py:372
  89.6 30.9 %collective-permute-start.20 = (bf16[768,512]{1,0:T(8,128)(2,1)S(1)}, bf16[768,512]{1,0:T(8,128)(2,1)S(1)}, u32[]{:S(2)}, u32[]{:S(2)}) collective-permute-start(bf16[768,512]{1,0:T(8,128)(2,1)S(1)} %shard_map.99.after_ref), channel_id=1, source_target_pairs={{0,1},{2,0},{4,2},{6,4},{7,6},{5,7},{3,5},{1,3},{8,9},{10,8},{12,1... | collective-permute-start | bytes 2359304 | tf_op jit(solution)/shard_map/ppermute | solution.py:372
  89.9 27.1 %collective-permute-start.14 = (bf16[64,384]{1,0:T(8,128)(2,1)S(1)}, bf16[64,384]{1,0:T(8,128)(2,1)S(1)}, u32[]{:S(2)}, u32[]{:S(2)}) collective-permute-start(bf16[64,384]{1,0:T(8,128)(2,1)S(1)} %shard_map.100.refs_1_.low_ref), channel_id=1, source_target_pairs={{0,1},{1,0},{2,3},{3,2},{4,5},{5,4},{6,7},{7,6},{8,9},{9,8},{10,11... | collective-permute-start | bytes 147464 | tf_op jit(solution)/shard_map/ppermute | solution.py:394
  101.4 15.6 %copy-start.3 = (f32[768,1024]{1,0:T(8,128)S(1)}, f32[768,1024]{1,0:T(8,128)}, u32[]{:S(2)}) copy-start(f32[768,1024]{1,0:T(8,128)} %copy-done.2) | copy-start | bytes 9437188
  101.4 15.6 %copy-start.8 = (s32[3,256]{1,0:T(4,128)S(1)}, s32[3,256]{1,0:T(4,128)}, u32[]{:S(2)}) copy-start(s32[3,256]{1,0:T(4,128)} %place_ref.3) | copy-start | bytes 9220
  101.4 15.6 %copy-start.10 = (bf16[24,64,1024]{2,1,0:T(8,128)(2,1)S(1)}, bf16[24,64,1024]{2,1,0:T(8,128)(2,1)}, u32[]{:S(2)}) copy-start(bf16[24,64,1024]{2,1,0:T(8,128)(2,1)} %copy-done.9) | copy-start | bytes 9437188
  101.4 30.5 %collective-permute-start.19 = (bf16[768,512]{1,0:T(8,128)(2,1)S(1)}, bf16[768,512]{1,0:T(8,128)(2,1)S(1)}, u32[]{:S(2)}, u32[]{:S(2)}) collective-permute-start(bf16[768,512]{1,0:T(8,128)(2,1)S(1)} %shard_map.101.refs_1_), channel_id=1, source_target_pairs={{0,2},{2,4},{4,6},{6,7},{7,5},{5,3},{3,1},{1,0},{8,10},{10,12},{12... | collective-permute-start | bytes 2359304 | tf_op jit(solution)/shard_map/ppermute | solution.py:372
  106.7 30.0 %collective-permute-start.18 = (bf16[768,512]{1,0:T(8,128)(2,1)S(1)}, bf16[768,512]{1,0:T(8,128)(2,1)S(1)}, u32[]{:S(2)}, u32[]{:S(2)}) collective-permute-start(bf16[768,512]{1,0:T(8,128)(2,1)S(1)} %shard_map.102.after_ref), channel_id=1, source_target_pairs={{0,1},{2,0},{4,2},{6,4},{7,6},{5,7},{3,5},{1,3},{8,9},{10,8},{12,1... | collective-permute-start | bytes 2359304 | tf_op jit(solution)/shard_map/ppermute | solution.py:372
  (9 other events, 52.7 us)

commit v7 on v6

--- a/solution.py
+++ b/solution.py
@@ -8,6 +8,7 @@
 from jax.sharding import PartitionSpec as P
 
 VMEM_LIMIT = 40 * 1024 * 1024
+FIRST_VMEM_LIMIT = 60 * 1024 * 1024
 SWAP = [(0, 1), (1, 0)]
 WHOLE = pl.BlockSpec(memory_space=pltpu.VMEM)
 ANYWHERE = pl.BlockSpec(memory_space=pl.ANY)
@@ -87,6 +88,46 @@
     )(dests, *operands)
 
 
+def first_hop_kernel(dests, x_ref, w_ref, out_ref, token_ref):
+    token_ref[...] = jnp.zeros_like(token_ref)
+    out_ref[...] = jnp.dot(
+        x_ref[...], w_ref[...], preferred_element_type=jnp.float32
+    ).astype(out_ref.dtype)
+
+
+def first_hop(dests, offset, half, x, weight):
+    rows, depth = x.shape
+    half_cols = weight.shape[1] // dests.shape[0] // 2
+    tile = min(256, half_cols)
+    tiles = half_cols // tile
+    row_tile = rows // 4
+    return pl.pallas_call(
+        first_hop_kernel,
+        grid_spec=pltpu.PrefetchScalarGridSpec(
+            num_scalar_prefetch=1,
+            grid=(tiles, rows // row_tile),
+            in_specs=[
+                pl.BlockSpec((row_tile, depth), lambda j, i, d: (i, 0)),
+                pl.BlockSpec(
+                    (depth, tile), lambda j, i, d: (0, (d[offset] * 2 + half) * tiles + j)
+                ),
+            ],
+            out_specs=[
+                pl.BlockSpec((row_tile, tile), lambda j, i, d: (i, j)),
+                pl.BlockSpec((8, 128), lambda j, i, d: (0, 0)),
+            ],
+        ),
+        out_shape=[
+            jax.ShapeDtypeStruct((rows, half_cols), jnp.bfloat16),
+            jax.ShapeDtypeStruct((8, 128), jnp.float32),
+        ],
+        compiler_params=pltpu.CompilerParams(vmem_limit_bytes=FIRST_VMEM_LIMIT),
+        cost_estimate=cost(
+            2 * rows * depth * half_cols, 2 * (rows * depth + depth * half_cols)
+        ),
+    )(dests, x, weight)
+
+
 def collect_kernel(count, index, table_ref, after_ref, out_ref, sems):
     copies = [
         pltpu.make_async_copy(table_ref.at[index[slot]], out_ref.at[slot], sems.at[slot])
@@ -116,7 +157,7 @@
     )(index, table, after)
 
 
-def load_pages(count, local, index, table_ref, got_ref, pages, sems):
+def start_pages(count, local, index, table_ref, got_ref, pages, sems):
     for slot in range(count):
         own = local[slot] == 1
 
@@ -130,7 +171,9 @@
         def _():
             pltpu.make_async_copy(got_ref.at[slot], pages.at[slot], sems.at[slot]).start()
 
-    for slot in range(count):
+
+def wait_pages(slots, got_ref, pages, sems):
+    for slot in slots:
         pltpu.make_async_copy(got_ref.at[slot], pages.at[slot], sems.at[slot]).wait()
 
 
@@ -140,10 +183,11 @@
 ):
     steps, blocks, listed, rank, block_rows = sizes
     half = steps * blocks // 2
-    load_pages(steps * blocks * listed, local, index, table_ref, got_ref, pages, sems)
+    start_pages(steps * blocks * listed, local, index, table_ref, got_ref, pages, sems)
     for step in range(steps):
         for block in range(blocks):
             at = step * blocks + block
+            wait_pages(range(at * listed, (at + 1) * listed), got_ref, pages, sems)
             listing = pages[at * listed : (at + 1) * listed].reshape(listed * rank, -1)
             every = lax.dot_general(
                 listing, x_ref[at * block_rows : (at + 1) * block_rows, :],
@@ -213,10 +257,14 @@
 
     @pl.when(now == 0)
     def _():
-        load_pages(count, local, index, table_ref, got_ref, pages, sems)
+        start_pages(count, local, index, table_ref, got_ref, pages, sems)
 
     columns = pl.ds(pl.multiple_of(now * tile, tile), tile)
     out_ref[:, columns] = jnp.dot(x_ref[...], w_ref[...], preferred_element_type=jnp.float32)
+
+    @pl.when(now == pl.num_programs(0) - 1)
+    def _():
+        wait_pages(range(count), got_ref, pages, sems)
 
 
 def own_terms(dests, local, index, x, weight, table, got, after):
@@ -360,7 +408,9 @@
     far = size // 2
     pairs = [[(0, 1, forward), (1, -1, backward)], [(1, 1, forward), (0, -1, backward)]]
     arrived = {}
-    last = None
+    half, sign, moves = pairs[0][0]
+    first, token = first_hop(dests, (sign * far) % size, half, x, output_weight)
+    arrived[half, sign] = lax.ppermute(first, "tp", moves)
 
     def turn(number, last):
         left = far - (number + 1) // 2
@@ -373,8 +423,10 @@
         return last
 
     ids = block_adapter_ids.reshape(-1)
-    ids_there = lax.ppermute(ids, "inst", SWAP)
-    last = turn(0, last)
+    ids_there = lax.ppermute(block_adapter_ids, "inst", SWAP).reshape(-1)
+    half, sign, moves = pairs[0][1]
+    last = hop(dests, (sign * far) % size, half, x, output_weight, None, token)
+    arrived[half, sign] = lax.ppermute(last, "tp", moves)
     pages = adapter_page_table[jnp.concatenate([ids, ids_there])]
     places = pages % resident
     index, index_there = places[: ids.shape[0]], places[ids.shape[0] :]

time: 139 us -> 143 us (1.029)
  Pallas kernels: 65.8 us -> 68.2 us
  waiting for transfers between devices: 42.7 us -> 45.1 us
    pallas_call x0 -> x1, Pallas kernels: none -> 7.66 us  [first_hop(): pl.pallas_call(first_hop_kernel, grid_spec=pltpu.PrefetchScalarGridSpec(n...]
    pallas_call x14 -> x13, Pallas kernels: 40.7 us -> 37.1 us  [hop(): pl.pallas_call(functools.partial(hop_kernel, received is not None), grid_...]
    ppermute x14 -> x12, starting transfers between devices: 16.2 us -> 13.2 us  [turn(): arrived[half, sign] = lax.ppermute(last, 'tp', moves)]
    ppermute x1 -> x3, starting transfers between devices: 0.45 us -> 3.1 us  [the longest x1 2.59 us: per_device(): arrived[half, sign] = lax.ppermute(first, 'tp', moves)]
    ppermute x4, waiting for transfers between devices: 15.3 us -> 17.3 us  [over(): return lax.ppermute(value, 'tp', [(i, i ^ apart) for i in range(size)])]
    unnamed x24 -> x26, local copies, waits for them, and re-layouts: 3.07 us -> 2.36 us
    ppermute x14 -> x12, waiting for transfers between devices: 27.3 us -> 27.8 us  [turn(): arrived[half, sign] = lax.ppermute(last, 'tp', moves)]
  transfers between devices with their start and end apart: 21 -> 21, of which waited for: 8 -> 9; matrix products, arithmetic and copies ran while one was open for 1% -> 1% of each run, Pallas kernels for 46% -> 47%
where the time goes in v7:
time: 143 us; the launch traced here: 142 us
  Pallas kernels  68.2 us (48%)
  waiting for transfers between devices  45.1 us (32%)
  starting transfers between devices  24.2 us (17%)
  local copies, waits for them, and re-layouts  3.39 us (2%)
    pallas_call x13, Pallas kernels, hop(): pl.pallas_call(functools.partial(hop_kernel, received is not None), grid_...  37.1 us
    ppermute x12, waiting for transfers between devices, turn(): arrived[half, sign] = lax.ppermute(last, 'tp', moves)  27.8 us
    ppermute x4, waiting for transfers between devices, over(): return lax.ppermute(value, 'tp', [(i, i ^ apart) for i in range(size)])  17.3 us
    ppermute x12, starting transfers between devices, turn(): arrived[half, sign] = lax.ppermute(last, 'tp', moves)  13.2 us
    pallas_call x1, Pallas kernels, first_hop(): pl.pallas_call(first_hop_kernel, grid_spec=pltpu.PrefetchScalarGridSpec(n...  7.66 us
    ppermute x4, starting transfers between devices, over(): return lax.ppermute(value, 'tp', [(i, i ^ apart) for i in range(size)])  7.6 us
    pallas_call x1, Pallas kernels, own_terms(): pl.pallas_call(own_kernel, grid_spec=pltpu.PrefetchScalarGridSpec(num_sca...  7.23 us
    pallas_call x1, Pallas kernels, low_rank(): pl.pallas_call(functools.partial(low_kernel, sizes), grid_spec=pltpu.Pref...  5.85 us
  transfers between devices with their start and end apart: 21, of which 9 were waited for; matrix products, arithmetic and copies ran while one was open for 1% of the time, Pallas kernels for 47%

profile of v7, /device:TPU:0, one launch (start us, length us, event | category | flops | bytes accessed | tf_op | source)
XLA Modules:
  0.0 142.0 jit_solution(7900276692295478683)
XLA Ops:
  1.0 7.7 %shard_map.82 = (bf16[768,512]{1,0:T(8,128)(2,1)}, f32[8,128]{1,0:T(8,128)}) custom-call(s32[8]{0:T(128)} %compare_select_fusion.3.dests, bf16[768,1024]{1,0:T(8,128)(2,1)} %bitcast.8, bf16[1024,8192]{1,0:T(8,128)(2,1)} %w_ref.29), custom_call_target="tpu_custom_call" | custom-call | flops 24159191040 | bytes 2621440 | tf_op jit(solution)/shard_map/pallas_call | solution.py:104
  12.0 2.8 %shard_map.83.after_ref = bf16[768,512]{1,0:T(8,128)(2,1)S(1)} custom-call(s32[8]{0:T(128)S(1)} %copy-done.8, bf16[768,1024]{1,0:T(8,128)(2,1)S(1)} %bitcast.9, bf16[1024,8192]{1,0:T(8,128)(2,1)} %w_ref.29, f32[8,128]{1,0:T(8,128)S(1)} %copy-done.11), custom_call_target="tpu_custom_call" | custom-call | flops 24159191040 | bytes 4194304 | tf_op jit(solution)/shard_map/pallas_call | solution.py:74
  16.0 2.7 %shard_map.84.refs_0_ = bf16[24,64,1024]{2,1,0:T(8,128)(2,1)S(1)} custom-call(s32[24]{0:T(128)S(1)} %get-tuple-element.17.index, bf16[96,64,1024]{2,1,0:T(8,128)(2,1)} %table_ref.6, bf16[768,512]{1,0:T(8,128)(2,1)S(1)} %shard_map.83.after_ref), custom_call_target="tpu_custom_call" | custom-call | bytes 6291456 | tf_op jit(solution)/shard_map/pallas_call | solution.py:145
  18.9 3.6 %shard_map.85.refs_0_ = bf16[768,512]{1,0:T(8,128)(2,1)} custom-call(s32[8]{0:T(128)S(1)} %copy-done.8, bf16[768,1024]{1,0:T(8,128)(2,1)S(1)} %bitcast.10, bf16[1024,8192]{1,0:T(8,128)(2,1)} %w_ref.29, bf16[24,64,1024]{2,1,0:T(8,128)(2,1)S(1)} %shard_map.84.refs_0_), custom_call_target="tpu_custom_call" | custom-call | flops 24159191040 | bytes 4194304 | tf_op jit(solution)/shard_map/pallas_call | solution.py:74
  24.4 2.8 %shard_map.86.after_ref = bf16[768,512]{1,0:T(8,128)(2,1)S(1)} custom-call(s32[8]{0:T(128)S(1)} %copy-done.8, bf16[768,1024]{1,0:T(8,128)(2,1)S(1)} %bitcast.11, bf16[1024,8192]{1,0:T(8,128)(2,1)} %w_ref.29, bf16[768,512]{1,0:T(8,128)(2,1)} %shard_map.85.refs_0_), custom_call_target="tpu_custom_call" | custom-call | flops 24159191040 | bytes 4194304 | tf_op jit(solution)/shard_map/pallas_call | solution.py:74
  27.4 2.7 %shard_map.87.after_ref = bf16[24,64,1024]{2,1,0:T(8,128)(2,1)S(1)} custom-call(s32[24]{0:T(128)S(1)} %get-tuple-element.17.index, bf16[96,64,1024]{2,1,0:T(8,128)(2,1)} %table_ref.7, bf16[768,512]{1,0:T(8,128)(2,1)S(1)} %shard_map.86.after_ref), custom_call_target="tpu_custom_call" | custom-call | bytes 6291456 | tf_op jit(solution)/shard_map/pallas_call | solution.py:145
  30.2 5.8 %shard_map.88 = (f32[64,384]{1,0:T(8,128)S(1)}, f32[64,384]{1,0:T(8,128)S(1)}) custom-call(s32[24]{0:T(128)S(1)} %compare_convert_fusion.local, s32[24]{0:T(128)S(1)} %get-tuple-element.18.index, s32[1]{0:T(128)} %bitcast.1.side, bf16[768,1024]{1,0:T(8,128)(2,1)S(1)} %bitcast.12, s32[3,256]{1,0:T(4,128)S(1)} %copy-done.6, bf16[96,64,1024]{2,1,0:T(8,128)(2,1)} %table_ref.6, ...), custom_call_target="tpu_custom_call" | custom-call | flops 12079595520 | bytes 4718592 | tf_op jit(solution)/shard_map/pallas_call | solution.py:216
  37.9 3.0 %shard_map.89.refs_1_ = bf16[768,512]{1,0:T(8,128)(2,1)S(1)} custom-call(s32[8]{0:T(128)S(1)} %copy-done.8, bf16[768,1024]{1,0:T(8,128)(2,1)S(1)} %bitcast.13, bf16[1024,8192]{1,0:T(8,128)(2,1)} %w_ref.29, bf16[768,512]{1,0:T(8,128)(2,1)} %collective-permute-done.3.refs_0_, f32[64,384]{1,0:T(8,128)S(1)} %get-tuple-element.13.refs_1_.low_ref), custom_call_target="tpu_custom_call" | custom-call | flops 24159191040 | bytes 4194304 | tf_op jit(solution)/shard_map/pallas_call | solution.py:74
  42.6 2.8 %shard_map.90.after_ref = bf16[768,512]{1,0:T(8,128)(2,1)S(1)} custom-call(s32[8]{0:T(128)S(1)} %copy-done.8, bf16[768,1024]{1,0:T(8,128)(2,1)S(1)} %bitcast.14, bf16[1024,8192]{1,0:T(8,128)(2,1)} %w_ref.29, bf16[768,512]{1,0:T(8,128)(2,1)S(1)} %collective-permute-done.2.refs_0_, bf16[768,512]{1,0:T(8,128)(2,1)S(1)} %shard_map.89.refs_1_), custom_call_target="tpu_custom_call" | custom-call | flops 24159191040 | bytes 4194304 | tf_op jit(solution)/shard_map/pallas_call | solution.py:74
  45.9 7.2 %shard_map.91 = (f32[768,1024]{1,0:T(8,128)S(1)}, bf16[24,64,1024]{2,1,0:T(8,128)(2,1)S(1)}) custom-call(s32[24]{0:T(128)S(1)} %compare_convert_fusion.local, s32[24]{0:T(128)S(1)} %get-tuple-element.18.index, s32[8]{0:T(128)S(1)} %copy-done.8, bf16[768,1024]{1,0:T(8,128)(2,1)S(1)} %bitcast.15, bf16[1024,8192]{1,0:T(8,128)(2,1)} %w_ref.29, ...), custom_call_target="tpu_custom_call" | custom-call | flops 48318382080 | bytes 13107200 | tf_op jit(solution)/shard_map/pallas_call | solution.py:275
  56.4 2.8 %shard_map.93.refs_1_ = bf16[768,512]{1,0:T(8,128)(2,1)S(1)} custom-call(s32[8]{0:T(128)S(1)} %copy-done.8, bf16[768,1024]{1,0:T(8,128)(2,1)S(1)} %bitcast.16, bf16[1024,8192]{1,0:T(8,128)(2,1)} %w_ref.29, bf16[768,512]{1,0:T(8,128)(2,1)S(1)} %collective-permute-done.8.refs_0_, f32[64,384]{1,0:T(8,128)S(1)} %shard_map.92.refs_1_.low_ref), custom_call_target="tpu_custom_call" | custom-call | flops 24159191040 | bytes 4194304 | tf_op jit(solution)/shard_map/pallas_call | solution.py:74
  59.7 2.8 %shard_map.94.after_ref = bf16[768,512]{1,0:T(8,128)(2,1)S(1)} custom-call(s32[8]{0:T(128)S(1)} %copy-done.8, bf16[768,1024]{1,0:T(8,128)(2,1)S(1)} %bitcast.17, bf16[1024,8192]{1,0:T(8,128)(2,1)} %w_ref.29, bf16[768,512]{1,0:T(8,128)(2,1)S(1)} %collective-permute-done.7.refs_0_, bf16[768,512]{1,0:T(8,128)(2,1)S(1)} %shard_map.93.refs_1_), custom_call_target="tpu_custom_call" | custom-call | flops 24159191040 | bytes 4194304 | tf_op jit(solution)/shard_map/pallas_call | solution.py:74
  64.1 6.9 %collective-permute-done.6.sent_ref = f32[64,384]{1,0:T(8,128)S(1)} collective-permute-done((f32[64,384]{1,0:T(8,128)S(1)}, f32[64,384]{1,0:T(8,128)S(1)}, u32[]{:S(2)}, u32[]{:S(2)}) %collective-permute-start.6) | collective-permute-done | bytes 98336 | tf_op jit(solution)/shard_map/ppermute | solution.py:446
  73.7 2.8 %shard_map.96.refs_1_ = bf16[768,512]{1,0:T(8,128)(2,1)S(1)} custom-call(s32[8]{0:T(128)S(1)} %copy-done.8, bf16[768,1024]{1,0:T(8,128)(2,1)S(1)} %bitcast.18, bf16[1024,8192]{1,0:T(8,128)(2,1)} %w_ref.29, bf16[768,512]{1,0:T(8,128)(2,1)S(1)} %collective-permute-done.13.refs_0_, f32[64,384]{1,0:T(8,128)S(1)} %shard_map.95.refs_1_.low_ref), custom_call_target="tpu_custom_call" | custom-call | flops 24159191040 | bytes 4194304 | tf_op jit(solution)/shard_map/pallas_call | solution.py:74
  76.5 2.8 %shard_map.97.refs_1_ = bf16[768,512]{1,0:T(8,128)(2,1)S(1)} custom-call(s32[8]{0:T(128)S(1)} %copy-done.8, bf16[768,1024]{1,0:T(8,128)(2,1)S(1)} %bitcast.19, bf16[1024,8192]{1,0:T(8,128)(2,1)} %w_ref.29, bf16[768,512]{1,0:T(8,128)(2,1)S(1)} %collective-permute-done.12.refs_0_, bf16[768,512]{1,0:T(8,128)(2,1)S(1)} %shard_map.96.refs_1_), custom_call_target="tpu_custom_call" | custom-call | flops 24159191040 | bytes 4194304 | tf_op jit(solution)/shard_map/pallas_call | solution.py:74
  82.5 2.8 %shard_map.98.refs_1_ = bf16[768,512]{1,0:T(8,128)(2,1)S(1)} custom-call(s32[8]{0:T(128)S(1)} %copy-done.8, bf16[768,1024]{1,0:T(8,128)(2,1)S(1)} %bitcast.20, bf16[1024,8192]{1,0:T(8,128)(2,1)} %w_ref.29, bf16[768,512]{1,0:T(8,128)(2,1)S(1)} %collective-permute-done.11.refs_0_, bf16[768,512]{1,0:T(8,128)(2,1)S(1)} %shard_map.97.refs_1_), custom_call_target="tpu_custom_call" | custom-call | flops 24159191040 | bytes 4194304 | tf_op jit(solution)/shard_map/pallas_call | solution.py:74
  90.0 2.8 %shard_map.99.after_ref = bf16[768,512]{1,0:T(8,128)(2,1)S(1)} custom-call(s32[8]{0:T(128)S(1)} %copy-done.8, bf16[768,1024]{1,0:T(8,128)(2,1)S(1)} %bitcast.21, bf16[1024,8192]{1,0:T(8,128)(2,1)} %w_ref.29, bf16[768,512]{1,0:T(8,128)(2,1)S(1)} %collective-permute-done.10.refs_0_, bf16[768,512]{1,0:T(8,128)(2,1)S(1)} %shard_map.98.refs_1_), custom_call_target="tpu_custom_call" | custom-call | flops 24159191040 | bytes 4194304 | tf_op jit(solution)/shard_map/pallas_call | solution.py:74
  94.3 6.7 %collective-permute-done.16.refs_0_ = bf16[768,512]{1,0:T(8,128)(2,1)S(1)} collective-permute-done((bf16[768,512]{1,0:T(8,128)(2,1)S(1)}, bf16[768,512]{1,0:T(8,128)(2,1)S(1)}, u32[]{:S(2)}, u32[]{:S(2)}) %collective-permute-start.16) | collective-permute-done | bytes 786464 | tf_op jit(solution)/shard_map/ppermute | solution.py:422
  101.0 2.8 %shard_map.101.refs_1_ = bf16[768,512]{1,0:T(8,128)(2,1)S(1)} custom-call(s32[8]{0:T(128)S(1)} %copy-done.8, bf16[768,1024]{1,0:T(8,128)(2,1)S(1)} %bitcast.22, bf16[1024,8192]{1,0:T(8,128)(2,1)} %w_ref.29, bf16[768,512]{1,0:T(8,128)(2,1)S(1)} %collective-permute-done.16.refs_0_, bf16[64,384]{1,0:T(8,128)(2,1)S(1)} %shard_map.100.refs_1_.low_ref), custom_call_target="tpu_custom_call" | custom-call | flops 24159191040 | bytes 4194304 | tf_op jit(solution)/shard_map/pallas_call | solution.py:74
  106.8 2.8 %shard_map.102.after_ref = bf16[768,512]{1,0:T(8,128)(2,1)S(1)} custom-call(s32[8]{0:T(128)S(1)} %copy-done.8, bf16[768,1024]{1,0:T(8,128)(2,1)S(1)} %bitcast.23, bf16[1024,8192]{1,0:T(8,128)(2,1)} %w_ref.29, bf16[768,512]{1,0:T(8,128)(2,1)S(1)} %collective-permute-done.15.refs_0_, bf16[768,512]{1,0:T(8,128)(2,1)S(1)} %shard_map.101.refs_1_), custom_call_target="tpu_custom_call" | custom-call | flops 24159191040 | bytes 4194304 | tf_op jit(solution)/shard_map/pallas_call | solution.py:74
  109.7 10.4 %collective-permute-done.14.other_ref = bf16[64,384]{1,0:T(8,128)(2,1)S(1)} collective-permute-done((bf16[64,384]{1,0:T(8,128)(2,1)S(1)}, bf16[64,384]{1,0:T(8,128)(2,1)S(1)}, u32[]{:S(2)}, u32[]{:S(2)}) %collective-permute-start.14) | collective-permute-done | bytes 49184 | tf_op jit(solution)/shard_map/ppermute | solution.py:446
  120.8 2.9 %collective-permute-done.20.two_ref = bf16[768,512]{1,0:T(8,128)(2,1)S(1)} collective-permute-done((bf16[768,512]{1,0:T(8,128)(2,1)S(1)}, bf16[768,512]{1,0:T(8,128)(2,1)S(1)}, u32[]{:S(2)}, u32[]{:S(2)}) %collective-permute-start.20) | collective-permute-done | bytes 786464 | tf_op jit(solution)/shard_map/ppermute | solution.py:422
  123.7 10.7 %collective-permute-done.19.one_ref = bf16[768,512]{1,0:T(8,128)(2,1)S(1)} collective-permute-done((bf16[768,512]{1,0:T(8,128)(2,1)S(1)}, bf16[768,512]{1,0:T(8,128)(2,1)S(1)}, u32[]{:S(2)}, u32[]{:S(2)}) %collective-permute-start.19) | collective-permute-done | bytes 786464 | tf_op jit(solution)/shard_map/ppermute | solution.py:422
  136.5 3.3 %collective-permute-done.18.two_ref = bf16[768,512]{1,0:T(8,128)(2,1)S(1)} collective-permute-done((bf16[768,512]{1,0:T(8,128)(2,1)S(1)}, bf16[768,512]{1,0:T(8,128)(2,1)S(1)}, u32[]{:S(2)}, u32[]{:S(2)}) %collective-permute-start.18) | collective-permute-done | bytes 786464 | tf_op jit(solution)/shard_map/ppermute | solution.py:422
  (77 shorter events, 37.6 us)
Async XLA Ops:
  0.0 14.9 %collective-permute-start = (s32[3,2,4]{2,1,0:T(2,128)}, s32[3,2,4]{2,1,0:T(2,128)S(1)}, u32[]{:S(2)}, u32[]{:S(2)}) collective-permute-start(s32[3,2,4]{2,1,0:T(2,128)} %param.13), channel_id=1, source_target_pairs={{0,8},{8,0},{1,9},{9,1},{2,10},{10,2},{3,11},{11,3},{4,12},{12,4},... | collective-permute-start | bytes 296 | tf_op jit(solution)/shard_map/ppermute | solution.py:426
  8.7 27.4 %collective-permute-start.3 = (bf16[768,512]{1,0:T(8,128)(2,1)}, bf16[768,512]{1,0:T(8,128)(2,1)}, u32[]{:S(2)}, u32[]{:S(2)}) collective-permute-start(bf16[768,512]{1,0:T(8,128)(2,1)} %get-tuple-element.12), channel_id=1, source_target_pairs={{0,2},{2,4},{4,6},{6,7},{7,5},{5,3},{3,1},{1,0},{8,10},{10,12},{12... | collective-permute-start | bytes 2359304 | tf_op jit(solution)/shard_map/ppermute | solution.py:413
  14.8 26.2 %collective-permute-start.2 = (bf16[768,512]{1,0:T(8,128)(2,1)S(1)}, bf16[768,512]{1,0:T(8,128)(2,1)S(1)}, u32[]{:S(2)}, u32[]{:S(2)}) collective-permute-start(bf16[768,512]{1,0:T(8,128)(2,1)S(1)} %shard_map.83.after_ref), channel_id=1, source_target_pairs={{0,1},{2,0},{4,2},{6,4},{7,6},{5,7},{3,5},{1,3},{8,9},{10,8},{12,1... | collective-permute-start | bytes 2359304 | tf_op jit(solution)/shard_map/ppermute | solution.py:429
  18.7 11.5 %collective-permute-start.4 = (bf16[24,64,1024]{2,1,0:T(8,128)(2,1)S(1)}, bf16[24,64,1024]{2,1,0:T(8,128)(2,1)S(1)}, u32[]{:S(2)}, u32[]{:S(2)}) collective-permute-start(bf16[24,64,1024]{2,1,0:T(8,128)(2,1)S(1)} %shard_map.84.refs_0_), channel_id=1, source_target_pairs={{0,8},{8,0},{1,9},{9,1},{2,10},{10,2},{3,11},{11,3},{4,12},{12,4},... | collective-permute-start | bytes 9437192 | tf_op jit(solution)/shard_map/ppermute | solution.py:435
  22.6 33.8 %collective-permute-start.8 = (bf16[768,512]{1,0:T(8,128)(2,1)}, bf16[768,512]{1,0:T(8,128)(2,1)S(1)}, u32[]{:S(2)}, u32[]{:S(2)}) collective-permute-start(bf16[768,512]{1,0:T(8,128)(2,1)} %shard_map.85.refs_0_), channel_id=1, source_target_pairs={{0,2},{2,4},{4,6},{6,7},{7,5},{5,3},{3,1},{1,0},{8,10},{10,12},{12... | collective-permute-start | bytes 2359304 | tf_op jit(solution)/shard_map/ppermute | solution.py:422
  27.2 32.6 %collective-permute-start.7 = (bf16[768,512]{1,0:T(8,128)(2,1)S(1)}, bf16[768,512]{1,0:T(8,128)(2,1)S(1)}, u32[]{:S(2)}, u32[]{:S(2)}) collective-permute-start(bf16[768,512]{1,0:T(8,128)(2,1)S(1)} %shard_map.86.after_ref), channel_id=1, source_target_pairs={{0,1},{2,0},{4,2},{6,4},{7,6},{5,7},{3,5},{1,3},{8,9},{10,8},{12,1... | collective-permute-start | bytes 2359304 | tf_op jit(solution)/shard_map/ppermute | solution.py:422
  30.1 15.2 %collective-permute-start.1 = (bf16[24,64,1024]{2,1,0:T(8,128)(2,1)S(1)}, bf16[24,64,1024]{2,1,0:T(8,128)(2,1)S(1)}, u32[]{:S(2)}, u32[]{:S(2)}) collective-permute-start(bf16[24,64,1024]{2,1,0:T(8,128)(2,1)S(1)} %shard_map.87.after_ref), channel_id=1, source_target_pairs={{0,8},{8,0},{1,9},{9,1},{2,10},{10,2},{3,11},{11,3},{4,12},{12,4},... | collective-permute-start | bytes 9437192 | tf_op jit(solution)/shard_map/ppermute | solution.py:438
  36.1 18.7 %collective-permute-start.5 = (f32[64,384]{1,0:T(8,128)S(1)}, f32[64,384]{1,0:T(8,128)S(1)}, u32[]{:S(2)}, u32[]{:S(2)}) collective-permute-start(f32[64,384]{1,0:T(8,128)S(1)} %get-tuple-element.16), channel_id=1, source_target_pairs={{0,1},{1,0},{2,3},{3,2},{4,5},{5,4},{6,7},{7,6},{8,9},{9,8},{10,11... | collective-permute-start | bytes 294920 | tf_op jit(solution)/shard_map/ppermute | solution.py:446
  41.0 32.7 %collective-permute-start.13 = (bf16[768,512]{1,0:T(8,128)(2,1)S(1)}, bf16[768,512]{1,0:T(8,128)(2,1)S(1)}, u32[]{:S(2)}, u32[]{:S(2)}) collective-permute-start(bf16[768,512]{1,0:T(8,128)(2,1)S(1)} %shard_map.89.refs_1_), channel_id=1, source_target_pairs={{0,2},{2,4},{4,6},{6,7},{7,5},{5,3},{3,1},{1,0},{8,10},{10,12},{12... | collective-permute-start | bytes 2359304 | tf_op jit(solution)/shard_map/ppermute | solution.py:422
  45.4 31.1 %collective-permute-start.12 = (bf16[768,512]{1,0:T(8,128)(2,1)S(1)}, bf16[768,512]{1,0:T(8,128)(2,1)S(1)}, u32[]{:S(2)}, u32[]{:S(2)}) collective-permute-start(bf16[768,512]{1,0:T(8,128)(2,1)S(1)} %shard_map.90.after_ref), channel_id=1, source_target_pairs={{0,1},{2,0},{4,2},{6,4},{7,6},{5,7},{3,5},{1,3},{8,9},{10,8},{12,1... | collective-permute-start | bytes 2359304 | tf_op jit(solution)/shard_map/ppermute | solution.py:422
  54.8 16.2 %collective-permute-start.6 = (f32[64,384]{1,0:T(8,128)S(1)}, f32[64,384]{1,0:T(8,128)S(1)}, u32[]{:S(2)}, u32[]{:S(2)}) collective-permute-start(f32[64,384]{1,0:T(8,128)S(1)} %shard_map.92.refs_1_.low_ref), channel_id=1, source_target_pairs={{0,2},{1,3},{2,0},{3,1},{4,6},{5,7},{6,4},{7,5},{8,10},{9,11},{10,... | collective-permute-start | bytes 294920 | tf_op jit(solution)/shard_map/ppermute | solution.py:446
  59.2 23.3 %collective-permute-start.11 = (bf16[768,512]{1,0:T(8,128)(2,1)S(1)}, bf16[768,512]{1,0:T(8,128)(2,1)S(1)}, u32[]{:S(2)}, u32[]{:S(2)}) collective-permute-start(bf16[768,512]{1,0:T(8,128)(2,1)S(1)} %shard_map.93.refs_1_), channel_id=1, source_target_pairs={{0,2},{2,4},{4,6},{6,7},{7,5},{5,3},{3,1},{1,0},{8,10},{10,12},{12... | collective-permute-start | bytes 2359304 | tf_op jit(solution)/shard_map/ppermute | solution.py:422
  62.5 27.5 %collective-permute-start.10 = (bf16[768,512]{1,0:T(8,128)(2,1)S(1)}, bf16[768,512]{1,0:T(8,128)(2,1)S(1)}, u32[]{:S(2)}, u32[]{:S(2)}) collective-permute-start(bf16[768,512]{1,0:T(8,128)(2,1)S(1)} %shard_map.94.after_ref), channel_id=1, source_target_pairs={{0,1},{2,0},{4,2},{6,4},{7,6},{5,7},{3,5},{1,3},{8,9},{10,8},{12,1... | collective-permute-start | bytes 2359304 | tf_op jit(solution)/shard_map/ppermute | solution.py:422
  71.0 21.8 %collective-permute-start.9 = (f32[64,384]{1,0:T(8,128)S(1)}, f32[64,384]{1,0:T(8,128)S(1)}, u32[]{:S(2)}, u32[]{:S(2)}) collective-permute-start(f32[64,384]{1,0:T(8,128)S(1)} %shard_map.95.refs_1_.low_ref), channel_id=1, source_target_pairs={{0,4},{1,5},{2,6},{3,7},{4,0},{5,1},{6,2},{7,3},{8,12},{9,13},{10,... | collective-permute-start | bytes 294920 | tf_op jit(solution)/shard_map/ppermute | solution.py:446
  76.4 24.6 %collective-permute-start.16 = (bf16[768,512]{1,0:T(8,128)(2,1)S(1)}, bf16[768,512]{1,0:T(8,128)(2,1)S(1)}, u32[]{:S(2)}, u32[]{:S(2)}) collective-permute-start(bf16[768,512]{1,0:T(8,128)(2,1)S(1)} %shard_map.96.refs_1_), channel_id=1, source_target_pairs={{0,2},{2,4},{4,6},{6,7},{7,5},{5,3},{3,1},{1,0},{8,10},{10,12},{12... | collective-permute-start | bytes 2359304 | tf_op jit(solution)/shard_map/ppermute | solution.py:422
  79.3 27.5 %collective-permute-start.15 = (bf16[768,512]{1,0:T(8,128)(2,1)S(1)}, bf16[768,512]{1,0:T(8,128)(2,1)S(1)}, u32[]{:S(2)}, u32[]{:S(2)}) collective-permute-start(bf16[768,512]{1,0:T(8,128)(2,1)S(1)} %shard_map.97.refs_1_), channel_id=1, source_target_pairs={{0,1},{2,0},{4,2},{6,4},{7,6},{5,7},{3,5},{1,3},{8,9},{10,8},{12,1... | collective-permute-start | bytes 2359304 | tf_op jit(solution)/shard_map/ppermute | solution.py:422
  85.3 51.2 %collective-permute-start.17 = (bf16[768,512]{1,0:T(8,128)(2,1)S(1)}, bf16[768,512]{1,0:T(8,128)(2,1)S(1)}, u32[]{:S(2)}, u32[]{:S(2)}) collective-permute-start(bf16[768,512]{1,0:T(8,128)(2,1)S(1)} %shard_map.98.refs_1_), channel_id=1, source_target_pairs={{0,2},{2,4},{4,6},{6,7},{7,5},{5,3},{3,1},{1,0},{8,10},{10,12},{12... | collective-permute-start | bytes 2359304 | tf_op jit(solution)/shard_map/ppermute | solution.py:422
  92.7 30.9 %collective-permute-start.20 = (bf16[768,512]{1,0:T(8,128)(2,1)S(1)}, bf16[768,512]{1,0:T(8,128)(2,1)S(1)}, u32[]{:S(2)}, u32[]{:S(2)}) collective-permute-start(bf16[768,512]{1,0:T(8,128)(2,1)S(1)} %shard_map.99.after_ref), channel_id=1, source_target_pairs={{0,1},{2,0},{4,2},{6,4},{7,6},{5,7},{3,5},{1,3},{8,9},{10,8},{12,1... | collective-permute-start | bytes 2359304 | tf_op jit(solution)/shard_map/ppermute | solution.py:422
  92.8 27.3 %collective-permute-start.14 = (bf16[64,384]{1,0:T(8,128)(2,1)S(1)}, bf16[64,384]{1,0:T(8,128)(2,1)S(1)}, u32[]{:S(2)}, u32[]{:S(2)}) collective-permute-start(bf16[64,384]{1,0:T(8,128)(2,1)S(1)} %shard_map.100.refs_1_.low_ref), channel_id=1, source_target_pairs={{0,1},{1,0},{2,3},{3,2},{4,5},{5,4},{6,7},{7,6},{8,9},{9,8},{10,11... | collective-permute-start | bytes 147464 | tf_op jit(solution)/shard_map/ppermute | solution.py:446
  103.8 16.3 %copy-start.3 = (f32[768,1024]{1,0:T(8,128)S(1)}, f32[768,1024]{1,0:T(8,128)}, u32[]{:S(2)}) copy-start(f32[768,1024]{1,0:T(8,128)} %copy-done.2) | copy-start | bytes 9437188
  103.8 16.3 %copy-start.7 = (s32[3,256]{1,0:T(4,128)S(1)}, s32[3,256]{1,0:T(4,128)}, u32[]{:S(2)}) copy-start(s32[3,256]{1,0:T(4,128)} %place_ref.3) | copy-start | bytes 9220
  103.8 16.3 %copy-start.10 = (bf16[24,64,1024]{2,1,0:T(8,128)(2,1)S(1)}, bf16[24,64,1024]{2,1,0:T(8,128)(2,1)}, u32[]{:S(2)}) copy-start(bf16[24,64,1024]{2,1,0:T(8,128)(2,1)} %copy-done.9) | copy-start | bytes 9437188
  103.8 30.5 %collective-permute-start.19 = (bf16[768,512]{1,0:T(8,128)(2,1)S(1)}, bf16[768,512]{1,0:T(8,128)(2,1)S(1)}, u32[]{:S(2)}, u32[]{:S(2)}) collective-permute-start(bf16[768,512]{1,0:T(8,128)(2,1)S(1)} %shard_map.101.refs_1_), channel_id=1, source_target_pairs={{0,2},{2,4},{4,6},{6,7},{7,5},{5,3},{3,1},{1,0},{8,10},{10,12},{12... | collective-permute-start | bytes 2359304 | tf_op jit(solution)/shard_map/ppermute | solution.py:422
  109.6 30.2 %collective-permute-start.18 = (bf16[768,512]{1,0:T(8,128)(2,1)S(1)}, bf16[768,512]{1,0:T(8,128)(2,1)S(1)}, u32[]{:S(2)}, u32[]{:S(2)}) collective-permute-start(bf16[768,512]{1,0:T(8,128)(2,1)S(1)} %shard_map.102.after_ref), channel_id=1, source_target_pairs={{0,1},{2,0},{4,2},{6,4},{7,6},{5,7},{3,5},{1,3},{8,9},{10,8},{12,1... | collective-permute-start | bytes 2359304 | tf_op jit(solution)/shard_map/ppermute | solution.py:422
  (10 other events, 70.2 us)

commit v8 on v7

--- a/solution.py
+++ b/solution.py
@@ -88,34 +88,42 @@
     )(dests, *operands)
 
 
-def first_hop_kernel(dests, x_ref, w_ref, out_ref, token_ref):
-    token_ref[...] = jnp.zeros_like(token_ref)
-    out_ref[...] = jnp.dot(
-        x_ref[...], w_ref[...], preferred_element_type=jnp.float32
-    ).astype(out_ref.dtype)
+def first_hop_kernel(dests, x_ref, w_ref, out_ref, token_ref, total_ref):
+    now = pl.program_id(0)
+    product = jnp.dot(x_ref[...], w_ref[...], preferred_element_type=jnp.float32)
+
+    @pl.when(now == 0)
+    def _():
+        total_ref[...] = product
+
+    @pl.when((now > 0) & (now < pl.num_programs(0) - 1))
+    def _():
+        total_ref[...] += product
+
+    @pl.when(now == pl.num_programs(0) - 1)
+    def _():
+        out_ref[...] = (total_ref[...] + product).astype(out_ref.dtype)
+        token_ref[...] = jnp.zeros_like(token_ref)
 
 
 def first_hop(dests, offset, half, x, weight):
     rows, depth = x.shape
     half_cols = weight.shape[1] // dests.shape[0] // 2
-    tile = min(256, half_cols)
-    tiles = half_cols // tile
-    row_tile = rows // 4
+    piece = max(256, depth // 4)
     return pl.pallas_call(
         first_hop_kernel,
         grid_spec=pltpu.PrefetchScalarGridSpec(
             num_scalar_prefetch=1,
-            grid=(tiles, rows // row_tile),
+            grid=(depth // piece,),
             in_specs=[
-                pl.BlockSpec((row_tile, depth), lambda j, i, d: (i, 0)),
-                pl.BlockSpec(
-                    (depth, tile), lambda j, i, d: (0, (d[offset] * 2 + half) * tiles + j)
-                ),
+                pl.BlockSpec((rows, piece), lambda k, d: (0, k)),
+                pl.BlockSpec((piece, half_cols), lambda k, d: (k, d[offset] * 2 + half)),
             ],
             out_specs=[
-                pl.BlockSpec((row_tile, tile), lambda j, i, d: (i, j)),
-                pl.BlockSpec((8, 128), lambda j, i, d: (0, 0)),
+                pl.BlockSpec((rows, half_cols), lambda k, d: (0, 0)),
+                pl.BlockSpec((8, 128), lambda k, d: (0, 0)),
             ],
+            scratch_shapes=[pltpu.VMEM((rows, half_cols), jnp.float32)],
         ),
         out_shape=[
             jax.ShapeDtypeStruct((rows, half_cols), jnp.bfloat16),
@@ -126,6 +134,20 @@
             2 * rows * depth * half_cols, 2 * (rows * depth + depth * half_cols)
         ),
     )(dests, x, weight)
+
+
+def touch_kernel(arrived_ref, after_ref, out_ref):
+    out_ref[...] = jnp.zeros_like(out_ref)
+
+
+def touch(arrived, after):
+    return pl.pallas_call(
+        touch_kernel,
+        in_specs=[ANYWHERE, ANYWHERE],
+        out_specs=WHOLE,
+        out_shape=jax.ShapeDtypeStruct((8, 128), jnp.float32),
+        compiler_params=params(),
+    )(arrived, after)
 
 
 def collect_kernel(count, index, table_ref, after_ref, out_ref, sems):
@@ -449,17 +471,18 @@
     apart = 1
     while apart < size:
         sent = over(give if apart == 1 else low, apart)
-        last = turn(number, last)
-        number += 1
-        if apart == 1:
-            own, up_pages = own_terms(
-                dests, local, index, x, output_weight, adapter_up_weight, got_up, last
-            )
-            last = own
+        until = turns - 1 if 2 * apart == size else number + (1 if apart == 1 else 2)
+        while number < min(until, turns - 1):
+            last = turn(number, last)
+            if number == 2:
+                last = touch(got_up, last)
+            if number == 3:
+                own, up_pages = own_terms(
+                    dests, local, index, x, output_weight, adapter_up_weight, got_up, last
+                )
+                last = own
+            number += 1
         apart *= 2
-        while apart == size and number < turns - 1:
-            last = turn(number, last)
-            number += 1
         low = last = add(low, sent, jnp.float32 if apart < size else jnp.bfloat16, last)
     other = over(low, 1)
     last = turn(number, last)

time: 143 us -> 140 us (0.979)
  waiting for transfers between devices: 45.1 us -> 43 us
  Pallas kernels: 68.2 us -> 66.7 us
    ppermute x12, waiting for transfers between devices: 27.8 us -> 17.4 us  [turn(): arrived[half, sign] = lax.ppermute(last, 'tp', moves)]
    ppermute x4, waiting for transfers between devices: 17.3 us -> 25.6 us  [over(): return lax.ppermute(value, 'tp', [(i, i ^ apart) for i in range(size)])]
    ppermute x12, starting transfers between devices: 13.2 us -> 16.5 us  [turn(): arrived[half, sign] = lax.ppermute(last, 'tp', moves)]
    pallas_call x1, Pallas kernels: 7.66 us -> 5.36 us  [first_hop(): pl.pallas_call(first_hop_kernel, grid_spec=pltpu.PrefetchScalarGridSpec(n...]
    ppermute x4, starting transfers between devices: 7.6 us -> 5.6 us  [over(): return lax.ppermute(value, 'tp', [(i, i ^ apart) for i in range(size)])]
    pallas_call x3, Pallas kernels: 0.04 us -> 1.62 us  [add(): pl.pallas_call(add_kernel, in_specs=[WHOLE, WHOLE, ANYWHERE], out_specs=W...]
  transfers between devices with their start and end apart: 21 -> 21, of which waited for: 9 -> 7; matrix products, arithmetic and copies ran while one was open for 1% -> 1% of each run, Pallas kernels for 47% -> 46%
where the time goes in v8:
time: 140 us
  Pallas kernels  66.7 us (48%)
  waiting for transfers between devices  43 us (31%)
  starting transfers between devices  25.6 us (18%)
  local copies, waits for them, and re-layouts  3.39 us (2%)
    pallas_call x13, Pallas kernels, hop(): pl.pallas_call(functools.partial(hop_kernel, received is not None), grid_...  36.6 us
    ppermute x4, waiting for transfers between devices, over(): return lax.ppermute(value, 'tp', [(i, i ^ apart) for i in range(size)])  25.6 us
    ppermute x12, waiting for transfers between devices, turn(): arrived[half, sign] = lax.ppermute(last, 'tp', moves)  17.4 us
    ppermute x12, starting transfers between devices, turn(): arrived[half, sign] = lax.ppermute(last, 'tp', moves)  16.5 us
    pallas_call x1, Pallas kernels, own_terms(): pl.pallas_call(own_kernel, grid_spec=pltpu.PrefetchScalarGridSpec(num_sca...  7.06 us
    pallas_call x1, Pallas kernels, low_rank(): pl.pallas_call(functools.partial(low_kernel, sizes), grid_spec=pltpu.Pref...  5.68 us
    ppermute x4, starting transfers between devices, over(): return lax.ppermute(value, 'tp', [(i, i ^ apart) for i in range(size)])  5.6 us
    pallas_call x1, Pallas kernels, first_hop(): pl.pallas_call(first_hop_kernel, grid_spec=pltpu.PrefetchScalarGridSpec(n...  5.36 us
  transfers between devices with their start and end apart: 21, of which 7 were waited for; matrix products, arithmetic and copies ran while one was open for 1% of the time, Pallas kernels for 46%

profile of v8, /device:TPU:0, one launch (start us, length us, event | category | flops | bytes accessed | tf_op | source)
XLA Modules:
  0.0 139.7 jit_solution(3024614003205889979)
XLA Ops:
  1.0 5.4 %shard_map.82 = (bf16[768,512]{1,0:T(8,128)(2,1)}, f32[8,128]{1,0:T(8,128)}) custom-call(s32[8]{0:T(128)} %compare_select_fusion.3.dests, bf16[768,1024]{1,0:T(8,128)(2,1)} %bitcast.8, bf16[1024,8192]{1,0:T(8,128)(2,1)} %w_ref.29), custom_call_target="tpu_custom_call" | custom-call | flops 24159191040 | bytes 2621440 | tf_op jit(solution)/shard_map/pallas_call | solution.py:113
  9.7 2.8 %shard_map.83.after_ref = bf16[768,512]{1,0:T(8,128)(2,1)S(1)} custom-call(s32[8]{0:T(128)S(1)} %copy-done.6, bf16[768,1024]{1,0:T(8,128)(2,1)S(1)} %bitcast.9, bf16[1024,8192]{1,0:T(8,128)(2,1)} %w_ref.29, f32[8,128]{1,0:T(8,128)S(1)} %copy-done.11), custom_call_target="tpu_custom_call" | custom-call | flops 24159191040 | bytes 4194304 | tf_op jit(solution)/shard_map/pallas_call | solution.py:74
  16.6 2.8 %shard_map.85.refs_0_ = bf16[768,512]{1,0:T(8,128)(2,1)S(1)} custom-call(s32[8]{0:T(128)S(1)} %copy-done.6, bf16[768,1024]{1,0:T(8,128)(2,1)S(1)} %bitcast.10, bf16[1024,8192]{1,0:T(8,128)(2,1)} %w_ref.29, bf16[24,64,1024]{2,1,0:T(8,128)(2,1)S(1)} %shard_map.84.refs_0_), custom_call_target="tpu_custom_call" | custom-call | flops 24159191040 | bytes 4194304 | tf_op jit(solution)/shard_map/pallas_call | solution.py:74
  27.1 5.7 %shard_map.88 = (f32[64,384]{1,0:T(8,128)S(1)}, f32[64,384]{1,0:T(8,128)S(1)}) custom-call(s32[24]{0:T(128)S(1)} %compare_convert_fusion.local, s32[24]{0:T(128)S(1)} %get-tuple-element.18.index, s32[1]{0:T(128)} %bitcast.1.side, bf16[768,1024]{1,0:T(8,128)(2,1)S(1)} %bitcast.12, s32[3,256]{1,0:T(4,128)S(1)} %copy-done.4, bf16[96,64,1024]{2,1,0:T(8,128)(2,1)} %table_ref.6, ...), custom_call_target="tpu_custom_call" | custom-call | flops 12079595520 | bytes 4718592 | tf_op jit(solution)/shard_map/pallas_call | solution.py:238
  34.7 3.0 %shard_map.89.refs_1_ = bf16[768,512]{1,0:T(8,128)(2,1)S(1)} custom-call(s32[8]{0:T(128)S(1)} %copy-done.6, bf16[768,1024]{1,0:T(8,128)(2,1)S(1)} %bitcast.13, bf16[1024,8192]{1,0:T(8,128)(2,1)} %w_ref.29, bf16[768,512]{1,0:T(8,128)(2,1)} %collective-permute-done.7.refs_0_, f32[64,384]{1,0:T(8,128)S(1)} %get-tuple-element.12.refs_1_.low_ref), custom_call_target="tpu_custom_call" | custom-call | flops 24159191040 | bytes 4194304 | tf_op jit(solution)/shard_map/pallas_call | solution.py:74
  39.4 2.8 %shard_map.90.after_ref = bf16[768,512]{1,0:T(8,128)(2,1)S(1)} custom-call(s32[8]{0:T(128)S(1)} %copy-done.6, bf16[768,1024]{1,0:T(8,128)(2,1)S(1)} %bitcast.14, bf16[1024,8192]{1,0:T(8,128)(2,1)} %w_ref.29, bf16[768,512]{1,0:T(8,128)(2,1)S(1)} %collective-permute-done.6.refs_0_, bf16[768,512]{1,0:T(8,128)(2,1)S(1)} %shard_map.89.refs_1_), custom_call_target="tpu_custom_call" | custom-call | flops 24159191040 | bytes 4194304 | tf_op jit(solution)/shard_map/pallas_call | solution.py:74
  42.6 6.7 %collective-permute-done.5.sent_ref = f32[64,384]{1,0:T(8,128)S(1)} collective-permute-done((f32[64,384]{1,0:T(8,128)S(1)}, f32[64,384]{1,0:T(8,128)S(1)}, u32[]{:S(2)}, u32[]{:S(2)}) %collective-permute-start.5) | collective-permute-done | bytes 98336 | tf_op jit(solution)/shard_map/ppermute | solution.py:468
  50.0 2.8 %shard_map.93.refs_1_ = bf16[768,512]{1,0:T(8,128)(2,1)S(1)} custom-call(s32[8]{0:T(128)S(1)} %copy-done.6, bf16[768,1024]{1,0:T(8,128)(2,1)S(1)} %bitcast.15, bf16[1024,8192]{1,0:T(8,128)(2,1)} %w_ref.29, bf16[768,512]{1,0:T(8,128)(2,1)S(1)} %collective-permute-done.3.refs_0_, f32[64,384]{1,0:T(8,128)} %shard_map.92.refs_1_.low_ref), custom_call_target="tpu_custom_call" | custom-call | flops 24159191040 | bytes 4194304 | tf_op jit(solution)/shard_map/pallas_call | solution.py:74
  54.9 2.8 %shard_map.94.after_ref = bf16[768,512]{1,0:T(8,128)(2,1)S(1)} custom-call(s32[8]{0:T(128)S(1)} %copy-done.6, bf16[768,1024]{1,0:T(8,128)(2,1)S(1)} %bitcast.16, bf16[1024,8192]{1,0:T(8,128)(2,1)} %w_ref.29, bf16[768,512]{1,0:T(8,128)(2,1)S(1)} %collective-permute-done.2.refs_0_, bf16[768,512]{1,0:T(8,128)(2,1)S(1)} %shard_map.93.refs_1_), custom_call_target="tpu_custom_call" | custom-call | flops 24159191040 | bytes 4194304 | tf_op jit(solution)/shard_map/pallas_call | solution.py:74
  58.2 7.1 %shard_map.95 = (f32[768,1024]{1,0:T(8,128)S(1)}, bf16[24,64,1024]{2,1,0:T(8,128)(2,1)S(1)}) custom-call(s32[24]{0:T(128)S(1)} %compare_convert_fusion.local, s32[24]{0:T(128)S(1)} %get-tuple-element.18.index, s32[8]{0:T(128)S(1)} %copy-done.6, bf16[768,1024]{1,0:T(8,128)(2,1)S(1)} %bitcast.17, bf16[1024,8192]{1,0:T(8,128)(2,1)} %w_ref.29, ...), custom_call_target="tpu_custom_call" | custom-call | flops 48318382080 | bytes 13107200 | tf_op jit(solution)/shard_map/pallas_call | solution.py:297
  66.9 3.2 %shard_map.96.refs_1_ = bf16[768,512]{1,0:T(8,128)(2,1)S(1)} custom-call(s32[8]{0:T(128)S(1)} %copy-done.6, bf16[768,1024]{1,0:T(8,128)(2,1)S(1)} %bitcast.18, bf16[1024,8192]{1,0:T(8,128)(2,1)} %w_ref.29, bf16[768,512]{1,0:T(8,128)(2,1)S(1)} %collective-permute-done.10.refs_0_, f32[768,1024]{1,0:T(8,128)S(1)} %get-tuple-element.15.refs_1_.own_ref), custom_call_target="tpu_custom_call" | custom-call | flops 24159191040 | bytes 4194304 | tf_op jit(solution)/shard_map/pallas_call | solution.py:74
  70.1 4.8 %collective-permute-start.16 = (bf16[768,512]{1,0:T(8,128)(2,1)S(1)}, bf16[768,512]{1,0:T(8,128)(2,1)S(1)}, u32[]{:S(2)}, u32[]{:S(2)}) collective-permute-start(bf16[768,512]{1,0:T(8,128)(2,1)S(1)} %shard_map.96.refs_1_), channel_id=1, source_target_pairs={{0,2},{2,4},{4,6},{6,7},{7,5},{5,3},{3,1},{1,0},{8,10},{10,12},{12... | collective-permute-start | bytes 2359304 | tf_op jit(solution)/shard_map/ppermute | solution.py:444
  74.8 2.8 %shard_map.97.after_ref = bf16[768,512]{1,0:T(8,128)(2,1)S(1)} custom-call(s32[8]{0:T(128)S(1)} %copy-done.6, bf16[768,1024]{1,0:T(8,128)(2,1)S(1)} %bitcast.19, bf16[1024,8192]{1,0:T(8,128)(2,1)} %w_ref.29, bf16[768,512]{1,0:T(8,128)(2,1)S(1)} %collective-permute-done.9.refs_0_, bf16[768,512]{1,0:T(8,128)(2,1)S(1)} %shard_map.96.refs_1_), custom_call_target="tpu_custom_call" | custom-call | flops 24159191040 | bytes 4194304 | tf_op jit(solution)/shard_map/pallas_call | solution.py:74
  78.6 3.5 %collective-permute-start.11 = (f32[64,384]{1,0:T(8,128)S(1)}, f32[64,384]{1,0:T(8,128)S(1)}, u32[]{:S(2)}, u32[]{:S(2)}) collective-permute-start(f32[64,384]{1,0:T(8,128)S(1)} %shard_map.98.refs_1_.low_ref), channel_id=1, source_target_pairs={{0,4},{1,5},{2,6},{3,7},{4,0},{5,1},{6,2},{7,3},{8,12},{9,13},{10,... | collective-permute-start | bytes 294920 | tf_op jit(solution)/shard_map/ppermute | solution.py:468
  82.1 2.8 %shard_map.99.refs_1_ = bf16[768,512]{1,0:T(8,128)(2,1)S(1)} custom-call(s32[8]{0:T(128)S(1)} %copy-done.6, bf16[768,1024]{1,0:T(8,128)(2,1)S(1)} %bitcast.20, bf16[1024,8192]{1,0:T(8,128)(2,1)} %w_ref.29, bf16[768,512]{1,0:T(8,128)(2,1)S(1)} %collective-permute-done.13.refs_0_, f32[64,384]{1,0:T(8,128)S(1)} %shard_map.98.refs_1_.low_ref), custom_call_target="tpu_custom_call" | custom-call | flops 24159191040 | bytes 4194304 | tf_op jit(solution)/shard_map/pallas_call | solution.py:74
  85.6 2.8 %shard_map.100.after_ref = bf16[768,512]{1,0:T(8,128)(2,1)S(1)} custom-call(s32[8]{0:T(128)S(1)} %copy-done.6, bf16[768,1024]{1,0:T(8,128)(2,1)S(1)} %bitcast.21, bf16[1024,8192]{1,0:T(8,128)(2,1)} %w_ref.29, bf16[768,512]{1,0:T(8,128)(2,1)S(1)} %collective-permute-done.12.refs_0_, bf16[768,512]{1,0:T(8,128)(2,1)S(1)} %shard_map.99.refs_1_), custom_call_target="tpu_custom_call" | custom-call | flops 24159191040 | bytes 4194304 | tf_op jit(solution)/shard_map/pallas_call | solution.py:74
  89.8 14.0 %collective-permute-done.11.sent_ref = f32[64,384]{1,0:T(8,128)S(1)} collective-permute-done((f32[64,384]{1,0:T(8,128)S(1)}, f32[64,384]{1,0:T(8,128)S(1)}, u32[]{:S(2)}, u32[]{:S(2)}) %collective-permute-start.11) | collective-permute-done | bytes 98336 | tf_op jit(solution)/shard_map/ppermute | solution.py:468
  104.1 2.8 %shard_map.102.refs_1_ = bf16[768,512]{1,0:T(8,128)(2,1)S(1)} custom-call(s32[8]{0:T(128)S(1)} %copy-done.6, bf16[768,1024]{1,0:T(8,128)(2,1)S(1)} %bitcast.22, bf16[1024,8192]{1,0:T(8,128)(2,1)} %w_ref.29, bf16[768,512]{1,0:T(8,128)(2,1)S(1)} %collective-permute-done.16.refs_0_, bf16[64,384]{1,0:T(8,128)(2,1)S(1)} %shard_map.101.refs_1_.low_ref), custom_call_target="tpu_custom_call" | custom-call | flops 24159191040 | bytes 4194304 | tf_op jit(solution)/shard_map/pallas_call | solution.py:74
  106.9 3.2 %collective-permute-start.19 = (bf16[768,512]{1,0:T(8,128)(2,1)S(1)}, bf16[768,512]{1,0:T(8,128)(2,1)S(1)}, u32[]{:S(2)}, u32[]{:S(2)}) collective-permute-start(bf16[768,512]{1,0:T(8,128)(2,1)S(1)} %shard_map.102.refs_1_), channel_id=1, source_target_pairs={{0,2},{2,4},{4,6},{6,7},{7,5},{5,3},{3,1},{1,0},{8,10},{10,12},{12... | collective-permute-start | bytes 2359304 | tf_op jit(solution)/shard_map/ppermute | solution.py:444
  110.1 2.8 %shard_map.103.after_ref = bf16[768,512]{1,0:T(8,128)(2,1)S(1)} custom-call(s32[8]{0:T(128)S(1)} %copy-done.6, bf16[768,1024]{1,0:T(8,128)(2,1)S(1)} %bitcast.23, bf16[1024,8192]{1,0:T(8,128)(2,1)} %w_ref.29, bf16[768,512]{1,0:T(8,128)(2,1)S(1)} %collective-permute-done.15.refs_0_, bf16[768,512]{1,0:T(8,128)(2,1)S(1)} %shard_map.102.refs_1_), custom_call_target="tpu_custom_call" | custom-call | flops 24159191040 | bytes 4194304 | tf_op jit(solution)/shard_map/pallas_call | solution.py:74
  112.9 4.9 %collective-permute-done.14.other_ref = bf16[64,384]{1,0:T(8,128)(2,1)S(1)} collective-permute-done((bf16[64,384]{1,0:T(8,128)(2,1)S(1)}, bf16[64,384]{1,0:T(8,128)(2,1)S(1)}, u32[]{:S(2)}, u32[]{:S(2)}) %collective-permute-start.14) | collective-permute-done | bytes 49184 | tf_op jit(solution)/shard_map/ppermute | solution.py:468
  118.5 2.9 %collective-permute-done.20.two_ref = bf16[768,512]{1,0:T(8,128)(2,1)S(1)} collective-permute-done((bf16[768,512]{1,0:T(8,128)(2,1)S(1)}, bf16[768,512]{1,0:T(8,128)(2,1)S(1)}, u32[]{:S(2)}, u32[]{:S(2)}) %collective-permute-start.20) | collective-permute-done | bytes 786464 | tf_op jit(solution)/shard_map/ppermute | solution.py:444
  121.4 10.7 %collective-permute-done.19.one_ref = bf16[768,512]{1,0:T(8,128)(2,1)S(1)} collective-permute-done((bf16[768,512]{1,0:T(8,128)(2,1)S(1)}, bf16[768,512]{1,0:T(8,128)(2,1)S(1)}, u32[]{:S(2)}, u32[]{:S(2)}) %collective-permute-start.19) | collective-permute-done | bytes 786464 | tf_op jit(solution)/shard_map/ppermute | solution.py:444
  134.2 3.3 %collective-permute-done.18.two_ref = bf16[768,512]{1,0:T(8,128)(2,1)S(1)} collective-permute-done((bf16[768,512]{1,0:T(8,128)(2,1)S(1)}, bf16[768,512]{1,0:T(8,128)(2,1)S(1)}, u32[]{:S(2)}, u32[]{:S(2)}) %collective-permute-start.18) | collective-permute-done | bytes 786464 | tf_op jit(solution)/shard_map/ppermute | solution.py:444
  (78 shorter events, 33.5 us)
Async XLA Ops:
  0.0 12.8 %copy-start = (s32[192]{0:T(256)S(1)}, s32[192]{0:T(256)}, u32[]{:S(2)}) copy-start(s32[192]{0:T(256)} %param.12) | copy-start | bytes 2308
  0.0 12.6 %collective-permute-start = (s32[3,2,4]{2,1,0:T(2,128)}, s32[3,2,4]{2,1,0:T(2,128)S(1)}, u32[]{:S(2)}, u32[]{:S(2)}) collective-permute-start(s32[3,2,4]{2,1,0:T(2,128)} %param.13), channel_id=1, source_target_pairs={{0,8},{8,0},{1,9},{9,1},{2,10},{10,2},{3,11},{11,3},{4,12},{12,4},... | collective-permute-start | bytes 296 | tf_op jit(solution)/shard_map/ppermute | solution.py:448
  6.4 26.4 %collective-permute-start.7 = (bf16[768,512]{1,0:T(8,128)(2,1)}, bf16[768,512]{1,0:T(8,128)(2,1)}, u32[]{:S(2)}, u32[]{:S(2)}) collective-permute-start(bf16[768,512]{1,0:T(8,128)(2,1)} %get-tuple-element.14), channel_id=1, source_target_pairs={{0,2},{2,4},{4,6},{6,7},{7,5},{5,3},{3,1},{1,0},{8,10},{10,12},{12... | collective-permute-start | bytes 2359304 | tf_op jit(solution)/shard_map/ppermute | solution.py:435
  12.5 25.2 %collective-permute-start.6 = (bf16[768,512]{1,0:T(8,128)(2,1)S(1)}, bf16[768,512]{1,0:T(8,128)(2,1)S(1)}, u32[]{:S(2)}, u32[]{:S(2)}) collective-permute-start(bf16[768,512]{1,0:T(8,128)(2,1)S(1)} %shard_map.83.after_ref), channel_id=1, source_target_pairs={{0,1},{2,0},{4,2},{6,4},{7,6},{5,7},{3,5},{1,3},{8,9},{10,8},{12,1... | collective-permute-start | bytes 2359304 | tf_op jit(solution)/shard_map/ppermute | solution.py:451
  16.4 10.7 %collective-permute-start.4 = (bf16[24,64,1024]{2,1,0:T(8,128)(2,1)S(1)}, bf16[24,64,1024]{2,1,0:T(8,128)(2,1)S(1)}, u32[]{:S(2)}, u32[]{:S(2)}) collective-permute-start(bf16[24,64,1024]{2,1,0:T(8,128)(2,1)S(1)} %shard_map.84.refs_0_), channel_id=1, source_target_pairs={{0,8},{8,0},{1,9},{9,1},{2,10},{10,2},{3,11},{11,3},{4,12},{12,4},... | collective-permute-start | bytes 9437192 | tf_op jit(solution)/shard_map/ppermute | solution.py:457
  19.4 30.6 %collective-permute-start.3 = (bf16[768,512]{1,0:T(8,128)(2,1)S(1)}, bf16[768,512]{1,0:T(8,128)(2,1)S(1)}, u32[]{:S(2)}, u32[]{:S(2)}) collective-permute-start(bf16[768,512]{1,0:T(8,128)(2,1)S(1)} %shard_map.85.refs_0_), channel_id=1, source_target_pairs={{0,2},{2,4},{4,6},{6,7},{7,5},{5,3},{3,1},{1,0},{8,10},{10,12},{12... | collective-permute-start | bytes 2359304 | tf_op jit(solution)/shard_map/ppermute | solution.py:444
  24.1 30.8 %collective-permute-start.2 = (bf16[768,512]{1,0:T(8,128)(2,1)S(1)}, bf16[768,512]{1,0:T(8,128)(2,1)S(1)}, u32[]{:S(2)}, u32[]{:S(2)}) collective-permute-start(bf16[768,512]{1,0:T(8,128)(2,1)S(1)} %shard_map.86.after_ref), channel_id=1, source_target_pairs={{0,1},{2,0},{4,2},{6,4},{7,6},{5,7},{3,5},{1,3},{8,9},{10,8},{12,1... | collective-permute-start | bytes 2359304 | tf_op jit(solution)/shard_map/ppermute | solution.py:444
  27.0 15.1 %collective-permute-start.1 = (bf16[24,64,1024]{2,1,0:T(8,128)(2,1)S(1)}, bf16[24,64,1024]{2,1,0:T(8,128)(2,1)S(1)}, u32[]{:S(2)}, u32[]{:S(2)}) collective-permute-start(bf16[24,64,1024]{2,1,0:T(8,128)(2,1)S(1)} %shard_map.87.after_ref), channel_id=1, source_target_pairs={{0,8},{8,0},{1,9},{9,1},{2,10},{10,2},{3,11},{11,3},{4,12},{12,4},... | collective-permute-start | bytes 9437192 | tf_op jit(solution)/shard_map/ppermute | solution.py:460
  32.8 16.5 %collective-permute-start.5 = (f32[64,384]{1,0:T(8,128)S(1)}, f32[64,384]{1,0:T(8,128)S(1)}, u32[]{:S(2)}, u32[]{:S(2)}) collective-permute-start(f32[64,384]{1,0:T(8,128)S(1)} %get-tuple-element.13), channel_id=1, source_target_pairs={{0,1},{1,0},{2,3},{3,2},{4,5},{5,4},{6,7},{7,6},{8,9},{9,8},{10,11... | collective-permute-start | bytes 294920 | tf_op jit(solution)/shard_map/ppermute | solution.py:468
  37.7 29.2 %collective-permute-start.10 = (bf16[768,512]{1,0:T(8,128)(2,1)S(1)}, bf16[768,512]{1,0:T(8,128)(2,1)S(1)}, u32[]{:S(2)}, u32[]{:S(2)}) collective-permute-start(bf16[768,512]{1,0:T(8,128)(2,1)S(1)} %shard_map.89.refs_1_), channel_id=1, source_target_pairs={{0,2},{2,4},{4,6},{6,7},{7,5},{5,3},{3,1},{1,0},{8,10},{10,12},{12... | collective-permute-start | bytes 2359304 | tf_op jit(solution)/shard_map/ppermute | solution.py:444
  42.1 32.7 %collective-permute-start.9 = (bf16[768,512]{1,0:T(8,128)(2,1)S(1)}, bf16[768,512]{1,0:T(8,128)(2,1)S(1)}, u32[]{:S(2)}, u32[]{:S(2)}) collective-permute-start(bf16[768,512]{1,0:T(8,128)(2,1)S(1)} %shard_map.90.after_ref), channel_id=1, source_target_pairs={{0,1},{2,0},{4,2},{6,4},{7,6},{5,7},{3,5},{1,3},{8,9},{10,8},{12,1... | collective-permute-start | bytes 2359304 | tf_op jit(solution)/shard_map/ppermute | solution.py:444
  50.0 27.7 %collective-permute-start.8 = (f32[64,384]{1,0:T(8,128)}, f32[64,384]{1,0:T(8,128)}, u32[]{:S(2)}, u32[]{:S(2)}) collective-permute-start(f32[64,384]{1,0:T(8,128)} %shard_map.92.refs_1_.low_ref), channel_id=1, source_target_pairs={{0,2},{1,3},{2,0},{3,1},{4,6},{5,7},{6,4},{7,5},{8,10},{9,11},{10,... | collective-permute-start | bytes 294920 | tf_op jit(solution)/shard_map/ppermute | solution.py:468
  52.8 29.4 %collective-permute-start.13 = (bf16[768,512]{1,0:T(8,128)(2,1)S(1)}, bf16[768,512]{1,0:T(8,128)(2,1)S(1)}, u32[]{:S(2)}, u32[]{:S(2)}) collective-permute-start(bf16[768,512]{1,0:T(8,128)(2,1)S(1)} %shard_map.93.refs_1_), channel_id=1, source_target_pairs={{0,2},{2,4},{4,6},{6,7},{7,5},{5,3},{3,1},{1,0},{8,10},{10,12},{12... | collective-permute-start | bytes 2359304 | tf_op jit(solution)/shard_map/ppermute | solution.py:444
  57.6 27.9 %collective-permute-start.12 = (bf16[768,512]{1,0:T(8,128)(2,1)S(1)}, bf16[768,512]{1,0:T(8,128)(2,1)S(1)}, u32[]{:S(2)}, u32[]{:S(2)}) collective-permute-start(bf16[768,512]{1,0:T(8,128)(2,1)S(1)} %shard_map.94.after_ref), channel_id=1, source_target_pairs={{0,1},{2,0},{4,2},{6,4},{7,6},{5,7},{3,5},{1,3},{8,9},{10,8},{12,1... | collective-permute-start | bytes 2359304 | tf_op jit(solution)/shard_map/ppermute | solution.py:444
  70.1 34.0 %collective-permute-start.16 = (bf16[768,512]{1,0:T(8,128)(2,1)S(1)}, bf16[768,512]{1,0:T(8,128)(2,1)S(1)}, u32[]{:S(2)}, u32[]{:S(2)}) collective-permute-start(bf16[768,512]{1,0:T(8,128)(2,1)S(1)} %shard_map.96.refs_1_), channel_id=1, source_target_pairs={{0,2},{2,4},{4,6},{6,7},{7,5},{5,3},{3,1},{1,0},{8,10},{10,12},{12... | collective-permute-start | bytes 2359304 | tf_op jit(solution)/shard_map/ppermute | solution.py:444
  77.6 32.5 %collective-permute-start.15 = (bf16[768,512]{1,0:T(8,128)(2,1)S(1)}, bf16[768,512]{1,0:T(8,128)(2,1)S(1)}, u32[]{:S(2)}, u32[]{:S(2)}) collective-permute-start(bf16[768,512]{1,0:T(8,128)(2,1)S(1)} %shard_map.97.after_ref), channel_id=1, source_target_pairs={{0,1},{2,0},{4,2},{6,4},{7,6},{5,7},{3,5},{1,3},{8,9},{10,8},{12,1... | collective-permute-start | bytes 2359304 | tf_op jit(solution)/shard_map/ppermute | solution.py:444
  78.6 25.2 %collective-permute-start.11 = (f32[64,384]{1,0:T(8,128)S(1)}, f32[64,384]{1,0:T(8,128)S(1)}, u32[]{:S(2)}, u32[]{:S(2)}) collective-permute-start(f32[64,384]{1,0:T(8,128)S(1)} %shard_map.98.refs_1_.low_ref), channel_id=1, source_target_pairs={{0,4},{1,5},{2,6},{3,7},{4,0},{5,1},{6,2},{7,3},{8,12},{9,13},{10,... | collective-permute-start | bytes 294920 | tf_op jit(solution)/shard_map/ppermute | solution.py:468
  84.9 49.3 %collective-permute-start.17 = (bf16[768,512]{1,0:T(8,128)(2,1)S(1)}, bf16[768,512]{1,0:T(8,128)(2,1)S(1)}, u32[]{:S(2)}, u32[]{:S(2)}) collective-permute-start(bf16[768,512]{1,0:T(8,128)(2,1)S(1)} %shard_map.99.refs_1_), channel_id=1, source_target_pairs={{0,2},{2,4},{4,6},{6,7},{7,5},{5,3},{3,1},{1,0},{8,10},{10,12},{12... | collective-permute-start | bytes 2359304 | tf_op jit(solution)/shard_map/ppermute | solution.py:444
  88.3 33.0 %collective-permute-start.20 = (bf16[768,512]{1,0:T(8,128)(2,1)S(1)}, bf16[768,512]{1,0:T(8,128)(2,1)S(1)}, u32[]{:S(2)}, u32[]{:S(2)}) collective-permute-start(bf16[768,512]{1,0:T(8,128)(2,1)S(1)} %shard_map.100.after_ref), channel_id=1, source_target_pairs={{0,1},{2,0},{4,2},{6,4},{7,6},{5,7},{3,5},{1,3},{8,9},{10,8},{12,1... | collective-permute-start | bytes 2359304 | tf_op jit(solution)/shard_map/ppermute | solution.py:444
  103.8 14.0 %collective-permute-start.14 = (bf16[64,384]{1,0:T(8,128)(2,1)S(1)}, bf16[64,384]{1,0:T(8,128)(2,1)S(1)}, u32[]{:S(2)}, u32[]{:S(2)}) collective-permute-start(bf16[64,384]{1,0:T(8,128)(2,1)S(1)} %shard_map.101.refs_1_.low_ref), channel_id=1, source_target_pairs={{0,1},{1,0},{2,3},{3,2},{4,5},{5,4},{6,7},{7,6},{8,9},{9,8},{10,11... | collective-permute-start | bytes 147464 | tf_op jit(solution)/shard_map/ppermute | solution.py:468
  106.9 10.9 %copy-start.5 = (s32[3,256]{1,0:T(4,128)S(1)}, s32[3,256]{1,0:T(4,128)}, u32[]{:S(2)}) copy-start(s32[3,256]{1,0:T(4,128)} %place_ref.3) | copy-start | bytes 9220
  106.9 25.1 %collective-permute-start.19 = (bf16[768,512]{1,0:T(8,128)(2,1)S(1)}, bf16[768,512]{1,0:T(8,128)(2,1)S(1)}, u32[]{:S(2)}, u32[]{:S(2)}) collective-permute-start(bf16[768,512]{1,0:T(8,128)(2,1)S(1)} %shard_map.102.refs_1_), channel_id=1, source_target_pairs={{0,2},{2,4},{4,6},{6,7},{7,5},{5,3},{3,1},{1,0},{8,10},{10,12},{12... | collective-permute-start | bytes 2359304 | tf_op jit(solution)/shard_map/ppermute | solution.py:444
  112.9 24.6 %collective-permute-start.18 = (bf16[768,512]{1,0:T(8,128)(2,1)S(1)}, bf16[768,512]{1,0:T(8,128)(2,1)S(1)}, u32[]{:S(2)}, u32[]{:S(2)}) collective-permute-start(bf16[768,512]{1,0:T(8,128)(2,1)S(1)} %shard_map.103.after_ref), channel_id=1, source_target_pairs={{0,1},{2,0},{4,2},{6,4},{7,6},{5,7},{3,5},{1,3},{8,9},{10,8},{12,1... | collective-permute-start | bytes 2359304 | tf_op jit(solution)/shard_map/ppermute | solution.py:444
  117.8 14.2 %copy-start.2 = (s32[3,1]{0,1:T(1,128)S(1)}, s32[3,1]{0,1:T(1,128)}, u32[]{:S(2)}) copy-start(s32[3,1]{0,1:T(1,128)} %param.15) | copy-start | bytes 40
  (10 other events, 56.8 us)

commit v9 on v8

--- a/solution.py
+++ b/solution.py
@@ -8,7 +8,7 @@
 from jax.sharding import PartitionSpec as P
 
 VMEM_LIMIT = 40 * 1024 * 1024
-FIRST_VMEM_LIMIT = 60 * 1024 * 1024
+LOW_SCALE = 16.0
 SWAP = [(0, 1), (1, 0)]
 WHOLE = pl.BlockSpec(memory_space=pltpu.VMEM)
 ANYWHERE = pl.BlockSpec(memory_space=pl.ANY)
@@ -44,39 +44,51 @@
     return pl.CostEstimate(flops=30 * flops, bytes_accessed=size, transcendentals=0)
 
 
-def hop_kernel(with_received, dests, x_ref, w_ref, *refs):
+def hop_kernel(pieces, dests, x_ref, w_ref, *refs):
     tile = w_ref.shape[1]
-    columns = pl.ds(pl.multiple_of(pl.program_id(0) * tile, tile), tile)
+    now = pl.program_id(0)
+    columns = pl.ds(pl.multiple_of(now * tile, tile), tile)
     total = jnp.dot(x_ref[...], w_ref[...], preferred_element_type=jnp.float32)
-    if with_received:
-        total = total + refs[0][:, columns].astype(jnp.float32)
-    refs[-1][:, columns] = total.astype(refs[-1].dtype)
+    out_ref = refs[-1]
+    if len(pieces) == 1:
+        out_ref[:, columns] = (total + refs[0][:, columns].astype(jnp.float32)).astype(
+            out_ref.dtype
+        )
+    elif pieces:
+        for piece, received_ref in zip(pieces, refs):
+
+            @pl.when(now == piece)
+            def _():
+                out_ref[:, columns] = (total + received_ref[...].astype(jnp.float32)).astype(
+                    out_ref.dtype
+                )
+
+    else:
+        out_ref[:, columns] = total.astype(out_ref.dtype)
+
+
+def tiling(dests, weight):
+    half_cols = weight.shape[1] // dests.shape[0] // 2
+    tile = min(256, half_cols)
+    return half_cols, tile, half_cols // tile
 
 
 def hop(dests, offset, half, x, weight, received, after):
     rows, depth = x.shape
-    half_cols = weight.shape[1] // dests.shape[0] // 2
-    tile = min(256, half_cols)
-    tiles = half_cols // tile
-    in_specs = [
-        WHOLE,
-        pl.BlockSpec(
-            (depth, tile), lambda j, d: (0, (d[offset] * 2 + half) * tiles + j)
-        ),
-    ]
-    operands = [x, weight]
-    if received is not None:
-        in_specs.append(WHOLE)
-        operands.append(received)
-    if after is not None:
-        in_specs.append(ANYWHERE)
-        operands.append(after)
-    return pl.pallas_call(
-        functools.partial(hop_kernel, received is not None),
+    half_cols, tile, tiles = tiling(dests, weight)
+    return pl.pallas_call(
+        functools.partial(hop_kernel, tuple(range(len(received)))),
         grid_spec=pltpu.PrefetchScalarGridSpec(
             num_scalar_prefetch=1,
             grid=(tiles,),
-            in_specs=in_specs,
+            in_specs=[
+                WHOLE,
+                pl.BlockSpec(
+                    (depth, tile), lambda j, d: (0, (d[offset] * 2 + half) * tiles + j)
+                ),
+            ]
+            + [WHOLE] * len(received)
+            + [ANYWHERE],
             out_specs=WHOLE,
         ),
         out_shape=jax.ShapeDtypeStruct((rows, half_cols), jnp.bfloat16),
@@ -85,69 +97,57 @@
             2 * rows * depth * half_cols,
             2 * (rows * depth + depth * half_cols + 2 * rows * half_cols),
         ),
-    )(dests, *operands)
-
-
-def first_hop_kernel(dests, x_ref, w_ref, out_ref, token_ref, total_ref):
-    now = pl.program_id(0)
-    product = jnp.dot(x_ref[...], w_ref[...], preferred_element_type=jnp.float32)
-
-    @pl.when(now == 0)
-    def _():
-        total_ref[...] = product
-
-    @pl.when((now > 0) & (now < pl.num_programs(0) - 1))
-    def _():
-        total_ref[...] += product
-
-    @pl.when(now == pl.num_programs(0) - 1)
-    def _():
-        out_ref[...] = (total_ref[...] + product).astype(out_ref.dtype)
-        token_ref[...] = jnp.zeros_like(token_ref)
-
-
-def first_hop(dests, offset, half, x, weight):
+    )(dests, x, weight, *received, after)
+
+
+def first_kernel(with_after, dests, x_ref, w_ref, *refs):
+    total = jnp.dot(x_ref[...], w_ref[...], preferred_element_type=jnp.float32)
+    for chain, out_ref in enumerate(refs[-2:]):
+
+        @pl.when(pl.program_id(0) == chain)
+        def _():
+            out_ref[...] = total.astype(out_ref.dtype)
+
+
+def first_pieces(dests, offset, piece, x, weight, after):
     rows, depth = x.shape
-    half_cols = weight.shape[1] // dests.shape[0] // 2
-    piece = max(256, depth // 4)
-    return pl.pallas_call(
-        first_hop_kernel,
+    _, tile, tiles = tiling(dests, weight)
+    size = dests.shape[0]
+
+    def place(j, d):
+        one = d[offset] * 2 * tiles + piece
+        two = (d[(size - offset) % size] * 2 + 1) * tiles + piece
+        return (0, jnp.where(j == 0, one, two))
+
+    tail = [] if after is None else [after]
+    return pl.pallas_call(
+        functools.partial(first_kernel, after is not None),
         grid_spec=pltpu.PrefetchScalarGridSpec(
             num_scalar_prefetch=1,
-            grid=(depth // piece,),
-            in_specs=[
-                pl.BlockSpec((rows, piece), lambda k, d: (0, k)),
-                pl.BlockSpec((piece, half_cols), lambda k, d: (k, d[offset] * 2 + half)),
-            ],
-            out_specs=[
-                pl.BlockSpec((rows, half_cols), lambda k, d: (0, 0)),
-                pl.BlockSpec((8, 128), lambda k, d: (0, 0)),
-            ],
-            scratch_shapes=[pltpu.VMEM((rows, half_cols), jnp.float32)],
-        ),
-        out_shape=[
-            jax.ShapeDtypeStruct((rows, half_cols), jnp.bfloat16),
-            jax.ShapeDtypeStruct((8, 128), jnp.float32),
-        ],
-        compiler_params=pltpu.CompilerParams(vmem_limit_bytes=FIRST_VMEM_LIMIT),
+            grid=(2,),
+            in_specs=[WHOLE, pl.BlockSpec((depth, tile), place)] + [ANYWHERE] * len(tail),
+            out_specs=[WHOLE, WHOLE],
+        ),
+        out_shape=[jax.ShapeDtypeStruct((rows, tile), jnp.bfloat16)] * 2,
+        compiler_params=params(),
         cost_estimate=cost(
-            2 * rows * depth * half_cols, 2 * (rows * depth + depth * half_cols)
-        ),
-    )(dests, x, weight)
-
-
-def touch_kernel(arrived_ref, after_ref, out_ref):
-    out_ref[...] = jnp.zeros_like(out_ref)
-
-
-def touch(arrived, after):
+            4 * rows * depth * tile, 2 * (rows * depth + 2 * depth * tile + 2 * rows * tile)
+        ),
+    )(dests, x, weight, *tail)
+
+
+def touch_kernel(*refs):
+    refs[-1][...] = jnp.zeros_like(refs[-1])
+
+
+def touch(*arrays):
     return pl.pallas_call(
         touch_kernel,
-        in_specs=[ANYWHERE, ANYWHERE],
+        in_specs=[ANYWHERE] * len(arrays),
         out_specs=WHOLE,
         out_shape=jax.ShapeDtypeStruct((8, 128), jnp.float32),
         compiler_params=params(),
-    )(arrived, after)
+    )(*arrays)
 
 
 def collect_kernel(count, index, table_ref, after_ref, out_ref, sems):
@@ -430,31 +430,31 @@
     far = size // 2
     pairs = [[(0, 1, forward), (1, -1, backward)], [(1, 1, forward), (0, -1, backward)]]
     arrived = {}
-    half, sign, moves = pairs[0][0]
-    first, token = first_hop(dests, (sign * far) % size, half, x, output_weight)
-    arrived[half, sign] = lax.ppermute(first, "tp", moves)
-
     def turn(number, last):
         left = far - (number + 1) // 2
         for half, sign, moves in pairs[number % 2]:
             last = hop(
                 dests, (sign * left) % size, half, x, output_weight,
-                arrived.get((half, sign)), last,
+                arrived.get((half, sign), []), last,
             )
-            arrived[half, sign] = lax.ppermute(last, "tp", moves)
+            arrived[half, sign] = [lax.ppermute(last, "tp", moves)]
         return last
 
     ids = block_adapter_ids.reshape(-1)
     ids_there = lax.ppermute(block_adapter_ids, "inst", SWAP).reshape(-1)
-    half, sign, moves = pairs[0][1]
-    last = hop(dests, (sign * far) % size, half, x, output_weight, None, token)
-    arrived[half, sign] = lax.ppermute(last, "tp", moves)
+    last = None
+    for piece in range(tiling(dests, output_weight)[2]):
+        both = first_pieces(dests, far % size, piece, x, output_weight, last)
+        for (half, sign, moves), part in zip(pairs[0], both):
+            arrived.setdefault((half, sign), []).append(lax.ppermute(part, "tp", moves))
+        last = both[1]
     pages = adapter_page_table[jnp.concatenate([ids, ids_there])]
     places = pages % resident
     index, index_there = places[: ids.shape[0]], places[ids.shape[0] :]
     local = (pages[: ids.shape[0]] // resident == instance).astype(jnp.int32)
     last = collect(index_there, adapter_down_weight, last)
     got_down = lax.ppermute(last, "inst", SWAP)
+    last = touch(last, *(arrived[half, sign][0] for half, sign, _ in pairs[0]))
     last = turn(1, last)
     last = collect(index_there, adapter_up_weight, last)
     got_up = lax.ppermute(last, "inst", SWAP)
@@ -470,7 +470,7 @@
     number, turns = 2, 2 * far - 1
     apart = 1
     while apart < size:
-        sent = over(give if apart == 1 else low, apart)
+        sent = over(((give if apart == 1 else low) * LOW_SCALE).astype(jnp.float16), apart)
         until = turns - 1 if 2 * apart == size else number + (1 if apart == 1 else 2)
         while number < min(until, turns - 1):
             last = turn(number, last)
@@ -483,6 +483,8 @@
                 last = own
             number += 1
         apart *= 2
+        zero = touch(last)[0, 0]
+        sent = sent.astype(jnp.float32) * (1.0 / LOW_SCALE) + zero
         low = last = add(low, sent, jnp.float32 if apart < size else jnp.bfloat16, last)
     other = over(low, 1)
     last = turn(number, last)
@@ -490,7 +492,7 @@
     result = None
     for half in range(2):
         result = finish(
-            live_row_count.reshape(-1), half, own, arrived[half, 1], arrived[half, -1], result
+            live_row_count.reshape(-1), half, own, arrived[half, 1][0], arrived[half, -1][0], result
         )
     return result.reshape(steps, row_count, -1)
 

time: 140 us -> 137 us (0.979)
  Pallas kernels: 66.7 us -> 63.3 us
  other arithmetic: 0.7 us -> 3.46 us
  starting transfers between devices: 25.6 us -> 23 us
    ppermute x4, waiting for transfers between devices: 25.6 us -> 17.5 us  [over(): return lax.ppermute(value, 'tp', [(i, i ^ apart) for i in range(size)])]
    ppermute x14 -> x16, waiting for transfers between devices: 17.4 us -> 24.4 us  [the longest x12 21.5 us: turn(): arrived[half, sign] = [lax.ppermute(last, 'tp', moves)]]
    add x0 -> x3, other arithmetic: none -> 2.67 us  [per_device(): sent = sent.astype(jnp.float32) * (1.0 / LOW_SCALE) + zero]
    pallas_call x15 -> x19, Pallas kernels: 42 us -> 40.1 us  [the longest x12 34.5 us: hop(): pl.pallas_call(functools.partial(hop_kernel, tuple(range(len(received))))...]
    ppermute x14 -> x16, starting transfers between devices: 19.2 us -> 17.3 us  [the longest x12 12.5 us: turn(): arrived[half, sign] = [lax.ppermute(last, 'tp', moves)]]
    pallas_call x3, Pallas kernels: 1.62 us -> 0.05 us  [add(): pl.pallas_call(add_kernel, in_specs=[WHOLE, WHOLE, ANYWHERE], out_specs=W...]
    slice x0 -> x3, local copies, waits for them, and re-layouts: none -> 1.5 us  [per_device(): zero = touch(last)[0, 0]]
  transfers between devices with their start and end apart: 21 -> 23, of which waited for: 7 -> 9; matrix products, arithmetic and copies ran while one was open for 1% -> 4% of each run, Pallas kernels for 46% -> 45%
where the time goes in v9:
time: 137 us; the launch traced here: 136 us
  Pallas kernels  63.3 us (46%)
  waiting for transfers between devices  41.9 us (31%)
  starting transfers between devices  23 us (17%)
  local copies, waits for them, and re-layouts  3.99 us (3%)
  other arithmetic  3.46 us (3%)
    pallas_call x12, Pallas kernels, hop(): pl.pallas_call(functools.partial(hop_kernel, tuple(range(len(received))))...  34.5 us
    ppermute x12, waiting for transfers between devices, turn(): arrived[half, sign] = [lax.ppermute(last, 'tp', moves)]  21.5 us
    ppermute x4, waiting for transfers between devices, over(): return lax.ppermute(value, 'tp', [(i, i ^ apart) for i in range(size)])  17.5 us
    ppermute x12, starting transfers between devices, turn(): arrived[half, sign] = [lax.ppermute(last, 'tp', moves)]  12.5 us
    pallas_call x1, Pallas kernels, own_terms(): pl.pallas_call(own_kernel, grid_spec=pltpu.PrefetchScalarGridSpec(num_sca...  7.06 us
    pallas_call x1, Pallas kernels, low_rank(): pl.pallas_call(functools.partial(low_kernel, sizes), grid_spec=pltpu.Pref...  5.68 us
    pallas_call x2, Pallas kernels, first_pieces(): pl.pallas_call(functools.partial(first_kernel, after is not None), grid_s...  5.67 us
    pallas_call x2, Pallas kernels, collect(): pl.pallas_call(functools.partial(collect_kernel, count), grid_spec=pltpu....  5.33 us
  transfers between devices with their start and end apart: 23, of which 9 were waited for; matrix products, arithmetic and copies ran while one was open for 4% of the time, Pallas kernels for 45%

profile of v9, /device:TPU:0, one launch (start us, length us, event | category | flops | bytes accessed | tf_op | source)
XLA Modules:
  0.0 136.1 jit_solution(16677264681199597695)
XLA Ops:
  1.9 2.8 %shard_map.82 = (bf16[768,256]{1,0:T(8,128)(2,1)S(1)}, bf16[768,256]{1,0:T(8,128)(2,1)S(1)}) custom-call(s32[8]{0:T(128)S(1)} %compare_select_fusion.3.dests, bf16[768,1024]{1,0:T(8,128)(2,1)S(1)} %bitcast.11, bf16[1024,8192]{1,0:T(8,128)(2,1)} %w_ref.29), custom_call_target="tpu_custom_call" | custom-call | flops 24159191040 | bytes 3407872 | tf_op jit(solution)/shard_map/pallas_call | solution.py:123
  4.7 2.6 %collective-permute-start.2 = (bf16[768,256]{1,0:T(8,128)(2,1)S(1)}, bf16[768,256]{1,0:T(8,128)(2,1)S(1)}, u32[]{:S(2)}, u32[]{:S(2)}) collective-permute-start(bf16[768,256]{1,0:T(8,128)(2,1)S(1)} %get-tuple-element.13.refs_0_), channel_id=1, source_target_pairs={{0,1},{2,0},{4,2},{6,4},{7,6},{5,7},{3,5},{1,3},{8,9},{10,8},{12,1... | collective-permute-start | bytes 1179656 | tf_op jit(solution)/shard_map/ppermute | solution.py:449
  7.4 2.8 %shard_map.83 = (bf16[768,256]{1,0:T(8,128)(2,1)S(1)}, bf16[768,256]{1,0:T(8,128)(2,1)S(1)}) custom-call(s32[8]{0:T(128)S(1)} %compare_select_fusion.3.dests, bf16[768,1024]{1,0:T(8,128)(2,1)S(1)} %bitcast.12, bf16[1024,8192]{1,0:T(8,128)(2,1)} %w_ref.29, bf16[768,256]{1,0:T(8,128)(2,1)S(1)} %get-tuple-element.13.refs_0_), custom_call_target="tpu_custom_call" | custom-call | flops 24159191040 | bytes 3407872 | tf_op jit(solution)/shard_map/pallas_call | solution.py:123
  13.5 2.7 %shard_map.84.refs_0_ = bf16[24,64,1024]{2,1,0:T(8,128)(2,1)S(1)} custom-call(s32[24]{0:T(128)S(1)} %get-tuple-element.21.index, bf16[96,64,1024]{2,1,0:T(8,128)(2,1)} %table_ref.6, bf16[768,256]{1,0:T(8,128)(2,1)S(1)} %get-tuple-element.14.after_ref), custom_call_target="tpu_custom_call" | custom-call | bytes 6291456 | tf_op jit(solution)/shard_map/pallas_call | solution.py:167
  19.3 2.8 %shard_map.86.refs_0_ = bf16[768,512]{1,0:T(8,128)(2,1)S(1)} custom-call(s32[8]{0:T(128)S(1)} %compare_select_fusion.3.dests, bf16[768,1024]{1,0:T(8,128)(2,1)S(1)} %bitcast.13, bf16[1024,8192]{1,0:T(8,128)(2,1)} %w_ref.29, f32[8,128]{1,0:T(8,128)S(1)} %shard_map.85.refs_0_), custom_call_target="tpu_custom_call" | custom-call | flops 24159191040 | bytes 4194304 | tf_op jit(solution)/shard_map/pallas_call | solution.py:79
  22.4 2.8 %shard_map.87.after_ref = bf16[768,512]{1,0:T(8,128)(2,1)S(1)} custom-call(s32[8]{0:T(128)S(1)} %compare_select_fusion.3.dests, bf16[768,1024]{1,0:T(8,128)(2,1)S(1)} %bitcast.14, bf16[1024,8192]{1,0:T(8,128)(2,1)} %w_ref.29, bf16[768,512]{1,0:T(8,128)(2,1)S(1)} %shard_map.86.refs_0_), custom_call_target="tpu_custom_call" | custom-call | flops 24159191040 | bytes 4194304 | tf_op jit(solution)/shard_map/pallas_call | solution.py:79
  27.0 2.7 %shard_map.88.after_ref = bf16[24,64,1024]{2,1,0:T(8,128)(2,1)S(1)} custom-call(s32[24]{0:T(128)S(1)} %get-tuple-element.21.index, bf16[96,64,1024]{2,1,0:T(8,128)(2,1)} %table_ref.7, bf16[768,512]{1,0:T(8,128)(2,1)S(1)} %shard_map.87.after_ref), custom_call_target="tpu_custom_call" | custom-call | bytes 6291456 | tf_op jit(solution)/shard_map/pallas_call | solution.py:167
  29.7 5.7 %shard_map.89 = (f32[64,384]{1,0:T(8,128)S(1)}, f32[64,384]{1,0:T(8,128)S(1)}) custom-call(s32[24]{0:T(128)S(1)} %compare_convert_fusion.local, s32[24]{0:T(128)S(1)} %get-tuple-element.22.index, s32[1]{0:T(128)} %bitcast.1.side, bf16[768,1024]{1,0:T(8,128)(2,1)S(1)} %bitcast.15, s32[3,256]{1,0:T(4,128)S(1)} %copy-done.5, bf16[96,64,1024]{2,1,0:T(8,128)(2,1)} %table_ref.6, ...), custom_call_target="tpu_custom_call" | custom-call | flops 12079595520 | bytes 4718592 | tf_op jit(solution)/shard_map/pallas_call | solution.py:238
  37.1 2.9 %shard_map.90.refs_2_ = bf16[768,512]{1,0:T(8,128)(2,1)S(1)} custom-call(s32[8]{0:T(128)S(1)} %compare_select_fusion.3.dests, bf16[768,1024]{1,0:T(8,128)(2,1)S(1)} %bitcast.16, bf16[1024,8192]{1,0:T(8,128)(2,1)} %w_ref.29, bf16[768,256]{1,0:T(8,128)(2,1)S(1)} %collective-permute-done.1.refs_1_.refs_0_, bf16[768,256]{1,0:T(8,128)(2,1)S(1)} %collective-permute-done.9.refs_1_, ...), custom_call_target="tpu_custom_call" | custom-call | flops 24159191040 | bytes 4194304 | tf_op jit(solution)/shard_map/pallas_call | solution.py:79
  41.7 2.9 %shard_map.91.refs_1_ = bf16[768,512]{1,0:T(8,128)(2,1)S(1)} custom-call(s32[8]{0:T(128)S(1)} %compare_select_fusion.3.dests, bf16[768,1024]{1,0:T(8,128)(2,1)S(1)} %bitcast.17, bf16[1024,8192]{1,0:T(8,128)(2,1)} %w_ref.29, bf16[768,256]{1,0:T(8,128)(2,1)S(1)} %collective-permute-done.2.refs_2_.refs_0_, bf16[768,256]{1,0:T(8,128)(2,1)S(1)} %collective-permute-done.8.refs_1_, ...), custom_call_target="tpu_custom_call" | custom-call | flops 24159191040 | bytes 4194304 | tf_op jit(solution)/shard_map/pallas_call | solution.py:79
  48.5 2.8 %shard_map.95.refs_1_ = bf16[768,512]{1,0:T(8,128)(2,1)S(1)} custom-call(s32[8]{0:T(128)S(1)} %compare_select_fusion.3.dests, bf16[768,1024]{1,0:T(8,128)(2,1)S(1)} %bitcast.18, bf16[1024,8192]{1,0:T(8,128)(2,1)} %w_ref.29, bf16[768,512]{1,0:T(8,128)(2,1)S(1)} %collective-permute-done.5.refs_0_, f32[64,384]{1,0:T(8,128)S(1)} %shard_map.94.refs_1_.low_ref), custom_call_target="tpu_custom_call" | custom-call | flops 24159191040 | bytes 4194304 | tf_op jit(solution)/shard_map/pallas_call | solution.py:79
  51.8 2.8 %shard_map.96.after_ref = bf16[768,512]{1,0:T(8,128)(2,1)S(1)} custom-call(s32[8]{0:T(128)S(1)} %compare_select_fusion.3.dests, bf16[768,1024]{1,0:T(8,128)(2,1)S(1)} %bitcast.19, bf16[1024,8192]{1,0:T(8,128)(2,1)} %w_ref.29, bf16[768,512]{1,0:T(8,128)(2,1)S(1)} %collective-permute-done.4.refs_0_, bf16[768,512]{1,0:T(8,128)(2,1)S(1)} %shard_map.95.refs_1_), custom_call_target="tpu_custom_call" | custom-call | flops 24159191040 | bytes 4194304 | tf_op jit(solution)/shard_map/pallas_call | solution.py:79
  56.2 7.1 %shard_map.97 = (f32[768,1024]{1,0:T(8,128)S(1)}, bf16[24,64,1024]{2,1,0:T(8,128)(2,1)S(1)}) custom-call(s32[24]{0:T(128)S(1)} %compare_convert_fusion.local, s32[24]{0:T(128)S(1)} %get-tuple-element.22.index, s32[8]{0:T(128)S(1)} %compare_select_fusion.3.dests, bf16[768,1024]{1,0:T(8,128)(2,1)S(1)} %bitcast.20, bf16[1024,8192]{1,0:T(8,128)(2,1)} %w_ref.29, ...), custom_call_target="tpu_custom_call" | custom-call | flops 48318382080 | bytes 13107200 | tf_op jit(solution)/shard_map/pallas_call | solution.py:297
  63.3 3.2 %shard_map.98.refs_1_ = bf16[768,512]{1,0:T(8,128)(2,1)S(1)} custom-call(s32[8]{0:T(128)S(1)} %compare_select_fusion.3.dests, bf16[768,1024]{1,0:T(8,128)(2,1)S(1)} %bitcast.21, bf16[1024,8192]{1,0:T(8,128)(2,1)} %w_ref.29, bf16[768,512]{1,0:T(8,128)(2,1)S(1)} %collective-permute-done.12.refs_0_, f32[768,1024]{1,0:T(8,128)S(1)} %get-tuple-element.19.refs_1_.own_ref), custom_call_target="tpu_custom_call" | custom-call | flops 24159191040 | bytes 4194304 | tf_op jit(solution)/shard_map/pallas_call | solution.py:79
  67.0 2.8 %shard_map.99.refs_0_.after_ref = bf16[768,512]{1,0:T(8,128)(2,1)S(1)} custom-call(s32[8]{0:T(128)S(1)} %compare_select_fusion.3.dests, bf16[768,1024]{1,0:T(8,128)(2,1)S(1)} %bitcast.22, bf16[1024,8192]{1,0:T(8,128)(2,1)} %w_ref.29, bf16[768,512]{1,0:T(8,128)(2,1)S(1)} %collective-permute-done.11.refs_0_, bf16[768,512]{1,0:T(8,128)(2,1)S(1)} %shard_map.98.refs_1_), custom_call_target="tpu_custom_call" | custom-call | flops 24159191040 | bytes 4194304 | tf_op jit(solution)/shard_map/pallas_call | solution.py:79
  75.1 4.2 %collective-permute-done.15.refs_0_ = bf16[768,512]{1,0:T(8,128)(2,1)S(1)} collective-permute-done((bf16[768,512]{1,0:T(8,128)(2,1)S(1)}, bf16[768,512]{1,0:T(8,128)(2,1)S(1)}, u32[]{:S(2)}, u32[]{:S(2)}) %collective-permute-start.15) | collective-permute-done | bytes 786464 | tf_op jit(solution)/shard_map/ppermute | solution.py:440
  79.3 2.8 %shard_map.102.refs_1_ = bf16[768,512]{1,0:T(8,128)(2,1)S(1)} custom-call(s32[8]{0:T(128)S(1)} %compare_select_fusion.3.dests, bf16[768,1024]{1,0:T(8,128)(2,1)S(1)} %bitcast.23, bf16[1024,8192]{1,0:T(8,128)(2,1)} %w_ref.29, bf16[768,512]{1,0:T(8,128)(2,1)S(1)} %collective-permute-done.15.refs_0_, f32[64,384]{1,0:T(8,128)S(1)} %shard_map.101.refs_1_.low_ref), custom_call_target="tpu_custom_call" | custom-call | flops 24159191040 | bytes 4194304 | tf_op jit(solution)/shard_map/pallas_call | solution.py:79
  82.9 2.8 %shard_map.103.refs_0_.after_ref = bf16[768,512]{1,0:T(8,128)(2,1)S(1)} custom-call(s32[8]{0:T(128)S(1)} %compare_select_fusion.3.dests, bf16[768,1024]{1,0:T(8,128)(2,1)S(1)} %bitcast.24, bf16[1024,8192]{1,0:T(8,128)(2,1)} %w_ref.29, bf16[768,512]{1,0:T(8,128)(2,1)S(1)} %collective-permute-done.14.refs_0_, bf16[768,512]{1,0:T(8,128)(2,1)S(1)} %shard_map.102.refs_1_), custom_call_target="tpu_custom_call" | custom-call | flops 24159191040 | bytes 4194304 | tf_op jit(solution)/shard_map/pallas_call | solution.py:79
  88.3 13.5 %collective-permute-done.13 = f16[64,384]{1,0:T(8,128)(2,1)S(1)} collective-permute-done((f16[64,384]{1,0:T(8,128)(2,1)S(1)}, f16[64,384]{1,0:T(8,128)(2,1)S(1)}, u32[]{:S(2)}, u32[]{:S(2)}) %collective-permute-start.13) | collective-permute-done | bytes 49184 | tf_op jit(solution)/shard_map/ppermute | solution.py:468
  102.6 2.8 %shard_map.106.refs_1_ = bf16[768,512]{1,0:T(8,128)(2,1)S(1)} custom-call(s32[8]{0:T(128)S(1)} %compare_select_fusion.3.dests, bf16[768,1024]{1,0:T(8,128)(2,1)S(1)} %bitcast.25, bf16[1024,8192]{1,0:T(8,128)(2,1)} %w_ref.29, bf16[768,512]{1,0:T(8,128)(2,1)S(1)} %collective-permute-done.18.refs_0_, bf16[64,384]{1,0:T(8,128)(2,1)S(1)} %shard_map.105.refs_1_.low_ref), custom_call_target="tpu_custom_call" | custom-call | flops 24159191040 | bytes 4194304 | tf_op jit(solution)/shard_map/pallas_call | solution.py:79
  106.0 3.3 %shard_map.107.after_ref = bf16[768,512]{1,0:T(8,128)(2,1)S(1)} custom-call(s32[8]{0:T(128)S(1)} %compare_select_fusion.3.dests, bf16[768,1024]{1,0:T(8,128)(2,1)S(1)} %bitcast.26, bf16[1024,8192]{1,0:T(8,128)(2,1)} %w_ref.29, bf16[768,512]{1,0:T(8,128)(2,1)S(1)} %collective-permute-done.17.refs_0_, bf16[768,512]{1,0:T(8,128)(2,1)S(1)} %shard_map.106.refs_1_), custom_call_target="tpu_custom_call" | custom-call | flops 24159191040 | bytes 4194304 | tf_op jit(solution)/shard_map/pallas_call | solution.py:79
  110.7 3.9 %collective-permute-done.16.other_ref = bf16[64,384]{1,0:T(8,128)(2,1)S(1)} collective-permute-done((bf16[64,384]{1,0:T(8,128)(2,1)S(1)}, bf16[64,384]{1,0:T(8,128)(2,1)S(1)}, u32[]{:S(2)}, u32[]{:S(2)}) %collective-permute-start.16) | collective-permute-done | bytes 49184 | tf_op jit(solution)/shard_map/ppermute | solution.py:468
  115.4 2.3 %collective-permute-done.22.two_ref = bf16[768,512]{1,0:T(8,128)(2,1)S(1)} collective-permute-done((bf16[768,512]{1,0:T(8,128)(2,1)S(1)}, bf16[768,512]{1,0:T(8,128)(2,1)S(1)}, u32[]{:S(2)}, u32[]{:S(2)}) %collective-permute-start.22) | collective-permute-done | bytes 786464 | tf_op jit(solution)/shard_map/ppermute | solution.py:440
  117.7 12.5 %collective-permute-done.21.one_ref = bf16[768,512]{1,0:T(8,128)(2,1)S(1)} collective-permute-done((bf16[768,512]{1,0:T(8,128)(2,1)S(1)}, bf16[768,512]{1,0:T(8,128)(2,1)S(1)}, u32[]{:S(2)}, u32[]{:S(2)}) %collective-permute-start.21) | collective-permute-done | bytes 786464 | tf_op jit(solution)/shard_map/ppermute | solution.py:440
  (93 shorter events, 38.3 us)
Async XLA Ops:
  0.0 12.5 %collective-permute-start = (s32[3,2,4]{2,1,0:T(2,128)}, s32[3,2,4]{2,1,0:T(2,128)S(1)}, u32[]{:S(2)}, u32[]{:S(2)}) collective-permute-start(s32[3,2,4]{2,1,0:T(2,128)} %param.13), channel_id=1, source_target_pairs={{0,8},{8,0},{1,9},{9,1},{2,10},{10,2},{3,11},{11,3},{4,12},{12,4},... | collective-permute-start | bytes 296 | tf_op jit(solution)/shard_map/ppermute | solution.py:444
  4.7 12.6 %collective-permute-start.2 = (bf16[768,256]{1,0:T(8,128)(2,1)S(1)}, bf16[768,256]{1,0:T(8,128)(2,1)S(1)}, u32[]{:S(2)}, u32[]{:S(2)}) collective-permute-start(bf16[768,256]{1,0:T(8,128)(2,1)S(1)} %get-tuple-element.13.refs_0_), channel_id=1, source_target_pairs={{0,1},{2,0},{4,2},{6,4},{7,6},{5,7},{3,5},{1,3},{8,9},{10,8},{12,1... | collective-permute-start | bytes 1179656 | tf_op jit(solution)/shard_map/ppermute | solution.py:449
  7.3 12.0 %collective-permute-start.1 = (bf16[768,256]{1,0:T(8,128)(2,1)S(1)}, bf16[768,256]{1,0:T(8,128)(2,1)S(1)}, u32[]{:S(2)}, u32[]{:S(2)}) collective-permute-start(bf16[768,256]{1,0:T(8,128)(2,1)S(1)} %get-tuple-element.15), channel_id=1, source_target_pairs={{0,2},{2,4},{4,6},{6,7},{7,5},{5,3},{3,1},{1,0},{8,10},{10,12},{12... | collective-permute-start | bytes 1179656 | tf_op jit(solution)/shard_map/ppermute | solution.py:449
  10.3 25.2 %collective-permute-start.9 = (bf16[768,256]{1,0:T(8,128)(2,1)S(1)}, bf16[768,256]{1,0:T(8,128)(2,1)S(1)}, u32[]{:S(2)}, u32[]{:S(2)}) collective-permute-start(bf16[768,256]{1,0:T(8,128)(2,1)S(1)} %get-tuple-element.18), channel_id=1, source_target_pairs={{0,2},{2,4},{4,6},{6,7},{7,5},{5,3},{3,1},{1,0},{8,10},{10,12},{12... | collective-permute-start | bytes 1179656 | tf_op jit(solution)/shard_map/ppermute | solution.py:449
  12.3 27.7 %collective-permute-start.8 = (bf16[768,256]{1,0:T(8,128)(2,1)S(1)}, bf16[768,256]{1,0:T(8,128)(2,1)S(1)}, u32[]{:S(2)}, u32[]{:S(2)}) collective-permute-start(bf16[768,256]{1,0:T(8,128)(2,1)S(1)} %get-tuple-element.14.after_ref), channel_id=1, source_target_pairs={{0,1},{2,0},{4,2},{6,4},{7,6},{5,7},{3,5},{1,3},{8,9},{10,8},{12,1... | collective-permute-start | bytes 1179656 | tf_op jit(solution)/shard_map/ppermute | solution.py:449
  16.2 13.4 %collective-permute-start.6 = (bf16[24,64,1024]{2,1,0:T(8,128)(2,1)S(1)}, bf16[24,64,1024]{2,1,0:T(8,128)(2,1)S(1)}, u32[]{:S(2)}, u32[]{:S(2)}) collective-permute-start(bf16[24,64,1024]{2,1,0:T(8,128)(2,1)S(1)} %shard_map.84.refs_0_), channel_id=1, source_target_pairs={{0,8},{8,0},{1,9},{9,1},{2,10},{10,2},{3,11},{11,3},{4,12},{12,4},... | collective-permute-start | bytes 9437192 | tf_op jit(solution)/shard_map/ppermute | solution.py:456
  22.0 26.5 %collective-permute-start.5 = (bf16[768,512]{1,0:T(8,128)(2,1)S(1)}, bf16[768,512]{1,0:T(8,128)(2,1)S(1)}, u32[]{:S(2)}, u32[]{:S(2)}) collective-permute-start(bf16[768,512]{1,0:T(8,128)(2,1)S(1)} %shard_map.86.refs_0_), channel_id=1, source_target_pairs={{0,2},{2,4},{4,6},{6,7},{7,5},{5,3},{3,1},{1,0},{8,10},{10,12},{12... | collective-permute-start | bytes 2359304 | tf_op jit(solution)/shard_map/ppermute | solution.py:440
  25.2 26.7 %collective-permute-start.4 = (bf16[768,512]{1,0:T(8,128)(2,1)S(1)}, bf16[768,512]{1,0:T(8,128)(2,1)S(1)}, u32[]{:S(2)}, u32[]{:S(2)}) collective-permute-start(bf16[768,512]{1,0:T(8,128)(2,1)S(1)} %shard_map.87.after_ref), channel_id=1, source_target_pairs={{0,1},{2,0},{4,2},{6,4},{7,6},{5,7},{3,5},{1,3},{8,9},{10,8},{12,1... | collective-permute-start | bytes 2359304 | tf_op jit(solution)/shard_map/ppermute | solution.py:440
  29.6 15.0 %collective-permute-start.3 = (bf16[24,64,1024]{2,1,0:T(8,128)(2,1)S(1)}, bf16[24,64,1024]{2,1,0:T(8,128)(2,1)S(1)}, u32[]{:S(2)}, u32[]{:S(2)}) collective-permute-start(bf16[24,64,1024]{2,1,0:T(8,128)(2,1)S(1)} %shard_map.88.after_ref), channel_id=1, source_target_pairs={{0,8},{8,0},{1,9},{9,1},{2,10},{10,2},{3,11},{11,3},{4,12},{12,4},... | collective-permute-start | bytes 9437192 | tf_op jit(solution)/shard_map/ppermute | solution.py:460
  35.5 10.2 %collective-permute-start.7 = (f16[64,384]{1,0:T(8,128)(2,1)S(1)}, f16[64,384]{1,0:T(8,128)(2,1)S(1)}, u32[]{:S(2)}, u32[]{:S(2)}) collective-permute-start(f16[64,384]{1,0:T(8,128)(2,1)S(1)} %multiply_convert_fusion.2), channel_id=1, source_target_pairs={{0,1},{1,0},{2,3},{3,2},{4,5},{5,4},{6,7},{7,6},{8,9},{9,8},{10,11... | collective-permute-start | bytes 147464 | tf_op jit(solution)/shard_map/ppermute | solution.py:468
  40.0 23.3 %collective-permute-start.12 = (bf16[768,512]{1,0:T(8,128)(2,1)S(1)}, bf16[768,512]{1,0:T(8,128)(2,1)S(1)}, u32[]{:S(2)}, u32[]{:S(2)}) collective-permute-start(bf16[768,512]{1,0:T(8,128)(2,1)S(1)} %shard_map.90.refs_2_), channel_id=1, source_target_pairs={{0,2},{2,4},{4,6},{6,7},{7,5},{5,3},{3,1},{1,0},{8,10},{10,12},{12... | collective-permute-start | bytes 2359304 | tf_op jit(solution)/shard_map/ppermute | solution.py:440
  44.6 22.4 %collective-permute-start.11 = (bf16[768,512]{1,0:T(8,128)(2,1)S(1)}, bf16[768,512]{1,0:T(8,128)(2,1)S(1)}, u32[]{:S(2)}, u32[]{:S(2)}) collective-permute-start(bf16[768,512]{1,0:T(8,128)(2,1)S(1)} %shard_map.91.refs_1_), channel_id=1, source_target_pairs={{0,1},{2,0},{4,2},{6,4},{7,6},{5,7},{3,5},{1,3},{8,9},{10,8},{12,1... | collective-permute-start | bytes 2359304 | tf_op jit(solution)/shard_map/ppermute | solution.py:440
  47.0 25.0 %collective-permute-start.10 = (f16[64,384]{1,0:T(8,128)(2,1)}, f16[64,384]{1,0:T(8,128)(2,1)}, u32[]{:S(2)}, u32[]{:S(2)}) collective-permute-start(f16[64,384]{1,0:T(8,128)(2,1)} %multiply_convert_fusion.1), channel_id=1, source_target_pairs={{0,2},{1,3},{2,0},{3,1},{4,6},{5,7},{6,4},{7,5},{8,10},{9,11},{10,... | collective-permute-start | bytes 147464 | tf_op jit(solution)/shard_map/ppermute | solution.py:468
  51.3 28.0 %collective-permute-start.15 = (bf16[768,512]{1,0:T(8,128)(2,1)S(1)}, bf16[768,512]{1,0:T(8,128)(2,1)S(1)}, u32[]{:S(2)}, u32[]{:S(2)}) collective-permute-start(bf16[768,512]{1,0:T(8,128)(2,1)S(1)} %shard_map.95.refs_1_), channel_id=1, source_target_pairs={{0,2},{2,4},{4,6},{6,7},{7,5},{5,3},{3,1},{1,0},{8,10},{10,12},{12... | collective-permute-start | bytes 2359304 | tf_op jit(solution)/shard_map/ppermute | solution.py:440
  54.6 28.3 %collective-permute-start.14 = (bf16[768,512]{1,0:T(8,128)(2,1)S(1)}, bf16[768,512]{1,0:T(8,128)(2,1)S(1)}, u32[]{:S(2)}, u32[]{:S(2)}) collective-permute-start(bf16[768,512]{1,0:T(8,128)(2,1)S(1)} %shard_map.96.after_ref), channel_id=1, source_target_pairs={{0,1},{2,0},{4,2},{6,4},{7,6},{5,7},{3,5},{1,3},{8,9},{10,8},{12,1... | collective-permute-start | bytes 2359304 | tf_op jit(solution)/shard_map/ppermute | solution.py:440
  66.5 36.1 %collective-permute-start.18 = (bf16[768,512]{1,0:T(8,128)(2,1)S(1)}, bf16[768,512]{1,0:T(8,128)(2,1)S(1)}, u32[]{:S(2)}, u32[]{:S(2)}) collective-permute-start(bf16[768,512]{1,0:T(8,128)(2,1)S(1)} %shard_map.98.refs_1_), channel_id=1, source_target_pairs={{0,2},{2,4},{4,6},{6,7},{7,5},{5,3},{3,1},{1,0},{8,10},{10,12},{12... | collective-permute-start | bytes 2359304 | tf_op jit(solution)/shard_map/ppermute | solution.py:440
  69.8 36.2 %collective-permute-start.17 = (bf16[768,512]{1,0:T(8,128)(2,1)S(1)}, bf16[768,512]{1,0:T(8,128)(2,1)S(1)}, u32[]{:S(2)}, u32[]{:S(2)}) collective-permute-start(bf16[768,512]{1,0:T(8,128)(2,1)S(1)} %shard_map.99.refs_0_.after_ref), channel_id=1, source_target_pairs={{0,1},{2,0},{4,2},{6,4},{7,6},{5,7},{3,5},{1,3},{8,9},{10,8},{12,1... | collective-permute-start | bytes 2359304 | tf_op jit(solution)/shard_map/ppermute | solution.py:440
  73.3 28.5 %collective-permute-start.13 = (f16[64,384]{1,0:T(8,128)(2,1)S(1)}, f16[64,384]{1,0:T(8,128)(2,1)S(1)}, u32[]{:S(2)}, u32[]{:S(2)}) collective-permute-start(f16[64,384]{1,0:T(8,128)(2,1)S(1)} %multiply_convert_fusion), channel_id=1, source_target_pairs={{0,4},{1,5},{2,6},{3,7},{4,0},{5,1},{6,2},{7,3},{8,12},{9,13},{10,... | collective-permute-start | bytes 147464 | tf_op jit(solution)/shard_map/ppermute | solution.py:468
  85.7 32.0 %collective-permute-start.22 = (bf16[768,512]{1,0:T(8,128)(2,1)S(1)}, bf16[768,512]{1,0:T(8,128)(2,1)S(1)}, u32[]{:S(2)}, u32[]{:S(2)}) collective-permute-start(bf16[768,512]{1,0:T(8,128)(2,1)S(1)} %shard_map.103.refs_0_.after_ref), channel_id=1, source_target_pairs={{0,1},{2,0},{4,2},{6,4},{7,6},{5,7},{3,5},{1,3},{8,9},{10,8},{12,1... | collective-permute-start | bytes 2359304 | tf_op jit(solution)/shard_map/ppermute | solution.py:440
  86.5 45.9 %collective-permute-start.19 = (bf16[768,512]{1,0:T(8,128)(2,1)S(1)}, bf16[768,512]{1,0:T(8,128)(2,1)S(1)}, u32[]{:S(2)}, u32[]{:S(2)}) collective-permute-start(bf16[768,512]{1,0:T(8,128)(2,1)S(1)} %shard_map.102.refs_1_), channel_id=1, source_target_pairs={{0,2},{2,4},{4,6},{6,7},{7,5},{5,3},{3,1},{1,0},{8,10},{10,12},{12... | collective-permute-start | bytes 2359304 | tf_op jit(solution)/shard_map/ppermute | solution.py:440
  102.6 12.1 %collective-permute-start.16 = (bf16[64,384]{1,0:T(8,128)(2,1)S(1)}, bf16[64,384]{1,0:T(8,128)(2,1)S(1)}, u32[]{:S(2)}, u32[]{:S(2)}) collective-permute-start(bf16[64,384]{1,0:T(8,128)(2,1)S(1)} %shard_map.105.refs_1_.low_ref), channel_id=1, source_target_pairs={{0,1},{1,0},{2,3},{3,2},{4,5},{5,4},{6,7},{7,6},{8,9},{9,8},{10,11... | collective-permute-start | bytes 147464 | tf_op jit(solution)/shard_map/ppermute | solution.py:468
  105.5 24.7 %collective-permute-start.21 = (bf16[768,512]{1,0:T(8,128)(2,1)S(1)}, bf16[768,512]{1,0:T(8,128)(2,1)S(1)}, u32[]{:S(2)}, u32[]{:S(2)}) collective-permute-start(bf16[768,512]{1,0:T(8,128)(2,1)S(1)} %shard_map.106.refs_1_), channel_id=1, source_target_pairs={{0,2},{2,4},{4,6},{6,7},{7,5},{5,3},{3,1},{1,0},{8,10},{10,12},{12... | collective-permute-start | bytes 2359304 | tf_op jit(solution)/shard_map/ppermute | solution.py:440
  109.3 24.5 %collective-permute-start.20 = (bf16[768,512]{1,0:T(8,128)(2,1)S(1)}, bf16[768,512]{1,0:T(8,128)(2,1)S(1)}, u32[]{:S(2)}, u32[]{:S(2)}) collective-permute-start(bf16[768,512]{1,0:T(8,128)(2,1)S(1)} %shard_map.107.after_ref), channel_id=1, source_target_pairs={{0,1},{2,0},{4,2},{6,4},{7,6},{5,7},{3,5},{1,3},{8,9},{10,8},{12,1... | collective-permute-start | bytes 2359304 | tf_op jit(solution)/shard_map/ppermute | solution.py:440
  114.6 15.6 %copy-start.2 = (s32[3,1]{0,1:T(1,128)S(1)}, s32[3,1]{0,1:T(1,128)}, u32[]{:S(2)}) copy-start(s32[3,1]{0,1:T(1,128)} %param.15) | copy-start | bytes 40
  (11 other events, 66.6 us)

commit v10 on v9

--- a/solution.py
+++ b/solution.py
@@ -430,7 +430,8 @@
     far = size // 2
     pairs = [[(0, 1, forward), (1, -1, backward)], [(1, 1, forward), (0, -1, backward)]]
     arrived = {}
-    def turn(number, last):
+
+    def turn(number, last, between=None):
         left = far - (number + 1) // 2
         for half, sign, moves in pairs[number % 2]:
             last = hop(
@@ -438,6 +439,8 @@
                 arrived.get((half, sign), []), last,
             )
             arrived[half, sign] = [lax.ppermute(last, "tp", moves)]
+            if between is not None:
+                last, between = touch(between, last), None
         return last
 
     ids = block_adapter_ids.reshape(-1)
@@ -458,24 +461,23 @@
     last = turn(1, last)
     last = collect(index_there, adapter_up_weight, last)
     got_up = lax.ppermute(last, "inst", SWAP)
+    last = turn(2, last, got_down)
     side = (lax.axis_index("tp") & 1).reshape(1)
     low, give = low_rank(
         sizes, local, index, side, x, row_list_position, adapter_down_weight, got_down, last
     )
-    last = low
+    last = touch(got_up, low)
 
     def over(value, apart):
         return lax.ppermute(value, "tp", [(i, i ^ apart) for i in range(size)])
 
-    number, turns = 2, 2 * far - 1
+    number, turns = 3, 2 * far - 1
     apart = 1
     while apart < size:
         sent = over(((give if apart == 1 else low) * LOW_SCALE).astype(jnp.float16), apart)
-        until = turns - 1 if 2 * apart == size else number + (1 if apart == 1 else 2)
+        until = turns - 1 if 2 * apart == size else number + 1
         while number < min(until, turns - 1):
             last = turn(number, last)
-            if number == 2:
-                last = touch(got_up, last)
             if number == 3:
                 own, up_pages = own_terms(
                     dests, local, index, x, output_weight, adapter_up_weight, got_up, last

time: 137 us -> 136 us (level)
    ppermute x4, waiting for transfers between devices: 17.5 us -> 24.2 us  [over(): return lax.ppermute(value, 'tp', [(i, i ^ apart) for i in range(size)])]
    ppermute x12, waiting for transfers between devices: 21.5 us -> 15.3 us  [turn(): arrived[half, sign] = [lax.ppermute(last, 'tp', moves)]]
    pallas_call x2, Pallas kernels: 5.67 us -> 7.27 us  [first_pieces(): pl.pallas_call(functools.partial(first_kernel, after is not None), grid_s...]
  transfers between devices with their start and end apart: 23 -> 23, of which waited for: 9 -> 8; matrix products, arithmetic and copies ran while one was open for 4% -> 4% of each run, Pallas kernels for 45% -> 45%
where the time goes in v10:
time: 136 us
  Pallas kernels  63.3 us (47%)
  waiting for transfers between devices  42.1 us (31%)
  starting transfers between devices  23.6 us (17%)
  local copies, waits for them, and re-layouts  4.07 us (3%)
  other arithmetic  2.14 us (2%)
    pallas_call x12, Pallas kernels, hop(): pl.pallas_call(functools.partial(hop_kernel, tuple(range(len(received))))...  33.5 us
    ppermute x4, waiting for transfers between devices, over(): return lax.ppermute(value, 'tp', [(i, i ^ apart) for i in range(size)])  24.2 us
    ppermute x12, waiting for transfers between devices, turn(): arrived[half, sign] = [lax.ppermute(last, 'tp', moves)]  15.3 us
    ppermute x12, starting transfers between devices, turn(): arrived[half, sign] = [lax.ppermute(last, 'tp', moves)]  13.1 us
    pallas_call x2, Pallas kernels, first_pieces(): pl.pallas_call(functools.partial(first_kernel, after is not None), grid_s...  7.27 us
    pallas_call x1, Pallas kernels, own_terms(): pl.pallas_call(own_kernel, grid_spec=pltpu.PrefetchScalarGridSpec(num_sca...  6.75 us
    pallas_call x1, Pallas kernels, low_rank(): pl.pallas_call(functools.partial(low_kernel, sizes), grid_spec=pltpu.Pref...  5.35 us
    pallas_call x2, Pallas kernels, collect(): pl.pallas_call(functools.partial(collect_kernel, count), grid_spec=pltpu....  5.33 us
  transfers between devices with their start and end apart: 23, of which 8 were waited for; matrix products, arithmetic and copies ran while one was open for 4% of the time, Pallas kernels for 45%

profile of v10, /device:TPU:0, one launch (start us, length us, event | category | flops | bytes accessed | tf_op | source)
XLA Modules:
  0.0 135.6 jit_solution(14851651398055629529)
XLA Ops:
  1.9 3.7 %shard_map.82 = (bf16[768,256]{1,0:T(8,128)(2,1)}, bf16[768,256]{1,0:T(8,128)(2,1)}) custom-call(s32[8]{0:T(128)S(1)} %compare_select_fusion.3.dests, bf16[768,1024]{1,0:T(8,128)(2,1)S(1)} %bitcast.11, bf16[1024,8192]{1,0:T(8,128)(2,1)} %w_ref.29), custom_call_target="tpu_custom_call" | custom-call | flops 24159191040 | bytes 3407872 | tf_op jit(solution)/shard_map/pallas_call | solution.py:123
  8.2 3.6 %shard_map.83 = (bf16[768,256]{1,0:T(8,128)(2,1)}, bf16[768,256]{1,0:T(8,128)(2,1)S(1)}) custom-call(s32[8]{0:T(128)S(1)} %compare_select_fusion.3.dests, bf16[768,1024]{1,0:T(8,128)(2,1)S(1)} %bitcast.12, bf16[1024,8192]{1,0:T(8,128)(2,1)} %w_ref.29, bf16[768,256]{1,0:T(8,128)(2,1)} %get-tuple-element.13.refs_0_), custom_call_target="tpu_custom_call" | custom-call | flops 24159191040 | bytes 3407872 | tf_op jit(solution)/shard_map/pallas_call | solution.py:123
  14.9 2.7 %shard_map.84.refs_0_ = bf16[24,64,1024]{2,1,0:T(8,128)(2,1)S(1)} custom-call(s32[24]{0:T(128)S(1)} %get-tuple-element.21.index, bf16[96,64,1024]{2,1,0:T(8,128)(2,1)} %table_ref.6, bf16[768,256]{1,0:T(8,128)(2,1)S(1)} %get-tuple-element.14.after_ref), custom_call_target="tpu_custom_call" | custom-call | bytes 6291456 | tf_op jit(solution)/shard_map/pallas_call | solution.py:167
  20.3 2.8 %shard_map.86.refs_0_ = bf16[768,512]{1,0:T(8,128)(2,1)S(1)} custom-call(s32[8]{0:T(128)S(1)} %compare_select_fusion.3.dests, bf16[768,1024]{1,0:T(8,128)(2,1)S(1)} %bitcast.13, bf16[1024,8192]{1,0:T(8,128)(2,1)} %w_ref.29, f32[8,128]{1,0:T(8,128)S(1)} %shard_map.85.refs_0_), custom_call_target="tpu_custom_call" | custom-call | flops 24159191040 | bytes 4194304 | tf_op jit(solution)/shard_map/pallas_call | solution.py:79
  23.1 2.8 %shard_map.87.after_ref = bf16[768,512]{1,0:T(8,128)(2,1)S(1)} custom-call(s32[8]{0:T(128)S(1)} %compare_select_fusion.3.dests, bf16[768,1024]{1,0:T(8,128)(2,1)S(1)} %bitcast.14, bf16[1024,8192]{1,0:T(8,128)(2,1)} %w_ref.29, bf16[768,512]{1,0:T(8,128)(2,1)S(1)} %shard_map.86.refs_0_), custom_call_target="tpu_custom_call" | custom-call | flops 24159191040 | bytes 4194304 | tf_op jit(solution)/shard_map/pallas_call | solution.py:79
  27.9 2.7 %shard_map.88.refs_2_ = bf16[24,64,1024]{2,1,0:T(8,128)(2,1)S(1)} custom-call(s32[24]{0:T(128)S(1)} %get-tuple-element.21.index, bf16[96,64,1024]{2,1,0:T(8,128)(2,1)} %table_ref.7, bf16[768,512]{1,0:T(8,128)(2,1)S(1)} %shard_map.87.after_ref), custom_call_target="tpu_custom_call" | custom-call | bytes 6291456 | tf_op jit(solution)/shard_map/pallas_call | solution.py:167
  30.7 2.9 %shard_map.89.refs_1_ = bf16[768,512]{1,0:T(8,128)(2,1)S(1)} custom-call(s32[8]{0:T(128)S(1)} %compare_select_fusion.3.dests, bf16[768,1024]{1,0:T(8,128)(2,1)S(1)} %bitcast.15, bf16[1024,8192]{1,0:T(8,128)(2,1)} %w_ref.29, bf16[768,256]{1,0:T(8,128)(2,1)S(1)} %collective-permute-done.1.refs_1_.refs_0_, bf16[768,256]{1,0:T(8,128)(2,1)S(1)} %collective-permute-done.8.refs_1_, ...), custom_call_target="tpu_custom_call" | custom-call | flops 24159191040 | bytes 4194304 | tf_op jit(solution)/shard_map/pallas_call | solution.py:79
  34.4 2.9 %shard_map.91.after_ref = bf16[768,512]{1,0:T(8,128)(2,1)S(1)} custom-call(s32[8]{0:T(128)S(1)} %compare_select_fusion.3.dests, bf16[768,1024]{1,0:T(8,128)(2,1)S(1)} %bitcast.16, bf16[1024,8192]{1,0:T(8,128)(2,1)} %w_ref.29, bf16[768,256]{1,0:T(8,128)(2,1)S(1)} %collective-permute-done.2.refs_2_.refs_0_, ...), custom_call_target="tpu_custom_call" | custom-call | flops 24159191040 | bytes 4194304 | tf_op jit(solution)/shard_map/pallas_call | solution.py:79
  38.7 5.3 %shard_map.92 = (f32[64,384]{1,0:T(8,128)S(1)}, f32[64,384]{1,0:T(8,128)S(1)}) custom-call(s32[24]{0:T(128)S(1)} %compare_convert_fusion.local, s32[24]{0:T(128)S(1)} %get-tuple-element.22.index, s32[1]{0:T(128)} %bitcast.1.side, bf16[768,1024]{1,0:T(8,128)(2,1)S(1)} %bitcast.17, s32[3,256]{1,0:T(4,128)S(1)} %copy-done.7, bf16[96,64,1024]{2,1,0:T(8,128)(2,1)} %table_ref.6, ...), custom_call_target="tpu_custom_call" | custom-call | flops 12079595520 | bytes 4718592 | tf_op jit(solution)/shard_map/pallas_call | solution.py:238
  46.4 2.8 %shard_map.94.refs_1_ = bf16[768,512]{1,0:T(8,128)(2,1)S(1)} custom-call(s32[8]{0:T(128)S(1)} %compare_select_fusion.3.dests, bf16[768,1024]{1,0:T(8,128)(2,1)S(1)} %bitcast.18, bf16[1024,8192]{1,0:T(8,128)(2,1)} %w_ref.29, bf16[768,512]{1,0:T(8,128)(2,1)S(1)} %collective-permute-done.5.refs_0_, f32[8,128]{1,0:T(8,128)S(1)} %shard_map.93.refs_1_), custom_call_target="tpu_custom_call" | custom-call | flops 24159191040 | bytes 4194304 | tf_op jit(solution)/shard_map/pallas_call | solution.py:79
  50.2 2.8 %shard_map.95.after_ref = bf16[768,512]{1,0:T(8,128)(2,1)S(1)} custom-call(s32[8]{0:T(128)S(1)} %compare_select_fusion.3.dests, bf16[768,1024]{1,0:T(8,128)(2,1)S(1)} %bitcast.19, bf16[1024,8192]{1,0:T(8,128)(2,1)} %w_ref.29, bf16[768,512]{1,0:T(8,128)(2,1)S(1)} %collective-permute-done.4.refs_0_, bf16[768,512]{1,0:T(8,128)(2,1)S(1)} %shard_map.94.refs_1_), custom_call_target="tpu_custom_call" | custom-call | flops 24159191040 | bytes 4194304 | tf_op jit(solution)/shard_map/pallas_call | solution.py:79
  54.0 6.7 %shard_map.96 = (f32[768,1024]{1,0:T(8,128)S(1)}, bf16[24,64,1024]{2,1,0:T(8,128)(2,1)S(1)}) custom-call(s32[24]{0:T(128)S(1)} %compare_convert_fusion.local, s32[24]{0:T(128)S(1)} %get-tuple-element.22.index, s32[8]{0:T(128)S(1)} %compare_select_fusion.3.dests, bf16[768,1024]{1,0:T(8,128)(2,1)S(1)} %bitcast.20, bf16[1024,8192]{1,0:T(8,128)(2,1)} %w_ref.29, ...), custom_call_target="tpu_custom_call" | custom-call | flops 48318382080 | bytes 13107200 | tf_op jit(solution)/shard_map/pallas_call | solution.py:297
  61.4 2.9 %collective-permute-done.9 = f16[64,384]{1,0:T(8,128)(2,1)S(1)} collective-permute-done((f16[64,384]{1,0:T(8,128)(2,1)S(1)}, f16[64,384]{1,0:T(8,128)(2,1)S(1)}, u32[]{:S(2)}, u32[]{:S(2)}) %collective-permute-start.9) | collective-permute-done | bytes 49184 | tf_op jit(solution)/shard_map/ppermute | solution.py:472
  65.1 2.8 %shard_map.99.refs_1_ = bf16[768,512]{1,0:T(8,128)(2,1)S(1)} custom-call(s32[8]{0:T(128)S(1)} %compare_select_fusion.3.dests, bf16[768,1024]{1,0:T(8,128)(2,1)S(1)} %bitcast.21, bf16[1024,8192]{1,0:T(8,128)(2,1)} %w_ref.29, bf16[768,512]{1,0:T(8,128)(2,1)S(1)} %collective-permute-done.12.refs_0_, f32[64,384]{1,0:T(8,128)S(1)} %shard_map.98.refs_1_.low_ref), custom_call_target="tpu_custom_call" | custom-call | flops 24159191040 | bytes 4194304 | tf_op jit(solution)/shard_map/pallas_call | solution.py:79
  69.9 2.8 %shard_map.100.refs_0_.after_ref = bf16[768,512]{1,0:T(8,128)(2,1)S(1)} custom-call(s32[8]{0:T(128)S(1)} %compare_select_fusion.3.dests, bf16[768,1024]{1,0:T(8,128)(2,1)S(1)} %bitcast.22, bf16[1024,8192]{1,0:T(8,128)(2,1)} %w_ref.29, bf16[768,512]{1,0:T(8,128)(2,1)S(1)} %collective-permute-done.11.refs_0_, bf16[768,512]{1,0:T(8,128)(2,1)S(1)} %shard_map.99.refs_1_), custom_call_target="tpu_custom_call" | custom-call | flops 24159191040 | bytes 4194304 | tf_op jit(solution)/shard_map/pallas_call | solution.py:79
  73.3 8.6 %collective-permute-done.10 = f16[64,384]{1,0:T(8,128)(2,1)S(1)} collective-permute-done((f16[64,384]{1,0:T(8,128)(2,1)S(1)}, f16[64,384]{1,0:T(8,128)(2,1)S(1)}, u32[]{:S(2)}, u32[]{:S(2)}) %collective-permute-start.10) | collective-permute-done | bytes 49184 | tf_op jit(solution)/shard_map/ppermute | solution.py:472
  82.6 2.7 %collective-permute-start.13 = (f16[64,384]{1,0:T(8,128)(2,1)S(1)}, f16[64,384]{1,0:T(8,128)(2,1)S(1)}, u32[]{:S(2)}, u32[]{:S(2)}) collective-permute-start(f16[64,384]{1,0:T(8,128)(2,1)S(1)} %multiply_convert_fusion), channel_id=1, source_target_pairs={{0,4},{1,5},{2,6},{3,7},{4,0},{5,1},{6,2},{7,3},{8,12},{9,13},{10,... | collective-permute-start | bytes 147464 | tf_op jit(solution)/shard_map/ppermute | solution.py:472
  85.2 2.8 %shard_map.103.refs_1_ = bf16[768,512]{1,0:T(8,128)(2,1)S(1)} custom-call(s32[8]{0:T(128)S(1)} %compare_select_fusion.3.dests, bf16[768,1024]{1,0:T(8,128)(2,1)S(1)} %bitcast.23, bf16[1024,8192]{1,0:T(8,128)(2,1)} %w_ref.29, bf16[768,512]{1,0:T(8,128)(2,1)S(1)} %collective-permute-done.15.refs_0_, f32[64,384]{1,0:T(8,128)S(1)} %shard_map.102.refs_1_.low_ref), custom_call_target="tpu_custom_call" | custom-call | flops 24159191040 | bytes 4194304 | tf_op jit(solution)/shard_map/pallas_call | solution.py:79
  88.0 2.8 %shard_map.104.refs_0_.after_ref = bf16[768,512]{1,0:T(8,128)(2,1)S(1)} custom-call(s32[8]{0:T(128)S(1)} %compare_select_fusion.3.dests, bf16[768,1024]{1,0:T(8,128)(2,1)S(1)} %bitcast.24, bf16[1024,8192]{1,0:T(8,128)(2,1)} %w_ref.29, bf16[768,512]{1,0:T(8,128)(2,1)S(1)} %collective-permute-done.14.refs_0_, bf16[768,512]{1,0:T(8,128)(2,1)S(1)} %shard_map.103.refs_1_), custom_call_target="tpu_custom_call" | custom-call | flops 24159191040 | bytes 4194304 | tf_op jit(solution)/shard_map/pallas_call | solution.py:79
  93.4 6.9 %collective-permute-done.13 = f16[64,384]{1,0:T(8,128)(2,1)S(1)} collective-permute-done((f16[64,384]{1,0:T(8,128)(2,1)S(1)}, f16[64,384]{1,0:T(8,128)(2,1)S(1)}, u32[]{:S(2)}, u32[]{:S(2)}) %collective-permute-start.13) | collective-permute-done | bytes 49184 | tf_op jit(solution)/shard_map/ppermute | solution.py:472
  101.9 2.8 %shard_map.107.refs_1_ = bf16[768,512]{1,0:T(8,128)(2,1)S(1)} custom-call(s32[8]{0:T(128)S(1)} %compare_select_fusion.3.dests, bf16[768,1024]{1,0:T(8,128)(2,1)S(1)} %bitcast.25, bf16[1024,8192]{1,0:T(8,128)(2,1)} %w_ref.29, bf16[768,512]{1,0:T(8,128)(2,1)S(1)} %collective-permute-done.18.refs_0_, bf16[64,384]{1,0:T(8,128)(2,1)S(1)} %shard_map.106.refs_1_.low_ref), custom_call_target="tpu_custom_call" | custom-call | flops 24159191040 | bytes 4194304 | tf_op jit(solution)/shard_map/pallas_call | solution.py:79
  106.8 2.8 %shard_map.108.after_ref = bf16[768,512]{1,0:T(8,128)(2,1)S(1)} custom-call(s32[8]{0:T(128)S(1)} %compare_select_fusion.3.dests, bf16[768,1024]{1,0:T(8,128)(2,1)S(1)} %bitcast.26, bf16[1024,8192]{1,0:T(8,128)(2,1)} %w_ref.29, bf16[768,512]{1,0:T(8,128)(2,1)S(1)} %collective-permute-done.17.refs_0_, bf16[768,512]{1,0:T(8,128)(2,1)S(1)} %shard_map.107.refs_1_), custom_call_target="tpu_custom_call" | custom-call | flops 24159191040 | bytes 4194304 | tf_op jit(solution)/shard_map/pallas_call | solution.py:79
  110.0 5.9 %collective-permute-done.16.other_ref = bf16[64,384]{1,0:T(8,128)(2,1)S(1)} collective-permute-done((bf16[64,384]{1,0:T(8,128)(2,1)S(1)}, bf16[64,384]{1,0:T(8,128)(2,1)S(1)}, u32[]{:S(2)}, u32[]{:S(2)}) %collective-permute-start.16) | collective-permute-done | bytes 49184 | tf_op jit(solution)/shard_map/ppermute | solution.py:472
  116.6 14.6 %collective-permute-done.21.one_ref = bf16[768,512]{1,0:T(8,128)(2,1)S(1)} collective-permute-done((bf16[768,512]{1,0:T(8,128)(2,1)S(1)}, bf16[768,512]{1,0:T(8,128)(2,1)S(1)}, u32[]{:S(2)}, u32[]{:S(2)}) %collective-permute-start.21) | collective-permute-done | bytes 786464 | tf_op jit(solution)/shard_map/ppermute | solution.py:441
  (94 shorter events, 35.5 us)
Async XLA Ops:
  0.0 13.9 %collective-permute-start = (s32[3,2,4]{2,1,0:T(2,128)}, s32[3,2,4]{2,1,0:T(2,128)S(1)}, u32[]{:S(2)}, u32[]{:S(2)}) collective-permute-start(s32[3,2,4]{2,1,0:T(2,128)} %param.13), channel_id=1, source_target_pairs={{0,8},{8,0},{1,9},{9,1},{2,10},{10,2},{3,11},{11,3},{4,12},{12,4},... | collective-permute-start | bytes 296 | tf_op jit(solution)/shard_map/ppermute | solution.py:447
  5.6 12.8 %collective-permute-start.2 = (bf16[768,256]{1,0:T(8,128)(2,1)}, bf16[768,256]{1,0:T(8,128)(2,1)S(1)}, u32[]{:S(2)}, u32[]{:S(2)}) collective-permute-start(bf16[768,256]{1,0:T(8,128)(2,1)} %get-tuple-element.13.refs_0_), channel_id=1, source_target_pairs={{0,1},{2,0},{4,2},{6,4},{7,6},{5,7},{3,5},{1,3},{8,9},{10,8},{12,1... | collective-permute-start | bytes 1179656 | tf_op jit(solution)/shard_map/ppermute | solution.py:452
  8.1 12.2 %collective-permute-start.1 = (bf16[768,256]{1,0:T(8,128)(2,1)}, bf16[768,256]{1,0:T(8,128)(2,1)S(1)}, u32[]{:S(2)}, u32[]{:S(2)}) collective-permute-start(bf16[768,256]{1,0:T(8,128)(2,1)} %get-tuple-element.15), channel_id=1, source_target_pairs={{0,2},{2,4},{4,6},{6,7},{7,5},{5,3},{3,1},{1,0},{8,10},{10,12},{12... | collective-permute-start | bytes 1179656 | tf_op jit(solution)/shard_map/ppermute | solution.py:452
  11.7 18.8 %collective-permute-start.8 = (bf16[768,256]{1,0:T(8,128)(2,1)}, bf16[768,256]{1,0:T(8,128)(2,1)S(1)}, u32[]{:S(2)}, u32[]{:S(2)}) collective-permute-start(bf16[768,256]{1,0:T(8,128)(2,1)} %get-tuple-element.16), channel_id=1, source_target_pairs={{0,2},{2,4},{4,6},{6,7},{7,5},{5,3},{3,1},{1,0},{8,10},{10,12},{12... | collective-permute-start | bytes 1179656 | tf_op jit(solution)/shard_map/ppermute | solution.py:452
  13.8 20.7 %collective-permute-start.7 = (bf16[768,256]{1,0:T(8,128)(2,1)S(1)}, bf16[768,256]{1,0:T(8,128)(2,1)S(1)}, u32[]{:S(2)}, u32[]{:S(2)}) collective-permute-start(bf16[768,256]{1,0:T(8,128)(2,1)S(1)} %get-tuple-element.14.after_ref), channel_id=1, source_target_pairs={{0,1},{2,0},{4,2},{6,4},{7,6},{5,7},{3,5},{1,3},{8,9},{10,8},{12,1... | collective-permute-start | bytes 1179656 | tf_op jit(solution)/shard_map/ppermute | solution.py:452
  17.6 16.0 %collective-permute-start.6 = (bf16[24,64,1024]{2,1,0:T(8,128)(2,1)S(1)}, bf16[24,64,1024]{2,1,0:T(8,128)(2,1)S(1)}, u32[]{:S(2)}, u32[]{:S(2)}) collective-permute-start(bf16[24,64,1024]{2,1,0:T(8,128)(2,1)S(1)} %shard_map.84.refs_0_), channel_id=1, source_target_pairs={{0,8},{8,0},{1,9},{9,1},{2,10},{10,2},{3,11},{11,3},{4,12},{12,4},... | collective-permute-start | bytes 9437192 | tf_op jit(solution)/shard_map/ppermute | solution.py:459
  25.8 20.5 %collective-permute-start.5 = (bf16[768,512]{1,0:T(8,128)(2,1)S(1)}, bf16[768,512]{1,0:T(8,128)(2,1)S(1)}, u32[]{:S(2)}, u32[]{:S(2)}) collective-permute-start(bf16[768,512]{1,0:T(8,128)(2,1)S(1)} %shard_map.86.refs_0_), channel_id=1, source_target_pairs={{0,2},{2,4},{4,6},{6,7},{7,5},{5,3},{3,1},{1,0},{8,10},{10,12},{12... | collective-permute-start | bytes 2359304 | tf_op jit(solution)/shard_map/ppermute | solution.py:441
  26.6 23.5 %collective-permute-start.4 = (bf16[768,512]{1,0:T(8,128)(2,1)S(1)}, bf16[768,512]{1,0:T(8,128)(2,1)S(1)}, u32[]{:S(2)}, u32[]{:S(2)}) collective-permute-start(bf16[768,512]{1,0:T(8,128)(2,1)S(1)} %shard_map.87.after_ref), channel_id=1, source_target_pairs={{0,1},{2,0},{4,2},{6,4},{7,6},{5,7},{3,5},{1,3},{8,9},{10,8},{12,1... | collective-permute-start | bytes 2359304 | tf_op jit(solution)/shard_map/ppermute | solution.py:441
  30.6 13.5 %collective-permute-start.3 = (bf16[24,64,1024]{2,1,0:T(8,128)(2,1)S(1)}, bf16[24,64,1024]{2,1,0:T(8,128)(2,1)S(1)}, u32[]{:S(2)}, u32[]{:S(2)}) collective-permute-start(bf16[24,64,1024]{2,1,0:T(8,128)(2,1)S(1)} %shard_map.88.refs_2_), channel_id=1, source_target_pairs={{0,8},{8,0},{1,9},{9,1},{2,10},{10,2},{3,11},{11,3},{4,12},{12,4},... | collective-permute-start | bytes 9437192 | tf_op jit(solution)/shard_map/ppermute | solution.py:463
  33.6 31.4 %collective-permute-start.12 = (bf16[768,512]{1,0:T(8,128)(2,1)S(1)}, bf16[768,512]{1,0:T(8,128)(2,1)S(1)}, u32[]{:S(2)}, u32[]{:S(2)}) collective-permute-start(bf16[768,512]{1,0:T(8,128)(2,1)S(1)} %shard_map.89.refs_1_), channel_id=1, source_target_pairs={{0,2},{2,4},{4,6},{6,7},{7,5},{5,3},{3,1},{1,0},{8,10},{10,12},{12... | collective-permute-start | bytes 2359304 | tf_op jit(solution)/shard_map/ppermute | solution.py:441
  37.4 32.5 %collective-permute-start.11 = (bf16[768,512]{1,0:T(8,128)(2,1)S(1)}, bf16[768,512]{1,0:T(8,128)(2,1)S(1)}, u32[]{:S(2)}, u32[]{:S(2)}) collective-permute-start(bf16[768,512]{1,0:T(8,128)(2,1)S(1)} %shard_map.91.after_ref), channel_id=1, source_target_pairs={{0,1},{2,0},{4,2},{6,4},{7,6},{5,7},{3,5},{1,3},{8,9},{10,8},{12,1... | collective-permute-start | bytes 2359304 | tf_op jit(solution)/shard_map/ppermute | solution.py:441
  44.1 20.2 %collective-permute-start.9 = (f16[64,384]{1,0:T(8,128)(2,1)S(1)}, f16[64,384]{1,0:T(8,128)(2,1)S(1)}, u32[]{:S(2)}, u32[]{:S(2)}) collective-permute-start(f16[64,384]{1,0:T(8,128)(2,1)S(1)} %multiply_convert_fusion.2), channel_id=1, source_target_pairs={{0,1},{1,0},{2,3},{3,2},{4,5},{5,4},{6,7},{7,6},{8,9},{9,8},{10,11... | collective-permute-start | bytes 147464 | tf_op jit(solution)/shard_map/ppermute | solution.py:472
  49.1 36.1 %collective-permute-start.15 = (bf16[768,512]{1,0:T(8,128)(2,1)S(1)}, bf16[768,512]{1,0:T(8,128)(2,1)S(1)}, u32[]{:S(2)}, u32[]{:S(2)}) collective-permute-start(bf16[768,512]{1,0:T(8,128)(2,1)S(1)} %shard_map.94.refs_1_), channel_id=1, source_target_pairs={{0,2},{2,4},{4,6},{6,7},{7,5},{5,3},{3,1},{1,0},{8,10},{10,12},{12... | collective-permute-start | bytes 2359304 | tf_op jit(solution)/shard_map/ppermute | solution.py:441
  52.9 35.1 %collective-permute-start.14 = (bf16[768,512]{1,0:T(8,128)(2,1)S(1)}, bf16[768,512]{1,0:T(8,128)(2,1)S(1)}, u32[]{:S(2)}, u32[]{:S(2)}) collective-permute-start(bf16[768,512]{1,0:T(8,128)(2,1)S(1)} %shard_map.95.after_ref), channel_id=1, source_target_pairs={{0,1},{2,0},{4,2},{6,4},{7,6},{5,7},{3,5},{1,3},{8,9},{10,8},{12,1... | collective-permute-start | bytes 2359304 | tf_op jit(solution)/shard_map/ppermute | solution.py:441
  65.0 16.9 %collective-permute-start.10 = (f16[64,384]{1,0:T(8,128)(2,1)S(1)}, f16[64,384]{1,0:T(8,128)(2,1)S(1)}, u32[]{:S(2)}, u32[]{:S(2)}) collective-permute-start(f16[64,384]{1,0:T(8,128)(2,1)S(1)} %multiply_convert_fusion.1), channel_id=1, source_target_pairs={{0,2},{1,3},{2,0},{3,1},{4,6},{5,7},{6,4},{7,5},{8,10},{9,11},{10,... | collective-permute-start | bytes 147464 | tf_op jit(solution)/shard_map/ppermute | solution.py:472
  67.9 34.0 %collective-permute-start.18 = (bf16[768,512]{1,0:T(8,128)(2,1)S(1)}, bf16[768,512]{1,0:T(8,128)(2,1)S(1)}, u32[]{:S(2)}, u32[]{:S(2)}) collective-permute-start(bf16[768,512]{1,0:T(8,128)(2,1)S(1)} %shard_map.99.refs_1_), channel_id=1, source_target_pairs={{0,2},{2,4},{4,6},{6,7},{7,5},{5,3},{3,1},{1,0},{8,10},{10,12},{12... | collective-permute-start | bytes 2359304 | tf_op jit(solution)/shard_map/ppermute | solution.py:441
  72.7 34.1 %collective-permute-start.17 = (bf16[768,512]{1,0:T(8,128)(2,1)S(1)}, bf16[768,512]{1,0:T(8,128)(2,1)S(1)}, u32[]{:S(2)}, u32[]{:S(2)}) collective-permute-start(bf16[768,512]{1,0:T(8,128)(2,1)S(1)} %shard_map.100.refs_0_.after_ref), channel_id=1, source_target_pairs={{0,1},{2,0},{4,2},{6,4},{7,6},{5,7},{3,5},{1,3},{8,9},{10,8},{12,1... | collective-permute-start | bytes 2359304 | tf_op jit(solution)/shard_map/ppermute | solution.py:441
  82.6 17.7 %collective-permute-start.13 = (f16[64,384]{1,0:T(8,128)(2,1)S(1)}, f16[64,384]{1,0:T(8,128)(2,1)S(1)}, u32[]{:S(2)}, u32[]{:S(2)}) collective-permute-start(f16[64,384]{1,0:T(8,128)(2,1)S(1)} %multiply_convert_fusion), channel_id=1, source_target_pairs={{0,4},{1,5},{2,6},{3,7},{4,0},{5,1},{6,2},{7,3},{8,12},{9,13},{10,... | collective-permute-start | bytes 147464 | tf_op jit(solution)/shard_map/ppermute | solution.py:472
  90.8 40.4 %collective-permute-start.22 = (bf16[768,512]{1,0:T(8,128)(2,1)S(1)}, bf16[768,512]{1,0:T(8,128)(2,1)S(1)}, u32[]{:S(2)}, u32[]{:S(2)}) collective-permute-start(bf16[768,512]{1,0:T(8,128)(2,1)S(1)} %shard_map.104.refs_0_.after_ref), channel_id=1, source_target_pairs={{0,1},{2,0},{4,2},{6,4},{7,6},{5,7},{3,5},{1,3},{8,9},{10,8},{12,1... | collective-permute-start | bytes 2359304 | tf_op jit(solution)/shard_map/ppermute | solution.py:441
  91.7 41.7 %collective-permute-start.19 = (bf16[768,512]{1,0:T(8,128)(2,1)S(1)}, bf16[768,512]{1,0:T(8,128)(2,1)S(1)}, u32[]{:S(2)}, u32[]{:S(2)}) collective-permute-start(bf16[768,512]{1,0:T(8,128)(2,1)S(1)} %shard_map.103.refs_1_), channel_id=1, source_target_pairs={{0,2},{2,4},{4,6},{6,7},{7,5},{5,3},{3,1},{1,0},{8,10},{10,12},{12... | collective-permute-start | bytes 2359304 | tf_op jit(solution)/shard_map/ppermute | solution.py:441
  101.0 14.9 %collective-permute-start.16 = (bf16[64,384]{1,0:T(8,128)(2,1)S(1)}, bf16[64,384]{1,0:T(8,128)(2,1)S(1)}, u32[]{:S(2)}, u32[]{:S(2)}) collective-permute-start(bf16[64,384]{1,0:T(8,128)(2,1)S(1)} %shard_map.106.refs_1_.low_ref), channel_id=1, source_target_pairs={{0,1},{1,0},{2,3},{3,2},{4,5},{5,4},{6,7},{7,6},{8,9},{9,8},{10,11... | collective-permute-start | bytes 147464 | tf_op jit(solution)/shard_map/ppermute | solution.py:472
  104.7 26.5 %collective-permute-start.21 = (bf16[768,512]{1,0:T(8,128)(2,1)S(1)}, bf16[768,512]{1,0:T(8,128)(2,1)S(1)}, u32[]{:S(2)}, u32[]{:S(2)}) collective-permute-start(bf16[768,512]{1,0:T(8,128)(2,1)S(1)} %shard_map.107.refs_1_), channel_id=1, source_target_pairs={{0,2},{2,4},{4,6},{6,7},{7,5},{5,3},{3,1},{1,0},{8,10},{10,12},{12... | collective-permute-start | bytes 2359304 | tf_op jit(solution)/shard_map/ppermute | solution.py:441
  109.6 23.8 %collective-permute-start.20 = (bf16[768,512]{1,0:T(8,128)(2,1)S(1)}, bf16[768,512]{1,0:T(8,128)(2,1)S(1)}, u32[]{:S(2)}, u32[]{:S(2)}) collective-permute-start(bf16[768,512]{1,0:T(8,128)(2,1)S(1)} %shard_map.108.after_ref), channel_id=1, source_target_pairs={{0,1},{2,0},{4,2},{6,4},{7,6},{5,7},{3,5},{1,3},{8,9},{10,8},{12,1... | collective-permute-start | bytes 2359304 | tf_op jit(solution)/shard_map/ppermute | solution.py:441
  115.9 15.3 %copy-start.4 = (s32[3,1]{0,1:T(1,128)S(1)}, s32[3,1]{0,1:T(1,128)}, u32[]{:S(2)}) copy-start(s32[3,1]{0,1:T(1,128)} %param.15) | copy-start | bytes 40
  (11 other events, 74.5 us)

commit v11 on v10

--- a/solution.py
+++ b/solution.py
@@ -9,6 +9,7 @@
 
 VMEM_LIMIT = 40 * 1024 * 1024
 LOW_SCALE = 16.0
+GRAIN = 16
 SWAP = [(0, 1), (1, 0)]
 WHOLE = pl.BlockSpec(memory_space=pltpu.VMEM)
 ANYWHERE = pl.BlockSpec(memory_space=pl.ANY)
@@ -364,30 +365,54 @@
     )(side, own, pages, place, low, other, after)
 
 
-def finish_kernel(half, live, own_ref, one_ref, two_ref, *refs):
+def chunks(count):
+    size = 32 if count % 32 == 0 else GRAIN
+    return [slice(at, at + size) for at in range(0, count, size)]
+
+
+def join_kernel(own_ref, left_ref, right_ref, out_ref):
+    cols = left_ref.shape[1]
+    for rows in chunks(own_ref.shape[0]):
+        for at, part_ref in ((0, left_ref), (cols, right_ref)):
+            out_ref[rows, at : at + cols] = own_ref[rows, at : at + cols] + part_ref[
+                rows, :
+            ].astype(jnp.float32)
+
+
+def join(own, left, right):
+    return pl.pallas_call(
+        join_kernel,
+        in_specs=[WHOLE] * 3,
+        out_specs=WHOLE,
+        out_shape=jax.ShapeDtypeStruct(own.shape, own.dtype),
+        compiler_params=params(),
+        cost_estimate=cost(own.size, 10 * own.size),
+    )(own, left, right)
+
+
+def finish_kernel(half, live, own_ref, last_ref, *refs):
     out_ref = refs[-1]
     count, cols = out_ref.shape
     step = pl.program_id(0)
-    rows = pl.ds(pl.multiple_of(step * count, count), count)
-    total = (
-        own_ref[rows, half * cols : (half + 1) * cols]
-        + one_ref[rows, :].astype(jnp.float32)
-        + two_ref[rows, :].astype(jnp.float32)
-    )
-    row = lax.broadcasted_iota(jnp.int32, total.shape, 0)
-    out_ref[...] = jnp.where(row < live[step], total, 0.0).astype(out_ref.dtype)
-
-
-def finish(live, half, own, one, two, result):
+    start = pl.multiple_of(step * count, count)
+    columns = slice(half * cols, (half + 1) * cols)
+    for rows in chunks(count):
+        here = pl.ds(start + rows.start, rows.stop - rows.start)
+        total = own_ref[here, columns] + last_ref[here, :].astype(jnp.float32)
+        row = rows.start + lax.broadcasted_iota(jnp.int32, total.shape, 0)
+        out_ref[rows, :] = jnp.where(row < live[step], total, 0.0).astype(out_ref.dtype)
+
+
+def finish(live, half, own, last, result):
     rows, cols = own.shape
     steps = live.shape[0]
-    in_specs = [WHOLE, WHOLE, WHOLE]
-    operands = [own, one, two]
+    in_specs = [WHOLE, WHOLE]
+    operands = [own, last]
     aliases = {}
     if result is not None:
         in_specs.append(ANYWHERE)
         operands.append(result)
-        aliases = {4: 0}
+        aliases = {3: 0}
     return pl.pallas_call(
         functools.partial(finish_kernel, half),
         grid_spec=pltpu.PrefetchScalarGridSpec(
@@ -491,11 +516,10 @@
     other = over(low, 1)
     last = turn(number, last)
     own = add_delta(sizes, side, own, up_pages, row_list_position, low, other, last)
+    own = join(own, arrived[0, -1][0], arrived[1, 1][0])
     result = None
-    for half in range(2):
-        result = finish(
-            live_row_count.reshape(-1), half, own, arrived[half, 1][0], arrived[half, -1][0], result
-        )
+    for half, sign, _ in pairs[0]:
+        result = finish(live_row_count.reshape(-1), half, own, arrived[half, sign][0], result)
     return result.reshape(steps, row_count, -1)
 
 

time: 136 us -> 136 us (level)
  waiting for transfers between devices: 42.1 us -> 40.4 us
  transfers between devices with their start and end apart: 23 -> 23, of which waited for: 8 -> 9; matrix products, arithmetic and copies ran while one was open for 4% -> 4% of each run, Pallas kernels for 45% -> 46%
where the time goes in v11:
time: 136 us; the launch traced here: 135 us
  Pallas kernels  64.5 us (47%)
  waiting for transfers between devices  40.4 us (30%)
  starting transfers between devices  24 us (18%)
  local copies, waits for them, and re-layouts  4.07 us (3%)
  other arithmetic  2.14 us (2%)
    pallas_call x12, Pallas kernels, hop(): pl.pallas_call(functools.partial(hop_kernel, tuple(range(len(received))))...  33.5 us
    ppermute x4, waiting for transfers between devices, over(): return lax.ppermute(value, 'tp', [(i, i ^ apart) for i in range(size)])  23.4 us
    ppermute x12, waiting for transfers between devices, turn(): arrived[half, sign] = [lax.ppermute(last, 'tp', moves)]  14.5 us
    ppermute x12, starting transfers between devices, turn(): arrived[half, sign] = [lax.ppermute(last, 'tp', moves)]  13.1 us
    pallas_call x2, Pallas kernels, first_pieces(): pl.pallas_call(functools.partial(first_kernel, after is not None), grid_s...  7.27 us
    pallas_call x1, Pallas kernels, own_terms(): pl.pallas_call(own_kernel, grid_spec=pltpu.PrefetchScalarGridSpec(num_sca...  7.23 us
    pallas_call x1, Pallas kernels, low_rank(): pl.pallas_call(functools.partial(low_kernel, sizes), grid_spec=pltpu.Pref...  5.84 us
    ppermute x4, starting transfers between devices, over(): return lax.ppermute(value, 'tp', [(i, i ^ apart) for i in range(size)])  5.65 us
  transfers between devices with their start and end apart: 23, of which 9 were waited for; matrix products, arithmetic and copies ran while one was open for 4% of the time, Pallas kernels for 46%

profile of v11, /device:TPU:0, one launch (start us, length us, event | category | flops | bytes accessed | tf_op | source)
XLA Modules:
  0.0 135.4 jit_solution(12010230073382587891)
XLA Ops:
  1.9 3.7 %shard_map.82 = (bf16[768,256]{1,0:T(8,128)(2,1)}, bf16[768,256]{1,0:T(8,128)(2,1)}) custom-call(s32[8]{0:T(128)S(1)} %compare_select_fusion.3.dests, bf16[768,1024]{1,0:T(8,128)(2,1)S(1)} %bitcast.11, bf16[1024,8192]{1,0:T(8,128)(2,1)} %w_ref.29), custom_call_target="tpu_custom_call" | custom-call | flops 24159191040 | bytes 3407872 | tf_op jit(solution)/shard_map/pallas_call | solution.py:124
  5.6 2.5 %collective-permute-start.2 = (bf16[768,256]{1,0:T(8,128)(2,1)}, bf16[768,256]{1,0:T(8,128)(2,1)S(1)}, u32[]{:S(2)}, u32[]{:S(2)}) collective-permute-start(bf16[768,256]{1,0:T(8,128)(2,1)} %get-tuple-element.13.refs_0_), channel_id=1, source_target_pairs={{0,1},{2,0},{4,2},{6,4},{7,6},{5,7},{3,5},{1,3},{8,9},{10,8},{12,1... | collective-permute-start | bytes 1179656 | tf_op jit(solution)/shard_map/ppermute | solution.py:477
  8.2 3.6 %shard_map.83 = (bf16[768,256]{1,0:T(8,128)(2,1)}, bf16[768,256]{1,0:T(8,128)(2,1)S(1)}) custom-call(s32[8]{0:T(128)S(1)} %compare_select_fusion.3.dests, bf16[768,1024]{1,0:T(8,128)(2,1)S(1)} %bitcast.12, bf16[1024,8192]{1,0:T(8,128)(2,1)} %w_ref.29, bf16[768,256]{1,0:T(8,128)(2,1)} %get-tuple-element.13.refs_0_), custom_call_target="tpu_custom_call" | custom-call | flops 24159191040 | bytes 3407872 | tf_op jit(solution)/shard_map/pallas_call | solution.py:124
  14.9 2.7 %shard_map.84.refs_0_ = bf16[24,64,1024]{2,1,0:T(8,128)(2,1)S(1)} custom-call(s32[24]{0:T(128)S(1)} %get-tuple-element.21.index, bf16[96,64,1024]{2,1,0:T(8,128)(2,1)} %table_ref.6, bf16[768,256]{1,0:T(8,128)(2,1)S(1)} %get-tuple-element.14.after_ref), custom_call_target="tpu_custom_call" | custom-call | bytes 6291456 | tf_op jit(solution)/shard_map/pallas_call | solution.py:168
  20.3 2.8 %shard_map.86.refs_0_ = bf16[768,512]{1,0:T(8,128)(2,1)S(1)} custom-call(s32[8]{0:T(128)S(1)} %compare_select_fusion.3.dests, bf16[768,1024]{1,0:T(8,128)(2,1)S(1)} %bitcast.13, bf16[1024,8192]{1,0:T(8,128)(2,1)} %w_ref.29, f32[8,128]{1,0:T(8,128)S(1)} %shard_map.85.refs_0_), custom_call_target="tpu_custom_call" | custom-call | flops 24159191040 | bytes 4194304 | tf_op jit(solution)/shard_map/pallas_call | solution.py:80
  23.1 2.8 %shard_map.87.after_ref = bf16[768,512]{1,0:T(8,128)(2,1)S(1)} custom-call(s32[8]{0:T(128)S(1)} %compare_select_fusion.3.dests, bf16[768,1024]{1,0:T(8,128)(2,1)S(1)} %bitcast.14, bf16[1024,8192]{1,0:T(8,128)(2,1)} %w_ref.29, bf16[768,512]{1,0:T(8,128)(2,1)S(1)} %shard_map.86.refs_0_), custom_call_target="tpu_custom_call" | custom-call | flops 24159191040 | bytes 4194304 | tf_op jit(solution)/shard_map/pallas_call | solution.py:80
  27.9 2.7 %shard_map.88.refs_2_ = bf16[24,64,1024]{2,1,0:T(8,128)(2,1)S(1)} custom-call(s32[24]{0:T(128)S(1)} %get-tuple-element.21.index, bf16[96,64,1024]{2,1,0:T(8,128)(2,1)} %table_ref.7, bf16[768,512]{1,0:T(8,128)(2,1)S(1)} %shard_map.87.after_ref), custom_call_target="tpu_custom_call" | custom-call | bytes 6291456 | tf_op jit(solution)/shard_map/pallas_call | solution.py:168
  30.7 2.9 %shard_map.89.refs_1_ = bf16[768,512]{1,0:T(8,128)(2,1)S(1)} custom-call(s32[8]{0:T(128)S(1)} %compare_select_fusion.3.dests, bf16[768,1024]{1,0:T(8,128)(2,1)S(1)} %bitcast.15, bf16[1024,8192]{1,0:T(8,128)(2,1)} %w_ref.29, bf16[768,256]{1,0:T(8,128)(2,1)S(1)} %collective-permute-done.1.refs_1_.refs_0_, bf16[768,256]{1,0:T(8,128)(2,1)S(1)} %collective-permute-done.8.refs_1_, ...), custom_call_target="tpu_custom_call" | custom-call | flops 24159191040 | bytes 4194304 | tf_op jit(solution)/shard_map/pallas_call | solution.py:80
  34.4 2.9 %shard_map.91.after_ref = bf16[768,512]{1,0:T(8,128)(2,1)S(1)} custom-call(s32[8]{0:T(128)S(1)} %compare_select_fusion.3.dests, bf16[768,1024]{1,0:T(8,128)(2,1)S(1)} %bitcast.16, bf16[1024,8192]{1,0:T(8,128)(2,1)} %w_ref.29, bf16[768,256]{1,0:T(8,128)(2,1)S(1)} %collective-permute-done.2.refs_2_.refs_0_, ...), custom_call_target="tpu_custom_call" | custom-call | flops 24159191040 | bytes 4194304 | tf_op jit(solution)/shard_map/pallas_call | solution.py:80
  38.7 5.8 %shard_map.92 = (f32[64,384]{1,0:T(8,128)S(1)}, f32[64,384]{1,0:T(8,128)S(1)}) custom-call(s32[24]{0:T(128)S(1)} %compare_convert_fusion.local, s32[24]{0:T(128)S(1)} %get-tuple-element.22.index, s32[1]{0:T(128)} %bitcast.1.side, bf16[768,1024]{1,0:T(8,128)(2,1)S(1)} %bitcast.17, s32[3,256]{1,0:T(4,128)S(1)} %copy-done.7, bf16[96,64,1024]{2,1,0:T(8,128)(2,1)} %table_ref.6, ...), custom_call_target="tpu_custom_call" | custom-call | flops 12079595520 | bytes 4718592 | tf_op jit(solution)/shard_map/pallas_call | solution.py:239
  46.4 2.8 %shard_map.94.refs_1_ = bf16[768,512]{1,0:T(8,128)(2,1)S(1)} custom-call(s32[8]{0:T(128)S(1)} %compare_select_fusion.3.dests, bf16[768,1024]{1,0:T(8,128)(2,1)S(1)} %bitcast.18, bf16[1024,8192]{1,0:T(8,128)(2,1)} %w_ref.29, bf16[768,512]{1,0:T(8,128)(2,1)S(1)} %collective-permute-done.5.refs_0_, f32[8,128]{1,0:T(8,128)S(1)} %shard_map.93.refs_1_), custom_call_target="tpu_custom_call" | custom-call | flops 24159191040 | bytes 4194304 | tf_op jit(solution)/shard_map/pallas_call | solution.py:80
  50.7 2.8 %shard_map.95.after_ref = bf16[768,512]{1,0:T(8,128)(2,1)S(1)} custom-call(s32[8]{0:T(128)S(1)} %compare_select_fusion.3.dests, bf16[768,1024]{1,0:T(8,128)(2,1)S(1)} %bitcast.19, bf16[1024,8192]{1,0:T(8,128)(2,1)} %w_ref.29, bf16[768,512]{1,0:T(8,128)(2,1)S(1)} %collective-permute-done.4.refs_0_, bf16[768,512]{1,0:T(8,128)(2,1)S(1)} %shard_map.94.refs_1_), custom_call_target="tpu_custom_call" | custom-call | flops 24159191040 | bytes 4194304 | tf_op jit(solution)/shard_map/pallas_call | solution.py:80
  54.0 7.2 %shard_map.96 = (f32[768,1024]{1,0:T(8,128)S(1)}, bf16[24,64,1024]{2,1,0:T(8,128)(2,1)S(1)}) custom-call(s32[24]{0:T(128)S(1)} %compare_convert_fusion.local, s32[24]{0:T(128)S(1)} %get-tuple-element.22.index, s32[8]{0:T(128)S(1)} %compare_select_fusion.3.dests, bf16[768,1024]{1,0:T(8,128)(2,1)S(1)} %bitcast.20, bf16[1024,8192]{1,0:T(8,128)(2,1)} %w_ref.29, ...), custom_call_target="tpu_custom_call" | custom-call | flops 48318382080 | bytes 13107200 | tf_op jit(solution)/shard_map/pallas_call | solution.py:298
  65.5 2.8 %shard_map.99.refs_1_ = bf16[768,512]{1,0:T(8,128)(2,1)S(1)} custom-call(s32[8]{0:T(128)S(1)} %compare_select_fusion.3.dests, bf16[768,1024]{1,0:T(8,128)(2,1)S(1)} %bitcast.21, bf16[1024,8192]{1,0:T(8,128)(2,1)} %w_ref.29, bf16[768,512]{1,0:T(8,128)(2,1)S(1)} %collective-permute-done.12.refs_0_, f32[64,384]{1,0:T(8,128)S(1)} %shard_map.98.refs_1_.low_ref), custom_call_target="tpu_custom_call" | custom-call | flops 24159191040 | bytes 4194304 | tf_op jit(solution)/shard_map/pallas_call | solution.py:80
  69.9 2.8 %shard_map.100.refs_0_.after_ref = bf16[768,512]{1,0:T(8,128)(2,1)S(1)} custom-call(s32[8]{0:T(128)S(1)} %compare_select_fusion.3.dests, bf16[768,1024]{1,0:T(8,128)(2,1)S(1)} %bitcast.22, bf16[1024,8192]{1,0:T(8,128)(2,1)} %w_ref.29, bf16[768,512]{1,0:T(8,128)(2,1)S(1)} %collective-permute-done.11.refs_0_, bf16[768,512]{1,0:T(8,128)(2,1)S(1)} %shard_map.99.refs_1_), custom_call_target="tpu_custom_call" | custom-call | flops 24159191040 | bytes 4194304 | tf_op jit(solution)/shard_map/pallas_call | solution.py:80
  73.7 8.2 %collective-permute-done.10 = f16[64,384]{1,0:T(8,128)(2,1)S(1)} collective-permute-done((f16[64,384]{1,0:T(8,128)(2,1)S(1)}, f16[64,384]{1,0:T(8,128)(2,1)S(1)}, u32[]{:S(2)}, u32[]{:S(2)}) %collective-permute-start.10) | collective-permute-done | bytes 49184 | tf_op jit(solution)/shard_map/ppermute | solution.py:497
  82.6 2.7 %collective-permute-start.13 = (f16[64,384]{1,0:T(8,128)(2,1)S(1)}, f16[64,384]{1,0:T(8,128)(2,1)S(1)}, u32[]{:S(2)}, u32[]{:S(2)}) collective-permute-start(f16[64,384]{1,0:T(8,128)(2,1)S(1)} %multiply_convert_fusion), channel_id=1, source_target_pairs={{0,4},{1,5},{2,6},{3,7},{4,0},{5,1},{6,2},{7,3},{8,12},{9,13},{10,... | collective-permute-start | bytes 147464 | tf_op jit(solution)/shard_map/ppermute | solution.py:497
  85.2 2.8 %shard_map.103.refs_1_ = bf16[768,512]{1,0:T(8,128)(2,1)S(1)} custom-call(s32[8]{0:T(128)S(1)} %compare_select_fusion.3.dests, bf16[768,1024]{1,0:T(8,128)(2,1)S(1)} %bitcast.23, bf16[1024,8192]{1,0:T(8,128)(2,1)} %w_ref.29, bf16[768,512]{1,0:T(8,128)(2,1)S(1)} %collective-permute-done.15.refs_0_, f32[64,384]{1,0:T(8,128)S(1)} %shard_map.102.refs_1_.low_ref), custom_call_target="tpu_custom_call" | custom-call | flops 24159191040 | bytes 4194304 | tf_op jit(solution)/shard_map/pallas_call | solution.py:80
  88.0 2.8 %shard_map.104.refs_0_.after_ref = bf16[768,512]{1,0:T(8,128)(2,1)S(1)} custom-call(s32[8]{0:T(128)S(1)} %compare_select_fusion.3.dests, bf16[768,1024]{1,0:T(8,128)(2,1)S(1)} %bitcast.24, bf16[1024,8192]{1,0:T(8,128)(2,1)} %w_ref.29, bf16[768,512]{1,0:T(8,128)(2,1)S(1)} %collective-permute-done.14.refs_0_, bf16[768,512]{1,0:T(8,128)(2,1)S(1)} %shard_map.103.refs_1_), custom_call_target="tpu_custom_call" | custom-call | flops 24159191040 | bytes 4194304 | tf_op jit(solution)/shard_map/pallas_call | solution.py:80
  93.4 6.9 %collective-permute-done.13 = f16[64,384]{1,0:T(8,128)(2,1)S(1)} collective-permute-done((f16[64,384]{1,0:T(8,128)(2,1)S(1)}, f16[64,384]{1,0:T(8,128)(2,1)S(1)}, u32[]{:S(2)}, u32[]{:S(2)}) %collective-permute-start.13) | collective-permute-done | bytes 49184 | tf_op jit(solution)/shard_map/ppermute | solution.py:497
  101.9 2.8 %shard_map.107.refs_1_ = bf16[768,512]{1,0:T(8,128)(2,1)S(1)} custom-call(s32[8]{0:T(128)S(1)} %compare_select_fusion.3.dests, bf16[768,1024]{1,0:T(8,128)(2,1)S(1)} %bitcast.25, bf16[1024,8192]{1,0:T(8,128)(2,1)} %w_ref.29, bf16[768,512]{1,0:T(8,128)(2,1)S(1)} %collective-permute-done.18.refs_0_, bf16[64,384]{1,0:T(8,128)(2,1)S(1)} %shard_map.106.refs_1_.low_ref), custom_call_target="tpu_custom_call" | custom-call | flops 24159191040 | bytes 4194304 | tf_op jit(solution)/shard_map/pallas_call | solution.py:80
  106.8 2.8 %shard_map.108.after_ref = bf16[768,512]{1,0:T(8,128)(2,1)S(1)} custom-call(s32[8]{0:T(128)S(1)} %compare_select_fusion.3.dests, bf16[768,1024]{1,0:T(8,128)(2,1)S(1)} %bitcast.26, bf16[1024,8192]{1,0:T(8,128)(2,1)} %w_ref.29, bf16[768,512]{1,0:T(8,128)(2,1)S(1)} %collective-permute-done.17.refs_0_, bf16[768,512]{1,0:T(8,128)(2,1)S(1)} %shard_map.107.refs_1_), custom_call_target="tpu_custom_call" | custom-call | flops 24159191040 | bytes 4194304 | tf_op jit(solution)/shard_map/pallas_call | solution.py:80
  110.0 5.9 %collective-permute-done.16.other_ref = bf16[64,384]{1,0:T(8,128)(2,1)S(1)} collective-permute-done((bf16[64,384]{1,0:T(8,128)(2,1)S(1)}, bf16[64,384]{1,0:T(8,128)(2,1)S(1)}, u32[]{:S(2)}, u32[]{:S(2)}) %collective-permute-start.16) | collective-permute-done | bytes 49184 | tf_op jit(solution)/shard_map/ppermute | solution.py:497
  117.0 14.2 %collective-permute-done.22.last_ref = bf16[768,512]{1,0:T(8,128)(2,1)S(1)} collective-permute-done((bf16[768,512]{1,0:T(8,128)(2,1)S(1)}, bf16[768,512]{1,0:T(8,128)(2,1)S(1)}, u32[]{:S(2)}, u32[]{:S(2)}) %collective-permute-start.22) | collective-permute-done | bytes 786464 | tf_op jit(solution)/shard_map/ppermute | solution.py:466
  (95 shorter events, 35.4 us)
Async XLA Ops:
  0.0 13.9 %collective-permute-start = (s32[3,2,4]{2,1,0:T(2,128)}, s32[3,2,4]{2,1,0:T(2,128)S(1)}, u32[]{:S(2)}, u32[]{:S(2)}) collective-permute-start(s32[3,2,4]{2,1,0:T(2,128)} %param.13), channel_id=1, source_target_pairs={{0,8},{8,0},{1,9},{9,1},{2,10},{10,2},{3,11},{11,3},{4,12},{12,4},... | collective-permute-start | bytes 296 | tf_op jit(solution)/shard_map/ppermute | solution.py:472
  5.6 12.8 %collective-permute-start.2 = (bf16[768,256]{1,0:T(8,128)(2,1)}, bf16[768,256]{1,0:T(8,128)(2,1)S(1)}, u32[]{:S(2)}, u32[]{:S(2)}) collective-permute-start(bf16[768,256]{1,0:T(8,128)(2,1)} %get-tuple-element.13.refs_0_), channel_id=1, source_target_pairs={{0,1},{2,0},{4,2},{6,4},{7,6},{5,7},{3,5},{1,3},{8,9},{10,8},{12,1... | collective-permute-start | bytes 1179656 | tf_op jit(solution)/shard_map/ppermute | solution.py:477
  8.1 12.2 %collective-permute-start.1 = (bf16[768,256]{1,0:T(8,128)(2,1)}, bf16[768,256]{1,0:T(8,128)(2,1)S(1)}, u32[]{:S(2)}, u32[]{:S(2)}) collective-permute-start(bf16[768,256]{1,0:T(8,128)(2,1)} %get-tuple-element.15), channel_id=1, source_target_pairs={{0,2},{2,4},{4,6},{6,7},{7,5},{5,3},{3,1},{1,0},{8,10},{10,12},{12... | collective-permute-start | bytes 1179656 | tf_op jit(solution)/shard_map/ppermute | solution.py:477
  11.7 18.8 %collective-permute-start.8 = (bf16[768,256]{1,0:T(8,128)(2,1)}, bf16[768,256]{1,0:T(8,128)(2,1)S(1)}, u32[]{:S(2)}, u32[]{:S(2)}) collective-permute-start(bf16[768,256]{1,0:T(8,128)(2,1)} %get-tuple-element.16), channel_id=1, source_target_pairs={{0,2},{2,4},{4,6},{6,7},{7,5},{5,3},{3,1},{1,0},{8,10},{10,12},{12... | collective-permute-start | bytes 1179656 | tf_op jit(solution)/shard_map/ppermute | solution.py:477
  13.8 20.7 %collective-permute-start.7 = (bf16[768,256]{1,0:T(8,128)(2,1)S(1)}, bf16[768,256]{1,0:T(8,128)(2,1)S(1)}, u32[]{:S(2)}, u32[]{:S(2)}) collective-permute-start(bf16[768,256]{1,0:T(8,128)(2,1)S(1)} %get-tuple-element.14.after_ref), channel_id=1, source_target_pairs={{0,1},{2,0},{4,2},{6,4},{7,6},{5,7},{3,5},{1,3},{8,9},{10,8},{12,1... | collective-permute-start | bytes 1179656 | tf_op jit(solution)/shard_map/ppermute | solution.py:477
  17.6 16.0 %collective-permute-start.6 = (bf16[24,64,1024]{2,1,0:T(8,128)(2,1)S(1)}, bf16[24,64,1024]{2,1,0:T(8,128)(2,1)S(1)}, u32[]{:S(2)}, u32[]{:S(2)}) collective-permute-start(bf16[24,64,1024]{2,1,0:T(8,128)(2,1)S(1)} %shard_map.84.refs_0_), channel_id=1, source_target_pairs={{0,8},{8,0},{1,9},{9,1},{2,10},{10,2},{3,11},{11,3},{4,12},{12,4},... | collective-permute-start | bytes 9437192 | tf_op jit(solution)/shard_map/ppermute | solution.py:484
  25.8 20.5 %collective-permute-start.5 = (bf16[768,512]{1,0:T(8,128)(2,1)S(1)}, bf16[768,512]{1,0:T(8,128)(2,1)S(1)}, u32[]{:S(2)}, u32[]{:S(2)}) collective-permute-start(bf16[768,512]{1,0:T(8,128)(2,1)S(1)} %shard_map.86.refs_0_), channel_id=1, source_target_pairs={{0,2},{2,4},{4,6},{6,7},{7,5},{5,3},{3,1},{1,0},{8,10},{10,12},{12... | collective-permute-start | bytes 2359304 | tf_op jit(solution)/shard_map/ppermute | solution.py:466
  26.6 24.0 %collective-permute-start.4 = (bf16[768,512]{1,0:T(8,128)(2,1)S(1)}, bf16[768,512]{1,0:T(8,128)(2,1)S(1)}, u32[]{:S(2)}, u32[]{:S(2)}) collective-permute-start(bf16[768,512]{1,0:T(8,128)(2,1)S(1)} %shard_map.87.after_ref), channel_id=1, source_target_pairs={{0,1},{2,0},{4,2},{6,4},{7,6},{5,7},{3,5},{1,3},{8,9},{10,8},{12,1... | collective-permute-start | bytes 2359304 | tf_op jit(solution)/shard_map/ppermute | solution.py:466
  30.6 14.0 %collective-permute-start.3 = (bf16[24,64,1024]{2,1,0:T(8,128)(2,1)S(1)}, bf16[24,64,1024]{2,1,0:T(8,128)(2,1)S(1)}, u32[]{:S(2)}, u32[]{:S(2)}) collective-permute-start(bf16[24,64,1024]{2,1,0:T(8,128)(2,1)S(1)} %shard_map.88.refs_2_), channel_id=1, source_target_pairs={{0,8},{8,0},{1,9},{9,1},{2,10},{10,2},{3,11},{11,3},{4,12},{12,4},... | collective-permute-start | bytes 9437192 | tf_op jit(solution)/shard_map/ppermute | solution.py:488
  33.6 31.8 %collective-permute-start.12 = (bf16[768,512]{1,0:T(8,128)(2,1)S(1)}, bf16[768,512]{1,0:T(8,128)(2,1)S(1)}, u32[]{:S(2)}, u32[]{:S(2)}) collective-permute-start(bf16[768,512]{1,0:T(8,128)(2,1)S(1)} %shard_map.89.refs_1_), channel_id=1, source_target_pairs={{0,2},{2,4},{4,6},{6,7},{7,5},{5,3},{3,1},{1,0},{8,10},{10,12},{12... | collective-permute-start | bytes 2359304 | tf_op jit(solution)/shard_map/ppermute | solution.py:466
  37.4 32.5 %collective-permute-start.11 = (bf16[768,512]{1,0:T(8,128)(2,1)S(1)}, bf16[768,512]{1,0:T(8,128)(2,1)S(1)}, u32[]{:S(2)}, u32[]{:S(2)}) collective-permute-start(bf16[768,512]{1,0:T(8,128)(2,1)S(1)} %shard_map.91.after_ref), channel_id=1, source_target_pairs={{0,1},{2,0},{4,2},{6,4},{7,6},{5,7},{3,5},{1,3},{8,9},{10,8},{12,1... | collective-permute-start | bytes 2359304 | tf_op jit(solution)/shard_map/ppermute | solution.py:466
  44.6 19.7 %collective-permute-start.9 = (f16[64,384]{1,0:T(8,128)(2,1)S(1)}, f16[64,384]{1,0:T(8,128)(2,1)S(1)}, u32[]{:S(2)}, u32[]{:S(2)}) collective-permute-start(f16[64,384]{1,0:T(8,128)(2,1)S(1)} %multiply_convert_fusion.2), channel_id=1, source_target_pairs={{0,1},{1,0},{2,3},{3,2},{4,5},{5,4},{6,7},{7,6},{8,9},{9,8},{10,11... | collective-permute-start | bytes 147464 | tf_op jit(solution)/shard_map/ppermute | solution.py:497
  49.1 36.1 %collective-permute-start.15 = (bf16[768,512]{1,0:T(8,128)(2,1)S(1)}, bf16[768,512]{1,0:T(8,128)(2,1)S(1)}, u32[]{:S(2)}, u32[]{:S(2)}) collective-permute-start(bf16[768,512]{1,0:T(8,128)(2,1)S(1)} %shard_map.94.refs_1_), channel_id=1, source_target_pairs={{0,2},{2,4},{4,6},{6,7},{7,5},{5,3},{3,1},{1,0},{8,10},{10,12},{12... | collective-permute-start | bytes 2359304 | tf_op jit(solution)/shard_map/ppermute | solution.py:466
  53.4 34.6 %collective-permute-start.14 = (bf16[768,512]{1,0:T(8,128)(2,1)S(1)}, bf16[768,512]{1,0:T(8,128)(2,1)S(1)}, u32[]{:S(2)}, u32[]{:S(2)}) collective-permute-start(bf16[768,512]{1,0:T(8,128)(2,1)S(1)} %shard_map.95.after_ref), channel_id=1, source_target_pairs={{0,1},{2,0},{4,2},{6,4},{7,6},{5,7},{3,5},{1,3},{8,9},{10,8},{12,1... | collective-permute-start | bytes 2359304 | tf_op jit(solution)/shard_map/ppermute | solution.py:466
  65.0 16.9 %collective-permute-start.10 = (f16[64,384]{1,0:T(8,128)(2,1)S(1)}, f16[64,384]{1,0:T(8,128)(2,1)S(1)}, u32[]{:S(2)}, u32[]{:S(2)}) collective-permute-start(f16[64,384]{1,0:T(8,128)(2,1)S(1)} %multiply_convert_fusion.1), channel_id=1, source_target_pairs={{0,2},{1,3},{2,0},{3,1},{4,6},{5,7},{6,4},{7,5},{8,10},{9,11},{10,... | collective-permute-start | bytes 147464 | tf_op jit(solution)/shard_map/ppermute | solution.py:497
  68.2 33.6 %collective-permute-start.18 = (bf16[768,512]{1,0:T(8,128)(2,1)S(1)}, bf16[768,512]{1,0:T(8,128)(2,1)S(1)}, u32[]{:S(2)}, u32[]{:S(2)}) collective-permute-start(bf16[768,512]{1,0:T(8,128)(2,1)S(1)} %shard_map.99.refs_1_), channel_id=1, source_target_pairs={{0,2},{2,4},{4,6},{6,7},{7,5},{5,3},{3,1},{1,0},{8,10},{10,12},{12... | collective-permute-start | bytes 2359304 | tf_op jit(solution)/shard_map/ppermute | solution.py:466
  72.7 34.1 %collective-permute-start.17 = (bf16[768,512]{1,0:T(8,128)(2,1)S(1)}, bf16[768,512]{1,0:T(8,128)(2,1)S(1)}, u32[]{:S(2)}, u32[]{:S(2)}) collective-permute-start(bf16[768,512]{1,0:T(8,128)(2,1)S(1)} %shard_map.100.refs_0_.after_ref), channel_id=1, source_target_pairs={{0,1},{2,0},{4,2},{6,4},{7,6},{5,7},{3,5},{1,3},{8,9},{10,8},{12,1... | collective-permute-start | bytes 2359304 | tf_op jit(solution)/shard_map/ppermute | solution.py:466
  82.6 17.7 %collective-permute-start.13 = (f16[64,384]{1,0:T(8,128)(2,1)S(1)}, f16[64,384]{1,0:T(8,128)(2,1)S(1)}, u32[]{:S(2)}, u32[]{:S(2)}) collective-permute-start(f16[64,384]{1,0:T(8,128)(2,1)S(1)} %multiply_convert_fusion), channel_id=1, source_target_pairs={{0,4},{1,5},{2,6},{3,7},{4,0},{5,1},{6,2},{7,3},{8,12},{9,13},{10,... | collective-permute-start | bytes 147464 | tf_op jit(solution)/shard_map/ppermute | solution.py:497
  90.8 25.8 %collective-permute-start.19 = (bf16[768,512]{1,0:T(8,128)(2,1)S(1)}, bf16[768,512]{1,0:T(8,128)(2,1)S(1)}, u32[]{:S(2)}, u32[]{:S(2)}) collective-permute-start(bf16[768,512]{1,0:T(8,128)(2,1)S(1)} %shard_map.104.refs_0_.after_ref), channel_id=1, source_target_pairs={{0,1},{2,0},{4,2},{6,4},{7,6},{5,7},{3,5},{1,3},{8,9},{10,8},{12,1... | collective-permute-start | bytes 2359304 | tf_op jit(solution)/shard_map/ppermute | solution.py:466
  91.7 24.9 %collective-permute-start.20 = (bf16[768,512]{1,0:T(8,128)(2,1)S(1)}, bf16[768,512]{1,0:T(8,128)(2,1)S(1)}, u32[]{:S(2)}, u32[]{:S(2)}) collective-permute-start(bf16[768,512]{1,0:T(8,128)(2,1)S(1)} %shard_map.103.refs_1_), channel_id=1, source_target_pairs={{0,2},{2,4},{4,6},{6,7},{7,5},{5,3},{3,1},{1,0},{8,10},{10,12},{12... | collective-permute-start | bytes 2359304 | tf_op jit(solution)/shard_map/ppermute | solution.py:466
  101.0 14.9 %collective-permute-start.16 = (bf16[64,384]{1,0:T(8,128)(2,1)S(1)}, bf16[64,384]{1,0:T(8,128)(2,1)S(1)}, u32[]{:S(2)}, u32[]{:S(2)}) collective-permute-start(bf16[64,384]{1,0:T(8,128)(2,1)S(1)} %shard_map.106.refs_1_.low_ref), channel_id=1, source_target_pairs={{0,1},{1,0},{2,3},{3,2},{4,5},{5,4},{6,7},{7,6},{8,9},{9,8},{10,11... | collective-permute-start | bytes 147464 | tf_op jit(solution)/shard_map/ppermute | solution.py:497
  104.7 26.5 %collective-permute-start.22 = (bf16[768,512]{1,0:T(8,128)(2,1)S(1)}, bf16[768,512]{1,0:T(8,128)(2,1)S(1)}, u32[]{:S(2)}, u32[]{:S(2)}) collective-permute-start(bf16[768,512]{1,0:T(8,128)(2,1)S(1)} %shard_map.107.refs_1_), channel_id=1, source_target_pairs={{0,2},{2,4},{4,6},{6,7},{7,5},{5,3},{3,1},{1,0},{8,10},{10,12},{12... | collective-permute-start | bytes 2359304 | tf_op jit(solution)/shard_map/ppermute | solution.py:466
  109.6 23.7 %collective-permute-start.21 = (bf16[768,512]{1,0:T(8,128)(2,1)S(1)}, bf16[768,512]{1,0:T(8,128)(2,1)S(1)}, u32[]{:S(2)}, u32[]{:S(2)}) collective-permute-start(bf16[768,512]{1,0:T(8,128)(2,1)S(1)} %shard_map.108.after_ref), channel_id=1, source_target_pairs={{0,1},{2,0},{4,2},{6,4},{7,6},{5,7},{3,5},{1,3},{8,9},{10,8},{12,1... | collective-permute-start | bytes 2359304 | tf_op jit(solution)/shard_map/ppermute | solution.py:466
  116.6 14.7 %copy-start.4 = (s32[3,1]{0,1:T(1,128)S(1)}, s32[3,1]{0,1:T(1,128)}, u32[]{:S(2)}) copy-start(s32[3,1]{0,1:T(1,128)} %param.15) | copy-start | bytes 40
  (11 other events, 73.4 us)

commit v12 on v11

--- a/solution.py
+++ b/solution.py
@@ -8,6 +8,7 @@
 from jax.sharding import PartitionSpec as P
 
 VMEM_LIMIT = 40 * 1024 * 1024
+FIRST_VMEM_LIMIT = 62 * 1024 * 1024
 LOW_SCALE = 16.0
 GRAIN = 16
 SWAP = [(0, 1), (1, 0)]
@@ -37,8 +38,8 @@
     return list(range(0, size, 2)) + list(range(size - 1, 0, -2))
 
 
-def params():
-    return pltpu.CompilerParams(vmem_limit_bytes=VMEM_LIMIT)
+def params(limit=VMEM_LIMIT):
+    return pltpu.CompilerParams(vmem_limit_bytes=limit)
 
 
 def cost(flops, size):
@@ -103,7 +104,8 @@
 
 def first_kernel(with_after, dests, x_ref, w_ref, *refs):
     total = jnp.dot(x_ref[...], w_ref[...], preferred_element_type=jnp.float32)
-    for chain, out_ref in enumerate(refs[-2:]):
+    refs[-1][...] = jnp.zeros_like(refs[-1])
+    for chain, out_ref in enumerate(refs[-3:-1]):
 
         @pl.when(pl.program_id(0) == chain)
         def _():
@@ -126,11 +128,16 @@
         grid_spec=pltpu.PrefetchScalarGridSpec(
             num_scalar_prefetch=1,
             grid=(2,),
-            in_specs=[WHOLE, pl.BlockSpec((depth, tile), place)] + [ANYWHERE] * len(tail),
-            out_specs=[WHOLE, WHOLE],
-        ),
-        out_shape=[jax.ShapeDtypeStruct((rows, tile), jnp.bfloat16)] * 2,
-        compiler_params=params(),
+            in_specs=[
+                pl.BlockSpec((rows, depth), lambda j, d: (0, 0)) if after is None else WHOLE,
+                pl.BlockSpec((depth, tile), place),
+            ]
+            + [ANYWHERE] * len(tail),
+            out_specs=[WHOLE, WHOLE, pl.BlockSpec((8, 128), lambda j, d: (0, 0))],
+        ),
+        out_shape=[jax.ShapeDtypeStruct((rows, tile), jnp.bfloat16)] * 2
+        + [jax.ShapeDtypeStruct((8, 128), jnp.float32)],
+        compiler_params=params(FIRST_VMEM_LIMIT if after is None else VMEM_LIMIT),
         cost_estimate=cost(
             4 * rows * depth * tile, 2 * (rows * depth + 2 * depth * tile + 2 * rows * tile)
         ),
@@ -391,16 +398,26 @@
 
 
 def finish_kernel(half, live, own_ref, last_ref, *refs):
-    out_ref = refs[-1]
-    count, cols = out_ref.shape
-    step = pl.program_id(0)
-    start = pl.multiple_of(step * count, count)
+    out_ref, held, sems = refs[-3:]
+    rows, cols = held.shape
+    count = rows // live.shape[0]
     columns = slice(half * cols, (half + 1) * cols)
-    for rows in chunks(count):
-        here = pl.ds(start + rows.start, rows.stop - rows.start)
-        total = own_ref[here, columns] + last_ref[here, :].astype(jnp.float32)
-        row = rows.start + lax.broadcasted_iota(jnp.int32, total.shape, 0)
-        out_ref[rows, :] = jnp.where(row < live[step], total, 0.0).astype(out_ref.dtype)
+    part = rows // sems.shape[0]
+    copies = []
+    for at in range(sems.shape[0]):
+        for chunk in chunks(part):
+            here = slice(at * part + chunk.start, at * part + chunk.stop)
+            total = own_ref[here, columns] + last_ref[here, :].astype(jnp.float32)
+            row = here.start % count + lax.broadcasted_iota(jnp.int32, total.shape, 0)
+            alive = row < live[here.start // count]
+            held[here, :] = jnp.where(alive, total, 0.0).astype(held.dtype)
+        rows_at = pl.ds(at * part, part)
+        copies.append(
+            pltpu.make_async_copy(held.at[rows_at], out_ref.at[rows_at, columns], sems.at[at])
+        )
+        copies[-1].start()
+    for copy in copies:
+        copy.wait()
 
 
 def finish(live, half, own, last, result):
@@ -417,9 +434,13 @@
         functools.partial(finish_kernel, half),
         grid_spec=pltpu.PrefetchScalarGridSpec(
             num_scalar_prefetch=1,
-            grid=(steps,),
+            grid=(1,),
             in_specs=in_specs,
-            out_specs=pl.BlockSpec((rows // steps, cols // 2), lambda s, l: (s, half)),
+            out_specs=ANYWHERE,
+            scratch_shapes=[
+                pltpu.VMEM((rows, cols // 2), jnp.bfloat16),
+                pltpu.SemaphoreType.DMA((2 * steps,)),
+            ],
         ),
         out_shape=jax.ShapeDtypeStruct((rows, cols), jnp.bfloat16),
         input_output_aliases=aliases,
@@ -472,10 +493,9 @@
     ids_there = lax.ppermute(block_adapter_ids, "inst", SWAP).reshape(-1)
     last = None
     for piece in range(tiling(dests, output_weight)[2]):
-        both = first_pieces(dests, far % size, piece, x, output_weight, last)
+        *both, last = first_pieces(dests, far % size, piece, x, output_weight, last)
         for (half, sign, moves), part in zip(pairs[0], both):
             arrived.setdefault((half, sign), []).append(lax.ppermute(part, "tp", moves))
-        last = both[1]
     pages = adapter_page_table[jnp.concatenate([ids, ids_there])]
     places = pages % resident
     index, index_there = places[: ids.shape[0]], places[ids.shape[0] :]

time: 136 us -> 134 us (0.985)
  starting transfers between devices: 24 us -> 22.3 us
    ppermute x4, starting transfers between devices: 5.65 us -> 4.07 us  [over(): return lax.ppermute(value, 'tp', [(i, i ^ apart) for i in range(size)])]
  transfers between devices with their start and end apart: 23 -> 23, of which waited for: 9 -> 8; matrix products, arithmetic and copies ran while one was open for 4% -> 4% of each run, Pallas kernels for 46% -> 48%
where the time goes in v12:
time: 134 us
  Pallas kernels  65.5 us (49%)
  waiting for transfers between devices  39.3 us (29%)
  starting transfers between devices  22.3 us (17%)
  local copies, waits for them, and re-layouts  3.34 us (2%)
  other arithmetic  2.68 us (2%)
    pallas_call x12, Pallas kernels, hop(): pl.pallas_call(functools.partial(hop_kernel, tuple(range(len(received))))...  33.6 us
    ppermute x4, waiting for transfers between devices, over(): return lax.ppermute(value, 'tp', [(i, i ^ apart) for i in range(size)])  22.8 us
    ppermute x12, waiting for transfers between devices, turn(): arrived[half, sign] = [lax.ppermute(last, 'tp', moves)]  14.5 us
    ppermute x12, starting transfers between devices, turn(): arrived[half, sign] = [lax.ppermute(last, 'tp', moves)]  13 us
    pallas_call x2, Pallas kernels, first_pieces(): pl.pallas_call(functools.partial(first_kernel, after is not None), grid_s...  8.09 us
    pallas_call x1, Pallas kernels, own_terms(): pl.pallas_call(own_kernel, grid_spec=pltpu.PrefetchScalarGridSpec(num_sca...  7.9 us
    pallas_call x1, Pallas kernels, low_rank(): pl.pallas_call(functools.partial(low_kernel, sizes), grid_spec=pltpu.Pref...  6.51 us
    pallas_call x2, Pallas kernels, collect(): pl.pallas_call(functools.partial(collect_kernel, count), grid_spec=pltpu....  5.34 us
  transfers between devices with their start and end apart: 23, of which 8 were waited for; matrix products, arithmetic and copies ran while one was open for 4% of the time, Pallas kernels for 48%

profile of v12, /device:TPU:0, one launch (start us, length us, event | category | flops | bytes accessed | tf_op | source)
XLA Modules:
  0.0 133.5 jit_solution(13389748471351638533)
XLA Ops:
  1.0 4.5 %shard_map.82 = (bf16[768,256]{1,0:T(8,128)(2,1)}, bf16[768,256]{1,0:T(8,128)(2,1)}, f32[8,128]{1,0:T(8,128)}) custom-call(s32[8]{0:T(128)} %compare_select_fusion.3.dests, bf16[768,1024]{1,0:T(8,128)(2,1)} %bitcast.11, bf16[1024,8192]{1,0:T(8,128)(2,1)} %w_ref.29), custom_call_target="tpu_custom_call" | custom-call | flops 24159191040 | bytes 3407872 | tf_op jit(solution)/shard_map/pallas_call | solution.py:126
  5.5 2.6 %collective-permute-start.1 = (bf16[768,256]{1,0:T(8,128)(2,1)}, bf16[768,256]{1,0:T(8,128)(2,1)S(1)}, u32[]{:S(2)}, u32[]{:S(2)}) collective-permute-start(bf16[768,256]{1,0:T(8,128)(2,1)} %get-tuple-element.17), channel_id=1, source_target_pairs={{0,2},{2,4},{4,6},{6,7},{7,5},{5,3},{3,1},{1,0},{8,10},{10,12},{12... | collective-permute-start | bytes 1179656 | tf_op jit(solution)/shard_map/ppermute | solution.py:498
  8.8 3.6 %shard_map.83 = (bf16[768,256]{1,0:T(8,128)(2,1)}, bf16[768,256]{1,0:T(8,128)(2,1)S(1)}, f32[8,128]{1,0:T(8,128)S(1)}) custom-call(s32[8]{0:T(128)S(1)} %copy-done.8, bf16[768,1024]{1,0:T(8,128)(2,1)S(1)} %bitcast.12, bf16[1024,8192]{1,0:T(8,128)(2,1)} %w_ref.29, f32[8,128]{1,0:T(8,128)S(1)} %copy-done.11), custom_call_target="tpu_custom_call" | custom-call | flops 24159191040 | bytes 3407872 | tf_op jit(solution)/shard_map/pallas_call | solution.py:126
  15.6 2.7 %shard_map.84.refs_0_ = bf16[24,64,1024]{2,1,0:T(8,128)(2,1)S(1)} custom-call(s32[24]{0:T(128)S(1)} %get-tuple-element.25.index, bf16[96,64,1024]{2,1,0:T(8,128)(2,1)} %table_ref.6, f32[8,128]{1,0:T(8,128)S(1)} %get-tuple-element.16.after_ref), custom_call_target="tpu_custom_call" | custom-call | bytes 6291456 | tf_op jit(solution)/shard_map/pallas_call | solution.py:175
  20.3 2.8 %shard_map.86.refs_0_ = bf16[768,512]{1,0:T(8,128)(2,1)S(1)} custom-call(s32[8]{0:T(128)S(1)} %copy-done.8, bf16[768,1024]{1,0:T(8,128)(2,1)S(1)} %bitcast.13, bf16[1024,8192]{1,0:T(8,128)(2,1)} %w_ref.29, f32[8,128]{1,0:T(8,128)S(1)} %shard_map.85.refs_0_), custom_call_target="tpu_custom_call" | custom-call | flops 24159191040 | bytes 4194304 | tf_op jit(solution)/shard_map/pallas_call | solution.py:81
  23.0 2.8 %shard_map.87.after_ref = bf16[768,512]{1,0:T(8,128)(2,1)S(1)} custom-call(s32[8]{0:T(128)S(1)} %copy-done.8, bf16[768,1024]{1,0:T(8,128)(2,1)S(1)} %bitcast.14, bf16[1024,8192]{1,0:T(8,128)(2,1)} %w_ref.29, bf16[768,512]{1,0:T(8,128)(2,1)S(1)} %shard_map.86.refs_0_), custom_call_target="tpu_custom_call" | custom-call | flops 24159191040 | bytes 4194304 | tf_op jit(solution)/shard_map/pallas_call | solution.py:81
  27.9 2.7 %shard_map.88.refs_2_ = bf16[24,64,1024]{2,1,0:T(8,128)(2,1)S(1)} custom-call(s32[24]{0:T(128)S(1)} %get-tuple-element.25.index, bf16[96,64,1024]{2,1,0:T(8,128)(2,1)} %table_ref.7, bf16[768,512]{1,0:T(8,128)(2,1)S(1)} %shard_map.87.after_ref), custom_call_target="tpu_custom_call" | custom-call | bytes 6291456 | tf_op jit(solution)/shard_map/pallas_call | solution.py:175
  30.7 3.0 %shard_map.89.refs_1_ = bf16[768,512]{1,0:T(8,128)(2,1)S(1)} custom-call(s32[8]{0:T(128)S(1)} %copy-done.8, bf16[768,1024]{1,0:T(8,128)(2,1)S(1)} %bitcast.15, bf16[1024,8192]{1,0:T(8,128)(2,1)} %w_ref.29, bf16[768,256]{1,0:T(8,128)(2,1)S(1)} %collective-permute-done.1.refs_1_.refs_0_, bf16[768,256]{1,0:T(8,128)(2,1)} %collective-permute-done.8.refs_1_, ...), custom_call_target="tpu_custom_call" | custom-call | flops 24159191040 | bytes 4194304 | tf_op jit(solution)/shard_map/pallas_call | solution.py:81
  35.3 2.9 %shard_map.91.after_ref = bf16[768,512]{1,0:T(8,128)(2,1)S(1)} custom-call(s32[8]{0:T(128)S(1)} %copy-done.8, bf16[768,1024]{1,0:T(8,128)(2,1)S(1)} %bitcast.16, bf16[1024,8192]{1,0:T(8,128)(2,1)} %w_ref.29, bf16[768,256]{1,0:T(8,128)(2,1)S(1)} %collective-permute-done.2.refs_2_.refs_0_, bf16[768,256]{1,0:T(8,128)(2,1)S(1)} %collective-permute-done.7.refs_1_, ...), custom_call_target="tpu_custom_call" | custom-call | flops 24159191040 | bytes 4194304 | tf_op jit(solution)/shard_map/pallas_call | solution.py:81
  38.8 6.5 %shard_map.92 = (f32[64,384]{1,0:T(8,128)S(1)}, f32[64,384]{1,0:T(8,128)S(1)}) custom-call(s32[24]{0:T(128)S(1)} %compare_convert_fusion.local, s32[24]{0:T(128)S(1)} %get-tuple-element.26.index, s32[1]{0:T(128)} %bitcast.1.side, bf16[768,1024]{1,0:T(8,128)(2,1)S(1)} %bitcast.17, s32[3,256]{1,0:T(4,128)S(1)} %copy-done.6, bf16[96,64,1024]{2,1,0:T(8,128)(2,1)} %table_ref.6, ...), custom_call_target="tpu_custom_call" | custom-call | flops 12079595520 | bytes 4718592 | tf_op jit(solution)/shard_map/pallas_call | solution.py:246
  46.3 2.8 %shard_map.94.refs_1_ = bf16[768,512]{1,0:T(8,128)(2,1)S(1)} custom-call(s32[8]{0:T(128)S(1)} %copy-done.8, bf16[768,1024]{1,0:T(8,128)(2,1)S(1)} %bitcast.18, bf16[1024,8192]{1,0:T(8,128)(2,1)} %w_ref.29, bf16[768,512]{1,0:T(8,128)(2,1)S(1)} %collective-permute-done.5.refs_0_, f32[8,128]{1,0:T(8,128)S(1)} %shard_map.93.refs_1_), custom_call_target="tpu_custom_call" | custom-call | flops 24159191040 | bytes 4194304 | tf_op jit(solution)/shard_map/pallas_call | solution.py:81
  50.8 2.8 %shard_map.95.after_ref = bf16[768,512]{1,0:T(8,128)(2,1)S(1)} custom-call(s32[8]{0:T(128)S(1)} %copy-done.8, bf16[768,1024]{1,0:T(8,128)(2,1)S(1)} %bitcast.19, bf16[1024,8192]{1,0:T(8,128)(2,1)} %w_ref.29, bf16[768,512]{1,0:T(8,128)(2,1)S(1)} %collective-permute-done.4.refs_0_, bf16[768,512]{1,0:T(8,128)(2,1)S(1)} %shard_map.94.refs_1_), custom_call_target="tpu_custom_call" | custom-call | flops 24159191040 | bytes 4194304 | tf_op jit(solution)/shard_map/pallas_call | solution.py:81
  54.0 7.9 %shard_map.96 = (f32[768,1024]{1,0:T(8,128)S(1)}, bf16[24,64,1024]{2,1,0:T(8,128)(2,1)S(1)}) custom-call(s32[24]{0:T(128)S(1)} %compare_convert_fusion.local, s32[24]{0:T(128)S(1)} %get-tuple-element.26.index, s32[8]{0:T(128)S(1)} %copy-done.8, bf16[768,1024]{1,0:T(8,128)(2,1)S(1)} %bitcast.20, bf16[1024,8192]{1,0:T(8,128)(2,1)} %w_ref.29, ...), custom_call_target="tpu_custom_call" | custom-call | flops 48318382080 | bytes 13107200 | tf_op jit(solution)/shard_map/pallas_call | solution.py:305
  66.2 2.8 %shard_map.99.refs_1_ = bf16[768,512]{1,0:T(8,128)(2,1)S(1)} custom-call(s32[8]{0:T(128)S(1)} %copy-done.8, bf16[768,1024]{1,0:T(8,128)(2,1)S(1)} %bitcast.21, bf16[1024,8192]{1,0:T(8,128)(2,1)} %w_ref.29, bf16[768,512]{1,0:T(8,128)(2,1)S(1)} %collective-permute-done.12.refs_0_, f32[64,384]{1,0:T(8,128)S(1)} %shard_map.98.refs_1_.low_ref), custom_call_target="tpu_custom_call" | custom-call | flops 24159191040 | bytes 4194304 | tf_op jit(solution)/shard_map/pallas_call | solution.py:81
  69.9 2.8 %shard_map.100.refs_0_.after_ref = bf16[768,512]{1,0:T(8,128)(2,1)S(1)} custom-call(s32[8]{0:T(128)S(1)} %copy-done.8, bf16[768,1024]{1,0:T(8,128)(2,1)S(1)} %bitcast.22, bf16[1024,8192]{1,0:T(8,128)(2,1)} %w_ref.29, bf16[768,512]{1,0:T(8,128)(2,1)S(1)} %collective-permute-done.11.refs_0_, bf16[768,512]{1,0:T(8,128)(2,1)S(1)} %shard_map.99.refs_1_), custom_call_target="tpu_custom_call" | custom-call | flops 24159191040 | bytes 4194304 | tf_op jit(solution)/shard_map/pallas_call | solution.py:81
  74.5 8.2 %collective-permute-done.10 = f16[64,384]{1,0:T(8,128)(2,1)S(1)} collective-permute-done((f16[64,384]{1,0:T(8,128)(2,1)S(1)}, f16[64,384]{1,0:T(8,128)(2,1)S(1)}, u32[]{:S(2)}, u32[]{:S(2)}) %collective-permute-start.10) | collective-permute-done | bytes 49184 | tf_op jit(solution)/shard_map/ppermute | solution.py:517
  83.4 2.6 %collective-permute-start.13 = (f16[64,384]{1,0:T(8,128)(2,1)S(1)}, f16[64,384]{1,0:T(8,128)(2,1)S(1)}, u32[]{:S(2)}, u32[]{:S(2)}) collective-permute-start(f16[64,384]{1,0:T(8,128)(2,1)S(1)} %multiply_convert_fusion), channel_id=1, source_target_pairs={{0,4},{1,5},{2,6},{3,7},{4,0},{5,1},{6,2},{7,3},{8,12},{9,13},{10,... | collective-permute-start | bytes 147464 | tf_op jit(solution)/shard_map/ppermute | solution.py:517
  86.0 2.8 %shard_map.103.refs_1_ = bf16[768,512]{1,0:T(8,128)(2,1)S(1)} custom-call(s32[8]{0:T(128)S(1)} %copy-done.8, bf16[768,1024]{1,0:T(8,128)(2,1)S(1)} %bitcast.23, bf16[1024,8192]{1,0:T(8,128)(2,1)} %w_ref.29, bf16[768,512]{1,0:T(8,128)(2,1)S(1)} %collective-permute-done.15.refs_0_, f32[64,384]{1,0:T(8,128)S(1)} %shard_map.102.refs_1_.low_ref), custom_call_target="tpu_custom_call" | custom-call | flops 24159191040 | bytes 4194304 | tf_op jit(solution)/shard_map/pallas_call | solution.py:81
  88.8 2.8 %shard_map.104.refs_0_.after_ref = bf16[768,512]{1,0:T(8,128)(2,1)S(1)} custom-call(s32[8]{0:T(128)S(1)} %copy-done.8, bf16[768,1024]{1,0:T(8,128)(2,1)S(1)} %bitcast.24, bf16[1024,8192]{1,0:T(8,128)(2,1)} %w_ref.29, bf16[768,512]{1,0:T(8,128)(2,1)S(1)} %collective-permute-done.14.refs_0_, bf16[768,512]{1,0:T(8,128)(2,1)S(1)} %shard_map.103.refs_1_), custom_call_target="tpu_custom_call" | custom-call | flops 24159191040 | bytes 4194304 | tf_op jit(solution)/shard_map/pallas_call | solution.py:81
  94.2 6.9 %collective-permute-done.13 = f16[64,384]{1,0:T(8,128)(2,1)S(1)} collective-permute-done((f16[64,384]{1,0:T(8,128)(2,1)S(1)}, f16[64,384]{1,0:T(8,128)(2,1)S(1)}, u32[]{:S(2)}, u32[]{:S(2)}) %collective-permute-start.13) | collective-permute-done | bytes 49184 | tf_op jit(solution)/shard_map/ppermute | solution.py:517
  101.9 2.8 %shard_map.107.refs_1_ = bf16[768,512]{1,0:T(8,128)(2,1)S(1)} custom-call(s32[8]{0:T(128)S(1)} %copy-done.8, bf16[768,1024]{1,0:T(8,128)(2,1)S(1)} %bitcast.25, bf16[1024,8192]{1,0:T(8,128)(2,1)} %w_ref.29, bf16[768,512]{1,0:T(8,128)(2,1)S(1)} %collective-permute-done.18.refs_0_, bf16[64,384]{1,0:T(8,128)(2,1)S(1)} %shard_map.106.refs_1_.low_ref), custom_call_target="tpu_custom_call" | custom-call | flops 24159191040 | bytes 4194304 | tf_op jit(solution)/shard_map/pallas_call | solution.py:81
  106.8 2.8 %shard_map.108.after_ref = bf16[768,512]{1,0:T(8,128)(2,1)S(1)} custom-call(s32[8]{0:T(128)S(1)} %copy-done.8, bf16[768,1024]{1,0:T(8,128)(2,1)S(1)} %bitcast.26, bf16[1024,8192]{1,0:T(8,128)(2,1)} %w_ref.29, bf16[768,512]{1,0:T(8,128)(2,1)S(1)} %collective-permute-done.17.refs_0_, bf16[768,512]{1,0:T(8,128)(2,1)S(1)} %shard_map.107.refs_1_), custom_call_target="tpu_custom_call" | custom-call | flops 24159191040 | bytes 4194304 | tf_op jit(solution)/shard_map/pallas_call | solution.py:81
  109.9 5.9 %collective-permute-done.16.other_ref = bf16[64,384]{1,0:T(8,128)(2,1)S(1)} collective-permute-done((bf16[64,384]{1,0:T(8,128)(2,1)S(1)}, bf16[64,384]{1,0:T(8,128)(2,1)S(1)}, u32[]{:S(2)}, u32[]{:S(2)}) %collective-permute-start.16) | collective-permute-done | bytes 49184 | tf_op jit(solution)/shard_map/ppermute | solution.py:517
  117.8 12.7 %collective-permute-done.22.last_ref = bf16[768,512]{1,0:T(8,128)(2,1)S(1)} collective-permute-done((bf16[768,512]{1,0:T(8,128)(2,1)S(1)}, bf16[768,512]{1,0:T(8,128)(2,1)S(1)}, u32[]{:S(2)}, u32[]{:S(2)}) %collective-permute-start.22) | collective-permute-done | bytes 786464 | tf_op jit(solution)/shard_map/ppermute | solution.py:487
  (97 shorter events, 32.6 us)
Async XLA Ops:
  0.0 14.7 %copy-start = (s32[192]{0:T(256)S(1)}, s32[192]{0:T(256)}, u32[]{:S(2)}) copy-start(s32[192]{0:T(256)} %param.12) | copy-start | bytes 2308
  0.0 14.5 %collective-permute-start = (s32[3,2,4]{2,1,0:T(2,128)}, s32[3,2,4]{2,1,0:T(2,128)S(1)}, u32[]{:S(2)}, u32[]{:S(2)}) collective-permute-start(s32[3,2,4]{2,1,0:T(2,128)} %param.13), channel_id=1, source_target_pairs={{0,8},{8,0},{1,9},{9,1},{2,10},{10,2},{3,11},{11,3},{4,12},{12,4},... | collective-permute-start | bytes 296 | tf_op jit(solution)/shard_map/ppermute | solution.py:493
  5.5 12.8 %collective-permute-start.1 = (bf16[768,256]{1,0:T(8,128)(2,1)}, bf16[768,256]{1,0:T(8,128)(2,1)S(1)}, u32[]{:S(2)}, u32[]{:S(2)}) collective-permute-start(bf16[768,256]{1,0:T(8,128)(2,1)} %get-tuple-element.17), channel_id=1, source_target_pairs={{0,2},{2,4},{4,6},{6,7},{7,5},{5,3},{3,1},{1,0},{8,10},{10,12},{12... | collective-permute-start | bytes 1179656 | tf_op jit(solution)/shard_map/ppermute | solution.py:498
  8.1 12.2 %collective-permute-start.2 = (bf16[768,256]{1,0:T(8,128)(2,1)}, bf16[768,256]{1,0:T(8,128)(2,1)S(1)}, u32[]{:S(2)}, u32[]{:S(2)}) collective-permute-start(bf16[768,256]{1,0:T(8,128)(2,1)} %get-tuple-element.18), channel_id=1, source_target_pairs={{0,1},{2,0},{4,2},{6,4},{7,6},{5,7},{3,5},{1,3},{8,9},{10,8},{12,1... | collective-permute-start | bytes 1179656 | tf_op jit(solution)/shard_map/ppermute | solution.py:498
  12.4 18.2 %collective-permute-start.8 = (bf16[768,256]{1,0:T(8,128)(2,1)}, bf16[768,256]{1,0:T(8,128)(2,1)}, u32[]{:S(2)}, u32[]{:S(2)}) collective-permute-start(bf16[768,256]{1,0:T(8,128)(2,1)} %get-tuple-element.20), channel_id=1, source_target_pairs={{0,2},{2,4},{4,6},{6,7},{7,5},{5,3},{3,1},{1,0},{8,10},{10,12},{12... | collective-permute-start | bytes 1179656 | tf_op jit(solution)/shard_map/ppermute | solution.py:498
  14.4 20.9 %collective-permute-start.7 = (bf16[768,256]{1,0:T(8,128)(2,1)S(1)}, bf16[768,256]{1,0:T(8,128)(2,1)S(1)}, u32[]{:S(2)}, u32[]{:S(2)}) collective-permute-start(bf16[768,256]{1,0:T(8,128)(2,1)S(1)} %get-tuple-element.19), channel_id=1, source_target_pairs={{0,1},{2,0},{4,2},{6,4},{7,6},{5,7},{3,5},{1,3},{8,9},{10,8},{12,1... | collective-permute-start | bytes 1179656 | tf_op jit(solution)/shard_map/ppermute | solution.py:498
  18.2 15.5 %collective-permute-start.6 = (bf16[24,64,1024]{2,1,0:T(8,128)(2,1)S(1)}, bf16[24,64,1024]{2,1,0:T(8,128)(2,1)S(1)}, u32[]{:S(2)}, u32[]{:S(2)}) collective-permute-start(bf16[24,64,1024]{2,1,0:T(8,128)(2,1)S(1)} %shard_map.84.refs_0_), channel_id=1, source_target_pairs={{0,8},{8,0},{1,9},{9,1},{2,10},{10,2},{3,11},{11,3},{4,12},{12,4},... | collective-permute-start | bytes 9437192 | tf_op jit(solution)/shard_map/ppermute | solution.py:504
  25.8 20.5 %collective-permute-start.5 = (bf16[768,512]{1,0:T(8,128)(2,1)S(1)}, bf16[768,512]{1,0:T(8,128)(2,1)S(1)}, u32[]{:S(2)}, u32[]{:S(2)}) collective-permute-start(bf16[768,512]{1,0:T(8,128)(2,1)S(1)} %shard_map.86.refs_0_), channel_id=1, source_target_pairs={{0,2},{2,4},{4,6},{6,7},{7,5},{5,3},{3,1},{1,0},{8,10},{10,12},{12... | collective-permute-start | bytes 2359304 | tf_op jit(solution)/shard_map/ppermute | solution.py:487
  27.4 23.3 %collective-permute-start.4 = (bf16[768,512]{1,0:T(8,128)(2,1)S(1)}, bf16[768,512]{1,0:T(8,128)(2,1)S(1)}, u32[]{:S(2)}, u32[]{:S(2)}) collective-permute-start(bf16[768,512]{1,0:T(8,128)(2,1)S(1)} %shard_map.87.after_ref), channel_id=1, source_target_pairs={{0,1},{2,0},{4,2},{6,4},{7,6},{5,7},{3,5},{1,3},{8,9},{10,8},{12,1... | collective-permute-start | bytes 2359304 | tf_op jit(solution)/shard_map/ppermute | solution.py:487
  30.6 14.7 %collective-permute-start.3 = (bf16[24,64,1024]{2,1,0:T(8,128)(2,1)S(1)}, bf16[24,64,1024]{2,1,0:T(8,128)(2,1)S(1)}, u32[]{:S(2)}, u32[]{:S(2)}) collective-permute-start(bf16[24,64,1024]{2,1,0:T(8,128)(2,1)S(1)} %shard_map.88.refs_2_), channel_id=1, source_target_pairs={{0,8},{8,0},{1,9},{9,1},{2,10},{10,2},{3,11},{11,3},{4,12},{12,4},... | collective-permute-start | bytes 9437192 | tf_op jit(solution)/shard_map/ppermute | solution.py:508
  33.7 32.5 %collective-permute-start.12 = (bf16[768,512]{1,0:T(8,128)(2,1)S(1)}, bf16[768,512]{1,0:T(8,128)(2,1)S(1)}, u32[]{:S(2)}, u32[]{:S(2)}) collective-permute-start(bf16[768,512]{1,0:T(8,128)(2,1)S(1)} %shard_map.89.refs_1_), channel_id=1, source_target_pairs={{0,2},{2,4},{4,6},{6,7},{7,5},{5,3},{3,1},{1,0},{8,10},{10,12},{12... | collective-permute-start | bytes 2359304 | tf_op jit(solution)/shard_map/ppermute | solution.py:487
  38.3 31.6 %collective-permute-start.11 = (bf16[768,512]{1,0:T(8,128)(2,1)S(1)}, bf16[768,512]{1,0:T(8,128)(2,1)S(1)}, u32[]{:S(2)}, u32[]{:S(2)}) collective-permute-start(bf16[768,512]{1,0:T(8,128)(2,1)S(1)} %shard_map.91.after_ref), channel_id=1, source_target_pairs={{0,1},{2,0},{4,2},{6,4},{7,6},{5,7},{3,5},{1,3},{8,9},{10,8},{12,1... | collective-permute-start | bytes 2359304 | tf_op jit(solution)/shard_map/ppermute | solution.py:487
  45.3 18.9 %collective-permute-start.9 = (f16[64,384]{1,0:T(8,128)(2,1)S(1)}, f16[64,384]{1,0:T(8,128)(2,1)S(1)}, u32[]{:S(2)}, u32[]{:S(2)}) collective-permute-start(f16[64,384]{1,0:T(8,128)(2,1)S(1)} %multiply_convert_fusion.2), channel_id=1, source_target_pairs={{0,1},{1,0},{2,3},{3,2},{4,5},{5,4},{6,7},{7,6},{8,9},{9,8},{10,11... | collective-permute-start | bytes 147464 | tf_op jit(solution)/shard_map/ppermute | solution.py:517
  49.1 36.9 %collective-permute-start.15 = (bf16[768,512]{1,0:T(8,128)(2,1)S(1)}, bf16[768,512]{1,0:T(8,128)(2,1)S(1)}, u32[]{:S(2)}, u32[]{:S(2)}) collective-permute-start(bf16[768,512]{1,0:T(8,128)(2,1)S(1)} %shard_map.94.refs_1_), channel_id=1, source_target_pairs={{0,2},{2,4},{4,6},{6,7},{7,5},{5,3},{3,1},{1,0},{8,10},{10,12},{12... | collective-permute-start | bytes 2359304 | tf_op jit(solution)/shard_map/ppermute | solution.py:487
  53.5 35.2 %collective-permute-start.14 = (bf16[768,512]{1,0:T(8,128)(2,1)S(1)}, bf16[768,512]{1,0:T(8,128)(2,1)S(1)}, u32[]{:S(2)}, u32[]{:S(2)}) collective-permute-start(bf16[768,512]{1,0:T(8,128)(2,1)S(1)} %shard_map.95.after_ref), channel_id=1, source_target_pairs={{0,1},{2,0},{4,2},{6,4},{7,6},{5,7},{3,5},{1,3},{8,9},{10,8},{12,1... | collective-permute-start | bytes 2359304 | tf_op jit(solution)/shard_map/ppermute | solution.py:487
  65.0 17.7 %collective-permute-start.10 = (f16[64,384]{1,0:T(8,128)(2,1)S(1)}, f16[64,384]{1,0:T(8,128)(2,1)S(1)}, u32[]{:S(2)}, u32[]{:S(2)}) collective-permute-start(f16[64,384]{1,0:T(8,128)(2,1)S(1)} %multiply_convert_fusion.1), channel_id=1, source_target_pairs={{0,2},{1,3},{2,0},{3,1},{4,6},{5,7},{6,4},{7,5},{8,10},{9,11},{10,... | collective-permute-start | bytes 147464 | tf_op jit(solution)/shard_map/ppermute | solution.py:517
  69.0 32.8 %collective-permute-start.18 = (bf16[768,512]{1,0:T(8,128)(2,1)S(1)}, bf16[768,512]{1,0:T(8,128)(2,1)S(1)}, u32[]{:S(2)}, u32[]{:S(2)}) collective-permute-start(bf16[768,512]{1,0:T(8,128)(2,1)S(1)} %shard_map.99.refs_1_), channel_id=1, source_target_pairs={{0,2},{2,4},{4,6},{6,7},{7,5},{5,3},{3,1},{1,0},{8,10},{10,12},{12... | collective-permute-start | bytes 2359304 | tf_op jit(solution)/shard_map/ppermute | solution.py:487
  72.7 34.1 %collective-permute-start.17 = (bf16[768,512]{1,0:T(8,128)(2,1)S(1)}, bf16[768,512]{1,0:T(8,128)(2,1)S(1)}, u32[]{:S(2)}, u32[]{:S(2)}) collective-permute-start(bf16[768,512]{1,0:T(8,128)(2,1)S(1)} %shard_map.100.refs_0_.after_ref), channel_id=1, source_target_pairs={{0,1},{2,0},{4,2},{6,4},{7,6},{5,7},{3,5},{1,3},{8,9},{10,8},{12,1... | collective-permute-start | bytes 2359304 | tf_op jit(solution)/shard_map/ppermute | solution.py:487
  83.4 17.7 %collective-permute-start.13 = (f16[64,384]{1,0:T(8,128)(2,1)S(1)}, f16[64,384]{1,0:T(8,128)(2,1)S(1)}, u32[]{:S(2)}, u32[]{:S(2)}) collective-permute-start(f16[64,384]{1,0:T(8,128)(2,1)S(1)} %multiply_convert_fusion), channel_id=1, source_target_pairs={{0,4},{1,5},{2,6},{3,7},{4,0},{5,1},{6,2},{7,3},{8,12},{9,13},{10,... | collective-permute-start | bytes 147464 | tf_op jit(solution)/shard_map/ppermute | solution.py:517
  91.6 25.9 %collective-permute-start.19 = (bf16[768,512]{1,0:T(8,128)(2,1)S(1)}, bf16[768,512]{1,0:T(8,128)(2,1)S(1)}, u32[]{:S(2)}, u32[]{:S(2)}) collective-permute-start(bf16[768,512]{1,0:T(8,128)(2,1)S(1)} %shard_map.104.refs_0_.after_ref), channel_id=1, source_target_pairs={{0,1},{2,0},{4,2},{6,4},{7,6},{5,7},{3,5},{1,3},{8,9},{10,8},{12,1... | collective-permute-start | bytes 2359304 | tf_op jit(solution)/shard_map/ppermute | solution.py:487
  91.6 25.8 %collective-permute-start.20 = (bf16[768,512]{1,0:T(8,128)(2,1)S(1)}, bf16[768,512]{1,0:T(8,128)(2,1)S(1)}, u32[]{:S(2)}, u32[]{:S(2)}) collective-permute-start(bf16[768,512]{1,0:T(8,128)(2,1)S(1)} %shard_map.103.refs_1_), channel_id=1, source_target_pairs={{0,2},{2,4},{4,6},{6,7},{7,5},{5,3},{3,1},{1,0},{8,10},{10,12},{12... | collective-permute-start | bytes 2359304 | tf_op jit(solution)/shard_map/ppermute | solution.py:487
  101.8 14.1 %collective-permute-start.16 = (bf16[64,384]{1,0:T(8,128)(2,1)S(1)}, bf16[64,384]{1,0:T(8,128)(2,1)S(1)}, u32[]{:S(2)}, u32[]{:S(2)}) collective-permute-start(bf16[64,384]{1,0:T(8,128)(2,1)S(1)} %shard_map.106.refs_1_.low_ref), channel_id=1, source_target_pairs={{0,1},{1,0},{2,3},{3,2},{4,5},{5,4},{6,7},{7,6},{8,9},{9,8},{10,11... | collective-permute-start | bytes 147464 | tf_op jit(solution)/shard_map/ppermute | solution.py:517
  104.7 25.8 %collective-permute-start.22 = (bf16[768,512]{1,0:T(8,128)(2,1)S(1)}, bf16[768,512]{1,0:T(8,128)(2,1)S(1)}, u32[]{:S(2)}, u32[]{:S(2)}) collective-permute-start(bf16[768,512]{1,0:T(8,128)(2,1)S(1)} %shard_map.107.refs_1_), channel_id=1, source_target_pairs={{0,2},{2,4},{4,6},{6,7},{7,5},{5,3},{3,1},{1,0},{8,10},{10,12},{12... | collective-permute-start | bytes 2359304 | tf_op jit(solution)/shard_map/ppermute | solution.py:487
  109.5 22.5 %collective-permute-start.21 = (bf16[768,512]{1,0:T(8,128)(2,1)S(1)}, bf16[768,512]{1,0:T(8,128)(2,1)S(1)}, u32[]{:S(2)}, u32[]{:S(2)}) collective-permute-start(bf16[768,512]{1,0:T(8,128)(2,1)S(1)} %shard_map.108.after_ref), channel_id=1, source_target_pairs={{0,1},{2,0},{4,2},{6,4},{7,6},{5,7},{3,5},{1,3},{8,9},{10,8},{12,1... | collective-permute-start | bytes 2359304 | tf_op jit(solution)/shard_map/ppermute | solution.py:487
  (12 other events, 80.6 us)

commit v13 on v12

--- a/solution.py
+++ b/solution.py
@@ -504,26 +504,26 @@
     got_down = lax.ppermute(last, "inst", SWAP)
     last = touch(last, *(arrived[half, sign][0] for half, sign, _ in pairs[0]))
     last = turn(1, last)
-    last = collect(index_there, adapter_up_weight, last)
-    got_up = lax.ppermute(last, "inst", SWAP)
-    last = turn(2, last, got_down)
     side = (lax.axis_index("tp") & 1).reshape(1)
     low, give = low_rank(
         sizes, local, index, side, x, row_list_position, adapter_down_weight, got_down, last
     )
-    last = touch(got_up, low)
+    last = low
 
     def over(value, apart):
         return lax.ppermute(value, "tp", [(i, i ^ apart) for i in range(size)])
 
-    number, turns = 3, 2 * far - 1
+    number, turns = 2, 2 * far - 1
     apart = 1
     while apart < size:
         sent = over(((give if apart == 1 else low) * LOW_SCALE).astype(jnp.float16), apart)
         until = turns - 1 if 2 * apart == size else number + 1
         while number < min(until, turns - 1):
             last = turn(number, last)
-            if number == 3:
+            if number == 4:
+                last = collect(index_there, adapter_up_weight, last)
+                got_up = lax.ppermute(last, "inst", SWAP)
+            if number == 5:
                 own, up_pages = own_terms(
                     dests, local, index, x, output_weight, adapter_up_weight, got_up, last
                 )

time: 134 us -> 135 us (level)
  waiting for transfers between devices: 39.3 us -> 35.2 us
  starting transfers between devices: 22.3 us -> 25.4 us
  other arithmetic: 2.68 us -> 4.03 us
    ppermute x4, waiting for transfers between devices: 22.8 us -> 18.1 us  [over(): return lax.ppermute(value, 'tp', [(i, i ^ apart) for i in range(size)])]
    ppermute x4, starting transfers between devices: 4.07 us -> 6.61 us  [over(): return lax.ppermute(value, 'tp', [(i, i ^ apart) for i in range(size)])]
  transfers between devices with their start and end apart: 23 -> 23, of which waited for: 8 -> 6; matrix products, arithmetic and copies ran while one was open for 4% -> 5% of each run, Pallas kernels for 48% -> 47%
where the time goes in v13:
time: 135 us; the launch traced here: 134 us
  Pallas kernels  64.8 us (48%)
  waiting for transfers between devices  35.2 us (26%)
  starting transfers between devices  25.4 us (19%)
  local copies, waits for them, and re-layouts  4.43 us (3%)
  other arithmetic  4.03 us (3%)
    pallas_call x12, Pallas kernels, hop(): pl.pallas_call(functools.partial(hop_kernel, tuple(range(len(received))))...  34.5 us
    ppermute x4, waiting for transfers between devices, over(): return lax.ppermute(value, 'tp', [(i, i ^ apart) for i in range(size)])  18.1 us
    ppermute x12, waiting for transfers between devices, turn(): arrived[half, sign] = [lax.ppermute(last, 'tp', moves)]  15.2 us
    ppermute x12, starting transfers between devices, turn(): arrived[half, sign] = [lax.ppermute(last, 'tp', moves)]  13.6 us
    pallas_call x2, Pallas kernels, first_pieces(): pl.pallas_call(functools.partial(first_kernel, after is not None), grid_s...  8.1 us
    pallas_call x1, Pallas kernels, own_terms(): pl.pallas_call(own_kernel, grid_spec=pltpu.PrefetchScalarGridSpec(num_sca...  7.06 us
    ppermute x4, starting transfers between devices, over(): return lax.ppermute(value, 'tp', [(i, i ^ apart) for i in range(size)])  6.61 us
    pallas_call x1, Pallas kernels, low_rank(): pl.pallas_call(functools.partial(low_kernel, sizes), grid_spec=pltpu.Pref...  5.68 us
  transfers between devices with their start and end apart: 23, of which 6 were waited for; matrix products, arithmetic and copies ran while one was open for 5% of the time, Pallas kernels for 47%

profile of v13, /device:TPU:0, one launch (start us, length us, event | category | flops | bytes accessed | tf_op | source)
XLA Modules:
  0.0 134.2 jit_solution(13586462274539956198)
XLA Ops:
  1.0 4.5 %shard_map.82 = (bf16[768,256]{1,0:T(8,128)(2,1)}, bf16[768,256]{1,0:T(8,128)(2,1)}, f32[8,128]{1,0:T(8,128)}) custom-call(s32[8]{0:T(128)} %compare_select_fusion.3.dests, bf16[768,1024]{1,0:T(8,128)(2,1)} %bitcast.11, bf16[1024,8192]{1,0:T(8,128)(2,1)} %w_ref.29), custom_call_target="tpu_custom_call" | custom-call | flops 24159191040 | bytes 3407872 | tf_op jit(solution)/shard_map/pallas_call | solution.py:126
  8.8 3.6 %shard_map.83 = (bf16[768,256]{1,0:T(8,128)(2,1)}, bf16[768,256]{1,0:T(8,128)(2,1)S(1)}, f32[8,128]{1,0:T(8,128)S(1)}) custom-call(s32[8]{0:T(128)S(1)} %copy-done.12, bf16[768,1024]{1,0:T(8,128)(2,1)S(1)} %bitcast.12, bf16[1024,8192]{1,0:T(8,128)(2,1)} %w_ref.29, f32[8,128]{1,0:T(8,128)S(1)} %copy-done.15), custom_call_target="tpu_custom_call" | custom-call | flops 24159191040 | bytes 3407872 | tf_op jit(solution)/shard_map/pallas_call | solution.py:126
  15.6 2.7 %shard_map.84.refs_0_ = bf16[24,64,1024]{2,1,0:T(8,128)(2,1)S(1)} custom-call(s32[24]{0:T(128)S(1)} %get-tuple-element.25.index, bf16[96,64,1024]{2,1,0:T(8,128)(2,1)} %table_ref.5, f32[8,128]{1,0:T(8,128)S(1)} %get-tuple-element.20.after_ref), custom_call_target="tpu_custom_call" | custom-call | bytes 6291456 | tf_op jit(solution)/shard_map/pallas_call | solution.py:175
  20.2 2.8 %shard_map.86.refs_0_ = bf16[768,512]{1,0:T(8,128)(2,1)S(1)} custom-call(s32[8]{0:T(128)S(1)} %copy-done.12, bf16[768,1024]{1,0:T(8,128)(2,1)S(1)} %bitcast.13, bf16[1024,8192]{1,0:T(8,128)(2,1)} %w_ref.29, f32[8,128]{1,0:T(8,128)S(1)} %shard_map.85.refs_0_), custom_call_target="tpu_custom_call" | custom-call | flops 24159191040 | bytes 4194304 | tf_op jit(solution)/shard_map/pallas_call | solution.py:81
  23.3 2.8 %shard_map.87.after_ref = bf16[768,512]{1,0:T(8,128)(2,1)S(1)} custom-call(s32[8]{0:T(128)S(1)} %copy-done.12, bf16[768,1024]{1,0:T(8,128)(2,1)S(1)} %bitcast.14, bf16[1024,8192]{1,0:T(8,128)(2,1)} %w_ref.29, bf16[768,512]{1,0:T(8,128)(2,1)S(1)} %shard_map.86.refs_0_), custom_call_target="tpu_custom_call" | custom-call | flops 24159191040 | bytes 4194304 | tf_op jit(solution)/shard_map/pallas_call | solution.py:81
  28.0 5.7 %shard_map.88 = (f32[64,384]{1,0:T(8,128)S(1)}, f32[64,384]{1,0:T(8,128)S(1)}) custom-call(s32[24]{0:T(128)S(1)} %compare_convert_fusion.local, s32[24]{0:T(128)S(1)} %get-tuple-element.26.index, s32[1]{0:T(128)} %bitcast.1.side, bf16[768,1024]{1,0:T(8,128)(2,1)S(1)} %bitcast.15, s32[3,256]{1,0:T(4,128)S(1)} %copy-done.8, bf16[96,64,1024]{2,1,0:T(8,128)(2,1)} %table_ref.5, ...), custom_call_target="tpu_custom_call" | custom-call | flops 12079595520 | bytes 4718592 | tf_op jit(solution)/shard_map/pallas_call | solution.py:246
  35.3 2.9 %shard_map.89.refs_2_ = bf16[768,512]{1,0:T(8,128)(2,1)S(1)} custom-call(s32[8]{0:T(128)S(1)} %copy-done.12, bf16[768,1024]{1,0:T(8,128)(2,1)S(1)} %bitcast.16, bf16[1024,8192]{1,0:T(8,128)(2,1)} %w_ref.29, bf16[768,256]{1,0:T(8,128)(2,1)S(1)} %collective-permute-done.3.refs_1_.refs_0_, bf16[768,256]{1,0:T(8,128)(2,1)S(1)} %collective-permute-done.4.refs_1_, ...), custom_call_target="tpu_custom_call" | custom-call | flops 24159191040 | bytes 4194304 | tf_op jit(solution)/shard_map/pallas_call | solution.py:81
  39.9 3.0 %shard_map.90.refs_0_.after_ref = bf16[768,512]{1,0:T(8,128)(2,1)S(1)} custom-call(s32[8]{0:T(128)S(1)} %copy-done.12, bf16[768,1024]{1,0:T(8,128)(2,1)S(1)} %bitcast.17, bf16[1024,8192]{1,0:T(8,128)(2,1)} %w_ref.29, bf16[768,256]{1,0:T(8,128)(2,1)S(1)} %collective-permute-done.1.refs_2_.refs_0_, bf16[768,256]{1,0:T(8,128)(2,1)} %collective-permute-done.2.refs_1_, ...), custom_call_target="tpu_custom_call" | custom-call | flops 24159191040 | bytes 4194304 | tf_op jit(solution)/shard_map/pallas_call | solution.py:81
  43.9 3.0 %collective-permute-done.8 = f16[64,384]{1,0:T(8,128)(2,1)S(1)} collective-permute-done((f16[64,384]{1,0:T(8,128)(2,1)S(1)}, f16[64,384]{1,0:T(8,128)(2,1)S(1)}, u32[]{:S(2)}, u32[]{:S(2)}) %collective-permute-start.8) | collective-permute-done | bytes 49184 | tf_op jit(solution)/shard_map/ppermute | solution.py:514
  47.8 2.8 %shard_map.93.refs_1_ = bf16[768,512]{1,0:T(8,128)(2,1)S(1)} custom-call(s32[8]{0:T(128)S(1)} %copy-done.12, bf16[768,1024]{1,0:T(8,128)(2,1)S(1)} %bitcast.18, bf16[1024,8192]{1,0:T(8,128)(2,1)} %w_ref.29, bf16[768,512]{1,0:T(8,128)(2,1)S(1)} %collective-permute-done.11.refs_0_, f32[64,384]{1,0:T(8,128)S(1)} %shard_map.92.refs_1_.low_ref), custom_call_target="tpu_custom_call" | custom-call | flops 24159191040 | bytes 4194304 | tf_op jit(solution)/shard_map/pallas_call | solution.py:81
  52.6 2.8 %shard_map.94.refs_0_.after_ref = bf16[768,512]{1,0:T(8,128)(2,1)S(1)} custom-call(s32[8]{0:T(128)S(1)} %copy-done.12, bf16[768,1024]{1,0:T(8,128)(2,1)S(1)} %bitcast.19, bf16[1024,8192]{1,0:T(8,128)(2,1)} %w_ref.29, bf16[768,512]{1,0:T(8,128)(2,1)S(1)} %collective-permute-done.10.refs_0_, bf16[768,512]{1,0:T(8,128)(2,1)S(1)} %shard_map.93.refs_1_), custom_call_target="tpu_custom_call" | custom-call | flops 24159191040 | bytes 4194304 | tf_op jit(solution)/shard_map/pallas_call | solution.py:81
  56.5 8.0 %collective-permute-done.9 = f16[64,384]{1,0:T(8,128)(2,1)S(1)} collective-permute-done((f16[64,384]{1,0:T(8,128)(2,1)S(1)}, f16[64,384]{1,0:T(8,128)(2,1)S(1)}, u32[]{:S(2)}, u32[]{:S(2)}) %collective-permute-start.9) | collective-permute-done | bytes 49184 | tf_op jit(solution)/shard_map/ppermute | solution.py:514
  65.8 2.8 %collective-permute-start.15 = (f16[64,384]{1,0:T(8,128)(2,1)}, f16[64,384]{1,0:T(8,128)(2,1)}, u32[]{:S(2)}, u32[]{:S(2)}) collective-permute-start(f16[64,384]{1,0:T(8,128)(2,1)} %multiply_convert_fusion), channel_id=1, source_target_pairs={{0,4},{1,5},{2,6},{3,7},{4,0},{5,1},{6,2},{7,3},{8,12},{9,13},{10,... | collective-permute-start | bytes 147464 | tf_op jit(solution)/shard_map/ppermute | solution.py:514
  68.6 3.6 %shard_map.97.refs_1_ = bf16[768,512]{1,0:T(8,128)(2,1)} custom-call(s32[8]{0:T(128)S(1)} %copy-done.12, bf16[768,1024]{1,0:T(8,128)(2,1)S(1)} %bitcast.20, bf16[1024,8192]{1,0:T(8,128)(2,1)} %w_ref.29, bf16[768,512]{1,0:T(8,128)(2,1)S(1)} %collective-permute-done.7.refs_0_, f32[64,384]{1,0:T(8,128)S(1)} %shard_map.96.refs_1_.low_ref), custom_call_target="tpu_custom_call" | custom-call | flops 24159191040 | bytes 4194304 | tf_op jit(solution)/shard_map/pallas_call | solution.py:81
  72.3 2.8 %shard_map.98.after_ref = bf16[768,512]{1,0:T(8,128)(2,1)S(1)} custom-call(s32[8]{0:T(128)S(1)} %copy-done.12, bf16[768,1024]{1,0:T(8,128)(2,1)S(1)} %bitcast.21, bf16[1024,8192]{1,0:T(8,128)(2,1)} %w_ref.29, bf16[768,512]{1,0:T(8,128)(2,1)S(1)} %collective-permute-done.6.refs_0_, bf16[768,512]{1,0:T(8,128)(2,1)} %shard_map.97.refs_1_), custom_call_target="tpu_custom_call" | custom-call | flops 24159191040 | bytes 4194304 | tf_op jit(solution)/shard_map/pallas_call | solution.py:81
  77.1 2.7 %shard_map.99.refs_1_ = bf16[24,64,1024]{2,1,0:T(8,128)(2,1)S(1)} custom-call(s32[24]{0:T(128)S(1)} %copy-done.3, bf16[96,64,1024]{2,1,0:T(8,128)(2,1)} %table_ref.7, bf16[768,512]{1,0:T(8,128)(2,1)S(1)} %shard_map.98.after_ref), custom_call_target="tpu_custom_call" | custom-call | bytes 6291456 | tf_op jit(solution)/shard_map/pallas_call | solution.py:175
  80.3 2.8 %shard_map.100.refs_1_ = bf16[768,512]{1,0:T(8,128)(2,1)S(1)} custom-call(s32[8]{0:T(128)S(1)} %copy-done.12, bf16[768,1024]{1,0:T(8,128)(2,1)S(1)} %bitcast.22, bf16[1024,8192]{1,0:T(8,128)(2,1)} %w_ref.29, bf16[768,512]{1,0:T(8,128)(2,1)S(1)} %collective-permute-done.14.refs_0_, bf16[24,64,1024]{2,1,0:T(8,128)(2,1)S(1)} %shard_map.99.refs_1_), custom_call_target="tpu_custom_call" | custom-call | flops 24159191040 | bytes 4194304 | tf_op jit(solution)/shard_map/pallas_call | solution.py:81
  83.2 2.8 %shard_map.101.after_ref = bf16[768,512]{1,0:T(8,128)(2,1)S(1)} custom-call(s32[8]{0:T(128)S(1)} %copy-done.12, bf16[768,1024]{1,0:T(8,128)(2,1)S(1)} %bitcast.23, bf16[1024,8192]{1,0:T(8,128)(2,1)} %w_ref.29, bf16[768,512]{1,0:T(8,128)(2,1)S(1)} %collective-permute-done.13.refs_0_, bf16[768,512]{1,0:T(8,128)(2,1)S(1)} %shard_map.100.refs_1_), custom_call_target="tpu_custom_call" | custom-call | flops 24159191040 | bytes 4194304 | tf_op jit(solution)/shard_map/pallas_call | solution.py:81
  86.0 2.6 %collective-permute-start.19 = (bf16[768,512]{1,0:T(8,128)(2,1)S(1)}, bf16[768,512]{1,0:T(8,128)(2,1)S(1)}, u32[]{:S(2)}, u32[]{:S(2)}) collective-permute-start(bf16[768,512]{1,0:T(8,128)(2,1)S(1)} %shard_map.101.after_ref), channel_id=1, source_target_pairs={{0,1},{2,0},{4,2},{6,4},{7,6},{5,7},{3,5},{1,3},{8,9},{10,8},{12,1... | collective-permute-start | bytes 2359304 | tf_op jit(solution)/shard_map/ppermute | solution.py:487
  88.5 7.1 %shard_map.102 = (f32[768,1024]{1,0:T(8,128)S(1)}, bf16[24,64,1024]{2,1,0:T(8,128)(2,1)S(1)}) custom-call(s32[24]{0:T(128)S(1)} %copy-done.11, s32[24]{0:T(128)S(1)} %copy-done.6, s32[8]{0:T(128)S(1)} %copy-done.12, bf16[768,1024]{1,0:T(8,128)(2,1)S(1)} %bitcast.24, bf16[1024,8192]{1,0:T(8,128)(2,1)} %w_ref.29, bf16[96,64,1024]{2,1,0:T(8,128)(2,1)} %table_ref.7, ...), custom_call_target="tpu_custom_call" | custom-call | flops 48318382080 | bytes 13107200 | tf_op jit(solution)/shard_map/pallas_call | solution.py:305
  100.7 2.8 %shard_map.105.refs_1_ = bf16[768,512]{1,0:T(8,128)(2,1)S(1)} custom-call(s32[8]{0:T(128)S(1)} %copy-done.12, bf16[768,1024]{1,0:T(8,128)(2,1)S(1)} %bitcast.25, bf16[1024,8192]{1,0:T(8,128)(2,1)} %w_ref.29, bf16[768,512]{1,0:T(8,128)(2,1)S(1)} %collective-permute-done.18.refs_0_, bf16[64,384]{1,0:T(8,128)(2,1)S(1)} %shard_map.104.refs_1_.low_ref), custom_call_target="tpu_custom_call" | custom-call | flops 24159191040 | bytes 4194304 | tf_op jit(solution)/shard_map/pallas_call | solution.py:81
  103.8 2.8 %shard_map.106.after_ref = bf16[768,512]{1,0:T(8,128)(2,1)S(1)} custom-call(s32[8]{0:T(128)S(1)} %copy-done.12, bf16[768,1024]{1,0:T(8,128)(2,1)S(1)} %bitcast.26, bf16[1024,8192]{1,0:T(8,128)(2,1)} %w_ref.29, bf16[768,512]{1,0:T(8,128)(2,1)S(1)} %collective-permute-done.17.refs_0_, bf16[768,512]{1,0:T(8,128)(2,1)S(1)} %shard_map.105.refs_1_), custom_call_target="tpu_custom_call" | custom-call | flops 24159191040 | bytes 4194304 | tf_op jit(solution)/shard_map/pallas_call | solution.py:81
  108.4 7.1 %collective-permute-done.16.other_ref = bf16[64,384]{1,0:T(8,128)(2,1)S(1)} collective-permute-done((bf16[64,384]{1,0:T(8,128)(2,1)S(1)}, bf16[64,384]{1,0:T(8,128)(2,1)S(1)}, u32[]{:S(2)}, u32[]{:S(2)}) %collective-permute-start.16) | collective-permute-done | bytes 49184 | tf_op jit(solution)/shard_map/ppermute | solution.py:514
  116.5 14.7 %collective-permute-done.22.last_ref = bf16[768,512]{1,0:T(8,128)(2,1)S(1)} collective-permute-done((bf16[768,512]{1,0:T(8,128)(2,1)S(1)}, bf16[768,512]{1,0:T(8,128)(2,1)S(1)}, u32[]{:S(2)}, u32[]{:S(2)}) %collective-permute-start.22) | collective-permute-done | bytes 786464 | tf_op jit(solution)/shard_map/ppermute | solution.py:487
  (103 shorter events, 34.9 us)
Async XLA Ops:
  0.0 14.5 %collective-permute-start = (s32[3,2,4]{2,1,0:T(2,128)}, s32[3,2,4]{2,1,0:T(2,128)S(1)}, u32[]{:S(2)}, u32[]{:S(2)}) collective-permute-start(s32[3,2,4]{2,1,0:T(2,128)} %param.13), channel_id=1, source_target_pairs={{0,8},{8,0},{1,9},{9,1},{2,10},{10,2},{3,11},{11,3},{4,12},{12,4},... | collective-permute-start | bytes 296 | tf_op jit(solution)/shard_map/ppermute | solution.py:493
  5.6 12.9 %collective-permute-start.1 = (bf16[768,256]{1,0:T(8,128)(2,1)}, bf16[768,256]{1,0:T(8,128)(2,1)S(1)}, u32[]{:S(2)}, u32[]{:S(2)}) collective-permute-start(bf16[768,256]{1,0:T(8,128)(2,1)} %get-tuple-element.15), channel_id=1, source_target_pairs={{0,1},{2,0},{4,2},{6,4},{7,6},{5,7},{3,5},{1,3},{8,9},{10,8},{12,1... | collective-permute-start | bytes 1179656 | tf_op jit(solution)/shard_map/ppermute | solution.py:498
  8.1 12.2 %collective-permute-start.3 = (bf16[768,256]{1,0:T(8,128)(2,1)}, bf16[768,256]{1,0:T(8,128)(2,1)S(1)}, u32[]{:S(2)}, u32[]{:S(2)}) collective-permute-start(bf16[768,256]{1,0:T(8,128)(2,1)} %get-tuple-element.18), channel_id=1, source_target_pairs={{0,2},{2,4},{4,6},{6,7},{7,5},{5,3},{3,1},{1,0},{8,10},{10,12},{12... | collective-permute-start | bytes 1179656 | tf_op jit(solution)/shard_map/ppermute | solution.py:498
  12.4 22.9 %collective-permute-start.4 = (bf16[768,256]{1,0:T(8,128)(2,1)}, bf16[768,256]{1,0:T(8,128)(2,1)S(1)}, u32[]{:S(2)}, u32[]{:S(2)}) collective-permute-start(bf16[768,256]{1,0:T(8,128)(2,1)} %get-tuple-element.19), channel_id=1, source_target_pairs={{0,2},{2,4},{4,6},{6,7},{7,5},{5,3},{3,1},{1,0},{8,10},{10,12},{12... | collective-permute-start | bytes 1179656 | tf_op jit(solution)/shard_map/ppermute | solution.py:498
  14.5 25.4 %collective-permute-start.2 = (bf16[768,256]{1,0:T(8,128)(2,1)S(1)}, bf16[768,256]{1,0:T(8,128)(2,1)}, u32[]{:S(2)}, u32[]{:S(2)}) collective-permute-start(bf16[768,256]{1,0:T(8,128)(2,1)S(1)} %get-tuple-element.17), channel_id=1, source_target_pairs={{0,1},{2,0},{4,2},{6,4},{7,6},{5,7},{3,5},{1,3},{8,9},{10,8},{12,1... | collective-permute-start | bytes 1179656 | tf_op jit(solution)/shard_map/ppermute | solution.py:498
  18.3 9.6 %collective-permute-start.5 = (bf16[24,64,1024]{2,1,0:T(8,128)(2,1)S(1)}, bf16[24,64,1024]{2,1,0:T(8,128)(2,1)S(1)}, u32[]{:S(2)}, u32[]{:S(2)}) collective-permute-start(bf16[24,64,1024]{2,1,0:T(8,128)(2,1)S(1)} %shard_map.84.refs_0_), channel_id=1, source_target_pairs={{0,8},{8,0},{1,9},{9,1},{2,10},{10,2},{3,11},{11,3},{4,12},{12,4},... | collective-permute-start | bytes 9437192 | tf_op jit(solution)/shard_map/ppermute | solution.py:504
  23.0 24.7 %collective-permute-start.11 = (bf16[768,512]{1,0:T(8,128)(2,1)S(1)}, bf16[768,512]{1,0:T(8,128)(2,1)S(1)}, u32[]{:S(2)}, u32[]{:S(2)}) collective-permute-start(bf16[768,512]{1,0:T(8,128)(2,1)S(1)} %shard_map.86.refs_0_), channel_id=1, source_target_pairs={{0,2},{2,4},{4,6},{6,7},{7,5},{5,3},{3,1},{1,0},{8,10},{10,12},{12... | collective-permute-start | bytes 2359304 | tf_op jit(solution)/shard_map/ppermute | solution.py:487
  26.1 26.6 %collective-permute-start.10 = (bf16[768,512]{1,0:T(8,128)(2,1)S(1)}, bf16[768,512]{1,0:T(8,128)(2,1)S(1)}, u32[]{:S(2)}, u32[]{:S(2)}) collective-permute-start(bf16[768,512]{1,0:T(8,128)(2,1)S(1)} %shard_map.87.after_ref), channel_id=1, source_target_pairs={{0,1},{2,0},{4,2},{6,4},{7,6},{5,7},{3,5},{1,3},{8,9},{10,8},{12,1... | collective-permute-start | bytes 2359304 | tf_op jit(solution)/shard_map/ppermute | solution.py:487
  33.7 13.3 %collective-permute-start.8 = (f16[64,384]{1,0:T(8,128)(2,1)S(1)}, f16[64,384]{1,0:T(8,128)(2,1)S(1)}, u32[]{:S(2)}, u32[]{:S(2)}) collective-permute-start(f16[64,384]{1,0:T(8,128)(2,1)S(1)} %multiply_convert_fusion.2), channel_id=1, source_target_pairs={{0,1},{1,0},{2,3},{3,2},{4,5},{5,4},{6,7},{7,6},{8,9},{9,8},{10,11... | collective-permute-start | bytes 147464 | tf_op jit(solution)/shard_map/ppermute | solution.py:514
  38.2 30.4 %collective-permute-start.7 = (bf16[768,512]{1,0:T(8,128)(2,1)S(1)}, bf16[768,512]{1,0:T(8,128)(2,1)S(1)}, u32[]{:S(2)}, u32[]{:S(2)}) collective-permute-start(bf16[768,512]{1,0:T(8,128)(2,1)S(1)} %shard_map.89.refs_2_), channel_id=1, source_target_pairs={{0,2},{2,4},{4,6},{6,7},{7,5},{5,3},{3,1},{1,0},{8,10},{10,12},{12... | collective-permute-start | bytes 2359304 | tf_op jit(solution)/shard_map/ppermute | solution.py:487
  42.9 29.4 %collective-permute-start.6 = (bf16[768,512]{1,0:T(8,128)(2,1)S(1)}, bf16[768,512]{1,0:T(8,128)(2,1)S(1)}, u32[]{:S(2)}, u32[]{:S(2)}) collective-permute-start(bf16[768,512]{1,0:T(8,128)(2,1)S(1)} %shard_map.90.refs_0_.after_ref), channel_id=1, source_target_pairs={{0,1},{2,0},{4,2},{6,4},{7,6},{5,7},{3,5},{1,3},{8,9},{10,8},{12,1... | collective-permute-start | bytes 2359304 | tf_op jit(solution)/shard_map/ppermute | solution.py:487
  47.7 16.8 %collective-permute-start.9 = (f16[64,384]{1,0:T(8,128)(2,1)S(1)}, f16[64,384]{1,0:T(8,128)(2,1)S(1)}, u32[]{:S(2)}, u32[]{:S(2)}) collective-permute-start(f16[64,384]{1,0:T(8,128)(2,1)S(1)} %multiply_convert_fusion.1), channel_id=1, source_target_pairs={{0,2},{1,3},{2,0},{3,1},{4,6},{5,7},{6,4},{7,5},{8,10},{9,11},{10,... | collective-permute-start | bytes 147464 | tf_op jit(solution)/shard_map/ppermute | solution.py:514
  50.6 29.7 %collective-permute-start.14 = (bf16[768,512]{1,0:T(8,128)(2,1)S(1)}, bf16[768,512]{1,0:T(8,128)(2,1)S(1)}, u32[]{:S(2)}, u32[]{:S(2)}) collective-permute-start(bf16[768,512]{1,0:T(8,128)(2,1)S(1)} %shard_map.93.refs_1_), channel_id=1, source_target_pairs={{0,2},{2,4},{4,6},{6,7},{7,5},{5,3},{3,1},{1,0},{8,10},{10,12},{12... | collective-permute-start | bytes 2359304 | tf_op jit(solution)/shard_map/ppermute | solution.py:487
  55.4 27.7 %collective-permute-start.13 = (bf16[768,512]{1,0:T(8,128)(2,1)S(1)}, bf16[768,512]{1,0:T(8,128)(2,1)S(1)}, u32[]{:S(2)}, u32[]{:S(2)}) collective-permute-start(bf16[768,512]{1,0:T(8,128)(2,1)S(1)} %shard_map.94.refs_0_.after_ref), channel_id=1, source_target_pairs={{0,1},{2,0},{4,2},{6,4},{7,6},{5,7},{3,5},{1,3},{8,9},{10,8},{12,1... | collective-permute-start | bytes 2359304 | tf_op jit(solution)/shard_map/ppermute | solution.py:487
  65.8 30.3 %collective-permute-start.15 = (f16[64,384]{1,0:T(8,128)(2,1)}, f16[64,384]{1,0:T(8,128)(2,1)}, u32[]{:S(2)}, u32[]{:S(2)}) collective-permute-start(f16[64,384]{1,0:T(8,128)(2,1)} %multiply_convert_fusion), channel_id=1, source_target_pairs={{0,4},{1,5},{2,6},{3,7},{4,0},{5,1},{6,2},{7,3},{8,12},{9,13},{10,... | collective-permute-start | bytes 147464 | tf_op jit(solution)/shard_map/ppermute | solution.py:514
  72.3 28.4 %collective-permute-start.18 = (bf16[768,512]{1,0:T(8,128)(2,1)}, bf16[768,512]{1,0:T(8,128)(2,1)S(1)}, u32[]{:S(2)}, u32[]{:S(2)}) collective-permute-start(bf16[768,512]{1,0:T(8,128)(2,1)} %shard_map.97.refs_1_), channel_id=1, source_target_pairs={{0,2},{2,4},{4,6},{6,7},{7,5},{5,3},{3,1},{1,0},{8,10},{10,12},{12... | collective-permute-start | bytes 2359304 | tf_op jit(solution)/shard_map/ppermute | solution.py:487
  75.1 28.7 %collective-permute-start.17 = (bf16[768,512]{1,0:T(8,128)(2,1)S(1)}, bf16[768,512]{1,0:T(8,128)(2,1)S(1)}, u32[]{:S(2)}, u32[]{:S(2)}) collective-permute-start(bf16[768,512]{1,0:T(8,128)(2,1)S(1)} %shard_map.98.after_ref), channel_id=1, source_target_pairs={{0,1},{2,0},{4,2},{6,4},{7,6},{5,7},{3,5},{1,3},{8,9},{10,8},{12,1... | collective-permute-start | bytes 2359304 | tf_op jit(solution)/shard_map/ppermute | solution.py:487
  80.3 5.7 %collective-permute-start.12 = (bf16[24,64,1024]{2,1,0:T(8,128)(2,1)S(1)}, bf16[24,64,1024]{2,1,0:T(8,128)(2,1)S(1)}, u32[]{:S(2)}, u32[]{:S(2)}) collective-permute-start(bf16[24,64,1024]{2,1,0:T(8,128)(2,1)S(1)} %shard_map.99.refs_1_), channel_id=1, source_target_pairs={{0,8},{8,0},{1,9},{9,1},{2,10},{10,2},{3,11},{11,3},{4,12},{12,4},... | collective-permute-start | bytes 9437192 | tf_op jit(solution)/shard_map/ppermute | solution.py:525
  83.1 33.1 %collective-permute-start.20 = (bf16[768,512]{1,0:T(8,128)(2,1)S(1)}, bf16[768,512]{1,0:T(8,128)(2,1)S(1)}, u32[]{:S(2)}, u32[]{:S(2)}) collective-permute-start(bf16[768,512]{1,0:T(8,128)(2,1)S(1)} %shard_map.100.refs_1_), channel_id=1, source_target_pairs={{0,2},{2,4},{4,6},{6,7},{7,5},{5,3},{3,1},{1,0},{8,10},{10,12},{12... | collective-permute-start | bytes 2359304 | tf_op jit(solution)/shard_map/ppermute | solution.py:487
  86.0 30.2 %collective-permute-start.19 = (bf16[768,512]{1,0:T(8,128)(2,1)S(1)}, bf16[768,512]{1,0:T(8,128)(2,1)S(1)}, u32[]{:S(2)}, u32[]{:S(2)}) collective-permute-start(bf16[768,512]{1,0:T(8,128)(2,1)S(1)} %shard_map.101.after_ref), channel_id=1, source_target_pairs={{0,1},{2,0},{4,2},{6,4},{7,6},{5,7},{3,5},{1,3},{8,9},{10,8},{12,1... | collective-permute-start | bytes 2359304 | tf_op jit(solution)/shard_map/ppermute | solution.py:487
  98.6 16.8 %collective-permute-start.16 = (bf16[64,384]{1,0:T(8,128)(2,1)S(1)}, bf16[64,384]{1,0:T(8,128)(2,1)S(1)}, u32[]{:S(2)}, u32[]{:S(2)}) collective-permute-start(bf16[64,384]{1,0:T(8,128)(2,1)S(1)} %shard_map.104.refs_1_.low_ref), channel_id=1, source_target_pairs={{0,1},{1,0},{2,3},{3,2},{4,5},{5,4},{6,7},{7,6},{8,9},{9,8},{10,11... | collective-permute-start | bytes 147464 | tf_op jit(solution)/shard_map/ppermute | solution.py:514
  103.5 27.7 %collective-permute-start.22 = (bf16[768,512]{1,0:T(8,128)(2,1)S(1)}, bf16[768,512]{1,0:T(8,128)(2,1)S(1)}, u32[]{:S(2)}, u32[]{:S(2)}) collective-permute-start(bf16[768,512]{1,0:T(8,128)(2,1)S(1)} %shard_map.105.refs_1_), channel_id=1, source_target_pairs={{0,2},{2,4},{4,6},{6,7},{7,5},{5,3},{3,1},{1,0},{8,10},{10,12},{12... | collective-permute-start | bytes 2359304 | tf_op jit(solution)/shard_map/ppermute | solution.py:487
  106.6 26.0 %collective-permute-start.21 = (bf16[768,512]{1,0:T(8,128)(2,1)S(1)}, bf16[768,512]{1,0:T(8,128)(2,1)S(1)}, u32[]{:S(2)}, u32[]{:S(2)}) collective-permute-start(bf16[768,512]{1,0:T(8,128)(2,1)S(1)} %shard_map.106.after_ref), channel_id=1, source_target_pairs={{0,1},{2,0},{4,2},{6,4},{7,6},{5,7},{3,5},{1,3},{8,9},{10,8},{12,1... | collective-permute-start | bytes 2359304 | tf_op jit(solution)/shard_map/ppermute | solution.py:487
  116.1 15.1 %copy-start.4 = (s32[3,1]{0,1:T(1,128)S(1)}, s32[3,1]{0,1:T(1,128)}, u32[]{:S(2)}) copy-start(s32[3,1]{0,1:T(1,128)} %param.15) | copy-start | bytes 40
  (16 other events, 109.1 us)

commit v14 on v12

--- a/solution.py
+++ b/solution.py
@@ -102,17 +102,64 @@
     )(dests, x, weight, *received, after)
 
 
-def first_kernel(with_after, dests, x_ref, w_ref, *refs):
+def first_kernel(dests, x_ref, w_ref, *refs):
+    *out_refs, token_ref, held = refs
     total = jnp.dot(x_ref[...], w_ref[...], preferred_element_type=jnp.float32)
-    refs[-1][...] = jnp.zeros_like(refs[-1])
-    for chain, out_ref in enumerate(refs[-3:-1]):
+    token_ref[...] = jnp.zeros_like(token_ref)
+    part, chain = pl.program_id(0), pl.program_id(1)
+
+    @pl.when(part == 0)
+    def _():
+        held[chain] = total
+
+    for number, out_ref in enumerate(out_refs):
+
+        @pl.when((part == 1) & (chain == number))
+        def _():
+            out_ref[...] = (held[number] + total).astype(out_ref.dtype)
+
+
+def first_pieces(dests, offset, x, weight):
+    rows, depth = x.shape
+    _, tile, tiles = tiling(dests, weight)
+    size = dests.shape[0]
+
+    def place(k, j, d):
+        one = d[offset] * 2 * tiles
+        two = (d[(size - offset) % size] * 2 + 1) * tiles
+        return (k, jnp.where(j == 0, one, two))
+
+    return pl.pallas_call(
+        first_kernel,
+        grid_spec=pltpu.PrefetchScalarGridSpec(
+            num_scalar_prefetch=1,
+            grid=(2, 2),
+            in_specs=[
+                pl.BlockSpec((rows, depth // 2), lambda k, j, d: (0, k)),
+                pl.BlockSpec((depth // 2, tile), place),
+            ],
+            out_specs=[WHOLE, WHOLE, pl.BlockSpec((8, 128), lambda k, j, d: (0, 0))],
+            scratch_shapes=[pltpu.VMEM((2, rows, tile), jnp.float32)],
+        ),
+        out_shape=[jax.ShapeDtypeStruct((rows, tile), jnp.bfloat16)] * 2
+        + [jax.ShapeDtypeStruct((8, 128), jnp.float32)],
+        compiler_params=params(FIRST_VMEM_LIMIT),
+        cost_estimate=cost(
+            4 * rows * depth * tile, 2 * (rows * depth + 2 * depth * tile + 2 * rows * tile)
+        ),
+    )(dests, x, weight)
+
+
+def next_kernel(dests, x_ref, w_ref, after_ref, *out_refs):
+    total = jnp.dot(x_ref[...], w_ref[...], preferred_element_type=jnp.float32)
+    for chain, out_ref in enumerate(out_refs):
 
         @pl.when(pl.program_id(0) == chain)
         def _():
             out_ref[...] = total.astype(out_ref.dtype)
 
 
-def first_pieces(dests, offset, piece, x, weight, after):
+def next_pieces(dests, offset, piece, x, weight, after):
     rows, depth = x.shape
     _, tile, tiles = tiling(dests, weight)
     size = dests.shape[0]
@@ -122,26 +169,20 @@
         two = (d[(size - offset) % size] * 2 + 1) * tiles + piece
         return (0, jnp.where(j == 0, one, two))
 
-    tail = [] if after is None else [after]
-    return pl.pallas_call(
-        functools.partial(first_kernel, after is not None),
+    return pl.pallas_call(
+        next_kernel,
         grid_spec=pltpu.PrefetchScalarGridSpec(
             num_scalar_prefetch=1,
             grid=(2,),
-            in_specs=[
-                pl.BlockSpec((rows, depth), lambda j, d: (0, 0)) if after is None else WHOLE,
-                pl.BlockSpec((depth, tile), place),
-            ]
-            + [ANYWHERE] * len(tail),
-            out_specs=[WHOLE, WHOLE, pl.BlockSpec((8, 128), lambda j, d: (0, 0))],
-        ),
-        out_shape=[jax.ShapeDtypeStruct((rows, tile), jnp.bfloat16)] * 2
-        + [jax.ShapeDtypeStruct((8, 128), jnp.float32)],
-        compiler_params=params(FIRST_VMEM_LIMIT if after is None else VMEM_LIMIT),
+            in_specs=[WHOLE, pl.BlockSpec((depth, tile), place), ANYWHERE],
+            out_specs=[WHOLE, WHOLE],
+        ),
+        out_shape=[jax.ShapeDtypeStruct((rows, tile), jnp.bfloat16)] * 2,
+        compiler_params=params(),
         cost_estimate=cost(
             4 * rows * depth * tile, 2 * (rows * depth + 2 * depth * tile + 2 * rows * tile)
         ),
-    )(dests, x, weight, *tail)
+    )(dests, x, weight, after)
 
 
 def touch_kernel(*refs):
@@ -397,56 +438,47 @@
     )(own, left, right)
 
 
-def finish_kernel(half, live, own_ref, last_ref, *refs):
-    out_ref, held, sems = refs[-3:]
+def finish_kernel(live, own_ref, left_ref, right_ref, out_ref, held, sems):
     rows, cols = held.shape
+    half = cols // 2
     count = rows // live.shape[0]
-    columns = slice(half * cols, (half + 1) * cols)
     part = rows // sems.shape[0]
     copies = []
     for at in range(sems.shape[0]):
         for chunk in chunks(part):
             here = slice(at * part + chunk.start, at * part + chunk.stop)
-            total = own_ref[here, columns] + last_ref[here, :].astype(jnp.float32)
-            row = here.start % count + lax.broadcasted_iota(jnp.int32, total.shape, 0)
+            row = here.start % count + lax.broadcasted_iota(
+                jnp.int32, (here.stop - here.start, half), 0
+            )
             alive = row < live[here.start // count]
-            held[here, :] = jnp.where(alive, total, 0.0).astype(held.dtype)
+            for columns, last_ref in ((slice(0, half), left_ref), (slice(half, cols), right_ref)):
+                total = own_ref[here, columns] + last_ref[here, :].astype(jnp.float32)
+                held[here, columns] = jnp.where(alive, total, 0.0).astype(held.dtype)
         rows_at = pl.ds(at * part, part)
-        copies.append(
-            pltpu.make_async_copy(held.at[rows_at], out_ref.at[rows_at, columns], sems.at[at])
-        )
+        copies.append(pltpu.make_async_copy(held.at[rows_at], out_ref.at[rows_at], sems.at[at]))
         copies[-1].start()
     for copy in copies:
         copy.wait()
 
 
-def finish(live, half, own, last, result):
+def finish(live, own, left, right):
     rows, cols = own.shape
-    steps = live.shape[0]
-    in_specs = [WHOLE, WHOLE]
-    operands = [own, last]
-    aliases = {}
-    if result is not None:
-        in_specs.append(ANYWHERE)
-        operands.append(result)
-        aliases = {3: 0}
-    return pl.pallas_call(
-        functools.partial(finish_kernel, half),
+    return pl.pallas_call(
+        finish_kernel,
         grid_spec=pltpu.PrefetchScalarGridSpec(
             num_scalar_prefetch=1,
             grid=(1,),
-            in_specs=in_specs,
+            in_specs=[WHOLE] * 3,
             out_specs=ANYWHERE,
             scratch_shapes=[
-                pltpu.VMEM((rows, cols // 2), jnp.bfloat16),
-                pltpu.SemaphoreType.DMA((2 * steps,)),
+                pltpu.VMEM((rows, cols), jnp.bfloat16),
+                pltpu.SemaphoreType.DMA((4 * live.shape[0],)),
             ],
         ),
         out_shape=jax.ShapeDtypeStruct((rows, cols), jnp.bfloat16),
-        input_output_aliases=aliases,
-        compiler_params=params(),
-        cost_estimate=cost(0, rows * cols * 5),
-    )(live, *operands)
+        compiler_params=params(),
+        cost_estimate=cost(0, rows * cols * 10),
+    )(live, own, left, right)
 
 
 def per_device(
@@ -493,7 +525,11 @@
     ids_there = lax.ppermute(block_adapter_ids, "inst", SWAP).reshape(-1)
     last = None
     for piece in range(tiling(dests, output_weight)[2]):
-        *both, last = first_pieces(dests, far % size, piece, x, output_weight, last)
+        if piece == 0:
+            *both, last = first_pieces(dests, far % size, x, output_weight)
+        else:
+            both = next_pieces(dests, far % size, piece, x, output_weight, last)
+            last = both[1]
         for (half, sign, moves), part in zip(pairs[0], both):
             arrived.setdefault((half, sign), []).append(lax.ppermute(part, "tp", moves))
     pages = adapter_page_table[jnp.concatenate([ids, ids_there])]
@@ -537,9 +573,7 @@
     last = turn(number, last)
     own = add_delta(sizes, side, own, up_pages, row_list_position, low, other, last)
     own = join(own, arrived[0, -1][0], arrived[1, 1][0])
-    result = None
-    for half, sign, _ in pairs[0]:
-        result = finish(live_row_count.reshape(-1), half, own, arrived[half, sign][0], result)
+    result = finish(live_row_count.reshape(-1), own, arrived[0, 1][0], arrived[1, -1][0])
     return result.reshape(steps, row_count, -1)
 
 

time: 134 us -> 135 us (level)
  waiting for transfers between devices: 39.3 us -> 43.3 us
  Pallas kernels: 65.5 us -> 63.6 us
    ppermute x12, waiting for transfers between devices: 14.5 us -> 16.9 us  [turn(): arrived[half, sign] = [lax.ppermute(last, 'tp', moves)]]
    ppermute x4, waiting for transfers between devices: 22.8 us -> 24.5 us  [over(): return lax.ppermute(value, 'tp', [(i, i ^ apart) for i in range(size)])]
    pallas_call x4 -> x3, Pallas kernels: 11.1 us -> 10.9 us  [the longest x1 5.41 us: first_pieces(): pl.pallas_call(first_kernel, grid_spec=pltpu.PrefetchScalarGridSpec(num_s...]
  transfers between devices with their start and end apart: 23 -> 23, of which waited for: 8 -> 9; matrix products, arithmetic and copies ran while one was open for 4% -> 4% of each run, Pallas kernels for 48% -> 46%
where the time goes in v14:
time: 135 us
  Pallas kernels  63.6 us (47%)
  waiting for transfers between devices  43.3 us (32%)
  starting transfers between devices  21.5 us (16%)
  local copies, waits for them, and re-layouts  3.34 us (2%)
  other arithmetic  2.68 us (2%)
    pallas_call x12, Pallas kernels, hop(): pl.pallas_call(functools.partial(hop_kernel, tuple(range(len(received))))...  33.6 us
    ppermute x4, waiting for transfers between devices, over(): return lax.ppermute(value, 'tp', [(i, i ^ apart) for i in range(size)])  24.5 us
    ppermute x12, waiting for transfers between devices, turn(): arrived[half, sign] = [lax.ppermute(last, 'tp', moves)]  16.9 us
    ppermute x12, starting transfers between devices, turn(): arrived[half, sign] = [lax.ppermute(last, 'tp', moves)]  13 us
    pallas_call x1, Pallas kernels, own_terms(): pl.pallas_call(own_kernel, grid_spec=pltpu.PrefetchScalarGridSpec(num_sca...  7.06 us
    pallas_call x1, Pallas kernels, low_rank(): pl.pallas_call(functools.partial(low_kernel, sizes), grid_spec=pltpu.Pref...  5.68 us
    pallas_call x1, Pallas kernels, first_pieces(): pl.pallas_call(first_kernel, grid_spec=pltpu.PrefetchScalarGridSpec(num_s...  5.41 us
    pallas_call x2, Pallas kernels, collect(): pl.pallas_call(functools.partial(collect_kernel, count), grid_spec=pltpu....  5.34 us
  transfers between devices with their start and end apart: 23, of which 9 were waited for; matrix products, arithmetic and copies ran while one was open for 4% of the time, Pallas kernels for 46%

profile of v14, /device:TPU:0, one launch (start us, length us, event | category | flops | bytes accessed | tf_op | source)
XLA Modules:
  0.0 134.8 jit_solution(16055941945933205790)
XLA Ops:
  1.0 5.4 %shard_map.82 = (bf16[768,256]{1,0:T(8,128)(2,1)}, bf16[768,256]{1,0:T(8,128)(2,1)}, f32[8,128]{1,0:T(8,128)}) custom-call(s32[8]{0:T(128)} %compare_select_fusion.3.dests, bf16[768,1024]{1,0:T(8,128)(2,1)} %bitcast.10, bf16[1024,8192]{1,0:T(8,128)(2,1)} %w_ref.29), custom_call_target="tpu_custom_call" | custom-call | flops 24159191040 | bytes 3407872 | tf_op jit(solution)/shard_map/pallas_call | solution.py:132
  6.4 2.6 %collective-permute-start.1 = (bf16[768,256]{1,0:T(8,128)(2,1)}, bf16[768,256]{1,0:T(8,128)(2,1)S(1)}, u32[]{:S(2)}, u32[]{:S(2)}) collective-permute-start(bf16[768,256]{1,0:T(8,128)(2,1)} %get-tuple-element.16), channel_id=1, source_target_pairs={{0,2},{2,4},{4,6},{6,7},{7,5},{5,3},{3,1},{1,0},{8,10},{10,12},{12... | collective-permute-start | bytes 1179656 | tf_op jit(solution)/shard_map/ppermute | solution.py:534
  9.7 3.6 %shard_map.83 = (bf16[768,256]{1,0:T(8,128)(2,1)}, bf16[768,256]{1,0:T(8,128)(2,1)S(1)}) custom-call(s32[8]{0:T(128)S(1)} %copy-done.8, bf16[768,1024]{1,0:T(8,128)(2,1)S(1)} %bitcast.11, bf16[1024,8192]{1,0:T(8,128)(2,1)} %w_ref.29, f32[8,128]{1,0:T(8,128)S(1)} %copy-done.11), custom_call_target="tpu_custom_call" | custom-call | flops 24159191040 | bytes 3407872 | tf_op jit(solution)/shard_map/pallas_call | solution.py:172
  16.5 2.7 %shard_map.84.refs_0_ = bf16[24,64,1024]{2,1,0:T(8,128)(2,1)S(1)} custom-call(s32[24]{0:T(128)S(1)} %get-tuple-element.23.index, bf16[96,64,1024]{2,1,0:T(8,128)(2,1)} %table_ref.6, bf16[768,256]{1,0:T(8,128)(2,1)S(1)} %get-tuple-element.15.after_ref), custom_call_target="tpu_custom_call" | custom-call | bytes 6291456 | tf_op jit(solution)/shard_map/pallas_call | solution.py:216
  21.2 2.8 %shard_map.86.refs_0_ = bf16[768,512]{1,0:T(8,128)(2,1)S(1)} custom-call(s32[8]{0:T(128)S(1)} %copy-done.8, bf16[768,1024]{1,0:T(8,128)(2,1)S(1)} %bitcast.12, bf16[1024,8192]{1,0:T(8,128)(2,1)} %w_ref.29, f32[8,128]{1,0:T(8,128)S(1)} %shard_map.85.refs_0_), custom_call_target="tpu_custom_call" | custom-call | flops 24159191040 | bytes 4194304 | tf_op jit(solution)/shard_map/pallas_call | solution.py:81
  23.9 2.8 %shard_map.87.after_ref = bf16[768,512]{1,0:T(8,128)(2,1)S(1)} custom-call(s32[8]{0:T(128)S(1)} %copy-done.8, bf16[768,1024]{1,0:T(8,128)(2,1)S(1)} %bitcast.13, bf16[1024,8192]{1,0:T(8,128)(2,1)} %w_ref.29, bf16[768,512]{1,0:T(8,128)(2,1)S(1)} %shard_map.86.refs_0_), custom_call_target="tpu_custom_call" | custom-call | flops 24159191040 | bytes 4194304 | tf_op jit(solution)/shard_map/pallas_call | solution.py:81
  28.8 2.7 %shard_map.88.refs_2_ = bf16[24,64,1024]{2,1,0:T(8,128)(2,1)S(1)} custom-call(s32[24]{0:T(128)S(1)} %get-tuple-element.23.index, bf16[96,64,1024]{2,1,0:T(8,128)(2,1)} %table_ref.7, bf16[768,512]{1,0:T(8,128)(2,1)S(1)} %shard_map.87.after_ref), custom_call_target="tpu_custom_call" | custom-call | bytes 6291456 | tf_op jit(solution)/shard_map/pallas_call | solution.py:216
  31.6 3.0 %shard_map.89.refs_1_ = bf16[768,512]{1,0:T(8,128)(2,1)S(1)} custom-call(s32[8]{0:T(128)S(1)} %copy-done.8, bf16[768,1024]{1,0:T(8,128)(2,1)S(1)} %bitcast.14, bf16[1024,8192]{1,0:T(8,128)(2,1)} %w_ref.29, bf16[768,256]{1,0:T(8,128)(2,1)S(1)} %collective-permute-done.1.refs_1_.refs_0_, bf16[768,256]{1,0:T(8,128)(2,1)} %collective-permute-done.8.refs_1_, ...), custom_call_target="tpu_custom_call" | custom-call | flops 24159191040 | bytes 4194304 | tf_op jit(solution)/shard_map/pallas_call | solution.py:81
  36.2 2.9 %shard_map.91.after_ref = bf16[768,512]{1,0:T(8,128)(2,1)S(1)} custom-call(s32[8]{0:T(128)S(1)} %copy-done.8, bf16[768,1024]{1,0:T(8,128)(2,1)S(1)} %bitcast.15, bf16[1024,8192]{1,0:T(8,128)(2,1)} %w_ref.29, bf16[768,256]{1,0:T(8,128)(2,1)S(1)} %collective-permute-done.2.refs_2_.refs_0_, bf16[768,256]{1,0:T(8,128)(2,1)S(1)} %collective-permute-done.7.refs_1_, ...), custom_call_target="tpu_custom_call" | custom-call | flops 24159191040 | bytes 4194304 | tf_op jit(solution)/shard_map/pallas_call | solution.py:81
  39.7 5.7 %shard_map.92 = (f32[64,384]{1,0:T(8,128)S(1)}, f32[64,384]{1,0:T(8,128)S(1)}) custom-call(s32[24]{0:T(128)S(1)} %compare_convert_fusion.local, s32[24]{0:T(128)S(1)} %get-tuple-element.24.index, s32[1]{0:T(128)} %bitcast.1.side, bf16[768,1024]{1,0:T(8,128)(2,1)S(1)} %bitcast.16, s32[3,256]{1,0:T(4,128)S(1)} %copy-done.6, bf16[96,64,1024]{2,1,0:T(8,128)(2,1)} %table_ref.6, ...), custom_call_target="tpu_custom_call" | custom-call | flops 12079595520 | bytes 4718592 | tf_op jit(solution)/shard_map/pallas_call | solution.py:287
  47.2 2.8 %shard_map.94.refs_1_ = bf16[768,512]{1,0:T(8,128)(2,1)S(1)} custom-call(s32[8]{0:T(128)S(1)} %copy-done.8, bf16[768,1024]{1,0:T(8,128)(2,1)S(1)} %bitcast.17, bf16[1024,8192]{1,0:T(8,128)(2,1)} %w_ref.29, bf16[768,512]{1,0:T(8,128)(2,1)S(1)} %collective-permute-done.5.refs_0_, f32[8,128]{1,0:T(8,128)S(1)} %shard_map.93.refs_1_), custom_call_target="tpu_custom_call" | custom-call | flops 24159191040 | bytes 4194304 | tf_op jit(solution)/shard_map/pallas_call | solution.py:81
  51.7 2.8 %shard_map.95.after_ref = bf16[768,512]{1,0:T(8,128)(2,1)S(1)} custom-call(s32[8]{0:T(128)S(1)} %copy-done.8, bf16[768,1024]{1,0:T(8,128)(2,1)S(1)} %bitcast.18, bf16[1024,8192]{1,0:T(8,128)(2,1)} %w_ref.29, bf16[768,512]{1,0:T(8,128)(2,1)S(1)} %collective-permute-done.4.refs_0_, bf16[768,512]{1,0:T(8,128)(2,1)S(1)} %shard_map.94.refs_1_), custom_call_target="tpu_custom_call" | custom-call | flops 24159191040 | bytes 4194304 | tf_op jit(solution)/shard_map/pallas_call | solution.py:81
  54.9 7.1 %shard_map.96 = (f32[768,1024]{1,0:T(8,128)S(1)}, bf16[24,64,1024]{2,1,0:T(8,128)(2,1)S(1)}) custom-call(s32[24]{0:T(128)S(1)} %compare_convert_fusion.local, s32[24]{0:T(128)S(1)} %get-tuple-element.24.index, s32[8]{0:T(128)S(1)} %copy-done.8, bf16[768,1024]{1,0:T(8,128)(2,1)S(1)} %bitcast.19, bf16[1024,8192]{1,0:T(8,128)(2,1)} %w_ref.29, ...), custom_call_target="tpu_custom_call" | custom-call | flops 48318382080 | bytes 13107200 | tf_op jit(solution)/shard_map/pallas_call | solution.py:346
  66.3 2.8 %shard_map.99.refs_1_ = bf16[768,512]{1,0:T(8,128)(2,1)S(1)} custom-call(s32[8]{0:T(128)S(1)} %copy-done.8, bf16[768,1024]{1,0:T(8,128)(2,1)S(1)} %bitcast.20, bf16[1024,8192]{1,0:T(8,128)(2,1)} %w_ref.29, bf16[768,512]{1,0:T(8,128)(2,1)S(1)} %collective-permute-done.12.refs_0_, f32[64,384]{1,0:T(8,128)S(1)} %shard_map.98.refs_1_.low_ref), custom_call_target="tpu_custom_call" | custom-call | flops 24159191040 | bytes 4194304 | tf_op jit(solution)/shard_map/pallas_call | solution.py:81
  70.8 2.8 %shard_map.100.refs_0_.after_ref = bf16[768,512]{1,0:T(8,128)(2,1)S(1)} custom-call(s32[8]{0:T(128)S(1)} %copy-done.8, bf16[768,1024]{1,0:T(8,128)(2,1)S(1)} %bitcast.21, bf16[1024,8192]{1,0:T(8,128)(2,1)} %w_ref.29, bf16[768,512]{1,0:T(8,128)(2,1)S(1)} %collective-permute-done.11.refs_0_, bf16[768,512]{1,0:T(8,128)(2,1)S(1)} %shard_map.99.refs_1_), custom_call_target="tpu_custom_call" | custom-call | flops 24159191040 | bytes 4194304 | tf_op jit(solution)/shard_map/pallas_call | solution.py:81
  74.5 9.1 %collective-permute-done.10 = f16[64,384]{1,0:T(8,128)(2,1)S(1)} collective-permute-done((f16[64,384]{1,0:T(8,128)(2,1)S(1)}, f16[64,384]{1,0:T(8,128)(2,1)S(1)}, u32[]{:S(2)}, u32[]{:S(2)}) %collective-permute-start.10) | collective-permute-done | bytes 49184 | tf_op jit(solution)/shard_map/ppermute | solution.py:553
  84.3 2.6 %collective-permute-start.13 = (f16[64,384]{1,0:T(8,128)(2,1)S(1)}, f16[64,384]{1,0:T(8,128)(2,1)S(1)}, u32[]{:S(2)}, u32[]{:S(2)}) collective-permute-start(f16[64,384]{1,0:T(8,128)(2,1)S(1)} %multiply_convert_fusion), channel_id=1, source_target_pairs={{0,4},{1,5},{2,6},{3,7},{4,0},{5,1},{6,2},{7,3},{8,12},{9,13},{10,... | collective-permute-start | bytes 147464 | tf_op jit(solution)/shard_map/ppermute | solution.py:553
  86.9 2.8 %shard_map.103.refs_1_ = bf16[768,512]{1,0:T(8,128)(2,1)S(1)} custom-call(s32[8]{0:T(128)S(1)} %copy-done.8, bf16[768,1024]{1,0:T(8,128)(2,1)S(1)} %bitcast.22, bf16[1024,8192]{1,0:T(8,128)(2,1)} %w_ref.29, bf16[768,512]{1,0:T(8,128)(2,1)S(1)} %collective-permute-done.15.refs_0_, f32[64,384]{1,0:T(8,128)S(1)} %shard_map.102.refs_1_.low_ref), custom_call_target="tpu_custom_call" | custom-call | flops 24159191040 | bytes 4194304 | tf_op jit(solution)/shard_map/pallas_call | solution.py:81
  89.7 2.8 %shard_map.104.refs_0_.after_ref = bf16[768,512]{1,0:T(8,128)(2,1)S(1)} custom-call(s32[8]{0:T(128)S(1)} %copy-done.8, bf16[768,1024]{1,0:T(8,128)(2,1)S(1)} %bitcast.23, bf16[1024,8192]{1,0:T(8,128)(2,1)} %w_ref.29, bf16[768,512]{1,0:T(8,128)(2,1)S(1)} %collective-permute-done.14.refs_0_, bf16[768,512]{1,0:T(8,128)(2,1)S(1)} %shard_map.103.refs_1_), custom_call_target="tpu_custom_call" | custom-call | flops 24159191040 | bytes 4194304 | tf_op jit(solution)/shard_map/pallas_call | solution.py:81
  95.1 6.9 %collective-permute-done.13 = f16[64,384]{1,0:T(8,128)(2,1)S(1)} collective-permute-done((f16[64,384]{1,0:T(8,128)(2,1)S(1)}, f16[64,384]{1,0:T(8,128)(2,1)S(1)}, u32[]{:S(2)}, u32[]{:S(2)}) %collective-permute-start.13) | collective-permute-done | bytes 49184 | tf_op jit(solution)/shard_map/ppermute | solution.py:553
  102.8 2.8 %shard_map.107.refs_1_ = bf16[768,512]{1,0:T(8,128)(2,1)S(1)} custom-call(s32[8]{0:T(128)S(1)} %copy-done.8, bf16[768,1024]{1,0:T(8,128)(2,1)S(1)} %bitcast.24, bf16[1024,8192]{1,0:T(8,128)(2,1)} %w_ref.29, bf16[768,512]{1,0:T(8,128)(2,1)S(1)} %collective-permute-done.18.refs_0_, bf16[64,384]{1,0:T(8,128)(2,1)S(1)} %shard_map.106.refs_1_.low_ref), custom_call_target="tpu_custom_call" | custom-call | flops 24159191040 | bytes 4194304 | tf_op jit(solution)/shard_map/pallas_call | solution.py:81
  107.7 2.8 %shard_map.108.after_ref = bf16[768,512]{1,0:T(8,128)(2,1)S(1)} custom-call(s32[8]{0:T(128)S(1)} %copy-done.8, bf16[768,1024]{1,0:T(8,128)(2,1)S(1)} %bitcast.25, bf16[1024,8192]{1,0:T(8,128)(2,1)} %w_ref.29, bf16[768,512]{1,0:T(8,128)(2,1)S(1)} %collective-permute-done.17.refs_0_, bf16[768,512]{1,0:T(8,128)(2,1)S(1)} %shard_map.107.refs_1_), custom_call_target="tpu_custom_call" | custom-call | flops 24159191040 | bytes 4194304 | tf_op jit(solution)/shard_map/pallas_call | solution.py:81
  110.8 5.9 %collective-permute-done.16.other_ref = bf16[64,384]{1,0:T(8,128)(2,1)S(1)} collective-permute-done((bf16[64,384]{1,0:T(8,128)(2,1)S(1)}, bf16[64,384]{1,0:T(8,128)(2,1)S(1)}, u32[]{:S(2)}, u32[]{:S(2)}) %collective-permute-start.16) | collective-permute-done | bytes 49184 | tf_op jit(solution)/shard_map/ppermute | solution.py:553
  118.7 12.7 %collective-permute-done.21.left_ref = bf16[768,512]{1,0:T(8,128)(2,1)S(1)} collective-permute-done((bf16[768,512]{1,0:T(8,128)(2,1)S(1)}, bf16[768,512]{1,0:T(8,128)(2,1)S(1)}, u32[]{:S(2)}, u32[]{:S(2)}) %collective-permute-start.21) | collective-permute-done | bytes 786464 | tf_op jit(solution)/shard_map/ppermute | solution.py:519
  (96 shorter events, 33.8 us)
Async XLA Ops:
  0.0 15.6 %copy-start = (s32[192]{0:T(256)S(1)}, s32[192]{0:T(256)}, u32[]{:S(2)}) copy-start(s32[192]{0:T(256)} %param.12) | copy-start | bytes 2308
  0.0 15.4 %collective-permute-start = (s32[3,2,4]{2,1,0:T(2,128)}, s32[3,2,4]{2,1,0:T(2,128)S(1)}, u32[]{:S(2)}, u32[]{:S(2)}) collective-permute-start(s32[3,2,4]{2,1,0:T(2,128)} %param.13), channel_id=1, source_target_pairs={{0,8},{8,0},{1,9},{9,1},{2,10},{10,2},{3,11},{11,3},{4,12},{12,4},... | collective-permute-start | bytes 296 | tf_op jit(solution)/shard_map/ppermute | solution.py:525
  6.4 12.8 %collective-permute-start.1 = (bf16[768,256]{1,0:T(8,128)(2,1)}, bf16[768,256]{1,0:T(8,128)(2,1)S(1)}, u32[]{:S(2)}, u32[]{:S(2)}) collective-permute-start(bf16[768,256]{1,0:T(8,128)(2,1)} %get-tuple-element.16), channel_id=1, source_target_pairs={{0,2},{2,4},{4,6},{6,7},{7,5},{5,3},{3,1},{1,0},{8,10},{10,12},{12... | collective-permute-start | bytes 1179656 | tf_op jit(solution)/shard_map/ppermute | solution.py:534
  9.0 12.2 %collective-permute-start.2 = (bf16[768,256]{1,0:T(8,128)(2,1)}, bf16[768,256]{1,0:T(8,128)(2,1)S(1)}, u32[]{:S(2)}, u32[]{:S(2)}) collective-permute-start(bf16[768,256]{1,0:T(8,128)(2,1)} %get-tuple-element.17), channel_id=1, source_target_pairs={{0,1},{2,0},{4,2},{6,4},{7,6},{5,7},{3,5},{1,3},{8,9},{10,8},{12,1... | collective-permute-start | bytes 1179656 | tf_op jit(solution)/shard_map/ppermute | solution.py:534
  13.3 18.2 %collective-permute-start.8 = (bf16[768,256]{1,0:T(8,128)(2,1)}, bf16[768,256]{1,0:T(8,128)(2,1)}, u32[]{:S(2)}, u32[]{:S(2)}) collective-permute-start(bf16[768,256]{1,0:T(8,128)(2,1)} %get-tuple-element.18), channel_id=1, source_target_pairs={{0,2},{2,4},{4,6},{6,7},{7,5},{5,3},{3,1},{1,0},{8,10},{10,12},{12... | collective-permute-start | bytes 1179656 | tf_op jit(solution)/shard_map/ppermute | solution.py:534
  15.3 20.9 %collective-permute-start.7 = (bf16[768,256]{1,0:T(8,128)(2,1)S(1)}, bf16[768,256]{1,0:T(8,128)(2,1)S(1)}, u32[]{:S(2)}, u32[]{:S(2)}) collective-permute-start(bf16[768,256]{1,0:T(8,128)(2,1)S(1)} %get-tuple-element.15.after_ref), channel_id=1, source_target_pairs={{0,1},{2,0},{4,2},{6,4},{7,6},{5,7},{3,5},{1,3},{8,9},{10,8},{12,1... | collective-permute-start | bytes 1179656 | tf_op jit(solution)/shard_map/ppermute | solution.py:534
  19.1 15.5 %collective-permute-start.6 = (bf16[24,64,1024]{2,1,0:T(8,128)(2,1)S(1)}, bf16[24,64,1024]{2,1,0:T(8,128)(2,1)S(1)}, u32[]{:S(2)}, u32[]{:S(2)}) collective-permute-start(bf16[24,64,1024]{2,1,0:T(8,128)(2,1)S(1)} %shard_map.84.refs_0_), channel_id=1, source_target_pairs={{0,8},{8,0},{1,9},{9,1},{2,10},{10,2},{3,11},{11,3},{4,12},{12,4},... | collective-permute-start | bytes 9437192 | tf_op jit(solution)/shard_map/ppermute | solution.py:540
  26.7 20.5 %collective-permute-start.5 = (bf16[768,512]{1,0:T(8,128)(2,1)S(1)}, bf16[768,512]{1,0:T(8,128)(2,1)S(1)}, u32[]{:S(2)}, u32[]{:S(2)}) collective-permute-start(bf16[768,512]{1,0:T(8,128)(2,1)S(1)} %shard_map.86.refs_0_), channel_id=1, source_target_pairs={{0,2},{2,4},{4,6},{6,7},{7,5},{5,3},{3,1},{1,0},{8,10},{10,12},{12... | collective-permute-start | bytes 2359304 | tf_op jit(solution)/shard_map/ppermute | solution.py:519
  28.3 23.3 %collective-permute-start.4 = (bf16[768,512]{1,0:T(8,128)(2,1)S(1)}, bf16[768,512]{1,0:T(8,128)(2,1)S(1)}, u32[]{:S(2)}, u32[]{:S(2)}) collective-permute-start(bf16[768,512]{1,0:T(8,128)(2,1)S(1)} %shard_map.87.after_ref), channel_id=1, source_target_pairs={{0,1},{2,0},{4,2},{6,4},{7,6},{5,7},{3,5},{1,3},{8,9},{10,8},{12,1... | collective-permute-start | bytes 2359304 | tf_op jit(solution)/shard_map/ppermute | solution.py:519
  31.5 13.9 %collective-permute-start.3 = (bf16[24,64,1024]{2,1,0:T(8,128)(2,1)S(1)}, bf16[24,64,1024]{2,1,0:T(8,128)(2,1)S(1)}, u32[]{:S(2)}, u32[]{:S(2)}) collective-permute-start(bf16[24,64,1024]{2,1,0:T(8,128)(2,1)S(1)} %shard_map.88.refs_2_), channel_id=1, source_target_pairs={{0,8},{8,0},{1,9},{9,1},{2,10},{10,2},{3,11},{11,3},{4,12},{12,4},... | collective-permute-start | bytes 9437192 | tf_op jit(solution)/shard_map/ppermute | solution.py:544
  34.6 31.7 %collective-permute-start.12 = (bf16[768,512]{1,0:T(8,128)(2,1)S(1)}, bf16[768,512]{1,0:T(8,128)(2,1)S(1)}, u32[]{:S(2)}, u32[]{:S(2)}) collective-permute-start(bf16[768,512]{1,0:T(8,128)(2,1)S(1)} %shard_map.89.refs_1_), channel_id=1, source_target_pairs={{0,2},{2,4},{4,6},{6,7},{7,5},{5,3},{3,1},{1,0},{8,10},{10,12},{12... | collective-permute-start | bytes 2359304 | tf_op jit(solution)/shard_map/ppermute | solution.py:519
  39.2 31.6 %collective-permute-start.11 = (bf16[768,512]{1,0:T(8,128)(2,1)S(1)}, bf16[768,512]{1,0:T(8,128)(2,1)S(1)}, u32[]{:S(2)}, u32[]{:S(2)}) collective-permute-start(bf16[768,512]{1,0:T(8,128)(2,1)S(1)} %shard_map.91.after_ref), channel_id=1, source_target_pairs={{0,1},{2,0},{4,2},{6,4},{7,6},{5,7},{3,5},{1,3},{8,9},{10,8},{12,1... | collective-permute-start | bytes 2359304 | tf_op jit(solution)/shard_map/ppermute | solution.py:519
  45.4 19.8 %collective-permute-start.9 = (f16[64,384]{1,0:T(8,128)(2,1)S(1)}, f16[64,384]{1,0:T(8,128)(2,1)S(1)}, u32[]{:S(2)}, u32[]{:S(2)}) collective-permute-start(f16[64,384]{1,0:T(8,128)(2,1)S(1)} %multiply_convert_fusion.2), channel_id=1, source_target_pairs={{0,1},{1,0},{2,3},{3,2},{4,5},{5,4},{6,7},{7,6},{8,9},{9,8},{10,11... | collective-permute-start | bytes 147464 | tf_op jit(solution)/shard_map/ppermute | solution.py:553
  50.0 36.9 %collective-permute-start.15 = (bf16[768,512]{1,0:T(8,128)(2,1)S(1)}, bf16[768,512]{1,0:T(8,128)(2,1)S(1)}, u32[]{:S(2)}, u32[]{:S(2)}) collective-permute-start(bf16[768,512]{1,0:T(8,128)(2,1)S(1)} %shard_map.94.refs_1_), channel_id=1, source_target_pairs={{0,2},{2,4},{4,6},{6,7},{7,5},{5,3},{3,1},{1,0},{8,10},{10,12},{12... | collective-permute-start | bytes 2359304 | tf_op jit(solution)/shard_map/ppermute | solution.py:519
  54.4 35.2 %collective-permute-start.14 = (bf16[768,512]{1,0:T(8,128)(2,1)S(1)}, bf16[768,512]{1,0:T(8,128)(2,1)S(1)}, u32[]{:S(2)}, u32[]{:S(2)}) collective-permute-start(bf16[768,512]{1,0:T(8,128)(2,1)S(1)} %shard_map.95.after_ref), channel_id=1, source_target_pairs={{0,1},{2,0},{4,2},{6,4},{7,6},{5,7},{3,5},{1,3},{8,9},{10,8},{12,1... | collective-permute-start | bytes 2359304 | tf_op jit(solution)/shard_map/ppermute | solution.py:519
  65.9 17.7 %collective-permute-start.10 = (f16[64,384]{1,0:T(8,128)(2,1)S(1)}, f16[64,384]{1,0:T(8,128)(2,1)S(1)}, u32[]{:S(2)}, u32[]{:S(2)}) collective-permute-start(f16[64,384]{1,0:T(8,128)(2,1)S(1)} %multiply_convert_fusion.1), channel_id=1, source_target_pairs={{0,2},{1,3},{2,0},{3,1},{4,6},{5,7},{6,4},{7,5},{8,10},{9,11},{10,... | collective-permute-start | bytes 147464 | tf_op jit(solution)/shard_map/ppermute | solution.py:553
  69.1 33.7 %collective-permute-start.18 = (bf16[768,512]{1,0:T(8,128)(2,1)S(1)}, bf16[768,512]{1,0:T(8,128)(2,1)S(1)}, u32[]{:S(2)}, u32[]{:S(2)}) collective-permute-start(bf16[768,512]{1,0:T(8,128)(2,1)S(1)} %shard_map.99.refs_1_), channel_id=1, source_target_pairs={{0,2},{2,4},{4,6},{6,7},{7,5},{5,3},{3,1},{1,0},{8,10},{10,12},{12... | collective-permute-start | bytes 2359304 | tf_op jit(solution)/shard_map/ppermute | solution.py:519
  73.6 34.1 %collective-permute-start.17 = (bf16[768,512]{1,0:T(8,128)(2,1)S(1)}, bf16[768,512]{1,0:T(8,128)(2,1)S(1)}, u32[]{:S(2)}, u32[]{:S(2)}) collective-permute-start(bf16[768,512]{1,0:T(8,128)(2,1)S(1)} %shard_map.100.refs_0_.after_ref), channel_id=1, source_target_pairs={{0,1},{2,0},{4,2},{6,4},{7,6},{5,7},{3,5},{1,3},{8,9},{10,8},{12,1... | collective-permute-start | bytes 2359304 | tf_op jit(solution)/shard_map/ppermute | solution.py:519
  84.3 17.7 %collective-permute-start.13 = (f16[64,384]{1,0:T(8,128)(2,1)S(1)}, f16[64,384]{1,0:T(8,128)(2,1)S(1)}, u32[]{:S(2)}, u32[]{:S(2)}) collective-permute-start(f16[64,384]{1,0:T(8,128)(2,1)S(1)} %multiply_convert_fusion), channel_id=1, source_target_pairs={{0,4},{1,5},{2,6},{3,7},{4,0},{5,1},{6,2},{7,3},{8,12},{9,13},{10,... | collective-permute-start | bytes 147464 | tf_op jit(solution)/shard_map/ppermute | solution.py:553
  92.5 25.9 %collective-permute-start.19 = (bf16[768,512]{1,0:T(8,128)(2,1)S(1)}, bf16[768,512]{1,0:T(8,128)(2,1)S(1)}, u32[]{:S(2)}, u32[]{:S(2)}) collective-permute-start(bf16[768,512]{1,0:T(8,128)(2,1)S(1)} %shard_map.104.refs_0_.after_ref), channel_id=1, source_target_pairs={{0,1},{2,0},{4,2},{6,4},{7,6},{5,7},{3,5},{1,3},{8,9},{10,8},{12,1... | collective-permute-start | bytes 2359304 | tf_op jit(solution)/shard_map/ppermute | solution.py:519
  92.5 25.8 %collective-permute-start.20 = (bf16[768,512]{1,0:T(8,128)(2,1)S(1)}, bf16[768,512]{1,0:T(8,128)(2,1)S(1)}, u32[]{:S(2)}, u32[]{:S(2)}) collective-permute-start(bf16[768,512]{1,0:T(8,128)(2,1)S(1)} %shard_map.103.refs_1_), channel_id=1, source_target_pairs={{0,2},{2,4},{4,6},{6,7},{7,5},{5,3},{3,1},{1,0},{8,10},{10,12},{12... | collective-permute-start | bytes 2359304 | tf_op jit(solution)/shard_map/ppermute | solution.py:519
  102.7 14.1 %collective-permute-start.16 = (bf16[64,384]{1,0:T(8,128)(2,1)S(1)}, bf16[64,384]{1,0:T(8,128)(2,1)S(1)}, u32[]{:S(2)}, u32[]{:S(2)}) collective-permute-start(bf16[64,384]{1,0:T(8,128)(2,1)S(1)} %shard_map.106.refs_1_.low_ref), channel_id=1, source_target_pairs={{0,1},{1,0},{2,3},{3,2},{4,5},{5,4},{6,7},{7,6},{8,9},{9,8},{10,11... | collective-permute-start | bytes 147464 | tf_op jit(solution)/shard_map/ppermute | solution.py:553
  105.6 25.8 %collective-permute-start.21 = (bf16[768,512]{1,0:T(8,128)(2,1)S(1)}, bf16[768,512]{1,0:T(8,128)(2,1)S(1)}, u32[]{:S(2)}, u32[]{:S(2)}) collective-permute-start(bf16[768,512]{1,0:T(8,128)(2,1)S(1)} %shard_map.107.refs_1_), channel_id=1, source_target_pairs={{0,2},{2,4},{4,6},{6,7},{7,5},{5,3},{3,1},{1,0},{8,10},{10,12},{12... | collective-permute-start | bytes 2359304 | tf_op jit(solution)/shard_map/ppermute | solution.py:519
  110.4 22.5 %collective-permute-start.22 = (bf16[768,512]{1,0:T(8,128)(2,1)S(1)}, bf16[768,512]{1,0:T(8,128)(2,1)S(1)}, u32[]{:S(2)}, u32[]{:S(2)}) collective-permute-start(bf16[768,512]{1,0:T(8,128)(2,1)S(1)} %shard_map.108.after_ref), channel_id=1, source_target_pairs={{0,1},{2,0},{4,2},{6,4},{7,6},{5,7},{3,5},{1,3},{8,9},{10,8},{12,1... | collective-permute-start | bytes 2359304 | tf_op jit(solution)/shard_map/ppermute | solution.py:519
  (12 other events, 84.5 us)

commit v15 on v13

--- a/solution.py
+++ b/solution.py
@@ -8,7 +8,6 @@
 from jax.sharding import PartitionSpec as P
 
 VMEM_LIMIT = 40 * 1024 * 1024
-FIRST_VMEM_LIMIT = 62 * 1024 * 1024
 LOW_SCALE = 16.0
 GRAIN = 16
 SWAP = [(0, 1), (1, 0)]
@@ -38,8 +37,8 @@
     return list(range(0, size, 2)) + list(range(size - 1, 0, -2))
 
 
-def params(limit=VMEM_LIMIT):
-    return pltpu.CompilerParams(vmem_limit_bytes=limit)
+def params():
+    return pltpu.CompilerParams(vmem_limit_bytes=VMEM_LIMIT)
 
 
 def cost(flops, size):
@@ -129,7 +128,7 @@
             num_scalar_prefetch=1,
             grid=(2,),
             in_specs=[
-                pl.BlockSpec((rows, depth), lambda j, d: (0, 0)) if after is None else WHOLE,
+                WHOLE,
                 pl.BlockSpec((depth, tile), place),
             ]
             + [ANYWHERE] * len(tail),
@@ -137,7 +136,7 @@
         ),
         out_shape=[jax.ShapeDtypeStruct((rows, tile), jnp.bfloat16)] * 2
         + [jax.ShapeDtypeStruct((8, 128), jnp.float32)],
-        compiler_params=params(FIRST_VMEM_LIMIT if after is None else VMEM_LIMIT),
+        compiler_params=params(),
         cost_estimate=cost(
             4 * rows * depth * tile, 2 * (rows * depth + 2 * depth * tile + 2 * rows * tile)
         ),
@@ -486,7 +485,7 @@
             )
             arrived[half, sign] = [lax.ppermute(last, "tp", moves)]
             if between is not None:
-                last, between = touch(between, last), None
+                last, between = touch(*between, last), None
         return last
 
     ids = block_adapter_ids.reshape(-1)
@@ -502,8 +501,7 @@
     local = (pages[: ids.shape[0]] // resident == instance).astype(jnp.int32)
     last = collect(index_there, adapter_down_weight, last)
     got_down = lax.ppermute(last, "inst", SWAP)
-    last = touch(last, *(arrived[half, sign][0] for half, sign, _ in pairs[0]))
-    last = turn(1, last)
+    last = turn(1, last, [arrived[half, sign][0] for half, sign, _ in pairs[0]])
     side = (lax.axis_index("tp") & 1).reshape(1)
     low, give = low_rank(
         sizes, local, index, side, x, row_list_position, adapter_down_weight, got_down, last

time: 135 us -> 135 us (level)
    ppermute x12, waiting for transfers between devices: 15.2 us -> 17.3 us  [turn(): arrived[half, sign] = [lax.ppermute(last, 'tp', moves)]]
    ppermute x4, waiting for transfers between devices: 1.84 us -> 0.01 us  [per_device(): arrived.setdefault((half, sign), []).append(lax.ppermute(part, 'tp', moves))]
  transfers between devices with their start and end apart: 23 -> 23, of which waited for: 6 -> 5; matrix products, arithmetic and copies ran while one was open for 5% -> 5% of each run, Pallas kernels for 47% -> 47%
where the time goes in v15:
time: 135 us; the launch traced here: 134 us
  Pallas kernels  64 us (47%)
  waiting for transfers between devices  36.1 us (27%)
  starting transfers between devices  25 us (19%)
  local copies, waits for them, and re-layouts  5.13 us (4%)
  other arithmetic  3.53 us (3%)
    pallas_call x12, Pallas kernels, hop(): pl.pallas_call(functools.partial(hop_kernel, tuple(range(len(received))))...  33.9 us
    ppermute x4, waiting for transfers between devices, over(): return lax.ppermute(value, 'tp', [(i, i ^ apart) for i in range(size)])  18.7 us
    ppermute x12, waiting for transfers between devices, turn(): arrived[half, sign] = [lax.ppermute(last, 'tp', moves)]  17.3 us
    ppermute x12, starting transfers between devices, turn(): arrived[half, sign] = [lax.ppermute(last, 'tp', moves)]  13.2 us
    pallas_call x1, Pallas kernels, own_terms(): pl.pallas_call(own_kernel, grid_spec=pltpu.PrefetchScalarGridSpec(num_sca...  7.43 us
    pallas_call x2, Pallas kernels, first_pieces(): pl.pallas_call(functools.partial(first_kernel, after is not None), grid_s...  7.27 us
    ppermute x4, starting transfers between devices, over(): return lax.ppermute(value, 'tp', [(i, i ^ apart) for i in range(size)])  6.73 us
    pallas_call x1, Pallas kernels, low_rank(): pl.pallas_call(functools.partial(low_kernel, sizes), grid_spec=pltpu.Pref...  6.02 us
  transfers between devices with their start and end apart: 23, of which 5 were waited for; matrix products, arithmetic and copies ran while one was open for 5% of the time, Pallas kernels for 47%

profile of v15, /device:TPU:0, one launch (start us, length us, event | category | flops | bytes accessed | tf_op | source)
XLA Modules:
  0.0 134.2 jit_solution(2932942068682986459)
XLA Ops:
  1.9 3.7 %shard_map.82 = (bf16[768,256]{1,0:T(8,128)(2,1)}, bf16[768,256]{1,0:T(8,128)(2,1)}, f32[8,128]{1,0:T(8,128)S(1)}) custom-call(s32[8]{0:T(128)S(1)} %compare_select_fusion.3.dests, bf16[768,1024]{1,0:T(8,128)(2,1)S(1)} %bitcast.11, bf16[1024,8192]{1,0:T(8,128)(2,1)} %w_ref.29), custom_call_target="tpu_custom_call" | custom-call | flops 24159191040 | bytes 3407872 | tf_op jit(solution)/shard_map/pallas_call | solution.py:125
  5.6 2.5 %collective-permute-start.1 = (bf16[768,256]{1,0:T(8,128)(2,1)}, bf16[768,256]{1,0:T(8,128)(2,1)S(1)}, u32[]{:S(2)}, u32[]{:S(2)}) collective-permute-start(bf16[768,256]{1,0:T(8,128)(2,1)} %get-tuple-element.15), channel_id=1, source_target_pairs={{0,1},{2,0},{4,2},{6,4},{7,6},{5,7},{3,5},{1,3},{8,9},{10,8},{12,1... | collective-permute-start | bytes 1179656 | tf_op jit(solution)/shard_map/ppermute | solution.py:497
  8.2 3.6 %shard_map.83 = (bf16[768,256]{1,0:T(8,128)(2,1)}, bf16[768,256]{1,0:T(8,128)(2,1)S(1)}, f32[8,128]{1,0:T(8,128)S(1)}) custom-call(s32[8]{0:T(128)S(1)} %compare_select_fusion.3.dests, bf16[768,1024]{1,0:T(8,128)(2,1)S(1)} %bitcast.12, bf16[1024,8192]{1,0:T(8,128)(2,1)} %w_ref.29, f32[8,128]{1,0:T(8,128)S(1)} %get-tuple-element.16.refs_0_), custom_call_target="tpu_custom_call" | custom-call | flops 24159191040 | bytes 3407872 | tf_op jit(solution)/shard_map/pallas_call | solution.py:125
  14.9 2.7 %shard_map.84.refs_0_ = bf16[24,64,1024]{2,1,0:T(8,128)(2,1)S(1)} custom-call(s32[24]{0:T(128)S(1)} %get-tuple-element.25.index, bf16[96,64,1024]{2,1,0:T(8,128)(2,1)} %table_ref.5, f32[8,128]{1,0:T(8,128)S(1)} %get-tuple-element.20.after_ref), custom_call_target="tpu_custom_call" | custom-call | bytes 6291456 | tf_op jit(solution)/shard_map/pallas_call | solution.py:174
  17.7 2.8 %shard_map.85.refs_2_ = bf16[768,512]{1,0:T(8,128)(2,1)S(1)} custom-call(s32[8]{0:T(128)S(1)} %compare_select_fusion.3.dests, bf16[768,1024]{1,0:T(8,128)(2,1)S(1)} %bitcast.13, bf16[1024,8192]{1,0:T(8,128)(2,1)} %w_ref.29, bf16[24,64,1024]{2,1,0:T(8,128)(2,1)S(1)} %shard_map.84.refs_0_), custom_call_target="tpu_custom_call" | custom-call | flops 24159191040 | bytes 4194304 | tf_op jit(solution)/shard_map/pallas_call | solution.py:80
  22.6 2.8 %shard_map.87.after_ref = bf16[768,512]{1,0:T(8,128)(2,1)S(1)} custom-call(s32[8]{0:T(128)S(1)} %compare_select_fusion.3.dests, bf16[768,1024]{1,0:T(8,128)(2,1)S(1)} %bitcast.14, bf16[1024,8192]{1,0:T(8,128)(2,1)} %w_ref.29, f32[8,128]{1,0:T(8,128)S(1)} %shard_map.86.refs_0_), custom_call_target="tpu_custom_call" | custom-call | flops 24159191040 | bytes 4194304 | tf_op jit(solution)/shard_map/pallas_call | solution.py:80
  25.5 6.0 %shard_map.88 = (f32[64,384]{1,0:T(8,128)S(1)}, f32[64,384]{1,0:T(8,128)S(1)}) custom-call(s32[24]{0:T(128)S(1)} %compare_convert_fusion.local, s32[24]{0:T(128)S(1)} %get-tuple-element.26.index, s32[1]{0:T(128)} %bitcast.1.side, bf16[768,1024]{1,0:T(8,128)(2,1)S(1)} %bitcast.15, s32[3,256]{1,0:T(4,128)S(1)} %copy-done.9, bf16[96,64,1024]{2,1,0:T(8,128)(2,1)} %table_ref.5, ...), custom_call_target="tpu_custom_call" | custom-call | flops 12079595520 | bytes 4718592 | tf_op jit(solution)/shard_map/pallas_call | solution.py:245
  33.6 3.0 %shard_map.89.refs_2_ = bf16[768,512]{1,0:T(8,128)(2,1)S(1)} custom-call(s32[8]{0:T(128)S(1)} %compare_select_fusion.3.dests, bf16[768,1024]{1,0:T(8,128)(2,1)S(1)} %bitcast.16, bf16[1024,8192]{1,0:T(8,128)(2,1)} %w_ref.29, bf16[768,256]{1,0:T(8,128)(2,1)S(1)} %collective-permute-done.3.refs_0_, bf16[768,256]{1,0:T(8,128)(2,1)S(1)} %collective-permute-done.4.refs_1_, ...), custom_call_target="tpu_custom_call" | custom-call | flops 24159191040 | bytes 4194304 | tf_op jit(solution)/shard_map/pallas_call | solution.py:80
  38.2 3.0 %shard_map.90.refs_0_.after_ref = bf16[768,512]{1,0:T(8,128)(2,1)S(1)} custom-call(s32[8]{0:T(128)S(1)} %compare_select_fusion.3.dests, bf16[768,1024]{1,0:T(8,128)(2,1)S(1)} %bitcast.17, bf16[1024,8192]{1,0:T(8,128)(2,1)} %w_ref.29, bf16[768,256]{1,0:T(8,128)(2,1)S(1)} %collective-permute-done.1.refs_1_.refs_0_, ...), custom_call_target="tpu_custom_call" | custom-call | flops 24159191040 | bytes 4194304 | tf_op jit(solution)/shard_map/pallas_call | solution.py:80
  42.1 4.5 %collective-permute-done.8 = f16[64,384]{1,0:T(8,128)(2,1)S(1)} collective-permute-done((f16[64,384]{1,0:T(8,128)(2,1)S(1)}, f16[64,384]{1,0:T(8,128)(2,1)S(1)}, u32[]{:S(2)}, u32[]{:S(2)}) %collective-permute-start.8) | collective-permute-done | bytes 49184 | tf_op jit(solution)/shard_map/ppermute | solution.py:512
  47.4 2.8 %shard_map.93.refs_1_ = bf16[768,512]{1,0:T(8,128)(2,1)S(1)} custom-call(s32[8]{0:T(128)S(1)} %compare_select_fusion.3.dests, bf16[768,1024]{1,0:T(8,128)(2,1)S(1)} %bitcast.18, bf16[1024,8192]{1,0:T(8,128)(2,1)} %w_ref.29, bf16[768,512]{1,0:T(8,128)(2,1)S(1)} %collective-permute-done.11.refs_0_, f32[64,384]{1,0:T(8,128)S(1)} %shard_map.92.refs_1_.low_ref), custom_call_target="tpu_custom_call" | custom-call | flops 24159191040 | bytes 4194304 | tf_op jit(solution)/shard_map/pallas_call | solution.py:80
  52.3 2.8 %shard_map.94.refs_0_.after_ref = bf16[768,512]{1,0:T(8,128)(2,1)S(1)} custom-call(s32[8]{0:T(128)S(1)} %compare_select_fusion.3.dests, bf16[768,1024]{1,0:T(8,128)(2,1)S(1)} %bitcast.19, bf16[1024,8192]{1,0:T(8,128)(2,1)} %w_ref.29, bf16[768,512]{1,0:T(8,128)(2,1)S(1)} %collective-permute-done.10.refs_0_, bf16[768,512]{1,0:T(8,128)(2,1)S(1)} %shard_map.93.refs_1_), custom_call_target="tpu_custom_call" | custom-call | flops 24159191040 | bytes 4194304 | tf_op jit(solution)/shard_map/pallas_call | solution.py:80
  55.6 8.1 %collective-permute-done.9 = f16[64,384]{1,0:T(8,128)(2,1)S(1)} collective-permute-done((f16[64,384]{1,0:T(8,128)(2,1)S(1)}, f16[64,384]{1,0:T(8,128)(2,1)S(1)}, u32[]{:S(2)}, u32[]{:S(2)}) %collective-permute-start.9) | collective-permute-done | bytes 49184 | tf_op jit(solution)/shard_map/ppermute | solution.py:512
  65.1 2.6 %collective-permute-start.15 = (f16[64,384]{1,0:T(8,128)(2,1)}, f16[64,384]{1,0:T(8,128)(2,1)}, u32[]{:S(2)}, u32[]{:S(2)}) collective-permute-start(f16[64,384]{1,0:T(8,128)(2,1)} %multiply_convert_fusion), channel_id=1, source_target_pairs={{0,4},{1,5},{2,6},{3,7},{4,0},{5,1},{6,2},{7,3},{8,12},{9,13},{10,... | collective-permute-start | bytes 147464 | tf_op jit(solution)/shard_map/ppermute | solution.py:512
  67.7 2.8 %shard_map.97.refs_1_ = bf16[768,512]{1,0:T(8,128)(2,1)S(1)} custom-call(s32[8]{0:T(128)S(1)} %compare_select_fusion.3.dests, bf16[768,1024]{1,0:T(8,128)(2,1)S(1)} %bitcast.20, bf16[1024,8192]{1,0:T(8,128)(2,1)} %w_ref.29, bf16[768,512]{1,0:T(8,128)(2,1)S(1)} %collective-permute-done.7.refs_0_, f32[64,384]{1,0:T(8,128)S(1)} %shard_map.96.refs_1_.low_ref), custom_call_target="tpu_custom_call" | custom-call | flops 24159191040 | bytes 4194304 | tf_op jit(solution)/shard_map/pallas_call | solution.py:80
  70.7 2.8 %shard_map.98.after_ref = bf16[768,512]{1,0:T(8,128)(2,1)S(1)} custom-call(s32[8]{0:T(128)S(1)} %compare_select_fusion.3.dests, bf16[768,1024]{1,0:T(8,128)(2,1)S(1)} %bitcast.21, bf16[1024,8192]{1,0:T(8,128)(2,1)} %w_ref.29, bf16[768,512]{1,0:T(8,128)(2,1)S(1)} %collective-permute-done.6.refs_0_, bf16[768,512]{1,0:T(8,128)(2,1)S(1)} %shard_map.97.refs_1_), custom_call_target="tpu_custom_call" | custom-call | flops 24159191040 | bytes 4194304 | tf_op jit(solution)/shard_map/pallas_call | solution.py:80
  75.4 2.7 %shard_map.99.refs_1_ = bf16[24,64,1024]{2,1,0:T(8,128)(2,1)S(1)} custom-call(s32[24]{0:T(128)S(1)} %copy-done.3, bf16[96,64,1024]{2,1,0:T(8,128)(2,1)} %table_ref.7, bf16[768,512]{1,0:T(8,128)(2,1)S(1)} %shard_map.98.after_ref), custom_call_target="tpu_custom_call" | custom-call | bytes 6291456 | tf_op jit(solution)/shard_map/pallas_call | solution.py:174
  80.3 2.8 %shard_map.100.refs_1_ = bf16[768,512]{1,0:T(8,128)(2,1)S(1)} custom-call(s32[8]{0:T(128)S(1)} %compare_select_fusion.3.dests, bf16[768,1024]{1,0:T(8,128)(2,1)S(1)} %bitcast.22, bf16[1024,8192]{1,0:T(8,128)(2,1)} %w_ref.29, bf16[768,512]{1,0:T(8,128)(2,1)S(1)} %collective-permute-done.14.refs_0_, bf16[24,64,1024]{2,1,0:T(8,128)(2,1)S(1)} %shard_map.99.refs_1_), custom_call_target="tpu_custom_call" | custom-call | flops 24159191040 | bytes 4194304 | tf_op jit(solution)/shard_map/pallas_call | solution.py:80
  83.2 2.8 %shard_map.101.after_ref = bf16[768,512]{1,0:T(8,128)(2,1)S(1)} custom-call(s32[8]{0:T(128)S(1)} %compare_select_fusion.3.dests, bf16[768,1024]{1,0:T(8,128)(2,1)S(1)} %bitcast.23, bf16[1024,8192]{1,0:T(8,128)(2,1)} %w_ref.29, bf16[768,512]{1,0:T(8,128)(2,1)S(1)} %collective-permute-done.13.refs_0_, bf16[768,512]{1,0:T(8,128)(2,1)S(1)} %shard_map.100.refs_1_), custom_call_target="tpu_custom_call" | custom-call | flops 24159191040 | bytes 4194304 | tf_op jit(solution)/shard_map/pallas_call | solution.py:80
  88.5 7.4 %shard_map.102 = (f32[768,1024]{1,0:T(8,128)S(1)}, bf16[24,64,1024]{2,1,0:T(8,128)(2,1)S(1)}) custom-call(s32[24]{0:T(128)S(1)} %compare_convert_fusion.local, s32[24]{0:T(128)S(1)} %copy-done.6, s32[8]{0:T(128)S(1)} %compare_select_fusion.3.dests, bf16[768,1024]{1,0:T(8,128)(2,1)S(1)} %bitcast.24, bf16[1024,8192]{1,0:T(8,128)(2,1)} %w_ref.29, ...), custom_call_target="tpu_custom_call" | custom-call | flops 48318382080 | bytes 13107200 | tf_op jit(solution)/shard_map/pallas_call | solution.py:304
  101.2 2.8 %shard_map.105.refs_1_ = bf16[768,512]{1,0:T(8,128)(2,1)S(1)} custom-call(s32[8]{0:T(128)S(1)} %compare_select_fusion.3.dests, bf16[768,1024]{1,0:T(8,128)(2,1)S(1)} %bitcast.25, bf16[1024,8192]{1,0:T(8,128)(2,1)} %w_ref.29, bf16[768,512]{1,0:T(8,128)(2,1)S(1)} %collective-permute-done.18.refs_0_, bf16[64,384]{1,0:T(8,128)(2,1)S(1)} %shard_map.104.refs_1_.low_ref), custom_call_target="tpu_custom_call" | custom-call | flops 24159191040 | bytes 4194304 | tf_op jit(solution)/shard_map/pallas_call | solution.py:80
  104.3 2.9 %shard_map.106.after_ref = bf16[768,512]{1,0:T(8,128)(2,1)S(1)} custom-call(s32[8]{0:T(128)S(1)} %compare_select_fusion.3.dests, bf16[768,1024]{1,0:T(8,128)(2,1)S(1)} %bitcast.26, bf16[1024,8192]{1,0:T(8,128)(2,1)} %w_ref.29, bf16[768,512]{1,0:T(8,128)(2,1)S(1)} %collective-permute-done.17.refs_0_, bf16[768,512]{1,0:T(8,128)(2,1)S(1)} %shard_map.105.refs_1_), custom_call_target="tpu_custom_call" | custom-call | flops 24159191040 | bytes 4194304 | tf_op jit(solution)/shard_map/pallas_call | solution.py:80
  108.9 6.2 %collective-permute-done.16.other_ref = bf16[64,384]{1,0:T(8,128)(2,1)S(1)} collective-permute-done((bf16[64,384]{1,0:T(8,128)(2,1)S(1)}, bf16[64,384]{1,0:T(8,128)(2,1)S(1)}, u32[]{:S(2)}, u32[]{:S(2)}) %collective-permute-start.16) | collective-permute-done | bytes 49184 | tf_op jit(solution)/shard_map/ppermute | solution.py:512
  116.1 15.1 %collective-permute-done.22.last_ref = bf16[768,512]{1,0:T(8,128)(2,1)S(1)} collective-permute-done((bf16[768,512]{1,0:T(8,128)(2,1)S(1)}, bf16[768,512]{1,0:T(8,128)(2,1)S(1)}, u32[]{:S(2)}, u32[]{:S(2)}) %collective-permute-start.22) | collective-permute-done | bytes 786464 | tf_op jit(solution)/shard_map/ppermute | solution.py:486
  (97 shorter events, 34.9 us)
Async XLA Ops:
  0.0 13.9 %collective-permute-start = (s32[3,2,4]{2,1,0:T(2,128)}, s32[3,2,4]{2,1,0:T(2,128)S(1)}, u32[]{:S(2)}, u32[]{:S(2)}) collective-permute-start(s32[3,2,4]{2,1,0:T(2,128)} %param.13), channel_id=1, source_target_pairs={{0,8},{8,0},{1,9},{9,1},{2,10},{10,2},{3,11},{11,3},{4,12},{12,4},... | collective-permute-start | bytes 296 | tf_op jit(solution)/shard_map/ppermute | solution.py:492
  5.6 15.0 %collective-permute-start.1 = (bf16[768,256]{1,0:T(8,128)(2,1)}, bf16[768,256]{1,0:T(8,128)(2,1)S(1)}, u32[]{:S(2)}, u32[]{:S(2)}) collective-permute-start(bf16[768,256]{1,0:T(8,128)(2,1)} %get-tuple-element.15), channel_id=1, source_target_pairs={{0,1},{2,0},{4,2},{6,4},{7,6},{5,7},{3,5},{1,3},{8,9},{10,8},{12,1... | collective-permute-start | bytes 1179656 | tf_op jit(solution)/shard_map/ppermute | solution.py:497
  8.1 14.5 %collective-permute-start.3 = (bf16[768,256]{1,0:T(8,128)(2,1)}, bf16[768,256]{1,0:T(8,128)(2,1)S(1)}, u32[]{:S(2)}, u32[]{:S(2)}) collective-permute-start(bf16[768,256]{1,0:T(8,128)(2,1)} %get-tuple-element.18), channel_id=1, source_target_pairs={{0,2},{2,4},{4,6},{6,7},{7,5},{5,3},{3,1},{1,0},{8,10},{10,12},{12... | collective-permute-start | bytes 1179656 | tf_op jit(solution)/shard_map/ppermute | solution.py:497
  11.7 21.8 %collective-permute-start.4 = (bf16[768,256]{1,0:T(8,128)(2,1)}, bf16[768,256]{1,0:T(8,128)(2,1)S(1)}, u32[]{:S(2)}, u32[]{:S(2)}) collective-permute-start(bf16[768,256]{1,0:T(8,128)(2,1)} %get-tuple-element.19), channel_id=1, source_target_pairs={{0,2},{2,4},{4,6},{6,7},{7,5},{5,3},{3,1},{1,0},{8,10},{10,12},{12... | collective-permute-start | bytes 1179656 | tf_op jit(solution)/shard_map/ppermute | solution.py:497
  13.8 24.4 %collective-permute-start.2 = (bf16[768,256]{1,0:T(8,128)(2,1)S(1)}, bf16[768,256]{1,0:T(8,128)(2,1)S(1)}, u32[]{:S(2)}, u32[]{:S(2)}) collective-permute-start(bf16[768,256]{1,0:T(8,128)(2,1)S(1)} %get-tuple-element.17), channel_id=1, source_target_pairs={{0,1},{2,0},{4,2},{6,4},{7,6},{5,7},{3,5},{1,3},{8,9},{10,8},{12,1... | collective-permute-start | bytes 1179656 | tf_op jit(solution)/shard_map/ppermute | solution.py:497
  17.6 7.9 %collective-permute-start.5 = (bf16[24,64,1024]{2,1,0:T(8,128)(2,1)S(1)}, bf16[24,64,1024]{2,1,0:T(8,128)(2,1)S(1)}, u32[]{:S(2)}, u32[]{:S(2)}) collective-permute-start(bf16[24,64,1024]{2,1,0:T(8,128)(2,1)S(1)} %shard_map.84.refs_0_), channel_id=1, source_target_pairs={{0,8},{8,0},{1,9},{9,1},{2,10},{10,2},{3,11},{11,3},{4,12},{12,4},... | collective-permute-start | bytes 9437192 | tf_op jit(solution)/shard_map/ppermute | solution.py:503
  20.5 26.9 %collective-permute-start.11 = (bf16[768,512]{1,0:T(8,128)(2,1)S(1)}, bf16[768,512]{1,0:T(8,128)(2,1)S(1)}, u32[]{:S(2)}, u32[]{:S(2)}) collective-permute-start(bf16[768,512]{1,0:T(8,128)(2,1)S(1)} %shard_map.85.refs_2_), channel_id=1, source_target_pairs={{0,2},{2,4},{4,6},{6,7},{7,5},{5,3},{3,1},{1,0},{8,10},{10,12},{12... | collective-permute-start | bytes 2359304 | tf_op jit(solution)/shard_map/ppermute | solution.py:486
  25.4 26.8 %collective-permute-start.10 = (bf16[768,512]{1,0:T(8,128)(2,1)S(1)}, bf16[768,512]{1,0:T(8,128)(2,1)S(1)}, u32[]{:S(2)}, u32[]{:S(2)}) collective-permute-start(bf16[768,512]{1,0:T(8,128)(2,1)S(1)} %shard_map.87.after_ref), channel_id=1, source_target_pairs={{0,1},{2,0},{4,2},{6,4},{7,6},{5,7},{3,5},{1,3},{8,9},{10,8},{12,1... | collective-permute-start | bytes 2359304 | tf_op jit(solution)/shard_map/ppermute | solution.py:486
  31.6 15.0 %collective-permute-start.8 = (f16[64,384]{1,0:T(8,128)(2,1)S(1)}, f16[64,384]{1,0:T(8,128)(2,1)S(1)}, u32[]{:S(2)}, u32[]{:S(2)}) collective-permute-start(f16[64,384]{1,0:T(8,128)(2,1)S(1)} %multiply_convert_fusion.2), channel_id=1, source_target_pairs={{0,1},{1,0},{2,3},{3,2},{4,5},{5,4},{6,7},{7,6},{8,9},{9,8},{10,11... | collective-permute-start | bytes 147464 | tf_op jit(solution)/shard_map/ppermute | solution.py:512
  36.5 31.1 %collective-permute-start.7 = (bf16[768,512]{1,0:T(8,128)(2,1)S(1)}, bf16[768,512]{1,0:T(8,128)(2,1)S(1)}, u32[]{:S(2)}, u32[]{:S(2)}) collective-permute-start(bf16[768,512]{1,0:T(8,128)(2,1)S(1)} %shard_map.89.refs_2_), channel_id=1, source_target_pairs={{0,2},{2,4},{4,6},{6,7},{7,5},{5,3},{3,1},{1,0},{8,10},{10,12},{12... | collective-permute-start | bytes 2359304 | tf_op jit(solution)/shard_map/ppermute | solution.py:486
  41.1 29.6 %collective-permute-start.6 = (bf16[768,512]{1,0:T(8,128)(2,1)S(1)}, bf16[768,512]{1,0:T(8,128)(2,1)S(1)}, u32[]{:S(2)}, u32[]{:S(2)}) collective-permute-start(bf16[768,512]{1,0:T(8,128)(2,1)S(1)} %shard_map.90.refs_0_.after_ref), channel_id=1, source_target_pairs={{0,1},{2,0},{4,2},{6,4},{7,6},{5,7},{3,5},{1,3},{8,9},{10,8},{12,1... | collective-permute-start | bytes 2359304 | tf_op jit(solution)/shard_map/ppermute | solution.py:486
  47.3 16.4 %collective-permute-start.9 = (f16[64,384]{1,0:T(8,128)(2,1)S(1)}, f16[64,384]{1,0:T(8,128)(2,1)S(1)}, u32[]{:S(2)}, u32[]{:S(2)}) collective-permute-start(f16[64,384]{1,0:T(8,128)(2,1)S(1)} %multiply_convert_fusion.1), channel_id=1, source_target_pairs={{0,2},{1,3},{2,0},{3,1},{4,6},{5,7},{6,4},{7,5},{8,10},{9,11},{10,... | collective-permute-start | bytes 147464 | tf_op jit(solution)/shard_map/ppermute | solution.py:512
  50.2 30.1 %collective-permute-start.14 = (bf16[768,512]{1,0:T(8,128)(2,1)S(1)}, bf16[768,512]{1,0:T(8,128)(2,1)S(1)}, u32[]{:S(2)}, u32[]{:S(2)}) collective-permute-start(bf16[768,512]{1,0:T(8,128)(2,1)S(1)} %shard_map.93.refs_1_), channel_id=1, source_target_pairs={{0,2},{2,4},{4,6},{6,7},{7,5},{5,3},{3,1},{1,0},{8,10},{10,12},{12... | collective-permute-start | bytes 2359304 | tf_op jit(solution)/shard_map/ppermute | solution.py:486
  55.1 28.1 %collective-permute-start.13 = (bf16[768,512]{1,0:T(8,128)(2,1)S(1)}, bf16[768,512]{1,0:T(8,128)(2,1)S(1)}, u32[]{:S(2)}, u32[]{:S(2)}) collective-permute-start(bf16[768,512]{1,0:T(8,128)(2,1)S(1)} %shard_map.94.refs_0_.after_ref), channel_id=1, source_target_pairs={{0,1},{2,0},{4,2},{6,4},{7,6},{5,7},{3,5},{1,3},{8,9},{10,8},{12,1... | collective-permute-start | bytes 2359304 | tf_op jit(solution)/shard_map/ppermute | solution.py:486
  65.1 31.5 %collective-permute-start.15 = (f16[64,384]{1,0:T(8,128)(2,1)}, f16[64,384]{1,0:T(8,128)(2,1)}, u32[]{:S(2)}, u32[]{:S(2)}) collective-permute-start(f16[64,384]{1,0:T(8,128)(2,1)} %multiply_convert_fusion), channel_id=1, source_target_pairs={{0,4},{1,5},{2,6},{3,7},{4,0},{5,1},{6,2},{7,3},{8,12},{9,13},{10,... | collective-permute-start | bytes 147464 | tf_op jit(solution)/shard_map/ppermute | solution.py:512
  70.5 30.7 %collective-permute-start.18 = (bf16[768,512]{1,0:T(8,128)(2,1)S(1)}, bf16[768,512]{1,0:T(8,128)(2,1)S(1)}, u32[]{:S(2)}, u32[]{:S(2)}) collective-permute-start(bf16[768,512]{1,0:T(8,128)(2,1)S(1)} %shard_map.97.refs_1_), channel_id=1, source_target_pairs={{0,2},{2,4},{4,6},{6,7},{7,5},{5,3},{3,1},{1,0},{8,10},{10,12},{12... | collective-permute-start | bytes 2359304 | tf_op jit(solution)/shard_map/ppermute | solution.py:486
  73.5 30.7 %collective-permute-start.17 = (bf16[768,512]{1,0:T(8,128)(2,1)S(1)}, bf16[768,512]{1,0:T(8,128)(2,1)S(1)}, u32[]{:S(2)}, u32[]{:S(2)}) collective-permute-start(bf16[768,512]{1,0:T(8,128)(2,1)S(1)} %shard_map.98.after_ref), channel_id=1, source_target_pairs={{0,1},{2,0},{4,2},{6,4},{7,6},{5,7},{3,5},{1,3},{8,9},{10,8},{12,1... | collective-permute-start | bytes 2359304 | tf_op jit(solution)/shard_map/ppermute | solution.py:486
  80.3 5.7 %collective-permute-start.12 = (bf16[24,64,1024]{2,1,0:T(8,128)(2,1)S(1)}, bf16[24,64,1024]{2,1,0:T(8,128)(2,1)S(1)}, u32[]{:S(2)}, u32[]{:S(2)}) collective-permute-start(bf16[24,64,1024]{2,1,0:T(8,128)(2,1)S(1)} %shard_map.99.refs_1_), channel_id=1, source_target_pairs={{0,8},{8,0},{1,9},{9,1},{2,10},{10,2},{3,11},{11,3},{4,12},{12,4},... | collective-permute-start | bytes 9437192 | tf_op jit(solution)/shard_map/ppermute | solution.py:523
  83.1 32.6 %collective-permute-start.20 = (bf16[768,512]{1,0:T(8,128)(2,1)S(1)}, bf16[768,512]{1,0:T(8,128)(2,1)S(1)}, u32[]{:S(2)}, u32[]{:S(2)}) collective-permute-start(bf16[768,512]{1,0:T(8,128)(2,1)S(1)} %shard_map.100.refs_1_), channel_id=1, source_target_pairs={{0,2},{2,4},{4,6},{6,7},{7,5},{5,3},{3,1},{1,0},{8,10},{10,12},{12... | collective-permute-start | bytes 2359304 | tf_op jit(solution)/shard_map/ppermute | solution.py:486
  86.0 29.7 %collective-permute-start.19 = (bf16[768,512]{1,0:T(8,128)(2,1)S(1)}, bf16[768,512]{1,0:T(8,128)(2,1)S(1)}, u32[]{:S(2)}, u32[]{:S(2)}) collective-permute-start(bf16[768,512]{1,0:T(8,128)(2,1)S(1)} %shard_map.101.after_ref), channel_id=1, source_target_pairs={{0,1},{2,0},{4,2},{6,4},{7,6},{5,7},{3,5},{1,3},{8,9},{10,8},{12,1... | collective-permute-start | bytes 2359304 | tf_op jit(solution)/shard_map/ppermute | solution.py:486
  99.1 16.0 %collective-permute-start.16 = (bf16[64,384]{1,0:T(8,128)(2,1)S(1)}, bf16[64,384]{1,0:T(8,128)(2,1)S(1)}, u32[]{:S(2)}, u32[]{:S(2)}) collective-permute-start(bf16[64,384]{1,0:T(8,128)(2,1)S(1)} %shard_map.104.refs_1_.low_ref), channel_id=1, source_target_pairs={{0,1},{1,0},{2,3},{3,2},{4,5},{5,4},{6,7},{7,6},{8,9},{9,8},{10,11... | collective-permute-start | bytes 147464 | tf_op jit(solution)/shard_map/ppermute | solution.py:512
  104.0 27.2 %collective-permute-start.22 = (bf16[768,512]{1,0:T(8,128)(2,1)S(1)}, bf16[768,512]{1,0:T(8,128)(2,1)S(1)}, u32[]{:S(2)}, u32[]{:S(2)}) collective-permute-start(bf16[768,512]{1,0:T(8,128)(2,1)S(1)} %shard_map.105.refs_1_), channel_id=1, source_target_pairs={{0,2},{2,4},{4,6},{6,7},{7,5},{5,3},{3,1},{1,0},{8,10},{10,12},{12... | collective-permute-start | bytes 2359304 | tf_op jit(solution)/shard_map/ppermute | solution.py:486
  107.2 25.6 %collective-permute-start.21 = (bf16[768,512]{1,0:T(8,128)(2,1)S(1)}, bf16[768,512]{1,0:T(8,128)(2,1)S(1)}, u32[]{:S(2)}, u32[]{:S(2)}) collective-permute-start(bf16[768,512]{1,0:T(8,128)(2,1)S(1)} %shard_map.106.after_ref), channel_id=1, source_target_pairs={{0,1},{2,0},{4,2},{6,4},{7,6},{5,7},{3,5},{1,3},{8,9},{10,8},{12,1... | collective-permute-start | bytes 2359304 | tf_op jit(solution)/shard_map/ppermute | solution.py:486
  115.7 15.5 %copy-start.4 = (s32[3,1]{0,1:T(1,128)S(1)}, s32[3,1]{0,1:T(1,128)}, u32[]{:S(2)}) copy-start(s32[3,1]{0,1:T(1,128)} %param.15) | copy-start | bytes 40
  (13 other events, 77.2 us)

commit v16 on v12

--- a/solution.py
+++ b/solution.py
@@ -8,7 +8,7 @@
 from jax.sharding import PartitionSpec as P
 
 VMEM_LIMIT = 40 * 1024 * 1024
-FIRST_VMEM_LIMIT = 62 * 1024 * 1024
+FIRST_VMEM_LIMIT = 52 * 1024 * 1024
 LOW_SCALE = 16.0
 GRAIN = 16
 SWAP = [(0, 1), (1, 0)]

time: 134 us -> 136 us (1.015)
  Pallas kernels: 65.5 us -> 63 us
    ppermute x4, waiting for transfers between devices: 1.92 us -> 0.01 us  [per_device(): arrived.setdefault((half, sign), []).append(lax.ppermute(part, 'tp', moves))]
    ppermute x4, waiting for transfers between devices: 22.8 us -> 24.6 us  [over(): return lax.ppermute(value, 'tp', [(i, i ^ apart) for i in range(size)])]
  transfers between devices with their start and end apart: 23 -> 23, of which waited for: 8 -> 7; matrix products, arithmetic and copies ran while one was open for 4% -> 6% of each run, Pallas kernels for 48% -> 45%
where the time goes in v16:
time: 136 us; the launch traced here: 135 us
  Pallas kernels  63 us (46%)
  waiting for transfers between devices  40.3 us (30%)
  starting transfers between devices  23.5 us (17%)
  local copies, waits for them, and re-layouts  4.43 us (3%)
  other arithmetic  3.42 us (3%)
    pallas_call x12, Pallas kernels, hop(): pl.pallas_call(functools.partial(hop_kernel, tuple(range(len(received))))...  33.7 us
    ppermute x4, waiting for transfers between devices, over(): return lax.ppermute(value, 'tp', [(i, i ^ apart) for i in range(size)])  24.6 us
    ppermute x12, waiting for transfers between devices, turn(): arrived[half, sign] = [lax.ppermute(last, 'tp', moves)]  15.7 us
    ppermute x12, starting transfers between devices, turn(): arrived[half, sign] = [lax.ppermute(last, 'tp', moves)]  13 us
    pallas_call x2, Pallas kernels, first_pieces(): pl.pallas_call(functools.partial(first_kernel, after is not None), grid_s...  7.84 us
    pallas_call x1, Pallas kernels, own_terms(): pl.pallas_call(own_kernel, grid_spec=pltpu.PrefetchScalarGridSpec(num_sca...  6.76 us
    pallas_call x1, Pallas kernels, low_rank(): pl.pallas_call(functools.partial(low_kernel, sizes), grid_spec=pltpu.Pref...  5.39 us
    pallas_call x2, Pallas kernels, collect(): pl.pallas_call(functools.partial(collect_kernel, count), grid_spec=pltpu....  5.36 us
  transfers between devices with their start and end apart: 23, of which 7 were waited for; matrix products, arithmetic and copies ran while one was open for 6% of the time, Pallas kernels for 45%

profile of v16, /device:TPU:0, one launch (start us, length us, event | category | flops | bytes accessed | tf_op | source)
XLA Modules:
  0.0 135.2 jit_solution(13342878650307786536)
XLA Ops:
  0.5 4.3 %shard_map.82 = (bf16[768,256]{1,0:T(8,128)(2,1)}, bf16[768,256]{1,0:T(8,128)(2,1)}, f32[8,128]{1,0:T(8,128)S(1)}) custom-call(s32[8]{0:T(128)S(1)} %compare_select_fusion.3.dests, bf16[768,1024]{1,0:T(8,128)(2,1)} %bitcast.11, bf16[1024,8192]{1,0:T(8,128)(2,1)} %w_ref.29), custom_call_target="tpu_custom_call" | custom-call | flops 24159191040 | bytes 3407872 | tf_op jit(solution)/shard_map/pallas_call | solution.py:126
  7.3 3.6 %shard_map.83 = (bf16[768,256]{1,0:T(8,128)(2,1)}, bf16[768,256]{1,0:T(8,128)(2,1)S(1)}, f32[8,128]{1,0:T(8,128)S(1)}) custom-call(s32[8]{0:T(128)S(1)} %compare_select_fusion.3.dests, bf16[768,1024]{1,0:T(8,128)(2,1)S(1)} %bitcast.12, bf16[1024,8192]{1,0:T(8,128)(2,1)} %w_ref.29, f32[8,128]{1,0:T(8,128)S(1)} %get-tuple-element.15.refs_0_), custom_call_target="tpu_custom_call" | custom-call | flops 24159191040 | bytes 3407872 | tf_op jit(solution)/shard_map/pallas_call | solution.py:126
  17.1 2.7 %shard_map.84.refs_0_ = bf16[24,64,1024]{2,1,0:T(8,128)(2,1)S(1)} custom-call(s32[24]{0:T(128)S(1)} %get-tuple-element.25.index, bf16[96,64,1024]{2,1,0:T(8,128)(2,1)} %table_ref.6, f32[8,128]{1,0:T(8,128)S(1)} %get-tuple-element.16.after_ref), custom_call_target="tpu_custom_call" | custom-call | bytes 6291456 | tf_op jit(solution)/shard_map/pallas_call | solution.py:175
  20.0 2.8 %shard_map.86.refs_0_ = bf16[768,512]{1,0:T(8,128)(2,1)S(1)} custom-call(s32[8]{0:T(128)S(1)} %compare_select_fusion.3.dests, bf16[768,1024]{1,0:T(8,128)(2,1)S(1)} %bitcast.13, bf16[1024,8192]{1,0:T(8,128)(2,1)} %w_ref.29, f32[8,128]{1,0:T(8,128)S(1)} %shard_map.85.refs_0_), custom_call_target="tpu_custom_call" | custom-call | flops 24159191040 | bytes 4194304 | tf_op jit(solution)/shard_map/pallas_call | solution.py:81
  22.7 2.8 %shard_map.87.after_ref = bf16[768,512]{1,0:T(8,128)(2,1)S(1)} custom-call(s32[8]{0:T(128)S(1)} %compare_select_fusion.3.dests, bf16[768,1024]{1,0:T(8,128)(2,1)S(1)} %bitcast.14, bf16[1024,8192]{1,0:T(8,128)(2,1)} %w_ref.29, bf16[768,512]{1,0:T(8,128)(2,1)S(1)} %shard_map.86.refs_0_), custom_call_target="tpu_custom_call" | custom-call | flops 24159191040 | bytes 4194304 | tf_op jit(solution)/shard_map/pallas_call | solution.py:81
  27.6 2.7 %shard_map.88.refs_2_ = bf16[24,64,1024]{2,1,0:T(8,128)(2,1)S(1)} custom-call(s32[24]{0:T(128)S(1)} %get-tuple-element.25.index, bf16[96,64,1024]{2,1,0:T(8,128)(2,1)} %table_ref.7, bf16[768,512]{1,0:T(8,128)(2,1)S(1)} %shard_map.87.after_ref), custom_call_target="tpu_custom_call" | custom-call | bytes 6291456 | tf_op jit(solution)/shard_map/pallas_call | solution.py:175
  30.6 2.9 %shard_map.89.refs_1_ = bf16[768,512]{1,0:T(8,128)(2,1)S(1)} custom-call(s32[8]{0:T(128)S(1)} %compare_select_fusion.3.dests, bf16[768,1024]{1,0:T(8,128)(2,1)S(1)} %bitcast.15, bf16[1024,8192]{1,0:T(8,128)(2,1)} %w_ref.29, bf16[768,256]{1,0:T(8,128)(2,1)S(1)} %collective-permute-done.1.refs_1_.refs_0_, bf16[768,256]{1,0:T(8,128)(2,1)S(1)} %collective-permute-done.8.refs_1_, ...), custom_call_target="tpu_custom_call" | custom-call | flops 24159191040 | bytes 4194304 | tf_op jit(solution)/shard_map/pallas_call | solution.py:81
  35.4 2.9 %shard_map.91.after_ref = bf16[768,512]{1,0:T(8,128)(2,1)S(1)} custom-call(s32[8]{0:T(128)S(1)} %compare_select_fusion.3.dests, bf16[768,1024]{1,0:T(8,128)(2,1)S(1)} %bitcast.16, bf16[1024,8192]{1,0:T(8,128)(2,1)} %w_ref.29, bf16[768,256]{1,0:T(8,128)(2,1)S(1)} %collective-permute-done.2.refs_2_.refs_0_, ...), custom_call_target="tpu_custom_call" | custom-call | flops 24159191040 | bytes 4194304 | tf_op jit(solution)/shard_map/pallas_call | solution.py:81
  38.6 5.4 %shard_map.92 = (f32[64,384]{1,0:T(8,128)S(1)}, f32[64,384]{1,0:T(8,128)S(1)}) custom-call(s32[24]{0:T(128)S(1)} %compare_convert_fusion.local, s32[24]{0:T(128)S(1)} %get-tuple-element.26.index, s32[1]{0:T(128)} %bitcast.1.side, bf16[768,1024]{1,0:T(8,128)(2,1)S(1)} %bitcast.17, s32[3,256]{1,0:T(4,128)S(1)} %copy-done.6, bf16[96,64,1024]{2,1,0:T(8,128)(2,1)} %table_ref.6, ...), custom_call_target="tpu_custom_call" | custom-call | flops 12079595520 | bytes 4718592 | tf_op jit(solution)/shard_map/pallas_call | solution.py:246
  46.0 2.8 %shard_map.94.refs_1_ = bf16[768,512]{1,0:T(8,128)(2,1)S(1)} custom-call(s32[8]{0:T(128)S(1)} %compare_select_fusion.3.dests, bf16[768,1024]{1,0:T(8,128)(2,1)S(1)} %bitcast.18, bf16[1024,8192]{1,0:T(8,128)(2,1)} %w_ref.29, bf16[768,512]{1,0:T(8,128)(2,1)S(1)} %collective-permute-done.5.refs_0_, f32[8,128]{1,0:T(8,128)S(1)} %shard_map.93.refs_1_), custom_call_target="tpu_custom_call" | custom-call | flops 24159191040 | bytes 4194304 | tf_op jit(solution)/shard_map/pallas_call | solution.py:81
  50.8 2.8 %shard_map.95.after_ref = bf16[768,512]{1,0:T(8,128)(2,1)S(1)} custom-call(s32[8]{0:T(128)S(1)} %compare_select_fusion.3.dests, bf16[768,1024]{1,0:T(8,128)(2,1)S(1)} %bitcast.19, bf16[1024,8192]{1,0:T(8,128)(2,1)} %w_ref.29, bf16[768,512]{1,0:T(8,128)(2,1)S(1)} %collective-permute-done.4.refs_0_, bf16[768,512]{1,0:T(8,128)(2,1)S(1)} %shard_map.94.refs_1_), custom_call_target="tpu_custom_call" | custom-call | flops 24159191040 | bytes 4194304 | tf_op jit(solution)/shard_map/pallas_call | solution.py:81
  53.7 6.8 %shard_map.96 = (f32[768,1024]{1,0:T(8,128)S(1)}, bf16[24,64,1024]{2,1,0:T(8,128)(2,1)S(1)}) custom-call(s32[24]{0:T(128)S(1)} %compare_convert_fusion.local, s32[24]{0:T(128)S(1)} %get-tuple-element.26.index, s32[8]{0:T(128)S(1)} %compare_select_fusion.3.dests, bf16[768,1024]{1,0:T(8,128)(2,1)S(1)} %bitcast.20, bf16[1024,8192]{1,0:T(8,128)(2,1)} %w_ref.29, ...), custom_call_target="tpu_custom_call" | custom-call | flops 48318382080 | bytes 13107200 | tf_op jit(solution)/shard_map/pallas_call | solution.py:305
  61.1 2.8 %collective-permute-done.9 = f16[64,384]{1,0:T(8,128)(2,1)S(1)} collective-permute-done((f16[64,384]{1,0:T(8,128)(2,1)S(1)}, f16[64,384]{1,0:T(8,128)(2,1)S(1)}, u32[]{:S(2)}, u32[]{:S(2)}) %collective-permute-start.9) | collective-permute-done | bytes 49184 | tf_op jit(solution)/shard_map/ppermute | solution.py:517
  65.1 2.8 %shard_map.99.refs_1_ = bf16[768,512]{1,0:T(8,128)(2,1)S(1)} custom-call(s32[8]{0:T(128)S(1)} %compare_select_fusion.3.dests, bf16[768,1024]{1,0:T(8,128)(2,1)S(1)} %bitcast.21, bf16[1024,8192]{1,0:T(8,128)(2,1)} %w_ref.29, bf16[768,512]{1,0:T(8,128)(2,1)S(1)} %collective-permute-done.12.refs_0_, f32[64,384]{1,0:T(8,128)S(1)} %shard_map.98.refs_1_.low_ref), custom_call_target="tpu_custom_call" | custom-call | flops 24159191040 | bytes 4194304 | tf_op jit(solution)/shard_map/pallas_call | solution.py:81
  69.6 2.8 %shard_map.100.refs_0_.after_ref = bf16[768,512]{1,0:T(8,128)(2,1)S(1)} custom-call(s32[8]{0:T(128)S(1)} %compare_select_fusion.3.dests, bf16[768,1024]{1,0:T(8,128)(2,1)S(1)} %bitcast.22, bf16[1024,8192]{1,0:T(8,128)(2,1)} %w_ref.29, bf16[768,512]{1,0:T(8,128)(2,1)S(1)} %collective-permute-done.11.refs_0_, bf16[768,512]{1,0:T(8,128)(2,1)S(1)} %shard_map.99.refs_1_), custom_call_target="tpu_custom_call" | custom-call | flops 24159191040 | bytes 4194304 | tf_op jit(solution)/shard_map/pallas_call | solution.py:81
  73.4 9.4 %collective-permute-done.10 = f16[64,384]{1,0:T(8,128)(2,1)S(1)} collective-permute-done((f16[64,384]{1,0:T(8,128)(2,1)S(1)}, f16[64,384]{1,0:T(8,128)(2,1)S(1)}, u32[]{:S(2)}, u32[]{:S(2)}) %collective-permute-start.10) | collective-permute-done | bytes 49184 | tf_op jit(solution)/shard_map/ppermute | solution.py:517
  83.5 2.7 %collective-permute-start.13 = (f16[64,384]{1,0:T(8,128)(2,1)S(1)}, f16[64,384]{1,0:T(8,128)(2,1)S(1)}, u32[]{:S(2)}, u32[]{:S(2)}) collective-permute-start(f16[64,384]{1,0:T(8,128)(2,1)S(1)} %multiply_convert_fusion), channel_id=1, source_target_pairs={{0,4},{1,5},{2,6},{3,7},{4,0},{5,1},{6,2},{7,3},{8,12},{9,13},{10,... | collective-permute-start | bytes 147464 | tf_op jit(solution)/shard_map/ppermute | solution.py:517
  86.1 2.8 %shard_map.103.refs_1_ = bf16[768,512]{1,0:T(8,128)(2,1)S(1)} custom-call(s32[8]{0:T(128)S(1)} %compare_select_fusion.3.dests, bf16[768,1024]{1,0:T(8,128)(2,1)S(1)} %bitcast.23, bf16[1024,8192]{1,0:T(8,128)(2,1)} %w_ref.29, bf16[768,512]{1,0:T(8,128)(2,1)S(1)} %collective-permute-done.15.refs_0_, f32[64,384]{1,0:T(8,128)S(1)} %shard_map.102.refs_1_.low_ref), custom_call_target="tpu_custom_call" | custom-call | flops 24159191040 | bytes 4194304 | tf_op jit(solution)/shard_map/pallas_call | solution.py:81
  88.9 2.8 %shard_map.104.refs_0_.after_ref = bf16[768,512]{1,0:T(8,128)(2,1)S(1)} custom-call(s32[8]{0:T(128)S(1)} %compare_select_fusion.3.dests, bf16[768,1024]{1,0:T(8,128)(2,1)S(1)} %bitcast.24, bf16[1024,8192]{1,0:T(8,128)(2,1)} %w_ref.29, bf16[768,512]{1,0:T(8,128)(2,1)S(1)} %collective-permute-done.14.refs_0_, bf16[768,512]{1,0:T(8,128)(2,1)S(1)} %shard_map.103.refs_1_), custom_call_target="tpu_custom_call" | custom-call | flops 24159191040 | bytes 4194304 | tf_op jit(solution)/shard_map/pallas_call | solution.py:81
  94.3 6.7 %collective-permute-done.13 = f16[64,384]{1,0:T(8,128)(2,1)S(1)} collective-permute-done((f16[64,384]{1,0:T(8,128)(2,1)S(1)}, f16[64,384]{1,0:T(8,128)(2,1)S(1)}, u32[]{:S(2)}, u32[]{:S(2)}) %collective-permute-start.13) | collective-permute-done | bytes 49184 | tf_op jit(solution)/shard_map/ppermute | solution.py:517
  101.8 2.8 %shard_map.107.refs_1_ = bf16[768,512]{1,0:T(8,128)(2,1)S(1)} custom-call(s32[8]{0:T(128)S(1)} %compare_select_fusion.3.dests, bf16[768,1024]{1,0:T(8,128)(2,1)S(1)} %bitcast.25, bf16[1024,8192]{1,0:T(8,128)(2,1)} %w_ref.29, bf16[768,512]{1,0:T(8,128)(2,1)S(1)} %collective-permute-done.18.refs_0_, bf16[64,384]{1,0:T(8,128)(2,1)S(1)} %shard_map.106.refs_1_.low_ref), custom_call_target="tpu_custom_call" | custom-call | flops 24159191040 | bytes 4194304 | tf_op jit(solution)/shard_map/pallas_call | solution.py:81
  106.9 2.8 %shard_map.108.after_ref = bf16[768,512]{1,0:T(8,128)(2,1)S(1)} custom-call(s32[8]{0:T(128)S(1)} %compare_select_fusion.3.dests, bf16[768,1024]{1,0:T(8,128)(2,1)S(1)} %bitcast.26, bf16[1024,8192]{1,0:T(8,128)(2,1)} %w_ref.29, bf16[768,512]{1,0:T(8,128)(2,1)S(1)} %collective-permute-done.17.refs_0_, bf16[768,512]{1,0:T(8,128)(2,1)S(1)} %shard_map.107.refs_1_), custom_call_target="tpu_custom_call" | custom-call | flops 24159191040 | bytes 4194304 | tf_op jit(solution)/shard_map/pallas_call | solution.py:81
  109.9 5.6 %collective-permute-done.16.other_ref = bf16[64,384]{1,0:T(8,128)(2,1)S(1)} collective-permute-done((bf16[64,384]{1,0:T(8,128)(2,1)S(1)}, bf16[64,384]{1,0:T(8,128)(2,1)S(1)}, u32[]{:S(2)}, u32[]{:S(2)}) %collective-permute-start.16) | collective-permute-done | bytes 49184 | tf_op jit(solution)/shard_map/ppermute | solution.py:517
  117.8 14.3 %collective-permute-done.22.last_ref = bf16[768,512]{1,0:T(8,128)(2,1)S(1)} collective-permute-done((bf16[768,512]{1,0:T(8,128)(2,1)S(1)}, bf16[768,512]{1,0:T(8,128)(2,1)S(1)}, u32[]{:S(2)}, u32[]{:S(2)}) %collective-permute-start.22) | collective-permute-done | bytes 786464 | tf_op jit(solution)/shard_map/ppermute | solution.py:487
  (95 shorter events, 34.1 us)
Async XLA Ops:
  0.0 13.6 %collective-permute-start = (s32[3,2,4]{2,1,0:T(2,128)}, s32[3,2,4]{2,1,0:T(2,128)}, u32[]{:S(2)}, u32[]{:S(2)}) collective-permute-start(s32[3,2,4]{2,1,0:T(2,128)} %param.13), channel_id=1, source_target_pairs={{0,8},{8,0},{1,9},{9,1},{2,10},{10,2},{3,11},{11,3},{4,12},{12,4},... | collective-permute-start | bytes 296 | tf_op jit(solution)/shard_map/ppermute | solution.py:493
  4.7 15.2 %collective-permute-start.1 = (bf16[768,256]{1,0:T(8,128)(2,1)}, bf16[768,256]{1,0:T(8,128)(2,1)S(1)}, u32[]{:S(2)}, u32[]{:S(2)}) collective-permute-start(bf16[768,256]{1,0:T(8,128)(2,1)} %get-tuple-element.17), channel_id=1, source_target_pairs={{0,2},{2,4},{4,6},{6,7},{7,5},{5,3},{3,1},{1,0},{8,10},{10,12},{12... | collective-permute-start | bytes 1179656 | tf_op jit(solution)/shard_map/ppermute | solution.py:498
  7.3 12.6 %collective-permute-start.2 = (bf16[768,256]{1,0:T(8,128)(2,1)}, bf16[768,256]{1,0:T(8,128)(2,1)S(1)}, u32[]{:S(2)}, u32[]{:S(2)}) collective-permute-start(bf16[768,256]{1,0:T(8,128)(2,1)} %get-tuple-element.18), channel_id=1, source_target_pairs={{0,1},{2,0},{4,2},{6,4},{7,6},{5,7},{3,5},{1,3},{8,9},{10,8},{12,1... | collective-permute-start | bytes 1179656 | tf_op jit(solution)/shard_map/ppermute | solution.py:498
  10.9 19.4 %collective-permute-start.8 = (bf16[768,256]{1,0:T(8,128)(2,1)}, bf16[768,256]{1,0:T(8,128)(2,1)S(1)}, u32[]{:S(2)}, u32[]{:S(2)}) collective-permute-start(bf16[768,256]{1,0:T(8,128)(2,1)} %get-tuple-element.20), channel_id=1, source_target_pairs={{0,2},{2,4},{4,6},{6,7},{7,5},{5,3},{3,1},{1,0},{8,10},{10,12},{12... | collective-permute-start | bytes 1179656 | tf_op jit(solution)/shard_map/ppermute | solution.py:498
  12.9 22.5 %collective-permute-start.7 = (bf16[768,256]{1,0:T(8,128)(2,1)S(1)}, bf16[768,256]{1,0:T(8,128)(2,1)S(1)}, u32[]{:S(2)}, u32[]{:S(2)}) collective-permute-start(bf16[768,256]{1,0:T(8,128)(2,1)S(1)} %get-tuple-element.19), channel_id=1, source_target_pairs={{0,1},{2,0},{4,2},{6,4},{7,6},{5,7},{3,5},{1,3},{8,9},{10,8},{12,1... | collective-permute-start | bytes 1179656 | tf_op jit(solution)/shard_map/ppermute | solution.py:498
  19.8 13.7 %collective-permute-start.6 = (bf16[24,64,1024]{2,1,0:T(8,128)(2,1)S(1)}, bf16[24,64,1024]{2,1,0:T(8,128)(2,1)S(1)}, u32[]{:S(2)}, u32[]{:S(2)}) collective-permute-start(bf16[24,64,1024]{2,1,0:T(8,128)(2,1)S(1)} %shard_map.84.refs_0_), channel_id=1, source_target_pairs={{0,8},{8,0},{1,9},{9,1},{2,10},{10,2},{3,11},{11,3},{4,12},{12,4},... | collective-permute-start | bytes 9437192 | tf_op jit(solution)/shard_map/ppermute | solution.py:504
  25.5 20.5 %collective-permute-start.5 = (bf16[768,512]{1,0:T(8,128)(2,1)S(1)}, bf16[768,512]{1,0:T(8,128)(2,1)S(1)}, u32[]{:S(2)}, u32[]{:S(2)}) collective-permute-start(bf16[768,512]{1,0:T(8,128)(2,1)S(1)} %shard_map.86.refs_0_), channel_id=1, source_target_pairs={{0,2},{2,4},{4,6},{6,7},{7,5},{5,3},{3,1},{1,0},{8,10},{10,12},{12... | collective-permute-start | bytes 2359304 | tf_op jit(solution)/shard_map/ppermute | solution.py:487
  27.6 23.2 %collective-permute-start.4 = (bf16[768,512]{1,0:T(8,128)(2,1)S(1)}, bf16[768,512]{1,0:T(8,128)(2,1)S(1)}, u32[]{:S(2)}, u32[]{:S(2)}) collective-permute-start(bf16[768,512]{1,0:T(8,128)(2,1)S(1)} %shard_map.87.after_ref), channel_id=1, source_target_pairs={{0,1},{2,0},{4,2},{6,4},{7,6},{5,7},{3,5},{1,3},{8,9},{10,8},{12,1... | collective-permute-start | bytes 2359304 | tf_op jit(solution)/shard_map/ppermute | solution.py:487
  30.3 13.7 %collective-permute-start.3 = (bf16[24,64,1024]{2,1,0:T(8,128)(2,1)S(1)}, bf16[24,64,1024]{2,1,0:T(8,128)(2,1)S(1)}, u32[]{:S(2)}, u32[]{:S(2)}) collective-permute-start(bf16[24,64,1024]{2,1,0:T(8,128)(2,1)S(1)} %shard_map.88.refs_2_), channel_id=1, source_target_pairs={{0,8},{8,0},{1,9},{9,1},{2,10},{10,2},{3,11},{11,3},{4,12},{12,4},... | collective-permute-start | bytes 9437192 | tf_op jit(solution)/shard_map/ppermute | solution.py:508
  33.5 31.6 %collective-permute-start.12 = (bf16[768,512]{1,0:T(8,128)(2,1)S(1)}, bf16[768,512]{1,0:T(8,128)(2,1)S(1)}, u32[]{:S(2)}, u32[]{:S(2)}) collective-permute-start(bf16[768,512]{1,0:T(8,128)(2,1)S(1)} %shard_map.89.refs_1_), channel_id=1, source_target_pairs={{0,2},{2,4},{4,6},{6,7},{7,5},{5,3},{3,1},{1,0},{8,10},{10,12},{12... | collective-permute-start | bytes 2359304 | tf_op jit(solution)/shard_map/ppermute | solution.py:487
  38.4 31.2 %collective-permute-start.11 = (bf16[768,512]{1,0:T(8,128)(2,1)S(1)}, bf16[768,512]{1,0:T(8,128)(2,1)S(1)}, u32[]{:S(2)}, u32[]{:S(2)}) collective-permute-start(bf16[768,512]{1,0:T(8,128)(2,1)S(1)} %shard_map.91.after_ref), channel_id=1, source_target_pairs={{0,1},{2,0},{4,2},{6,4},{7,6},{5,7},{3,5},{1,3},{8,9},{10,8},{12,1... | collective-permute-start | bytes 2359304 | tf_op jit(solution)/shard_map/ppermute | solution.py:487
  44.1 19.8 %collective-permute-start.9 = (f16[64,384]{1,0:T(8,128)(2,1)S(1)}, f16[64,384]{1,0:T(8,128)(2,1)S(1)}, u32[]{:S(2)}, u32[]{:S(2)}) collective-permute-start(f16[64,384]{1,0:T(8,128)(2,1)S(1)} %multiply_convert_fusion.2), channel_id=1, source_target_pairs={{0,1},{1,0},{2,3},{3,2},{4,5},{5,4},{6,7},{7,6},{8,9},{9,8},{10,11... | collective-permute-start | bytes 147464 | tf_op jit(solution)/shard_map/ppermute | solution.py:517
  48.8 37.3 %collective-permute-start.15 = (bf16[768,512]{1,0:T(8,128)(2,1)S(1)}, bf16[768,512]{1,0:T(8,128)(2,1)S(1)}, u32[]{:S(2)}, u32[]{:S(2)}) collective-permute-start(bf16[768,512]{1,0:T(8,128)(2,1)S(1)} %shard_map.94.refs_1_), channel_id=1, source_target_pairs={{0,2},{2,4},{4,6},{6,7},{7,5},{5,3},{3,1},{1,0},{8,10},{10,12},{12... | collective-permute-start | bytes 2359304 | tf_op jit(solution)/shard_map/ppermute | solution.py:487
  53.6 35.3 %collective-permute-start.14 = (bf16[768,512]{1,0:T(8,128)(2,1)S(1)}, bf16[768,512]{1,0:T(8,128)(2,1)S(1)}, u32[]{:S(2)}, u32[]{:S(2)}) collective-permute-start(bf16[768,512]{1,0:T(8,128)(2,1)S(1)} %shard_map.95.after_ref), channel_id=1, source_target_pairs={{0,1},{2,0},{4,2},{6,4},{7,6},{5,7},{3,5},{1,3},{8,9},{10,8},{12,1... | collective-permute-start | bytes 2359304 | tf_op jit(solution)/shard_map/ppermute | solution.py:487
  64.6 18.1 %collective-permute-start.10 = (f16[64,384]{1,0:T(8,128)(2,1)S(1)}, f16[64,384]{1,0:T(8,128)(2,1)S(1)}, u32[]{:S(2)}, u32[]{:S(2)}) collective-permute-start(f16[64,384]{1,0:T(8,128)(2,1)S(1)} %multiply_convert_fusion.1), channel_id=1, source_target_pairs={{0,2},{1,3},{2,0},{3,1},{4,6},{5,7},{6,4},{7,5},{8,10},{9,11},{10,... | collective-permute-start | bytes 147464 | tf_op jit(solution)/shard_map/ppermute | solution.py:517
  67.9 33.9 %collective-permute-start.18 = (bf16[768,512]{1,0:T(8,128)(2,1)S(1)}, bf16[768,512]{1,0:T(8,128)(2,1)S(1)}, u32[]{:S(2)}, u32[]{:S(2)}) collective-permute-start(bf16[768,512]{1,0:T(8,128)(2,1)S(1)} %shard_map.99.refs_1_), channel_id=1, source_target_pairs={{0,2},{2,4},{4,6},{6,7},{7,5},{5,3},{3,1},{1,0},{8,10},{10,12},{12... | collective-permute-start | bytes 2359304 | tf_op jit(solution)/shard_map/ppermute | solution.py:487
  72.4 34.5 %collective-permute-start.17 = (bf16[768,512]{1,0:T(8,128)(2,1)S(1)}, bf16[768,512]{1,0:T(8,128)(2,1)S(1)}, u32[]{:S(2)}, u32[]{:S(2)}) collective-permute-start(bf16[768,512]{1,0:T(8,128)(2,1)S(1)} %shard_map.100.refs_0_.after_ref), channel_id=1, source_target_pairs={{0,1},{2,0},{4,2},{6,4},{7,6},{5,7},{3,5},{1,3},{8,9},{10,8},{12,1... | collective-permute-start | bytes 2359304 | tf_op jit(solution)/shard_map/ppermute | solution.py:487
  83.5 17.6 %collective-permute-start.13 = (f16[64,384]{1,0:T(8,128)(2,1)S(1)}, f16[64,384]{1,0:T(8,128)(2,1)S(1)}, u32[]{:S(2)}, u32[]{:S(2)}) collective-permute-start(f16[64,384]{1,0:T(8,128)(2,1)S(1)} %multiply_convert_fusion), channel_id=1, source_target_pairs={{0,4},{1,5},{2,6},{3,7},{4,0},{5,1},{6,2},{7,3},{8,12},{9,13},{10,... | collective-permute-start | bytes 147464 | tf_op jit(solution)/shard_map/ppermute | solution.py:517
  91.7 25.8 %collective-permute-start.19 = (bf16[768,512]{1,0:T(8,128)(2,1)S(1)}, bf16[768,512]{1,0:T(8,128)(2,1)S(1)}, u32[]{:S(2)}, u32[]{:S(2)}) collective-permute-start(bf16[768,512]{1,0:T(8,128)(2,1)S(1)} %shard_map.104.refs_0_.after_ref), channel_id=1, source_target_pairs={{0,1},{2,0},{4,2},{6,4},{7,6},{5,7},{3,5},{1,3},{8,9},{10,8},{12,1... | collective-permute-start | bytes 2359304 | tf_op jit(solution)/shard_map/ppermute | solution.py:487
  91.8 25.7 %collective-permute-start.20 = (bf16[768,512]{1,0:T(8,128)(2,1)S(1)}, bf16[768,512]{1,0:T(8,128)(2,1)S(1)}, u32[]{:S(2)}, u32[]{:S(2)}) collective-permute-start(bf16[768,512]{1,0:T(8,128)(2,1)S(1)} %shard_map.103.refs_1_), channel_id=1, source_target_pairs={{0,2},{2,4},{4,6},{6,7},{7,5},{5,3},{3,1},{1,0},{8,10},{10,12},{12... | collective-permute-start | bytes 2359304 | tf_op jit(solution)/shard_map/ppermute | solution.py:487
  101.7 13.8 %collective-permute-start.16 = (bf16[64,384]{1,0:T(8,128)(2,1)S(1)}, bf16[64,384]{1,0:T(8,128)(2,1)S(1)}, u32[]{:S(2)}, u32[]{:S(2)}) collective-permute-start(bf16[64,384]{1,0:T(8,128)(2,1)S(1)} %shard_map.106.refs_1_.low_ref), channel_id=1, source_target_pairs={{0,1},{1,0},{2,3},{3,2},{4,5},{5,4},{6,7},{7,6},{8,9},{9,8},{10,11... | collective-permute-start | bytes 147464 | tf_op jit(solution)/shard_map/ppermute | solution.py:517
  104.6 27.5 %collective-permute-start.22 = (bf16[768,512]{1,0:T(8,128)(2,1)S(1)}, bf16[768,512]{1,0:T(8,128)(2,1)S(1)}, u32[]{:S(2)}, u32[]{:S(2)}) collective-permute-start(bf16[768,512]{1,0:T(8,128)(2,1)S(1)} %shard_map.107.refs_1_), channel_id=1, source_target_pairs={{0,2},{2,4},{4,6},{6,7},{7,5},{5,3},{3,1},{1,0},{8,10},{10,12},{12... | collective-permute-start | bytes 2359304 | tf_op jit(solution)/shard_map/ppermute | solution.py:487
  109.7 23.9 %collective-permute-start.21 = (bf16[768,512]{1,0:T(8,128)(2,1)S(1)}, bf16[768,512]{1,0:T(8,128)(2,1)S(1)}, u32[]{:S(2)}, u32[]{:S(2)}) collective-permute-start(bf16[768,512]{1,0:T(8,128)(2,1)S(1)} %shard_map.108.after_ref), channel_id=1, source_target_pairs={{0,1},{2,0},{4,2},{6,4},{7,6},{5,7},{3,5},{1,3},{8,9},{10,8},{12,1... | collective-permute-start | bytes 2359304 | tf_op jit(solution)/shard_map/ppermute | solution.py:487
  116.2 15.9 %copy-start.4 = (s32[3,1]{0,1:T(1,128)S(1)}, s32[3,1]{0,1:T(1,128)}, u32[]{:S(2)}) copy-start(s32[3,1]{0,1:T(1,128)} %param.15) | copy-start | bytes 40
  (11 other events, 77.5 us)

commit v17 on v16

--- a/solution.py
+++ b/solution.py
@@ -469,10 +469,17 @@
 
     instance = lax.axis_index("inst")
     place = ring_place(lax.axis_index("tp"), size)
-    dests = ring_index(lax.rem(place + jnp.arange(size, dtype=jnp.int32), size), size)
-
-    forward = [(ring[i], ring[(i + 1) % size]) for i in range(size)]
-    backward = [(ring[i], ring[i - 1]) for i in range(size)]
+    steps_on = jnp.arange(size, dtype=jnp.int32)
+    steps_on = jnp.where(instance == 0, steps_on, size - steps_on)
+    dests = ring_index(lax.rem(place + steps_on, size), size)
+
+    up = [(ring[i], ring[(i + 1) % size]) for i in range(size)]
+    down = [(ring[i], ring[i - 1]) for i in range(size)]
+
+    def both_instances(first, second):
+        return first + [(size + source, size + target) for source, target in second]
+
+    forward, backward = both_instances(up, down), both_instances(down, up)
     far = size // 2
     pairs = [[(0, 1, forward), (1, -1, backward)], [(1, 1, forward), (0, -1, backward)]]
     arrived = {}
@@ -484,7 +491,7 @@
                 dests, (sign * left) % size, half, x, output_weight,
                 arrived.get((half, sign), []), last,
             )
-            arrived[half, sign] = [lax.ppermute(last, "tp", moves)]
+            arrived[half, sign] = [lax.ppermute(last, ("inst", "tp"), moves)]
             if between is not None:
                 last, between = touch(between, last), None
         return last
@@ -495,7 +502,7 @@
     for piece in range(tiling(dests, output_weight)[2]):
         *both, last = first_pieces(dests, far % size, piece, x, output_weight, last)
         for (half, sign, moves), part in zip(pairs[0], both):
-            arrived.setdefault((half, sign), []).append(lax.ppermute(part, "tp", moves))
+            arrived.setdefault((half, sign), []).append(lax.ppermute(part, ("inst", "tp"), moves))
     pages = adapter_page_table[jnp.concatenate([ids, ids_there])]
     places = pages % resident
     index, index_there = places[: ids.shape[0]], places[ids.shape[0] :]

time: 136 us -> 135 us (level)
  transfers between devices with their start and end apart: 23 -> 23, of which waited for: 7 -> 6; matrix products, arithmetic and copies ran while one was open for 6% -> 6% of each run, Pallas kernels for 45% -> 45%
where the time goes in v17:
time: 135 us
  Pallas kernels  62.7 us (46%)
  waiting for transfers between devices  39.5 us (29%)
  starting transfers between devices  24.1 us (18%)
  local copies, waits for them, and re-layouts  4.43 us (3%)
  other arithmetic  3.42 us (3%)
    pallas_call x12, Pallas kernels, hop(): pl.pallas_call(functools.partial(hop_kernel, tuple(range(len(received))))...  33.7 us
    ppermute x4, waiting for transfers between devices, over(): return lax.ppermute(value, 'tp', [(i, i ^ apart) for i in range(size)])  24 us
    ppermute x12, waiting for transfers between devices, turn(): arrived[half, sign] = [lax.ppermute(last, ('inst', 'tp'), moves)]  15.5 us
    ppermute x12, starting transfers between devices, turn(): arrived[half, sign] = [lax.ppermute(last, ('inst', 'tp'), moves)]  13.3 us
    pallas_call x2, Pallas kernels, first_pieces(): pl.pallas_call(functools.partial(first_kernel, after is not None), grid_s...  7.85 us
    pallas_call x1, Pallas kernels, own_terms(): pl.pallas_call(own_kernel, grid_spec=pltpu.PrefetchScalarGridSpec(num_sca...  6.59 us
    ppermute x4, starting transfers between devices, over(): return lax.ppermute(value, 'tp', [(i, i ^ apart) for i in range(size)])  5.36 us
    pallas_call x2, Pallas kernels, collect(): pl.pallas_call(functools.partial(collect_kernel, count), grid_spec=pltpu....  5.33 us
  transfers between devices with their start and end apart: 23, of which 6 were waited for; matrix products, arithmetic and copies ran while one was open for 6% of the time, Pallas kernels for 45%

profile of v17, /device:TPU:0, one launch (start us, length us, event | category | flops | bytes accessed | tf_op | source)
XLA Modules:
  0.0 134.5 jit_solution(13448554917128353785)
XLA Ops:
  0.5 4.3 %shard_map.82 = (bf16[768,256]{1,0:T(8,128)(2,1)}, bf16[768,256]{1,0:T(8,128)(2,1)}, f32[8,128]{1,0:T(8,128)S(1)}) custom-call(s32[8]{0:T(128)S(1)} %compare_select_fusion.3.dests, bf16[768,1024]{1,0:T(8,128)(2,1)} %bitcast.11, bf16[1024,8192]{1,0:T(8,128)(2,1)} %w_ref.29), custom_call_target="tpu_custom_call" | custom-call | flops 24159191040 | bytes 3407872 | tf_op jit(solution)/shard_map/pallas_call | solution.py:126
  4.8 2.6 %collective-permute-start.1 = (bf16[768,256]{1,0:T(8,128)(2,1)}, bf16[768,256]{1,0:T(8,128)(2,1)S(1)}, u32[]{:S(2)}, u32[]{:S(2)}) collective-permute-start(bf16[768,256]{1,0:T(8,128)(2,1)} %get-tuple-element.17), channel_id=1, source_target_pairs={{0,2},{2,4},{4,6},{6,7},{7,5},{5,3},{3,1},{1,0},{8,9},{10,8},{12,1... | collective-permute-start | bytes 1179656 | tf_op jit(solution)/shard_map/ppermute | solution.py:505
  7.3 3.6 %shard_map.83 = (bf16[768,256]{1,0:T(8,128)(2,1)}, bf16[768,256]{1,0:T(8,128)(2,1)S(1)}, f32[8,128]{1,0:T(8,128)S(1)}) custom-call(s32[8]{0:T(128)S(1)} %compare_select_fusion.3.dests, bf16[768,1024]{1,0:T(8,128)(2,1)S(1)} %bitcast.12, bf16[1024,8192]{1,0:T(8,128)(2,1)} %w_ref.29, f32[8,128]{1,0:T(8,128)S(1)} %get-tuple-element.15.refs_0_), custom_call_target="tpu_custom_call" | custom-call | flops 24159191040 | bytes 3407872 | tf_op jit(solution)/shard_map/pallas_call | solution.py:126
  17.1 2.7 %shard_map.84.refs_0_ = bf16[24,64,1024]{2,1,0:T(8,128)(2,1)S(1)} custom-call(s32[24]{0:T(128)S(1)} %get-tuple-element.25.index, bf16[96,64,1024]{2,1,0:T(8,128)(2,1)} %table_ref.6, f32[8,128]{1,0:T(8,128)S(1)} %get-tuple-element.16.after_ref), custom_call_target="tpu_custom_call" | custom-call | bytes 6291456 | tf_op jit(solution)/shard_map/pallas_call | solution.py:175
  20.0 2.8 %shard_map.86.refs_0_ = bf16[768,512]{1,0:T(8,128)(2,1)S(1)} custom-call(s32[8]{0:T(128)S(1)} %compare_select_fusion.3.dests, bf16[768,1024]{1,0:T(8,128)(2,1)S(1)} %bitcast.13, bf16[1024,8192]{1,0:T(8,128)(2,1)} %w_ref.29, f32[8,128]{1,0:T(8,128)S(1)} %shard_map.85.refs_0_), custom_call_target="tpu_custom_call" | custom-call | flops 24159191040 | bytes 4194304 | tf_op jit(solution)/shard_map/pallas_call | solution.py:81
  22.8 2.8 %shard_map.87.after_ref = bf16[768,512]{1,0:T(8,128)(2,1)S(1)} custom-call(s32[8]{0:T(128)S(1)} %compare_select_fusion.3.dests, bf16[768,1024]{1,0:T(8,128)(2,1)S(1)} %bitcast.14, bf16[1024,8192]{1,0:T(8,128)(2,1)} %w_ref.29, bf16[768,512]{1,0:T(8,128)(2,1)S(1)} %shard_map.86.refs_0_), custom_call_target="tpu_custom_call" | custom-call | flops 24159191040 | bytes 4194304 | tf_op jit(solution)/shard_map/pallas_call | solution.py:81
  27.6 2.7 %shard_map.88.refs_2_ = bf16[24,64,1024]{2,1,0:T(8,128)(2,1)S(1)} custom-call(s32[24]{0:T(128)S(1)} %get-tuple-element.25.index, bf16[96,64,1024]{2,1,0:T(8,128)(2,1)} %table_ref.7, bf16[768,512]{1,0:T(8,128)(2,1)S(1)} %shard_map.87.after_ref), custom_call_target="tpu_custom_call" | custom-call | bytes 6291456 | tf_op jit(solution)/shard_map/pallas_call | solution.py:175
  30.6 2.9 %shard_map.89.refs_1_ = bf16[768,512]{1,0:T(8,128)(2,1)S(1)} custom-call(s32[8]{0:T(128)S(1)} %compare_select_fusion.3.dests, bf16[768,1024]{1,0:T(8,128)(2,1)S(1)} %bitcast.15, bf16[1024,8192]{1,0:T(8,128)(2,1)} %w_ref.29, bf16[768,256]{1,0:T(8,128)(2,1)S(1)} %collective-permute-done.1.refs_1_.refs_0_, bf16[768,256]{1,0:T(8,128)(2,1)S(1)} %collective-permute-done.8.refs_1_, ...), custom_call_target="tpu_custom_call" | custom-call | flops 24159191040 | bytes 4194304 | tf_op jit(solution)/shard_map/pallas_call | solution.py:81
  35.4 2.9 %shard_map.91.after_ref = bf16[768,512]{1,0:T(8,128)(2,1)S(1)} custom-call(s32[8]{0:T(128)S(1)} %compare_select_fusion.3.dests, bf16[768,1024]{1,0:T(8,128)(2,1)S(1)} %bitcast.16, bf16[1024,8192]{1,0:T(8,128)(2,1)} %w_ref.29, bf16[768,256]{1,0:T(8,128)(2,1)S(1)} %collective-permute-done.2.refs_2_.refs_0_, ...), custom_call_target="tpu_custom_call" | custom-call | flops 24159191040 | bytes 4194304 | tf_op jit(solution)/shard_map/pallas_call | solution.py:81
  38.7 5.2 %shard_map.92 = (f32[64,384]{1,0:T(8,128)S(1)}, f32[64,384]{1,0:T(8,128)S(1)}) custom-call(s32[24]{0:T(128)S(1)} %compare_convert_fusion.local, s32[24]{0:T(128)S(1)} %get-tuple-element.26.index, s32[1]{0:T(128)} %bitcast.1.side, bf16[768,1024]{1,0:T(8,128)(2,1)S(1)} %bitcast.17, s32[3,256]{1,0:T(4,128)S(1)} %copy-done.6, bf16[96,64,1024]{2,1,0:T(8,128)(2,1)} %table_ref.6, ...), custom_call_target="tpu_custom_call" | custom-call | flops 12079595520 | bytes 4718592 | tf_op jit(solution)/shard_map/pallas_call | solution.py:246
  45.7 2.8 %shard_map.94.refs_1_ = bf16[768,512]{1,0:T(8,128)(2,1)S(1)} custom-call(s32[8]{0:T(128)S(1)} %compare_select_fusion.3.dests, bf16[768,1024]{1,0:T(8,128)(2,1)S(1)} %bitcast.18, bf16[1024,8192]{1,0:T(8,128)(2,1)} %w_ref.29, bf16[768,512]{1,0:T(8,128)(2,1)S(1)} %collective-permute-done.5.refs_0_, f32[8,128]{1,0:T(8,128)S(1)} %shard_map.93.refs_1_), custom_call_target="tpu_custom_call" | custom-call | flops 24159191040 | bytes 4194304 | tf_op jit(solution)/shard_map/pallas_call | solution.py:81
  50.8 2.8 %shard_map.95.after_ref = bf16[768,512]{1,0:T(8,128)(2,1)S(1)} custom-call(s32[8]{0:T(128)S(1)} %compare_select_fusion.3.dests, bf16[768,1024]{1,0:T(8,128)(2,1)S(1)} %bitcast.19, bf16[1024,8192]{1,0:T(8,128)(2,1)} %w_ref.29, bf16[768,512]{1,0:T(8,128)(2,1)S(1)} %collective-permute-done.4.refs_0_, bf16[768,512]{1,0:T(8,128)(2,1)S(1)} %shard_map.94.refs_1_), custom_call_target="tpu_custom_call" | custom-call | flops 24159191040 | bytes 4194304 | tf_op jit(solution)/shard_map/pallas_call | solution.py:81
  53.6 6.6 %shard_map.96 = (f32[768,1024]{1,0:T(8,128)S(1)}, bf16[24,64,1024]{2,1,0:T(8,128)(2,1)S(1)}) custom-call(s32[24]{0:T(128)S(1)} %compare_convert_fusion.local, s32[24]{0:T(128)S(1)} %get-tuple-element.26.index, s32[8]{0:T(128)S(1)} %compare_select_fusion.3.dests, bf16[768,1024]{1,0:T(8,128)(2,1)S(1)} %bitcast.20, bf16[1024,8192]{1,0:T(8,128)(2,1)} %w_ref.29, ...), custom_call_target="tpu_custom_call" | custom-call | flops 48318382080 | bytes 13107200 | tf_op jit(solution)/shard_map/pallas_call | solution.py:305
  65.0 2.8 %shard_map.99.refs_1_ = bf16[768,512]{1,0:T(8,128)(2,1)S(1)} custom-call(s32[8]{0:T(128)S(1)} %compare_select_fusion.3.dests, bf16[768,1024]{1,0:T(8,128)(2,1)S(1)} %bitcast.21, bf16[1024,8192]{1,0:T(8,128)(2,1)} %w_ref.29, bf16[768,512]{1,0:T(8,128)(2,1)S(1)} %collective-permute-done.12.refs_0_, f32[64,384]{1,0:T(8,128)S(1)} %shard_map.98.refs_1_.low_ref), custom_call_target="tpu_custom_call" | custom-call | flops 24159191040 | bytes 4194304 | tf_op jit(solution)/shard_map/pallas_call | solution.py:81
  69.1 2.8 %shard_map.100.refs_0_.after_ref = bf16[768,512]{1,0:T(8,128)(2,1)S(1)} custom-call(s32[8]{0:T(128)S(1)} %compare_select_fusion.3.dests, bf16[768,1024]{1,0:T(8,128)(2,1)S(1)} %bitcast.22, bf16[1024,8192]{1,0:T(8,128)(2,1)} %w_ref.29, bf16[768,512]{1,0:T(8,128)(2,1)S(1)} %collective-permute-done.11.refs_0_, bf16[768,512]{1,0:T(8,128)(2,1)S(1)} %shard_map.99.refs_1_), custom_call_target="tpu_custom_call" | custom-call | flops 24159191040 | bytes 4194304 | tf_op jit(solution)/shard_map/pallas_call | solution.py:81
  73.2 9.7 %collective-permute-done.10 = f16[64,384]{1,0:T(8,128)(2,1)S(1)} collective-permute-done((f16[64,384]{1,0:T(8,128)(2,1)S(1)}, f16[64,384]{1,0:T(8,128)(2,1)S(1)}, u32[]{:S(2)}, u32[]{:S(2)}) %collective-permute-start.10) | collective-permute-done | bytes 49184 | tf_op jit(solution)/shard_map/ppermute | solution.py:524
  83.6 2.7 %collective-permute-start.13 = (f16[64,384]{1,0:T(8,128)(2,1)S(1)}, f16[64,384]{1,0:T(8,128)(2,1)S(1)}, u32[]{:S(2)}, u32[]{:S(2)}) collective-permute-start(f16[64,384]{1,0:T(8,128)(2,1)S(1)} %multiply_convert_fusion), channel_id=1, source_target_pairs={{0,4},{1,5},{2,6},{3,7},{4,0},{5,1},{6,2},{7,3},{8,12},{9,13},{10,... | collective-permute-start | bytes 147464 | tf_op jit(solution)/shard_map/ppermute | solution.py:524
  86.2 2.8 %shard_map.103.refs_1_ = bf16[768,512]{1,0:T(8,128)(2,1)S(1)} custom-call(s32[8]{0:T(128)S(1)} %compare_select_fusion.3.dests, bf16[768,1024]{1,0:T(8,128)(2,1)S(1)} %bitcast.23, bf16[1024,8192]{1,0:T(8,128)(2,1)} %w_ref.29, bf16[768,512]{1,0:T(8,128)(2,1)S(1)} %collective-permute-done.15.refs_0_, f32[64,384]{1,0:T(8,128)S(1)} %shard_map.102.refs_1_.low_ref), custom_call_target="tpu_custom_call" | custom-call | flops 24159191040 | bytes 4194304 | tf_op jit(solution)/shard_map/pallas_call | solution.py:81
  89.0 2.8 %shard_map.104.refs_0_.after_ref = bf16[768,512]{1,0:T(8,128)(2,1)S(1)} custom-call(s32[8]{0:T(128)S(1)} %compare_select_fusion.3.dests, bf16[768,1024]{1,0:T(8,128)(2,1)S(1)} %bitcast.24, bf16[1024,8192]{1,0:T(8,128)(2,1)} %w_ref.29, bf16[768,512]{1,0:T(8,128)(2,1)S(1)} %collective-permute-done.14.refs_0_, bf16[768,512]{1,0:T(8,128)(2,1)S(1)} %shard_map.103.refs_1_), custom_call_target="tpu_custom_call" | custom-call | flops 24159191040 | bytes 4194304 | tf_op jit(solution)/shard_map/pallas_call | solution.py:81
  94.4 6.8 %collective-permute-done.13 = f16[64,384]{1,0:T(8,128)(2,1)S(1)} collective-permute-done((f16[64,384]{1,0:T(8,128)(2,1)S(1)}, f16[64,384]{1,0:T(8,128)(2,1)S(1)}, u32[]{:S(2)}, u32[]{:S(2)}) %collective-permute-start.13) | collective-permute-done | bytes 49184 | tf_op jit(solution)/shard_map/ppermute | solution.py:524
  102.0 2.8 %shard_map.107.refs_1_ = bf16[768,512]{1,0:T(8,128)(2,1)S(1)} custom-call(s32[8]{0:T(128)S(1)} %compare_select_fusion.3.dests, bf16[768,1024]{1,0:T(8,128)(2,1)S(1)} %bitcast.25, bf16[1024,8192]{1,0:T(8,128)(2,1)} %w_ref.29, bf16[768,512]{1,0:T(8,128)(2,1)S(1)} %collective-permute-done.18.refs_0_, bf16[64,384]{1,0:T(8,128)(2,1)S(1)} %shard_map.106.refs_1_.low_ref), custom_call_target="tpu_custom_call" | custom-call | flops 24159191040 | bytes 4194304 | tf_op jit(solution)/shard_map/pallas_call | solution.py:81
  107.0 2.8 %shard_map.108.after_ref = bf16[768,512]{1,0:T(8,128)(2,1)S(1)} custom-call(s32[8]{0:T(128)S(1)} %compare_select_fusion.3.dests, bf16[768,1024]{1,0:T(8,128)(2,1)S(1)} %bitcast.26, bf16[1024,8192]{1,0:T(8,128)(2,1)} %w_ref.29, bf16[768,512]{1,0:T(8,128)(2,1)S(1)} %collective-permute-done.17.refs_0_, bf16[768,512]{1,0:T(8,128)(2,1)S(1)} %shard_map.107.refs_1_), custom_call_target="tpu_custom_call" | custom-call | flops 24159191040 | bytes 4194304 | tf_op jit(solution)/shard_map/pallas_call | solution.py:81
  110.1 4.9 %collective-permute-done.16.other_ref = bf16[64,384]{1,0:T(8,128)(2,1)S(1)} collective-permute-done((bf16[64,384]{1,0:T(8,128)(2,1)S(1)}, bf16[64,384]{1,0:T(8,128)(2,1)S(1)}, u32[]{:S(2)}, u32[]{:S(2)}) %collective-permute-start.16) | collective-permute-done | bytes 49184 | tf_op jit(solution)/shard_map/ppermute | solution.py:524
  118.0 13.5 %collective-permute-done.22.last_ref = bf16[768,512]{1,0:T(8,128)(2,1)S(1)} collective-permute-done((bf16[768,512]{1,0:T(8,128)(2,1)S(1)}, bf16[768,512]{1,0:T(8,128)(2,1)S(1)}, u32[]{:S(2)}, u32[]{:S(2)}) %collective-permute-start.22) | collective-permute-done | bytes 786464 | tf_op jit(solution)/shard_map/ppermute | solution.py:494
  (95 shorter events, 35.3 us)
Async XLA Ops:
  0.0 13.6 %collective-permute-start = (s32[3,2,4]{2,1,0:T(2,128)}, s32[3,2,4]{2,1,0:T(2,128)}, u32[]{:S(2)}, u32[]{:S(2)}) collective-permute-start(s32[3,2,4]{2,1,0:T(2,128)} %param.13), channel_id=1, source_target_pairs={{0,8},{8,0},{1,9},{9,1},{2,10},{10,2},{3,11},{11,3},{4,12},{12,4},... | collective-permute-start | bytes 296 | tf_op jit(solution)/shard_map/ppermute | solution.py:500
  4.8 15.2 %collective-permute-start.1 = (bf16[768,256]{1,0:T(8,128)(2,1)}, bf16[768,256]{1,0:T(8,128)(2,1)S(1)}, u32[]{:S(2)}, u32[]{:S(2)}) collective-permute-start(bf16[768,256]{1,0:T(8,128)(2,1)} %get-tuple-element.17), channel_id=1, source_target_pairs={{0,2},{2,4},{4,6},{6,7},{7,5},{5,3},{3,1},{1,0},{8,9},{10,8},{12,1... | collective-permute-start | bytes 1179656 | tf_op jit(solution)/shard_map/ppermute | solution.py:505
  7.3 12.6 %collective-permute-start.2 = (bf16[768,256]{1,0:T(8,128)(2,1)}, bf16[768,256]{1,0:T(8,128)(2,1)S(1)}, u32[]{:S(2)}, u32[]{:S(2)}) collective-permute-start(bf16[768,256]{1,0:T(8,128)(2,1)} %get-tuple-element.18), channel_id=1, source_target_pairs={{0,1},{2,0},{4,2},{6,4},{7,6},{5,7},{3,5},{1,3},{8,10},{10,12},{12... | collective-permute-start | bytes 1179656 | tf_op jit(solution)/shard_map/ppermute | solution.py:505
  10.9 19.4 %collective-permute-start.8 = (bf16[768,256]{1,0:T(8,128)(2,1)}, bf16[768,256]{1,0:T(8,128)(2,1)S(1)}, u32[]{:S(2)}, u32[]{:S(2)}) collective-permute-start(bf16[768,256]{1,0:T(8,128)(2,1)} %get-tuple-element.20), channel_id=1, source_target_pairs={{0,2},{2,4},{4,6},{6,7},{7,5},{5,3},{3,1},{1,0},{8,9},{10,8},{12,1... | collective-permute-start | bytes 1179656 | tf_op jit(solution)/shard_map/ppermute | solution.py:505
  13.0 22.5 %collective-permute-start.7 = (bf16[768,256]{1,0:T(8,128)(2,1)S(1)}, bf16[768,256]{1,0:T(8,128)(2,1)S(1)}, u32[]{:S(2)}, u32[]{:S(2)}) collective-permute-start(bf16[768,256]{1,0:T(8,128)(2,1)S(1)} %get-tuple-element.19), channel_id=1, source_target_pairs={{0,1},{2,0},{4,2},{6,4},{7,6},{5,7},{3,5},{1,3},{8,10},{10,12},{12... | collective-permute-start | bytes 1179656 | tf_op jit(solution)/shard_map/ppermute | solution.py:505
  19.8 13.8 %collective-permute-start.6 = (bf16[24,64,1024]{2,1,0:T(8,128)(2,1)S(1)}, bf16[24,64,1024]{2,1,0:T(8,128)(2,1)S(1)}, u32[]{:S(2)}, u32[]{:S(2)}) collective-permute-start(bf16[24,64,1024]{2,1,0:T(8,128)(2,1)S(1)} %shard_map.84.refs_0_), channel_id=1, source_target_pairs={{0,8},{8,0},{1,9},{9,1},{2,10},{10,2},{3,11},{11,3},{4,12},{12,4},... | collective-permute-start | bytes 9437192 | tf_op jit(solution)/shard_map/ppermute | solution.py:511
  25.5 20.1 %collective-permute-start.5 = (bf16[768,512]{1,0:T(8,128)(2,1)S(1)}, bf16[768,512]{1,0:T(8,128)(2,1)S(1)}, u32[]{:S(2)}, u32[]{:S(2)}) collective-permute-start(bf16[768,512]{1,0:T(8,128)(2,1)S(1)} %shard_map.86.refs_0_), channel_id=1, source_target_pairs={{0,2},{2,4},{4,6},{6,7},{7,5},{5,3},{3,1},{1,0},{8,9},{10,8},{12,1... | collective-permute-start | bytes 2359304 | tf_op jit(solution)/shard_map/ppermute | solution.py:494
  27.6 23.2 %collective-permute-start.4 = (bf16[768,512]{1,0:T(8,128)(2,1)S(1)}, bf16[768,512]{1,0:T(8,128)(2,1)S(1)}, u32[]{:S(2)}, u32[]{:S(2)}) collective-permute-start(bf16[768,512]{1,0:T(8,128)(2,1)S(1)} %shard_map.87.after_ref), channel_id=1, source_target_pairs={{0,1},{2,0},{4,2},{6,4},{7,6},{5,7},{3,5},{1,3},{8,10},{10,12},{12... | collective-permute-start | bytes 2359304 | tf_op jit(solution)/shard_map/ppermute | solution.py:494
  30.3 13.6 %collective-permute-start.3 = (bf16[24,64,1024]{2,1,0:T(8,128)(2,1)S(1)}, bf16[24,64,1024]{2,1,0:T(8,128)(2,1)S(1)}, u32[]{:S(2)}, u32[]{:S(2)}) collective-permute-start(bf16[24,64,1024]{2,1,0:T(8,128)(2,1)S(1)} %shard_map.88.refs_2_), channel_id=1, source_target_pairs={{0,8},{8,0},{1,9},{9,1},{2,10},{10,2},{3,11},{11,3},{4,12},{12,4},... | collective-permute-start | bytes 9437192 | tf_op jit(solution)/shard_map/ppermute | solution.py:515
  33.6 31.4 %collective-permute-start.12 = (bf16[768,512]{1,0:T(8,128)(2,1)S(1)}, bf16[768,512]{1,0:T(8,128)(2,1)S(1)}, u32[]{:S(2)}, u32[]{:S(2)}) collective-permute-start(bf16[768,512]{1,0:T(8,128)(2,1)S(1)} %shard_map.89.refs_1_), channel_id=1, source_target_pairs={{0,2},{2,4},{4,6},{6,7},{7,5},{5,3},{3,1},{1,0},{8,9},{10,8},{12,1... | collective-permute-start | bytes 2359304 | tf_op jit(solution)/shard_map/ppermute | solution.py:494
  38.4 30.7 %collective-permute-start.11 = (bf16[768,512]{1,0:T(8,128)(2,1)S(1)}, bf16[768,512]{1,0:T(8,128)(2,1)S(1)}, u32[]{:S(2)}, u32[]{:S(2)}) collective-permute-start(bf16[768,512]{1,0:T(8,128)(2,1)S(1)} %shard_map.91.after_ref), channel_id=1, source_target_pairs={{0,1},{2,0},{4,2},{6,4},{7,6},{5,7},{3,5},{1,3},{8,10},{10,12},{12... | collective-permute-start | bytes 2359304 | tf_op jit(solution)/shard_map/ppermute | solution.py:494
  43.9 19.5 %collective-permute-start.9 = (f16[64,384]{1,0:T(8,128)(2,1)S(1)}, f16[64,384]{1,0:T(8,128)(2,1)S(1)}, u32[]{:S(2)}, u32[]{:S(2)}) collective-permute-start(f16[64,384]{1,0:T(8,128)(2,1)S(1)} %multiply_convert_fusion.2), channel_id=1, source_target_pairs={{0,1},{1,0},{2,3},{3,2},{4,5},{5,4},{6,7},{7,6},{8,9},{9,8},{10,11... | collective-permute-start | bytes 147464 | tf_op jit(solution)/shard_map/ppermute | solution.py:524
  48.5 37.8 %collective-permute-start.15 = (bf16[768,512]{1,0:T(8,128)(2,1)S(1)}, bf16[768,512]{1,0:T(8,128)(2,1)S(1)}, u32[]{:S(2)}, u32[]{:S(2)}) collective-permute-start(bf16[768,512]{1,0:T(8,128)(2,1)S(1)} %shard_map.94.refs_1_), channel_id=1, source_target_pairs={{0,2},{2,4},{4,6},{6,7},{7,5},{5,3},{3,1},{1,0},{8,9},{10,8},{12,1... | collective-permute-start | bytes 2359304 | tf_op jit(solution)/shard_map/ppermute | solution.py:494
  53.6 35.4 %collective-permute-start.14 = (bf16[768,512]{1,0:T(8,128)(2,1)S(1)}, bf16[768,512]{1,0:T(8,128)(2,1)S(1)}, u32[]{:S(2)}, u32[]{:S(2)}) collective-permute-start(bf16[768,512]{1,0:T(8,128)(2,1)S(1)} %shard_map.95.after_ref), channel_id=1, source_target_pairs={{0,1},{2,0},{4,2},{6,4},{7,6},{5,7},{3,5},{1,3},{8,10},{10,12},{12... | collective-permute-start | bytes 2359304 | tf_op jit(solution)/shard_map/ppermute | solution.py:494
  64.1 18.7 %collective-permute-start.10 = (f16[64,384]{1,0:T(8,128)(2,1)S(1)}, f16[64,384]{1,0:T(8,128)(2,1)S(1)}, u32[]{:S(2)}, u32[]{:S(2)}) collective-permute-start(f16[64,384]{1,0:T(8,128)(2,1)S(1)} %multiply_convert_fusion.1), channel_id=1, source_target_pairs={{0,2},{1,3},{2,0},{3,1},{4,6},{5,7},{6,4},{7,5},{8,10},{9,11},{10,... | collective-permute-start | bytes 147464 | tf_op jit(solution)/shard_map/ppermute | solution.py:524
  67.8 34.3 %collective-permute-start.18 = (bf16[768,512]{1,0:T(8,128)(2,1)S(1)}, bf16[768,512]{1,0:T(8,128)(2,1)S(1)}, u32[]{:S(2)}, u32[]{:S(2)}) collective-permute-start(bf16[768,512]{1,0:T(8,128)(2,1)S(1)} %shard_map.99.refs_1_), channel_id=1, source_target_pairs={{0,2},{2,4},{4,6},{6,7},{7,5},{5,3},{3,1},{1,0},{8,9},{10,8},{12,1... | collective-permute-start | bytes 2359304 | tf_op jit(solution)/shard_map/ppermute | solution.py:494
  71.9 35.1 %collective-permute-start.17 = (bf16[768,512]{1,0:T(8,128)(2,1)S(1)}, bf16[768,512]{1,0:T(8,128)(2,1)S(1)}, u32[]{:S(2)}, u32[]{:S(2)}) collective-permute-start(bf16[768,512]{1,0:T(8,128)(2,1)S(1)} %shard_map.100.refs_0_.after_ref), channel_id=1, source_target_pairs={{0,1},{2,0},{4,2},{6,4},{7,6},{5,7},{3,5},{1,3},{8,10},{10,12},{12... | collective-permute-start | bytes 2359304 | tf_op jit(solution)/shard_map/ppermute | solution.py:494
  83.6 17.7 %collective-permute-start.13 = (f16[64,384]{1,0:T(8,128)(2,1)S(1)}, f16[64,384]{1,0:T(8,128)(2,1)S(1)}, u32[]{:S(2)}, u32[]{:S(2)}) collective-permute-start(f16[64,384]{1,0:T(8,128)(2,1)S(1)} %multiply_convert_fusion), channel_id=1, source_target_pairs={{0,4},{1,5},{2,6},{3,7},{4,0},{5,1},{6,2},{7,3},{8,12},{9,13},{10,... | collective-permute-start | bytes 147464 | tf_op jit(solution)/shard_map/ppermute | solution.py:524
  91.8 25.8 %collective-permute-start.19 = (bf16[768,512]{1,0:T(8,128)(2,1)S(1)}, bf16[768,512]{1,0:T(8,128)(2,1)S(1)}, u32[]{:S(2)}, u32[]{:S(2)}) collective-permute-start(bf16[768,512]{1,0:T(8,128)(2,1)S(1)} %shard_map.104.refs_0_.after_ref), channel_id=1, source_target_pairs={{0,1},{2,0},{4,2},{6,4},{7,6},{5,7},{3,5},{1,3},{8,10},{10,12},{12... | collective-permute-start | bytes 2359304 | tf_op jit(solution)/shard_map/ppermute | solution.py:494
  91.9 25.7 %collective-permute-start.20 = (bf16[768,512]{1,0:T(8,128)(2,1)S(1)}, bf16[768,512]{1,0:T(8,128)(2,1)S(1)}, u32[]{:S(2)}, u32[]{:S(2)}) collective-permute-start(bf16[768,512]{1,0:T(8,128)(2,1)S(1)} %shard_map.103.refs_1_), channel_id=1, source_target_pairs={{0,2},{2,4},{4,6},{6,7},{7,5},{5,3},{3,1},{1,0},{8,9},{10,8},{12,1... | collective-permute-start | bytes 2359304 | tf_op jit(solution)/shard_map/ppermute | solution.py:494
  101.9 13.1 %collective-permute-start.16 = (bf16[64,384]{1,0:T(8,128)(2,1)S(1)}, bf16[64,384]{1,0:T(8,128)(2,1)S(1)}, u32[]{:S(2)}, u32[]{:S(2)}) collective-permute-start(bf16[64,384]{1,0:T(8,128)(2,1)S(1)} %shard_map.106.refs_1_.low_ref), channel_id=1, source_target_pairs={{0,1},{1,0},{2,3},{3,2},{4,5},{5,4},{6,7},{7,6},{8,9},{9,8},{10,11... | collective-permute-start | bytes 147464 | tf_op jit(solution)/shard_map/ppermute | solution.py:524
  104.8 26.6 %collective-permute-start.22 = (bf16[768,512]{1,0:T(8,128)(2,1)S(1)}, bf16[768,512]{1,0:T(8,128)(2,1)S(1)}, u32[]{:S(2)}, u32[]{:S(2)}) collective-permute-start(bf16[768,512]{1,0:T(8,128)(2,1)S(1)} %shard_map.107.refs_1_), channel_id=1, source_target_pairs={{0,2},{2,4},{4,6},{6,7},{7,5},{5,3},{3,1},{1,0},{8,9},{10,8},{12,1... | collective-permute-start | bytes 2359304 | tf_op jit(solution)/shard_map/ppermute | solution.py:494
  109.8 23.2 %collective-permute-start.21 = (bf16[768,512]{1,0:T(8,128)(2,1)S(1)}, bf16[768,512]{1,0:T(8,128)(2,1)S(1)}, u32[]{:S(2)}, u32[]{:S(2)}) collective-permute-start(bf16[768,512]{1,0:T(8,128)(2,1)S(1)} %shard_map.108.after_ref), channel_id=1, source_target_pairs={{0,1},{2,0},{4,2},{6,4},{7,6},{5,7},{3,5},{1,3},{8,10},{10,12},{12... | collective-permute-start | bytes 2359304 | tf_op jit(solution)/shard_map/ppermute | solution.py:494
  115.7 15.8 %copy-start.4 = (s32[3,1]{0,1:T(1,128)S(1)}, s32[3,1]{0,1:T(1,128)}, u32[]{:S(2)}) copy-start(s32[3,1]{0,1:T(1,128)} %param.15) | copy-start | bytes 40
  (11 other events, 74.9 us)

commit v18 on v17

--- a/solution.py
+++ b/solution.py
@@ -493,7 +493,7 @@
             )
             arrived[half, sign] = [lax.ppermute(last, ("inst", "tp"), moves)]
             if between is not None:
-                last, between = touch(between, last), None
+                last, between = touch(*between, last), None
         return last
 
     ids = block_adapter_ids.reshape(-1)
@@ -509,28 +509,27 @@
     local = (pages[: ids.shape[0]] // resident == instance).astype(jnp.int32)
     last = collect(index_there, adapter_down_weight, last)
     got_down = lax.ppermute(last, "inst", SWAP)
-    last = touch(last, *(arrived[half, sign][0] for half, sign, _ in pairs[0]))
-    last = turn(1, last)
-    last = collect(index_there, adapter_up_weight, last)
-    got_up = lax.ppermute(last, "inst", SWAP)
-    last = turn(2, last, got_down)
+    last = turn(1, last, [arrived[half, sign][0] for half, sign, _ in pairs[0]])
     side = (lax.axis_index("tp") & 1).reshape(1)
     low, give = low_rank(
         sizes, local, index, side, x, row_list_position, adapter_down_weight, got_down, last
     )
-    last = touch(got_up, low)
+    last = low
 
     def over(value, apart):
         return lax.ppermute(value, "tp", [(i, i ^ apart) for i in range(size)])
 
-    number, turns = 3, 2 * far - 1
+    number, turns = 2, 2 * far - 1
     apart = 1
     while apart < size:
         sent = over(((give if apart == 1 else low) * LOW_SCALE).astype(jnp.float16), apart)
         until = turns - 1 if 2 * apart == size else number + 1
         while number < min(until, turns - 1):
             last = turn(number, last)
-            if number == 3:
+            if number == 4:
+                last = collect(index_there, adapter_up_weight, last)
+                got_up = lax.ppermute(last, "inst", SWAP)
+            if number == 5:
                 own, up_pages = own_terms(
                     dests, local, index, x, output_weight, adapter_up_weight, got_up, last
                 )

time: 135 us -> 132 us (0.978)
  waiting for transfers between devices: 39.5 us -> 32.1 us
  Pallas kernels: 62.7 us -> 64.9 us
  other arithmetic: 3.42 us -> 4.86 us
    ppermute x4, waiting for transfers between devices: 24 us -> 19.7 us  [over(): return lax.ppermute(value, 'tp', [(i, i ^ apart) for i in range(size)])]
    ppermute x12, waiting for transfers between devices: 15.5 us -> 12.4 us  [turn(): arrived[half, sign] = [lax.ppermute(last, ('inst', 'tp'), moves)]]
  transfers between devices with their start and end apart: 23 -> 23, of which waited for: 6 -> 6; matrix products, arithmetic and copies ran while one was open for 6% -> 7% of each run, Pallas kernels for 45% -> 48%
where the time goes in v18:
time: 132 us; the launch traced here: 131 us
  Pallas kernels  64.9 us (49%)
  waiting for transfers between devices  32.1 us (24%)
  starting transfers between devices  23.5 us (18%)
  local copies, waits for them, and re-layouts  5.53 us (4%)
  other arithmetic  4.86 us (4%)
    pallas_call x12, Pallas kernels, hop(): pl.pallas_call(functools.partial(hop_kernel, tuple(range(len(received))))...  33.7 us
    ppermute x4, waiting for transfers between devices, over(): return lax.ppermute(value, 'tp', [(i, i ^ apart) for i in range(size)])  19.7 us
    ppermute x12, starting transfers between devices, turn(): arrived[half, sign] = [lax.ppermute(last, ('inst', 'tp'), moves)]  13.2 us
    ppermute x12, waiting for transfers between devices, turn(): arrived[half, sign] = [lax.ppermute(last, ('inst', 'tp'), moves)]  12.4 us
    pallas_call x2, Pallas kernels, first_pieces(): pl.pallas_call(functools.partial(first_kernel, after is not None), grid_s...  7.85 us
    pallas_call x1, Pallas kernels, own_terms(): pl.pallas_call(own_kernel, grid_spec=pltpu.PrefetchScalarGridSpec(num_sca...  7.74 us
    pallas_call x1, Pallas kernels, low_rank(): pl.pallas_call(functools.partial(low_kernel, sizes), grid_spec=pltpu.Pref...  6.39 us
    pallas_call x2, Pallas kernels, collect(): pl.pallas_call(functools.partial(collect_kernel, count), grid_spec=pltpu....  5.33 us
  transfers between devices with their start and end apart: 23, of which 6 were waited for; matrix products, arithmetic and copies ran while one was open for 7% of the time, Pallas kernels for 48%

profile of v18, /device:TPU:0, one launch (start us, length us, event | category | flops | bytes accessed | tf_op | source)
XLA Modules:
  0.0 131.4 jit_solution(14159191894088542272)
XLA Ops:
  0.5 4.3 %shard_map.82 = (bf16[768,256]{1,0:T(8,128)(2,1)}, bf16[768,256]{1,0:T(8,128)(2,1)}, f32[8,128]{1,0:T(8,128)S(1)}) custom-call(s32[8]{0:T(128)S(1)} %compare_select_fusion.3.dests, bf16[768,1024]{1,0:T(8,128)(2,1)} %bitcast.11, bf16[1024,8192]{1,0:T(8,128)(2,1)} %w_ref.29), custom_call_target="tpu_custom_call" | custom-call | flops 24159191040 | bytes 3407872 | tf_op jit(solution)/shard_map/pallas_call | solution.py:126
  4.7 2.5 %collective-permute-start.1 = (bf16[768,256]{1,0:T(8,128)(2,1)}, bf16[768,256]{1,0:T(8,128)(2,1)S(1)}, u32[]{:S(2)}, u32[]{:S(2)}) collective-permute-start(bf16[768,256]{1,0:T(8,128)(2,1)} %get-tuple-element.15), channel_id=1, source_target_pairs={{0,1},{2,0},{4,2},{6,4},{7,6},{5,7},{3,5},{1,3},{8,10},{10,12},{12... | collective-permute-start | bytes 1179656 | tf_op jit(solution)/shard_map/ppermute | solution.py:505
  7.3 3.6 %shard_map.83 = (bf16[768,256]{1,0:T(8,128)(2,1)}, bf16[768,256]{1,0:T(8,128)(2,1)S(1)}, f32[8,128]{1,0:T(8,128)S(1)}) custom-call(s32[8]{0:T(128)S(1)} %compare_select_fusion.3.dests, bf16[768,1024]{1,0:T(8,128)(2,1)S(1)} %bitcast.12, bf16[1024,8192]{1,0:T(8,128)(2,1)} %w_ref.29, f32[8,128]{1,0:T(8,128)S(1)} %get-tuple-element.16.refs_0_), custom_call_target="tpu_custom_call" | custom-call | flops 24159191040 | bytes 3407872 | tf_op jit(solution)/shard_map/pallas_call | solution.py:126
  17.2 2.7 %shard_map.84.refs_0_ = bf16[24,64,1024]{2,1,0:T(8,128)(2,1)S(1)} custom-call(s32[24]{0:T(128)S(1)} %get-tuple-element.25.index, bf16[96,64,1024]{2,1,0:T(8,128)(2,1)} %table_ref.5, f32[8,128]{1,0:T(8,128)S(1)} %get-tuple-element.20.after_ref), custom_call_target="tpu_custom_call" | custom-call | bytes 6291456 | tf_op jit(solution)/shard_map/pallas_call | solution.py:175
  20.0 2.8 %shard_map.85.refs_2_ = bf16[768,512]{1,0:T(8,128)(2,1)S(1)} custom-call(s32[8]{0:T(128)S(1)} %compare_select_fusion.3.dests, bf16[768,1024]{1,0:T(8,128)(2,1)S(1)} %bitcast.13, bf16[1024,8192]{1,0:T(8,128)(2,1)} %w_ref.29, bf16[24,64,1024]{2,1,0:T(8,128)(2,1)S(1)} %shard_map.84.refs_0_), custom_call_target="tpu_custom_call" | custom-call | flops 24159191040 | bytes 4194304 | tf_op jit(solution)/shard_map/pallas_call | solution.py:81
  22.8 2.1 %collective-permute-start.11 = (bf16[768,512]{1,0:T(8,128)(2,1)S(1)}, bf16[768,512]{1,0:T(8,128)(2,1)S(1)}, u32[]{:S(2)}, u32[]{:S(2)}) collective-permute-start(bf16[768,512]{1,0:T(8,128)(2,1)S(1)} %shard_map.85.refs_2_), channel_id=1, source_target_pairs={{0,2},{2,4},{4,6},{6,7},{7,5},{5,3},{3,1},{1,0},{8,9},{10,8},{12,1... | collective-permute-start | bytes 2359304 | tf_op jit(solution)/shard_map/ppermute | solution.py:494
  24.9 2.8 %shard_map.87.after_ref = bf16[768,512]{1,0:T(8,128)(2,1)S(1)} custom-call(s32[8]{0:T(128)S(1)} %compare_select_fusion.3.dests, bf16[768,1024]{1,0:T(8,128)(2,1)S(1)} %bitcast.14, bf16[1024,8192]{1,0:T(8,128)(2,1)} %w_ref.29, f32[8,128]{1,0:T(8,128)S(1)} %shard_map.86.refs_0_), custom_call_target="tpu_custom_call" | custom-call | flops 24159191040 | bytes 4194304 | tf_op jit(solution)/shard_map/pallas_call | solution.py:81
  27.8 6.4 %shard_map.88 = (f32[64,384]{1,0:T(8,128)S(1)}, f32[64,384]{1,0:T(8,128)S(1)}) custom-call(s32[24]{0:T(128)S(1)} %compare_convert_fusion.local, s32[24]{0:T(128)S(1)} %get-tuple-element.26.index, s32[1]{0:T(128)} %bitcast.1.side, bf16[768,1024]{1,0:T(8,128)(2,1)S(1)} %bitcast.15, s32[3,256]{1,0:T(4,128)S(1)} %copy-done.8, bf16[96,64,1024]{2,1,0:T(8,128)(2,1)} %table_ref.5, ...), custom_call_target="tpu_custom_call" | custom-call | flops 12079595520 | bytes 4718592 | tf_op jit(solution)/shard_map/pallas_call | solution.py:246
  36.2 2.9 %shard_map.89.refs_2_ = bf16[768,512]{1,0:T(8,128)(2,1)S(1)} custom-call(s32[8]{0:T(128)S(1)} %compare_select_fusion.3.dests, bf16[768,1024]{1,0:T(8,128)(2,1)S(1)} %bitcast.16, bf16[1024,8192]{1,0:T(8,128)(2,1)} %w_ref.29, bf16[768,256]{1,0:T(8,128)(2,1)S(1)} %collective-permute-done.3.refs_0_, bf16[768,256]{1,0:T(8,128)(2,1)S(1)} %collective-permute-done.4.refs_1_, ...), custom_call_target="tpu_custom_call" | custom-call | flops 24159191040 | bytes 4194304 | tf_op jit(solution)/shard_map/pallas_call | solution.py:81
  40.8 2.9 %shard_map.90.refs_0_.after_ref = bf16[768,512]{1,0:T(8,128)(2,1)S(1)} custom-call(s32[8]{0:T(128)S(1)} %compare_select_fusion.3.dests, bf16[768,1024]{1,0:T(8,128)(2,1)S(1)} %bitcast.17, bf16[1024,8192]{1,0:T(8,128)(2,1)} %w_ref.29, bf16[768,256]{1,0:T(8,128)(2,1)S(1)} %collective-permute-done.1.refs_1_.refs_0_, ...), custom_call_target="tpu_custom_call" | custom-call | flops 24159191040 | bytes 4194304 | tf_op jit(solution)/shard_map/pallas_call | solution.py:81
  47.6 2.8 %shard_map.93.refs_1_ = bf16[768,512]{1,0:T(8,128)(2,1)S(1)} custom-call(s32[8]{0:T(128)S(1)} %compare_select_fusion.3.dests, bf16[768,1024]{1,0:T(8,128)(2,1)S(1)} %bitcast.18, bf16[1024,8192]{1,0:T(8,128)(2,1)} %w_ref.29, bf16[768,512]{1,0:T(8,128)(2,1)S(1)} %collective-permute-done.11.refs_0_, f32[64,384]{1,0:T(8,128)S(1)} %shard_map.92.refs_1_.low_ref), custom_call_target="tpu_custom_call" | custom-call | flops 24159191040 | bytes 4194304 | tf_op jit(solution)/shard_map/pallas_call | solution.py:81
  52.5 2.8 %shard_map.94.refs_0_.after_ref = bf16[768,512]{1,0:T(8,128)(2,1)S(1)} custom-call(s32[8]{0:T(128)S(1)} %compare_select_fusion.3.dests, bf16[768,1024]{1,0:T(8,128)(2,1)S(1)} %bitcast.19, bf16[1024,8192]{1,0:T(8,128)(2,1)} %w_ref.29, bf16[768,512]{1,0:T(8,128)(2,1)S(1)} %collective-permute-done.10.refs_0_, bf16[768,512]{1,0:T(8,128)(2,1)S(1)} %shard_map.93.refs_1_), custom_call_target="tpu_custom_call" | custom-call | flops 24159191040 | bytes 4194304 | tf_op jit(solution)/shard_map/pallas_call | solution.py:81
  56.3 9.0 %collective-permute-done.9 = f16[64,384]{1,0:T(8,128)(2,1)S(1)} collective-permute-done((f16[64,384]{1,0:T(8,128)(2,1)S(1)}, f16[64,384]{1,0:T(8,128)(2,1)S(1)}, u32[]{:S(2)}, u32[]{:S(2)}) %collective-permute-start.9) | collective-permute-done | bytes 49184 | tf_op jit(solution)/shard_map/ppermute | solution.py:520
  66.7 2.6 %collective-permute-start.15 = (f16[64,384]{1,0:T(8,128)(2,1)}, f16[64,384]{1,0:T(8,128)(2,1)}, u32[]{:S(2)}, u32[]{:S(2)}) collective-permute-start(f16[64,384]{1,0:T(8,128)(2,1)} %multiply_convert_fusion), channel_id=1, source_target_pairs={{0,4},{1,5},{2,6},{3,7},{4,0},{5,1},{6,2},{7,3},{8,12},{9,13},{10,... | collective-permute-start | bytes 147464 | tf_op jit(solution)/shard_map/ppermute | solution.py:520
  69.3 2.8 %shard_map.97.refs_1_ = bf16[768,512]{1,0:T(8,128)(2,1)S(1)} custom-call(s32[8]{0:T(128)S(1)} %compare_select_fusion.3.dests, bf16[768,1024]{1,0:T(8,128)(2,1)S(1)} %bitcast.20, bf16[1024,8192]{1,0:T(8,128)(2,1)} %w_ref.29, bf16[768,512]{1,0:T(8,128)(2,1)S(1)} %collective-permute-done.7.refs_0_, f32[64,384]{1,0:T(8,128)S(1)} %shard_map.96.refs_1_.low_ref), custom_call_target="tpu_custom_call" | custom-call | flops 24159191040 | bytes 4194304 | tf_op jit(solution)/shard_map/pallas_call | solution.py:81
  72.1 2.8 %shard_map.98.after_ref = bf16[768,512]{1,0:T(8,128)(2,1)S(1)} custom-call(s32[8]{0:T(128)S(1)} %compare_select_fusion.3.dests, bf16[768,1024]{1,0:T(8,128)(2,1)S(1)} %bitcast.21, bf16[1024,8192]{1,0:T(8,128)(2,1)} %w_ref.29, bf16[768,512]{1,0:T(8,128)(2,1)S(1)} %collective-permute-done.6.refs_0_, bf16[768,512]{1,0:T(8,128)(2,1)S(1)} %shard_map.97.refs_1_), custom_call_target="tpu_custom_call" | custom-call | flops 24159191040 | bytes 4194304 | tf_op jit(solution)/shard_map/pallas_call | solution.py:81
  77.0 2.7 %shard_map.99.refs_1_ = bf16[24,64,1024]{2,1,0:T(8,128)(2,1)S(1)} custom-call(s32[24]{0:T(128)S(1)} %copy-done.3, bf16[96,64,1024]{2,1,0:T(8,128)(2,1)} %table_ref.7, bf16[768,512]{1,0:T(8,128)(2,1)S(1)} %shard_map.98.after_ref), custom_call_target="tpu_custom_call" | custom-call | bytes 6291456 | tf_op jit(solution)/shard_map/pallas_call | solution.py:175
  79.7 2.8 %shard_map.100.refs_1_ = bf16[768,512]{1,0:T(8,128)(2,1)S(1)} custom-call(s32[8]{0:T(128)S(1)} %compare_select_fusion.3.dests, bf16[768,1024]{1,0:T(8,128)(2,1)S(1)} %bitcast.22, bf16[1024,8192]{1,0:T(8,128)(2,1)} %w_ref.29, bf16[768,512]{1,0:T(8,128)(2,1)S(1)} %collective-permute-done.14.refs_0_, bf16[24,64,1024]{2,1,0:T(8,128)(2,1)S(1)} %shard_map.99.refs_1_), custom_call_target="tpu_custom_call" | custom-call | flops 24159191040 | bytes 4194304 | tf_op jit(solution)/shard_map/pallas_call | solution.py:81
  83.2 2.8 %shard_map.101.after_ref = bf16[768,512]{1,0:T(8,128)(2,1)S(1)} custom-call(s32[8]{0:T(128)S(1)} %compare_select_fusion.3.dests, bf16[768,1024]{1,0:T(8,128)(2,1)S(1)} %bitcast.23, bf16[1024,8192]{1,0:T(8,128)(2,1)} %w_ref.29, bf16[768,512]{1,0:T(8,128)(2,1)S(1)} %collective-permute-done.13.refs_0_, bf16[768,512]{1,0:T(8,128)(2,1)S(1)} %shard_map.100.refs_1_), custom_call_target="tpu_custom_call" | custom-call | flops 24159191040 | bytes 4194304 | tf_op jit(solution)/shard_map/pallas_call | solution.py:81
  87.7 7.7 %shard_map.102 = (f32[768,1024]{1,0:T(8,128)S(1)}, bf16[24,64,1024]{2,1,0:T(8,128)(2,1)S(1)}) custom-call(s32[24]{0:T(128)S(1)} %compare_convert_fusion.local, s32[24]{0:T(128)S(1)} %copy-done.6, s32[8]{0:T(128)S(1)} %compare_select_fusion.3.dests, bf16[768,1024]{1,0:T(8,128)(2,1)S(1)} %bitcast.24, bf16[1024,8192]{1,0:T(8,128)(2,1)} %w_ref.29, ...), custom_call_target="tpu_custom_call" | custom-call | flops 48318382080 | bytes 13107200 | tf_op jit(solution)/shard_map/pallas_call | solution.py:305
  98.9 2.8 %shard_map.105.refs_1_ = bf16[768,512]{1,0:T(8,128)(2,1)S(1)} custom-call(s32[8]{0:T(128)S(1)} %compare_select_fusion.3.dests, bf16[768,1024]{1,0:T(8,128)(2,1)S(1)} %bitcast.25, bf16[1024,8192]{1,0:T(8,128)(2,1)} %w_ref.29, bf16[768,512]{1,0:T(8,128)(2,1)S(1)} %collective-permute-done.18.refs_0_, bf16[64,384]{1,0:T(8,128)(2,1)S(1)} %shard_map.104.refs_1_.low_ref), custom_call_target="tpu_custom_call" | custom-call | flops 24159191040 | bytes 4194304 | tf_op jit(solution)/shard_map/pallas_call | solution.py:81
  103.7 2.8 %shard_map.106.after_ref = bf16[768,512]{1,0:T(8,128)(2,1)S(1)} custom-call(s32[8]{0:T(128)S(1)} %compare_select_fusion.3.dests, bf16[768,1024]{1,0:T(8,128)(2,1)S(1)} %bitcast.26, bf16[1024,8192]{1,0:T(8,128)(2,1)} %w_ref.29, bf16[768,512]{1,0:T(8,128)(2,1)S(1)} %collective-permute-done.17.refs_0_, bf16[768,512]{1,0:T(8,128)(2,1)S(1)} %shard_map.105.refs_1_), custom_call_target="tpu_custom_call" | custom-call | flops 24159191040 | bytes 4194304 | tf_op jit(solution)/shard_map/pallas_call | solution.py:81
  106.6 8.6 %collective-permute-done.16.other_ref = bf16[64,384]{1,0:T(8,128)(2,1)S(1)} collective-permute-done((bf16[64,384]{1,0:T(8,128)(2,1)S(1)}, bf16[64,384]{1,0:T(8,128)(2,1)S(1)}, u32[]{:S(2)}, u32[]{:S(2)}) %collective-permute-start.16) | collective-permute-done | bytes 49184 | tf_op jit(solution)/shard_map/ppermute | solution.py:520
  117.2 11.1 %collective-permute-done.22.last_ref = bf16[768,512]{1,0:T(8,128)(2,1)S(1)} collective-permute-done((bf16[768,512]{1,0:T(8,128)(2,1)S(1)}, bf16[768,512]{1,0:T(8,128)(2,1)S(1)}, u32[]{:S(2)}, u32[]{:S(2)}) %collective-permute-start.22) | collective-permute-done | bytes 786464 | tf_op jit(solution)/shard_map/ppermute | solution.py:494
  (97 shorter events, 34.0 us)
Async XLA Ops:
  0.0 15.1 %copy-start = (s32[192]{0:T(256)S(1)}, s32[192]{0:T(256)}, u32[]{:S(2)}) copy-start(s32[192]{0:T(256)} %param.12) | copy-start | bytes 2308
  0.0 13.6 %collective-permute-start = (s32[3,2,4]{2,1,0:T(2,128)}, s32[3,2,4]{2,1,0:T(2,128)}, u32[]{:S(2)}, u32[]{:S(2)}) collective-permute-start(s32[3,2,4]{2,1,0:T(2,128)} %param.13), channel_id=1, source_target_pairs={{0,8},{8,0},{1,9},{9,1},{2,10},{10,2},{3,11},{11,3},{4,12},{12,4},... | collective-permute-start | bytes 296 | tf_op jit(solution)/shard_map/ppermute | solution.py:500
  4.7 18.1 %collective-permute-start.1 = (bf16[768,256]{1,0:T(8,128)(2,1)}, bf16[768,256]{1,0:T(8,128)(2,1)S(1)}, u32[]{:S(2)}, u32[]{:S(2)}) collective-permute-start(bf16[768,256]{1,0:T(8,128)(2,1)} %get-tuple-element.15), channel_id=1, source_target_pairs={{0,1},{2,0},{4,2},{6,4},{7,6},{5,7},{3,5},{1,3},{8,10},{10,12},{12... | collective-permute-start | bytes 1179656 | tf_op jit(solution)/shard_map/ppermute | solution.py:505
  7.3 17.6 %collective-permute-start.3 = (bf16[768,256]{1,0:T(8,128)(2,1)}, bf16[768,256]{1,0:T(8,128)(2,1)S(1)}, u32[]{:S(2)}, u32[]{:S(2)}) collective-permute-start(bf16[768,256]{1,0:T(8,128)(2,1)} %get-tuple-element.18), channel_id=1, source_target_pairs={{0,2},{2,4},{4,6},{6,7},{7,5},{5,3},{3,1},{1,0},{8,9},{10,8},{12,1... | collective-permute-start | bytes 1179656 | tf_op jit(solution)/shard_map/ppermute | solution.py:505
  10.9 25.3 %collective-permute-start.4 = (bf16[768,256]{1,0:T(8,128)(2,1)}, bf16[768,256]{1,0:T(8,128)(2,1)S(1)}, u32[]{:S(2)}, u32[]{:S(2)}) collective-permute-start(bf16[768,256]{1,0:T(8,128)(2,1)} %get-tuple-element.19), channel_id=1, source_target_pairs={{0,2},{2,4},{4,6},{6,7},{7,5},{5,3},{3,1},{1,0},{8,9},{10,8},{12,1... | collective-permute-start | bytes 1179656 | tf_op jit(solution)/shard_map/ppermute | solution.py:505
  12.9 27.9 %collective-permute-start.2 = (bf16[768,256]{1,0:T(8,128)(2,1)S(1)}, bf16[768,256]{1,0:T(8,128)(2,1)S(1)}, u32[]{:S(2)}, u32[]{:S(2)}) collective-permute-start(bf16[768,256]{1,0:T(8,128)(2,1)S(1)} %get-tuple-element.17), channel_id=1, source_target_pairs={{0,1},{2,0},{4,2},{6,4},{7,6},{5,7},{3,5},{1,3},{8,10},{10,12},{12... | collective-permute-start | bytes 1179656 | tf_op jit(solution)/shard_map/ppermute | solution.py:505
  19.9 7.8 %collective-permute-start.5 = (bf16[24,64,1024]{2,1,0:T(8,128)(2,1)S(1)}, bf16[24,64,1024]{2,1,0:T(8,128)(2,1)S(1)}, u32[]{:S(2)}, u32[]{:S(2)}) collective-permute-start(bf16[24,64,1024]{2,1,0:T(8,128)(2,1)S(1)} %shard_map.84.refs_0_), channel_id=1, source_target_pairs={{0,8},{8,0},{1,9},{9,1},{2,10},{10,2},{3,11},{11,3},{4,12},{12,4},... | collective-permute-start | bytes 9437192 | tf_op jit(solution)/shard_map/ppermute | solution.py:511
  22.8 24.8 %collective-permute-start.11 = (bf16[768,512]{1,0:T(8,128)(2,1)S(1)}, bf16[768,512]{1,0:T(8,128)(2,1)S(1)}, u32[]{:S(2)}, u32[]{:S(2)}) collective-permute-start(bf16[768,512]{1,0:T(8,128)(2,1)S(1)} %shard_map.85.refs_2_), channel_id=1, source_target_pairs={{0,2},{2,4},{4,6},{6,7},{7,5},{5,3},{3,1},{1,0},{8,9},{10,8},{12,1... | collective-permute-start | bytes 2359304 | tf_op jit(solution)/shard_map/ppermute | solution.py:494
  27.7 24.8 %collective-permute-start.10 = (bf16[768,512]{1,0:T(8,128)(2,1)S(1)}, bf16[768,512]{1,0:T(8,128)(2,1)S(1)}, u32[]{:S(2)}, u32[]{:S(2)}) collective-permute-start(bf16[768,512]{1,0:T(8,128)(2,1)S(1)} %shard_map.87.after_ref), channel_id=1, source_target_pairs={{0,1},{2,0},{4,2},{6,4},{7,6},{5,7},{3,5},{1,3},{8,10},{10,12},{12... | collective-permute-start | bytes 2359304 | tf_op jit(solution)/shard_map/ppermute | solution.py:494
  34.2 12.6 %collective-permute-start.8 = (f16[64,384]{1,0:T(8,128)(2,1)S(1)}, f16[64,384]{1,0:T(8,128)(2,1)S(1)}, u32[]{:S(2)}, u32[]{:S(2)}) collective-permute-start(f16[64,384]{1,0:T(8,128)(2,1)S(1)} %multiply_convert_fusion.2), channel_id=1, source_target_pairs={{0,1},{1,0},{2,3},{3,2},{4,5},{5,4},{6,7},{7,6},{8,9},{9,8},{10,11... | collective-permute-start | bytes 147464 | tf_op jit(solution)/shard_map/ppermute | solution.py:520
  39.2 30.1 %collective-permute-start.7 = (bf16[768,512]{1,0:T(8,128)(2,1)S(1)}, bf16[768,512]{1,0:T(8,128)(2,1)S(1)}, u32[]{:S(2)}, u32[]{:S(2)}) collective-permute-start(bf16[768,512]{1,0:T(8,128)(2,1)S(1)} %shard_map.89.refs_2_), channel_id=1, source_target_pairs={{0,2},{2,4},{4,6},{6,7},{7,5},{5,3},{3,1},{1,0},{8,9},{10,8},{12,1... | collective-permute-start | bytes 2359304 | tf_op jit(solution)/shard_map/ppermute | solution.py:494
  43.8 28.3 %collective-permute-start.6 = (bf16[768,512]{1,0:T(8,128)(2,1)S(1)}, bf16[768,512]{1,0:T(8,128)(2,1)S(1)}, u32[]{:S(2)}, u32[]{:S(2)}) collective-permute-start(bf16[768,512]{1,0:T(8,128)(2,1)S(1)} %shard_map.90.refs_0_.after_ref), channel_id=1, source_target_pairs={{0,1},{2,0},{4,2},{6,4},{7,6},{5,7},{3,5},{1,3},{8,10},{10,12},{12... | collective-permute-start | bytes 2359304 | tf_op jit(solution)/shard_map/ppermute | solution.py:494
  47.5 17.8 %collective-permute-start.9 = (f16[64,384]{1,0:T(8,128)(2,1)S(1)}, f16[64,384]{1,0:T(8,128)(2,1)S(1)}, u32[]{:S(2)}, u32[]{:S(2)}) collective-permute-start(f16[64,384]{1,0:T(8,128)(2,1)S(1)} %multiply_convert_fusion.1), channel_id=1, source_target_pairs={{0,2},{1,3},{2,0},{3,1},{4,6},{5,7},{6,4},{7,5},{8,10},{9,11},{10,... | collective-permute-start | bytes 147464 | tf_op jit(solution)/shard_map/ppermute | solution.py:520
  50.4 29.3 %collective-permute-start.14 = (bf16[768,512]{1,0:T(8,128)(2,1)S(1)}, bf16[768,512]{1,0:T(8,128)(2,1)S(1)}, u32[]{:S(2)}, u32[]{:S(2)}) collective-permute-start(bf16[768,512]{1,0:T(8,128)(2,1)S(1)} %shard_map.93.refs_1_), channel_id=1, source_target_pairs={{0,2},{2,4},{4,6},{6,7},{7,5},{5,3},{3,1},{1,0},{8,9},{10,8},{12,1... | collective-permute-start | bytes 2359304 | tf_op jit(solution)/shard_map/ppermute | solution.py:494
  55.2 27.5 %collective-permute-start.13 = (bf16[768,512]{1,0:T(8,128)(2,1)S(1)}, bf16[768,512]{1,0:T(8,128)(2,1)S(1)}, u32[]{:S(2)}, u32[]{:S(2)}) collective-permute-start(bf16[768,512]{1,0:T(8,128)(2,1)S(1)} %shard_map.94.refs_0_.after_ref), channel_id=1, source_target_pairs={{0,1},{2,0},{4,2},{6,4},{7,6},{5,7},{3,5},{1,3},{8,10},{10,12},{12... | collective-permute-start | bytes 2359304 | tf_op jit(solution)/shard_map/ppermute | solution.py:494
  66.7 29.4 %collective-permute-start.15 = (f16[64,384]{1,0:T(8,128)(2,1)}, f16[64,384]{1,0:T(8,128)(2,1)}, u32[]{:S(2)}, u32[]{:S(2)}) collective-permute-start(f16[64,384]{1,0:T(8,128)(2,1)} %multiply_convert_fusion), channel_id=1, source_target_pairs={{0,4},{1,5},{2,6},{3,7},{4,0},{5,1},{6,2},{7,3},{8,12},{9,13},{10,... | collective-permute-start | bytes 147464 | tf_op jit(solution)/shard_map/ppermute | solution.py:520
  72.1 26.8 %collective-permute-start.18 = (bf16[768,512]{1,0:T(8,128)(2,1)S(1)}, bf16[768,512]{1,0:T(8,128)(2,1)S(1)}, u32[]{:S(2)}, u32[]{:S(2)}) collective-permute-start(bf16[768,512]{1,0:T(8,128)(2,1)S(1)} %shard_map.97.refs_1_), channel_id=1, source_target_pairs={{0,2},{2,4},{4,6},{6,7},{7,5},{5,3},{3,1},{1,0},{8,9},{10,8},{12,1... | collective-permute-start | bytes 2359304 | tf_op jit(solution)/shard_map/ppermute | solution.py:494
  74.9 28.8 %collective-permute-start.17 = (bf16[768,512]{1,0:T(8,128)(2,1)S(1)}, bf16[768,512]{1,0:T(8,128)(2,1)S(1)}, u32[]{:S(2)}, u32[]{:S(2)}) collective-permute-start(bf16[768,512]{1,0:T(8,128)(2,1)S(1)} %shard_map.98.after_ref), channel_id=1, source_target_pairs={{0,1},{2,0},{4,2},{6,4},{7,6},{5,7},{3,5},{1,3},{8,10},{10,12},{12... | collective-permute-start | bytes 2359304 | tf_op jit(solution)/shard_map/ppermute | solution.py:494
  79.7 6.4 %collective-permute-start.12 = (bf16[24,64,1024]{2,1,0:T(8,128)(2,1)S(1)}, bf16[24,64,1024]{2,1,0:T(8,128)(2,1)S(1)}, u32[]{:S(2)}, u32[]{:S(2)}) collective-permute-start(bf16[24,64,1024]{2,1,0:T(8,128)(2,1)S(1)} %shard_map.99.refs_1_), channel_id=1, source_target_pairs={{0,8},{8,0},{1,9},{9,1},{2,10},{10,2},{3,11},{11,3},{4,12},{12,4},... | collective-permute-start | bytes 9437192 | tf_op jit(solution)/shard_map/ppermute | solution.py:531
  82.8 34.2 %collective-permute-start.20 = (bf16[768,512]{1,0:T(8,128)(2,1)S(1)}, bf16[768,512]{1,0:T(8,128)(2,1)S(1)}, u32[]{:S(2)}, u32[]{:S(2)}) collective-permute-start(bf16[768,512]{1,0:T(8,128)(2,1)S(1)} %shard_map.100.refs_1_), channel_id=1, source_target_pairs={{0,2},{2,4},{4,6},{6,7},{7,5},{5,3},{3,1},{1,0},{8,9},{10,8},{12,1... | collective-permute-start | bytes 2359304 | tf_op jit(solution)/shard_map/ppermute | solution.py:494
  86.0 30.9 %collective-permute-start.19 = (bf16[768,512]{1,0:T(8,128)(2,1)S(1)}, bf16[768,512]{1,0:T(8,128)(2,1)S(1)}, u32[]{:S(2)}, u32[]{:S(2)}) collective-permute-start(bf16[768,512]{1,0:T(8,128)(2,1)S(1)} %shard_map.101.after_ref), channel_id=1, source_target_pairs={{0,1},{2,0},{4,2},{6,4},{7,6},{5,7},{3,5},{1,3},{8,10},{10,12},{12... | collective-permute-start | bytes 2359304 | tf_op jit(solution)/shard_map/ppermute | solution.py:494
  98.5 16.8 %collective-permute-start.16 = (bf16[64,384]{1,0:T(8,128)(2,1)S(1)}, bf16[64,384]{1,0:T(8,128)(2,1)S(1)}, u32[]{:S(2)}, u32[]{:S(2)}) collective-permute-start(bf16[64,384]{1,0:T(8,128)(2,1)S(1)} %shard_map.104.refs_1_.low_ref), channel_id=1, source_target_pairs={{0,1},{1,0},{2,3},{3,2},{4,5},{5,4},{6,7},{7,6},{8,9},{9,8},{10,11... | collective-permute-start | bytes 147464 | tf_op jit(solution)/shard_map/ppermute | solution.py:520
  101.7 26.6 %collective-permute-start.22 = (bf16[768,512]{1,0:T(8,128)(2,1)S(1)}, bf16[768,512]{1,0:T(8,128)(2,1)S(1)}, u32[]{:S(2)}, u32[]{:S(2)}) collective-permute-start(bf16[768,512]{1,0:T(8,128)(2,1)S(1)} %shard_map.105.refs_1_), channel_id=1, source_target_pairs={{0,2},{2,4},{4,6},{6,7},{7,5},{5,3},{3,1},{1,0},{8,9},{10,8},{12,1... | collective-permute-start | bytes 2359304 | tf_op jit(solution)/shard_map/ppermute | solution.py:494
  106.5 23.3 %collective-permute-start.21 = (bf16[768,512]{1,0:T(8,128)(2,1)S(1)}, bf16[768,512]{1,0:T(8,128)(2,1)S(1)}, u32[]{:S(2)}, u32[]{:S(2)}) collective-permute-start(bf16[768,512]{1,0:T(8,128)(2,1)S(1)} %shard_map.106.after_ref), channel_id=1, source_target_pairs={{0,1},{2,0},{4,2},{6,4},{7,6},{5,7},{3,5},{1,3},{8,10},{10,12},{12... | collective-permute-start | bytes 2359304 | tf_op jit(solution)/shard_map/ppermute | solution.py:494
  (13 other events, 85.8 us)

commit v19 on v18

--- a/solution.py
+++ b/solution.py
@@ -397,56 +397,47 @@
     )(own, left, right)
 
 
-def finish_kernel(half, live, own_ref, last_ref, *refs):
-    out_ref, held, sems = refs[-3:]
+def finish_kernel(live, own_ref, left_ref, right_ref, out_ref, held, sems):
     rows, cols = held.shape
+    half = cols // 2
     count = rows // live.shape[0]
-    columns = slice(half * cols, (half + 1) * cols)
     part = rows // sems.shape[0]
     copies = []
     for at in range(sems.shape[0]):
         for chunk in chunks(part):
             here = slice(at * part + chunk.start, at * part + chunk.stop)
-            total = own_ref[here, columns] + last_ref[here, :].astype(jnp.float32)
-            row = here.start % count + lax.broadcasted_iota(jnp.int32, total.shape, 0)
+            row = here.start % count + lax.broadcasted_iota(
+                jnp.int32, (here.stop - here.start, half), 0
+            )
             alive = row < live[here.start // count]
-            held[here, :] = jnp.where(alive, total, 0.0).astype(held.dtype)
+            for columns, last_ref in ((slice(0, half), left_ref), (slice(half, cols), right_ref)):
+                total = own_ref[here, columns] + last_ref[here, :].astype(jnp.float32)
+                held[here, columns] = jnp.where(alive, total, 0.0).astype(held.dtype)
         rows_at = pl.ds(at * part, part)
-        copies.append(
-            pltpu.make_async_copy(held.at[rows_at], out_ref.at[rows_at, columns], sems.at[at])
-        )
+        copies.append(pltpu.make_async_copy(held.at[rows_at], out_ref.at[rows_at], sems.at[at]))
         copies[-1].start()
     for copy in copies:
         copy.wait()
 
 
-def finish(live, half, own, last, result):
+def finish(live, own, left, right):
     rows, cols = own.shape
-    steps = live.shape[0]
-    in_specs = [WHOLE, WHOLE]
-    operands = [own, last]
-    aliases = {}
-    if result is not None:
-        in_specs.append(ANYWHERE)
-        operands.append(result)
-        aliases = {3: 0}
-    return pl.pallas_call(
-        functools.partial(finish_kernel, half),
+    return pl.pallas_call(
+        finish_kernel,
         grid_spec=pltpu.PrefetchScalarGridSpec(
             num_scalar_prefetch=1,
             grid=(1,),
-            in_specs=in_specs,
+            in_specs=[WHOLE] * 3,
             out_specs=ANYWHERE,
             scratch_shapes=[
-                pltpu.VMEM((rows, cols // 2), jnp.bfloat16),
-                pltpu.SemaphoreType.DMA((2 * steps,)),
+                pltpu.VMEM((rows, cols), jnp.bfloat16),
+                pltpu.SemaphoreType.DMA((4 * live.shape[0],)),
             ],
         ),
         out_shape=jax.ShapeDtypeStruct((rows, cols), jnp.bfloat16),
-        input_output_aliases=aliases,
-        compiler_params=params(),
-        cost_estimate=cost(0, rows * cols * 5),
-    )(live, *operands)
+        compiler_params=params(),
+        cost_estimate=cost(0, rows * cols * 10),
+    )(live, own, left, right)
 
 
 def per_device(
@@ -543,9 +534,7 @@
     last = turn(number, last)
     own = add_delta(sizes, side, own, up_pages, row_list_position, low, other, last)
     own = join(own, arrived[0, -1][0], arrived[1, 1][0])
-    result = None
-    for half, sign, _ in pairs[0]:
-        result = finish(live_row_count.reshape(-1), half, own, arrived[half, sign][0], result)
+    result = finish(live_row_count.reshape(-1), own, arrived[0, 1][0], arrived[1, -1][0])
     return result.reshape(steps, row_count, -1)
 
 

time: 132 us -> 132 us (level)
  Pallas kernels: 64.9 us -> 62.8 us
  waiting for transfers between devices: 32.1 us -> 33.5 us
    pallas_call x2 -> x1, Pallas kernels: 3 us -> 1.88 us  [finish(): pl.pallas_call(finish_kernel, grid_spec=pltpu.PrefetchScalarGridSpec(num_...]
  transfers between devices with their start and end apart: 23 -> 23, of which waited for: 6 -> 6; matrix products, arithmetic and copies ran while one was open for 7% -> 7% of each run, Pallas kernels for 48% -> 46%
where the time goes in v19:
time: 132 us; the launch traced here: 131 us
  Pallas kernels  62.8 us (48%)
  waiting for transfers between devices  33.5 us (25%)
  starting transfers between devices  24.2 us (18%)
  local copies, waits for them, and re-layouts  5.53 us (4%)
  other arithmetic  4.86 us (4%)
    pallas_call x12, Pallas kernels, hop(): pl.pallas_call(functools.partial(hop_kernel, tuple(range(len(received))))...  33.7 us
    ppermute x4, waiting for transfers between devices, over(): return lax.ppermute(value, 'tp', [(i, i ^ apart) for i in range(size)])  20 us
    ppermute x12, waiting for transfers between devices, turn(): arrived[half, sign] = [lax.ppermute(last, ('inst', 'tp'), moves)]  13.5 us
    ppermute x12, starting transfers between devices, turn(): arrived[half, sign] = [lax.ppermute(last, ('inst', 'tp'), moves)]  13.2 us
    pallas_call x2, Pallas kernels, first_pieces(): pl.pallas_call(functools.partial(first_kernel, after is not None), grid_s...  7.85 us
    pallas_call x1, Pallas kernels, own_terms(): pl.pallas_call(own_kernel, grid_spec=pltpu.PrefetchScalarGridSpec(num_sca...  7.24 us
    pallas_call x1, Pallas kernels, low_rank(): pl.pallas_call(functools.partial(low_kernel, sizes), grid_spec=pltpu.Pref...  5.89 us
    ppermute x4, starting transfers between devices, over(): return lax.ppermute(value, 'tp', [(i, i ^ apart) for i in range(size)])  5.82 us
  transfers between devices with their start and end apart: 23, of which 6 were waited for; matrix products, arithmetic and copies ran while one was open for 7% of the time, Pallas kernels for 46%

profile of v19, /device:TPU:0, one launch (start us, length us, event | category | flops | bytes accessed | tf_op | source)
XLA Modules:
  0.0 131.4 jit_solution(2350048011238656652)
XLA Ops:
  0.5 4.3 %shard_map.82 = (bf16[768,256]{1,0:T(8,128)(2,1)}, bf16[768,256]{1,0:T(8,128)(2,1)}, f32[8,128]{1,0:T(8,128)S(1)}) custom-call(s32[8]{0:T(128)S(1)} %compare_select_fusion.3.dests, bf16[768,1024]{1,0:T(8,128)(2,1)} %bitcast.10, bf16[1024,8192]{1,0:T(8,128)(2,1)} %w_ref.29), custom_call_target="tpu_custom_call" | custom-call | flops 24159191040 | bytes 3407872 | tf_op jit(solution)/shard_map/pallas_call | solution.py:126
  4.7 2.5 %collective-permute-start.1 = (bf16[768,256]{1,0:T(8,128)(2,1)}, bf16[768,256]{1,0:T(8,128)(2,1)S(1)}, u32[]{:S(2)}, u32[]{:S(2)}) collective-permute-start(bf16[768,256]{1,0:T(8,128)(2,1)} %get-tuple-element.15), channel_id=1, source_target_pairs={{0,1},{2,0},{4,2},{6,4},{7,6},{5,7},{3,5},{1,3},{8,10},{10,12},{12... | collective-permute-start | bytes 1179656 | tf_op jit(solution)/shard_map/ppermute | solution.py:496
  7.3 3.6 %shard_map.83 = (bf16[768,256]{1,0:T(8,128)(2,1)}, bf16[768,256]{1,0:T(8,128)(2,1)S(1)}, f32[8,128]{1,0:T(8,128)S(1)}) custom-call(s32[8]{0:T(128)S(1)} %compare_select_fusion.3.dests, bf16[768,1024]{1,0:T(8,128)(2,1)S(1)} %bitcast.11, bf16[1024,8192]{1,0:T(8,128)(2,1)} %w_ref.29, f32[8,128]{1,0:T(8,128)S(1)} %get-tuple-element.16.refs_0_), custom_call_target="tpu_custom_call" | custom-call | flops 24159191040 | bytes 3407872 | tf_op jit(solution)/shard_map/pallas_call | solution.py:126
  17.2 2.7 %shard_map.84.refs_0_ = bf16[24,64,1024]{2,1,0:T(8,128)(2,1)S(1)} custom-call(s32[24]{0:T(128)S(1)} %get-tuple-element.25.index, bf16[96,64,1024]{2,1,0:T(8,128)(2,1)} %table_ref.5, f32[8,128]{1,0:T(8,128)S(1)} %get-tuple-element.20.after_ref), custom_call_target="tpu_custom_call" | custom-call | bytes 6291456 | tf_op jit(solution)/shard_map/pallas_call | solution.py:175
  20.0 2.8 %shard_map.85.refs_2_ = bf16[768,512]{1,0:T(8,128)(2,1)S(1)} custom-call(s32[8]{0:T(128)S(1)} %compare_select_fusion.3.dests, bf16[768,1024]{1,0:T(8,128)(2,1)S(1)} %bitcast.12, bf16[1024,8192]{1,0:T(8,128)(2,1)} %w_ref.29, bf16[24,64,1024]{2,1,0:T(8,128)(2,1)S(1)} %shard_map.84.refs_0_), custom_call_target="tpu_custom_call" | custom-call | flops 24159191040 | bytes 4194304 | tf_op jit(solution)/shard_map/pallas_call | solution.py:81
  24.9 2.8 %shard_map.87.after_ref = bf16[768,512]{1,0:T(8,128)(2,1)S(1)} custom-call(s32[8]{0:T(128)S(1)} %compare_select_fusion.3.dests, bf16[768,1024]{1,0:T(8,128)(2,1)S(1)} %bitcast.13, bf16[1024,8192]{1,0:T(8,128)(2,1)} %w_ref.29, f32[8,128]{1,0:T(8,128)S(1)} %shard_map.86.refs_0_), custom_call_target="tpu_custom_call" | custom-call | flops 24159191040 | bytes 4194304 | tf_op jit(solution)/shard_map/pallas_call | solution.py:81
  27.8 5.9 %shard_map.88 = (f32[64,384]{1,0:T(8,128)S(1)}, f32[64,384]{1,0:T(8,128)S(1)}) custom-call(s32[24]{0:T(128)S(1)} %compare_convert_fusion.local, s32[24]{0:T(128)S(1)} %get-tuple-element.26.index, s32[1]{0:T(128)} %bitcast.1.side, bf16[768,1024]{1,0:T(8,128)(2,1)S(1)} %bitcast.14, s32[3,256]{1,0:T(4,128)S(1)} %copy-done.8, bf16[96,64,1024]{2,1,0:T(8,128)(2,1)} %table_ref.5, ...), custom_call_target="tpu_custom_call" | custom-call | flops 12079595520 | bytes 4718592 | tf_op jit(solution)/shard_map/pallas_call | solution.py:246
  35.7 2.9 %shard_map.89.refs_2_ = bf16[768,512]{1,0:T(8,128)(2,1)S(1)} custom-call(s32[8]{0:T(128)S(1)} %compare_select_fusion.3.dests, bf16[768,1024]{1,0:T(8,128)(2,1)S(1)} %bitcast.15, bf16[1024,8192]{1,0:T(8,128)(2,1)} %w_ref.29, bf16[768,256]{1,0:T(8,128)(2,1)S(1)} %collective-permute-done.3.refs_0_, bf16[768,256]{1,0:T(8,128)(2,1)S(1)} %collective-permute-done.4.refs_1_, ...), custom_call_target="tpu_custom_call" | custom-call | flops 24159191040 | bytes 4194304 | tf_op jit(solution)/shard_map/pallas_call | solution.py:81
  40.3 2.9 %shard_map.90.refs_0_.after_ref = bf16[768,512]{1,0:T(8,128)(2,1)S(1)} custom-call(s32[8]{0:T(128)S(1)} %compare_select_fusion.3.dests, bf16[768,1024]{1,0:T(8,128)(2,1)S(1)} %bitcast.16, bf16[1024,8192]{1,0:T(8,128)(2,1)} %w_ref.29, bf16[768,256]{1,0:T(8,128)(2,1)S(1)} %collective-permute-done.1.refs_1_.refs_0_, ...), custom_call_target="tpu_custom_call" | custom-call | flops 24159191040 | bytes 4194304 | tf_op jit(solution)/shard_map/pallas_call | solution.py:81
  44.3 2.5 %collective-permute-done.8 = f16[64,384]{1,0:T(8,128)(2,1)S(1)} collective-permute-done((f16[64,384]{1,0:T(8,128)(2,1)S(1)}, f16[64,384]{1,0:T(8,128)(2,1)S(1)}, u32[]{:S(2)}, u32[]{:S(2)}) %collective-permute-start.8) | collective-permute-done | bytes 49184 | tf_op jit(solution)/shard_map/ppermute | solution.py:511
  47.6 2.8 %shard_map.93.refs_1_ = bf16[768,512]{1,0:T(8,128)(2,1)S(1)} custom-call(s32[8]{0:T(128)S(1)} %compare_select_fusion.3.dests, bf16[768,1024]{1,0:T(8,128)(2,1)S(1)} %bitcast.17, bf16[1024,8192]{1,0:T(8,128)(2,1)} %w_ref.29, bf16[768,512]{1,0:T(8,128)(2,1)S(1)} %collective-permute-done.11.refs_0_, f32[64,384]{1,0:T(8,128)S(1)} %shard_map.92.refs_1_.low_ref), custom_call_target="tpu_custom_call" | custom-call | flops 24159191040 | bytes 4194304 | tf_op jit(solution)/shard_map/pallas_call | solution.py:81
  52.5 2.8 %shard_map.94.refs_0_.after_ref = bf16[768,512]{1,0:T(8,128)(2,1)S(1)} custom-call(s32[8]{0:T(128)S(1)} %compare_select_fusion.3.dests, bf16[768,1024]{1,0:T(8,128)(2,1)S(1)} %bitcast.18, bf16[1024,8192]{1,0:T(8,128)(2,1)} %w_ref.29, bf16[768,512]{1,0:T(8,128)(2,1)S(1)} %collective-permute-done.10.refs_0_, bf16[768,512]{1,0:T(8,128)(2,1)S(1)} %shard_map.93.refs_1_), custom_call_target="tpu_custom_call" | custom-call | flops 24159191040 | bytes 4194304 | tf_op jit(solution)/shard_map/pallas_call | solution.py:81
  56.3 8.5 %collective-permute-done.9 = f16[64,384]{1,0:T(8,128)(2,1)S(1)} collective-permute-done((f16[64,384]{1,0:T(8,128)(2,1)S(1)}, f16[64,384]{1,0:T(8,128)(2,1)S(1)}, u32[]{:S(2)}, u32[]{:S(2)}) %collective-permute-start.9) | collective-permute-done | bytes 49184 | tf_op jit(solution)/shard_map/ppermute | solution.py:511
  66.2 2.6 %collective-permute-start.15 = (f16[64,384]{1,0:T(8,128)(2,1)}, f16[64,384]{1,0:T(8,128)(2,1)}, u32[]{:S(2)}, u32[]{:S(2)}) collective-permute-start(f16[64,384]{1,0:T(8,128)(2,1)} %multiply_convert_fusion), channel_id=1, source_target_pairs={{0,4},{1,5},{2,6},{3,7},{4,0},{5,1},{6,2},{7,3},{8,12},{9,13},{10,... | collective-permute-start | bytes 147464 | tf_op jit(solution)/shard_map/ppermute | solution.py:511
  68.8 2.8 %shard_map.97.refs_1_ = bf16[768,512]{1,0:T(8,128)(2,1)S(1)} custom-call(s32[8]{0:T(128)S(1)} %compare_select_fusion.3.dests, bf16[768,1024]{1,0:T(8,128)(2,1)S(1)} %bitcast.19, bf16[1024,8192]{1,0:T(8,128)(2,1)} %w_ref.29, bf16[768,512]{1,0:T(8,128)(2,1)S(1)} %collective-permute-done.7.refs_0_, f32[64,384]{1,0:T(8,128)S(1)} %shard_map.96.refs_1_.low_ref), custom_call_target="tpu_custom_call" | custom-call | flops 24159191040 | bytes 4194304 | tf_op jit(solution)/shard_map/pallas_call | solution.py:81
  71.6 2.8 %shard_map.98.after_ref = bf16[768,512]{1,0:T(8,128)(2,1)S(1)} custom-call(s32[8]{0:T(128)S(1)} %compare_select_fusion.3.dests, bf16[768,1024]{1,0:T(8,128)(2,1)S(1)} %bitcast.20, bf16[1024,8192]{1,0:T(8,128)(2,1)} %w_ref.29, bf16[768,512]{1,0:T(8,128)(2,1)S(1)} %collective-permute-done.6.refs_0_, bf16[768,512]{1,0:T(8,128)(2,1)S(1)} %shard_map.97.refs_1_), custom_call_target="tpu_custom_call" | custom-call | flops 24159191040 | bytes 4194304 | tf_op jit(solution)/shard_map/pallas_call | solution.py:81
  76.5 2.7 %shard_map.99.refs_1_ = bf16[24,64,1024]{2,1,0:T(8,128)(2,1)S(1)} custom-call(s32[24]{0:T(128)S(1)} %copy-done.3, bf16[96,64,1024]{2,1,0:T(8,128)(2,1)} %table_ref.7, bf16[768,512]{1,0:T(8,128)(2,1)S(1)} %shard_map.98.after_ref), custom_call_target="tpu_custom_call" | custom-call | bytes 6291456 | tf_op jit(solution)/shard_map/pallas_call | solution.py:175
  79.2 2.8 %shard_map.100.refs_1_ = bf16[768,512]{1,0:T(8,128)(2,1)S(1)} custom-call(s32[8]{0:T(128)S(1)} %compare_select_fusion.3.dests, bf16[768,1024]{1,0:T(8,128)(2,1)S(1)} %bitcast.21, bf16[1024,8192]{1,0:T(8,128)(2,1)} %w_ref.29, bf16[768,512]{1,0:T(8,128)(2,1)S(1)} %collective-permute-done.14.refs_0_, bf16[24,64,1024]{2,1,0:T(8,128)(2,1)S(1)} %shard_map.99.refs_1_), custom_call_target="tpu_custom_call" | custom-call | flops 24159191040 | bytes 4194304 | tf_op jit(solution)/shard_map/pallas_call | solution.py:81
  82.7 2.8 %shard_map.101.after_ref = bf16[768,512]{1,0:T(8,128)(2,1)S(1)} custom-call(s32[8]{0:T(128)S(1)} %compare_select_fusion.3.dests, bf16[768,1024]{1,0:T(8,128)(2,1)S(1)} %bitcast.22, bf16[1024,8192]{1,0:T(8,128)(2,1)} %w_ref.29, bf16[768,512]{1,0:T(8,128)(2,1)S(1)} %collective-permute-done.13.refs_0_, bf16[768,512]{1,0:T(8,128)(2,1)S(1)} %shard_map.100.refs_1_), custom_call_target="tpu_custom_call" | custom-call | flops 24159191040 | bytes 4194304 | tf_op jit(solution)/shard_map/pallas_call | solution.py:81
  87.2 7.2 %shard_map.102 = (f32[768,1024]{1,0:T(8,128)S(1)}, bf16[24,64,1024]{2,1,0:T(8,128)(2,1)S(1)}) custom-call(s32[24]{0:T(128)S(1)} %compare_convert_fusion.local, s32[24]{0:T(128)S(1)} %copy-done.6, s32[8]{0:T(128)S(1)} %compare_select_fusion.3.dests, bf16[768,1024]{1,0:T(8,128)(2,1)S(1)} %bitcast.23, bf16[1024,8192]{1,0:T(8,128)(2,1)} %w_ref.29, ...), custom_call_target="tpu_custom_call" | custom-call | flops 48318382080 | bytes 13107200 | tf_op jit(solution)/shard_map/pallas_call | solution.py:305
  98.6 2.8 %shard_map.105.refs_1_ = bf16[768,512]{1,0:T(8,128)(2,1)S(1)} custom-call(s32[8]{0:T(128)S(1)} %compare_select_fusion.3.dests, bf16[768,1024]{1,0:T(8,128)(2,1)S(1)} %bitcast.24, bf16[1024,8192]{1,0:T(8,128)(2,1)} %w_ref.29, bf16[768,512]{1,0:T(8,128)(2,1)S(1)} %collective-permute-done.18.refs_0_, bf16[64,384]{1,0:T(8,128)(2,1)S(1)} %shard_map.104.refs_1_.low_ref), custom_call_target="tpu_custom_call" | custom-call | flops 24159191040 | bytes 4194304 | tf_op jit(solution)/shard_map/pallas_call | solution.py:81
  103.5 2.8 %shard_map.106.after_ref = bf16[768,512]{1,0:T(8,128)(2,1)S(1)} custom-call(s32[8]{0:T(128)S(1)} %compare_select_fusion.3.dests, bf16[768,1024]{1,0:T(8,128)(2,1)S(1)} %bitcast.25, bf16[1024,8192]{1,0:T(8,128)(2,1)} %w_ref.29, bf16[768,512]{1,0:T(8,128)(2,1)S(1)} %collective-permute-done.17.refs_0_, bf16[768,512]{1,0:T(8,128)(2,1)S(1)} %shard_map.105.refs_1_), custom_call_target="tpu_custom_call" | custom-call | flops 24159191040 | bytes 4194304 | tf_op jit(solution)/shard_map/pallas_call | solution.py:81
  106.4 8.9 %collective-permute-done.16.other_ref = bf16[64,384]{1,0:T(8,128)(2,1)S(1)} collective-permute-done((bf16[64,384]{1,0:T(8,128)(2,1)S(1)}, bf16[64,384]{1,0:T(8,128)(2,1)S(1)}, u32[]{:S(2)}, u32[]{:S(2)}) %collective-permute-start.16) | collective-permute-done | bytes 49184 | tf_op jit(solution)/shard_map/ppermute | solution.py:511
  116.7 12.7 %collective-permute-done.22.right_ref = bf16[768,512]{1,0:T(8,128)(2,1)S(1)} collective-permute-done((bf16[768,512]{1,0:T(8,128)(2,1)S(1)}, bf16[768,512]{1,0:T(8,128)(2,1)S(1)}, u32[]{:S(2)}, u32[]{:S(2)}) %collective-permute-start.22) | collective-permute-done | bytes 786464 | tf_op jit(solution)/shard_map/ppermute | solution.py:485
  (96 shorter events, 33.1 us)
Async XLA Ops:
  0.0 15.1 %copy-start = (s32[192]{0:T(256)S(1)}, s32[192]{0:T(256)}, u32[]{:S(2)}) copy-start(s32[192]{0:T(256)} %param.12) | copy-start | bytes 2308
  0.0 13.6 %collective-permute-start = (s32[3,2,4]{2,1,0:T(2,128)}, s32[3,2,4]{2,1,0:T(2,128)}, u32[]{:S(2)}, u32[]{:S(2)}) collective-permute-start(s32[3,2,4]{2,1,0:T(2,128)} %param.13), channel_id=1, source_target_pairs={{0,8},{8,0},{1,9},{9,1},{2,10},{10,2},{3,11},{11,3},{4,12},{12,4},... | collective-permute-start | bytes 296 | tf_op jit(solution)/shard_map/ppermute | solution.py:491
  4.7 18.1 %collective-permute-start.1 = (bf16[768,256]{1,0:T(8,128)(2,1)}, bf16[768,256]{1,0:T(8,128)(2,1)S(1)}, u32[]{:S(2)}, u32[]{:S(2)}) collective-permute-start(bf16[768,256]{1,0:T(8,128)(2,1)} %get-tuple-element.15), channel_id=1, source_target_pairs={{0,1},{2,0},{4,2},{6,4},{7,6},{5,7},{3,5},{1,3},{8,10},{10,12},{12... | collective-permute-start | bytes 1179656 | tf_op jit(solution)/shard_map/ppermute | solution.py:496
  7.3 17.6 %collective-permute-start.3 = (bf16[768,256]{1,0:T(8,128)(2,1)}, bf16[768,256]{1,0:T(8,128)(2,1)S(1)}, u32[]{:S(2)}, u32[]{:S(2)}) collective-permute-start(bf16[768,256]{1,0:T(8,128)(2,1)} %get-tuple-element.18), channel_id=1, source_target_pairs={{0,2},{2,4},{4,6},{6,7},{7,5},{5,3},{3,1},{1,0},{8,9},{10,8},{12,1... | collective-permute-start | bytes 1179656 | tf_op jit(solution)/shard_map/ppermute | solution.py:496
  10.9 24.8 %collective-permute-start.4 = (bf16[768,256]{1,0:T(8,128)(2,1)}, bf16[768,256]{1,0:T(8,128)(2,1)S(1)}, u32[]{:S(2)}, u32[]{:S(2)}) collective-permute-start(bf16[768,256]{1,0:T(8,128)(2,1)} %get-tuple-element.19), channel_id=1, source_target_pairs={{0,2},{2,4},{4,6},{6,7},{7,5},{5,3},{3,1},{1,0},{8,9},{10,8},{12,1... | collective-permute-start | bytes 1179656 | tf_op jit(solution)/shard_map/ppermute | solution.py:496
  12.9 27.4 %collective-permute-start.2 = (bf16[768,256]{1,0:T(8,128)(2,1)S(1)}, bf16[768,256]{1,0:T(8,128)(2,1)S(1)}, u32[]{:S(2)}, u32[]{:S(2)}) collective-permute-start(bf16[768,256]{1,0:T(8,128)(2,1)S(1)} %get-tuple-element.17), channel_id=1, source_target_pairs={{0,1},{2,0},{4,2},{6,4},{7,6},{5,7},{3,5},{1,3},{8,10},{10,12},{12... | collective-permute-start | bytes 1179656 | tf_op jit(solution)/shard_map/ppermute | solution.py:496
  19.9 7.8 %collective-permute-start.5 = (bf16[24,64,1024]{2,1,0:T(8,128)(2,1)S(1)}, bf16[24,64,1024]{2,1,0:T(8,128)(2,1)S(1)}, u32[]{:S(2)}, u32[]{:S(2)}) collective-permute-start(bf16[24,64,1024]{2,1,0:T(8,128)(2,1)S(1)} %shard_map.84.refs_0_), channel_id=1, source_target_pairs={{0,8},{8,0},{1,9},{9,1},{2,10},{10,2},{3,11},{11,3},{4,12},{12,4},... | collective-permute-start | bytes 9437192 | tf_op jit(solution)/shard_map/ppermute | solution.py:502
  22.8 24.8 %collective-permute-start.11 = (bf16[768,512]{1,0:T(8,128)(2,1)S(1)}, bf16[768,512]{1,0:T(8,128)(2,1)S(1)}, u32[]{:S(2)}, u32[]{:S(2)}) collective-permute-start(bf16[768,512]{1,0:T(8,128)(2,1)S(1)} %shard_map.85.refs_2_), channel_id=1, source_target_pairs={{0,2},{2,4},{4,6},{6,7},{7,5},{5,3},{3,1},{1,0},{8,9},{10,8},{12,1... | collective-permute-start | bytes 2359304 | tf_op jit(solution)/shard_map/ppermute | solution.py:485
  27.7 24.8 %collective-permute-start.10 = (bf16[768,512]{1,0:T(8,128)(2,1)S(1)}, bf16[768,512]{1,0:T(8,128)(2,1)S(1)}, u32[]{:S(2)}, u32[]{:S(2)}) collective-permute-start(bf16[768,512]{1,0:T(8,128)(2,1)S(1)} %shard_map.87.after_ref), channel_id=1, source_target_pairs={{0,1},{2,0},{4,2},{6,4},{7,6},{5,7},{3,5},{1,3},{8,10},{10,12},{12... | collective-permute-start | bytes 2359304 | tf_op jit(solution)/shard_map/ppermute | solution.py:485
  33.7 13.1 %collective-permute-start.8 = (f16[64,384]{1,0:T(8,128)(2,1)S(1)}, f16[64,384]{1,0:T(8,128)(2,1)S(1)}, u32[]{:S(2)}, u32[]{:S(2)}) collective-permute-start(f16[64,384]{1,0:T(8,128)(2,1)S(1)} %multiply_convert_fusion.2), channel_id=1, source_target_pairs={{0,1},{1,0},{2,3},{3,2},{4,5},{5,4},{6,7},{7,6},{8,9},{9,8},{10,11... | collective-permute-start | bytes 147464 | tf_op jit(solution)/shard_map/ppermute | solution.py:511
  38.7 30.1 %collective-permute-start.7 = (bf16[768,512]{1,0:T(8,128)(2,1)S(1)}, bf16[768,512]{1,0:T(8,128)(2,1)S(1)}, u32[]{:S(2)}, u32[]{:S(2)}) collective-permute-start(bf16[768,512]{1,0:T(8,128)(2,1)S(1)} %shard_map.89.refs_2_), channel_id=1, source_target_pairs={{0,2},{2,4},{4,6},{6,7},{7,5},{5,3},{3,1},{1,0},{8,9},{10,8},{12,1... | collective-permute-start | bytes 2359304 | tf_op jit(solution)/shard_map/ppermute | solution.py:485
  43.3 28.4 %collective-permute-start.6 = (bf16[768,512]{1,0:T(8,128)(2,1)S(1)}, bf16[768,512]{1,0:T(8,128)(2,1)S(1)}, u32[]{:S(2)}, u32[]{:S(2)}) collective-permute-start(bf16[768,512]{1,0:T(8,128)(2,1)S(1)} %shard_map.90.refs_0_.after_ref), channel_id=1, source_target_pairs={{0,1},{2,0},{4,2},{6,4},{7,6},{5,7},{3,5},{1,3},{8,10},{10,12},{12... | collective-permute-start | bytes 2359304 | tf_op jit(solution)/shard_map/ppermute | solution.py:485
  47.5 17.3 %collective-permute-start.9 = (f16[64,384]{1,0:T(8,128)(2,1)S(1)}, f16[64,384]{1,0:T(8,128)(2,1)S(1)}, u32[]{:S(2)}, u32[]{:S(2)}) collective-permute-start(f16[64,384]{1,0:T(8,128)(2,1)S(1)} %multiply_convert_fusion.1), channel_id=1, source_target_pairs={{0,2},{1,3},{2,0},{3,1},{4,6},{5,7},{6,4},{7,5},{8,10},{9,11},{10,... | collective-permute-start | bytes 147464 | tf_op jit(solution)/shard_map/ppermute | solution.py:511
  50.4 28.8 %collective-permute-start.14 = (bf16[768,512]{1,0:T(8,128)(2,1)S(1)}, bf16[768,512]{1,0:T(8,128)(2,1)S(1)}, u32[]{:S(2)}, u32[]{:S(2)}) collective-permute-start(bf16[768,512]{1,0:T(8,128)(2,1)S(1)} %shard_map.93.refs_1_), channel_id=1, source_target_pairs={{0,2},{2,4},{4,6},{6,7},{7,5},{5,3},{3,1},{1,0},{8,9},{10,8},{12,1... | collective-permute-start | bytes 2359304 | tf_op jit(solution)/shard_map/ppermute | solution.py:485
  55.2 27.0 %collective-permute-start.13 = (bf16[768,512]{1,0:T(8,128)(2,1)S(1)}, bf16[768,512]{1,0:T(8,128)(2,1)S(1)}, u32[]{:S(2)}, u32[]{:S(2)}) collective-permute-start(bf16[768,512]{1,0:T(8,128)(2,1)S(1)} %shard_map.94.refs_0_.after_ref), channel_id=1, source_target_pairs={{0,1},{2,0},{4,2},{6,4},{7,6},{5,7},{3,5},{1,3},{8,10},{10,12},{12... | collective-permute-start | bytes 2359304 | tf_op jit(solution)/shard_map/ppermute | solution.py:485
  66.2 28.9 %collective-permute-start.15 = (f16[64,384]{1,0:T(8,128)(2,1)}, f16[64,384]{1,0:T(8,128)(2,1)}, u32[]{:S(2)}, u32[]{:S(2)}) collective-permute-start(f16[64,384]{1,0:T(8,128)(2,1)} %multiply_convert_fusion), channel_id=1, source_target_pairs={{0,4},{1,5},{2,6},{3,7},{4,0},{5,1},{6,2},{7,3},{8,12},{9,13},{10,... | collective-permute-start | bytes 147464 | tf_op jit(solution)/shard_map/ppermute | solution.py:511
  71.6 27.1 %collective-permute-start.18 = (bf16[768,512]{1,0:T(8,128)(2,1)S(1)}, bf16[768,512]{1,0:T(8,128)(2,1)S(1)}, u32[]{:S(2)}, u32[]{:S(2)}) collective-permute-start(bf16[768,512]{1,0:T(8,128)(2,1)S(1)} %shard_map.97.refs_1_), channel_id=1, source_target_pairs={{0,2},{2,4},{4,6},{6,7},{7,5},{5,3},{3,1},{1,0},{8,9},{10,8},{12,1... | collective-permute-start | bytes 2359304 | tf_op jit(solution)/shard_map/ppermute | solution.py:485
  74.4 29.1 %collective-permute-start.17 = (bf16[768,512]{1,0:T(8,128)(2,1)S(1)}, bf16[768,512]{1,0:T(8,128)(2,1)S(1)}, u32[]{:S(2)}, u32[]{:S(2)}) collective-permute-start(bf16[768,512]{1,0:T(8,128)(2,1)S(1)} %shard_map.98.after_ref), channel_id=1, source_target_pairs={{0,1},{2,0},{4,2},{6,4},{7,6},{5,7},{3,5},{1,3},{8,10},{10,12},{12... | collective-permute-start | bytes 2359304 | tf_op jit(solution)/shard_map/ppermute | solution.py:485
  79.2 6.4 %collective-permute-start.12 = (bf16[24,64,1024]{2,1,0:T(8,128)(2,1)S(1)}, bf16[24,64,1024]{2,1,0:T(8,128)(2,1)S(1)}, u32[]{:S(2)}, u32[]{:S(2)}) collective-permute-start(bf16[24,64,1024]{2,1,0:T(8,128)(2,1)S(1)} %shard_map.99.refs_1_), channel_id=1, source_target_pairs={{0,8},{8,0},{1,9},{9,1},{2,10},{10,2},{3,11},{11,3},{4,12},{12,4},... | collective-permute-start | bytes 9437192 | tf_op jit(solution)/shard_map/ppermute | solution.py:522
  82.3 34.2 %collective-permute-start.20 = (bf16[768,512]{1,0:T(8,128)(2,1)S(1)}, bf16[768,512]{1,0:T(8,128)(2,1)S(1)}, u32[]{:S(2)}, u32[]{:S(2)}) collective-permute-start(bf16[768,512]{1,0:T(8,128)(2,1)S(1)} %shard_map.100.refs_1_), channel_id=1, source_target_pairs={{0,2},{2,4},{4,6},{6,7},{7,5},{5,3},{3,1},{1,0},{8,9},{10,8},{12,1... | collective-permute-start | bytes 2359304 | tf_op jit(solution)/shard_map/ppermute | solution.py:485
  85.5 30.9 %collective-permute-start.19 = (bf16[768,512]{1,0:T(8,128)(2,1)S(1)}, bf16[768,512]{1,0:T(8,128)(2,1)S(1)}, u32[]{:S(2)}, u32[]{:S(2)}) collective-permute-start(bf16[768,512]{1,0:T(8,128)(2,1)S(1)} %shard_map.101.after_ref), channel_id=1, source_target_pairs={{0,1},{2,0},{4,2},{6,4},{7,6},{5,7},{3,5},{1,3},{8,10},{10,12},{12... | collective-permute-start | bytes 2359304 | tf_op jit(solution)/shard_map/ppermute | solution.py:485
  97.5 17.8 %collective-permute-start.16 = (bf16[64,384]{1,0:T(8,128)(2,1)S(1)}, bf16[64,384]{1,0:T(8,128)(2,1)S(1)}, u32[]{:S(2)}, u32[]{:S(2)}) collective-permute-start(bf16[64,384]{1,0:T(8,128)(2,1)S(1)} %shard_map.104.refs_1_.low_ref), channel_id=1, source_target_pairs={{0,1},{1,0},{2,3},{3,2},{4,5},{5,4},{6,7},{7,6},{8,9},{9,8},{10,11... | collective-permute-start | bytes 147464 | tf_op jit(solution)/shard_map/ppermute | solution.py:511
  101.5 28.0 %collective-permute-start.21 = (bf16[768,512]{1,0:T(8,128)(2,1)S(1)}, bf16[768,512]{1,0:T(8,128)(2,1)S(1)}, u32[]{:S(2)}, u32[]{:S(2)}) collective-permute-start(bf16[768,512]{1,0:T(8,128)(2,1)S(1)} %shard_map.105.refs_1_), channel_id=1, source_target_pairs={{0,2},{2,4},{4,6},{6,7},{7,5},{5,3},{3,1},{1,0},{8,9},{10,8},{12,1... | collective-permute-start | bytes 2359304 | tf_op jit(solution)/shard_map/ppermute | solution.py:485
  106.3 23.2 %collective-permute-start.22 = (bf16[768,512]{1,0:T(8,128)(2,1)S(1)}, bf16[768,512]{1,0:T(8,128)(2,1)S(1)}, u32[]{:S(2)}, u32[]{:S(2)}) collective-permute-start(bf16[768,512]{1,0:T(8,128)(2,1)S(1)} %shard_map.106.after_ref), channel_id=1, source_target_pairs={{0,1},{2,0},{4,2},{6,4},{7,6},{5,7},{3,5},{1,3},{8,10},{10,12},{12... | collective-permute-start | bytes 2359304 | tf_op jit(solution)/shard_map/ppermute | solution.py:485
  (13 other events, 86.3 us)

commit v20 on v18

--- a/solution.py
+++ b/solution.py
@@ -9,7 +9,6 @@
 
 VMEM_LIMIT = 40 * 1024 * 1024
 FIRST_VMEM_LIMIT = 52 * 1024 * 1024
-LOW_SCALE = 16.0
 GRAIN = 16
 SWAP = [(0, 1), (1, 0)]
 WHOLE = pl.BlockSpec(memory_space=pltpu.VMEM)
@@ -522,7 +521,7 @@
     number, turns = 2, 2 * far - 1
     apart = 1
     while apart < size:
-        sent = over(((give if apart == 1 else low) * LOW_SCALE).astype(jnp.float16), apart)
+        sent = over(give if apart == 1 else low, apart)
         until = turns - 1 if 2 * apart == size else number + 1
         while number < min(until, turns - 1):
             last = turn(number, last)
@@ -536,8 +535,6 @@
                 last = own
             number += 1
         apart *= 2
-        zero = touch(last)[0, 0]
-        sent = sent.astype(jnp.float32) * (1.0 / LOW_SCALE) + zero
         low = last = add(low, sent, jnp.float32 if apart < size else jnp.bfloat16, last)
     other = over(low, 1)
     last = turn(number, last)

time: 132 us -> 134 us (1.015)
  waiting for transfers between devices: 32.1 us -> 38.1 us
  other arithmetic: 4.86 us -> 1.45 us
    ppermute x4, waiting for transfers between devices: 19.7 us -> 22.8 us  [over(): return lax.ppermute(value, 'tp', [(i, i ^ apart) for i in range(size)])]
    ppermute x12, waiting for transfers between devices: 12.4 us -> 15.3 us  [turn(): arrived[half, sign] = [lax.ppermute(last, ('inst', 'tp'), moves)]]
    add x3 -> x0, other arithmetic: 2.74 us -> none  [per_device(): sent = sent.astype(jnp.float32) * (1.0 / LOW_SCALE) + zero]
    slice x3 -> x0, local copies, waits for them, and re-layouts: 1.63 us -> none  [per_device(): zero = touch(last)[0, 0]]
    pallas_call x3, Pallas kernels: 0.04 us -> 1.62 us  [add(): pl.pallas_call(add_kernel, in_specs=[WHOLE, WHOLE, ANYWHERE], out_specs=W...]
  transfers between devices with their start and end apart: 23 -> 23, of which waited for: 6 -> 7; matrix products, arithmetic and copies ran while one was open for 7% -> 3% of each run, Pallas kernels for 48% -> 48%
where the time goes in v20:
time: 134 us; the launch traced here: 133 us
  Pallas kernels  65.2 us (49%)
  waiting for transfers between devices  38.1 us (28%)
  starting transfers between devices  23.5 us (18%)
  local copies, waits for them, and re-layouts  4.52 us (3%)
  other arithmetic  1.45 us (1%)
    pallas_call x12, Pallas kernels, hop(): pl.pallas_call(functools.partial(hop_kernel, tuple(range(len(received))))...  33.7 us
    ppermute x4, waiting for transfers between devices, over(): return lax.ppermute(value, 'tp', [(i, i ^ apart) for i in range(size)])  22.8 us
    ppermute x12, waiting for transfers between devices, turn(): arrived[half, sign] = [lax.ppermute(last, ('inst', 'tp'), moves)]  15.3 us
    ppermute x12, starting transfers between devices, turn(): arrived[half, sign] = [lax.ppermute(last, ('inst', 'tp'), moves)]  13.5 us
    pallas_call x2, Pallas kernels, first_pieces(): pl.pallas_call(functools.partial(first_kernel, after is not None), grid_s...  7.85 us
    pallas_call x1, Pallas kernels, own_terms(): pl.pallas_call(own_kernel, grid_spec=pltpu.PrefetchScalarGridSpec(num_sca...  7.08 us
    pallas_call x1, Pallas kernels, low_rank(): pl.pallas_call(functools.partial(low_kernel, sizes), grid_spec=pltpu.Pref...  5.72 us
    pallas_call x2, Pallas kernels, collect(): pl.pallas_call(functools.partial(collect_kernel, count), grid_spec=pltpu....  5.33 us
  transfers between devices with their start and end apart: 23, of which 7 were waited for; matrix products, arithmetic and copies ran while one was open for 3% of the time, Pallas kernels for 48%

profile of v20, /device:TPU:0, one launch (start us, length us, event | category | flops | bytes accessed | tf_op | source)
XLA Modules:
  0.0 133.1 jit_solution(7360840702498103132)
XLA Ops:
  0.5 4.3 %shard_map.82 = (bf16[768,256]{1,0:T(8,128)(2,1)}, bf16[768,256]{1,0:T(8,128)(2,1)}, f32[8,128]{1,0:T(8,128)S(1)}) custom-call(s32[8]{0:T(128)S(1)} %compare_select_fusion.3.dests, bf16[768,1024]{1,0:T(8,128)(2,1)} %bitcast.8, bf16[1024,8192]{1,0:T(8,128)(2,1)} %w_ref.29), custom_call_target="tpu_custom_call" | custom-call | flops 24159191040 | bytes 3407872 | tf_op jit(solution)/shard_map/pallas_call | solution.py:125
  4.7 2.5 %collective-permute-start.1 = (bf16[768,256]{1,0:T(8,128)(2,1)}, bf16[768,256]{1,0:T(8,128)(2,1)S(1)}, u32[]{:S(2)}, u32[]{:S(2)}) collective-permute-start(bf16[768,256]{1,0:T(8,128)(2,1)} %get-tuple-element.15), channel_id=1, source_target_pairs={{0,1},{2,0},{4,2},{6,4},{7,6},{5,7},{3,5},{1,3},{8,10},{10,12},{12... | collective-permute-start | bytes 1179656 | tf_op jit(solution)/shard_map/ppermute | solution.py:504
  7.3 3.6 %shard_map.83 = (bf16[768,256]{1,0:T(8,128)(2,1)}, bf16[768,256]{1,0:T(8,128)(2,1)S(1)}, f32[8,128]{1,0:T(8,128)S(1)}) custom-call(s32[8]{0:T(128)S(1)} %compare_select_fusion.3.dests, bf16[768,1024]{1,0:T(8,128)(2,1)S(1)} %bitcast.9, bf16[1024,8192]{1,0:T(8,128)(2,1)} %w_ref.29, f32[8,128]{1,0:T(8,128)S(1)} %get-tuple-element.16.refs_0_), custom_call_target="tpu_custom_call" | custom-call | flops 24159191040 | bytes 3407872 | tf_op jit(solution)/shard_map/pallas_call | solution.py:125
  17.2 2.7 %shard_map.84.refs_0_ = bf16[24,64,1024]{2,1,0:T(8,128)(2,1)S(1)} custom-call(s32[24]{0:T(128)S(1)} %get-tuple-element.25.index, bf16[96,64,1024]{2,1,0:T(8,128)(2,1)} %table_ref.5, f32[8,128]{1,0:T(8,128)S(1)} %get-tuple-element.20.after_ref), custom_call_target="tpu_custom_call" | custom-call | bytes 6291456 | tf_op jit(solution)/shard_map/pallas_call | solution.py:174
  20.0 2.8 %shard_map.85.refs_2_ = bf16[768,512]{1,0:T(8,128)(2,1)S(1)} custom-call(s32[8]{0:T(128)S(1)} %compare_select_fusion.3.dests, bf16[768,1024]{1,0:T(8,128)(2,1)S(1)} %bitcast.10, bf16[1024,8192]{1,0:T(8,128)(2,1)} %w_ref.29, bf16[24,64,1024]{2,1,0:T(8,128)(2,1)S(1)} %shard_map.84.refs_0_), custom_call_target="tpu_custom_call" | custom-call | flops 24159191040 | bytes 4194304 | tf_op jit(solution)/shard_map/pallas_call | solution.py:80
  24.9 2.8 %shard_map.87.after_ref = bf16[768,512]{1,0:T(8,128)(2,1)S(1)} custom-call(s32[8]{0:T(128)S(1)} %compare_select_fusion.3.dests, bf16[768,1024]{1,0:T(8,128)(2,1)S(1)} %bitcast.11, bf16[1024,8192]{1,0:T(8,128)(2,1)} %w_ref.29, f32[8,128]{1,0:T(8,128)S(1)} %shard_map.86.refs_0_), custom_call_target="tpu_custom_call" | custom-call | flops 24159191040 | bytes 4194304 | tf_op jit(solution)/shard_map/pallas_call | solution.py:80
  27.8 5.7 %shard_map.88 = (f32[64,384]{1,0:T(8,128)S(1)}, f32[64,384]{1,0:T(8,128)S(1)}) custom-call(s32[24]{0:T(128)S(1)} %compare_convert_fusion.local, s32[24]{0:T(128)S(1)} %get-tuple-element.26.index, s32[1]{0:T(128)} %bitcast.1.side, bf16[768,1024]{1,0:T(8,128)(2,1)S(1)} %bitcast.12, s32[3,256]{1,0:T(4,128)S(1)} %copy-done.8, bf16[96,64,1024]{2,1,0:T(8,128)(2,1)} %table_ref.5, ...), custom_call_target="tpu_custom_call" | custom-call | flops 12079595520 | bytes 4718592 | tf_op jit(solution)/shard_map/pallas_call | solution.py:245
  35.5 2.9 %shard_map.89.refs_2_ = bf16[768,512]{1,0:T(8,128)(2,1)S(1)} custom-call(s32[8]{0:T(128)S(1)} %compare_select_fusion.3.dests, bf16[768,1024]{1,0:T(8,128)(2,1)S(1)} %bitcast.13, bf16[1024,8192]{1,0:T(8,128)(2,1)} %w_ref.29, bf16[768,256]{1,0:T(8,128)(2,1)S(1)} %collective-permute-done.3.refs_0_, bf16[768,256]{1,0:T(8,128)(2,1)S(1)} %collective-permute-done.4.refs_1_, ...), custom_call_target="tpu_custom_call" | custom-call | flops 24159191040 | bytes 4194304 | tf_op jit(solution)/shard_map/pallas_call | solution.py:80
  40.1 2.9 %shard_map.90.after_ref = bf16[768,512]{1,0:T(8,128)(2,1)S(1)} custom-call(s32[8]{0:T(128)S(1)} %compare_select_fusion.3.dests, bf16[768,1024]{1,0:T(8,128)(2,1)S(1)} %bitcast.14, bf16[1024,8192]{1,0:T(8,128)(2,1)} %w_ref.29, bf16[768,256]{1,0:T(8,128)(2,1)S(1)} %collective-permute-done.1.refs_1_.refs_0_, ...), custom_call_target="tpu_custom_call" | custom-call | flops 24159191040 | bytes 4194304 | tf_op jit(solution)/shard_map/pallas_call | solution.py:80
  43.6 4.3 %collective-permute-done.8.sent_ref = f32[64,384]{1,0:T(8,128)S(1)} collective-permute-done((f32[64,384]{1,0:T(8,128)S(1)}, f32[64,384]{1,0:T(8,128)S(1)}, u32[]{:S(2)}, u32[]{:S(2)}) %collective-permute-start.8) | collective-permute-done | bytes 98336 | tf_op jit(solution)/shard_map/ppermute | solution.py:519
  48.0 2.8 %shard_map.92.refs_1_ = bf16[768,512]{1,0:T(8,128)(2,1)S(1)} custom-call(s32[8]{0:T(128)S(1)} %compare_select_fusion.3.dests, bf16[768,1024]{1,0:T(8,128)(2,1)S(1)} %bitcast.15, bf16[1024,8192]{1,0:T(8,128)(2,1)} %w_ref.29, bf16[768,512]{1,0:T(8,128)(2,1)S(1)} %collective-permute-done.11.refs_0_, f32[64,384]{1,0:T(8,128)S(1)} %shard_map.91.refs_1_.low_ref), custom_call_target="tpu_custom_call" | custom-call | flops 24159191040 | bytes 4194304 | tf_op jit(solution)/shard_map/pallas_call | solution.py:80
  52.8 2.8 %shard_map.93.after_ref = bf16[768,512]{1,0:T(8,128)(2,1)S(1)} custom-call(s32[8]{0:T(128)S(1)} %compare_select_fusion.3.dests, bf16[768,1024]{1,0:T(8,128)(2,1)S(1)} %bitcast.16, bf16[1024,8192]{1,0:T(8,128)(2,1)} %w_ref.29, bf16[768,512]{1,0:T(8,128)(2,1)S(1)} %collective-permute-done.10.refs_0_, bf16[768,512]{1,0:T(8,128)(2,1)S(1)} %shard_map.92.refs_1_), custom_call_target="tpu_custom_call" | custom-call | flops 24159191040 | bytes 4194304 | tf_op jit(solution)/shard_map/pallas_call | solution.py:80
  56.2 9.6 %collective-permute-done.9.sent_ref = f32[64,384]{1,0:T(8,128)S(1)} collective-permute-done((f32[64,384]{1,0:T(8,128)S(1)}, f32[64,384]{1,0:T(8,128)S(1)}, u32[]{:S(2)}, u32[]{:S(2)}) %collective-permute-start.9) | collective-permute-done | bytes 98336 | tf_op jit(solution)/shard_map/ppermute | solution.py:519
  66.4 2.6 %collective-permute-start.15 = (f32[64,384]{1,0:T(8,128)}, f32[64,384]{1,0:T(8,128)}, u32[]{:S(2)}, u32[]{:S(2)}) collective-permute-start(f32[64,384]{1,0:T(8,128)} %shard_map.94.refs_1_.low_ref), channel_id=1, source_target_pairs={{0,4},{1,5},{2,6},{3,7},{4,0},{5,1},{6,2},{7,3},{8,12},{9,13},{10,... | collective-permute-start | bytes 294920 | tf_op jit(solution)/shard_map/ppermute | solution.py:519
  68.9 2.8 %shard_map.95.refs_1_ = bf16[768,512]{1,0:T(8,128)(2,1)S(1)} custom-call(s32[8]{0:T(128)S(1)} %compare_select_fusion.3.dests, bf16[768,1024]{1,0:T(8,128)(2,1)S(1)} %bitcast.17, bf16[1024,8192]{1,0:T(8,128)(2,1)} %w_ref.29, bf16[768,512]{1,0:T(8,128)(2,1)S(1)} %collective-permute-done.7.refs_0_, f32[64,384]{1,0:T(8,128)} %shard_map.94.refs_1_.low_ref), custom_call_target="tpu_custom_call" | custom-call | flops 24159191040 | bytes 4194304 | tf_op jit(solution)/shard_map/pallas_call | solution.py:80
  71.8 2.8 %shard_map.96.after_ref = bf16[768,512]{1,0:T(8,128)(2,1)S(1)} custom-call(s32[8]{0:T(128)S(1)} %compare_select_fusion.3.dests, bf16[768,1024]{1,0:T(8,128)(2,1)S(1)} %bitcast.18, bf16[1024,8192]{1,0:T(8,128)(2,1)} %w_ref.29, bf16[768,512]{1,0:T(8,128)(2,1)S(1)} %collective-permute-done.6.refs_0_, bf16[768,512]{1,0:T(8,128)(2,1)S(1)} %shard_map.95.refs_1_), custom_call_target="tpu_custom_call" | custom-call | flops 24159191040 | bytes 4194304 | tf_op jit(solution)/shard_map/pallas_call | solution.py:80
  76.7 2.7 %shard_map.97.refs_1_ = bf16[24,64,1024]{2,1,0:T(8,128)(2,1)S(1)} custom-call(s32[24]{0:T(128)S(1)} %copy-done.3, bf16[96,64,1024]{2,1,0:T(8,128)(2,1)} %table_ref.7, bf16[768,512]{1,0:T(8,128)(2,1)S(1)} %shard_map.96.after_ref), custom_call_target="tpu_custom_call" | custom-call | bytes 6291456 | tf_op jit(solution)/shard_map/pallas_call | solution.py:174
  79.4 2.8 %shard_map.98.refs_1_ = bf16[768,512]{1,0:T(8,128)(2,1)S(1)} custom-call(s32[8]{0:T(128)S(1)} %compare_select_fusion.3.dests, bf16[768,1024]{1,0:T(8,128)(2,1)S(1)} %bitcast.19, bf16[1024,8192]{1,0:T(8,128)(2,1)} %w_ref.29, bf16[768,512]{1,0:T(8,128)(2,1)S(1)} %collective-permute-done.14.refs_0_, bf16[24,64,1024]{2,1,0:T(8,128)(2,1)S(1)} %shard_map.97.refs_1_), custom_call_target="tpu_custom_call" | custom-call | flops 24159191040 | bytes 4194304 | tf_op jit(solution)/shard_map/pallas_call | solution.py:80
  84.7 2.8 %shard_map.99.after_ref = bf16[768,512]{1,0:T(8,128)(2,1)S(1)} custom-call(s32[8]{0:T(128)S(1)} %compare_select_fusion.3.dests, bf16[768,1024]{1,0:T(8,128)(2,1)S(1)} %bitcast.20, bf16[1024,8192]{1,0:T(8,128)(2,1)} %w_ref.29, bf16[768,512]{1,0:T(8,128)(2,1)S(1)} %collective-permute-done.13.refs_0_, bf16[768,512]{1,0:T(8,128)(2,1)S(1)} %shard_map.98.refs_1_), custom_call_target="tpu_custom_call" | custom-call | flops 24159191040 | bytes 4194304 | tf_op jit(solution)/shard_map/pallas_call | solution.py:80
  89.5 7.1 %shard_map.100 = (f32[768,1024]{1,0:T(8,128)S(1)}, bf16[24,64,1024]{2,1,0:T(8,128)(2,1)S(1)}) custom-call(s32[24]{0:T(128)S(1)} %compare_convert_fusion.local, s32[24]{0:T(128)S(1)} %copy-done.6, s32[8]{0:T(128)S(1)} %compare_select_fusion.3.dests, bf16[768,1024]{1,0:T(8,128)(2,1)S(1)} %bitcast.21, bf16[1024,8192]{1,0:T(8,128)(2,1)} %w_ref.29, ...), custom_call_target="tpu_custom_call" | custom-call | flops 48318382080 | bytes 13107200 | tf_op jit(solution)/shard_map/pallas_call | solution.py:304
  99.3 2.8 %shard_map.102.refs_1_ = bf16[768,512]{1,0:T(8,128)(2,1)S(1)} custom-call(s32[8]{0:T(128)S(1)} %compare_select_fusion.3.dests, bf16[768,1024]{1,0:T(8,128)(2,1)S(1)} %bitcast.22, bf16[1024,8192]{1,0:T(8,128)(2,1)} %w_ref.29, bf16[768,512]{1,0:T(8,128)(2,1)S(1)} %collective-permute-done.18.refs_0_, bf16[64,384]{1,0:T(8,128)(2,1)S(1)} %shard_map.101.refs_1_.low_ref), custom_call_target="tpu_custom_call" | custom-call | flops 24159191040 | bytes 4194304 | tf_op jit(solution)/shard_map/pallas_call | solution.py:80
  103.3 2.8 %shard_map.103.after_ref = bf16[768,512]{1,0:T(8,128)(2,1)S(1)} custom-call(s32[8]{0:T(128)S(1)} %compare_select_fusion.3.dests, bf16[768,1024]{1,0:T(8,128)(2,1)S(1)} %bitcast.23, bf16[1024,8192]{1,0:T(8,128)(2,1)} %w_ref.29, bf16[768,512]{1,0:T(8,128)(2,1)S(1)} %collective-permute-done.17.refs_0_, bf16[768,512]{1,0:T(8,128)(2,1)S(1)} %shard_map.102.refs_1_), custom_call_target="tpu_custom_call" | custom-call | flops 24159191040 | bytes 4194304 | tf_op jit(solution)/shard_map/pallas_call | solution.py:80
  107.4 9.0 %collective-permute-done.16.other_ref = bf16[64,384]{1,0:T(8,128)(2,1)S(1)} collective-permute-done((bf16[64,384]{1,0:T(8,128)(2,1)S(1)}, bf16[64,384]{1,0:T(8,128)(2,1)S(1)}, u32[]{:S(2)}, u32[]{:S(2)}) %collective-permute-start.16) | collective-permute-done | bytes 49184 | tf_op jit(solution)/shard_map/ppermute | solution.py:519
  118.6 11.1 %collective-permute-done.22.last_ref = bf16[768,512]{1,0:T(8,128)(2,1)S(1)} collective-permute-done((bf16[768,512]{1,0:T(8,128)(2,1)S(1)}, bf16[768,512]{1,0:T(8,128)(2,1)S(1)}, u32[]{:S(2)}, u32[]{:S(2)}) %collective-permute-start.22) | collective-permute-done | bytes 786464 | tf_op jit(solution)/shard_map/ppermute | solution.py:493
  (85 shorter events, 34.0 us)
Async XLA Ops:
  0.0 15.1 %copy-start = (s32[192]{0:T(256)S(1)}, s32[192]{0:T(256)}, u32[]{:S(2)}) copy-start(s32[192]{0:T(256)} %param.12) | copy-start | bytes 2308
  0.0 13.6 %collective-permute-start = (s32[3,2,4]{2,1,0:T(2,128)}, s32[3,2,4]{2,1,0:T(2,128)}, u32[]{:S(2)}, u32[]{:S(2)}) collective-permute-start(s32[3,2,4]{2,1,0:T(2,128)} %param.13), channel_id=1, source_target_pairs={{0,8},{8,0},{1,9},{9,1},{2,10},{10,2},{3,11},{11,3},{4,12},{12,4},... | collective-permute-start | bytes 296 | tf_op jit(solution)/shard_map/ppermute | solution.py:499
  4.7 18.1 %collective-permute-start.1 = (bf16[768,256]{1,0:T(8,128)(2,1)}, bf16[768,256]{1,0:T(8,128)(2,1)S(1)}, u32[]{:S(2)}, u32[]{:S(2)}) collective-permute-start(bf16[768,256]{1,0:T(8,128)(2,1)} %get-tuple-element.15), channel_id=1, source_target_pairs={{0,1},{2,0},{4,2},{6,4},{7,6},{5,7},{3,5},{1,3},{8,10},{10,12},{12... | collective-permute-start | bytes 1179656 | tf_op jit(solution)/shard_map/ppermute | solution.py:504
  7.3 17.6 %collective-permute-start.3 = (bf16[768,256]{1,0:T(8,128)(2,1)}, bf16[768,256]{1,0:T(8,128)(2,1)S(1)}, u32[]{:S(2)}, u32[]{:S(2)}) collective-permute-start(bf16[768,256]{1,0:T(8,128)(2,1)} %get-tuple-element.18), channel_id=1, source_target_pairs={{0,2},{2,4},{4,6},{6,7},{7,5},{5,3},{3,1},{1,0},{8,9},{10,8},{12,1... | collective-permute-start | bytes 1179656 | tf_op jit(solution)/shard_map/ppermute | solution.py:504
  10.9 24.6 %collective-permute-start.4 = (bf16[768,256]{1,0:T(8,128)(2,1)}, bf16[768,256]{1,0:T(8,128)(2,1)S(1)}, u32[]{:S(2)}, u32[]{:S(2)}) collective-permute-start(bf16[768,256]{1,0:T(8,128)(2,1)} %get-tuple-element.19), channel_id=1, source_target_pairs={{0,2},{2,4},{4,6},{6,7},{7,5},{5,3},{3,1},{1,0},{8,9},{10,8},{12,1... | collective-permute-start | bytes 1179656 | tf_op jit(solution)/shard_map/ppermute | solution.py:504
  12.9 27.2 %collective-permute-start.2 = (bf16[768,256]{1,0:T(8,128)(2,1)S(1)}, bf16[768,256]{1,0:T(8,128)(2,1)S(1)}, u32[]{:S(2)}, u32[]{:S(2)}) collective-permute-start(bf16[768,256]{1,0:T(8,128)(2,1)S(1)} %get-tuple-element.17), channel_id=1, source_target_pairs={{0,1},{2,0},{4,2},{6,4},{7,6},{5,7},{3,5},{1,3},{8,10},{10,12},{12... | collective-permute-start | bytes 1179656 | tf_op jit(solution)/shard_map/ppermute | solution.py:504
  19.9 7.8 %collective-permute-start.5 = (bf16[24,64,1024]{2,1,0:T(8,128)(2,1)S(1)}, bf16[24,64,1024]{2,1,0:T(8,128)(2,1)S(1)}, u32[]{:S(2)}, u32[]{:S(2)}) collective-permute-start(bf16[24,64,1024]{2,1,0:T(8,128)(2,1)S(1)} %shard_map.84.refs_0_), channel_id=1, source_target_pairs={{0,8},{8,0},{1,9},{9,1},{2,10},{10,2},{3,11},{11,3},{4,12},{12,4},... | collective-permute-start | bytes 9437192 | tf_op jit(solution)/shard_map/ppermute | solution.py:510
  22.8 25.1 %collective-permute-start.11 = (bf16[768,512]{1,0:T(8,128)(2,1)S(1)}, bf16[768,512]{1,0:T(8,128)(2,1)S(1)}, u32[]{:S(2)}, u32[]{:S(2)}) collective-permute-start(bf16[768,512]{1,0:T(8,128)(2,1)S(1)} %shard_map.85.refs_2_), channel_id=1, source_target_pairs={{0,2},{2,4},{4,6},{6,7},{7,5},{5,3},{3,1},{1,0},{8,9},{10,8},{12,1... | collective-permute-start | bytes 2359304 | tf_op jit(solution)/shard_map/ppermute | solution.py:493
  27.7 25.1 %collective-permute-start.10 = (bf16[768,512]{1,0:T(8,128)(2,1)S(1)}, bf16[768,512]{1,0:T(8,128)(2,1)S(1)}, u32[]{:S(2)}, u32[]{:S(2)}) collective-permute-start(bf16[768,512]{1,0:T(8,128)(2,1)S(1)} %shard_map.87.after_ref), channel_id=1, source_target_pairs={{0,1},{2,0},{4,2},{6,4},{7,6},{5,7},{3,5},{1,3},{8,10},{10,12},{12... | collective-permute-start | bytes 2359304 | tf_op jit(solution)/shard_map/ppermute | solution.py:493
  33.5 14.3 %collective-permute-start.8 = (f32[64,384]{1,0:T(8,128)S(1)}, f32[64,384]{1,0:T(8,128)S(1)}, u32[]{:S(2)}, u32[]{:S(2)}) collective-permute-start(f32[64,384]{1,0:T(8,128)S(1)} %get-tuple-element.22), channel_id=1, source_target_pairs={{0,1},{1,0},{2,3},{3,2},{4,5},{5,4},{6,7},{7,6},{8,9},{9,8},{10,11... | collective-permute-start | bytes 294920 | tf_op jit(solution)/shard_map/ppermute | solution.py:519
  38.5 30.5 %collective-permute-start.7 = (bf16[768,512]{1,0:T(8,128)(2,1)S(1)}, bf16[768,512]{1,0:T(8,128)(2,1)S(1)}, u32[]{:S(2)}, u32[]{:S(2)}) collective-permute-start(bf16[768,512]{1,0:T(8,128)(2,1)S(1)} %shard_map.89.refs_2_), channel_id=1, source_target_pairs={{0,2},{2,4},{4,6},{6,7},{7,5},{5,3},{3,1},{1,0},{8,9},{10,8},{12,1... | collective-permute-start | bytes 2359304 | tf_op jit(solution)/shard_map/ppermute | solution.py:493
  43.1 28.7 %collective-permute-start.6 = (bf16[768,512]{1,0:T(8,128)(2,1)S(1)}, bf16[768,512]{1,0:T(8,128)(2,1)S(1)}, u32[]{:S(2)}, u32[]{:S(2)}) collective-permute-start(bf16[768,512]{1,0:T(8,128)(2,1)S(1)} %shard_map.90.after_ref), channel_id=1, source_target_pairs={{0,1},{2,0},{4,2},{6,4},{7,6},{5,7},{3,5},{1,3},{8,10},{10,12},{12... | collective-permute-start | bytes 2359304 | tf_op jit(solution)/shard_map/ppermute | solution.py:493
  47.9 17.8 %collective-permute-start.9 = (f32[64,384]{1,0:T(8,128)S(1)}, f32[64,384]{1,0:T(8,128)S(1)}, u32[]{:S(2)}, u32[]{:S(2)}) collective-permute-start(f32[64,384]{1,0:T(8,128)S(1)} %shard_map.91.refs_1_.low_ref), channel_id=1, source_target_pairs={{0,2},{1,3},{2,0},{3,1},{4,6},{5,7},{6,4},{7,5},{8,10},{9,11},{10,... | collective-permute-start | bytes 294920 | tf_op jit(solution)/shard_map/ppermute | solution.py:519
  50.8 28.6 %collective-permute-start.14 = (bf16[768,512]{1,0:T(8,128)(2,1)S(1)}, bf16[768,512]{1,0:T(8,128)(2,1)S(1)}, u32[]{:S(2)}, u32[]{:S(2)}) collective-permute-start(bf16[768,512]{1,0:T(8,128)(2,1)S(1)} %shard_map.92.refs_1_), channel_id=1, source_target_pairs={{0,2},{2,4},{4,6},{6,7},{7,5},{5,3},{3,1},{1,0},{8,9},{10,8},{12,1... | collective-permute-start | bytes 2359304 | tf_op jit(solution)/shard_map/ppermute | solution.py:493
  55.6 29.1 %collective-permute-start.13 = (bf16[768,512]{1,0:T(8,128)(2,1)S(1)}, bf16[768,512]{1,0:T(8,128)(2,1)S(1)}, u32[]{:S(2)}, u32[]{:S(2)}) collective-permute-start(bf16[768,512]{1,0:T(8,128)(2,1)S(1)} %shard_map.93.after_ref), channel_id=1, source_target_pairs={{0,1},{2,0},{4,2},{6,4},{7,6},{5,7},{3,5},{1,3},{8,10},{10,12},{12... | collective-permute-start | bytes 2359304 | tf_op jit(solution)/shard_map/ppermute | solution.py:493
  66.4 31.9 %collective-permute-start.15 = (f32[64,384]{1,0:T(8,128)}, f32[64,384]{1,0:T(8,128)}, u32[]{:S(2)}, u32[]{:S(2)}) collective-permute-start(f32[64,384]{1,0:T(8,128)} %shard_map.94.refs_1_.low_ref), channel_id=1, source_target_pairs={{0,4},{1,5},{2,6},{3,7},{4,0},{5,1},{6,2},{7,3},{8,12},{9,13},{10,... | collective-permute-start | bytes 294920 | tf_op jit(solution)/shard_map/ppermute | solution.py:519
  71.7 27.6 %collective-permute-start.18 = (bf16[768,512]{1,0:T(8,128)(2,1)S(1)}, bf16[768,512]{1,0:T(8,128)(2,1)S(1)}, u32[]{:S(2)}, u32[]{:S(2)}) collective-permute-start(bf16[768,512]{1,0:T(8,128)(2,1)S(1)} %shard_map.95.refs_1_), channel_id=1, source_target_pairs={{0,2},{2,4},{4,6},{6,7},{7,5},{5,3},{3,1},{1,0},{8,9},{10,8},{12,1... | collective-permute-start | bytes 2359304 | tf_op jit(solution)/shard_map/ppermute | solution.py:493
  74.6 28.7 %collective-permute-start.17 = (bf16[768,512]{1,0:T(8,128)(2,1)S(1)}, bf16[768,512]{1,0:T(8,128)(2,1)S(1)}, u32[]{:S(2)}, u32[]{:S(2)}) collective-permute-start(bf16[768,512]{1,0:T(8,128)(2,1)S(1)} %shard_map.96.after_ref), channel_id=1, source_target_pairs={{0,1},{2,0},{4,2},{6,4},{7,6},{5,7},{3,5},{1,3},{8,10},{10,12},{12... | collective-permute-start | bytes 2359304 | tf_op jit(solution)/shard_map/ppermute | solution.py:493
  79.3 8.1 %collective-permute-start.12 = (bf16[24,64,1024]{2,1,0:T(8,128)(2,1)S(1)}, bf16[24,64,1024]{2,1,0:T(8,128)(2,1)S(1)}, u32[]{:S(2)}, u32[]{:S(2)}) collective-permute-start(bf16[24,64,1024]{2,1,0:T(8,128)(2,1)S(1)} %shard_map.97.refs_1_), channel_id=1, source_target_pairs={{0,8},{8,0},{1,9},{9,1},{2,10},{10,2},{3,11},{11,3},{4,12},{12,4},... | collective-permute-start | bytes 9437192 | tf_op jit(solution)/shard_map/ppermute | solution.py:530
  84.7 33.7 %collective-permute-start.20 = (bf16[768,512]{1,0:T(8,128)(2,1)S(1)}, bf16[768,512]{1,0:T(8,128)(2,1)S(1)}, u32[]{:S(2)}, u32[]{:S(2)}) collective-permute-start(bf16[768,512]{1,0:T(8,128)(2,1)S(1)} %shard_map.98.refs_1_), channel_id=1, source_target_pairs={{0,2},{2,4},{4,6},{6,7},{7,5},{5,3},{3,1},{1,0},{8,9},{10,8},{12,1... | collective-permute-start | bytes 2359304 | tf_op jit(solution)/shard_map/ppermute | solution.py:493
  87.5 30.9 %collective-permute-start.19 = (bf16[768,512]{1,0:T(8,128)(2,1)S(1)}, bf16[768,512]{1,0:T(8,128)(2,1)S(1)}, u32[]{:S(2)}, u32[]{:S(2)}) collective-permute-start(bf16[768,512]{1,0:T(8,128)(2,1)S(1)} %shard_map.99.after_ref), channel_id=1, source_target_pairs={{0,1},{2,0},{4,2},{6,4},{7,6},{5,7},{3,5},{1,3},{8,10},{10,12},{12... | collective-permute-start | bytes 2359304 | tf_op jit(solution)/shard_map/ppermute | solution.py:493
  99.2 17.1 %collective-permute-start.16 = (bf16[64,384]{1,0:T(8,128)(2,1)S(1)}, bf16[64,384]{1,0:T(8,128)(2,1)S(1)}, u32[]{:S(2)}, u32[]{:S(2)}) collective-permute-start(bf16[64,384]{1,0:T(8,128)(2,1)S(1)} %shard_map.101.refs_1_.low_ref), channel_id=1, source_target_pairs={{0,1},{1,0},{2,3},{3,2},{4,5},{5,4},{6,7},{7,6},{8,9},{9,8},{10,11... | collective-permute-start | bytes 147464 | tf_op jit(solution)/shard_map/ppermute | solution.py:519
  102.1 27.6 %collective-permute-start.22 = (bf16[768,512]{1,0:T(8,128)(2,1)S(1)}, bf16[768,512]{1,0:T(8,128)(2,1)S(1)}, u32[]{:S(2)}, u32[]{:S(2)}) collective-permute-start(bf16[768,512]{1,0:T(8,128)(2,1)S(1)} %shard_map.102.refs_1_), channel_id=1, source_target_pairs={{0,2},{2,4},{4,6},{6,7},{7,5},{5,3},{3,1},{1,0},{8,9},{10,8},{12,1... | collective-permute-start | bytes 2359304 | tf_op jit(solution)/shard_map/ppermute | solution.py:493
  106.0 25.5 %collective-permute-start.21 = (bf16[768,512]{1,0:T(8,128)(2,1)S(1)}, bf16[768,512]{1,0:T(8,128)(2,1)S(1)}, u32[]{:S(2)}, u32[]{:S(2)}) collective-permute-start(bf16[768,512]{1,0:T(8,128)(2,1)S(1)} %shard_map.103.after_ref), channel_id=1, source_target_pairs={{0,1},{2,0},{4,2},{6,4},{7,6},{5,7},{3,5},{1,3},{8,10},{10,12},{12... | collective-permute-start | bytes 2359304 | tf_op jit(solution)/shard_map/ppermute | solution.py:493
  (13 other events, 89.9 us)

commit v21 on v19

--- a/solution.py
+++ b/solution.py
@@ -475,9 +475,9 @@
     pairs = [[(0, 1, forward), (1, -1, backward)], [(1, 1, forward), (0, -1, backward)]]
     arrived = {}
 
-    def turn(number, last, between=None):
+    def turn(number, last, between=None, which=(0, 1)):
         left = far - (number + 1) // 2
-        for half, sign, moves in pairs[number % 2]:
+        for half, sign, moves in [pairs[number % 2][side] for side in which]:
             last = hop(
                 dests, (sign * left) % size, half, x, output_weight,
                 arrived.get((half, sign), []), last,
@@ -510,28 +510,29 @@
     def over(value, apart):
         return lax.ppermute(value, "tp", [(i, i ^ apart) for i in range(size)])
 
-    number, turns = 2, 2 * far - 1
+    number, turns, ahead = 2, 2 * far - 1, False
     apart = 1
     while apart < size:
         sent = over(((give if apart == 1 else low) * LOW_SCALE).astype(jnp.float16), apart)
         until = turns - 1 if 2 * apart == size else number + 1
         while number < min(until, turns - 1):
-            last = turn(number, last)
-            if number == 4:
+            last = turn(number, last, which=(1,) if number == 4 and ahead else (0, 1))
+            if number == 5:
                 last = collect(index_there, adapter_up_weight, last)
                 got_up = lax.ppermute(last, "inst", SWAP)
-            if number == 5:
-                own, up_pages = own_terms(
-                    dests, local, index, x, output_weight, adapter_up_weight, got_up, last
-                )
-                last = own
             number += 1
         apart *= 2
+        if number == 4 and not ahead and number < turns - 1:
+            last, ahead = turn(number, last, which=(0,)), True
         zero = touch(last)[0, 0]
         sent = sent.astype(jnp.float32) * (1.0 / LOW_SCALE) + zero
         low = last = add(low, sent, jnp.float32 if apart < size else jnp.bfloat16, last)
     other = over(low, 1)
     last = turn(number, last)
+    own, up_pages = own_terms(
+        dests, local, index, x, output_weight, adapter_up_weight, got_up, last
+    )
+    last = own
     own = add_delta(sizes, side, own, up_pages, row_list_position, low, other, last)
     own = join(own, arrived[0, -1][0], arrived[1, 1][0])
     result = finish(live_row_count.reshape(-1), own, arrived[0, 1][0], arrived[1, -1][0])

time: 132 us -> 132 us (level)
  starting transfers between devices: 24.2 us -> 27.4 us
  other arithmetic: 4.86 us -> 3.42 us
  Pallas kernels: 62.8 us -> 61.4 us
    ppermute x12, waiting for transfers between devices: 13.5 us -> 23 us  [turn(): arrived[half, sign] = [lax.ppermute(last, ('inst', 'tp'), moves)]]
    ppermute x4, waiting for transfers between devices: 20 us -> 11.5 us  [over(): return lax.ppermute(value, 'tp', [(i, i ^ apart) for i in range(size)])]
    ppermute x12, starting transfers between devices: 13.2 us -> 16.4 us  [turn(): arrived[half, sign] = [lax.ppermute(last, ('inst', 'tp'), moves)]]
  transfers between devices with their start and end apart: 23 -> 23, of which waited for: 6 -> 9; matrix products, arithmetic and copies ran while one was open for 7% -> 6% of each run, Pallas kernels for 46% -> 45%
where the time goes in v21:
time: 132 us; the launch traced here: 131 us
  Pallas kernels  61.4 us (47%)
  waiting for transfers between devices  34.5 us (26%)
  starting transfers between devices  27.4 us (21%)
  local copies, waits for them, and re-layouts  4.37 us (3%)
  other arithmetic  3.42 us (3%)
    pallas_call x12, Pallas kernels, hop(): pl.pallas_call(functools.partial(hop_kernel, tuple(range(len(received))))...  33.7 us
    ppermute x12, waiting for transfers between devices, turn(): arrived[half, sign] = [lax.ppermute(last, ('inst', 'tp'), moves)]  23 us
    ppermute x12, starting transfers between devices, turn(): arrived[half, sign] = [lax.ppermute(last, ('inst', 'tp'), moves)]  16.4 us
    ppermute x4, waiting for transfers between devices, over(): return lax.ppermute(value, 'tp', [(i, i ^ apart) for i in range(size)])  11.5 us
    pallas_call x2, Pallas kernels, first_pieces(): pl.pallas_call(functools.partial(first_kernel, after is not None), grid_s...  7.85 us
    pallas_call x1, Pallas kernels, own_terms(): pl.pallas_call(own_kernel, grid_spec=pltpu.PrefetchScalarGridSpec(num_sca...  6.4 us
    ppermute x4, starting transfers between devices, over(): return lax.ppermute(value, 'tp', [(i, i ^ apart) for i in range(size)])  5.67 us
    pallas_call x2, Pallas kernels, collect(): pl.pallas_call(functools.partial(collect_kernel, count), grid_spec=pltpu....  5.34 us
  transfers between devices with their start and end apart: 23, of which 9 were waited for; matrix products, arithmetic and copies ran while one was open for 6% of the time, Pallas kernels for 45%

profile of v21, /device:TPU:0, one launch (start us, length us, event | category | flops | bytes accessed | tf_op | source)
XLA Modules:
  0.0 131.5 jit_solution(9498912300070910424)
XLA Ops:
  0.5 4.3 %shard_map.82 = (bf16[768,256]{1,0:T(8,128)(2,1)}, bf16[768,256]{1,0:T(8,128)(2,1)}, f32[8,128]{1,0:T(8,128)S(1)}) custom-call(s32[8]{0:T(128)S(1)} %compare_select_fusion.3.dests, bf16[768,1024]{1,0:T(8,128)(2,1)} %bitcast.10, bf16[1024,8192]{1,0:T(8,128)(2,1)} %w_ref.29), custom_call_target="tpu_custom_call" | custom-call | flops 24159191040 | bytes 3407872 | tf_op jit(solution)/shard_map/pallas_call | solution.py:126
  7.3 3.6 %shard_map.83 = (bf16[768,256]{1,0:T(8,128)(2,1)}, bf16[768,256]{1,0:T(8,128)(2,1)S(1)}, f32[8,128]{1,0:T(8,128)S(1)}) custom-call(s32[8]{0:T(128)S(1)} %compare_select_fusion.3.dests, bf16[768,1024]{1,0:T(8,128)(2,1)S(1)} %bitcast.11, bf16[1024,8192]{1,0:T(8,128)(2,1)} %w_ref.29, f32[8,128]{1,0:T(8,128)S(1)} %get-tuple-element.17.refs_0_), custom_call_target="tpu_custom_call" | custom-call | flops 24159191040 | bytes 3407872 | tf_op jit(solution)/shard_map/pallas_call | solution.py:126
  19.9 2.8 %shard_map.85.refs_2_ = bf16[768,512]{1,0:T(8,128)(2,1)S(1)} custom-call(s32[8]{0:T(128)S(1)} %compare_select_fusion.3.dests, bf16[768,1024]{1,0:T(8,128)(2,1)S(1)} %bitcast.12, bf16[1024,8192]{1,0:T(8,128)(2,1)} %w_ref.29, bf16[24,64,1024]{2,1,0:T(8,128)(2,1)S(1)} %shard_map.84.refs_0_), custom_call_target="tpu_custom_call" | custom-call | flops 24159191040 | bytes 4194304 | tf_op jit(solution)/shard_map/pallas_call | solution.py:81
  24.8 2.8 %shard_map.87.after_ref = bf16[768,512]{1,0:T(8,128)(2,1)S(1)} custom-call(s32[8]{0:T(128)S(1)} %compare_select_fusion.3.dests, bf16[768,1024]{1,0:T(8,128)(2,1)S(1)} %bitcast.13, bf16[1024,8192]{1,0:T(8,128)(2,1)} %w_ref.29, f32[8,128]{1,0:T(8,128)S(1)} %shard_map.86.refs_0_), custom_call_target="tpu_custom_call" | custom-call | flops 24159191040 | bytes 4194304 | tf_op jit(solution)/shard_map/pallas_call | solution.py:81
  27.7 5.1 %shard_map.88 = (f32[64,384]{1,0:T(8,128)S(1)}, f32[64,384]{1,0:T(8,128)S(1)}) custom-call(s32[24]{0:T(128)S(1)} %compare_convert_fusion.local, s32[24]{0:T(128)S(1)} %get-tuple-element.26.index, s32[1]{0:T(128)} %bitcast.1.side, bf16[768,1024]{1,0:T(8,128)(2,1)S(1)} %bitcast.14, s32[3,256]{1,0:T(4,128)S(1)} %copy-done.8, bf16[96,64,1024]{2,1,0:T(8,128)(2,1)} %table_ref.5, ...), custom_call_target="tpu_custom_call" | custom-call | flops 12079595520 | bytes 4718592 | tf_op jit(solution)/shard_map/pallas_call | solution.py:246
  34.8 2.9 %shard_map.89.refs_2_ = bf16[768,512]{1,0:T(8,128)(2,1)S(1)} custom-call(s32[8]{0:T(128)S(1)} %compare_select_fusion.3.dests, bf16[768,1024]{1,0:T(8,128)(2,1)S(1)} %bitcast.15, bf16[1024,8192]{1,0:T(8,128)(2,1)} %w_ref.29, bf16[768,256]{1,0:T(8,128)(2,1)S(1)} %collective-permute-done.1.refs_0_, bf16[768,256]{1,0:T(8,128)(2,1)S(1)} %collective-permute-done.8.refs_1_, ...), custom_call_target="tpu_custom_call" | custom-call | flops 24159191040 | bytes 4194304 | tf_op jit(solution)/shard_map/pallas_call | solution.py:81
  39.4 2.9 %shard_map.90.refs_0_.after_ref = bf16[768,512]{1,0:T(8,128)(2,1)S(1)} custom-call(s32[8]{0:T(128)S(1)} %compare_select_fusion.3.dests, bf16[768,1024]{1,0:T(8,128)(2,1)S(1)} %bitcast.16, bf16[1024,8192]{1,0:T(8,128)(2,1)} %w_ref.29, bf16[768,256]{1,0:T(8,128)(2,1)S(1)} %collective-permute-done.2.refs_1_.refs_0_, ...), custom_call_target="tpu_custom_call" | custom-call | flops 24159191040 | bytes 4194304 | tf_op jit(solution)/shard_map/pallas_call | solution.py:81
  43.4 3.4 %collective-permute-done.6 = f16[64,384]{1,0:T(8,128)(2,1)S(1)} collective-permute-done((f16[64,384]{1,0:T(8,128)(2,1)S(1)}, f16[64,384]{1,0:T(8,128)(2,1)S(1)}, u32[]{:S(2)}, u32[]{:S(2)}) %collective-permute-start.6) | collective-permute-done | bytes 49184 | tf_op jit(solution)/shard_map/ppermute | solution.py:511
  47.5 2.8 %shard_map.93.refs_1_ = bf16[768,512]{1,0:T(8,128)(2,1)S(1)} custom-call(s32[8]{0:T(128)S(1)} %compare_select_fusion.3.dests, bf16[768,1024]{1,0:T(8,128)(2,1)S(1)} %bitcast.17, bf16[1024,8192]{1,0:T(8,128)(2,1)} %w_ref.29, bf16[768,512]{1,0:T(8,128)(2,1)S(1)} %collective-permute-done.4.refs_0_, f32[64,384]{1,0:T(8,128)S(1)} %shard_map.92.refs_1_.low_ref), custom_call_target="tpu_custom_call" | custom-call | flops 24159191040 | bytes 4194304 | tf_op jit(solution)/shard_map/pallas_call | solution.py:81
  52.4 2.8 %shard_map.94.refs_1_ = bf16[768,512]{1,0:T(8,128)(2,1)S(1)} custom-call(s32[8]{0:T(128)S(1)} %compare_select_fusion.3.dests, bf16[768,1024]{1,0:T(8,128)(2,1)S(1)} %bitcast.18, bf16[1024,8192]{1,0:T(8,128)(2,1)} %w_ref.29, bf16[768,512]{1,0:T(8,128)(2,1)S(1)} %collective-permute-done.3.refs_0_, bf16[768,512]{1,0:T(8,128)(2,1)S(1)} %shard_map.93.refs_1_), custom_call_target="tpu_custom_call" | custom-call | flops 24159191040 | bytes 4194304 | tf_op jit(solution)/shard_map/pallas_call | solution.py:81
  58.3 2.8 %shard_map.95.refs_0_.after_ref = bf16[768,512]{1,0:T(8,128)(2,1)S(1)} custom-call(s32[8]{0:T(128)S(1)} %compare_select_fusion.3.dests, bf16[768,1024]{1,0:T(8,128)(2,1)S(1)} %bitcast.19, bf16[1024,8192]{1,0:T(8,128)(2,1)} %w_ref.29, bf16[768,512]{1,0:T(8,128)(2,1)S(1)} %collective-permute-done.13.refs_0_, bf16[768,512]{1,0:T(8,128)(2,1)S(1)} %shard_map.94.refs_1_), custom_call_target="tpu_custom_call" | custom-call | flops 24159191040 | bytes 4194304 | tf_op jit(solution)/shard_map/pallas_call | solution.py:81
  67.3 2.8 %shard_map.98.refs_1_ = bf16[768,512]{1,0:T(8,128)(2,1)S(1)} custom-call(s32[8]{0:T(128)S(1)} %compare_select_fusion.3.dests, bf16[768,1024]{1,0:T(8,128)(2,1)S(1)} %bitcast.20, bf16[1024,8192]{1,0:T(8,128)(2,1)} %w_ref.29, bf16[768,512]{1,0:T(8,128)(2,1)S(1)} %collective-permute-done.11.refs_0_, f32[64,384]{1,0:T(8,128)S(1)} %shard_map.97.refs_1_.low_ref), custom_call_target="tpu_custom_call" | custom-call | flops 24159191040 | bytes 4194304 | tf_op jit(solution)/shard_map/pallas_call | solution.py:81
  71.3 4.0 %collective-permute-done.10.refs_0_ = bf16[768,512]{1,0:T(8,128)(2,1)S(1)} collective-permute-done((bf16[768,512]{1,0:T(8,128)(2,1)S(1)}, bf16[768,512]{1,0:T(8,128)(2,1)S(1)}, u32[]{:S(2)}, u32[]{:S(2)}) %collective-permute-start.10) | collective-permute-done | bytes 786464 | tf_op jit(solution)/shard_map/ppermute | solution.py:485
  75.3 2.8 %shard_map.99.refs_1_ = bf16[768,512]{1,0:T(8,128)(2,1)S(1)} custom-call(s32[8]{0:T(128)S(1)} %compare_select_fusion.3.dests, bf16[768,1024]{1,0:T(8,128)(2,1)S(1)} %bitcast.21, bf16[1024,8192]{1,0:T(8,128)(2,1)} %w_ref.29, bf16[768,512]{1,0:T(8,128)(2,1)S(1)} %collective-permute-done.10.refs_0_, bf16[768,512]{1,0:T(8,128)(2,1)S(1)} %shard_map.98.refs_1_), custom_call_target="tpu_custom_call" | custom-call | flops 24159191040 | bytes 4194304 | tf_op jit(solution)/shard_map/pallas_call | solution.py:81
  78.1 2.7 %collective-permute-done.9.refs_0_ = bf16[768,512]{1,0:T(8,128)(2,1)S(1)} collective-permute-done((bf16[768,512]{1,0:T(8,128)(2,1)S(1)}, bf16[768,512]{1,0:T(8,128)(2,1)S(1)}, u32[]{:S(2)}, u32[]{:S(2)}) %collective-permute-start.9) | collective-permute-done | bytes 786464 | tf_op jit(solution)/shard_map/ppermute | solution.py:485
  80.8 2.8 %shard_map.100.after_ref = bf16[768,512]{1,0:T(8,128)(2,1)S(1)} custom-call(s32[8]{0:T(128)S(1)} %compare_select_fusion.3.dests, bf16[768,1024]{1,0:T(8,128)(2,1)S(1)} %bitcast.22, bf16[1024,8192]{1,0:T(8,128)(2,1)} %w_ref.29, bf16[768,512]{1,0:T(8,128)(2,1)S(1)} %collective-permute-done.9.refs_0_, bf16[768,512]{1,0:T(8,128)(2,1)S(1)} %shard_map.99.refs_1_), custom_call_target="tpu_custom_call" | custom-call | flops 24159191040 | bytes 4194304 | tf_op jit(solution)/shard_map/pallas_call | solution.py:81
  83.6 2.7 %shard_map.101.refs_0_.after_ref = bf16[24,64,1024]{2,1,0:T(8,128)(2,1)S(1)} custom-call(s32[24]{0:T(128)S(1)} %copy-done.3, bf16[96,64,1024]{2,1,0:T(8,128)(2,1)} %table_ref.7, bf16[768,512]{1,0:T(8,128)(2,1)S(1)} %shard_map.100.after_ref), custom_call_target="tpu_custom_call" | custom-call | bytes 6291456 | tf_op jit(solution)/shard_map/pallas_call | solution.py:175
  86.5 3.4 %collective-permute-start.19 = (bf16[768,512]{1,0:T(8,128)(2,1)S(1)}, bf16[768,512]{1,0:T(8,128)(2,1)S(1)}, u32[]{:S(2)}, u32[]{:S(2)}) collective-permute-start(bf16[768,512]{1,0:T(8,128)(2,1)S(1)} %shard_map.100.after_ref), channel_id=1, source_target_pairs={{0,1},{2,0},{4,2},{6,4},{7,6},{5,7},{3,5},{1,3},{8,10},{10,12},{12... | collective-permute-start | bytes 2359304 | tf_op jit(solution)/shard_map/ppermute | solution.py:485
  90.3 2.8 %collective-permute-done.17 = f16[64,384]{1,0:T(8,128)(2,1)S(1)} collective-permute-done((f16[64,384]{1,0:T(8,128)(2,1)S(1)}, f16[64,384]{1,0:T(8,128)(2,1)S(1)}, u32[]{:S(2)}, u32[]{:S(2)}) %collective-permute-start.17) | collective-permute-done | bytes 49184 | tf_op jit(solution)/shard_map/ppermute | solution.py:511
  96.0 2.8 %shard_map.104.refs_1_ = bf16[768,512]{1,0:T(8,128)(2,1)S(1)} custom-call(s32[8]{0:T(128)S(1)} %compare_select_fusion.3.dests, bf16[768,1024]{1,0:T(8,128)(2,1)S(1)} %bitcast.23, bf16[1024,8192]{1,0:T(8,128)(2,1)} %w_ref.29, bf16[768,512]{1,0:T(8,128)(2,1)S(1)} %collective-permute-done.16.refs_0_, bf16[64,384]{1,0:T(8,128)(2,1)S(1)} %shard_map.103.refs_1_.low_ref), custom_call_target="tpu_custom_call" | custom-call | flops 24159191040 | bytes 4194304 | tf_op jit(solution)/shard_map/pallas_call | solution.py:81
  100.8 2.8 %shard_map.105.after_ref = bf16[768,512]{1,0:T(8,128)(2,1)S(1)} custom-call(s32[8]{0:T(128)S(1)} %compare_select_fusion.3.dests, bf16[768,1024]{1,0:T(8,128)(2,1)S(1)} %bitcast.24, bf16[1024,8192]{1,0:T(8,128)(2,1)} %w_ref.29, bf16[768,512]{1,0:T(8,128)(2,1)S(1)} %collective-permute-done.15.refs_0_, bf16[768,512]{1,0:T(8,128)(2,1)S(1)} %shard_map.104.refs_1_), custom_call_target="tpu_custom_call" | custom-call | flops 24159191040 | bytes 4194304 | tf_op jit(solution)/shard_map/pallas_call | solution.py:81
  103.7 6.4 %shard_map.106 = (f32[768,1024]{1,0:T(8,128)S(1)}, bf16[24,64,1024]{2,1,0:T(8,128)(2,1)S(1)}) custom-call(s32[24]{0:T(128)S(1)} %compare_convert_fusion.local, s32[24]{0:T(128)S(1)} %copy-done.6, s32[8]{0:T(128)S(1)} %compare_select_fusion.3.dests, bf16[768,1024]{1,0:T(8,128)(2,1)S(1)} %bitcast.25, bf16[1024,8192]{1,0:T(8,128)(2,1)} %w_ref.29, ...), custom_call_target="tpu_custom_call" | custom-call | flops 48318382080 | bytes 13107200 | tf_op jit(solution)/shard_map/pallas_call | solution.py:305
  110.1 4.6 %collective-permute-done.18.other_ref = bf16[64,384]{1,0:T(8,128)(2,1)S(1)} collective-permute-done((bf16[64,384]{1,0:T(8,128)(2,1)S(1)}, bf16[64,384]{1,0:T(8,128)(2,1)S(1)}, u32[]{:S(2)}, u32[]{:S(2)}) %collective-permute-start.18) | collective-permute-done | bytes 49184 | tf_op jit(solution)/shard_map/ppermute | solution.py:511
  115.9 12.8 %collective-permute-done.22.right_ref = bf16[768,512]{1,0:T(8,128)(2,1)S(1)} collective-permute-done((bf16[768,512]{1,0:T(8,128)(2,1)S(1)}, bf16[768,512]{1,0:T(8,128)(2,1)S(1)}, u32[]{:S(2)}, u32[]{:S(2)}) %collective-permute-start.22) | collective-permute-done | bytes 786464 | tf_op jit(solution)/shard_map/ppermute | solution.py:485
  (92 shorter events, 41.7 us)
Async XLA Ops:
  0.0 15.0 %copy-start = (s32[192]{0:T(256)S(1)}, s32[192]{0:T(256)}, u32[]{:S(2)}) copy-start(s32[192]{0:T(256)} %param.12) | copy-start | bytes 2308
  0.0 13.6 %collective-permute-start = (s32[3,2,4]{2,1,0:T(2,128)}, s32[3,2,4]{2,1,0:T(2,128)}, u32[]{:S(2)}, u32[]{:S(2)}) collective-permute-start(s32[3,2,4]{2,1,0:T(2,128)} %param.13), channel_id=1, source_target_pairs={{0,8},{8,0},{1,9},{9,1},{2,10},{10,2},{3,11},{11,3},{4,12},{12,4},... | collective-permute-start | bytes 296 | tf_op jit(solution)/shard_map/ppermute | solution.py:491
  4.8 18.0 %collective-permute-start.1 = (bf16[768,256]{1,0:T(8,128)(2,1)}, bf16[768,256]{1,0:T(8,128)(2,1)S(1)}, u32[]{:S(2)}, u32[]{:S(2)}) collective-permute-start(bf16[768,256]{1,0:T(8,128)(2,1)} %get-tuple-element.15), channel_id=1, source_target_pairs={{0,2},{2,4},{4,6},{6,7},{7,5},{5,3},{3,1},{1,0},{8,9},{10,8},{12,1... | collective-permute-start | bytes 1179656 | tf_op jit(solution)/shard_map/ppermute | solution.py:496
  7.3 17.5 %collective-permute-start.2 = (bf16[768,256]{1,0:T(8,128)(2,1)}, bf16[768,256]{1,0:T(8,128)(2,1)S(1)}, u32[]{:S(2)}, u32[]{:S(2)}) collective-permute-start(bf16[768,256]{1,0:T(8,128)(2,1)} %get-tuple-element.16), channel_id=1, source_target_pairs={{0,1},{2,0},{4,2},{6,4},{7,6},{5,7},{3,5},{1,3},{8,10},{10,12},{12... | collective-permute-start | bytes 1179656 | tf_op jit(solution)/shard_map/ppermute | solution.py:496
  10.9 23.9 %collective-permute-start.8 = (bf16[768,256]{1,0:T(8,128)(2,1)}, bf16[768,256]{1,0:T(8,128)(2,1)S(1)}, u32[]{:S(2)}, u32[]{:S(2)}) collective-permute-start(bf16[768,256]{1,0:T(8,128)(2,1)} %get-tuple-element.22), channel_id=1, source_target_pairs={{0,2},{2,4},{4,6},{6,7},{7,5},{5,3},{3,1},{1,0},{8,9},{10,8},{12,1... | collective-permute-start | bytes 1179656 | tf_op jit(solution)/shard_map/ppermute | solution.py:496
  13.0 26.4 %collective-permute-start.7 = (bf16[768,256]{1,0:T(8,128)(2,1)S(1)}, bf16[768,256]{1,0:T(8,128)(2,1)S(1)}, u32[]{:S(2)}, u32[]{:S(2)}) collective-permute-start(bf16[768,256]{1,0:T(8,128)(2,1)S(1)} %get-tuple-element.21), channel_id=1, source_target_pairs={{0,1},{2,0},{4,2},{6,4},{7,6},{5,7},{3,5},{1,3},{8,10},{10,12},{12... | collective-permute-start | bytes 1179656 | tf_op jit(solution)/shard_map/ppermute | solution.py:496
  19.8 7.8 %collective-permute-start.5 = (bf16[24,64,1024]{2,1,0:T(8,128)(2,1)S(1)}, bf16[24,64,1024]{2,1,0:T(8,128)(2,1)S(1)}, u32[]{:S(2)}, u32[]{:S(2)}) collective-permute-start(bf16[24,64,1024]{2,1,0:T(8,128)(2,1)S(1)} %shard_map.84.refs_0_), channel_id=1, source_target_pairs={{0,8},{8,0},{1,9},{9,1},{2,10},{10,2},{3,11},{11,3},{4,12},{12,4},... | collective-permute-start | bytes 9437192 | tf_op jit(solution)/shard_map/ppermute | solution.py:502
  22.7 24.8 %collective-permute-start.4 = (bf16[768,512]{1,0:T(8,128)(2,1)S(1)}, bf16[768,512]{1,0:T(8,128)(2,1)S(1)}, u32[]{:S(2)}, u32[]{:S(2)}) collective-permute-start(bf16[768,512]{1,0:T(8,128)(2,1)S(1)} %shard_map.85.refs_2_), channel_id=1, source_target_pairs={{0,2},{2,4},{4,6},{6,7},{7,5},{5,3},{3,1},{1,0},{8,9},{10,8},{12,1... | collective-permute-start | bytes 2359304 | tf_op jit(solution)/shard_map/ppermute | solution.py:485
  27.6 24.8 %collective-permute-start.3 = (bf16[768,512]{1,0:T(8,128)(2,1)S(1)}, bf16[768,512]{1,0:T(8,128)(2,1)S(1)}, u32[]{:S(2)}, u32[]{:S(2)}) collective-permute-start(bf16[768,512]{1,0:T(8,128)(2,1)S(1)} %shard_map.87.after_ref), channel_id=1, source_target_pairs={{0,1},{2,0},{4,2},{6,4},{7,6},{5,7},{3,5},{1,3},{8,10},{10,12},{12... | collective-permute-start | bytes 2359304 | tf_op jit(solution)/shard_map/ppermute | solution.py:485
  32.8 13.9 %collective-permute-start.6 = (f16[64,384]{1,0:T(8,128)(2,1)S(1)}, f16[64,384]{1,0:T(8,128)(2,1)S(1)}, u32[]{:S(2)}, u32[]{:S(2)}) collective-permute-start(f16[64,384]{1,0:T(8,128)(2,1)S(1)} %multiply_convert_fusion.2), channel_id=1, source_target_pairs={{0,1},{1,0},{2,3},{3,2},{4,5},{5,4},{6,7},{7,6},{8,9},{9,8},{10,11... | collective-permute-start | bytes 147464 | tf_op jit(solution)/shard_map/ppermute | solution.py:511
  37.7 20.5 %collective-permute-start.13 = (bf16[768,512]{1,0:T(8,128)(2,1)S(1)}, bf16[768,512]{1,0:T(8,128)(2,1)S(1)}, u32[]{:S(2)}, u32[]{:S(2)}) collective-permute-start(bf16[768,512]{1,0:T(8,128)(2,1)S(1)} %shard_map.89.refs_2_), channel_id=1, source_target_pairs={{0,2},{2,4},{4,6},{6,7},{7,5},{5,3},{3,1},{1,0},{8,9},{10,8},{12,1... | collective-permute-start | bytes 2359304 | tf_op jit(solution)/shard_map/ppermute | solution.py:485
  42.3 24.9 %collective-permute-start.11 = (bf16[768,512]{1,0:T(8,128)(2,1)S(1)}, bf16[768,512]{1,0:T(8,128)(2,1)S(1)}, u32[]{:S(2)}, u32[]{:S(2)}) collective-permute-start(bf16[768,512]{1,0:T(8,128)(2,1)S(1)} %shard_map.90.refs_0_.after_ref), channel_id=1, source_target_pairs={{0,1},{2,0},{4,2},{6,4},{7,6},{5,7},{3,5},{1,3},{8,10},{10,12},{12... | collective-permute-start | bytes 2359304 | tf_op jit(solution)/shard_map/ppermute | solution.py:485
  47.4 16.5 %collective-permute-start.12 = (f16[64,384]{1,0:T(8,128)(2,1)S(1)}, f16[64,384]{1,0:T(8,128)(2,1)S(1)}, u32[]{:S(2)}, u32[]{:S(2)}) collective-permute-start(f16[64,384]{1,0:T(8,128)(2,1)S(1)} %multiply_convert_fusion.1), channel_id=1, source_target_pairs={{0,2},{1,3},{2,0},{3,1},{4,6},{5,7},{6,4},{7,5},{8,10},{9,11},{10,... | collective-permute-start | bytes 147464 | tf_op jit(solution)/shard_map/ppermute | solution.py:511
  50.3 25.0 %collective-permute-start.10 = (bf16[768,512]{1,0:T(8,128)(2,1)S(1)}, bf16[768,512]{1,0:T(8,128)(2,1)S(1)}, u32[]{:S(2)}, u32[]{:S(2)}) collective-permute-start(bf16[768,512]{1,0:T(8,128)(2,1)S(1)} %shard_map.93.refs_1_), channel_id=1, source_target_pairs={{0,2},{2,4},{4,6},{6,7},{7,5},{5,3},{3,1},{1,0},{8,9},{10,8},{12,1... | collective-permute-start | bytes 2359304 | tf_op jit(solution)/shard_map/ppermute | solution.py:485
  55.1 25.7 %collective-permute-start.9 = (bf16[768,512]{1,0:T(8,128)(2,1)S(1)}, bf16[768,512]{1,0:T(8,128)(2,1)S(1)}, u32[]{:S(2)}, u32[]{:S(2)}) collective-permute-start(bf16[768,512]{1,0:T(8,128)(2,1)S(1)} %shard_map.94.refs_1_), channel_id=1, source_target_pairs={{0,1},{2,0},{4,2},{6,4},{7,6},{5,7},{3,5},{1,3},{8,10},{10,12},{12... | collective-permute-start | bytes 2359304 | tf_op jit(solution)/shard_map/ppermute | solution.py:485
  61.1 34.0 %collective-permute-start.16 = (bf16[768,512]{1,0:T(8,128)(2,1)S(1)}, bf16[768,512]{1,0:T(8,128)(2,1)S(1)}, u32[]{:S(2)}, u32[]{:S(2)}) collective-permute-start(bf16[768,512]{1,0:T(8,128)(2,1)S(1)} %shard_map.95.refs_0_.after_ref), channel_id=1, source_target_pairs={{0,2},{2,4},{4,6},{6,7},{7,5},{5,3},{3,1},{1,0},{8,9},{10,8},{12,1... | collective-permute-start | bytes 2359304 | tf_op jit(solution)/shard_map/ppermute | solution.py:485
  64.6 28.6 %collective-permute-start.17 = (f16[64,384]{1,0:T(8,128)(2,1)S(1)}, f16[64,384]{1,0:T(8,128)(2,1)S(1)}, u32[]{:S(2)}, u32[]{:S(2)}) collective-permute-start(f16[64,384]{1,0:T(8,128)(2,1)S(1)} %multiply_convert_fusion), channel_id=1, source_target_pairs={{0,4},{1,5},{2,6},{3,7},{4,0},{5,1},{6,2},{7,3},{8,12},{9,13},{10,... | collective-permute-start | bytes 147464 | tf_op jit(solution)/shard_map/ppermute | solution.py:511
  70.1 28.7 %collective-permute-start.15 = (bf16[768,512]{1,0:T(8,128)(2,1)S(1)}, bf16[768,512]{1,0:T(8,128)(2,1)S(1)}, u32[]{:S(2)}, u32[]{:S(2)}) collective-permute-start(bf16[768,512]{1,0:T(8,128)(2,1)S(1)} %shard_map.98.refs_1_), channel_id=1, source_target_pairs={{0,1},{2,0},{4,2},{6,4},{7,6},{5,7},{3,5},{1,3},{8,10},{10,12},{12... | collective-permute-start | bytes 2359304 | tf_op jit(solution)/shard_map/ppermute | solution.py:485
  86.3 17.3 %collective-permute-start.14 = (bf16[24,64,1024]{2,1,0:T(8,128)(2,1)S(1)}, bf16[24,64,1024]{2,1,0:T(8,128)(2,1)S(1)}, u32[]{:S(2)}, u32[]{:S(2)}) collective-permute-start(bf16[24,64,1024]{2,1,0:T(8,128)(2,1)S(1)} %shard_map.101.refs_0_.after_ref), channel_id=1, source_target_pairs={{0,8},{8,0},{1,9},{9,1},{2,10},{10,2},{3,11},{11,3},{4,12},{12,4},... | collective-permute-start | bytes 9437192 | tf_op jit(solution)/shard_map/ppermute | solution.py:522
  86.5 29.0 %collective-permute-start.19 = (bf16[768,512]{1,0:T(8,128)(2,1)S(1)}, bf16[768,512]{1,0:T(8,128)(2,1)S(1)}, u32[]{:S(2)}, u32[]{:S(2)}) collective-permute-start(bf16[768,512]{1,0:T(8,128)(2,1)S(1)} %shard_map.100.after_ref), channel_id=1, source_target_pairs={{0,1},{2,0},{4,2},{6,4},{7,6},{5,7},{3,5},{1,3},{8,10},{10,12},{12... | collective-permute-start | bytes 2359304 | tf_op jit(solution)/shard_map/ppermute | solution.py:485
  93.2 22.3 %collective-permute-start.20 = (bf16[768,512]{1,0:T(8,128)(2,1)S(1)}, bf16[768,512]{1,0:T(8,128)(2,1)S(1)}, u32[]{:S(2)}, u32[]{:S(2)}) collective-permute-start(bf16[768,512]{1,0:T(8,128)(2,1)S(1)} %shard_map.99.refs_1_), channel_id=1, source_target_pairs={{0,2},{2,4},{4,6},{6,7},{7,5},{5,3},{3,1},{1,0},{8,9},{10,8},{12,1... | collective-permute-start | bytes 2359304 | tf_op jit(solution)/shard_map/ppermute | solution.py:485
  95.1 19.7 %collective-permute-start.18 = (bf16[64,384]{1,0:T(8,128)(2,1)S(1)}, bf16[64,384]{1,0:T(8,128)(2,1)S(1)}, u32[]{:S(2)}, u32[]{:S(2)}) collective-permute-start(bf16[64,384]{1,0:T(8,128)(2,1)S(1)} %shard_map.103.refs_1_.low_ref), channel_id=1, source_target_pairs={{0,1},{1,0},{2,3},{3,2},{4,5},{5,4},{6,7},{7,6},{8,9},{9,8},{10,11... | collective-permute-start | bytes 147464 | tf_op jit(solution)/shard_map/ppermute | solution.py:511
  98.8 30.8 %collective-permute-start.21 = (bf16[768,512]{1,0:T(8,128)(2,1)S(1)}, bf16[768,512]{1,0:T(8,128)(2,1)S(1)}, u32[]{:S(2)}, u32[]{:S(2)}) collective-permute-start(bf16[768,512]{1,0:T(8,128)(2,1)S(1)} %shard_map.104.refs_1_), channel_id=1, source_target_pairs={{0,2},{2,4},{4,6},{6,7},{7,5},{5,3},{3,1},{1,0},{8,9},{10,8},{12,1... | collective-permute-start | bytes 2359304 | tf_op jit(solution)/shard_map/ppermute | solution.py:485
  103.6 25.1 %collective-permute-start.22 = (bf16[768,512]{1,0:T(8,128)(2,1)S(1)}, bf16[768,512]{1,0:T(8,128)(2,1)S(1)}, u32[]{:S(2)}, u32[]{:S(2)}) collective-permute-start(bf16[768,512]{1,0:T(8,128)(2,1)S(1)} %shard_map.105.after_ref), channel_id=1, source_target_pairs={{0,1},{2,0},{4,2},{6,4},{7,6},{5,7},{3,5},{1,3},{8,10},{10,12},{12... | collective-permute-start | bytes 2359304 | tf_op jit(solution)/shard_map/ppermute | solution.py:485
  (11 other events, 69.1 us)

commit v22 on v21

--- a/solution.py
+++ b/solution.py
@@ -431,7 +431,7 @@
             out_specs=ANYWHERE,
             scratch_shapes=[
                 pltpu.VMEM((rows, cols), jnp.bfloat16),
-                pltpu.SemaphoreType.DMA((4 * live.shape[0],)),
+                pltpu.SemaphoreType.DMA((2 * live.shape[0],)),
             ],
         ),
         out_shape=jax.ShapeDtypeStruct((rows, cols), jnp.bfloat16),

time: 132 us -> 132 us (level)
  starting transfers between devices: 27.4 us -> 23.6 us
  Pallas kernels: 61.4 us -> 64 us
    ppermute x12, starting transfers between devices: 16.4 us -> 12.7 us  [turn(): arrived[half, sign] = [lax.ppermute(last, ('inst', 'tp'), moves)]]
    pallas_call x1, Pallas kernels: 6.4 us -> 7.75 us  [own_terms(): pl.pallas_call(own_kernel, grid_spec=pltpu.PrefetchScalarGridSpec(num_sca...]
    pallas_call x1, Pallas kernels: 5.06 us -> 6.39 us  [low_rank(): pl.pallas_call(functools.partial(low_kernel, sizes), grid_spec=pltpu.Pref...]
  transfers between devices with their start and end apart: 23 -> 23, of which waited for: 9 -> 9; matrix products, arithmetic and copies ran while one was open for 6% -> 6% of each run, Pallas kernels for 45% -> 47%
where the time goes in v22:
time: 132 us; the launch traced here: 131 us
  Pallas kernels  64 us (48%)
  waiting for transfers between devices  35.6 us (27%)
  starting transfers between devices  23.6 us (18%)
  local copies, waits for them, and re-layouts  4.37 us (3%)
  other arithmetic  3.42 us (3%)
    pallas_call x12, Pallas kernels, hop(): pl.pallas_call(functools.partial(hop_kernel, tuple(range(len(received))))...  33.7 us
    ppermute x12, waiting for transfers between devices, turn(): arrived[half, sign] = [lax.ppermute(last, ('inst', 'tp'), moves)]  24.2 us
    ppermute x12, starting transfers between devices, turn(): arrived[half, sign] = [lax.ppermute(last, ('inst', 'tp'), moves)]  12.7 us
    ppermute x4, waiting for transfers between devices, over(): return lax.ppermute(value, 'tp', [(i, i ^ apart) for i in range(size)])  11.5 us
    pallas_call x2, Pallas kernels, first_pieces(): pl.pallas_call(functools.partial(first_kernel, after is not None), grid_s...  7.85 us
    pallas_call x1, Pallas kernels, own_terms(): pl.pallas_call(own_kernel, grid_spec=pltpu.PrefetchScalarGridSpec(num_sca...  7.75 us
    pallas_call x1, Pallas kernels, low_rank(): pl.pallas_call(functools.partial(low_kernel, sizes), grid_spec=pltpu.Pref...  6.39 us
    ppermute x4, starting transfers between devices, over(): return lax.ppermute(value, 'tp', [(i, i ^ apart) for i in range(size)])  5.66 us
  transfers between devices with their start and end apart: 23, of which 9 were waited for; matrix products, arithmetic and copies ran while one was open for 6% of the time, Pallas kernels for 47%

profile of v22, /device:TPU:0, one launch (start us, length us, event | category | flops | bytes accessed | tf_op | source)
XLA Modules:
  0.0 131.4 jit_solution(1266570739828574335)
XLA Ops:
  0.5 4.3 %shard_map.82 = (bf16[768,256]{1,0:T(8,128)(2,1)}, bf16[768,256]{1,0:T(8,128)(2,1)}, f32[8,128]{1,0:T(8,128)S(1)}) custom-call(s32[8]{0:T(128)S(1)} %compare_select_fusion.3.dests, bf16[768,1024]{1,0:T(8,128)(2,1)} %bitcast.10, bf16[1024,8192]{1,0:T(8,128)(2,1)} %w_ref.29), custom_call_target="tpu_custom_call" | custom-call | flops 24159191040 | bytes 3407872 | tf_op jit(solution)/shard_map/pallas_call | solution.py:126
  7.3 3.6 %shard_map.83 = (bf16[768,256]{1,0:T(8,128)(2,1)}, bf16[768,256]{1,0:T(8,128)(2,1)S(1)}, f32[8,128]{1,0:T(8,128)S(1)}) custom-call(s32[8]{0:T(128)S(1)} %compare_select_fusion.3.dests, bf16[768,1024]{1,0:T(8,128)(2,1)S(1)} %bitcast.11, bf16[1024,8192]{1,0:T(8,128)(2,1)} %w_ref.29, f32[8,128]{1,0:T(8,128)S(1)} %get-tuple-element.17.refs_0_), custom_call_target="tpu_custom_call" | custom-call | flops 24159191040 | bytes 3407872 | tf_op jit(solution)/shard_map/pallas_call | solution.py:126
  17.1 2.7 %shard_map.84.refs_0_ = bf16[24,64,1024]{2,1,0:T(8,128)(2,1)S(1)} custom-call(s32[24]{0:T(128)S(1)} %get-tuple-element.25.index, bf16[96,64,1024]{2,1,0:T(8,128)(2,1)} %table_ref.5, f32[8,128]{1,0:T(8,128)S(1)} %get-tuple-element.18.after_ref), custom_call_target="tpu_custom_call" | custom-call | bytes 6291456 | tf_op jit(solution)/shard_map/pallas_call | solution.py:175
  19.9 2.8 %shard_map.85.refs_2_ = bf16[768,512]{1,0:T(8,128)(2,1)S(1)} custom-call(s32[8]{0:T(128)S(1)} %compare_select_fusion.3.dests, bf16[768,1024]{1,0:T(8,128)(2,1)S(1)} %bitcast.12, bf16[1024,8192]{1,0:T(8,128)(2,1)} %w_ref.29, bf16[24,64,1024]{2,1,0:T(8,128)(2,1)S(1)} %shard_map.84.refs_0_), custom_call_target="tpu_custom_call" | custom-call | flops 24159191040 | bytes 4194304 | tf_op jit(solution)/shard_map/pallas_call | solution.py:81
  24.8 2.8 %shard_map.87.after_ref = bf16[768,512]{1,0:T(8,128)(2,1)S(1)} custom-call(s32[8]{0:T(128)S(1)} %compare_select_fusion.3.dests, bf16[768,1024]{1,0:T(8,128)(2,1)S(1)} %bitcast.13, bf16[1024,8192]{1,0:T(8,128)(2,1)} %w_ref.29, f32[8,128]{1,0:T(8,128)S(1)} %shard_map.86.refs_0_), custom_call_target="tpu_custom_call" | custom-call | flops 24159191040 | bytes 4194304 | tf_op jit(solution)/shard_map/pallas_call | solution.py:81
  27.7 6.4 %shard_map.88 = (f32[64,384]{1,0:T(8,128)S(1)}, f32[64,384]{1,0:T(8,128)S(1)}) custom-call(s32[24]{0:T(128)S(1)} %compare_convert_fusion.local, s32[24]{0:T(128)S(1)} %get-tuple-element.26.index, s32[1]{0:T(128)} %bitcast.1.side, bf16[768,1024]{1,0:T(8,128)(2,1)S(1)} %bitcast.14, s32[3,256]{1,0:T(4,128)S(1)} %copy-done.8, bf16[96,64,1024]{2,1,0:T(8,128)(2,1)} %table_ref.5, ...), custom_call_target="tpu_custom_call" | custom-call | flops 12079595520 | bytes 4718592 | tf_op jit(solution)/shard_map/pallas_call | solution.py:246
  36.1 2.9 %shard_map.89.refs_2_ = bf16[768,512]{1,0:T(8,128)(2,1)S(1)} custom-call(s32[8]{0:T(128)S(1)} %compare_select_fusion.3.dests, bf16[768,1024]{1,0:T(8,128)(2,1)S(1)} %bitcast.15, bf16[1024,8192]{1,0:T(8,128)(2,1)} %w_ref.29, bf16[768,256]{1,0:T(8,128)(2,1)S(1)} %collective-permute-done.1.refs_0_, bf16[768,256]{1,0:T(8,128)(2,1)S(1)} %collective-permute-done.8.refs_1_, ...), custom_call_target="tpu_custom_call" | custom-call | flops 24159191040 | bytes 4194304 | tf_op jit(solution)/shard_map/pallas_call | solution.py:81
  40.7 2.9 %shard_map.90.refs_0_.after_ref = bf16[768,512]{1,0:T(8,128)(2,1)S(1)} custom-call(s32[8]{0:T(128)S(1)} %compare_select_fusion.3.dests, bf16[768,1024]{1,0:T(8,128)(2,1)S(1)} %bitcast.16, bf16[1024,8192]{1,0:T(8,128)(2,1)} %w_ref.29, bf16[768,256]{1,0:T(8,128)(2,1)S(1)} %collective-permute-done.2.refs_1_.refs_0_, ...), custom_call_target="tpu_custom_call" | custom-call | flops 24159191040 | bytes 4194304 | tf_op jit(solution)/shard_map/pallas_call | solution.py:81
  47.5 2.8 %shard_map.93.refs_1_ = bf16[768,512]{1,0:T(8,128)(2,1)S(1)} custom-call(s32[8]{0:T(128)S(1)} %compare_select_fusion.3.dests, bf16[768,1024]{1,0:T(8,128)(2,1)S(1)} %bitcast.17, bf16[1024,8192]{1,0:T(8,128)(2,1)} %w_ref.29, bf16[768,512]{1,0:T(8,128)(2,1)S(1)} %collective-permute-done.4.refs_0_, f32[64,384]{1,0:T(8,128)S(1)} %shard_map.92.refs_1_.low_ref), custom_call_target="tpu_custom_call" | custom-call | flops 24159191040 | bytes 4194304 | tf_op jit(solution)/shard_map/pallas_call | solution.py:81
  52.4 2.8 %shard_map.94.refs_1_ = bf16[768,512]{1,0:T(8,128)(2,1)S(1)} custom-call(s32[8]{0:T(128)S(1)} %compare_select_fusion.3.dests, bf16[768,1024]{1,0:T(8,128)(2,1)S(1)} %bitcast.18, bf16[1024,8192]{1,0:T(8,128)(2,1)} %w_ref.29, bf16[768,512]{1,0:T(8,128)(2,1)S(1)} %collective-permute-done.3.refs_0_, bf16[768,512]{1,0:T(8,128)(2,1)S(1)} %shard_map.93.refs_1_), custom_call_target="tpu_custom_call" | custom-call | flops 24159191040 | bytes 4194304 | tf_op jit(solution)/shard_map/pallas_call | solution.py:81
  55.7 3.9 %collective-permute-done.13.refs_0_ = bf16[768,512]{1,0:T(8,128)(2,1)S(1)} collective-permute-done((bf16[768,512]{1,0:T(8,128)(2,1)S(1)}, bf16[768,512]{1,0:T(8,128)(2,1)S(1)}, u32[]{:S(2)}, u32[]{:S(2)}) %collective-permute-start.13) | collective-permute-done | bytes 786464 | tf_op jit(solution)/shard_map/ppermute | solution.py:485
  59.6 2.8 %shard_map.95.refs_0_.after_ref = bf16[768,512]{1,0:T(8,128)(2,1)S(1)} custom-call(s32[8]{0:T(128)S(1)} %compare_select_fusion.3.dests, bf16[768,1024]{1,0:T(8,128)(2,1)S(1)} %bitcast.19, bf16[1024,8192]{1,0:T(8,128)(2,1)} %w_ref.29, bf16[768,512]{1,0:T(8,128)(2,1)S(1)} %collective-permute-done.13.refs_0_, bf16[768,512]{1,0:T(8,128)(2,1)S(1)} %shard_map.94.refs_1_), custom_call_target="tpu_custom_call" | custom-call | flops 24159191040 | bytes 4194304 | tf_op jit(solution)/shard_map/pallas_call | solution.py:81
  68.6 2.8 %shard_map.98.refs_1_ = bf16[768,512]{1,0:T(8,128)(2,1)S(1)} custom-call(s32[8]{0:T(128)S(1)} %compare_select_fusion.3.dests, bf16[768,1024]{1,0:T(8,128)(2,1)S(1)} %bitcast.20, bf16[1024,8192]{1,0:T(8,128)(2,1)} %w_ref.29, bf16[768,512]{1,0:T(8,128)(2,1)S(1)} %collective-permute-done.11.refs_0_, f32[64,384]{1,0:T(8,128)S(1)} %shard_map.97.refs_1_.low_ref), custom_call_target="tpu_custom_call" | custom-call | flops 24159191040 | bytes 4194304 | tf_op jit(solution)/shard_map/pallas_call | solution.py:81
  71.5 5.1 %collective-permute-done.10.refs_0_ = bf16[768,512]{1,0:T(8,128)(2,1)S(1)} collective-permute-done((bf16[768,512]{1,0:T(8,128)(2,1)S(1)}, bf16[768,512]{1,0:T(8,128)(2,1)S(1)}, u32[]{:S(2)}, u32[]{:S(2)}) %collective-permute-start.10) | collective-permute-done | bytes 786464 | tf_op jit(solution)/shard_map/ppermute | solution.py:485
  76.6 2.8 %shard_map.99.refs_1_ = bf16[768,512]{1,0:T(8,128)(2,1)S(1)} custom-call(s32[8]{0:T(128)S(1)} %compare_select_fusion.3.dests, bf16[768,1024]{1,0:T(8,128)(2,1)S(1)} %bitcast.21, bf16[1024,8192]{1,0:T(8,128)(2,1)} %w_ref.29, bf16[768,512]{1,0:T(8,128)(2,1)S(1)} %collective-permute-done.10.refs_0_, bf16[768,512]{1,0:T(8,128)(2,1)S(1)} %shard_map.98.refs_1_), custom_call_target="tpu_custom_call" | custom-call | flops 24159191040 | bytes 4194304 | tf_op jit(solution)/shard_map/pallas_call | solution.py:81
  79.4 2.7 %collective-permute-done.9.refs_0_ = bf16[768,512]{1,0:T(8,128)(2,1)S(1)} collective-permute-done((bf16[768,512]{1,0:T(8,128)(2,1)S(1)}, bf16[768,512]{1,0:T(8,128)(2,1)S(1)}, u32[]{:S(2)}, u32[]{:S(2)}) %collective-permute-start.9) | collective-permute-done | bytes 786464 | tf_op jit(solution)/shard_map/ppermute | solution.py:485
  82.2 2.8 %shard_map.100.after_ref = bf16[768,512]{1,0:T(8,128)(2,1)S(1)} custom-call(s32[8]{0:T(128)S(1)} %compare_select_fusion.3.dests, bf16[768,1024]{1,0:T(8,128)(2,1)S(1)} %bitcast.22, bf16[1024,8192]{1,0:T(8,128)(2,1)} %w_ref.29, bf16[768,512]{1,0:T(8,128)(2,1)S(1)} %collective-permute-done.9.refs_0_, bf16[768,512]{1,0:T(8,128)(2,1)S(1)} %shard_map.99.refs_1_), custom_call_target="tpu_custom_call" | custom-call | flops 24159191040 | bytes 4194304 | tf_op jit(solution)/shard_map/pallas_call | solution.py:81
  85.0 2.7 %shard_map.101.refs_0_.after_ref = bf16[24,64,1024]{2,1,0:T(8,128)(2,1)S(1)} custom-call(s32[24]{0:T(128)S(1)} %copy-done.3, bf16[96,64,1024]{2,1,0:T(8,128)(2,1)} %table_ref.7, bf16[768,512]{1,0:T(8,128)(2,1)S(1)} %shard_map.100.after_ref), custom_call_target="tpu_custom_call" | custom-call | bytes 6291456 | tf_op jit(solution)/shard_map/pallas_call | solution.py:175
  89.0 5.5 %collective-permute-done.17 = f16[64,384]{1,0:T(8,128)(2,1)S(1)} collective-permute-done((f16[64,384]{1,0:T(8,128)(2,1)S(1)}, f16[64,384]{1,0:T(8,128)(2,1)S(1)}, u32[]{:S(2)}, u32[]{:S(2)}) %collective-permute-start.17) | collective-permute-done | bytes 49184 | tf_op jit(solution)/shard_map/ppermute | solution.py:511
  97.3 2.8 %shard_map.104.refs_1_ = bf16[768,512]{1,0:T(8,128)(2,1)S(1)} custom-call(s32[8]{0:T(128)S(1)} %compare_select_fusion.3.dests, bf16[768,1024]{1,0:T(8,128)(2,1)S(1)} %bitcast.23, bf16[1024,8192]{1,0:T(8,128)(2,1)} %w_ref.29, bf16[768,512]{1,0:T(8,128)(2,1)S(1)} %collective-permute-done.16.refs_0_, bf16[64,384]{1,0:T(8,128)(2,1)S(1)} %shard_map.103.refs_1_.low_ref), custom_call_target="tpu_custom_call" | custom-call | flops 24159191040 | bytes 4194304 | tf_op jit(solution)/shard_map/pallas_call | solution.py:81
  102.1 2.8 %shard_map.105.after_ref = bf16[768,512]{1,0:T(8,128)(2,1)S(1)} custom-call(s32[8]{0:T(128)S(1)} %compare_select_fusion.3.dests, bf16[768,1024]{1,0:T(8,128)(2,1)S(1)} %bitcast.24, bf16[1024,8192]{1,0:T(8,128)(2,1)} %w_ref.29, bf16[768,512]{1,0:T(8,128)(2,1)S(1)} %collective-permute-done.15.refs_0_, bf16[768,512]{1,0:T(8,128)(2,1)S(1)} %shard_map.104.refs_1_), custom_call_target="tpu_custom_call" | custom-call | flops 24159191040 | bytes 4194304 | tf_op jit(solution)/shard_map/pallas_call | solution.py:81
  105.1 7.8 %shard_map.106 = (f32[768,1024]{1,0:T(8,128)S(1)}, bf16[24,64,1024]{2,1,0:T(8,128)(2,1)S(1)}) custom-call(s32[24]{0:T(128)S(1)} %compare_convert_fusion.local, s32[24]{0:T(128)S(1)} %copy-done.6, s32[8]{0:T(128)S(1)} %compare_select_fusion.3.dests, bf16[768,1024]{1,0:T(8,128)(2,1)S(1)} %bitcast.25, bf16[1024,8192]{1,0:T(8,128)(2,1)} %w_ref.29, ...), custom_call_target="tpu_custom_call" | custom-call | flops 48318382080 | bytes 13107200 | tf_op jit(solution)/shard_map/pallas_call | solution.py:305
  112.8 3.2 %collective-permute-done.18.other_ref = bf16[64,384]{1,0:T(8,128)(2,1)S(1)} collective-permute-done((bf16[64,384]{1,0:T(8,128)(2,1)S(1)}, bf16[64,384]{1,0:T(8,128)(2,1)S(1)}, u32[]{:S(2)}, u32[]{:S(2)}) %collective-permute-start.18) | collective-permute-done | bytes 49184 | tf_op jit(solution)/shard_map/ppermute | solution.py:511
  117.2 12.2 %collective-permute-done.22.right_ref = bf16[768,512]{1,0:T(8,128)(2,1)S(1)} collective-permute-done((bf16[768,512]{1,0:T(8,128)(2,1)S(1)}, bf16[768,512]{1,0:T(8,128)(2,1)S(1)}, u32[]{:S(2)}, u32[]{:S(2)}) %collective-permute-start.22) | collective-permute-done | bytes 786464 | tf_op jit(solution)/shard_map/ppermute | solution.py:485
  (92 shorter events, 37.3 us)
Async XLA Ops:
  0.0 15.0 %copy-start = (s32[192]{0:T(256)S(1)}, s32[192]{0:T(256)}, u32[]{:S(2)}) copy-start(s32[192]{0:T(256)} %param.12) | copy-start | bytes 2308
  0.0 13.6 %collective-permute-start = (s32[3,2,4]{2,1,0:T(2,128)}, s32[3,2,4]{2,1,0:T(2,128)}, u32[]{:S(2)}, u32[]{:S(2)}) collective-permute-start(s32[3,2,4]{2,1,0:T(2,128)} %param.13), channel_id=1, source_target_pairs={{0,8},{8,0},{1,9},{9,1},{2,10},{10,2},{3,11},{11,3},{4,12},{12,4},... | collective-permute-start | bytes 296 | tf_op jit(solution)/shard_map/ppermute | solution.py:491
  4.8 18.0 %collective-permute-start.1 = (bf16[768,256]{1,0:T(8,128)(2,1)}, bf16[768,256]{1,0:T(8,128)(2,1)S(1)}, u32[]{:S(2)}, u32[]{:S(2)}) collective-permute-start(bf16[768,256]{1,0:T(8,128)(2,1)} %get-tuple-element.15), channel_id=1, source_target_pairs={{0,2},{2,4},{4,6},{6,7},{7,5},{5,3},{3,1},{1,0},{8,9},{10,8},{12,1... | collective-permute-start | bytes 1179656 | tf_op jit(solution)/shard_map/ppermute | solution.py:496
  7.3 17.5 %collective-permute-start.2 = (bf16[768,256]{1,0:T(8,128)(2,1)}, bf16[768,256]{1,0:T(8,128)(2,1)S(1)}, u32[]{:S(2)}, u32[]{:S(2)}) collective-permute-start(bf16[768,256]{1,0:T(8,128)(2,1)} %get-tuple-element.16), channel_id=1, source_target_pairs={{0,1},{2,0},{4,2},{6,4},{7,6},{5,7},{3,5},{1,3},{8,10},{10,12},{12... | collective-permute-start | bytes 1179656 | tf_op jit(solution)/shard_map/ppermute | solution.py:496
  10.9 25.2 %collective-permute-start.8 = (bf16[768,256]{1,0:T(8,128)(2,1)}, bf16[768,256]{1,0:T(8,128)(2,1)S(1)}, u32[]{:S(2)}, u32[]{:S(2)}) collective-permute-start(bf16[768,256]{1,0:T(8,128)(2,1)} %get-tuple-element.22), channel_id=1, source_target_pairs={{0,2},{2,4},{4,6},{6,7},{7,5},{5,3},{3,1},{1,0},{8,9},{10,8},{12,1... | collective-permute-start | bytes 1179656 | tf_op jit(solution)/shard_map/ppermute | solution.py:496
  13.0 27.8 %collective-permute-start.7 = (bf16[768,256]{1,0:T(8,128)(2,1)S(1)}, bf16[768,256]{1,0:T(8,128)(2,1)S(1)}, u32[]{:S(2)}, u32[]{:S(2)}) collective-permute-start(bf16[768,256]{1,0:T(8,128)(2,1)S(1)} %get-tuple-element.21), channel_id=1, source_target_pairs={{0,1},{2,0},{4,2},{6,4},{7,6},{5,7},{3,5},{1,3},{8,10},{10,12},{12... | collective-permute-start | bytes 1179656 | tf_op jit(solution)/shard_map/ppermute | solution.py:496
  19.8 7.8 %collective-permute-start.5 = (bf16[24,64,1024]{2,1,0:T(8,128)(2,1)S(1)}, bf16[24,64,1024]{2,1,0:T(8,128)(2,1)S(1)}, u32[]{:S(2)}, u32[]{:S(2)}) collective-permute-start(bf16[24,64,1024]{2,1,0:T(8,128)(2,1)S(1)} %shard_map.84.refs_0_), channel_id=1, source_target_pairs={{0,8},{8,0},{1,9},{9,1},{2,10},{10,2},{3,11},{11,3},{4,12},{12,4},... | collective-permute-start | bytes 9437192 | tf_op jit(solution)/shard_map/ppermute | solution.py:502
  22.7 24.8 %collective-permute-start.4 = (bf16[768,512]{1,0:T(8,128)(2,1)S(1)}, bf16[768,512]{1,0:T(8,128)(2,1)S(1)}, u32[]{:S(2)}, u32[]{:S(2)}) collective-permute-start(bf16[768,512]{1,0:T(8,128)(2,1)S(1)} %shard_map.85.refs_2_), channel_id=1, source_target_pairs={{0,2},{2,4},{4,6},{6,7},{7,5},{5,3},{3,1},{1,0},{8,9},{10,8},{12,1... | collective-permute-start | bytes 2359304 | tf_op jit(solution)/shard_map/ppermute | solution.py:485
  27.6 24.8 %collective-permute-start.3 = (bf16[768,512]{1,0:T(8,128)(2,1)S(1)}, bf16[768,512]{1,0:T(8,128)(2,1)S(1)}, u32[]{:S(2)}, u32[]{:S(2)}) collective-permute-start(bf16[768,512]{1,0:T(8,128)(2,1)S(1)} %shard_map.87.after_ref), channel_id=1, source_target_pairs={{0,1},{2,0},{4,2},{6,4},{7,6},{5,7},{3,5},{1,3},{8,10},{10,12},{12... | collective-permute-start | bytes 2359304 | tf_op jit(solution)/shard_map/ppermute | solution.py:485
  34.1 12.6 %collective-permute-start.6 = (f16[64,384]{1,0:T(8,128)(2,1)S(1)}, f16[64,384]{1,0:T(8,128)(2,1)S(1)}, u32[]{:S(2)}, u32[]{:S(2)}) collective-permute-start(f16[64,384]{1,0:T(8,128)(2,1)S(1)} %multiply_convert_fusion.2), channel_id=1, source_target_pairs={{0,1},{1,0},{2,3},{3,2},{4,5},{5,4},{6,7},{7,6},{8,9},{9,8},{10,11... | collective-permute-start | bytes 147464 | tf_op jit(solution)/shard_map/ppermute | solution.py:511
  39.1 20.5 %collective-permute-start.13 = (bf16[768,512]{1,0:T(8,128)(2,1)S(1)}, bf16[768,512]{1,0:T(8,128)(2,1)S(1)}, u32[]{:S(2)}, u32[]{:S(2)}) collective-permute-start(bf16[768,512]{1,0:T(8,128)(2,1)S(1)} %shard_map.89.refs_2_), channel_id=1, source_target_pairs={{0,2},{2,4},{4,6},{6,7},{7,5},{5,3},{3,1},{1,0},{8,9},{10,8},{12,1... | collective-permute-start | bytes 2359304 | tf_op jit(solution)/shard_map/ppermute | solution.py:485
  43.7 24.9 %collective-permute-start.11 = (bf16[768,512]{1,0:T(8,128)(2,1)S(1)}, bf16[768,512]{1,0:T(8,128)(2,1)S(1)}, u32[]{:S(2)}, u32[]{:S(2)}) collective-permute-start(bf16[768,512]{1,0:T(8,128)(2,1)S(1)} %shard_map.90.refs_0_.after_ref), channel_id=1, source_target_pairs={{0,1},{2,0},{4,2},{6,4},{7,6},{5,7},{3,5},{1,3},{8,10},{10,12},{12... | collective-permute-start | bytes 2359304 | tf_op jit(solution)/shard_map/ppermute | solution.py:485
  47.4 17.8 %collective-permute-start.12 = (f16[64,384]{1,0:T(8,128)(2,1)S(1)}, f16[64,384]{1,0:T(8,128)(2,1)S(1)}, u32[]{:S(2)}, u32[]{:S(2)}) collective-permute-start(f16[64,384]{1,0:T(8,128)(2,1)S(1)} %multiply_convert_fusion.1), channel_id=1, source_target_pairs={{0,2},{1,3},{2,0},{3,1},{4,6},{5,7},{6,4},{7,5},{8,10},{9,11},{10,... | collective-permute-start | bytes 147464 | tf_op jit(solution)/shard_map/ppermute | solution.py:511
  50.3 26.3 %collective-permute-start.10 = (bf16[768,512]{1,0:T(8,128)(2,1)S(1)}, bf16[768,512]{1,0:T(8,128)(2,1)S(1)}, u32[]{:S(2)}, u32[]{:S(2)}) collective-permute-start(bf16[768,512]{1,0:T(8,128)(2,1)S(1)} %shard_map.93.refs_1_), channel_id=1, source_target_pairs={{0,2},{2,4},{4,6},{6,7},{7,5},{5,3},{3,1},{1,0},{8,9},{10,8},{12,1... | collective-permute-start | bytes 2359304 | tf_op jit(solution)/shard_map/ppermute | solution.py:485
  55.1 27.0 %collective-permute-start.9 = (bf16[768,512]{1,0:T(8,128)(2,1)S(1)}, bf16[768,512]{1,0:T(8,128)(2,1)S(1)}, u32[]{:S(2)}, u32[]{:S(2)}) collective-permute-start(bf16[768,512]{1,0:T(8,128)(2,1)S(1)} %shard_map.94.refs_1_), channel_id=1, source_target_pairs={{0,1},{2,0},{4,2},{6,4},{7,6},{5,7},{3,5},{1,3},{8,10},{10,12},{12... | collective-permute-start | bytes 2359304 | tf_op jit(solution)/shard_map/ppermute | solution.py:485
  62.4 34.0 %collective-permute-start.16 = (bf16[768,512]{1,0:T(8,128)(2,1)S(1)}, bf16[768,512]{1,0:T(8,128)(2,1)S(1)}, u32[]{:S(2)}, u32[]{:S(2)}) collective-permute-start(bf16[768,512]{1,0:T(8,128)(2,1)S(1)} %shard_map.95.refs_0_.after_ref), channel_id=1, source_target_pairs={{0,2},{2,4},{4,6},{6,7},{7,5},{5,3},{3,1},{1,0},{8,9},{10,8},{12,1... | collective-permute-start | bytes 2359304 | tf_op jit(solution)/shard_map/ppermute | solution.py:485
  66.0 28.6 %collective-permute-start.17 = (f16[64,384]{1,0:T(8,128)(2,1)S(1)}, f16[64,384]{1,0:T(8,128)(2,1)S(1)}, u32[]{:S(2)}, u32[]{:S(2)}) collective-permute-start(f16[64,384]{1,0:T(8,128)(2,1)S(1)} %multiply_convert_fusion), channel_id=1, source_target_pairs={{0,4},{1,5},{2,6},{3,7},{4,0},{5,1},{6,2},{7,3},{8,12},{9,13},{10,... | collective-permute-start | bytes 147464 | tf_op jit(solution)/shard_map/ppermute | solution.py:511
  71.4 28.7 %collective-permute-start.15 = (bf16[768,512]{1,0:T(8,128)(2,1)S(1)}, bf16[768,512]{1,0:T(8,128)(2,1)S(1)}, u32[]{:S(2)}, u32[]{:S(2)}) collective-permute-start(bf16[768,512]{1,0:T(8,128)(2,1)S(1)} %shard_map.98.refs_1_), channel_id=1, source_target_pairs={{0,1},{2,0},{4,2},{6,4},{7,6},{5,7},{3,5},{1,3},{8,10},{10,12},{12... | collective-permute-start | bytes 2359304 | tf_op jit(solution)/shard_map/ppermute | solution.py:485
  87.6 17.3 %collective-permute-start.14 = (bf16[24,64,1024]{2,1,0:T(8,128)(2,1)S(1)}, bf16[24,64,1024]{2,1,0:T(8,128)(2,1)S(1)}, u32[]{:S(2)}, u32[]{:S(2)}) collective-permute-start(bf16[24,64,1024]{2,1,0:T(8,128)(2,1)S(1)} %shard_map.101.refs_0_.after_ref), channel_id=1, source_target_pairs={{0,8},{8,0},{1,9},{9,1},{2,10},{10,2},{3,11},{11,3},{4,12},{12,4},... | collective-permute-start | bytes 9437192 | tf_op jit(solution)/shard_map/ppermute | solution.py:522
  87.7 29.1 %collective-permute-start.19 = (bf16[768,512]{1,0:T(8,128)(2,1)S(1)}, bf16[768,512]{1,0:T(8,128)(2,1)S(1)}, u32[]{:S(2)}, u32[]{:S(2)}) collective-permute-start(bf16[768,512]{1,0:T(8,128)(2,1)S(1)} %shard_map.100.after_ref), channel_id=1, source_target_pairs={{0,1},{2,0},{4,2},{6,4},{7,6},{5,7},{3,5},{1,3},{8,10},{10,12},{12... | collective-permute-start | bytes 2359304 | tf_op jit(solution)/shard_map/ppermute | solution.py:485
  94.5 22.3 %collective-permute-start.20 = (bf16[768,512]{1,0:T(8,128)(2,1)S(1)}, bf16[768,512]{1,0:T(8,128)(2,1)S(1)}, u32[]{:S(2)}, u32[]{:S(2)}) collective-permute-start(bf16[768,512]{1,0:T(8,128)(2,1)S(1)} %shard_map.99.refs_1_), channel_id=1, source_target_pairs={{0,2},{2,4},{4,6},{6,7},{7,5},{5,3},{3,1},{1,0},{8,9},{10,8},{12,1... | collective-permute-start | bytes 2359304 | tf_op jit(solution)/shard_map/ppermute | solution.py:485
  96.4 19.7 %collective-permute-start.18 = (bf16[64,384]{1,0:T(8,128)(2,1)S(1)}, bf16[64,384]{1,0:T(8,128)(2,1)S(1)}, u32[]{:S(2)}, u32[]{:S(2)}) collective-permute-start(bf16[64,384]{1,0:T(8,128)(2,1)S(1)} %shard_map.103.refs_1_.low_ref), channel_id=1, source_target_pairs={{0,1},{1,0},{2,3},{3,2},{4,5},{5,4},{6,7},{7,6},{8,9},{9,8},{10,11... | collective-permute-start | bytes 147464 | tf_op jit(solution)/shard_map/ppermute | solution.py:511
  100.1 29.5 %collective-permute-start.21 = (bf16[768,512]{1,0:T(8,128)(2,1)S(1)}, bf16[768,512]{1,0:T(8,128)(2,1)S(1)}, u32[]{:S(2)}, u32[]{:S(2)}) collective-permute-start(bf16[768,512]{1,0:T(8,128)(2,1)S(1)} %shard_map.104.refs_1_), channel_id=1, source_target_pairs={{0,2},{2,4},{4,6},{6,7},{7,5},{5,3},{3,1},{1,0},{8,9},{10,8},{12,1... | collective-permute-start | bytes 2359304 | tf_op jit(solution)/shard_map/ppermute | solution.py:485
  105.0 24.4 %collective-permute-start.22 = (bf16[768,512]{1,0:T(8,128)(2,1)S(1)}, bf16[768,512]{1,0:T(8,128)(2,1)S(1)}, u32[]{:S(2)}, u32[]{:S(2)}) collective-permute-start(bf16[768,512]{1,0:T(8,128)(2,1)S(1)} %shard_map.105.after_ref), channel_id=1, source_target_pairs={{0,1},{2,0},{4,2},{6,4},{7,6},{5,7},{3,5},{1,3},{8,10},{10,12},{12... | collective-permute-start | bytes 2359304 | tf_op jit(solution)/shard_map/ppermute | solution.py:485
  (11 other events, 67.7 us)
